TPU v7x, 32 devices: a whole 2x2x4 slice. The times are simulated.
32 devices in a mesh: leaf: 2 (over core), row: 4 (over y, x), col: 4 (over z).
Axes of the slice: x: 2, y: 2, z: 4, core: 2. Of those that a mesh axis runs over, the one named last changes fastest.
Arguments:
- child_rhs: float32 [64, 256, 256], P(('leaf', 'row', 'col')), may hold values from -6 to 6
- child_diag: float32 [64, 256, 256], P(('leaf', 'row', 'col')), may hold values from -0.375 to 0.375
- child_off: float32 [64, 256, 256], P(('leaf', 'row', 'col')), may hold values from -0.125 to 0.125
- live: int32 [64], P(('leaf', 'row', 'col')), may hold values from 1 to 256, 10240 in all
- targets: int32 [64, 256], P(('leaf', 'row', 'col')), may hold values from 0 to 2047
- top_rhs: float32 [2048, 256], P('row'), may hold values from -6 to 6
- top_factor: float32 [2048, 2048], P('row', 'col'), may hold values from -0.125 to 0.125
- top_diag: float32 [2048, 512], P('row'), may hold values from -0.25 to 0.25
Outputs:
- child_sol: float32 [64, 256, 256], P(('leaf', 'row', 'col'))
- top_sol: float32 [2048, 256], P('row')
All inputs are finite; a program needn't handle non-finite values. No bound on the sum of `live` on one device may be relied on, other than what follows from the above.
Results may differ from a plain program's by a relative error of at most 0.0003.
Values sent between devices are 32-bit elements; how exact they have to be, the bound alone decides.
No kernel may reach another device: no remote copies, remote signals or barrier semaphores. Data moves between devices by JAX's collectives and lax.ppermute only.
A program may use at most 64 MiB of HBM per device.

v0:
```python
import jax
import jax.numpy as jnp
from jax import lax
from jax.sharding import PartitionSpec as P


def spread(value, axis, source):
    kept = jnp.where(lax.axis_index(axis) == source, value, 0).astype(value.dtype)
    return lax.psum(kept, axis)


def unit_lower(matrix):
    return jnp.tril(matrix) + jnp.eye(matrix.shape[-1], dtype=matrix.dtype)


def shards(child_rhs, child_diag, child_off, live, targets, top_rhs, top_factor, top_diag):
    highest = lax.Precision.HIGHEST
    owned_rows = top_rhs.shape[0]
    right_count = top_rhs.shape[1]
    block_size = top_diag.shape[1]
    owned_blocks = owned_rows // block_size
    row_count = lax.axis_size("row")
    top_order = owned_rows * row_count
    col_width = top_factor.shape[1]
    my_row = lax.axis_index("row")
    my_col = lax.axis_index("col")
    child_sol = jnp.einsum("bij,bjr->bir", unit_lower(child_diag), child_rhs, precision=highest)
    tiles = jnp.einsum("btj,bjr->btr", child_off, child_sol, precision=highest)
    slot_index = jnp.arange(child_off.shape[1], dtype=jnp.int32)
    keep = slot_index[None, :] < live[:, None]
    tiles = jnp.where(keep[:, :, None], tiles, jnp.zeros_like(tiles))
    contrib = jnp.zeros((top_order, right_count), jnp.float32)
    contrib = contrib.at[targets.reshape(-1)].add(tiles.reshape(-1, right_count))
    row_part = lax.psum_scatter(contrib, "row", scatter_dimension=0, tiled=True)
    share = lax.psum_scatter(row_part, ("leaf", "col"), scatter_dimension=0, tiled=True)
    updates = lax.all_gather(share, ("leaf", "col"), axis=0, tiled=True)
    reduced = top_rhs - updates
    inverse_all = unit_lower(top_diag.reshape(owned_blocks, block_size, block_size))
    col_global = my_col * col_width + jnp.arange(col_width, dtype=jnp.int32)

    def step(block, solution):
        local = block % owned_blocks
        owner = block // owned_blocks
        factor_rows = top_factor
        factor_rows = jnp.where(
            (col_global < block * block_size)[None, :], factor_rows, jnp.zeros_like(factor_rows)
        )
        columns = lax.dynamic_slice_in_dim(solution, my_col * col_width, col_width, 0)
        partial_value = jnp.dot(
            factor_rows, columns, precision=highest, preferred_element_type=jnp.float32
        )
        block_inverse = lax.dynamic_index_in_dim(inverse_all, local, 0, keepdims=False)
        before = lax.psum(partial_value, "col")
        solved = jnp.dot(
            block_inverse, reduced - before, precision=highest, preferred_element_type=jnp.float32
        )
        solved = spread(solved, "row", owner)
        return lax.dynamic_update_slice_in_dim(solution, solved, block * block_size, 0)

    solution = lax.fori_loop(
        0, row_count * owned_blocks, step, jnp.zeros((top_order, right_count), jnp.float32)
    )
    top_sol = lax.dynamic_slice_in_dim(solution, my_row * owned_rows, owned_rows, 0)
    return (child_sol, top_sol)


def solution(mesh):
    in_specs = (
        P(("leaf", "row", "col"), None, None),
        P(("leaf", "row", "col"), None, None),
        P(("leaf", "row", "col"), None, None),
        P(("leaf", "row", "col")),
        P(("leaf", "row", "col"), None),
        P("row", None),
        P("row", "col"),
        P("row", None),
    )
    out_specs = (P(("leaf", "row", "col"), None, None), P("row", None))
    return jax.shard_map(shards, mesh=mesh, in_specs=in_specs, out_specs=out_specs, check_vma=False)
```

profile of v0, /device:TPU:15, one launch (start us, length us, event | category | flops | bytes accessed | tf_op | source)
XLA Modules:
  0.0 495.6 jit_solution(7571788434740364663)
XLA Ops:
  7.2 0.0 reduce-scatter.3.cloned.1.call-start
  7.3 0.8 iota_compare_fusion.4
  8.1 0.7 copy.18
  8.8 1.2 copy.10
  10.0 1.1 fusion.14
  11.1 0.8 copy-done.2
  11.9 0.7 convolution_select_fusion.1
  12.6 4.7 scatter_custom_fusion
  17.3 0.0 reduce-scatter.3.cloned.1.call-update
  17.3 0.0 reduce-scatter.5.cloned.1.call-start
  17.4 35.5 %reduce-scatter.3.cloned.1.call-done = f32[512,256]{1,0:T(8,128)} async-done(((f32[2048,256]{1,0:T(8,128)}), f32[512,256]{1,0:T(8,128)}) %reduce-scatter.3.cloned.1.call-update) | async-done | bytes 524304 | tf_op jit(solution)/shard_map/reduce_scatter | solution.py:34
  52.9 0.1 add_bitcast_fusion
  53.0 33.6 %reduce-scatter.5.cloned.1.call-done = f32[64,256]{1,0:T(8,128)} async-done(((f32[512,256]{1,0:T(8,128)}), f32[64,256]{1,0:T(8,128)}) %reduce-scatter.5.cloned.1.call-update) | async-done | bytes 65552 | tf_op jit(solution)/shard_map/reduce_scatter | solution.py:35
  86.7 26.6 %all_gather.3 = f32[512,256]{1,0:T(8,128)S(1)} all-gather(f32[64,256]{1,0:T(8,128)} %reduce-scatter.5.cloned.1.call-done), channel_id=1, replica_groups=mesh['leaf'=2,'row'=4,'col'=4] {'leaf','col'}, dimensions={0}, use_global_device_ids=true | all-gather | bytes 589824 | tf_op jit(solution)/shard_map/all_gather | solution.py:36
  113.2 0.9 sub.17
  114.1 1.5 broadcast.60.clone
  115.6 371.3 %while.16 = (s32[]{:T(128)}, f32[2048,256]{1,0:T(8,128)}, f32[512,512]{1,0:T(8,128)S(1)}, s32[]{:T(128)}, f32[512,256]{1,0:T(8,128)}, /*index=5*/f32[1,512,512]{...) while((s32[]{:T(128)}, f32[2048,256]{1,0:T(8,128)}, ...), condition=%wide.region_6.7_spmd.clone, body=%wide.region_3.6_spmd.clone.sunk | while | flops 1611400192 | bytes 13109041 | solution.py:60
  115.6 2.8 fusion.35
  118.4 0.0 all-reduce.3.cloned.1.call-update
  118.5 0.0 all-reduce.5.cloned.1.call-start
  118.5 38.1 %all-reduce.3.cloned.1.call-done = f32[512,256]{1,0:T(8,128)} async-done(((f32[512,256]{1,0:T(8,128)}), f32[512,256]{1,0:T(8,128)}) %all-reduce.3.cloned.1.call-update) | async-done | bytes 524304 | tf_op jit(solution)/shard_map/while/body/eval_jaxpr/psum | solution.py:53
  156.6 3.9 fusion.36
  160.5 0.0 all-reduce.5.cloned.1.call-update
  160.5 45.7 %all-reduce.5.cloned.1.call-done = f32[512,256]{0,1:T(8,128)} async-done(((f32[512,256]{0,1:T(8,128)}), f32[512,256]{0,1:T(8,128)}) %all-reduce.5.cloned.1.call-update) | async-done | bytes 524304 | tf_op jit(solution)/shard_map/while/body/eval_jaxpr/psum | solution.py:9
  206.2 1.2 copy.20
  207.4 0.8 constant_dynamic-update-slice_fusion.2
  208.2 2.8 fusion.35
  211.1 0.0 all-reduce.5.cloned.1.call-start
  211.2 38.2 %all-reduce.3.cloned.1.call-done = f32[512,256]{1,0:T(8,128)} async-done(((f32[512,256]{1,0:T(8,128)}), f32[512,256]{1,0:T(8,128)}) %all-reduce.3.cloned.1.call-update) | async-done | bytes 524304 | tf_op jit(solution)/shard_map/while/body/eval_jaxpr/psum | solution.py:53
  249.4 3.9 fusion.36
  253.3 45.7 %all-reduce.5.cloned.1.call-done = f32[512,256]{0,1:T(8,128)} async-done(((f32[512,256]{0,1:T(8,128)}), f32[512,256]{0,1:T(8,128)}) %all-reduce.5.cloned.1.call-update) | async-done | bytes 524304 | tf_op jit(solution)/shard_map/while/body/eval_jaxpr/psum | solution.py:9
  298.9 1.2 copy.20
  300.2 0.8 constant_dynamic-update-slice_fusion.2
  301.0 2.8 fusion.35
  303.9 0.0 all-reduce.5.cloned.1.call-start
  303.9 38.4 %all-reduce.3.cloned.1.call-done = f32[512,256]{1,0:T(8,128)} async-done(((f32[512,256]{1,0:T(8,128)}), f32[512,256]{1,0:T(8,128)}) %all-reduce.3.cloned.1.call-update) | async-done | bytes 524304 | tf_op jit(solution)/shard_map/while/body/eval_jaxpr/psum | solution.py:53
  342.3 3.9 fusion.36
  346.2 45.7 %all-reduce.5.cloned.1.call-done = f32[512,256]{0,1:T(8,128)} async-done(((f32[512,256]{0,1:T(8,128)}), f32[512,256]{0,1:T(8,128)}) %all-reduce.5.cloned.1.call-update) | async-done | bytes 524304 | tf_op jit(solution)/shard_map/while/body/eval_jaxpr/psum | solution.py:9
  391.9 1.2 copy.20
  393.1 0.8 constant_dynamic-update-slice_fusion.2
  394.0 2.8 fusion.35
  396.8 0.0 all-reduce.5.cloned.1.call-start
  396.9 38.4 %all-reduce.3.cloned.1.call-done = f32[512,256]{1,0:T(8,128)} async-done(((f32[512,256]{1,0:T(8,128)}), f32[512,256]{1,0:T(8,128)}) %all-reduce.3.cloned.1.call-update) | async-done | bytes 524304 | tf_op jit(solution)/shard_map/while/body/eval_jaxpr/psum | solution.py:53
  435.3 3.9 fusion.36
  439.2 45.7 %all-reduce.5.cloned.1.call-done = f32[512,256]{0,1:T(8,128)} async-done(((f32[512,256]{0,1:T(8,128)}), f32[512,256]{0,1:T(8,128)}) %all-reduce.5.cloned.1.call-update) | async-done | bytes 524304 | tf_op jit(solution)/shard_map/while/body/eval_jaxpr/psum | solution.py:9
  484.9 1.2 copy.20
  486.1 0.8 constant_dynamic-update-slice_fusion.2
  486.9 1.9 constant_dynamic-slice_fusion
  (28 shorter events, 0.2 us)
Async XLA Ops:
  7.2 2.9 copy-start
  7.2 4.7 copy-start.5
  7.2 45.7 %reduce-scatter.3.cloned.1.call-start = ((), (), s32[]{:S(2)}) async-start(), calls=%async_computation.2 | async-start | bytes 2621440 | tf_op jit(solution)/shard_map/reduce_scatter | solution.py:34
  11.1 0.8 copy-start.2
  12.6 40.3 %copy-start.3 = (f32[512,512]{1,0:T(8,128)S(1)}, f32[512,512]{1,0:T(8,128)}, u32[]{:S(2)}) copy-start(f32[512,512]{1,0:T(8,128)} %param.17) | copy-start | bytes 3145732
  17.3 95.9 %copy-start.4 = (f32[512,256]{1,0:T(8,128)S(1)}, f32[512,256]{1,0:T(8,128)}, u32[]{:S(2)}) copy-start(f32[512,256]{1,0:T(8,128)} %param.15) | copy-start | bytes 1572868
  17.3 69.3 %reduce-scatter.5.cloned.1.call-start = ((), (), s32[]{:S(2)}) async-start(), calls=%async_computation.3 | async-start | bytes 589824 | tf_op jit(solution)/shard_map/reduce_scatter | solution.py:35
  53.0 62.6 %copy-start.1 = (f32[512,512]{1,0:T(8,128)S(1)}, f32[512,512]{1,0:T(8,128)}, u32[]{:S(2)}) copy-start(f32[512,512]{1,0:T(8,128)} %param.16) | copy-start | bytes 3145732
  115.6 41.0 %all-reduce.3.cloned.1.call-start = ((), (), s32[]{:S(2)}) async-start(), calls=%async_computation.4 | async-start | bytes 1048576 | tf_op jit(solution)/shard_map/while/body/eval_jaxpr/psum | solution.py:53
  118.5 87.7 %all-reduce.5.cloned.1.call-start = ((), (), s32[]{:S(2)}) async-start(), calls=%async_computation.5 | async-start | bytes 1048576 | tf_op jit(solution)/shard_map/while/body/eval_jaxpr/psum | solution.py:9
  208.2 41.1 %all-reduce.3.cloned.1.call-start = ((), (), s32[]{:S(2)}) async-start(), calls=%async_computation.4 | async-start | bytes 1048576 | tf_op jit(solution)/shard_map/while/body/eval_jaxpr/psum | solution.py:53
  211.1 87.8 %all-reduce.5.cloned.1.call-start = ((), (), s32[]{:S(2)}) async-start(), calls=%async_computation.5 | async-start | bytes 1048576 | tf_op jit(solution)/shard_map/while/body/eval_jaxpr/psum | solution.py:9
  301.0 41.3 %all-reduce.3.cloned.1.call-start = ((), (), s32[]{:S(2)}) async-start(), calls=%async_computation.4 | async-start | bytes 1048576 | tf_op jit(solution)/shard_map/while/body/eval_jaxpr/psum | solution.py:53
  303.9 88.0 %all-reduce.5.cloned.1.call-start = ((), (), s32[]{:S(2)}) async-start(), calls=%async_computation.5 | async-start | bytes 1048576 | tf_op jit(solution)/shard_map/while/body/eval_jaxpr/psum | solution.py:9
  394.0 41.3 %all-reduce.3.cloned.1.call-start = ((), (), s32[]{:S(2)}) async-start(), calls=%async_computation.4 | async-start | bytes 1048576 | tf_op jit(solution)/shard_map/while/body/eval_jaxpr/psum | solution.py:53
  396.8 88.0 %all-reduce.5.cloned.1.call-start = ((), (), s32[]{:S(2)}) async-start(), calls=%async_computation.5 | async-start | bytes 1048576 | tf_op jit(solution)/shard_map/while/body/eval_jaxpr/psum | solution.py:9
Sparse Core Ops, SparseCore 0:
  17.4 35.3 reduce-scatter.2
  55.2 31.4 reduce-scatter.4
  118.8 37.8 all-reduce.2
  160.6 45.4 all-reduce.4
  211.2 38.1 all-reduce.2
  253.4 45.4 all-reduce.4
  304.2 38.1 all-reduce.2
  346.3 45.4 all-reduce.4
  397.1 38.1 all-reduce.2
  439.3 45.5 all-reduce.4
where the time goes:
time: 499 us; the launch traced here: 496 us
  waiting for transfers between devices  405 us (81%)
  matrix products  28.5 us (6%)
  blocking collectives  26.6 us (5%)
  local copies, waits for them, and re-layouts  14.4 us (3%)
  between operations  14.2 us (3%)
  other arithmetic  6.59 us (1%)
    psum x4, waiting for transfers between devices, spread(): return lax.psum(kept, axis)  183 us
    psum x4, waiting for transfers between devices, step(): before = lax.psum(partial_value, 'col')  153 us
    reduce_scatter x1, waiting for transfers between devices, shards(): row_part = lax.psum_scatter(contrib, 'row', scatter_dimension=0, tiled=True)  35.5 us
    reduce_scatter x1, waiting for transfers between devices, shards(): lax.psum_scatter(row_part, ('leaf', 'col'), scatter_dimension=0, tiled=True)  33.6 us
    all_gather x1, blocking collectives, shards(): updates = lax.all_gather(share, ('leaf', 'col'), axis=0, tiled=True)  26.6 us
    dot_general x4, matrix products, step(): jnp.dot(block_inverse, reduced - before, precision=highest, preferred_ele...  15.5 us
    dot_general x4, matrix products, step(): jnp.dot(factor_rows, columns, precision=highest, preferred_element_type=j...  11.3 us
  transfers between devices with their start and end apart: 10, of which 10 were waited for; matrix products, arithmetic and copies ran while one was open for 0% of the time, Pallas kernels for 0%

commit v1 on v0

--- a/solution.py
+++ b/solution.py
@@ -1,7 +1,18 @@
+import functools
+
 import jax
 import jax.numpy as jnp
 from jax import lax
+from jax.experimental import pallas as pl
+from jax.experimental.pallas import tpu as pltpu
 from jax.sharding import PartitionSpec as P
+
+F32 = jnp.float32
+BF16 = jnp.bfloat16
+NT = (((1,), (1,)), ((), ()))
+NN = (((1,), (0,)), ((), ()))
+VM = pl.BlockSpec(memory_space=pltpu.VMEM)
+SM = pl.BlockSpec(memory_space=pltpu.SMEM)
 
 
 def spread(value, axis, source):
@@ -13,7 +24,7 @@
     return jnp.tril(matrix) + jnp.eye(matrix.shape[-1], dtype=matrix.dtype)
 
 
-def shards(child_rhs, child_diag, child_off, live, targets, top_rhs, top_factor, top_diag):
+def any_mesh(child_rhs, child_diag, child_off, live, targets, top_rhs, top_factor, top_diag):
     highest = lax.Precision.HIGHEST
     owned_rows = top_rhs.shape[0]
     right_count = top_rhs.shape[1]
@@ -29,7 +40,7 @@
     slot_index = jnp.arange(child_off.shape[1], dtype=jnp.int32)
     keep = slot_index[None, :] < live[:, None]
     tiles = jnp.where(keep[:, :, None], tiles, jnp.zeros_like(tiles))
-    contrib = jnp.zeros((top_order, right_count), jnp.float32)
+    contrib = jnp.zeros((top_order, right_count), F32)
     contrib = contrib.at[targets.reshape(-1)].add(tiles.reshape(-1, right_count))
     row_part = lax.psum_scatter(contrib, "row", scatter_dimension=0, tiled=True)
     share = lax.psum_scatter(row_part, ("leaf", "col"), scatter_dimension=0, tiled=True)
@@ -41,26 +52,225 @@
     def step(block, solution):
         local = block % owned_blocks
         owner = block // owned_blocks
-        factor_rows = top_factor
         factor_rows = jnp.where(
-            (col_global < block * block_size)[None, :], factor_rows, jnp.zeros_like(factor_rows)
+            (col_global < block * block_size)[None, :], top_factor, jnp.zeros_like(top_factor)
         )
         columns = lax.dynamic_slice_in_dim(solution, my_col * col_width, col_width, 0)
         partial_value = jnp.dot(
-            factor_rows, columns, precision=highest, preferred_element_type=jnp.float32
+            factor_rows, columns, precision=highest, preferred_element_type=F32
         )
         block_inverse = lax.dynamic_index_in_dim(inverse_all, local, 0, keepdims=False)
         before = lax.psum(partial_value, "col")
         solved = jnp.dot(
-            block_inverse, reduced - before, precision=highest, preferred_element_type=jnp.float32
+            block_inverse, reduced - before, precision=highest, preferred_element_type=F32
         )
         solved = spread(solved, "row", owner)
         return lax.dynamic_update_slice_in_dim(solution, solved, block * block_size, 0)
 
     solution = lax.fori_loop(
-        0, row_count * owned_blocks, step, jnp.zeros((top_order, right_count), jnp.float32)
+        0, row_count * owned_blocks, step, jnp.zeros((top_order, right_count), F32)
     )
     top_sol = lax.dynamic_slice_in_dim(solution, my_row * owned_rows, owned_rows, 0)
+    return (child_sol, top_sol)
+
+
+def split(value):
+    high = value.astype(BF16)
+    return high, (value - high.astype(F32)).astype(BF16)
+
+
+def dot3(left, right, dims):
+    left_high, left_low = split(left)
+    right_high, right_low = split(right)
+    rows = left.shape[0]
+    both = lax.dot_general(
+        jnp.concatenate([left_high, left_low], axis=0), right_high, dims, preferred_element_type=F32
+    )
+    cross = lax.dot_general(left_high, right_low, dims, preferred_element_type=F32)
+    return both[:rows] + both[rows:] + cross
+
+
+def lower(matrix):
+    row = lax.broadcasted_iota(jnp.int32, matrix.shape, 0)
+    col = lax.broadcasted_iota(jnp.int32, matrix.shape, 1)
+    return jnp.where(col <= row, matrix, 0.0)
+
+
+def child_kernel(where_ref, live_ref, rhs_ref, diag_ref, off_ref, tgt_ref, sol_ref, keep_ref, send_ref, tiles_ref):
+    leaf = where_ref[0]
+    children, slots = off_ref.shape[0], off_ref.shape[1]
+    half = keep_ref.shape[0]
+    for s in range(children):
+        rhs = rhs_ref[s]
+        sol = rhs + dot3(lower(diag_ref[s]), rhs, NN)
+        sol_ref[s] = sol
+        tiles = dot3(sol.T, off_ref[s], NT)
+        slot = lax.broadcasted_iota(jnp.int32, tiles.shape, 1)
+        tiles_ref[:, s * slots:(s + 1) * slots] = jnp.where(slot < live_ref[s], tiles, 0.0)
+        send_ref[half:half + 8, s * slots:(s + 1) * slots] = jnp.broadcast_to(
+            tgt_ref[s:s + 1, :].astype(F32), (8, slots)
+        )
+    keep_ref[...] = tiles_ref[pl.ds(pl.multiple_of(leaf * half, half), half), :]
+    send_ref[0:half, :] = tiles_ref[pl.ds(pl.multiple_of((1 - leaf) * half, half), half), :]
+
+
+def scatter_kernel(where_ref, keep_ref, recv_ref, tgt_ref, *out_refs):
+    row = where_ref[1]
+    half, slots_all = keep_ref.shape
+    size = out_refs[0].shape[1]
+    children, slots = tgt_ref.shape
+    mine = [split(keep_ref[...]), split(recv_ref[0:half, :])]
+    stacked = [jnp.concatenate(pair, axis=0) for pair in mine]
+    mine_targets = jnp.concatenate([tgt_ref[s:s + 1, :] for s in range(children)], axis=1)
+    target = [mine_targets, recv_ref[half:half + 1, :].astype(jnp.int32)]
+    for s, out_ref in enumerate(out_refs):
+        block = jnp.bitwise_xor(row, s)
+        index = lax.broadcasted_iota(jnp.int32, (size, slots_all), 0) + block * size
+        total = None
+        for t, value in zip(target, stacked):
+            hot = jnp.where(index == t, 1.0, 0.0).astype(BF16)
+            product = lax.dot_general(value, hot, NT, preferred_element_type=F32)
+            total = product if total is None else total + product
+        out_ref[...] = total[:half] + total[half:]
+
+
+def pieces_kernel(where_ref, a_ref, b_ref, c_ref, d_ref, first_ref, second_ref, sum_ref):
+    odd = where_ref[2] % 2
+    piece = first_ref.shape[0]
+    sum_ref[...] = (a_ref[...] + b_ref[...]) + (c_ref[...] + d_ref[...])
+    first_ref[...] = sum_ref[pl.ds(pl.multiple_of(odd * piece, piece), piece), :]
+    second_ref[...] = sum_ref[pl.ds(pl.multiple_of((1 - odd) * piece, piece), piece), :]
+
+
+def first_kernel(rhs_ref, a_ref, b_ref, c_ref, d_ref, diag_ref, res_ref, x_ref):
+    res = rhs_ref[...] - ((a_ref[...] + b_ref[...]) + (c_ref[...] + d_ref[...]))
+    res_ref[...] = res
+    x_ref[...] = res + dot3(res, lower(diag_ref[...]), NT)
+
+
+def step_kernel(count, *refs):
+    res_ref, diag_ref = refs[0], refs[1]
+    given, factors = refs[2:2 + count], refs[2 + count:2 + 2 * count]
+    res_out, x_out = refs[2 + 2 * count], refs[3 + 2 * count]
+    res = res_ref[...]
+    for x_ref, factor_ref in zip(given, factors):
+        res = res - dot3(x_ref[...], factor_ref[...], NT)
+    res_out[...] = res
+    x_out[...] = res + dot3(res, lower(diag_ref[...]), NT)
+
+
+def half_kernel(where_ref, x_ref, a_ref, b_ref, c_ref, out_ref):
+    z = where_ref[2]
+    piece = x_ref.shape[0]
+    x, a, b, c = x_ref[...], a_ref[...], b_ref[...], c_ref[...]
+    out_ref[0:piece, :] = jnp.where(z == 0, a, jnp.where(z == 1, x, jnp.where(z == 2, b, c)))
+    out_ref[piece:2 * piece, :] = jnp.where(z == 0, c, jnp.where(z == 1, b, jnp.where(z == 2, x, a)))
+
+
+def last_kernel(where_ref, own_ref, other_ref, out_ref):
+    leaf = where_ref[0]
+    half = own_ref.shape[0]
+    own, other = own_ref[...].T, other_ref[...].T
+    out_ref[:, 0:half] = jnp.where(leaf == 0, own, other)
+    out_ref[:, half:2 * half] = jnp.where(leaf == 0, other, own)
+
+
+def call(kernel, ins, outs, scratch=(), flops=0):
+    return pl.pallas_call(
+        kernel,
+        out_shape=[jax.ShapeDtypeStruct(shape, F32) for shape in outs],
+        in_specs=[SM if a.ndim == 1 else VM for a in ins],
+        out_specs=[VM] * len(outs),
+        scratch_shapes=list(scratch),
+        cost_estimate=pl.CostEstimate(flops=flops, bytes_accessed=4 * sum(a.size for a in ins), transcendentals=0),
+        compiler_params=pltpu.CompilerParams(vmem_limit_bytes=40 * 1024 * 1024),
+    )(*ins)
+
+
+def central(child_rhs, child_diag, child_off, live, targets, top_rhs, top_factor, top_diag):
+    leaf, row, col = (lax.axis_index(a) for a in ("leaf", "row", "col"))
+    where = jnp.stack([leaf, row, col]).astype(jnp.int32)
+    rows, cols = lax.axis_size("row"), lax.axis_size("col")
+    size = top_diag.shape[1]
+    right = top_rhs.shape[1]
+    half, piece = right // 2, right // 4
+    children, slots = targets.shape
+
+    def swap(value):
+        return lax.ppermute(value, "leaf", [(0, 1), (1, 0)])
+
+    def along_row(value, pairs):
+        return lax.ppermute(value, "row", pairs)
+
+    def along_col(value, pairs):
+        return lax.ppermute(value, "col", pairs)
+
+    def at(r, c):
+        return r * cols + c
+
+    part = lax.dynamic_slice_in_dim(top_factor, leaf * (size // 2), size // 2, 0)
+    near = [(at(k, 0), at(k, 1)) for k in (1, 2, 3)] + [(at(k, 1), at(k, 2)) for k in (2, 3)]
+    far = [(at(k, 0), at(k, 2)) for k in (1, 2, 3)] + [(at(3, 2), at(3, 1))]
+    near_part = lax.ppermute(part, ("row", "col"), near)
+    far_part = lax.ppermute(part, ("row", "col"), far)
+
+    start = leaf * half + (col // 2) * piece
+    rhs_piece = lax.dynamic_slice_in_dim(top_rhs, start, piece, 1).T
+
+    child_sol, keep, send = call(
+        child_kernel,
+        [where, live, child_rhs, child_diag, child_off, targets],
+        [child_rhs.shape, (half, children * slots), (half + 8, children * slots)],
+        [pltpu.VMEM((right, children * slots), F32)],
+    )
+    recv = swap(send)
+    sums = call(scatter_kernel, [where, keep, recv, targets], [(half, size)] * rows)
+    got = [along_row(sums[s], [(i, i ^ s) for i in range(rows)]) for s in (1, 2, 3)]
+
+    near_other, far_other = swap(near_part), swap(far_part)
+
+    def whole(mine, other):
+        return jnp.where(
+            leaf == 0, jnp.concatenate([mine, other], 0), jnp.concatenate([other, mine], 0)
+        )
+
+    near_whole, far_whole = whole(near_part, near_other), whole(far_part, far_other)
+    factor0 = jnp.where(col == 1, near_whole, far_whole)
+    factor1 = jnp.where(col == 1, top_factor, near_whole)
+    factor2 = jnp.where(col == 1, far_whole, top_factor)
+
+    first, second = call(
+        pieces_kernel, [where, sums[0]] + got, [(piece, size)] * 2, [pltpu.VMEM((half, size), F32)]
+    )
+    q = [
+        along_col(first, [(0, 1), (3, 2)]),
+        along_col(first, [(1, 2), (2, 1)]),
+        along_col(second, [(0, 2), (3, 1)]),
+    ]
+    shape = (piece, size)
+    res, x = call(first_kernel, [rhs_piece, second] + q + [top_diag], [shape] * 2)
+    x0 = along_row(x, [(0, 1)]) + along_row(x, [(0, 2)])
+    res, x = call(
+        functools.partial(step_kernel, 1), [res, top_diag, x0, factor0], [shape] * 2
+    )
+    on = along_row(jnp.where(row == 2, x0, x), [(1, 2), (2, 3)])
+    x1 = along_row(x, [(1, 3)])
+    x0 = jnp.where(row == 3, on, 0.0)
+    x1 = jnp.where(row == 2, on, x1)
+    res, x = call(
+        functools.partial(step_kernel, 2), [res, top_diag, x0, x1, factor0, factor1], [shape] * 2
+    )
+    x2 = along_row(x, [(2, 3)])
+    res, x = call(
+        functools.partial(step_kernel, 1), [res, top_diag, x2, factor2], [shape] * 2
+    )
+    z = [
+        along_col(x, [(1, 0), (2, 3)]),
+        along_col(x, [(1, 2), (2, 1)]),
+        along_col(x, [(1, 3), (2, 0)]),
+    ]
+    (own,) = call(half_kernel, [where, x] + z, [(half, size)])
+    (top_sol,) = call(last_kernel, [where, own, swap(own)], [top_rhs.shape])
     return (child_sol, top_sol)
 
 
@@ -76,4 +286,12 @@
         P("row", None),
     )
     out_specs = (P(("leaf", "row", "col"), None, None), P("row", None))
+    axes = tuple(mesh.shape[a] for a in ("leaf", "row", "col"))
+
+    def shards(*args):
+        top_rhs, top_factor, top_diag = args[5:]
+        size = top_diag.shape[1]
+        fits = axes == (2, 4, 4) and top_rhs.shape[0] == size and top_factor.shape[1] == size
+        return (central if fits else any_mesh)(*args)
+
     return jax.shard_map(shards, mesh=mesh, in_specs=in_specs, out_specs=out_specs, check_vma=False)

time: 499 us -> 88.9 us (0.18)
  the two profiles are of different devices: /device:TPU:15 before, /device:TPU:7 now
where the time goes in v1:
time: 88.9 us; the launch traced here: 88.4 us
  waiting for transfers between devices  35.1 us (39%)
  starting transfers between devices  33.5 us (38%)
  Pallas kernels  10.2 us (11%)
  local copies, waits for them, and re-layouts  4.33 us (5%)
  other arithmetic  4.33 us (5%)
  between operations  0.97 us (1%)
    ppermute x8, waiting for transfers between devices, along_row(): return lax.ppermute(value, 'row', pairs)  13.4 us
    ppermute x6, starting transfers between devices, along_col(): return lax.ppermute(value, 'col', pairs)  11.8 us
    ppermute x6, waiting for transfers between devices, along_col(): return lax.ppermute(value, 'col', pairs)  11.2 us
    pallas_call x9, Pallas kernels, call(): pl.pallas_call(kernel, out_shape=[jax.ShapeDtypeStruct(shape, F32) for sh...  10.2 us
    ppermute x1, waiting for transfers between devices, central(): near_part = lax.ppermute(part, ('row', 'col'), near)  8.15 us
    ppermute x8, starting transfers between devices, along_row(): return lax.ppermute(value, 'row', pairs)  7.93 us
    ppermute x4, starting transfers between devices, swap(): return lax.ppermute(value, 'leaf', [(0, 1), (1, 0)])  7.44 us
    ppermute x1, starting transfers between devices, central(): far_part = lax.ppermute(part, ('row', 'col'), far)  4.25 us
  transfers between devices with their start and end apart: 20, of which 9 were waited for; matrix products, arithmetic and copies ran while one was open for 0% of the time, Pallas kernels for 5%

profile of v1, /device:TPU:7, one launch (start us, length us, event | category | flops | bytes accessed | tf_op | source)
XLA Modules:
  0.0 88.4 jit_solution(3071001114393532427)
XLA Ops:
  0.6 0.0 copy-start
  0.7 1.2 %constant_dynamic-slice_fusion = f32[256,512]{1,0:T(8,128)S(1)} fusion(f32[512,512]{1,0:T(8,128)} %param.14, s32[]{:T(128)S(6)} %select_n.61), kind=kLoop, calls=%fused_computation.9 | loop fusion | bytes 1048580 | tf_op jit(solution)/shard_map/dynamic_slice | solution.py:211
  1.9 4.2 %collective-permute-start.11 = (f32[256,512]{1,0:T(8,128)S(1)}, f32[256,512]{1,0:T(8,128)S(1)}, u32[]{:S(2)}, u32[]{:S(2)}) collective-permute-start(f32[256,512]{1,0:T(8,128)S(1)} %constant_dynamic-slice_fusion), channel_id=1, source_target_pairs={{4,6},{8,10},{12,14},{14,13},{20,22},{24,26},{28,30},{30,29}} | collective-permute-start | bytes 1572872 | tf_op jit(solution)/shard_map/ppermute | solution.py:215
  6.1 2.1 %collective-permute-start.9 = (f32[256,512]{1,0:T(8,128)S(1)}, f32[256,512]{1,0:T(8,128)}, u32[]{:S(2)}, u32[]{:S(2)}) collective-permute-start(f32[256,512]{1,0:T(8,128)S(1)} %constant_dynamic-slice_fusion), channel_id=1, source_target_pairs={{4,5},{8,9},{12,13},{9,10},{13,14},{20,21},{24,25},{28,29},{25,26}... | collective-permute-start | bytes 1572872 | tf_op jit(solution)/shard_map/ppermute | solution.py:214
  8.2 0.1 pad_add_fusion.where_ref
  8.3 0.6 copy-done.7
  8.9 1.0 %copy-done.6 = f32[2,256,256]{2,1,0:T(8,128)S(1)} copy-done((f32[2,256,256]{2,1,0:T(8,128)S(1)}, f32[2,256,256]{2,1,0:T(8,128)}, u32[]{:S(2)}) %copy-start.6) | copy-done | bytes 524312
  9.9 1.9 %shard_map.95 = (f32[2,256,256]{2,1,0:T(8,128)}, f32[128,512]{1,0:T(8,128)S(1)}, f32[136,512]{1,0:T(8,128)S(1)}) custom-call(s32[3]{0:T(128)S(1)} %pad_add_fusion.where_ref, s32[2]{0:T(128)S(1)} %copy-done.8, f32[2,256,256]{2,1,0:T(8,128)S(1)} %copy-done.4, f32[2,256,256]{2,1,0:T(8,128)S(1)} %copy-done.5, f32[2,256,256]{2,1,0:T(8,128)S(1)} %copy-done.6, ...), custom_call_target="tpu_custom_call" | custom-call | bytes 1574932 | tf_op jit(solution)/shard_map/pallas_call | solution.py:179
  11.9 1.0 %collective-permute-start = (f32[136,512]{1,0:T(8,128)S(1)}, f32[136,512]{1,0:T(8,128)S(1)}, u32[]{:S(2)}, u32[]{:S(2)}) collective-permute-start(f32[136,512]{1,0:T(8,128)S(1)} %get-tuple-element.20), channel_id=1, source_target_pairs={{0,16},{16,0},{1,17},{17,1},{2,18},{18,2},{3,19},{19,3},{4,20},{20... | collective-permute-start | bytes 835592 | tf_op jit(solution)/shard_map/ppermute | solution.py:200
  12.8 1.2 %collective-permute-done.recv_ref = f32[136,512]{1,0:T(8,128)S(1)} collective-permute-done((f32[136,512]{1,0:T(8,128)S(1)}, f32[136,512]{1,0:T(8,128)S(1)}, u32[]{:S(2)}, u32[]{:S(2)}) %collective-permute-start) | collective-permute-done | bytes 278560 | tf_op jit(solution)/shard_map/ppermute | solution.py:200
  14.0 1.8 %shard_map.96 = (f32[128,512]{1,0:T(8,128)S(1)}, f32[128,512]{1,0:T(8,128)S(1)}, f32[128,512]{1,0:T(8,128)S(1)}, f32[128,512]{1,0:T(8,128)S(1)}) custom-call(s32[3]{0:T(128)S(1)} %pad_add_fusion.where_ref, f32[128,512]{1,0:T(8,128)S(1)} %get-tuple-element.19.keep_ref, f32[136,512]{1,0:T(8,128)S(1)} %collective-permute-done.recv_ref, s32[2,256]{1,0:T(2,128)S(1)} %copy-done.7), custom_call_target="tpu_custom_call" | custom-call | bytes 542732 | tf_op jit(solution)/shard_map/pallas_call | solution.py:179
  15.8 0.0 copy-start.1
  15.9 0.3 collective-permute-start.1
  16.2 0.1 collective-permute-start.2
  16.2 2.3 %collective-permute-start.3 = (f32[128,512]{1,0:T(8,128)S(1)}, f32[128,512]{1,0:T(8,128)S(1)}, u32[]{:S(2)}, u32[]{:S(2)}) collective-permute-start(f32[128,512]{1,0:T(8,128)S(1)} %get-tuple-element.24), channel_id=1, source_target_pairs={{0,12},{4,8},{8,4},{12,0},{1,13},{5,9},{9,5},{13,1},{2,14},{6,10},... | collective-permute-start | bytes 786440 | tf_op jit(solution)/shard_map/ppermute | solution.py:203
  18.6 1.2 %collective-permute-start.12 = (f32[256,512]{1,0:T(8,128)S(1)}, f32[256,512]{1,0:T(8,128)}, u32[]{:S(2)}, u32[]{:S(2)}) collective-permute-start(f32[256,512]{1,0:T(8,128)S(1)} %collective-permute-done.11), channel_id=1, source_target_pairs={{0,16},{16,0},{1,17},{17,1},{2,18},{18,2},{3,19},{19,3},{4,20},{20... | collective-permute-start | bytes 1572872 | tf_op jit(solution)/shard_map/ppermute | solution.py:200
  19.8 8.2 %collective-permute-done.9 = f32[256,512]{1,0:T(8,128)} collective-permute-done((f32[256,512]{1,0:T(8,128)S(1)}, f32[256,512]{1,0:T(8,128)}, u32[]{:S(2)}, u32[]{:S(2)}) %collective-permute-start.9) | collective-permute-done | bytes 524320 | tf_op jit(solution)/shard_map/ppermute | solution.py:214
  27.9 1.5 %collective-permute-start.10 = (f32[256,512]{1,0:T(8,128)}, f32[256,512]{1,0:T(8,128)}, u32[]{:S(2)}, u32[]{:S(2)}) collective-permute-start(f32[256,512]{1,0:T(8,128)} %collective-permute-done.9), channel_id=1, source_target_pairs={{0,16},{16,0},{1,17},{17,1},{2,18},{18,2},{3,19},{19,3},{4,20},{20... | collective-permute-start | bytes 1572872 | tf_op jit(solution)/shard_map/ppermute | solution.py:200
  29.5 0.6 shard_map.97
  30.1 5.1 %collective-permute-start.6 = (f32[64,512]{1,0:T(8,128)S(1)}, f32[64,512]{1,0:T(8,128)S(1)}, u32[]{:S(2)}, u32[]{:S(2)}) collective-permute-start(f32[64,512]{1,0:T(8,128)S(1)} %get-tuple-element.25.a_ref), channel_id=1, source_target_pairs={{0,2},{3,1},{4,6},{7,5},{8,10},{11,9},{12,14},{15,13},{16,18},{19,... | collective-permute-start | bytes 393224 | tf_op jit(solution)/shard_map/ppermute | solution.py:206
  35.2 0.7 collective-permute-start.5
  35.9 2.8 %collective-permute-start.4 = (f32[64,512]{1,0:T(8,128)S(1)}, f32[64,512]{1,0:T(8,128)S(1)}, u32[]{:S(2)}, u32[]{:S(2)}) collective-permute-start(f32[64,512]{1,0:T(8,128)S(1)} %get-tuple-element.26), channel_id=1, source_target_pairs={{0,1},{3,2},{4,5},{7,6},{8,9},{11,10},{12,13},{15,14},{16,17},{19,... | collective-permute-start | bytes 393224 | tf_op jit(solution)/shard_map/ppermute | solution.py:206
  38.7 0.1 constant_dynamic-slice_fusion.1
  38.9 0.1 copy.11
  39.0 2.3 %collective-permute-done.4.b_ref = f32[64,512]{1,0:T(8,128)S(1)} collective-permute-done((f32[64,512]{1,0:T(8,128)S(1)}, f32[64,512]{1,0:T(8,128)S(1)}, u32[]{:S(2)}, u32[]{:S(2)}) %collective-permute-start.4) | collective-permute-done | bytes 131104 | tf_op jit(solution)/shard_map/ppermute | solution.py:206
  41.3 0.4 shard_map.98
  41.7 0.7 collective-permute-start.8
  42.4 0.7 collective-permute-start.7
  43.2 4.2 %fusion = (f32[512,512]{1,0:T(8,128)}, f32[512,512]{1,0:T(8,128)S(1)}, f32[512,512]{1,0:T(8,128)}) fusion(f32[512,512]{1,0:T(8,128)} %param.14, f32[256,512]{1,0:T(8,128)S(1)} %collective-permute-done.11, f32[256,512]{1,0:T(8,128)} %collective-permute-done.12, pred[]{:T(512)S(6)} %eq.17, pred[]{:T(512)S(6)} %eq.16, f32[256,512]{1,0:T(8,128)} %collective-permute-done.9, ...), kind=kLoop, calls=%fused_computation.2 | loop fusion | flops 2359296 | bytes 6291458 | tf_op jit(solution)/shard_map/jit(_where)/select_n | solution.py:240
  47.4 0.8 shard_map.99
  48.2 1.3 %collective-permute-start.13 = (f32[64,512]{1,0:T(8,128)S(1)}, f32[64,512]{1,0:T(8,128)S(1)}, u32[]{:S(2)}, u32[]{:S(2)}) collective-permute-start(f32[64,512]{1,0:T(8,128)S(1)} %broadcast_select_fusion.2), channel_id=1, source_target_pairs={{4,8},{8,12},{5,9},{9,13},{6,10},{10,14},{7,11},{11,15},{20,24},{2... | collective-permute-start | bytes 393224 | tf_op jit(solution)/shard_map/ppermute | solution.py:203
  49.5 1.3 %collective-permute-start.14 = (f32[64,512]{1,0:T(8,128)S(1)}, f32[64,512]{1,0:T(8,128)S(1)}, u32[]{:S(2)}, u32[]{:S(2)}) collective-permute-start(f32[64,512]{1,0:T(8,128)S(1)} %get-tuple-element.30), channel_id=1, source_target_pairs={{4,12},{5,13},{6,14},{7,15},{20,28},{21,29},{22,30},{23,31}} | collective-permute-start | bytes 393224 | tf_op jit(solution)/shard_map/ppermute | solution.py:203
  50.8 6.2 %collective-permute-done.13 = f32[64,512]{1,0:T(8,128)S(1)} collective-permute-done((f32[64,512]{1,0:T(8,128)S(1)}, f32[64,512]{1,0:T(8,128)S(1)}, u32[]{:S(2)}, u32[]{:S(2)}) %collective-permute-start.13) | collective-permute-done | bytes 131104 | tf_op jit(solution)/shard_map/ppermute | solution.py:203
  57.1 2.7 %collective-permute-done.14 = f32[64,512]{1,0:T(8,128)S(1)} collective-permute-done((f32[64,512]{1,0:T(8,128)S(1)}, f32[64,512]{1,0:T(8,128)S(1)}, u32[]{:S(2)}, u32[]{:S(2)}) %collective-permute-start.14) | collective-permute-done | bytes 131104 | tf_op jit(solution)/shard_map/ppermute | solution.py:203
  59.8 1.2 %copy-done.2 = f32[512,512]{1,0:T(8,128)S(1)} copy-done((f32[512,512]{1,0:T(8,128)S(1)}, f32[512,512]{1,0:T(8,128)}, u32[]{:S(2)}) %copy-start.2) | copy-done | bytes 1048600
  61.0 1.2 %shard_map.100 = (f32[64,512]{1,0:T(8,128)S(1)}, f32[64,512]{1,0:T(8,128)S(1)}) custom-call(f32[64,512]{1,0:T(8,128)S(1)} %get-tuple-element.29.refs_0_, f32[512,512]{1,0:T(8,128)S(1)} %copy-done.1, f32[64,512]{1,0:T(8,128)S(1)} %get-tuple-element.38.refs_2_, f32[64,512]{1,0:T(8,128)S(1)} %get-tuple-element.37.refs_3_, ...), custom_call_target="tpu_custom_call" | custom-call | bytes 3538944 | tf_op jit(solution)/shard_map/pallas_call | solution.py:179
  62.2 1.3 %collective-permute-start.15 = (f32[64,512]{1,0:T(8,128)S(1)}, f32[64,512]{1,0:T(8,128)S(1)}, u32[]{:S(2)}, u32[]{:S(2)}) collective-permute-start(f32[64,512]{1,0:T(8,128)S(1)} %get-tuple-element.32), channel_id=1, source_target_pairs={{8,12},{9,13},{10,14},{11,15},{24,28},{25,29},{26,30},{27,31}} | collective-permute-start | bytes 393224 | tf_op jit(solution)/shard_map/ppermute | solution.py:203
  63.5 4.4 %collective-permute-done.15.refs_2_ = f32[64,512]{1,0:T(8,128)S(1)} collective-permute-done((f32[64,512]{1,0:T(8,128)S(1)}, f32[64,512]{1,0:T(8,128)S(1)}, u32[]{:S(2)}, u32[]{:S(2)}) %collective-permute-start.15) | collective-permute-done | bytes 131104 | tf_op jit(solution)/shard_map/ppermute | solution.py:203
  67.9 1.3 %shard_map.101 = (f32[64,512]{1,0:T(8,128)}, f32[64,512]{1,0:T(8,128)S(1)}) custom-call(f32[64,512]{1,0:T(8,128)S(1)} %get-tuple-element.31.refs_0_, f32[512,512]{1,0:T(8,128)S(1)} %copy-done.1, f32[64,512]{1,0:T(8,128)S(1)} %collective-permute-done.15.refs_2_, f32[512,512]{1,0:T(8,128)S(1)} %copy-done.3), custom_call_target="tpu_custom_call" | custom-call | bytes 2359296 | tf_op jit(solution)/shard_map/pallas_call | solution.py:179
  69.2 1.3 %collective-permute-start.18 = (f32[64,512]{1,0:T(8,128)S(1)}, f32[64,512]{1,0:T(8,128)S(1)}, u32[]{:S(2)}, u32[]{:S(2)}) collective-permute-start(f32[64,512]{1,0:T(8,128)S(1)} %get-tuple-element.33.x_ref), channel_id=1, source_target_pairs={{1,3},{2,0},{5,7},{6,4},{9,11},{10,8},{13,15},{14,12},{17,19},{18,... | collective-permute-start | bytes 393224 | tf_op jit(solution)/shard_map/ppermute | solution.py:206
  70.5 0.7 collective-permute-start.17
  71.2 1.3 %collective-permute-start.16 = (f32[64,512]{1,0:T(8,128)S(1)}, f32[64,512]{1,0:T(8,128)S(1)}, u32[]{:S(2)}, u32[]{:S(2)}) collective-permute-start(f32[64,512]{1,0:T(8,128)S(1)} %get-tuple-element.33.x_ref), channel_id=1, source_target_pairs={{1,0},{2,3},{5,4},{6,7},{9,8},{10,11},{13,12},{14,15},{17,16},{18,... | collective-permute-start | bytes 393224 | tf_op jit(solution)/shard_map/ppermute | solution.py:206
  72.5 4.0 %collective-permute-done.18.c_ref = f32[64,512]{1,0:T(8,128)S(1)} collective-permute-done((f32[64,512]{1,0:T(8,128)S(1)}, f32[64,512]{1,0:T(8,128)S(1)}, u32[]{:S(2)}, u32[]{:S(2)}) %collective-permute-start.18) | collective-permute-done | bytes 131104 | tf_op jit(solution)/shard_map/ppermute | solution.py:206
  76.5 4.9 %collective-permute-done.16.a_ref = f32[64,512]{1,0:T(8,128)S(1)} collective-permute-done((f32[64,512]{1,0:T(8,128)S(1)}, f32[64,512]{1,0:T(8,128)S(1)}, u32[]{:S(2)}, u32[]{:S(2)}) %collective-permute-start.16) | collective-permute-done | bytes 131104 | tf_op jit(solution)/shard_map/ppermute | solution.py:206
  81.4 0.6 shard_map.102.own_ref
  82.0 3.7 %collective-permute-start.19 = (f32[128,512]{1,0:T(8,128)S(1)}, f32[128,512]{1,0:T(8,128)S(1)}, u32[]{:S(2)}, u32[]{:S(2)}) collective-permute-start(f32[128,512]{1,0:T(8,128)S(1)} %shard_map.102.own_ref), channel_id=1, source_target_pairs={{0,16},{16,0},{1,17},{17,1},{2,18},{18,2},{3,19},{19,3},{4,20},{20... | collective-permute-start | bytes 786440 | tf_op jit(solution)/shard_map/ppermute | solution.py:200
  85.7 1.2 %collective-permute-done.19.other_ref = f32[128,512]{1,0:T(8,128)S(1)} collective-permute-done((f32[128,512]{1,0:T(8,128)S(1)}, f32[128,512]{1,0:T(8,128)S(1)}, u32[]{:S(2)}, u32[]{:S(2)}) %collective-permute-start.19) | collective-permute-done | bytes 262176 | tf_op jit(solution)/shard_map/ppermute | solution.py:200
  86.9 1.5 %shard_map.103 = f32[512,256]{1,0:T(8,128)} custom-call(s32[3]{0:T(128)S(1)} %pad_add_fusion.where_ref, f32[128,512]{1,0:T(8,128)S(1)} %shard_map.102.own_ref, f32[128,512]{1,0:T(8,128)S(1)} %collective-permute-done.19.other_ref), custom_call_target="tpu_custom_call" | custom-call | bytes 524300 | tf_op jit(solution)/shard_map/pallas_call | solution.py:179
  (27 shorter events, 0.1 us)
Async XLA Ops:
  0.6 38.1 %copy-start = (f32[512,256]{1,0:T(8,128)S(1)}, f32[512,256]{1,0:T(8,128)}, u32[]{:S(2)}) copy-start(f32[512,256]{1,0:T(8,128)} %param.13) | copy-start | bytes 1572868
  0.7 7.7 %copy-start.4 = (f32[2,256,256]{2,1,0:T(8,128)S(1)}, f32[2,256,256]{2,1,0:T(8,128)}, u32[]{:S(2)}) copy-start(f32[2,256,256]{2,1,0:T(8,128)} %rhs_ref.1) | copy-start | bytes 1572868
  0.7 7.6 %copy-start.5 = (f32[2,256,256]{2,1,0:T(8,128)S(1)}, f32[2,256,256]{2,1,0:T(8,128)}, u32[]{:S(2)}) copy-start(f32[2,256,256]{2,1,0:T(8,128)} %diag_ref.2) | copy-start | bytes 1572868
  1.9 16.7 %collective-permute-start.11 = (f32[256,512]{1,0:T(8,128)S(1)}, f32[256,512]{1,0:T(8,128)S(1)}, u32[]{:S(2)}, u32[]{:S(2)}) collective-permute-start(f32[256,512]{1,0:T(8,128)S(1)} %constant_dynamic-slice_fusion), channel_id=1, source_target_pairs={{4,6},{8,10},{12,14},{14,13},{20,22},{24,26},{28,30},{30,29}} | collective-permute-start | bytes 1572872 | tf_op jit(solution)/shard_map/ppermute | solution.py:215
  6.1 21.8 %collective-permute-start.9 = (f32[256,512]{1,0:T(8,128)S(1)}, f32[256,512]{1,0:T(8,128)}, u32[]{:S(2)}, u32[]{:S(2)}) collective-permute-start(f32[256,512]{1,0:T(8,128)S(1)} %constant_dynamic-slice_fusion), channel_id=1, source_target_pairs={{4,5},{8,9},{12,13},{9,10},{13,14},{20,21},{24,25},{28,29},{25,26}... | collective-permute-start | bytes 1572872 | tf_op jit(solution)/shard_map/ppermute | solution.py:214
  8.2 0.7 copy-start.7
  8.2 0.7 copy-start.8
  8.9 1.0 %copy-start.6 = (f32[2,256,256]{2,1,0:T(8,128)S(1)}, f32[2,256,256]{2,1,0:T(8,128)}, u32[]{:S(2)}) copy-start(f32[2,256,256]{2,1,0:T(8,128)} %off_ref.1) | copy-start | bytes 1572868
  11.9 2.1 %collective-permute-start = (f32[136,512]{1,0:T(8,128)S(1)}, f32[136,512]{1,0:T(8,128)S(1)}, u32[]{:S(2)}, u32[]{:S(2)}) collective-permute-start(f32[136,512]{1,0:T(8,128)S(1)} %get-tuple-element.20), channel_id=1, source_target_pairs={{0,16},{16,0},{1,17},{17,1},{2,18},{18,2},{3,19},{19,3},{4,20},{20... | collective-permute-start | bytes 835592 | tf_op jit(solution)/shard_map/ppermute | solution.py:200
  15.8 25.4 %copy-start.1 = (f32[512,512]{1,0:T(8,128)S(1)}, f32[512,512]{1,0:T(8,128)}, u32[]{:S(2)}) copy-start(f32[512,512]{1,0:T(8,128)} %refs_1_.5) | copy-start | bytes 3145732
  15.9 13.6 %collective-permute-start.1 = (f32[128,512]{1,0:T(8,128)S(1)}, f32[128,512]{1,0:T(8,128)S(1)}, u32[]{:S(2)}, u32[]{:S(2)}) collective-permute-start(f32[128,512]{1,0:T(8,128)S(1)} %get-tuple-element.22), channel_id=1, source_target_pairs={{0,4},{4,0},{8,12},{12,8},{1,5},{5,1},{9,13},{13,9},{2,6},{6,2},{1... | collective-permute-start | bytes 786440 | tf_op jit(solution)/shard_map/ppermute | solution.py:203
  16.2 13.3 %collective-permute-start.2 = (f32[128,512]{1,0:T(8,128)S(1)}, f32[128,512]{1,0:T(8,128)S(1)}, u32[]{:S(2)}, u32[]{:S(2)}) collective-permute-start(f32[128,512]{1,0:T(8,128)S(1)} %get-tuple-element.23), channel_id=1, source_target_pairs={{0,8},{4,12},{8,0},{12,4},{1,9},{5,13},{9,1},{13,5},{2,10},{6,14},... | collective-permute-start | bytes 786440 | tf_op jit(solution)/shard_map/ppermute | solution.py:203
  16.2 13.3 %collective-permute-start.3 = (f32[128,512]{1,0:T(8,128)S(1)}, f32[128,512]{1,0:T(8,128)S(1)}, u32[]{:S(2)}, u32[]{:S(2)}) collective-permute-start(f32[128,512]{1,0:T(8,128)S(1)} %get-tuple-element.24), channel_id=1, source_target_pairs={{0,12},{4,8},{8,4},{12,0},{1,13},{5,9},{9,5},{13,1},{2,14},{6,10},... | collective-permute-start | bytes 786440 | tf_op jit(solution)/shard_map/ppermute | solution.py:203
  18.6 24.6 %collective-permute-start.12 = (f32[256,512]{1,0:T(8,128)S(1)}, f32[256,512]{1,0:T(8,128)}, u32[]{:S(2)}, u32[]{:S(2)}) collective-permute-start(f32[256,512]{1,0:T(8,128)S(1)} %collective-permute-done.11), channel_id=1, source_target_pairs={{0,16},{16,0},{1,17},{17,1},{2,18},{18,2},{3,19},{19,3},{4,20},{20... | collective-permute-start | bytes 1572872 | tf_op jit(solution)/shard_map/ppermute | solution.py:200
  27.9 15.2 %collective-permute-start.10 = (f32[256,512]{1,0:T(8,128)}, f32[256,512]{1,0:T(8,128)}, u32[]{:S(2)}, u32[]{:S(2)}) collective-permute-start(f32[256,512]{1,0:T(8,128)} %collective-permute-done.9), channel_id=1, source_target_pairs={{0,16},{16,0},{1,17},{17,1},{2,18},{18,2},{3,19},{19,3},{4,20},{20... | collective-permute-start | bytes 1572872 | tf_op jit(solution)/shard_map/ppermute | solution.py:200
  30.1 8.9 %collective-permute-start.6 = (f32[64,512]{1,0:T(8,128)S(1)}, f32[64,512]{1,0:T(8,128)S(1)}, u32[]{:S(2)}, u32[]{:S(2)}) collective-permute-start(f32[64,512]{1,0:T(8,128)S(1)} %get-tuple-element.25.a_ref), channel_id=1, source_target_pairs={{0,2},{3,1},{4,6},{7,5},{8,10},{11,9},{12,14},{15,13},{16,18},{19,... | collective-permute-start | bytes 393224 | tf_op jit(solution)/shard_map/ppermute | solution.py:206
  35.2 3.8 %collective-permute-start.5 = (f32[64,512]{1,0:T(8,128)S(1)}, f32[64,512]{1,0:T(8,128)S(1)}, u32[]{:S(2)}, u32[]{:S(2)}) collective-permute-start(f32[64,512]{1,0:T(8,128)S(1)} %get-tuple-element.26), channel_id=1, source_target_pairs={{1,2},{2,1},{5,6},{6,5},{9,10},{10,9},{13,14},{14,13},{17,18},{18,... | collective-permute-start | bytes 393224 | tf_op jit(solution)/shard_map/ppermute | solution.py:206
  35.9 5.4 %collective-permute-start.4 = (f32[64,512]{1,0:T(8,128)S(1)}, f32[64,512]{1,0:T(8,128)S(1)}, u32[]{:S(2)}, u32[]{:S(2)}) collective-permute-start(f32[64,512]{1,0:T(8,128)S(1)} %get-tuple-element.26), channel_id=1, source_target_pairs={{0,1},{3,2},{4,5},{7,6},{8,9},{11,10},{12,13},{15,14},{16,17},{19,... | collective-permute-start | bytes 393224 | tf_op jit(solution)/shard_map/ppermute | solution.py:206
  41.7 1.4 %collective-permute-start.8 = (f32[64,512]{1,0:T(8,128)S(1)}, f32[64,512]{1,0:T(8,128)S(1)}, u32[]{:S(2)}, u32[]{:S(2)}) collective-permute-start(f32[64,512]{1,0:T(8,128)S(1)} %get-tuple-element.28), channel_id=1, source_target_pairs={{0,8},{1,9},{2,10},{3,11},{16,24},{17,25},{18,26},{19,27}} | collective-permute-start | bytes 393224 | tf_op jit(solution)/shard_map/ppermute | solution.py:203
  42.4 0.7 collective-permute-start.7
  48.2 8.8 %collective-permute-start.13 = (f32[64,512]{1,0:T(8,128)S(1)}, f32[64,512]{1,0:T(8,128)S(1)}, u32[]{:S(2)}, u32[]{:S(2)}) collective-permute-start(f32[64,512]{1,0:T(8,128)S(1)} %broadcast_select_fusion.2), channel_id=1, source_target_pairs={{4,8},{8,12},{5,9},{9,13},{6,10},{10,14},{7,11},{11,15},{20,24},{2... | collective-permute-start | bytes 393224 | tf_op jit(solution)/shard_map/ppermute | solution.py:203
  49.5 10.3 %collective-permute-start.14 = (f32[64,512]{1,0:T(8,128)S(1)}, f32[64,512]{1,0:T(8,128)S(1)}, u32[]{:S(2)}, u32[]{:S(2)}) collective-permute-start(f32[64,512]{1,0:T(8,128)S(1)} %get-tuple-element.30), channel_id=1, source_target_pairs={{4,12},{5,13},{6,14},{7,15},{20,28},{21,29},{22,30},{23,31}} | collective-permute-start | bytes 393224 | tf_op jit(solution)/shard_map/ppermute | solution.py:203
  59.8 1.2 %copy-start.2 = (f32[512,512]{1,0:T(8,128)S(1)}, f32[512,512]{1,0:T(8,128)}, u32[]{:S(2)}) copy-start(f32[512,512]{1,0:T(8,128)} %get-tuple-element.36.refs_5_) | copy-start | bytes 3145732
  61.0 6.9 %copy-start.3 = (f32[512,512]{1,0:T(8,128)S(1)}, f32[512,512]{1,0:T(8,128)}, u32[]{:S(2)}) copy-start(f32[512,512]{1,0:T(8,128)} %get-tuple-element.34.refs_3_) | copy-start | bytes 3145732
  62.2 5.7 %collective-permute-start.15 = (f32[64,512]{1,0:T(8,128)S(1)}, f32[64,512]{1,0:T(8,128)S(1)}, u32[]{:S(2)}, u32[]{:S(2)}) collective-permute-start(f32[64,512]{1,0:T(8,128)S(1)} %get-tuple-element.32), channel_id=1, source_target_pairs={{8,12},{9,13},{10,14},{11,15},{24,28},{25,29},{26,30},{27,31}} | collective-permute-start | bytes 393224 | tf_op jit(solution)/shard_map/ppermute | solution.py:203
  69.2 7.3 %collective-permute-start.18 = (f32[64,512]{1,0:T(8,128)S(1)}, f32[64,512]{1,0:T(8,128)S(1)}, u32[]{:S(2)}, u32[]{:S(2)}) collective-permute-start(f32[64,512]{1,0:T(8,128)S(1)} %get-tuple-element.33.x_ref), channel_id=1, source_target_pairs={{1,3},{2,0},{5,7},{6,4},{9,11},{10,8},{13,15},{14,12},{17,19},{18,... | collective-permute-start | bytes 393224 | tf_op jit(solution)/shard_map/ppermute | solution.py:206
  70.5 6.0 %collective-permute-start.17 = (f32[64,512]{1,0:T(8,128)S(1)}, f32[64,512]{1,0:T(8,128)S(1)}, u32[]{:S(2)}, u32[]{:S(2)}) collective-permute-start(f32[64,512]{1,0:T(8,128)S(1)} %get-tuple-element.33.x_ref), channel_id=1, source_target_pairs={{1,2},{2,1},{5,6},{6,5},{9,10},{10,9},{13,14},{14,13},{17,18},{18,... | collective-permute-start | bytes 393224 | tf_op jit(solution)/shard_map/ppermute | solution.py:206
  71.2 10.2 %collective-permute-start.16 = (f32[64,512]{1,0:T(8,128)S(1)}, f32[64,512]{1,0:T(8,128)S(1)}, u32[]{:S(2)}, u32[]{:S(2)}) collective-permute-start(f32[64,512]{1,0:T(8,128)S(1)} %get-tuple-element.33.x_ref), channel_id=1, source_target_pairs={{1,0},{2,3},{5,4},{6,7},{9,8},{10,11},{13,12},{14,15},{17,16},{18,... | collective-permute-start | bytes 393224 | tf_op jit(solution)/shard_map/ppermute | solution.py:206
  82.0 4.9 %collective-permute-start.19 = (f32[128,512]{1,0:T(8,128)S(1)}, f32[128,512]{1,0:T(8,128)S(1)}, u32[]{:S(2)}, u32[]{:S(2)}) collective-permute-start(f32[128,512]{1,0:T(8,128)S(1)} %shard_map.102.own_ref), channel_id=1, source_target_pairs={{0,16},{16,0},{1,17},{17,1},{2,18},{18,2},{3,19},{19,3},{4,20},{20... | collective-permute-start | bytes 786440 | tf_op jit(solution)/shard_map/ppermute | solution.py:200

commit v2 on v1

v2 whole, which is shorter than its diff:
```python
import functools

import jax
import jax.numpy as jnp
from jax import lax
from jax.experimental import pallas as pl
from jax.experimental.pallas import tpu as pltpu
from jax.sharding import PartitionSpec as P

F32 = jnp.float32
BF16 = jnp.bfloat16
NT = (((1,), (1,)), ((), ()))
NN = (((1,), (0,)), ((), ()))
VM = pl.BlockSpec(memory_space=pltpu.VMEM)
SM = pl.BlockSpec(memory_space=pltpu.SMEM)


def spread(value, axis, source):
    kept = jnp.where(lax.axis_index(axis) == source, value, 0).astype(value.dtype)
    return lax.psum(kept, axis)


def unit_lower(matrix):
    return jnp.tril(matrix) + jnp.eye(matrix.shape[-1], dtype=matrix.dtype)


def any_mesh(child_rhs, child_diag, child_off, live, targets, top_rhs, top_factor, top_diag):
    highest = lax.Precision.HIGHEST
    owned_rows = top_rhs.shape[0]
    right_count = top_rhs.shape[1]
    block_size = top_diag.shape[1]
    owned_blocks = owned_rows // block_size
    row_count = lax.axis_size("row")
    top_order = owned_rows * row_count
    col_width = top_factor.shape[1]
    my_row = lax.axis_index("row")
    my_col = lax.axis_index("col")
    child_sol = jnp.einsum("bij,bjr->bir", unit_lower(child_diag), child_rhs, precision=highest)
    tiles = jnp.einsum("btj,bjr->btr", child_off, child_sol, precision=highest)
    slot_index = jnp.arange(child_off.shape[1], dtype=jnp.int32)
    keep = slot_index[None, :] < live[:, None]
    tiles = jnp.where(keep[:, :, None], tiles, jnp.zeros_like(tiles))
    contrib = jnp.zeros((top_order, right_count), F32)
    contrib = contrib.at[targets.reshape(-1)].add(tiles.reshape(-1, right_count))
    row_part = lax.psum_scatter(contrib, "row", scatter_dimension=0, tiled=True)
    share = lax.psum_scatter(row_part, ("leaf", "col"), scatter_dimension=0, tiled=True)
    updates = lax.all_gather(share, ("leaf", "col"), axis=0, tiled=True)
    reduced = top_rhs - updates
    inverse_all = unit_lower(top_diag.reshape(owned_blocks, block_size, block_size))
    col_global = my_col * col_width + jnp.arange(col_width, dtype=jnp.int32)

    def step(block, solution):
        local = block % owned_blocks
        owner = block // owned_blocks
        factor_rows = jnp.where(
            (col_global < block * block_size)[None, :], top_factor, jnp.zeros_like(top_factor)
        )
        columns = lax.dynamic_slice_in_dim(solution, my_col * col_width, col_width, 0)
        partial_value = jnp.dot(
            factor_rows, columns, precision=highest, preferred_element_type=F32
        )
        block_inverse = lax.dynamic_index_in_dim(inverse_all, local, 0, keepdims=False)
        before = lax.psum(partial_value, "col")
        solved = jnp.dot(
            block_inverse, reduced - before, precision=highest, preferred_element_type=F32
        )
        solved = spread(solved, "row", owner)
        return lax.dynamic_update_slice_in_dim(solution, solved, block * block_size, 0)

    solution = lax.fori_loop(
        0, row_count * owned_blocks, step, jnp.zeros((top_order, right_count), F32)
    )
    top_sol = lax.dynamic_slice_in_dim(solution, my_row * owned_rows, owned_rows, 0)
    return (child_sol, top_sol)


def split(value):
    high = value.astype(BF16)
    return high, (value - high.astype(F32)).astype(BF16)


def dot3(left, right, dims):
    left_high, left_low = split(left)
    right_high, right_low = split(right)
    rows = left.shape[0]
    both = lax.dot_general(
        jnp.concatenate([left_high, left_low], axis=0), right_high, dims, preferred_element_type=F32
    )
    cross = lax.dot_general(left_high, right_low, dims, preferred_element_type=F32)
    return both[:rows] + both[rows:] + cross


def lower(matrix, first_row=0):
    row = lax.broadcasted_iota(jnp.int32, matrix.shape, 0) + first_row
    col = lax.broadcasted_iota(jnp.int32, matrix.shape, 1)
    return jnp.where(col <= row, matrix, 0.0)


def pack_kernel(where_ref, factor_ref, diag_ref, rhs_ref, out_ref, turned_ref):
    leaf, row, z = where_ref[0], where_ref[1], where_ref[2]
    part = factor_ref.shape[0] // 2
    half = rhs_ref.shape[1] // 2
    piece = half // 2
    mine = pl.ds(pl.multiple_of(leaf * part, part), part)

    @pl.when(row == 0)
    def _():
        out_ref[0:part, :] = diag_ref[mine, :]

    @pl.when(row != 0)
    def _():
        out_ref[0:part, :] = factor_ref[mine, :]

    turned_ref[...] = rhs_ref[:, pl.ds(pl.multiple_of(leaf * half, half), half)].T
    out_ref[part:part + piece, :] = turned_ref[pl.ds(pl.multiple_of((z // 2) * piece, piece), piece), :]


def child_kernel(live_ref, rhs_ref, diag_ref, off_ref, tgt_ref, sol_ref, send_ref):
    children, slots = off_ref.shape[0], off_ref.shape[1]
    right = rhs_ref.shape[2]
    groups = send_ref.shape[0]
    lanes = send_ref.shape[2]
    width = right // groups
    rows = groups // 2
    tiles_each = slots // lanes
    count = children * tiles_each
    for s in range(children):
        rhs = rhs_ref[s]
        sol = rhs + dot3(lower(diag_ref[s]), rhs, NN)
        sol_ref[s] = sol
        tiles = dot3(sol.T, off_ref[s], NT)
        slot = lax.broadcasted_iota(jnp.int32, tiles.shape, 1)
        tiles = jnp.where(slot < live_ref[s], tiles, 0.0)
        for g in range(groups):
            leaf, row = g // rows, g % rows
            for h in range(2):
                start = leaf * (right // 2) + h * (right // 4) + row * (width // 2)
                for t in range(tiles_each):
                    at = (s * tiles_each + t) * width + h * (width // 2)
                    send_ref[g, at:at + width // 2, :] = tiles[
                        start:start + width // 2, t * lanes:(t + 1) * lanes
                    ]
    target = jnp.concatenate(
        [tgt_ref[s:s + 1, t * lanes:(t + 1) * lanes] for s in range(children) for t in range(tiles_each)]
        + [jnp.zeros((send_ref.shape[1] - count * width - count, lanes), jnp.int32)],
        axis=0,
    ).astype(F32)
    for g in range(groups):
        send_ref[g, count * width:, :] = target


def scatter_kernel(blocks, where_ref, recv_ref, first_ref, second_ref, sum_ref):
    odd = where_ref[2] % 2
    groups, lanes = recv_ref.shape[0], recv_ref.shape[2]
    width = sum_ref.shape[0]
    size = sum_ref.shape[1] // blocks
    piece = first_ref.shape[0]
    count = (recv_ref.shape[1] - 1) // width
    total = None
    for g in range(groups):
        lefts, targets = [], []
        for t in range(count):
            target = recv_ref[g, count * width + t:count * width + t + 1, :].astype(jnp.int32)
            value = recv_ref[g, t * width:(t + 1) * width, :]
            parts = []
            for b in range(blocks):
                inside = (target >= b * size) & (target < (b + 1) * size)
                parts.append(jnp.where(inside, value, 0.0))
            lefts.append(jnp.concatenate(parts, axis=0))
            targets.append(target)
        left = jnp.concatenate(lefts, axis=1)
        target = jnp.concatenate(targets, axis=1)
        within = target
        for b in range(1, blocks):
            within = jnp.where(target >= b * size, target - b * size, within)
        index = lax.broadcasted_iota(jnp.int32, (size, count * lanes), 0)
        hot = jnp.where(index == within, 1.0, 0.0).astype(BF16)
        high, low = split(left)
        product = lax.dot_general(
            jnp.concatenate([high, low], axis=0), hot, NT, preferred_element_type=F32
        )
        total = product if total is None else total + product
    total = total[:blocks * width] + total[blocks * width:]
    for b in range(blocks):
        sum_ref[:, b * size:(b + 1) * size] = total[b * width:(b + 1) * width]
    first_ref[...] = sum_ref[pl.ds(pl.multiple_of(odd * piece, piece), piece), :]
    second_ref[...] = sum_ref[pl.ds(pl.multiple_of((1 - odd) * piece, piece), piece), :]


def add_kernel(a_ref, b_ref, c_ref, d_ref, out_ref):
    out_ref[...] = (a_ref[...] + b_ref[...]) + (c_ref[...] + d_ref[...])


def halves(x, mine_ref, other_ref, leaf, out_ref, tri=False):
    part = out_ref.shape[1] // 2
    for ref, at in ((mine_ref, leaf), (other_ref, 1 - leaf)):
        start = pl.multiple_of(at * part, part)
        block = ref[0:part, :]
        if tri:
            block = lower(block, start)
        out_ref[:, pl.ds(start, part)] = dot3(x, block, NT)
    return out_ref[...]


def first_kernel(where_ref, pack_ref, a_ref, b_ref, c_ref, d_ref, diag_ref, nm_ref, no_ref, fm_ref, fo_ref,
                 res_ref, x_ref, sum_ref, tmp_ref):
    leaf, row, z = where_ref[0], where_ref[1], where_ref[2]
    size = diag_ref.shape[0]
    part = size // 2
    piece = a_ref.shape[0]
    for s, ref in enumerate((a_ref, b_ref, c_ref, d_ref)):
        at = jnp.bitwise_xor(row, s) * piece
        sum_ref[pl.ds(pl.multiple_of(at, piece), piece), :] = ref[...]
    res = pack_ref[part:, :] - sum_ref[:, pl.ds(pl.multiple_of(row * size, size), size)]
    res_ref[...] = res
    x_ref[...] = res

    def solve(value):
        x_ref[...] = value + dot3(value, lower(diag_ref[...]), NT)

    @pl.when(row == 0)
    def _():
        solve(res)

    def both(factor_mine, factor_other, diag_mine, diag_other):
        before = diag_mine[part:, :] - sum_ref[:, 0:size]
        x0 = before + halves(before, diag_mine, diag_other, leaf, tmp_ref, tri=True)
        solve(res_ref[...] - halves(x0, factor_mine, factor_other, leaf, tmp_ref))

    @pl.when((row == 1) & (z == 1))
    def _():
        both(nm_ref, no_ref, fm_ref, fo_ref)

    @pl.when((row == 1) & (z == 2))
    def _():
        both(fm_ref, fo_ref, nm_ref, no_ref)


def earlier(res, x0, x1, leaf, z, refs, out_ref, tmp_ref):
    factor_ref, nm_ref, no_ref, fm_ref, fo_ref = refs

    @pl.when(z == 1)
    def _():
        value = res - halves(x0, nm_ref, no_ref, leaf, tmp_ref)
        out_ref[...] = value - dot3(x1, factor_ref[...], NT)

    @pl.when(z == 2)
    def _():
        value = res - halves(x0, fm_ref, fo_ref, leaf, tmp_ref)
        out_ref[...] = value - halves(x1, nm_ref, no_ref, leaf, tmp_ref)


def second_kernel(where_ref, res_ref, x_ref, diag_ref, hb_ref, ha_ref, factor_ref, nm_ref, no_ref, fm_ref, fo_ref,
                  out_ref, left_ref, tmp_ref):
    leaf, row, z = where_ref[0], where_ref[1], where_ref[2]
    out_ref[...] = x_ref[...]

    @pl.when((row == 2) & ((z == 1) | (z == 2)))
    def _():
        refs = (factor_ref, nm_ref, no_ref, fm_ref, fo_ref)
        earlier(res_ref[...], ha_ref[...], hb_ref[...], leaf, z, refs, left_ref, tmp_ref)
        value = left_ref[...]
        out_ref[...] = value + dot3(value, lower(diag_ref[...]), NT)


def third_kernel(where_ref, res_ref, hb_ref, ha_ref, factor_ref, nm_ref, no_ref, fm_ref, fo_ref, out_ref, tmp_ref):
    leaf, row, z = where_ref[0], where_ref[1], where_ref[2]
    out_ref[...] = res_ref[...]

    @pl.when(row == 3)
    def _():
        refs = (factor_ref, nm_ref, no_ref, fm_ref, fo_ref)
        earlier(res_ref[...], hb_ref[...], ha_ref[...], leaf, z, refs, out_ref, tmp_ref)


def fourth_kernel(where_ref, res_ref, x_ref, diag_ref, h_ref, factor_ref, fm_ref, fo_ref, out_ref, left_ref, tmp_ref):
    leaf, row, z = where_ref[0], where_ref[1], where_ref[2]
    out_ref[...] = x_ref[...]

    @pl.when((row == 3) & ((z == 1) | (z == 2)))
    def _():
        @pl.when(z == 1)
        def _():
            left_ref[...] = res_ref[...] - halves(h_ref[...], fm_ref, fo_ref, leaf, tmp_ref)

        @pl.when(z == 2)
        def _():
            left_ref[...] = res_ref[...] - dot3(h_ref[...], factor_ref[...], NT)

        value = left_ref[...]
        out_ref[...] = value + dot3(value, lower(diag_ref[...]), NT)


def half_kernel(where_ref, x_ref, a_ref, b_ref, c_ref, out_ref):
    z = where_ref[2]
    x, a, b, c = x_ref[...], a_ref[...], b_ref[...], c_ref[...]
    low = jnp.where(z == 0, a, jnp.where(z == 1, x, jnp.where(z == 2, b, c)))
    high = jnp.where(z == 0, c, jnp.where(z == 1, b, jnp.where(z == 2, x, a)))
    out_ref[...] = jnp.concatenate([low, high], axis=0).T


def last_kernel(where_ref, own_ref, other_ref, out_ref):
    leaf = where_ref[0]
    half = own_ref.shape[1]
    own, other = own_ref[...], other_ref[...]
    out_ref[:, 0:half] = jnp.where(leaf == 0, own, other)
    out_ref[:, half:2 * half] = jnp.where(leaf == 0, other, own)


def call(kernel, ins, outs, scratch=(), flops=0):
    return pl.pallas_call(
        kernel,
        out_shape=[jax.ShapeDtypeStruct(shape, F32) for shape in outs],
        in_specs=[SM if a.ndim == 1 else VM for a in ins],
        out_specs=[VM] * len(outs),
        scratch_shapes=[pltpu.VMEM(shape, F32) for shape in scratch],
        cost_estimate=pl.CostEstimate(
            flops=flops, bytes_accessed=4 * sum(a.size for a in ins), transcendentals=0
        ),
        compiler_params=pltpu.CompilerParams(vmem_limit_bytes=40 * 1024 * 1024),
    )(*ins)


def central(child_rhs, child_diag, child_off, live, targets, top_rhs, top_factor, top_diag):
    leaf, row, col = (lax.axis_index(a) for a in ("leaf", "row", "col"))
    where = jnp.stack([leaf, row, col]).astype(jnp.int32)
    rows, cols = lax.axis_size("row"), lax.axis_size("col")
    size = top_diag.shape[1]
    right = top_rhs.shape[1]
    half, piece = right // 2, right // 4
    children, slots = targets.shape
    lanes = 128
    groups = 2 * rows
    width = right // groups

    def at(r, c):
        return r * cols + c

    def swap(value):
        return lax.ppermute(value, "leaf", [(0, 1), (1, 0)])

    def plane(value, pairs):
        return lax.ppermute(value, ("row", "col"), pairs)

    def hop(value, pairs):
        return plane(value, [(at(a, z), at(b, z)) for a, b in pairs for z in (1, 2)])

    def along_col(value, pairs):
        return lax.ppermute(value, "col", pairs)

    (pack,) = call(
        pack_kernel, [where, top_factor, top_diag, top_rhs], [(size // 2 + piece, size)], [(half, size)]
    )
    near = plane(
        pack,
        [(at(k, 0), at(k, 1)) for k in (1, 2, 3)]
        + [(at(k, 1), at(k, 2)) for k in (2, 3)]
        + [(at(0, 2), at(1, 2))],
    )
    far = plane(
        pack, [(at(k, 0), at(k, 2)) for k in (1, 2, 3)] + [(at(3, 2), at(3, 1)), (at(0, 1), at(1, 1))]
    )

    tiles = children * slots // lanes
    child_sol, send = call(
        child_kernel,
        [live, child_rhs, child_diag, child_off, targets],
        [child_rhs.shape, (groups, tiles * width + 8 * pl.cdiv(tiles, 8), lanes)],
    )
    recv = lax.all_to_all(send, ("leaf", "row"), 0, 0, tiled=True)
    first, second = call(
        functools.partial(scatter_kernel, rows),
        [where, recv],
        [(width // 2, rows * size)] * 2,
        [(width, rows * size)],
    )
    q = [
        along_col(first, [(0, 1), (3, 2)]),
        along_col(first, [(1, 2), (2, 1)]),
        along_col(second, [(0, 2), (3, 1)]),
    ]
    (sums,) = call(add_kernel, [second] + q, [second.shape])
    got = [hop(sums, [(i, i ^ s) for i in range(rows)]) for s in (1, 2, 3)]
    moved = [near, swap(near), far, swap(far)]

    shape = (piece, size)
    res, x = call(
        first_kernel,
        [where, pack, sums] + got + [top_diag] + moved,
        [shape] * 2,
        [(piece, rows * size), shape],
    )
    hb = hop(x, [(1, 2), (0, 3)])
    ha = hop(x, [(0, 2), (1, 3)])
    (x,) = call(
        second_kernel, [where, res, x, top_diag, hb, ha, top_factor] + moved, [shape], [shape] * 2
    )
    h = hop(x, [(2, 3)])
    (res,) = call(third_kernel, [where, res, hb, ha, top_factor] + moved, [shape], [shape])
    (x,) = call(
        fourth_kernel, [where, res, x, top_diag, h, top_factor] + moved[2:], [shape], [shape] * 2
    )
    z = [
        along_col(x, [(1, 0), (2, 3)]),
        along_col(x, [(1, 2), (2, 1)]),
        along_col(x, [(1, 3), (2, 0)]),
    ]
    (own,) = call(half_kernel, [where, x] + z, [(size, half)])
    (top_sol,) = call(last_kernel, [where, own, swap(own)], [top_rhs.shape])
    return (child_sol, top_sol)


def solution(mesh):
    in_specs = (
        P(("leaf", "row", "col"), None, None),
        P(("leaf", "row", "col"), None, None),
        P(("leaf", "row", "col"), None, None),
        P(("leaf", "row", "col")),
        P(("leaf", "row", "col"), None),
        P("row", None),
        P("row", "col"),
        P("row", None),
    )
    out_specs = (P(("leaf", "row", "col"), None, None), P("row", None))
    axes = tuple(mesh.shape[a] for a in ("leaf", "row", "col"))

    def shards(*args):
        top_rhs, top_factor, top_diag = args[5:]
        size = top_diag.shape[1]
        fits = axes == (2, 4, 4) and top_rhs.shape[0] == size and top_factor.shape[1] == size
        return (central if fits else any_mesh)(*args)

    return jax.shard_map(shards, mesh=mesh, in_specs=in_specs, out_specs=out_specs, check_vma=False)
```

time: 88.9 us -> 101 us (1.14)
  waiting for transfers between devices: 35.1 us -> 47.4 us
  other arithmetic: 4.33 us -> 0.08 us
  starting transfers between devices: 33.5 us -> 36.3 us
    ppermute x6, waiting for transfers between devices: 11.2 us -> 31.5 us  [along_col(): return lax.ppermute(value, 'col', pairs)]
    ppermute x10 -> x8, waiting for transfers between devices: 21.5 us -> 14.8 us  [plane(): return lax.ppermute(value, ('row', 'col'), pairs)]
    all_to_all x0 -> x1, starting transfers between devices: none -> 4.92 us  [central(): recv = lax.all_to_all(send, ('leaf', 'row'), 0, 0, tiled=True)]
    ppermute x10 -> x8, starting transfers between devices: 14.3 us -> 9.69 us  [plane(): return lax.ppermute(value, ('row', 'col'), pairs)]
    select_n x3 -> x0, other arithmetic: 4.23 us -> none  [the longest x1 4.19 us: central(): factor2 = jnp.where(col == 1, far_whole, top_factor)]
    ppermute x4 -> x3, starting transfers between devices: 7.44 us -> 10.1 us  [swap(): return lax.ppermute(value, 'leaf', [(0, 1), (1, 0)])]
    dynamic_slice x2 -> x0, local copies, waits for them, and re-layouts: 1.33 us -> none  [the longest x1 1.19 us: central(): lax.dynamic_slice_in_dim(top_factor, leaf * (size // 2), size // 2, 0)]
    unnamed x19 -> x26, local copies, waits for them, and re-layouts: 3 us -> 4.33 us
  transfers between devices with their start and end apart: 20 -> 18, of which waited for: 9 -> 6; matrix products, arithmetic and copies ran while one was open for 0% -> 0% of each run, Pallas kernels for 5% -> 6%
where the time goes in v2:
time: 101 us; the launch traced here: 100 us
  waiting for transfers between devices  47.4 us (47%)
  starting transfers between devices  36.3 us (36%)
  Pallas kernels  11.2 us (11%)
  local copies, waits for them, and re-layouts  4.33 us (4%)
    ppermute x6, waiting for transfers between devices, along_col(): return lax.ppermute(value, 'col', pairs)  31.5 us
    ppermute x8, waiting for transfers between devices, plane(): return lax.ppermute(value, ('row', 'col'), pairs)  14.8 us
    ppermute x6, starting transfers between devices, along_col(): return lax.ppermute(value, 'col', pairs)  11.6 us
    pallas_call x10, Pallas kernels, call(): pl.pallas_call(kernel, out_shape=[jax.ShapeDtypeStruct(shape, F32) for sh...  11.2 us
    ppermute x3, starting transfers between devices, swap(): return lax.ppermute(value, 'leaf', [(0, 1), (1, 0)])  10.1 us
    ppermute x8, starting transfers between devices, plane(): return lax.ppermute(value, ('row', 'col'), pairs)  9.69 us
    all_to_all x1, starting transfers between devices, central(): recv = lax.all_to_all(send, ('leaf', 'row'), 0, 0, tiled=True)  4.92 us
    unnamed x26, local copies, waits for them, and re-layouts  4.33 us
  transfers between devices with their start and end apart: 18, of which 6 were waited for; matrix products, arithmetic and copies ran while one was open for 0% of the time, Pallas kernels for 6%

profile of v2, /device:TPU:7, one launch (start us, length us, event | category | flops | bytes accessed | tf_op | source)
XLA Modules:
  0.0 100.2 jit_solution(4553589887528486762)
XLA Ops:
  0.6 0.1 pad_add_fusion.where_ref
  0.7 1.2 %copy-done = f32[512,512]{1,0:T(8,128)S(1)} copy-done((f32[512,512]{1,0:T(8,128)S(1)}, f32[512,512]{1,0:T(8,128)}, u32[]{:S(2)}) %copy-start) | copy-done | bytes 1048600
  1.9 1.2 %copy-done.2 = f32[512,512]{1,0:T(8,128)S(1)} copy-done((f32[512,512]{1,0:T(8,128)S(1)}, f32[512,512]{1,0:T(8,128)}, u32[]{:S(2)}) %copy-start.2) | copy-done | bytes 1048600
  3.2 1.0 %copy-done.10 = f32[512,256]{1,0:T(8,128)S(1)} copy-done((f32[512,256]{1,0:T(8,128)S(1)}, f32[512,256]{1,0:T(8,128)}, u32[]{:S(2)}) %copy-start.10) | copy-done | bytes 524312
  4.2 0.0 copy-start.12
  4.2 0.7 shard_map.96.pack_ref
  5.0 3.2 %collective-permute-start.6 = (f32[320,512]{1,0:T(8,128)S(1)}, f32[320,512]{1,0:T(8,128)S(1)}, u32[]{:S(2)}, u32[]{:S(2)}) collective-permute-start(f32[320,512]{1,0:T(8,128)S(1)} %shard_map.96.pack_ref), channel_id=1, source_target_pairs={{4,5},{8,9},{12,13},{9,10},{13,14},{2,6},{20,21},{24,25},{28,29},{... | collective-permute-start | bytes 1966088 | tf_op jit(solution)/shard_map/ppermute | solution.py:343
  8.2 2.3 %collective-permute-start.8 = (f32[320,512]{1,0:T(8,128)S(1)}, f32[320,512]{1,0:T(8,128)S(1)}, u32[]{:S(2)}, u32[]{:S(2)}) collective-permute-start(f32[320,512]{1,0:T(8,128)S(1)} %shard_map.96.pack_ref), channel_id=1, source_target_pairs={{4,6},{8,10},{12,14},{14,13},{1,5},{20,22},{24,26},{28,30},{30,29}... | collective-permute-start | bytes 1966088 | tf_op jit(solution)/shard_map/ppermute | solution.py:343
  10.6 1.9 %shard_map.95 = (f32[2,256,256]{2,1,0:T(8,128)}, f32[8,136,128]{2,1,0:T(8,128)S(1)}) custom-call(s32[2]{0:T(128)S(1)} %copy-done.12, f32[2,256,256]{2,1,0:T(8,128)S(1)} %copy-done.7, f32[2,256,256]{2,1,0:T(8,128)S(1)} %copy-done.8, f32[2,256,256]{2,1,0:T(8,128)S(1)} %copy-done.9, s32[2,256]{1,0:T(2,128)S(1)} %copy-done.11), custom_call_target="tpu_custom_call" | custom-call | bytes 1574920 | tf_op jit(solution)/shard_map/pallas_call | solution.py:311
  12.5 0.8 copy-done.6
  13.3 4.9 %all-to-all-start = ((f32[8,136,128]{2,1,0:T(8,128)}), f32[8,136,128]{2,1,0:T(8,128)}, u32[]{:S(2)}, u32[]{:S(2)}) async-start(f32[8,136,128]{2,1,0:T(8,128)} %copy-done.6), calls=%async_computation | async-start | bytes 1114112 | tf_op jit(solution)/shard_map/all_to_all | solution.py:370
  18.2 3.3 %collective-permute-done.6.nm_ref = f32[320,512]{1,0:T(8,128)S(1)} collective-permute-done((f32[320,512]{1,0:T(8,128)S(1)}, f32[320,512]{1,0:T(8,128)S(1)}, u32[]{:S(2)}, u32[]{:S(2)}) %collective-permute-start.6) | collective-permute-done | bytes 655392 | tf_op jit(solution)/shard_map/ppermute | solution.py:343
  21.6 2.7 %collective-permute-start.7 = (f32[320,512]{1,0:T(8,128)S(1)}, f32[320,512]{1,0:T(8,128)}, u32[]{:S(2)}, u32[]{:S(2)}) collective-permute-start(f32[320,512]{1,0:T(8,128)S(1)} %collective-permute-done.6.nm_ref), channel_id=1, source_target_pairs={{0,16},{16,0},{1,17},{17,1},{2,18},{18,2},{3,19},{19,3},{4,20},{20... | collective-permute-start | bytes 1966088 | tf_op jit(solution)/shard_map/ppermute | solution.py:340
  24.3 11.4 %collective-permute-done.8.fm_ref = f32[320,512]{1,0:T(8,128)S(1)} collective-permute-done((f32[320,512]{1,0:T(8,128)S(1)}, f32[320,512]{1,0:T(8,128)S(1)}, u32[]{:S(2)}, u32[]{:S(2)}) %collective-permute-start.8) | collective-permute-done | bytes 655392 | tf_op jit(solution)/shard_map/ppermute | solution.py:343
  35.7 1.5 %collective-permute-start.9 = (f32[320,512]{1,0:T(8,128)S(1)}, f32[320,512]{1,0:T(8,128)S(1)}, u32[]{:S(2)}, u32[]{:S(2)}) collective-permute-start(f32[320,512]{1,0:T(8,128)S(1)} %collective-permute-done.8.fm_ref), channel_id=1, source_target_pairs={{0,16},{16,0},{1,17},{17,1},{2,18},{18,2},{3,19},{19,3},{4,20},{20... | collective-permute-start | bytes 1966088 | tf_op jit(solution)/shard_map/ppermute | solution.py:340
  37.2 0.0 all-to-all-done.recv_ref
  37.2 2.5 %shard_map.97 = (f32[16,2048]{1,0:T(8,128)S(1)}, f32[16,2048]{1,0:T(8,128)S(1)}) custom-call(s32[3]{0:T(128)S(1)} %pad_add_fusion.where_ref, f32[8,136,128]{2,1,0:T(8,128)} %all-to-all-done.recv_ref), custom_call_target="tpu_custom_call" | custom-call | bytes 557068 | tf_op jit(solution)/shard_map/pallas_call | solution.py:311
  39.7 1.3 %collective-permute-start = (f32[16,2048]{1,0:T(8,128)S(1)}, f32[16,2048]{1,0:T(8,128)S(1)}, u32[]{:S(2)}, u32[]{:S(2)}) collective-permute-start(f32[16,2048]{1,0:T(8,128)S(1)} %get-tuple-element.11), channel_id=1, source_target_pairs={{0,1},{3,2},{4,5},{7,6},{8,9},{11,10},{12,13},{15,14},{16,17},{19,... | collective-permute-start | bytes 393224 | tf_op jit(solution)/shard_map/ppermute | solution.py:349
  41.0 0.7 collective-permute-start.1
  41.7 6.3 %collective-permute-start.2 = (f32[16,2048]{1,0:T(8,128)S(1)}, f32[16,2048]{1,0:T(8,128)S(1)}, u32[]{:S(2)}, u32[]{:S(2)}) collective-permute-start(f32[16,2048]{1,0:T(8,128)S(1)} %get-tuple-element.10.a_ref), channel_id=1, source_target_pairs={{0,2},{3,1},{4,6},{7,5},{8,10},{11,9},{12,14},{15,13},{16,18},{19,... | collective-permute-start | bytes 393224 | tf_op jit(solution)/shard_map/ppermute | solution.py:349
  48.0 0.0 collective-permute-done.b_ref
  48.0 0.0 collective-permute-done.1.c_ref
  48.0 2.3 %collective-permute-done.2.d_ref = f32[16,2048]{1,0:T(8,128)S(1)} collective-permute-done((f32[16,2048]{1,0:T(8,128)S(1)}, f32[16,2048]{1,0:T(8,128)S(1)}, u32[]{:S(2)}, u32[]{:S(2)}) %collective-permute-start.2) | collective-permute-done | bytes 131104 | tf_op jit(solution)/shard_map/ppermute | solution.py:349
  50.4 0.0 copy-start.1
  50.4 0.8 collective-permute-start.3
  51.2 0.7 collective-permute-start.4
  51.9 0.7 collective-permute-start.5
  52.6 0.0 collective-permute-done.4.c_ref
  52.6 0.0 collective-permute-done.5.d_ref
  52.6 1.2 %shard_map.99 = (f32[64,512]{1,0:T(8,128)S(1)}, f32[64,512]{1,0:T(8,128)S(1)}) custom-call(s32[3]{0:T(128)S(1)} %pad_add_fusion.where_ref, f32[320,512]{1,0:T(8,128)S(1)} %copy-done.5, f32[16,2048]{1,0:T(8,128)S(1)} %shard_map.98.a_ref, f32[16,2048]{1,0:T(8,128)S(1)} %collective-permute-done.3.b_ref, f32[16,2048]{1,0:T(8,128)S(1)} %collective-permute-done.4.c_ref, ...), custom_call_target="tpu_custom_call" | custom-call | bytes 4849676 | tf_op jit(solution)/shard_map/pallas_call | solution.py:311
  53.8 0.7 collective-permute-start.10
  54.5 0.7 collective-permute-start.11
  55.2 0.0 collective-permute-done.11.ha_ref
  55.2 1.1 %shard_map.101.x_ref = f32[64,512]{1,0:T(8,128)S(1)} custom-call(s32[3]{0:T(128)S(1)} %pad_add_fusion.where_ref, f32[64,512]{1,0:T(8,128)S(1)} %get-tuple-element.12.res_ref, f32[64,512]{1,0:T(8,128)S(1)} %get-tuple-element.13.x_ref, f32[512,512]{1,0:T(8,128)S(1)} %copy-done.3, f32[64,512]{1,0:T(8,128)S(1)} %collective-permute-done.10.hb_ref, ...), custom_call_target="tpu_custom_call" | custom-call | bytes 5242892 | tf_op jit(solution)/shard_map/pallas_call | solution.py:311
  56.3 0.7 collective-permute-start.12
  57.0 1.1 %shard_map.100.res_ref = f32[64,512]{1,0:T(8,128)S(1)} custom-call(s32[3]{0:T(128)S(1)} %pad_add_fusion.where_ref, f32[64,512]{1,0:T(8,128)S(1)} %get-tuple-element.12.res_ref, f32[64,512]{1,0:T(8,128)S(1)} %collective-permute-done.10.hb_ref, f32[64,512]{1,0:T(8,128)S(1)} %collective-permute-done.11.ha_ref, f32[512,512]{1,0:T(8,128)S(1)} %copy-done.1, ...), custom_call_target="tpu_custom_call" | custom-call | bytes 4063244 | tf_op jit(solution)/shard_map/pallas_call | solution.py:311
  58.1 0.0 collective-permute-done.12.h_ref
  58.1 0.6 shard_map.102.x_ref
  58.7 1.3 %collective-permute-start.13 = (f32[64,512]{1,0:T(8,128)S(1)}, f32[64,512]{1,0:T(8,128)S(1)}, u32[]{:S(2)}, u32[]{:S(2)}) collective-permute-start(f32[64,512]{1,0:T(8,128)S(1)} %shard_map.102.x_ref), channel_id=1, source_target_pairs={{1,0},{2,3},{5,4},{6,7},{9,8},{10,11},{13,12},{14,15},{17,16},{18,... | collective-permute-start | bytes 393224 | tf_op jit(solution)/shard_map/ppermute | solution.py:349
  60.0 0.7 collective-permute-start.14
  60.7 1.3 %collective-permute-start.15 = (f32[64,512]{1,0:T(8,128)S(1)}, f32[64,512]{1,0:T(8,128)S(1)}, u32[]{:S(2)}, u32[]{:S(2)}) collective-permute-start(f32[64,512]{1,0:T(8,128)S(1)} %shard_map.102.x_ref), channel_id=1, source_target_pairs={{1,3},{2,0},{5,7},{6,4},{9,11},{10,8},{13,15},{14,12},{17,19},{18,... | collective-permute-start | bytes 393224 | tf_op jit(solution)/shard_map/ppermute | solution.py:349
  62.0 24.6 %collective-permute-done.13.a_ref = f32[64,512]{1,0:T(8,128)S(1)} collective-permute-done((f32[64,512]{1,0:T(8,128)S(1)}, f32[64,512]{1,0:T(8,128)S(1)}, u32[]{:S(2)}, u32[]{:S(2)}) %collective-permute-start.13) | collective-permute-done | bytes 131104 | tf_op jit(solution)/shard_map/ppermute | solution.py:349
  86.5 0.0 collective-permute-done.14.b_ref
  86.5 4.6 %collective-permute-done.15.c_ref = f32[64,512]{1,0:T(8,128)S(1)} collective-permute-done((f32[64,512]{1,0:T(8,128)S(1)}, f32[64,512]{1,0:T(8,128)S(1)}, u32[]{:S(2)}, u32[]{:S(2)}) %collective-permute-start.15) | collective-permute-done | bytes 131104 | tf_op jit(solution)/shard_map/ppermute | solution.py:349
  91.2 0.7 shard_map.103.own_ref
  91.8 5.8 %collective-permute-start.16 = (f32[512,128]{1,0:T(8,128)S(1)}, f32[512,128]{1,0:T(8,128)S(1)}, u32[]{:S(2)}, u32[]{:S(2)}) collective-permute-start(f32[512,128]{1,0:T(8,128)S(1)} %shard_map.103.own_ref), channel_id=1, source_target_pairs={{0,16},{16,0},{1,17},{17,1},{2,18},{18,2},{3,19},{19,3},{4,20},{20... | collective-permute-start | bytes 786440 | tf_op jit(solution)/shard_map/ppermute | solution.py:340
  97.7 1.2 %collective-permute-done.16.other_ref = f32[512,128]{1,0:T(8,128)S(1)} collective-permute-done((f32[512,128]{1,0:T(8,128)S(1)}, f32[512,128]{1,0:T(8,128)S(1)}, u32[]{:S(2)}, u32[]{:S(2)}) %collective-permute-start.16) | collective-permute-done | bytes 262176 | tf_op jit(solution)/shard_map/ppermute | solution.py:340
  98.9 1.4 %shard_map.104 = f32[512,256]{1,0:T(8,128)} custom-call(s32[3]{0:T(128)S(1)} %pad_add_fusion.where_ref, f32[512,128]{1,0:T(8,128)S(1)} %shard_map.103.own_ref, f32[512,128]{1,0:T(8,128)S(1)} %collective-permute-done.16.other_ref), custom_call_target="tpu_custom_call" | custom-call | bytes 524300 | tf_op jit(solution)/shard_map/pallas_call | solution.py:311
  (25 shorter events, 0.1 us)
Async XLA Ops:
  0.7 1.2 %copy-start = (f32[512,512]{1,0:T(8,128)S(1)}, f32[512,512]{1,0:T(8,128)}, u32[]{:S(2)}) copy-start(f32[512,512]{1,0:T(8,128)} %factor_ref.7) | copy-start | bytes 3145732
  1.9 1.2 %copy-start.2 = (f32[512,512]{1,0:T(8,128)S(1)}, f32[512,512]{1,0:T(8,128)}, u32[]{:S(2)}) copy-start(f32[512,512]{1,0:T(8,128)} %diag_ref.9) | copy-start | bytes 3145732
  3.2 1.0 %copy-start.10 = (f32[512,256]{1,0:T(8,128)S(1)}, f32[512,256]{1,0:T(8,128)}, u32[]{:S(2)}) copy-start(f32[512,256]{1,0:T(8,128)} %rhs_ref.3) | copy-start | bytes 1572868
  4.2 6.3 %copy-start.7 = (f32[2,256,256]{2,1,0:T(8,128)S(1)}, f32[2,256,256]{2,1,0:T(8,128)}, u32[]{:S(2)}) copy-start(f32[2,256,256]{2,1,0:T(8,128)} %rhs_ref.2) | copy-start | bytes 1572868
  4.2 6.3 %copy-start.8 = (f32[2,256,256]{2,1,0:T(8,128)S(1)}, f32[2,256,256]{2,1,0:T(8,128)}, u32[]{:S(2)}) copy-start(f32[2,256,256]{2,1,0:T(8,128)} %diag_ref.5) | copy-start | bytes 1572868
  4.2 6.3 %copy-start.9 = (f32[2,256,256]{2,1,0:T(8,128)S(1)}, f32[2,256,256]{2,1,0:T(8,128)}, u32[]{:S(2)}) copy-start(f32[2,256,256]{2,1,0:T(8,128)} %off_ref.1) | copy-start | bytes 1572868
  4.2 6.4 %copy-start.11 = (s32[2,256]{1,0:T(2,128)S(1)}, s32[2,256]{1,0:T(2,128)}, u32[]{:S(2)}) copy-start(s32[2,256]{1,0:T(2,128)} %tgt_ref.1) | copy-start | bytes 6148
  4.2 6.4 %copy-start.12 = (s32[2]{0:T(128)S(1)}, s32[2]{0:T(128)}, u32[]{:S(2)}) copy-start(s32[2]{0:T(128)} %live_ref.1) | copy-start | bytes 28
  5.0 7.5 %copy-start.4 = (f32[320,512]{1,0:T(8,128)}, f32[320,512]{1,0:T(8,128)S(1)}, u32[]{:S(2)}) copy-start(f32[320,512]{1,0:T(8,128)S(1)} %shard_map.96.pack_ref) | copy-start | bytes 1966084
  5.0 16.6 %collective-permute-start.6 = (f32[320,512]{1,0:T(8,128)S(1)}, f32[320,512]{1,0:T(8,128)S(1)}, u32[]{:S(2)}, u32[]{:S(2)}) collective-permute-start(f32[320,512]{1,0:T(8,128)S(1)} %shard_map.96.pack_ref), channel_id=1, source_target_pairs={{4,5},{8,9},{12,13},{9,10},{13,14},{2,6},{20,21},{24,25},{28,29},{... | collective-permute-start | bytes 1966088 | tf_op jit(solution)/shard_map/ppermute | solution.py:343
  8.2 27.4 %collective-permute-start.8 = (f32[320,512]{1,0:T(8,128)S(1)}, f32[320,512]{1,0:T(8,128)S(1)}, u32[]{:S(2)}, u32[]{:S(2)}) collective-permute-start(f32[320,512]{1,0:T(8,128)S(1)} %shard_map.96.pack_ref), channel_id=1, source_target_pairs={{4,6},{8,10},{12,14},{14,13},{1,5},{20,22},{24,26},{28,30},{30,29}... | collective-permute-start | bytes 1966088 | tf_op jit(solution)/shard_map/ppermute | solution.py:343
  12.5 0.8 copy-start.6
  13.3 39.3 %copy-start.3 = (f32[512,512]{1,0:T(8,128)S(1)}, f32[512,512]{1,0:T(8,128)}, u32[]{:S(2)}) copy-start(f32[512,512]{1,0:T(8,128)} %diag_ref.9) | copy-start | bytes 3145732
  13.3 23.9 %all-to-all-start = ((f32[8,136,128]{2,1,0:T(8,128)}), f32[8,136,128]{2,1,0:T(8,128)}, u32[]{:S(2)}, u32[]{:S(2)}) async-start(f32[8,136,128]{2,1,0:T(8,128)} %copy-done.6), calls=%async_computation | async-start | bytes 1114112 | tf_op jit(solution)/shard_map/all_to_all | solution.py:370
  21.6 31.0 %collective-permute-start.7 = (f32[320,512]{1,0:T(8,128)S(1)}, f32[320,512]{1,0:T(8,128)}, u32[]{:S(2)}, u32[]{:S(2)}) collective-permute-start(f32[320,512]{1,0:T(8,128)S(1)} %collective-permute-done.6.nm_ref), channel_id=1, source_target_pairs={{0,16},{16,0},{1,17},{17,1},{2,18},{18,2},{3,19},{19,3},{4,20},{20... | collective-permute-start | bytes 1966088 | tf_op jit(solution)/shard_map/ppermute | solution.py:340
  35.7 16.9 %collective-permute-start.9 = (f32[320,512]{1,0:T(8,128)S(1)}, f32[320,512]{1,0:T(8,128)S(1)}, u32[]{:S(2)}, u32[]{:S(2)}) collective-permute-start(f32[320,512]{1,0:T(8,128)S(1)} %collective-permute-done.8.fm_ref), channel_id=1, source_target_pairs={{0,16},{16,0},{1,17},{17,1},{2,18},{18,2},{3,19},{19,3},{4,20},{20... | collective-permute-start | bytes 1966088 | tf_op jit(solution)/shard_map/ppermute | solution.py:340
  37.2 15.4 %copy-start.5 = (f32[320,512]{1,0:T(8,128)S(1)}, f32[320,512]{1,0:T(8,128)}, u32[]{:S(2)}) copy-start(f32[320,512]{1,0:T(8,128)} %copy-done.4) | copy-start | bytes 1966084
  39.7 8.3 %collective-permute-start = (f32[16,2048]{1,0:T(8,128)S(1)}, f32[16,2048]{1,0:T(8,128)S(1)}, u32[]{:S(2)}, u32[]{:S(2)}) collective-permute-start(f32[16,2048]{1,0:T(8,128)S(1)} %get-tuple-element.11), channel_id=1, source_target_pairs={{0,1},{3,2},{4,5},{7,6},{8,9},{11,10},{12,13},{15,14},{16,17},{19,... | collective-permute-start | bytes 393224 | tf_op jit(solution)/shard_map/ppermute | solution.py:349
  41.0 7.0 %collective-permute-start.1 = (f32[16,2048]{1,0:T(8,128)S(1)}, f32[16,2048]{1,0:T(8,128)S(1)}, u32[]{:S(2)}, u32[]{:S(2)}) collective-permute-start(f32[16,2048]{1,0:T(8,128)S(1)} %get-tuple-element.11), channel_id=1, source_target_pairs={{1,2},{2,1},{5,6},{6,5},{9,10},{10,9},{13,14},{14,13},{17,18},{18,... | collective-permute-start | bytes 393224 | tf_op jit(solution)/shard_map/ppermute | solution.py:349
  41.7 8.7 %collective-permute-start.2 = (f32[16,2048]{1,0:T(8,128)S(1)}, f32[16,2048]{1,0:T(8,128)S(1)}, u32[]{:S(2)}, u32[]{:S(2)}) collective-permute-start(f32[16,2048]{1,0:T(8,128)S(1)} %get-tuple-element.10.a_ref), channel_id=1, source_target_pairs={{0,2},{3,1},{4,6},{7,5},{8,10},{11,9},{12,14},{15,13},{16,18},{19,... | collective-permute-start | bytes 393224 | tf_op jit(solution)/shard_map/ppermute | solution.py:349
  50.4 4.8 %copy-start.1 = (f32[512,512]{1,0:T(8,128)S(1)}, f32[512,512]{1,0:T(8,128)}, u32[]{:S(2)}) copy-start(f32[512,512]{1,0:T(8,128)} %factor_ref.7) | copy-start | bytes 3145732
  50.4 2.2 %collective-permute-start.3 = (f32[16,2048]{1,0:T(8,128)S(1)}, f32[16,2048]{1,0:T(8,128)S(1)}, u32[]{:S(2)}, u32[]{:S(2)}) collective-permute-start(f32[16,2048]{1,0:T(8,128)S(1)} %shard_map.98.a_ref), channel_id=1, source_target_pairs={{1,5},{2,6},{5,1},{6,2},{9,13},{10,14},{13,9},{14,10},{17,21},{18,... | collective-permute-start | bytes 393224 | tf_op jit(solution)/shard_map/ppermute | solution.py:343
  51.2 1.4 %collective-permute-start.4 = (f32[16,2048]{1,0:T(8,128)S(1)}, f32[16,2048]{1,0:T(8,128)S(1)}, u32[]{:S(2)}, u32[]{:S(2)}) collective-permute-start(f32[16,2048]{1,0:T(8,128)S(1)} %shard_map.98.a_ref), channel_id=1, source_target_pairs={{1,9},{2,10},{5,13},{6,14},{9,1},{10,2},{13,5},{14,6},{17,25},{18,... | collective-permute-start | bytes 393224 | tf_op jit(solution)/shard_map/ppermute | solution.py:343
  51.9 0.7 collective-permute-start.5
  53.8 1.4 %collective-permute-start.10 = (f32[64,512]{1,0:T(8,128)S(1)}, f32[64,512]{1,0:T(8,128)S(1)}, u32[]{:S(2)}, u32[]{:S(2)}) collective-permute-start(f32[64,512]{1,0:T(8,128)S(1)} %get-tuple-element.13.x_ref), channel_id=1, source_target_pairs={{5,9},{6,10},{1,13},{2,14},{21,25},{22,26},{17,29},{18,30}} | collective-permute-start | bytes 393224 | tf_op jit(solution)/shard_map/ppermute | solution.py:343
  54.5 0.7 collective-permute-start.11
  56.3 1.8 %collective-permute-start.12 = (f32[64,512]{1,0:T(8,128)S(1)}, f32[64,512]{1,0:T(8,128)S(1)}, u32[]{:S(2)}, u32[]{:S(2)}) collective-permute-start(f32[64,512]{1,0:T(8,128)S(1)} %shard_map.101.x_ref), channel_id=1, source_target_pairs={{9,13},{10,14},{25,29},{26,30}} | collective-permute-start | bytes 393224 | tf_op jit(solution)/shard_map/ppermute | solution.py:343
  58.7 27.8 %collective-permute-start.13 = (f32[64,512]{1,0:T(8,128)S(1)}, f32[64,512]{1,0:T(8,128)S(1)}, u32[]{:S(2)}, u32[]{:S(2)}) collective-permute-start(f32[64,512]{1,0:T(8,128)S(1)} %shard_map.102.x_ref), channel_id=1, source_target_pairs={{1,0},{2,3},{5,4},{6,7},{9,8},{10,11},{13,12},{14,15},{17,16},{18,... | collective-permute-start | bytes 393224 | tf_op jit(solution)/shard_map/ppermute | solution.py:349
  60.0 26.5 %collective-permute-start.14 = (f32[64,512]{1,0:T(8,128)S(1)}, f32[64,512]{1,0:T(8,128)S(1)}, u32[]{:S(2)}, u32[]{:S(2)}) collective-permute-start(f32[64,512]{1,0:T(8,128)S(1)} %shard_map.102.x_ref), channel_id=1, source_target_pairs={{1,2},{2,1},{5,6},{6,5},{9,10},{10,9},{13,14},{14,13},{17,18},{18,... | collective-permute-start | bytes 393224 | tf_op jit(solution)/shard_map/ppermute | solution.py:349
  60.7 30.5 %collective-permute-start.15 = (f32[64,512]{1,0:T(8,128)S(1)}, f32[64,512]{1,0:T(8,128)S(1)}, u32[]{:S(2)}, u32[]{:S(2)}) collective-permute-start(f32[64,512]{1,0:T(8,128)S(1)} %shard_map.102.x_ref), channel_id=1, source_target_pairs={{1,3},{2,0},{5,7},{6,4},{9,11},{10,8},{13,15},{14,12},{17,19},{18,... | collective-permute-start | bytes 393224 | tf_op jit(solution)/shard_map/ppermute | solution.py:349
  91.8 7.0 %collective-permute-start.16 = (f32[512,128]{1,0:T(8,128)S(1)}, f32[512,128]{1,0:T(8,128)S(1)}, u32[]{:S(2)}, u32[]{:S(2)}) collective-permute-start(f32[512,128]{1,0:T(8,128)S(1)} %shard_map.103.own_ref), channel_id=1, source_target_pairs={{0,16},{16,0},{1,17},{17,1},{2,18},{18,2},{3,19},{19,3},{4,20},{20... | collective-permute-start | bytes 786440 | tf_op jit(solution)/shard_map/ppermute | solution.py:340

commit v3 on v1

--- a/solution.py
+++ b/solution.py
@@ -12,6 +12,7 @@
 NT = (((1,), (1,)), ((), ()))
 NN = (((1,), (0,)), ((), ()))
 VM = pl.BlockSpec(memory_space=pltpu.VMEM)
+ANY = pl.BlockSpec(memory_space=pl.ANY)
 SM = pl.BlockSpec(memory_space=pltpu.SMEM)
 
 
@@ -90,20 +91,40 @@
     return both[:rows] + both[rows:] + cross
 
 
-def lower(matrix):
-    row = lax.broadcasted_iota(jnp.int32, matrix.shape, 0)
+def lower(matrix, first_row=0):
+    row = lax.broadcasted_iota(jnp.int32, matrix.shape, 0) + first_row
     col = lax.broadcasted_iota(jnp.int32, matrix.shape, 1)
     return jnp.where(col <= row, matrix, 0.0)
 
 
-def child_kernel(where_ref, live_ref, rhs_ref, diag_ref, off_ref, tgt_ref, sol_ref, keep_ref, send_ref, tiles_ref):
+def pack_kernel(where_ref, factor_ref, rhs_ref, after_ref, part_ref, rhs_out_ref, turned_ref):
+    leaf, z = where_ref[0], where_ref[2]
+    part, half, piece = part_ref.shape[0], turned_ref.shape[0], rhs_out_ref.shape[0]
+    part_ref[...] = factor_ref[pl.ds(pl.multiple_of(leaf * part, part), part), :]
+    turned_ref[...] = rhs_ref[:, pl.ds(pl.multiple_of(leaf * half, half), half)].T
+    rhs_out_ref[...] = turned_ref[pl.ds(pl.multiple_of((z // 2) * piece, piece), piece), :]
+
+
+def child_kernel(where_ref, live_ref, rhs_hbm, diag_hbm, off_hbm, tgt_ref, sol_ref, keep_ref, send_ref,
+                 rhs_ref, diag_ref, off_ref, tiles_ref, sems):
     leaf = where_ref[0]
     children, slots = off_ref.shape[0], off_ref.shape[1]
     half = keep_ref.shape[0]
+    pairs = ((rhs_hbm, rhs_ref), (diag_hbm, diag_ref), (off_hbm, off_ref))
+    copies = [
+        [pltpu.make_async_copy(source.at[s], target.at[s], sems.at[i, s]) for i, (source, target) in enumerate(pairs)]
+        for s in range(children)
+    ]
     for s in range(children):
+        for copy in copies[s]:
+            copy.start()
+    for s in range(children):
+        copies[s][0].wait()
+        copies[s][1].wait()
         rhs = rhs_ref[s]
         sol = rhs + dot3(lower(diag_ref[s]), rhs, NN)
         sol_ref[s] = sol
+        copies[s][2].wait()
         tiles = dot3(sol.T, off_ref[s], NT)
         slot = lax.broadcasted_iota(jnp.int32, tiles.shape, 1)
         tiles_ref[:, s * slots:(s + 1) * slots] = jnp.where(slot < live_ref[s], tiles, 0.0)
@@ -142,48 +163,127 @@
     second_ref[...] = sum_ref[pl.ds(pl.multiple_of((1 - odd) * piece, piece), piece), :]
 
 
-def first_kernel(rhs_ref, a_ref, b_ref, c_ref, d_ref, diag_ref, res_ref, x_ref):
+def halves(x, mine_ref, other_ref, leaf, out_ref):
+    part = out_ref.shape[1] // 2
+    for ref, at in ((mine_ref, leaf), (other_ref, 1 - leaf)):
+        start = pl.multiple_of(at * part, part)
+        block = ref[0:part, :]
+        out_ref[:, pl.ds(start, part)] = dot3(x, block, NT)
+    return out_ref[...]
+
+
+def zeroth_kernel(where_ref, rhs_ref, a_ref, b_ref, c_ref, d_ref, diag_ref, res_ref, x_ref):
+    row = where_ref[1]
     res = rhs_ref[...] - ((a_ref[...] + b_ref[...]) + (c_ref[...] + d_ref[...]))
     res_ref[...] = res
-    x_ref[...] = res + dot3(res, lower(diag_ref[...]), NT)
-
-
-def step_kernel(count, *refs):
-    res_ref, diag_ref = refs[0], refs[1]
-    given, factors = refs[2:2 + count], refs[2 + count:2 + 2 * count]
-    res_out, x_out = refs[2 + 2 * count], refs[3 + 2 * count]
-    res = res_ref[...]
-    for x_ref, factor_ref in zip(given, factors):
-        res = res - dot3(x_ref[...], factor_ref[...], NT)
-    res_out[...] = res
-    x_out[...] = res + dot3(res, lower(diag_ref[...]), NT)
+    x_ref[...] = res
+
+    @pl.when(row == 0)
+    def _():
+        x_ref[...] = res + dot3(res, lower(diag_ref[...]), NT)
+
+
+def first_kernel(where_ref, res_ref, x_ref, diag_ref, h_ref, nm_ref, no_ref, fm_ref, fo_ref, out_ref, left_ref, tmp_ref):
+    leaf, row, z = where_ref[0], where_ref[1], where_ref[2]
+    out_ref[...] = x_ref[...]
+
+    @pl.when((row == 1) & ((z == 1) | (z == 2)))
+    def _():
+        @pl.when(z == 1)
+        def _():
+            left_ref[...] = res_ref[...] - halves(h_ref[...], nm_ref, no_ref, leaf, tmp_ref)
+
+        @pl.when(z == 2)
+        def _():
+            left_ref[...] = res_ref[...] - halves(h_ref[...], fm_ref, fo_ref, leaf, tmp_ref)
+
+        value = left_ref[...]
+        out_ref[...] = value + dot3(value, lower(diag_ref[...]), NT)
+
+
+def earlier(res, x0, x1, leaf, z, refs, out_ref, tmp_ref):
+    factor_ref, nm_ref, no_ref, fm_ref, fo_ref = refs
+
+    @pl.when(z == 1)
+    def _():
+        value = res - halves(x0, nm_ref, no_ref, leaf, tmp_ref)
+        out_ref[...] = value - dot3(x1, factor_ref[...], NT)
+
+    @pl.when(z == 2)
+    def _():
+        value = res - halves(x0, fm_ref, fo_ref, leaf, tmp_ref)
+        out_ref[...] = value - halves(x1, nm_ref, no_ref, leaf, tmp_ref)
+
+
+def second_kernel(where_ref, res_ref, x_ref, diag_ref, hb_ref, ha_ref, factor_ref, nm_ref, no_ref, fm_ref, fo_ref,
+                  out_ref, left_ref, tmp_ref):
+    leaf, row, z = where_ref[0], where_ref[1], where_ref[2]
+    out_ref[...] = x_ref[...]
+
+    @pl.when((row == 2) & ((z == 1) | (z == 2)))
+    def _():
+        refs = (factor_ref, nm_ref, no_ref, fm_ref, fo_ref)
+        earlier(res_ref[...], ha_ref[...], hb_ref[...], leaf, z, refs, left_ref, tmp_ref)
+        value = left_ref[...]
+        out_ref[...] = value + dot3(value, lower(diag_ref[...]), NT)
+
+
+def third_kernel(where_ref, res_ref, hb_ref, ha_ref, factor_ref, nm_ref, no_ref, fm_ref, fo_ref, out_ref, tmp_ref):
+    leaf, row, z = where_ref[0], where_ref[1], where_ref[2]
+    out_ref[...] = res_ref[...]
+
+    @pl.when(row == 3)
+    def _():
+        refs = (factor_ref, nm_ref, no_ref, fm_ref, fo_ref)
+        earlier(res_ref[...], hb_ref[...], ha_ref[...], leaf, z, refs, out_ref, tmp_ref)
+
+
+def fourth_kernel(where_ref, res_ref, x_ref, diag_ref, h_ref, factor_ref, fm_ref, fo_ref, out_ref, left_ref, tmp_ref):
+    leaf, row, z = where_ref[0], where_ref[1], where_ref[2]
+    out_ref[...] = x_ref[...]
+
+    @pl.when((row == 3) & ((z == 1) | (z == 2)))
+    def _():
+        @pl.when(z == 1)
+        def _():
+            left_ref[...] = res_ref[...] - halves(h_ref[...], fm_ref, fo_ref, leaf, tmp_ref)
+
+        @pl.when(z == 2)
+        def _():
+            left_ref[...] = res_ref[...] - dot3(h_ref[...], factor_ref[...], NT)
+
+        value = left_ref[...]
+        out_ref[...] = value + dot3(value, lower(diag_ref[...]), NT)
 
 
 def half_kernel(where_ref, x_ref, a_ref, b_ref, c_ref, out_ref):
     z = where_ref[2]
-    piece = x_ref.shape[0]
     x, a, b, c = x_ref[...], a_ref[...], b_ref[...], c_ref[...]
-    out_ref[0:piece, :] = jnp.where(z == 0, a, jnp.where(z == 1, x, jnp.where(z == 2, b, c)))
-    out_ref[piece:2 * piece, :] = jnp.where(z == 0, c, jnp.where(z == 1, b, jnp.where(z == 2, x, a)))
+    low = jnp.where(z == 0, a, jnp.where(z == 1, x, jnp.where(z == 2, b, c)))
+    high = jnp.where(z == 0, c, jnp.where(z == 1, b, jnp.where(z == 2, x, a)))
+    out_ref[...] = jnp.concatenate([low, high], axis=0).T
 
 
 def last_kernel(where_ref, own_ref, other_ref, out_ref):
     leaf = where_ref[0]
-    half = own_ref.shape[0]
-    own, other = own_ref[...].T, other_ref[...].T
+    half = own_ref.shape[1]
+    own, other = own_ref[...], other_ref[...]
     out_ref[:, 0:half] = jnp.where(leaf == 0, own, other)
     out_ref[:, half:2 * half] = jnp.where(leaf == 0, other, own)
 
 
-def call(kernel, ins, outs, scratch=(), flops=0):
+def call(kernel, ins, outs, scratch=(), outside=(), limit=40):
+    def spec(i, a):
+        return ANY if i in outside else SM if a.ndim == 1 else VM
+
     return pl.pallas_call(
         kernel,
         out_shape=[jax.ShapeDtypeStruct(shape, F32) for shape in outs],
-        in_specs=[SM if a.ndim == 1 else VM for a in ins],
+        in_specs=[spec(i, a) for i, a in enumerate(ins)],
         out_specs=[VM] * len(outs),
-        scratch_shapes=list(scratch),
-        cost_estimate=pl.CostEstimate(flops=flops, bytes_accessed=4 * sum(a.size for a in ins), transcendentals=0),
-        compiler_params=pltpu.CompilerParams(vmem_limit_bytes=40 * 1024 * 1024),
+        scratch_shapes=[pltpu.VMEM(s, F32) if isinstance(s, tuple) else s for s in scratch],
+        cost_estimate=pl.CostEstimate(flops=0, bytes_accessed=4 * sum(a.size for a in ins), transcendentals=0),
+        compiler_params=pltpu.CompilerParams(vmem_limit_bytes=limit * 1024 * 1024),
     )(*ins)
 
 
@@ -196,51 +296,51 @@
     half, piece = right // 2, right // 4
     children, slots = targets.shape
 
+    def at(r, c):
+        return r * cols + c
+
     def swap(value):
         return lax.ppermute(value, "leaf", [(0, 1), (1, 0)])
 
+    def plane(value, pairs):
+        return lax.ppermute(value, ("row", "col"), pairs)
+
+    def hop(value, pairs):
+        return plane(value, [(at(a, z), at(b, z)) for a, b in pairs for z in (1, 2)])
+
     def along_row(value, pairs):
         return lax.ppermute(value, "row", pairs)
 
     def along_col(value, pairs):
         return lax.ppermute(value, "col", pairs)
-
-    def at(r, c):
-        return r * cols + c
-
-    part = lax.dynamic_slice_in_dim(top_factor, leaf * (size // 2), size // 2, 0)
-    near = [(at(k, 0), at(k, 1)) for k in (1, 2, 3)] + [(at(k, 1), at(k, 2)) for k in (2, 3)]
-    far = [(at(k, 0), at(k, 2)) for k in (1, 2, 3)] + [(at(3, 2), at(3, 1))]
-    near_part = lax.ppermute(part, ("row", "col"), near)
-    far_part = lax.ppermute(part, ("row", "col"), far)
-
-    start = leaf * half + (col // 2) * piece
-    rhs_piece = lax.dynamic_slice_in_dim(top_rhs, start, piece, 1).T
 
     child_sol, keep, send = call(
         child_kernel,
         [where, live, child_rhs, child_diag, child_off, targets],
         [child_rhs.shape, (half, children * slots), (half + 8, children * slots)],
-        [pltpu.VMEM((right, children * slots), F32)],
-    )
-    recv = swap(send)
-    sums = call(scatter_kernel, [where, keep, recv, targets], [(half, size)] * rows)
+        [child_rhs.shape, child_diag.shape, child_off.shape, (right, children * slots),
+         pltpu.SemaphoreType.DMA((3, children))],
+        outside=(2, 3, 4),
+        limit=56,
+    )
+    sums = call(scatter_kernel, [where, keep, swap(send), targets], [(half, size)] * rows)
     got = [along_row(sums[s], [(i, i ^ s) for i in range(rows)]) for s in (1, 2, 3)]
 
-    near_other, far_other = swap(near_part), swap(far_part)
-
-    def whole(mine, other):
-        return jnp.where(
-            leaf == 0, jnp.concatenate([mine, other], 0), jnp.concatenate([other, mine], 0)
-        )
-
-    near_whole, far_whole = whole(near_part, near_other), whole(far_part, far_other)
-    factor0 = jnp.where(col == 1, near_whole, far_whole)
-    factor1 = jnp.where(col == 1, top_factor, near_whole)
-    factor2 = jnp.where(col == 1, far_whole, top_factor)
+    part, rhs_piece = call(
+        pack_kernel,
+        [where, top_factor, top_rhs, got[0]],
+        [(size // 2, size), (piece, size)],
+        [(half, size)],
+        outside=(3,),
+    )
+    near = plane(
+        part,
+        [(at(k, 0), at(k, 1)) for k in (1, 2, 3)] + [(at(k, 1), at(k, 2)) for k in (2, 3)],
+    )
+    far = plane(part, [(at(k, 0), at(k, 2)) for k in (1, 2, 3)] + [(at(3, 2), at(3, 1))])
 
     first, second = call(
-        pieces_kernel, [where, sums[0]] + got, [(piece, size)] * 2, [pltpu.VMEM((half, size), F32)]
+        pieces_kernel, [where, sums[0]] + got, [(piece, size)] * 2, [(half, size)]
     )
     q = [
         along_col(first, [(0, 1), (3, 2)]),
@@ -248,28 +348,29 @@
         along_col(second, [(0, 2), (3, 1)]),
     ]
     shape = (piece, size)
-    res, x = call(first_kernel, [rhs_piece, second] + q + [top_diag], [shape] * 2)
-    x0 = along_row(x, [(0, 1)]) + along_row(x, [(0, 2)])
-    res, x = call(
-        functools.partial(step_kernel, 1), [res, top_diag, x0, factor0], [shape] * 2
-    )
-    on = along_row(jnp.where(row == 2, x0, x), [(1, 2), (2, 3)])
-    x1 = along_row(x, [(1, 3)])
-    x0 = jnp.where(row == 3, on, 0.0)
-    x1 = jnp.where(row == 2, on, x1)
-    res, x = call(
-        functools.partial(step_kernel, 2), [res, top_diag, x0, x1, factor0, factor1], [shape] * 2
-    )
-    x2 = along_row(x, [(2, 3)])
-    res, x = call(
-        functools.partial(step_kernel, 1), [res, top_diag, x2, factor2], [shape] * 2
+    res, x = call(zeroth_kernel, [where, rhs_piece, second] + q + [top_diag], [shape] * 2)
+    h = hop(x, [(0, 1)])
+    near, far, x = lax.optimization_barrier((near, far, x))
+    moved = [near, swap(near), far, swap(far)]
+    (x,) = call(
+        first_kernel, [where, res, x, top_diag, h] + moved, [shape], [shape] * 2
+    )
+    hb = hop(x, [(1, 2), (0, 3)])
+    ha = hop(x, [(0, 2), (1, 3)])
+    (x,) = call(
+        second_kernel, [where, res, x, top_diag, hb, ha, top_factor] + moved, [shape], [shape] * 2
+    )
+    h = hop(x, [(2, 3)])
+    (res,) = call(third_kernel, [where, res, hb, ha, top_factor] + moved, [shape], [shape])
+    (x,) = call(
+        fourth_kernel, [where, res, x, top_diag, h, top_factor] + moved[2:], [shape], [shape] * 2
     )
     z = [
         along_col(x, [(1, 0), (2, 3)]),
         along_col(x, [(1, 2), (2, 1)]),
         along_col(x, [(1, 3), (2, 0)]),
     ]
-    (own,) = call(half_kernel, [where, x] + z, [(half, size)])
+    (own,) = call(half_kernel, [where, x] + z, [(size, half)])
     (top_sol,) = call(last_kernel, [where, own, swap(own)], [top_rhs.shape])
     return (child_sol, top_sol)
 

time: 88.9 us -> 92.3 us (1.038)
  the two profiles are of different devices: /device:TPU:7 before, /device:TPU:15 now
where the time goes in v3:
time: 92.3 us; the launch traced here: 90.6 us
  waiting for transfers between devices  49.3 us (53%)
  starting transfers between devices  24.9 us (27%)
  Pallas kernels  14 us (15%)
  local copies, waits for them, and re-layouts  0.97 us (1%)
    ppermute x3, waiting for transfers between devices, along_row(): return lax.ppermute(value, 'row', pairs)  19.4 us
    ppermute x6, waiting for transfers between devices, plane(): return lax.ppermute(value, ('row', 'col'), pairs)  14 us
    pallas_call x11, Pallas kernels, call(): pl.pallas_call(kernel, out_shape=[jax.ShapeDtypeStruct(shape, F32) for sh...  14 us
    ppermute x6, waiting for transfers between devices, along_col(): return lax.ppermute(value, 'col', pairs)  11.7 us
    ppermute x6, starting transfers between devices, plane(): return lax.ppermute(value, ('row', 'col'), pairs)  9.82 us
    ppermute x6, starting transfers between devices, along_col(): return lax.ppermute(value, 'col', pairs)  9.02 us
    ppermute x4, starting transfers between devices, swap(): return lax.ppermute(value, 'leaf', [(0, 1), (1, 0)])  4.99 us
    ppermute x4, waiting for transfers between devices, swap(): return lax.ppermute(value, 'leaf', [(0, 1), (1, 0)])  4.09 us
  transfers between devices with their start and end apart: 19, of which 11 were waited for; matrix products, arithmetic and copies ran while one was open for 0% of the time, Pallas kernels for 3%

profile of v3, /device:TPU:15, one launch (start us, length us, event | category | flops | bytes accessed | tf_op | source)
XLA Modules:
  0.0 90.6 jit_solution(1653932163985299101)
XLA Ops:
  0.6 0.7 pad_add_fusion.where_ref
  1.3 4.2 %shard_map.95 = (f32[2,256,256]{2,1,0:T(8,128)}, f32[128,512]{1,0:T(8,128)}, f32[136,512]{1,0:T(8,128)}) custom-call(s32[3]{0:T(128)} %pad_add_fusion.where_ref, s32[2]{0:T(128)} %live_ref.1, f32[2,256,256]{2,1,0:T(8,128)} %rhs_hbm.1, f32[2,256,256]{2,1,0:T(8,128)} %diag_hbm.1, f32[2,256,256]{2,1,0:T(8,128)} %off_hbm.1, s32[2,256]{1,0:T(2,128)} %tgt_ref.3), custom_call_target="tpu_custom_call" | custom-call | bytes 1574932 | tf_op jit(solution)/shard_map/pallas_call | solution.py:279
  5.5 0.0 copy-start.2
  5.5 0.7 collective-permute-start
  6.2 1.4 %collective-permute-done.recv_ref = f32[136,512]{1,0:T(8,128)S(1)} collective-permute-done((f32[136,512]{1,0:T(8,128)}, f32[136,512]{1,0:T(8,128)S(1)}, u32[]{:S(2)}, u32[]{:S(2)}) %collective-permute-start) | collective-permute-done | bytes 278560 | tf_op jit(solution)/shard_map/ppermute | solution.py:303
  7.6 0.9 %copy-done.3 = f32[128,512]{1,0:T(8,128)S(1)} copy-done((f32[128,512]{1,0:T(8,128)S(1)}, f32[128,512]{1,0:T(8,128)}, u32[]{:S(2)}) %copy-start.3) | copy-done | bytes 262168
  8.6 1.8 %shard_map.96 = (f32[128,512]{1,0:T(8,128)S(1)}, f32[128,512]{1,0:T(8,128)S(1)}, f32[128,512]{1,0:T(8,128)S(1)}, f32[128,512]{1,0:T(8,128)S(1)}) custom-call(s32[3]{0:T(128)S(1)} %copy-done.4, f32[128,512]{1,0:T(8,128)S(1)} %copy-done.3, f32[136,512]{1,0:T(8,128)S(1)} %collective-permute-done.recv_ref, s32[2,256]{1,0:T(2,128)S(1)} %copy-done.5), custom_call_target="tpu_custom_call" | custom-call | bytes 542732 | tf_op jit(solution)/shard_map/pallas_call | solution.py:279
  10.4 0.0 copy-start
  10.4 0.3 collective-permute-start.1
  10.8 7.2 %collective-permute-done.1.after_ref.b_ref = f32[128,512]{1,0:T(8,128)S(1)} collective-permute-done((f32[128,512]{1,0:T(8,128)S(1)}, f32[128,512]{1,0:T(8,128)S(1)}, u32[]{:S(2)}, u32[]{:S(2)}) %collective-permute-start.1) | collective-permute-done | bytes 262176 | tf_op jit(solution)/shard_map/ppermute | solution.py:312
  18.0 0.7 shard_map.97
  18.8 1.3 %collective-permute-start.8 = (f32[256,512]{1,0:T(8,128)S(1)}, f32[256,512]{1,0:T(8,128)S(1)}, u32[]{:S(2)}, u32[]{:S(2)}) collective-permute-start(f32[256,512]{1,0:T(8,128)S(1)} %get-tuple-element.29), channel_id=1, source_target_pairs={{4,6},{8,10},{12,14},{14,13},{20,22},{24,26},{28,30},{30,29}} | collective-permute-start | bytes 1572872 | tf_op jit(solution)/shard_map/ppermute | solution.py:306
  20.1 4.0 %collective-permute-start.7 = (f32[256,512]{1,0:T(8,128)S(1)}, f32[256,512]{1,0:T(8,128)S(1)}, u32[]{:S(2)}, u32[]{:S(2)}) collective-permute-start(f32[256,512]{1,0:T(8,128)S(1)} %get-tuple-element.29), channel_id=1, source_target_pairs={{4,5},{8,9},{12,13},{9,10},{13,14},{20,21},{24,25},{28,29},{25,26}... | collective-permute-start | bytes 1572872 | tf_op jit(solution)/shard_map/ppermute | solution.py:306
  24.1 0.1 collective-permute-start.2
  24.1 0.7 collective-permute-start.3
  24.8 12.1 %collective-permute-done.2.c_ref = f32[128,512]{1,0:T(8,128)S(1)} collective-permute-done((f32[128,512]{1,0:T(8,128)S(1)}, f32[128,512]{1,0:T(8,128)S(1)}, u32[]{:S(2)}, u32[]{:S(2)}) %collective-permute-start.2) | collective-permute-done | bytes 262176 | tf_op jit(solution)/shard_map/ppermute | solution.py:312
  36.9 0.6 shard_map.98
  37.6 1.3 %collective-permute-start.6 = (f32[64,512]{1,0:T(8,128)S(1)}, f32[64,512]{1,0:T(8,128)S(1)}, u32[]{:S(2)}, u32[]{:S(2)}) collective-permute-start(f32[64,512]{1,0:T(8,128)S(1)} %get-tuple-element.26.a_ref), channel_id=1, source_target_pairs={{0,2},{3,1},{4,6},{7,5},{8,10},{11,9},{12,14},{15,13},{16,18},{19,... | collective-permute-start | bytes 393224 | tf_op jit(solution)/shard_map/ppermute | solution.py:315
  38.9 1.9 %collective-permute-start.5 = (f32[64,512]{1,0:T(8,128)S(1)}, f32[64,512]{1,0:T(8,128)S(1)}, u32[]{:S(2)}, u32[]{:S(2)}) collective-permute-start(f32[64,512]{1,0:T(8,128)S(1)} %get-tuple-element.27), channel_id=1, source_target_pairs={{1,2},{2,1},{5,6},{6,5},{9,10},{10,9},{13,14},{14,13},{17,18},{18,... | collective-permute-start | bytes 393224 | tf_op jit(solution)/shard_map/ppermute | solution.py:315
  40.8 1.3 %collective-permute-start.4 = (f32[64,512]{1,0:T(8,128)S(1)}, f32[64,512]{1,0:T(8,128)S(1)}, u32[]{:S(2)}, u32[]{:S(2)}) collective-permute-start(f32[64,512]{1,0:T(8,128)S(1)} %get-tuple-element.27), channel_id=1, source_target_pairs={{0,1},{3,2},{4,5},{7,6},{8,9},{11,10},{12,13},{15,14},{16,17},{19,... | collective-permute-start | bytes 393224 | tf_op jit(solution)/shard_map/ppermute | solution.py:315
  42.1 2.2 %collective-permute-done.6.d_ref = f32[64,512]{1,0:T(8,128)S(1)} collective-permute-done((f32[64,512]{1,0:T(8,128)S(1)}, f32[64,512]{1,0:T(8,128)S(1)}, u32[]{:S(2)}, u32[]{:S(2)}) %collective-permute-start.6) | collective-permute-done | bytes 131104 | tf_op jit(solution)/shard_map/ppermute | solution.py:315
  44.3 7.1 %collective-permute-done.5.c_ref = f32[64,512]{1,0:T(8,128)S(1)} collective-permute-done((f32[64,512]{1,0:T(8,128)S(1)}, f32[64,512]{1,0:T(8,128)S(1)}, u32[]{:S(2)}, u32[]{:S(2)}) %collective-permute-start.5) | collective-permute-done | bytes 131104 | tf_op jit(solution)/shard_map/ppermute | solution.py:315
  51.4 0.0 collective-permute-done.4.b_ref
  51.4 0.6 shard_map.99
  52.0 0.0 collective-permute-done.7.nm_ref
  52.0 1.6 %collective-permute-start.10 = (f32[256,512]{1,0:T(8,128)S(1)}, f32[256,512]{1,0:T(8,128)S(1)}, u32[]{:S(2)}, u32[]{:S(2)}) collective-permute-start(f32[256,512]{1,0:T(8,128)S(1)} %collective-permute-done.7.nm_ref), channel_id=1, source_target_pairs={{0,16},{16,0},{1,17},{17,1},{2,18},{18,2},{3,19},{19,3},{4,20},{20... | collective-permute-start | bytes 1572872 | tf_op jit(solution)/shard_map/ppermute | solution.py:303
  53.6 0.1 collective-permute-start.11
  53.7 0.7 collective-permute-start.9
  54.3 0.0 collective-permute-done.9.h_ref
  54.3 0.8 collective-permute-done.10.no_ref
  55.1 0.7 collective-permute-done.11.fo_ref
  55.9 0.6 shard_map.100.x_ref
  56.4 1.3 %collective-permute-start.13 = (f32[64,512]{1,0:T(8,128)S(1)}, f32[64,512]{1,0:T(8,128)S(1)}, u32[]{:S(2)}, u32[]{:S(2)}) collective-permute-start(f32[64,512]{1,0:T(8,128)S(1)} %shard_map.100.x_ref), channel_id=1, source_target_pairs={{1,9},{2,10},{5,13},{6,14},{17,25},{18,26},{21,29},{22,30}} | collective-permute-start | bytes 393224 | tf_op jit(solution)/shard_map/ppermute | solution.py:306
  57.7 1.3 %collective-permute-start.12 = (f32[64,512]{1,0:T(8,128)S(1)}, f32[64,512]{1,0:T(8,128)S(1)}, u32[]{:S(2)}, u32[]{:S(2)}) collective-permute-start(f32[64,512]{1,0:T(8,128)S(1)} %shard_map.100.x_ref), channel_id=1, source_target_pairs={{5,9},{6,10},{1,13},{2,14},{21,25},{22,26},{17,29},{18,30}} | collective-permute-start | bytes 393224 | tf_op jit(solution)/shard_map/ppermute | solution.py:306
  59.0 10.3 %collective-permute-done.13.ha_ref = f32[64,512]{1,0:T(8,128)S(1)} collective-permute-done((f32[64,512]{1,0:T(8,128)S(1)}, f32[64,512]{1,0:T(8,128)S(1)}, u32[]{:S(2)}, u32[]{:S(2)}) %collective-permute-start.13) | collective-permute-done | bytes 131104 | tf_op jit(solution)/shard_map/ppermute | solution.py:306
  69.3 0.6 shard_map.102.x_ref
  69.9 1.3 %collective-permute-start.14 = (f32[64,512]{1,0:T(8,128)S(1)}, f32[64,512]{1,0:T(8,128)S(1)}, u32[]{:S(2)}, u32[]{:S(2)}) collective-permute-start(f32[64,512]{1,0:T(8,128)S(1)} %shard_map.102.x_ref), channel_id=1, source_target_pairs={{9,13},{10,14},{25,29},{26,30}} | collective-permute-start | bytes 393224 | tf_op jit(solution)/shard_map/ppermute | solution.py:306
  71.2 1.4 %shard_map.101.res_ref = f32[64,512]{1,0:T(8,128)S(1)} custom-call(s32[3]{0:T(128)S(1)} %copy-done.4, f32[64,512]{1,0:T(8,128)S(1)} %get-tuple-element.28.res_ref, f32[64,512]{1,0:T(8,128)S(1)} %collective-permute-done.12.hb_ref, f32[64,512]{1,0:T(8,128)S(1)} %collective-permute-done.13.ha_ref, f32[512,512]{1,0:T(8,128)S(1)} %copy-done.1, ...), custom_call_target="tpu_custom_call" | custom-call | bytes 3538956 | tf_op jit(solution)/shard_map/pallas_call | solution.py:279
  72.5 3.8 %collective-permute-done.14.h_ref = f32[64,512]{1,0:T(8,128)S(1)} collective-permute-done((f32[64,512]{1,0:T(8,128)S(1)}, f32[64,512]{1,0:T(8,128)S(1)}, u32[]{:S(2)}, u32[]{:S(2)}) %collective-permute-start.14) | collective-permute-done | bytes 131104 | tf_op jit(solution)/shard_map/ppermute | solution.py:306
  76.3 1.5 %shard_map.103.x_ref = f32[64,512]{1,0:T(8,128)S(1)} custom-call(s32[3]{0:T(128)S(1)} %copy-done.4, f32[64,512]{1,0:T(8,128)S(1)} %shard_map.101.res_ref, f32[64,512]{1,0:T(8,128)S(1)} %shard_map.102.x_ref, f32[512,512]{1,0:T(8,128)S(1)} %copy-done, f32[64,512]{1,0:T(8,128)S(1)} %collective-permute-done.14.h_ref, f32[512,512]{1,0:T(8,128)S(1)} %copy-done.1, ...), custom_call_target="tpu_custom_call" | custom-call | bytes 3538956 | tf_op jit(solution)/shard_map/pallas_call | solution.py:279
  77.8 1.3 %collective-permute-start.17 = (f32[64,512]{1,0:T(8,128)S(1)}, f32[64,512]{1,0:T(8,128)S(1)}, u32[]{:S(2)}, u32[]{:S(2)}) collective-permute-start(f32[64,512]{1,0:T(8,128)S(1)} %shard_map.103.x_ref), channel_id=1, source_target_pairs={{1,3},{2,0},{5,7},{6,4},{9,11},{10,8},{13,15},{14,12},{17,19},{18,... | collective-permute-start | bytes 393224 | tf_op jit(solution)/shard_map/ppermute | solution.py:315
  79.1 1.9 %collective-permute-start.16 = (f32[64,512]{1,0:T(8,128)S(1)}, f32[64,512]{1,0:T(8,128)S(1)}, u32[]{:S(2)}, u32[]{:S(2)}) collective-permute-start(f32[64,512]{1,0:T(8,128)S(1)} %shard_map.103.x_ref), channel_id=1, source_target_pairs={{1,2},{2,1},{5,6},{6,5},{9,10},{10,9},{13,14},{14,13},{17,18},{18,... | collective-permute-start | bytes 393224 | tf_op jit(solution)/shard_map/ppermute | solution.py:315
  81.0 1.3 %collective-permute-start.15 = (f32[64,512]{1,0:T(8,128)S(1)}, f32[64,512]{1,0:T(8,128)S(1)}, u32[]{:S(2)}, u32[]{:S(2)}) collective-permute-start(f32[64,512]{1,0:T(8,128)S(1)} %shard_map.103.x_ref), channel_id=1, source_target_pairs={{1,0},{2,3},{5,4},{6,7},{9,8},{10,11},{13,12},{14,15},{17,16},{18,... | collective-permute-start | bytes 393224 | tf_op jit(solution)/shard_map/ppermute | solution.py:315
  82.3 2.5 %collective-permute-done.16.b_ref = f32[64,512]{1,0:T(8,128)S(1)} collective-permute-done((f32[64,512]{1,0:T(8,128)S(1)}, f32[64,512]{1,0:T(8,128)S(1)}, u32[]{:S(2)}, u32[]{:S(2)}) %collective-permute-start.16) | collective-permute-done | bytes 131104 | tf_op jit(solution)/shard_map/ppermute | solution.py:315
  84.8 0.7 shard_map.104.own_ref
  85.5 2.6 %collective-permute-start.18 = (f32[512,128]{1,0:T(8,128)S(1)}, f32[512,128]{1,0:T(8,128)S(1)}, u32[]{:S(2)}, u32[]{:S(2)}) collective-permute-start(f32[512,128]{1,0:T(8,128)S(1)} %shard_map.104.own_ref), channel_id=1, source_target_pairs={{0,16},{16,0},{1,17},{17,1},{2,18},{18,2},{3,19},{19,3},{4,20},{20... | collective-permute-start | bytes 786440 | tf_op jit(solution)/shard_map/ppermute | solution.py:303
  88.1 1.2 %collective-permute-done.18.other_ref = f32[512,128]{1,0:T(8,128)S(1)} collective-permute-done((f32[512,128]{1,0:T(8,128)S(1)}, f32[512,128]{1,0:T(8,128)S(1)}, u32[]{:S(2)}, u32[]{:S(2)}) %collective-permute-start.18) | collective-permute-done | bytes 262176 | tf_op jit(solution)/shard_map/ppermute | solution.py:303
  89.2 1.4 %shard_map.105 = f32[512,256]{1,0:T(8,128)} custom-call(s32[3]{0:T(128)S(1)} %copy-done.4, f32[512,128]{1,0:T(8,128)S(1)} %shard_map.104.own_ref, f32[512,128]{1,0:T(8,128)S(1)} %collective-permute-done.18.other_ref), custom_call_target="tpu_custom_call" | custom-call | bytes 524300 | tf_op jit(solution)/shard_map/pallas_call | solution.py:279
  (14 shorter events, 0.0 us)
Async XLA Ops:
  1.3 6.4 %copy-start.4 = (s32[3]{0:T(128)S(1)}, s32[3]{0:T(128)}, u32[]{:S(2)}) copy-start(s32[3]{0:T(128)} %pad_add_fusion.where_ref) | copy-start | bytes 40
  1.3 6.4 %copy-start.5 = (s32[2,256]{1,0:T(2,128)S(1)}, s32[2,256]{1,0:T(2,128)}, u32[]{:S(2)}) copy-start(s32[2,256]{1,0:T(2,128)} %tgt_ref.3) | copy-start | bytes 6148
  1.3 16.7 %copy-start.1 = (f32[512,512]{1,0:T(8,128)S(1)}, f32[512,512]{1,0:T(8,128)}, u32[]{:S(2)}) copy-start(f32[512,512]{1,0:T(8,128)} %factor_ref.7) | copy-start | bytes 3145732
  5.5 12.5 %copy-start.2 = (f32[512,256]{1,0:T(8,128)S(1)}, f32[512,256]{1,0:T(8,128)}, u32[]{:S(2)}) copy-start(f32[512,256]{1,0:T(8,128)} %rhs_ref.1) | copy-start | bytes 1572868
  5.5 2.1 %collective-permute-start = (f32[136,512]{1,0:T(8,128)}, f32[136,512]{1,0:T(8,128)S(1)}, u32[]{:S(2)}, u32[]{:S(2)}) collective-permute-start(f32[136,512]{1,0:T(8,128)} %get-tuple-element.20), channel_id=1, source_target_pairs={{0,16},{16,0},{1,17},{17,1},{2,18},{18,2},{3,19},{19,3},{4,20},{20... | collective-permute-start | bytes 835592 | tf_op jit(solution)/shard_map/ppermute | solution.py:303
  7.6 1.0 %copy-start.3 = (f32[128,512]{1,0:T(8,128)S(1)}, f32[128,512]{1,0:T(8,128)}, u32[]{:S(2)}) copy-start(f32[128,512]{1,0:T(8,128)} %get-tuple-element.19.keep_ref) | copy-start | bytes 786436
  10.4 40.9 %copy-start = (f32[512,512]{1,0:T(8,128)S(1)}, f32[512,512]{1,0:T(8,128)}, u32[]{:S(2)}) copy-start(f32[512,512]{1,0:T(8,128)} %diag_ref.7) | copy-start | bytes 3145732
  10.4 7.6 %collective-permute-start.1 = (f32[128,512]{1,0:T(8,128)S(1)}, f32[128,512]{1,0:T(8,128)S(1)}, u32[]{:S(2)}, u32[]{:S(2)}) collective-permute-start(f32[128,512]{1,0:T(8,128)S(1)} %get-tuple-element.21), channel_id=1, source_target_pairs={{0,4},{4,0},{8,12},{12,8},{1,5},{5,1},{9,13},{13,9},{2,6},{6,2},{1... | collective-permute-start | bytes 786440 | tf_op jit(solution)/shard_map/ppermute | solution.py:312
  18.8 33.2 %collective-permute-start.8 = (f32[256,512]{1,0:T(8,128)S(1)}, f32[256,512]{1,0:T(8,128)S(1)}, u32[]{:S(2)}, u32[]{:S(2)}) collective-permute-start(f32[256,512]{1,0:T(8,128)S(1)} %get-tuple-element.29), channel_id=1, source_target_pairs={{4,6},{8,10},{12,14},{14,13},{20,22},{24,26},{28,30},{30,29}} | collective-permute-start | bytes 1572872 | tf_op jit(solution)/shard_map/ppermute | solution.py:306
  20.1 31.9 %collective-permute-start.7 = (f32[256,512]{1,0:T(8,128)S(1)}, f32[256,512]{1,0:T(8,128)S(1)}, u32[]{:S(2)}, u32[]{:S(2)}) collective-permute-start(f32[256,512]{1,0:T(8,128)S(1)} %get-tuple-element.29), channel_id=1, source_target_pairs={{4,5},{8,9},{12,13},{9,10},{13,14},{20,21},{24,25},{28,29},{25,26}... | collective-permute-start | bytes 1572872 | tf_op jit(solution)/shard_map/ppermute | solution.py:306
  24.1 12.9 %collective-permute-start.2 = (f32[128,512]{1,0:T(8,128)S(1)}, f32[128,512]{1,0:T(8,128)S(1)}, u32[]{:S(2)}, u32[]{:S(2)}) collective-permute-start(f32[128,512]{1,0:T(8,128)S(1)} %get-tuple-element.24), channel_id=1, source_target_pairs={{0,8},{4,12},{8,0},{12,4},{1,9},{5,13},{9,1},{13,5},{2,10},{6,14},... | collective-permute-start | bytes 786440 | tf_op jit(solution)/shard_map/ppermute | solution.py:312
  24.1 12.8 %collective-permute-start.3 = (f32[128,512]{1,0:T(8,128)S(1)}, f32[128,512]{1,0:T(8,128)S(1)}, u32[]{:S(2)}, u32[]{:S(2)}) collective-permute-start(f32[128,512]{1,0:T(8,128)S(1)} %get-tuple-element.25), channel_id=1, source_target_pairs={{0,12},{4,8},{8,4},{12,0},{1,13},{5,9},{9,5},{13,1},{2,14},{6,10},... | collective-permute-start | bytes 786440 | tf_op jit(solution)/shard_map/ppermute | solution.py:312
  37.6 6.7 %collective-permute-start.6 = (f32[64,512]{1,0:T(8,128)S(1)}, f32[64,512]{1,0:T(8,128)S(1)}, u32[]{:S(2)}, u32[]{:S(2)}) collective-permute-start(f32[64,512]{1,0:T(8,128)S(1)} %get-tuple-element.26.a_ref), channel_id=1, source_target_pairs={{0,2},{3,1},{4,6},{7,5},{8,10},{11,9},{12,14},{15,13},{16,18},{19,... | collective-permute-start | bytes 393224 | tf_op jit(solution)/shard_map/ppermute | solution.py:315
  38.9 12.5 %collective-permute-start.5 = (f32[64,512]{1,0:T(8,128)S(1)}, f32[64,512]{1,0:T(8,128)S(1)}, u32[]{:S(2)}, u32[]{:S(2)}) collective-permute-start(f32[64,512]{1,0:T(8,128)S(1)} %get-tuple-element.27), channel_id=1, source_target_pairs={{1,2},{2,1},{5,6},{6,5},{9,10},{10,9},{13,14},{14,13},{17,18},{18,... | collective-permute-start | bytes 393224 | tf_op jit(solution)/shard_map/ppermute | solution.py:315
  40.8 10.6 %collective-permute-start.4 = (f32[64,512]{1,0:T(8,128)S(1)}, f32[64,512]{1,0:T(8,128)S(1)}, u32[]{:S(2)}, u32[]{:S(2)}) collective-permute-start(f32[64,512]{1,0:T(8,128)S(1)} %get-tuple-element.27), channel_id=1, source_target_pairs={{0,1},{3,2},{4,5},{7,6},{8,9},{11,10},{12,13},{15,14},{16,17},{19,... | collective-permute-start | bytes 393224 | tf_op jit(solution)/shard_map/ppermute | solution.py:315
  52.0 3.2 %collective-permute-start.10 = (f32[256,512]{1,0:T(8,128)S(1)}, f32[256,512]{1,0:T(8,128)S(1)}, u32[]{:S(2)}, u32[]{:S(2)}) collective-permute-start(f32[256,512]{1,0:T(8,128)S(1)} %collective-permute-done.7.nm_ref), channel_id=1, source_target_pairs={{0,16},{16,0},{1,17},{17,1},{2,18},{18,2},{3,19},{19,3},{4,20},{20... | collective-permute-start | bytes 1572872 | tf_op jit(solution)/shard_map/ppermute | solution.py:303
  53.6 2.3 %collective-permute-start.11 = (f32[256,512]{1,0:T(8,128)S(1)}, f32[256,512]{1,0:T(8,128)S(1)}, u32[]{:S(2)}, u32[]{:S(2)}) collective-permute-start(f32[256,512]{1,0:T(8,128)S(1)} %collective-permute-done.8.fm_ref), channel_id=1, source_target_pairs={{0,16},{16,0},{1,17},{17,1},{2,18},{18,2},{3,19},{19,3},{4,20},{20... | collective-permute-start | bytes 1572872 | tf_op jit(solution)/shard_map/ppermute | solution.py:303
  53.7 0.7 collective-permute-start.9
  56.4 12.9 %collective-permute-start.13 = (f32[64,512]{1,0:T(8,128)S(1)}, f32[64,512]{1,0:T(8,128)S(1)}, u32[]{:S(2)}, u32[]{:S(2)}) collective-permute-start(f32[64,512]{1,0:T(8,128)S(1)} %shard_map.100.x_ref), channel_id=1, source_target_pairs={{1,9},{2,10},{5,13},{6,14},{17,25},{18,26},{21,29},{22,30}} | collective-permute-start | bytes 393224 | tf_op jit(solution)/shard_map/ppermute | solution.py:306
  57.7 11.6 %collective-permute-start.12 = (f32[64,512]{1,0:T(8,128)S(1)}, f32[64,512]{1,0:T(8,128)S(1)}, u32[]{:S(2)}, u32[]{:S(2)}) collective-permute-start(f32[64,512]{1,0:T(8,128)S(1)} %shard_map.100.x_ref), channel_id=1, source_target_pairs={{5,9},{6,10},{1,13},{2,14},{21,25},{22,26},{17,29},{18,30}} | collective-permute-start | bytes 393224 | tf_op jit(solution)/shard_map/ppermute | solution.py:306
  69.9 6.5 %collective-permute-start.14 = (f32[64,512]{1,0:T(8,128)S(1)}, f32[64,512]{1,0:T(8,128)S(1)}, u32[]{:S(2)}, u32[]{:S(2)}) collective-permute-start(f32[64,512]{1,0:T(8,128)S(1)} %shard_map.102.x_ref), channel_id=1, source_target_pairs={{9,13},{10,14},{25,29},{26,30}} | collective-permute-start | bytes 393224 | tf_op jit(solution)/shard_map/ppermute | solution.py:306
  77.8 4.5 %collective-permute-start.17 = (f32[64,512]{1,0:T(8,128)S(1)}, f32[64,512]{1,0:T(8,128)S(1)}, u32[]{:S(2)}, u32[]{:S(2)}) collective-permute-start(f32[64,512]{1,0:T(8,128)S(1)} %shard_map.103.x_ref), channel_id=1, source_target_pairs={{1,3},{2,0},{5,7},{6,4},{9,11},{10,8},{13,15},{14,12},{17,19},{18,... | collective-permute-start | bytes 393224 | tf_op jit(solution)/shard_map/ppermute | solution.py:315
  79.1 5.7 %collective-permute-start.16 = (f32[64,512]{1,0:T(8,128)S(1)}, f32[64,512]{1,0:T(8,128)S(1)}, u32[]{:S(2)}, u32[]{:S(2)}) collective-permute-start(f32[64,512]{1,0:T(8,128)S(1)} %shard_map.103.x_ref), channel_id=1, source_target_pairs={{1,2},{2,1},{5,6},{6,5},{9,10},{10,9},{13,14},{14,13},{17,18},{18,... | collective-permute-start | bytes 393224 | tf_op jit(solution)/shard_map/ppermute | solution.py:315
  81.0 3.8 %collective-permute-start.15 = (f32[64,512]{1,0:T(8,128)S(1)}, f32[64,512]{1,0:T(8,128)S(1)}, u32[]{:S(2)}, u32[]{:S(2)}) collective-permute-start(f32[64,512]{1,0:T(8,128)S(1)} %shard_map.103.x_ref), channel_id=1, source_target_pairs={{1,0},{2,3},{5,4},{6,7},{9,8},{10,11},{13,12},{14,15},{17,16},{18,... | collective-permute-start | bytes 393224 | tf_op jit(solution)/shard_map/ppermute | solution.py:315
  85.5 3.7 %collective-permute-start.18 = (f32[512,128]{1,0:T(8,128)S(1)}, f32[512,128]{1,0:T(8,128)S(1)}, u32[]{:S(2)}, u32[]{:S(2)}) collective-permute-start(f32[512,128]{1,0:T(8,128)S(1)} %shard_map.104.own_ref), channel_id=1, source_target_pairs={{0,16},{16,0},{1,17},{17,1},{2,18},{18,2},{3,19},{19,3},{4,20},{20... | collective-permute-start | bytes 786440 | tf_op jit(solution)/shard_map/ppermute | solution.py:303

commit v4 on v3

--- a/solution.py
+++ b/solution.py
@@ -97,12 +97,11 @@
     return jnp.where(col <= row, matrix, 0.0)
 
 
-def pack_kernel(where_ref, factor_ref, rhs_ref, after_ref, part_ref, rhs_out_ref, turned_ref):
+def turn_kernel(where_ref, rhs_ref, out_ref, turned_ref):
     leaf, z = where_ref[0], where_ref[2]
-    part, half, piece = part_ref.shape[0], turned_ref.shape[0], rhs_out_ref.shape[0]
-    part_ref[...] = factor_ref[pl.ds(pl.multiple_of(leaf * part, part), part), :]
+    half, piece = turned_ref.shape[0], out_ref.shape[0]
     turned_ref[...] = rhs_ref[:, pl.ds(pl.multiple_of(leaf * half, half), half)].T
-    rhs_out_ref[...] = turned_ref[pl.ds(pl.multiple_of((z // 2) * piece, piece), piece), :]
+    out_ref[...] = turned_ref[pl.ds(pl.multiple_of((z // 2) * piece, piece), piece), :]
 
 
 def child_kernel(where_ref, live_ref, rhs_hbm, diag_hbm, off_hbm, tgt_ref, sol_ref, keep_ref, send_ref,
@@ -163,15 +162,6 @@
     second_ref[...] = sum_ref[pl.ds(pl.multiple_of((1 - odd) * piece, piece), piece), :]
 
 
-def halves(x, mine_ref, other_ref, leaf, out_ref):
-    part = out_ref.shape[1] // 2
-    for ref, at in ((mine_ref, leaf), (other_ref, 1 - leaf)):
-        start = pl.multiple_of(at * part, part)
-        block = ref[0:part, :]
-        out_ref[:, pl.ds(start, part)] = dot3(x, block, NT)
-    return out_ref[...]
-
-
 def zeroth_kernel(where_ref, rhs_ref, a_ref, b_ref, c_ref, d_ref, diag_ref, res_ref, x_ref):
     row = where_ref[1]
     res = rhs_ref[...] - ((a_ref[...] + b_ref[...]) + (c_ref[...] + d_ref[...]))
@@ -183,76 +173,56 @@
         x_ref[...] = res + dot3(res, lower(diag_ref[...]), NT)
 
 
-def first_kernel(where_ref, res_ref, x_ref, diag_ref, h_ref, nm_ref, no_ref, fm_ref, fo_ref, out_ref, left_ref, tmp_ref):
-    leaf, row, z = where_ref[0], where_ref[1], where_ref[2]
+def column(where_ref, block, own_ref, got_ref, other_ref):
+    leaf, z = where_ref[0], where_ref[2]
+    if block == 0:
+        return jnp.where((leaf == 0) == (z == 1), got_ref[...], other_ref[...])
+    sent = jnp.where((leaf == 0) == (block == 1), got_ref[...], other_ref[...])
+    return jnp.where(z == block, own_ref[...], sent)
+
+
+def first_kernel(where_ref, res_ref, x_ref, diag_ref, h_ref, *refs):
+    row, z = where_ref[1], where_ref[2]
+    blocks, out_ref = refs[:3], refs[3]
     out_ref[...] = x_ref[...]
 
     @pl.when((row == 1) & ((z == 1) | (z == 2)))
     def _():
-        @pl.when(z == 1)
-        def _():
-            left_ref[...] = res_ref[...] - halves(h_ref[...], nm_ref, no_ref, leaf, tmp_ref)
-
-        @pl.when(z == 2)
-        def _():
-            left_ref[...] = res_ref[...] - halves(h_ref[...], fm_ref, fo_ref, leaf, tmp_ref)
-
-        value = left_ref[...]
+        value = res_ref[...] - dot3(h_ref[...], column(where_ref, 0, *blocks), NT)
         out_ref[...] = value + dot3(value, lower(diag_ref[...]), NT)
 
 
-def earlier(res, x0, x1, leaf, z, refs, out_ref, tmp_ref):
-    factor_ref, nm_ref, no_ref, fm_ref, fo_ref = refs
-
-    @pl.when(z == 1)
-    def _():
-        value = res - halves(x0, nm_ref, no_ref, leaf, tmp_ref)
-        out_ref[...] = value - dot3(x1, factor_ref[...], NT)
-
-    @pl.when(z == 2)
-    def _():
-        value = res - halves(x0, fm_ref, fo_ref, leaf, tmp_ref)
-        out_ref[...] = value - halves(x1, nm_ref, no_ref, leaf, tmp_ref)
-
-
-def second_kernel(where_ref, res_ref, x_ref, diag_ref, hb_ref, ha_ref, factor_ref, nm_ref, no_ref, fm_ref, fo_ref,
-                  out_ref, left_ref, tmp_ref):
-    leaf, row, z = where_ref[0], where_ref[1], where_ref[2]
+def second_kernel(where_ref, res_ref, x_ref, diag_ref, hb_ref, ha_ref, *refs):
+    row, z = where_ref[1], where_ref[2]
+    blocks, out_ref = refs[:3], refs[3]
     out_ref[...] = x_ref[...]
 
     @pl.when((row == 2) & ((z == 1) | (z == 2)))
     def _():
-        refs = (factor_ref, nm_ref, no_ref, fm_ref, fo_ref)
-        earlier(res_ref[...], ha_ref[...], hb_ref[...], leaf, z, refs, left_ref, tmp_ref)
-        value = left_ref[...]
+        value = res_ref[...] - dot3(ha_ref[...], column(where_ref, 0, *blocks), NT)
+        value = value - dot3(hb_ref[...], column(where_ref, 1, *blocks), NT)
         out_ref[...] = value + dot3(value, lower(diag_ref[...]), NT)
 
 
-def third_kernel(where_ref, res_ref, hb_ref, ha_ref, factor_ref, nm_ref, no_ref, fm_ref, fo_ref, out_ref, tmp_ref):
-    leaf, row, z = where_ref[0], where_ref[1], where_ref[2]
+def third_kernel(where_ref, res_ref, hb_ref, ha_ref, *refs):
+    row, z = where_ref[1], where_ref[2]
+    blocks, out_ref = refs[:3], refs[3]
     out_ref[...] = res_ref[...]
 
-    @pl.when(row == 3)
-    def _():
-        refs = (factor_ref, nm_ref, no_ref, fm_ref, fo_ref)
-        earlier(res_ref[...], hb_ref[...], ha_ref[...], leaf, z, refs, out_ref, tmp_ref)
-
-
-def fourth_kernel(where_ref, res_ref, x_ref, diag_ref, h_ref, factor_ref, fm_ref, fo_ref, out_ref, left_ref, tmp_ref):
-    leaf, row, z = where_ref[0], where_ref[1], where_ref[2]
+    @pl.when((row == 3) & ((z == 1) | (z == 2)))
+    def _():
+        value = res_ref[...] - dot3(hb_ref[...], column(where_ref, 0, *blocks), NT)
+        out_ref[...] = value - dot3(ha_ref[...], column(where_ref, 1, *blocks), NT)
+
+
+def fourth_kernel(where_ref, res_ref, x_ref, diag_ref, h_ref, *refs):
+    row, z = where_ref[1], where_ref[2]
+    blocks, out_ref = refs[:3], refs[3]
     out_ref[...] = x_ref[...]
 
     @pl.when((row == 3) & ((z == 1) | (z == 2)))
     def _():
-        @pl.when(z == 1)
-        def _():
-            left_ref[...] = res_ref[...] - halves(h_ref[...], fm_ref, fo_ref, leaf, tmp_ref)
-
-        @pl.when(z == 2)
-        def _():
-            left_ref[...] = res_ref[...] - dot3(h_ref[...], factor_ref[...], NT)
-
-        value = left_ref[...]
+        value = res_ref[...] - dot3(h_ref[...], column(where_ref, 2, *blocks), NT)
         out_ref[...] = value + dot3(value, lower(diag_ref[...]), NT)
 
 
@@ -314,6 +284,12 @@
     def along_col(value, pairs):
         return lax.ppermute(value, "col", pairs)
 
+    near = [(at(k, 0), at(k, 1)) for k in (1, 2, 3)] + [(at(k, 1), at(k, 2)) for k in (2, 3)]
+    far = [(at(k, 0), at(k, 2)) for k in (1, 2, 3)] + [(at(3, 2), at(3, 1))]
+    shift = rows * cols
+    sent = lax.ppermute(
+        top_factor, ("leaf", "row", "col"), near + [(a + shift, b + shift) for a, b in far]
+    )
     child_sol, keep, send = call(
         child_kernel,
         [where, live, child_rhs, child_diag, child_off, targets],
@@ -326,19 +302,7 @@
     sums = call(scatter_kernel, [where, keep, swap(send), targets], [(half, size)] * rows)
     got = [along_row(sums[s], [(i, i ^ s) for i in range(rows)]) for s in (1, 2, 3)]
 
-    part, rhs_piece = call(
-        pack_kernel,
-        [where, top_factor, top_rhs, got[0]],
-        [(size // 2, size), (piece, size)],
-        [(half, size)],
-        outside=(3,),
-    )
-    near = plane(
-        part,
-        [(at(k, 0), at(k, 1)) for k in (1, 2, 3)] + [(at(k, 1), at(k, 2)) for k in (2, 3)],
-    )
-    far = plane(part, [(at(k, 0), at(k, 2)) for k in (1, 2, 3)] + [(at(3, 2), at(3, 1))])
-
+    (rhs_piece,) = call(turn_kernel, [where, top_rhs], [(piece, size)], [(half, size)])
     first, second = call(
         pieces_kernel, [where, sums[0]] + got, [(piece, size)] * 2, [(half, size)]
     )
@@ -350,21 +314,15 @@
     shape = (piece, size)
     res, x = call(zeroth_kernel, [where, rhs_piece, second] + q + [top_diag], [shape] * 2)
     h = hop(x, [(0, 1)])
-    near, far, x = lax.optimization_barrier((near, far, x))
-    moved = [near, swap(near), far, swap(far)]
-    (x,) = call(
-        first_kernel, [where, res, x, top_diag, h] + moved, [shape], [shape] * 2
-    )
+    sent, x = lax.optimization_barrier((sent, x))
+    blocks = [top_factor, sent, swap(sent)]
+    (x,) = call(first_kernel, [where, res, x, top_diag, h] + blocks, [shape])
     hb = hop(x, [(1, 2), (0, 3)])
     ha = hop(x, [(0, 2), (1, 3)])
-    (x,) = call(
-        second_kernel, [where, res, x, top_diag, hb, ha, top_factor] + moved, [shape], [shape] * 2
-    )
+    (x,) = call(second_kernel, [where, res, x, top_diag, hb, ha] + blocks, [shape])
     h = hop(x, [(2, 3)])
-    (res,) = call(third_kernel, [where, res, hb, ha, top_factor] + moved, [shape], [shape])
-    (x,) = call(
-        fourth_kernel, [where, res, x, top_diag, h, top_factor] + moved[2:], [shape], [shape] * 2
-    )
+    (res,) = call(third_kernel, [where, res, hb, ha] + blocks, [shape])
+    (x,) = call(fourth_kernel, [where, res, x, top_diag, h] + blocks, [shape])
     z = [
         along_col(x, [(1, 0), (2, 3)]),
         along_col(x, [(1, 2), (2, 1)]),

time: 92.3 us -> 81.3 us (0.88)
  the two profiles are of different devices: /device:TPU:15 before, /device:TPU:7 now
where the time goes in v4:
time: 81.3 us; the launch traced here: 81 us
  waiting for transfers between devices  42.9 us (53%)
  starting transfers between devices  23.5 us (29%)
  Pallas kernels  12.1 us (15%)
  local copies, waits for them, and re-layouts  0.98 us (1%)
  between operations  0.9 us (1%)
    ppermute x6, waiting for transfers between devices, along_col(): return lax.ppermute(value, 'col', pairs)  27.6 us
    pallas_call x11, Pallas kernels, call(): pl.pallas_call(kernel, out_shape=[jax.ShapeDtypeStruct(shape, F32) for sh...  12.1 us
    ppermute x3, waiting for transfers between devices, along_row(): return lax.ppermute(value, 'row', pairs)  10.7 us
    ppermute x6, starting transfers between devices, along_col(): return lax.ppermute(value, 'col', pairs)  9.01 us
    ppermute x3, starting transfers between devices, swap(): return lax.ppermute(value, 'leaf', [(0, 1), (1, 0)])  4.82 us
    ppermute x3, waiting for transfers between devices, swap(): return lax.ppermute(value, 'leaf', [(0, 1), (1, 0)])  4.53 us
    ppermute x1, starting transfers between devices, central(): lax.ppermute(top_factor, ('leaf', 'row', 'col'), near + [(a + shift, b +...  4.28 us
    ppermute x3, starting transfers between devices, along_row(): return lax.ppermute(value, 'row', pairs)  2.71 us
  transfers between devices with their start and end apart: 17, of which 8 were waited for; matrix products, arithmetic and copies ran while one was open for 1% of the time, Pallas kernels for 10%

profile of v4, /device:TPU:7, one launch (start us, length us, event | category | flops | bytes accessed | tf_op | source)
XLA Modules:
  0.0 81.0 jit_solution(3927447452336147021)
XLA Ops:
  0.6 4.3 %collective-permute-start.7 = (f32[512,512]{1,0:T(8,128)}, f32[512,512]{1,0:T(8,128)S(1)}, u32[]{:S(2)}, u32[]{:S(2)}) collective-permute-start(f32[512,512]{1,0:T(8,128)} %refs_0_.7), channel_id=1, source_target_pairs={{4,5},{8,9},{12,13},{9,10},{13,14},{20,22},{24,26},{28,30},{30,29}} | collective-permute-start | bytes 3145736 | tf_op jit(solution)/shard_map/ppermute | solution.py:290
  4.9 0.6 pad_add_fusion.where_ref
  5.5 4.1 %shard_map.95 = (f32[2,256,256]{2,1,0:T(8,128)}, f32[128,512]{1,0:T(8,128)}, f32[136,512]{1,0:T(8,128)}) custom-call(s32[3]{0:T(128)} %pad_add_fusion.where_ref, s32[2]{0:T(128)} %live_ref.1, f32[2,256,256]{2,1,0:T(8,128)} %rhs_hbm.1, f32[2,256,256]{2,1,0:T(8,128)} %diag_hbm.1, f32[2,256,256]{2,1,0:T(8,128)} %off_hbm.1, s32[2,256]{1,0:T(2,128)} %tgt_ref.3), custom_call_target="tpu_custom_call" | custom-call | bytes 1574932 | tf_op jit(solution)/shard_map/pallas_call | solution.py:249
  9.6 0.0 copy-start.5
  9.6 0.1 collective-permute-start
  9.7 1.8 %collective-permute-done.recv_ref = f32[136,512]{1,0:T(8,128)S(1)} collective-permute-done((f32[136,512]{1,0:T(8,128)}, f32[136,512]{1,0:T(8,128)S(1)}, u32[]{:S(2)}, u32[]{:S(2)}) %collective-permute-start) | collective-permute-done | bytes 278560 | tf_op jit(solution)/shard_map/ppermute | solution.py:273
  11.5 0.9 %copy-done.3 = f32[128,512]{1,0:T(8,128)S(1)} copy-done((f32[128,512]{1,0:T(8,128)S(1)}, f32[128,512]{1,0:T(8,128)}, u32[]{:S(2)}) %copy-start.3) | copy-done | bytes 262168
  12.4 1.8 %shard_map.97 = (f32[128,512]{1,0:T(8,128)S(1)}, f32[128,512]{1,0:T(8,128)S(1)}, f32[128,512]{1,0:T(8,128)S(1)}, f32[128,512]{1,0:T(8,128)S(1)}) custom-call(s32[3]{0:T(128)S(1)} %copy-done.4, f32[128,512]{1,0:T(8,128)S(1)} %copy-done.3, f32[136,512]{1,0:T(8,128)S(1)} %collective-permute-done.recv_ref, s32[2,256]{1,0:T(2,128)S(1)} %copy-done.5), custom_call_target="tpu_custom_call" | custom-call | bytes 542732 | tf_op jit(solution)/shard_map/pallas_call | solution.py:249
  14.3 0.3 collective-permute-start.1
  14.6 0.0 collective-permute-start.2
  14.6 2.3 %collective-permute-start.3 = (f32[128,512]{1,0:T(8,128)S(1)}, f32[128,512]{1,0:T(8,128)S(1)}, u32[]{:S(2)}, u32[]{:S(2)}) collective-permute-start(f32[128,512]{1,0:T(8,128)S(1)} %get-tuple-element.21), channel_id=1, source_target_pairs={{0,12},{4,8},{8,4},{12,0},{1,13},{5,9},{9,5},{13,1},{2,14},{6,10},... | collective-permute-start | bytes 786440 | tf_op jit(solution)/shard_map/ppermute | solution.py:282
  17.0 5.1 %collective-permute-done.1.b_ref = f32[128,512]{1,0:T(8,128)S(1)} collective-permute-done((f32[128,512]{1,0:T(8,128)S(1)}, f32[128,512]{1,0:T(8,128)S(1)}, u32[]{:S(2)}, u32[]{:S(2)}) %collective-permute-start.1) | collective-permute-done | bytes 262176 | tf_op jit(solution)/shard_map/ppermute | solution.py:282
  22.1 0.0 collective-permute-done.2.c_ref
  22.1 5.6 %collective-permute-done.3.d_ref = f32[128,512]{1,0:T(8,128)S(1)} collective-permute-done((f32[128,512]{1,0:T(8,128)S(1)}, f32[128,512]{1,0:T(8,128)S(1)}, u32[]{:S(2)}, u32[]{:S(2)}) %collective-permute-start.3) | collective-permute-done | bytes 262176 | tf_op jit(solution)/shard_map/ppermute | solution.py:282
  27.7 0.6 shard_map.98
  28.3 1.9 %collective-permute-start.6 = (f32[64,512]{1,0:T(8,128)S(1)}, f32[64,512]{1,0:T(8,128)S(1)}, u32[]{:S(2)}, u32[]{:S(2)}) collective-permute-start(f32[64,512]{1,0:T(8,128)S(1)} %get-tuple-element.22.a_ref), channel_id=1, source_target_pairs={{0,2},{3,1},{4,6},{7,5},{8,10},{11,9},{12,14},{15,13},{16,18},{19,... | collective-permute-start | bytes 393224 | tf_op jit(solution)/shard_map/ppermute | solution.py:285
  30.2 0.0 copy-start.1
  30.2 0.8 collective-permute-start.5
  31.0 3.1 %collective-permute-start.4 = (f32[64,512]{1,0:T(8,128)S(1)}, f32[64,512]{1,0:T(8,128)S(1)}, u32[]{:S(2)}, u32[]{:S(2)}) collective-permute-start(f32[64,512]{1,0:T(8,128)S(1)} %get-tuple-element.23), channel_id=1, source_target_pairs={{0,1},{3,2},{4,5},{7,6},{8,9},{11,10},{12,13},{15,14},{16,17},{19,... | collective-permute-start | bytes 393224 | tf_op jit(solution)/shard_map/ppermute | solution.py:285
  34.1 0.7 shard_map.96.rhs_ref
  34.8 0.0 collective-permute-done.6.d_ref
  34.8 0.0 collective-permute-done.5.c_ref
  34.9 1.2 %collective-permute-done.4.b_ref = f32[64,512]{1,0:T(8,128)S(1)} collective-permute-done((f32[64,512]{1,0:T(8,128)S(1)}, f32[64,512]{1,0:T(8,128)S(1)}, u32[]{:S(2)}, u32[]{:S(2)}) %collective-permute-start.4) | collective-permute-done | bytes 131104 | tf_op jit(solution)/shard_map/ppermute | solution.py:285
  36.1 0.6 shard_map.99
  36.6 0.0 collective-permute-done.7.refs_1_
  36.7 2.4 %collective-permute-start.9 = (f32[512,512]{1,0:T(8,128)S(1)}, f32[512,512]{1,0:T(8,128)S(1)}, u32[]{:S(2)}, u32[]{:S(2)}) collective-permute-start(f32[512,512]{1,0:T(8,128)S(1)} %collective-permute-done.7.refs_1_), channel_id=1, source_target_pairs={{0,16},{16,0},{1,17},{17,1},{2,18},{18,2},{3,19},{19,3},{4,20},{20... | collective-permute-start | bytes 3145736 | tf_op jit(solution)/shard_map/ppermute | solution.py:273
  39.1 0.7 collective-permute-start.8
  39.8 0.0 collective-permute-done.8.h_ref
  39.8 1.6 %collective-permute-done.9.refs_2_ = f32[512,512]{1,0:T(8,128)S(1)} collective-permute-done((f32[512,512]{1,0:T(8,128)S(1)}, f32[512,512]{1,0:T(8,128)S(1)}, u32[]{:S(2)}, u32[]{:S(2)}) %collective-permute-start.9) | collective-permute-done | bytes 1048608 | tf_op jit(solution)/shard_map/ppermute | solution.py:273
  41.4 0.6 shard_map.100.x_ref
  41.9 0.7 collective-permute-start.11
  42.6 0.7 collective-permute-start.10
  43.3 0.0 collective-permute-done.11.ha_ref
  43.3 0.0 collective-permute-done.10.hb_ref
  43.3 0.6 shard_map.102.x_ref
  43.9 0.7 collective-permute-start.12
  44.6 0.6 shard_map.101.res_ref
  45.1 0.0 collective-permute-done.12.h_ref
  45.1 0.6 shard_map.103.x_ref
  45.7 1.3 %collective-permute-start.15 = (f32[64,512]{1,0:T(8,128)S(1)}, f32[64,512]{1,0:T(8,128)S(1)}, u32[]{:S(2)}, u32[]{:S(2)}) collective-permute-start(f32[64,512]{1,0:T(8,128)S(1)} %shard_map.103.x_ref), channel_id=1, source_target_pairs={{1,3},{2,0},{5,7},{6,4},{9,11},{10,8},{13,15},{14,12},{17,19},{18,... | collective-permute-start | bytes 393224 | tf_op jit(solution)/shard_map/ppermute | solution.py:285
  47.0 0.7 collective-permute-start.14
  47.7 1.3 %collective-permute-start.13 = (f32[64,512]{1,0:T(8,128)S(1)}, f32[64,512]{1,0:T(8,128)S(1)}, u32[]{:S(2)}, u32[]{:S(2)}) collective-permute-start(f32[64,512]{1,0:T(8,128)S(1)} %shard_map.103.x_ref), channel_id=1, source_target_pairs={{1,0},{2,3},{5,4},{6,7},{9,8},{10,11},{13,12},{14,15},{17,16},{18,... | collective-permute-start | bytes 393224 | tf_op jit(solution)/shard_map/ppermute | solution.py:285
  49.0 22.7 %collective-permute-done.15.c_ref = f32[64,512]{1,0:T(8,128)S(1)} collective-permute-done((f32[64,512]{1,0:T(8,128)S(1)}, f32[64,512]{1,0:T(8,128)S(1)}, u32[]{:S(2)}, u32[]{:S(2)}) %collective-permute-start.15) | collective-permute-done | bytes 131104 | tf_op jit(solution)/shard_map/ppermute | solution.py:285
  71.7 3.7 %collective-permute-done.13.a_ref = f32[64,512]{1,0:T(8,128)S(1)} collective-permute-done((f32[64,512]{1,0:T(8,128)S(1)}, f32[64,512]{1,0:T(8,128)S(1)}, u32[]{:S(2)}, u32[]{:S(2)}) %collective-permute-start.13) | collective-permute-done | bytes 131104 | tf_op jit(solution)/shard_map/ppermute | solution.py:285
  75.4 0.7 shard_map.104.own_ref
  76.1 2.3 %collective-permute-start.16 = (f32[512,128]{1,0:T(8,128)S(1)}, f32[512,128]{1,0:T(8,128)S(1)}, u32[]{:S(2)}, u32[]{:S(2)}) collective-permute-start(f32[512,128]{1,0:T(8,128)S(1)} %shard_map.104.own_ref), channel_id=1, source_target_pairs={{0,16},{16,0},{1,17},{17,1},{2,18},{18,2},{3,19},{19,3},{4,20},{20... | collective-permute-start | bytes 786440 | tf_op jit(solution)/shard_map/ppermute | solution.py:273
  78.4 1.2 %collective-permute-done.16.other_ref = f32[512,128]{1,0:T(8,128)S(1)} collective-permute-done((f32[512,128]{1,0:T(8,128)S(1)}, f32[512,128]{1,0:T(8,128)S(1)}, u32[]{:S(2)}, u32[]{:S(2)}) %collective-permute-start.16) | collective-permute-done | bytes 262176 | tf_op jit(solution)/shard_map/ppermute | solution.py:273
  79.6 1.4 %shard_map.105 = f32[512,256]{1,0:T(8,128)} custom-call(s32[3]{0:T(128)S(1)} %copy-done.4, f32[512,128]{1,0:T(8,128)S(1)} %shard_map.104.own_ref, f32[512,128]{1,0:T(8,128)S(1)} %collective-permute-done.16.other_ref), custom_call_target="tpu_custom_call" | custom-call | bytes 524300 | tf_op jit(solution)/shard_map/pallas_call | solution.py:249
  (10 shorter events, 0.0 us)
Async XLA Ops:
  0.6 36.0 %collective-permute-start.7 = (f32[512,512]{1,0:T(8,128)}, f32[512,512]{1,0:T(8,128)S(1)}, u32[]{:S(2)}, u32[]{:S(2)}) collective-permute-start(f32[512,512]{1,0:T(8,128)} %refs_0_.7), channel_id=1, source_target_pairs={{4,5},{8,9},{12,13},{9,10},{13,14},{20,22},{24,26},{28,30},{30,29}} | collective-permute-start | bytes 3145736 | tf_op jit(solution)/shard_map/ppermute | solution.py:290
  9.6 1.9 %copy-start.5 = (s32[2,256]{1,0:T(2,128)S(1)}, s32[2,256]{1,0:T(2,128)}, u32[]{:S(2)}) copy-start(s32[2,256]{1,0:T(2,128)} %tgt_ref.3) | copy-start | bytes 6148
  9.6 1.9 %copy-start.4 = (s32[3]{0:T(128)S(1)}, s32[3]{0:T(128)}, u32[]{:S(2)}) copy-start(s32[3]{0:T(128)} %pad_add_fusion.where_ref) | copy-start | bytes 40
  9.6 1.8 %collective-permute-start = (f32[136,512]{1,0:T(8,128)}, f32[136,512]{1,0:T(8,128)S(1)}, u32[]{:S(2)}, u32[]{:S(2)}) collective-permute-start(f32[136,512]{1,0:T(8,128)} %get-tuple-element.17), channel_id=1, source_target_pairs={{0,16},{16,0},{1,17},{17,1},{2,18},{18,2},{3,19},{19,3},{4,20},{20... | collective-permute-start | bytes 835592 | tf_op jit(solution)/shard_map/ppermute | solution.py:273
  11.5 1.0 %copy-start.3 = (f32[128,512]{1,0:T(8,128)S(1)}, f32[128,512]{1,0:T(8,128)}, u32[]{:S(2)}) copy-start(f32[128,512]{1,0:T(8,128)} %get-tuple-element.16.keep_ref) | copy-start | bytes 786436
  12.4 23.6 %copy-start = (f32[512,512]{1,0:T(8,128)S(1)}, f32[512,512]{1,0:T(8,128)}, u32[]{:S(2)}) copy-start(f32[512,512]{1,0:T(8,128)} %diag_ref.7) | copy-start | bytes 3145732
  14.3 7.8 %collective-permute-start.1 = (f32[128,512]{1,0:T(8,128)S(1)}, f32[128,512]{1,0:T(8,128)S(1)}, u32[]{:S(2)}, u32[]{:S(2)}) collective-permute-start(f32[128,512]{1,0:T(8,128)S(1)} %get-tuple-element.19), channel_id=1, source_target_pairs={{0,4},{4,0},{8,12},{12,8},{1,5},{5,1},{9,13},{13,9},{2,6},{6,2},{1... | collective-permute-start | bytes 786440 | tf_op jit(solution)/shard_map/ppermute | solution.py:282
  14.6 7.5 %collective-permute-start.2 = (f32[128,512]{1,0:T(8,128)S(1)}, f32[128,512]{1,0:T(8,128)S(1)}, u32[]{:S(2)}, u32[]{:S(2)}) collective-permute-start(f32[128,512]{1,0:T(8,128)S(1)} %get-tuple-element.20), channel_id=1, source_target_pairs={{0,8},{4,12},{8,0},{12,4},{1,9},{5,13},{9,1},{13,5},{2,10},{6,14},... | collective-permute-start | bytes 786440 | tf_op jit(solution)/shard_map/ppermute | solution.py:282
  14.6 13.1 %collective-permute-start.3 = (f32[128,512]{1,0:T(8,128)S(1)}, f32[128,512]{1,0:T(8,128)S(1)}, u32[]{:S(2)}, u32[]{:S(2)}) collective-permute-start(f32[128,512]{1,0:T(8,128)S(1)} %get-tuple-element.21), channel_id=1, source_target_pairs={{0,12},{4,8},{8,4},{12,0},{1,13},{5,9},{9,5},{13,1},{2,14},{6,10},... | collective-permute-start | bytes 786440 | tf_op jit(solution)/shard_map/ppermute | solution.py:282
  27.7 6.4 %copy-start.2 = (f32[512,256]{1,0:T(8,128)S(1)}, f32[512,256]{1,0:T(8,128)}, u32[]{:S(2)}) copy-start(f32[512,256]{1,0:T(8,128)} %rhs_ref.1) | copy-start | bytes 1572868
  28.3 6.5 %collective-permute-start.6 = (f32[64,512]{1,0:T(8,128)S(1)}, f32[64,512]{1,0:T(8,128)S(1)}, u32[]{:S(2)}, u32[]{:S(2)}) collective-permute-start(f32[64,512]{1,0:T(8,128)S(1)} %get-tuple-element.22.a_ref), channel_id=1, source_target_pairs={{0,2},{3,1},{4,6},{7,5},{8,10},{11,9},{12,14},{15,13},{16,18},{19,... | collective-permute-start | bytes 393224 | tf_op jit(solution)/shard_map/ppermute | solution.py:285
  30.2 11.2 %copy-start.1 = (f32[512,512]{1,0:T(8,128)S(1)}, f32[512,512]{1,0:T(8,128)}, u32[]{:S(2)}) copy-start(f32[512,512]{1,0:T(8,128)} %refs_0_.7) | copy-start | bytes 3145732
  30.2 4.6 %collective-permute-start.5 = (f32[64,512]{1,0:T(8,128)S(1)}, f32[64,512]{1,0:T(8,128)S(1)}, u32[]{:S(2)}, u32[]{:S(2)}) collective-permute-start(f32[64,512]{1,0:T(8,128)S(1)} %get-tuple-element.23), channel_id=1, source_target_pairs={{1,2},{2,1},{5,6},{6,5},{9,10},{10,9},{13,14},{14,13},{17,18},{18,... | collective-permute-start | bytes 393224 | tf_op jit(solution)/shard_map/ppermute | solution.py:285
  31.0 5.0 %collective-permute-start.4 = (f32[64,512]{1,0:T(8,128)S(1)}, f32[64,512]{1,0:T(8,128)S(1)}, u32[]{:S(2)}, u32[]{:S(2)}) collective-permute-start(f32[64,512]{1,0:T(8,128)S(1)} %get-tuple-element.23), channel_id=1, source_target_pairs={{0,1},{3,2},{4,5},{7,6},{8,9},{11,10},{12,13},{15,14},{16,17},{19,... | collective-permute-start | bytes 393224 | tf_op jit(solution)/shard_map/ppermute | solution.py:285
  36.7 4.7 %collective-permute-start.9 = (f32[512,512]{1,0:T(8,128)S(1)}, f32[512,512]{1,0:T(8,128)S(1)}, u32[]{:S(2)}, u32[]{:S(2)}) collective-permute-start(f32[512,512]{1,0:T(8,128)S(1)} %collective-permute-done.7.refs_1_), channel_id=1, source_target_pairs={{0,16},{16,0},{1,17},{17,1},{2,18},{18,2},{3,19},{19,3},{4,20},{20... | collective-permute-start | bytes 3145736 | tf_op jit(solution)/shard_map/ppermute | solution.py:273
  39.1 0.7 collective-permute-start.8
  41.9 1.4 %collective-permute-start.11 = (f32[64,512]{1,0:T(8,128)S(1)}, f32[64,512]{1,0:T(8,128)S(1)}, u32[]{:S(2)}, u32[]{:S(2)}) collective-permute-start(f32[64,512]{1,0:T(8,128)S(1)} %shard_map.100.x_ref), channel_id=1, source_target_pairs={{1,9},{2,10},{5,13},{6,14},{17,25},{18,26},{21,29},{22,30}} | collective-permute-start | bytes 393224 | tf_op jit(solution)/shard_map/ppermute | solution.py:276
  42.6 0.7 collective-permute-start.10
  43.9 1.2 %collective-permute-start.12 = (f32[64,512]{1,0:T(8,128)S(1)}, f32[64,512]{1,0:T(8,128)S(1)}, u32[]{:S(2)}, u32[]{:S(2)}) collective-permute-start(f32[64,512]{1,0:T(8,128)S(1)} %shard_map.102.x_ref), channel_id=1, source_target_pairs={{9,13},{10,14},{25,29},{26,30}} | collective-permute-start | bytes 393224 | tf_op jit(solution)/shard_map/ppermute | solution.py:276
  45.7 26.0 %collective-permute-start.15 = (f32[64,512]{1,0:T(8,128)S(1)}, f32[64,512]{1,0:T(8,128)S(1)}, u32[]{:S(2)}, u32[]{:S(2)}) collective-permute-start(f32[64,512]{1,0:T(8,128)S(1)} %shard_map.103.x_ref), channel_id=1, source_target_pairs={{1,3},{2,0},{5,7},{6,4},{9,11},{10,8},{13,15},{14,12},{17,19},{18,... | collective-permute-start | bytes 393224 | tf_op jit(solution)/shard_map/ppermute | solution.py:285
  47.0 24.7 %collective-permute-start.14 = (f32[64,512]{1,0:T(8,128)S(1)}, f32[64,512]{1,0:T(8,128)S(1)}, u32[]{:S(2)}, u32[]{:S(2)}) collective-permute-start(f32[64,512]{1,0:T(8,128)S(1)} %shard_map.103.x_ref), channel_id=1, source_target_pairs={{1,2},{2,1},{5,6},{6,5},{9,10},{10,9},{13,14},{14,13},{17,18},{18,... | collective-permute-start | bytes 393224 | tf_op jit(solution)/shard_map/ppermute | solution.py:285
  47.7 27.7 %collective-permute-start.13 = (f32[64,512]{1,0:T(8,128)S(1)}, f32[64,512]{1,0:T(8,128)S(1)}, u32[]{:S(2)}, u32[]{:S(2)}) collective-permute-start(f32[64,512]{1,0:T(8,128)S(1)} %shard_map.103.x_ref), channel_id=1, source_target_pairs={{1,0},{2,3},{5,4},{6,7},{9,8},{10,11},{13,12},{14,15},{17,16},{18,... | collective-permute-start | bytes 393224 | tf_op jit(solution)/shard_map/ppermute | solution.py:285
  76.1 3.5 %collective-permute-start.16 = (f32[512,128]{1,0:T(8,128)S(1)}, f32[512,128]{1,0:T(8,128)S(1)}, u32[]{:S(2)}, u32[]{:S(2)}) collective-permute-start(f32[512,128]{1,0:T(8,128)S(1)} %shard_map.104.own_ref), channel_id=1, source_target_pairs={{0,16},{16,0},{1,17},{17,1},{2,18},{18,2},{3,19},{19,3},{4,20},{20... | collective-permute-start | bytes 786440 | tf_op jit(solution)/shard_map/ppermute | solution.py:273

commit v5 on v4

v5 whole, which is shorter than its diff:
```python
import functools

import jax
import jax.numpy as jnp
from jax import lax
from jax.experimental import pallas as pl
from jax.experimental.pallas import tpu as pltpu
from jax.sharding import PartitionSpec as P

F32 = jnp.float32
BF16 = jnp.bfloat16
NT = (((1,), (1,)), ((), ()))
NN = (((1,), (0,)), ((), ()))
VM = pl.BlockSpec(memory_space=pltpu.VMEM)
ANY = pl.BlockSpec(memory_space=pl.ANY)
SM = pl.BlockSpec(memory_space=pltpu.SMEM)


def spread(value, axis, source):
    kept = jnp.where(lax.axis_index(axis) == source, value, 0).astype(value.dtype)
    return lax.psum(kept, axis)


def unit_lower(matrix):
    return jnp.tril(matrix) + jnp.eye(matrix.shape[-1], dtype=matrix.dtype)


def any_mesh(child_rhs, child_diag, child_off, live, targets, top_rhs, top_factor, top_diag):
    highest = lax.Precision.HIGHEST
    owned_rows = top_rhs.shape[0]
    right_count = top_rhs.shape[1]
    block_size = top_diag.shape[1]
    owned_blocks = owned_rows // block_size
    row_count = lax.axis_size("row")
    top_order = owned_rows * row_count
    col_width = top_factor.shape[1]
    my_row = lax.axis_index("row")
    my_col = lax.axis_index("col")
    child_sol = jnp.einsum("bij,bjr->bir", unit_lower(child_diag), child_rhs, precision=highest)
    tiles = jnp.einsum("btj,bjr->btr", child_off, child_sol, precision=highest)
    slot_index = jnp.arange(child_off.shape[1], dtype=jnp.int32)
    keep = slot_index[None, :] < live[:, None]
    tiles = jnp.where(keep[:, :, None], tiles, jnp.zeros_like(tiles))
    contrib = jnp.zeros((top_order, right_count), F32)
    contrib = contrib.at[targets.reshape(-1)].add(tiles.reshape(-1, right_count))
    row_part = lax.psum_scatter(contrib, "row", scatter_dimension=0, tiled=True)
    share = lax.psum_scatter(row_part, ("leaf", "col"), scatter_dimension=0, tiled=True)
    updates = lax.all_gather(share, ("leaf", "col"), axis=0, tiled=True)
    reduced = top_rhs - updates
    inverse_all = unit_lower(top_diag.reshape(owned_blocks, block_size, block_size))
    col_global = my_col * col_width + jnp.arange(col_width, dtype=jnp.int32)

    def step(block, solution):
        local = block % owned_blocks
        owner = block // owned_blocks
        factor_rows = jnp.where(
            (col_global < block * block_size)[None, :], top_factor, jnp.zeros_like(top_factor)
        )
        columns = lax.dynamic_slice_in_dim(solution, my_col * col_width, col_width, 0)
        partial_value = jnp.dot(
            factor_rows, columns, precision=highest, preferred_element_type=F32
        )
        block_inverse = lax.dynamic_index_in_dim(inverse_all, local, 0, keepdims=False)
        before = lax.psum(partial_value, "col")
        solved = jnp.dot(
            block_inverse, reduced - before, precision=highest, preferred_element_type=F32
        )
        solved = spread(solved, "row", owner)
        return lax.dynamic_update_slice_in_dim(solution, solved, block * block_size, 0)

    solution = lax.fori_loop(
        0, row_count * owned_blocks, step, jnp.zeros((top_order, right_count), F32)
    )
    top_sol = lax.dynamic_slice_in_dim(solution, my_row * owned_rows, owned_rows, 0)
    return (child_sol, top_sol)


def place():
    return tuple(lax.axis_index(a) for a in ("leaf", "row", "col"))


def split(value):
    high = value.astype(BF16)
    return high, (value - high.astype(F32)).astype(BF16)


def dot3(left, high, low, dims):
    left_high, left_low = split(left)
    rows = left.shape[0]
    both = lax.dot_general(
        jnp.concatenate([left_high, left_low], axis=0), high, dims, preferred_element_type=F32
    )
    cross = lax.dot_general(left_high, low, dims, preferred_element_type=F32)
    return both[:rows] + both[rows:] + cross


def lower(matrix):
    row = lax.broadcasted_iota(jnp.int32, matrix.shape, 0)
    col = lax.broadcasted_iota(jnp.int32, matrix.shape, 1)
    return jnp.where(col <= row, matrix, 0.0)


def turn_kernel(rhs_ref, diag_ref, out_ref, high_ref, low_ref, turned_ref):
    leaf, _, z = place()
    half, piece = turned_ref.shape[0], out_ref.shape[0]
    turned_ref[...] = rhs_ref[:, pl.ds(pl.multiple_of(leaf * half, half), half)].T
    out_ref[...] = turned_ref[pl.ds(pl.multiple_of((z // 2) * piece, piece), piece), :]
    high_ref[...], low_ref[...] = split(lower(diag_ref[...]).T)


def child_kernel(live_ref, rhs_hbm, diag_hbm, off_hbm, tgt_ref, sol_hbm, keep_ref, send_ref,
                 rhs_ref, diag_ref, off_ref, sol_ref, tiles_ref, sems):
    leaf, _, _ = place()
    children, slots = off_ref.shape[0], off_ref.shape[1]
    half = keep_ref.shape[0]
    pairs = ((rhs_hbm, rhs_ref), (diag_hbm, diag_ref), (off_hbm, off_ref))
    copies = [
        [pltpu.make_async_copy(source.at[s], target.at[s], sems.at[i, s]) for i, (source, target) in enumerate(pairs)]
        for s in range(children)
    ]
    back = [pltpu.make_async_copy(sol_ref.at[s], sol_hbm.at[s], sems.at[3, s]) for s in range(children)]
    for s in range(children):
        for copy in copies[s]:
            copy.start()
    for s in range(children):
        copies[s][0].wait()
        copies[s][1].wait()
        rhs = rhs_ref[s]
        sol = rhs + dot3(lower(diag_ref[s]), *split(rhs), NN)
        sol_ref[s] = sol
        back[s].start()
        copies[s][2].wait()
        tiles = dot3(sol.T, *split(off_ref[s]), NT)
        slot = lax.broadcasted_iota(jnp.int32, tiles.shape, 1)
        tiles_ref[:, s * slots:(s + 1) * slots] = jnp.where(slot < live_ref[s], tiles, 0.0)
        send_ref[half:half + 8, s * slots:(s + 1) * slots] = jnp.broadcast_to(
            tgt_ref[s:s + 1, :].astype(F32), (8, slots)
        )
    keep_ref[...] = tiles_ref[pl.ds(pl.multiple_of(leaf * half, half), half), :]
    send_ref[0:half, :] = tiles_ref[pl.ds(pl.multiple_of((1 - leaf) * half, half), half), :]
    for copy in back:
        copy.wait()


def scatter_kernel(keep_ref, recv_ref, tgt_ref, *out_refs):
    _, row, _ = place()
    half, slots_all = keep_ref.shape
    size = out_refs[0].shape[1]
    children, slots = tgt_ref.shape
    mine = [split(keep_ref[...]), split(recv_ref[0:half, :])]
    stacked = [jnp.concatenate(pair, axis=0) for pair in mine]
    mine_targets = jnp.concatenate([tgt_ref[s:s + 1, :] for s in range(children)], axis=1)
    target = [mine_targets, recv_ref[half:half + 1, :].astype(jnp.int32)]
    for s, out_ref in enumerate(out_refs):
        block = jnp.bitwise_xor(row, s)
        index = lax.broadcasted_iota(jnp.int32, (size, slots_all), 0) + block * size
        total = None
        for t, value in zip(target, stacked):
            hot = jnp.where(index == t, 1.0, 0.0).astype(BF16)
            product = lax.dot_general(value, hot, NT, preferred_element_type=F32)
            total = product if total is None else total + product
        out_ref[...] = total[:half] + total[half:]


def pieces_kernel(a_ref, b_ref, c_ref, d_ref, first_ref, second_ref, sum_ref):
    _, _, z = place()
    odd = z % 2
    piece = first_ref.shape[0]
    sum_ref[...] = (a_ref[...] + b_ref[...]) + (c_ref[...] + d_ref[...])
    first_ref[...] = sum_ref[pl.ds(pl.multiple_of(odd * piece, piece), piece), :]
    second_ref[...] = sum_ref[pl.ds(pl.multiple_of((1 - odd) * piece, piece), piece), :]


def factor_kernel(own_ref, sent_ref, other_ref, *out_refs):
    leaf, row, z = place()
    for block in range(3):
        high_ref, low_ref = out_refs[2 * block], out_refs[2 * block + 1]

        @pl.when((row > block) & ((z == 1) | (z == 2)))
        def _():
            if block == 0:
                value = jnp.where((leaf == 0) == (z == 1), sent_ref[...], other_ref[...])
            else:
                sent = jnp.where((leaf == 0) == (block == 1), sent_ref[...], other_ref[...])
                value = jnp.where(z == block, own_ref[...], sent)
            high_ref[...], low_ref[...] = split(value.T)


def chain_kernel(owner, has_sums, solves, *refs):
    refs = list(refs)
    out_refs = [refs.pop()]
    if has_sums:
        out_refs.insert(0, refs.pop())
    _, row, z = place()
    given_ref = refs[0]
    if has_sums:
        value = given_ref[...] - ((refs[1][...] + refs[2][...]) + (refs[3][...] + refs[4][...]))
        out_refs[0][...] = value
        out_refs[1][...] = value
        refs = refs[5:]
    else:
        out_refs[0][...] = refs[1][...]
        refs = refs[2:]

    @pl.when((row == owner) & ((z == 1) | (z == 2)))
    def _():
        left = out_refs[0][...] if has_sums else given_ref[...]
        used = refs[2:] if solves else refs
        for i in range(0, len(used), 3):
            left = left - dot3(used[i][...], used[i + 1][...], used[i + 2][...], NN)
        if solves:
            left = left + dot3(left, refs[0][...], refs[1][...], NN)
        out_refs[-1][...] = left


def half_kernel(x_ref, a_ref, b_ref, c_ref, out_ref):
    _, _, z = place()
    x, a, b, c = x_ref[...], a_ref[...], b_ref[...], c_ref[...]
    low = jnp.where(z == 0, a, jnp.where(z == 1, x, jnp.where(z == 2, b, c)))
    high = jnp.where(z == 0, c, jnp.where(z == 1, b, jnp.where(z == 2, x, a)))
    out_ref[...] = jnp.concatenate([low, high], axis=0).T


def write_kernel(mine, part_ref, *refs):
    out_hbm, sem = refs[-2:]
    leaf, _, _ = place()
    half = part_ref.shape[1]
    at = leaf if mine else 1 - leaf
    copy = pltpu.make_async_copy(part_ref, out_hbm.at[:, pl.ds(pl.multiple_of(at * half, half), half)], sem)
    copy.start()
    copy.wait()


def call(kernel, ins, outs, scratch=(), outside=(), outs_outside=(), pinned=(), aliases=None, limit=24):
    def spec(i, a):
        return ANY if i in outside else SM if a.ndim == 1 else VM

    def shape(i, out):
        dims, dtype = out if isinstance(out[0], tuple) else (out, F32)
        return pltpu.VMEM(dims, dtype) if i in pinned else jax.ShapeDtypeStruct(dims, dtype)

    outs = pl.pallas_call(
        kernel,
        out_shape=[shape(i, out) for i, out in enumerate(outs)],
        in_specs=[spec(i, a) for i, a in enumerate(ins)],
        out_specs=[ANY if i in outs_outside else VM for i in range(len(outs))],
        scratch_shapes=[pltpu.VMEM(s, F32) if isinstance(s, tuple) else s for s in scratch],
        input_output_aliases=aliases or {},
        cost_estimate=pl.CostEstimate(flops=0, bytes_accessed=4 * sum(a.size for a in ins), transcendentals=0),
        compiler_params=pltpu.CompilerParams(vmem_limit_bytes=limit * 1024 * 1024),
    )(*ins)
    return list(outs)


def central(child_rhs, child_diag, child_off, live, targets, top_rhs, top_factor, top_diag):
    rows, cols = lax.axis_size("row"), lax.axis_size("col")
    size = top_diag.shape[1]
    right = top_rhs.shape[1]
    half, piece = right // 2, right // 4
    children, slots = targets.shape
    shape = (piece, size)
    block = ((size, size), BF16)
    dma = pltpu.SemaphoreType.DMA

    def at(r, c):
        return r * cols + c

    def swap(value):
        return lax.ppermute(value, "leaf", [(0, 1), (1, 0)])

    def hop(value, pairs):
        pairs = [(at(a, z), at(b, z)) for a, b in pairs for z in (1, 2)]
        return lax.ppermute(value, ("row", "col"), pairs)

    def along_row(value, pairs):
        return lax.ppermute(value, "row", pairs)

    def along_col(value, pairs):
        return lax.ppermute(value, "col", pairs)

    near = [(at(k, 0), at(k, 1)) for k in (1, 2, 3)] + [(at(k, 1), at(k, 2)) for k in (2, 3)]
    far = [(at(k, 0), at(k, 2)) for k in (1, 2, 3)] + [(at(3, 2), at(3, 1))]
    shift = rows * cols
    sent = lax.ppermute(
        top_factor, ("leaf", "row", "col"), near + [(a + shift, b + shift) for a, b in far]
    )
    child_sol, keep, send = call(
        child_kernel,
        [live, child_rhs, child_diag, child_off, targets],
        [child_rhs.shape, (half, children * slots), (half + 8, children * slots)],
        [child_rhs.shape, child_diag.shape, child_off.shape, child_rhs.shape, (right, children * slots),
         dma((4, children))],
        outside=(1, 2, 3),
        outs_outside=(0,),
        pinned=(1, 2),
        limit=56,
    )
    sums = call(scatter_kernel, [keep, swap(send), targets], [(half, size)] * rows)
    got = [along_row(sums[s], [(i, i ^ s) for i in range(rows)]) for s in (1, 2, 3)]
    rhs_piece, diag_high, diag_low = call(
        turn_kernel, [top_rhs, top_diag], [shape, block, block], [(half, size)]
    )
    diag = [diag_high, diag_low]
    first, second = call(pieces_kernel, [sums[0]] + got, [shape] * 2, [(half, size)])
    sent, first, second = lax.optimization_barrier((sent, first, second))
    q = [
        along_col(first, [(0, 1), (3, 2)]),
        along_col(first, [(1, 2), (2, 1)]),
        along_col(second, [(0, 2), (3, 1)]),
    ]
    factor = call(factor_kernel, [top_factor, sent, swap(sent)], [block] * 6)
    factor = [factor[0:2], factor[2:4], factor[4:6]]

    def chain(owner, ins, has_sums=False, solves=True):
        outs = call(
            functools.partial(chain_kernel, owner, has_sums, solves), ins, [shape] * (1 + has_sums)
        )
        return outs if has_sums else outs[0]

    res, x = chain(0, [rhs_piece, second] + q + diag, has_sums=True)
    to1 = hop(x, [(0, 1)])
    to2 = hop(x, [(0, 2)])
    x = chain(1, [res, x] + diag + [to1] + factor[0])
    on = hop(x, [(1, 2), (0, 3)])
    res = chain(2, [res, res, to2] + factor[0], solves=False)
    x = chain(2, [res, x] + diag + [on] + factor[1])
    to3 = hop(x, [(2, 3)])
    late = hop(x, [(1, 3)])
    res = chain(3, [res, res, on] + factor[0], solves=False)
    x = chain(3, [res, x] + diag + [late] + factor[1] + [to3] + factor[2])

    both = along_col(x, [(1, 2), (2, 1)])
    step = along_col(x, [(1, 0), (2, 3)])
    over = along_col(x, [(1, 3), (2, 0)])
    (own,) = call(half_kernel, [x, step, both, over], [(size, half)])
    (top_sol,) = call(
        functools.partial(write_kernel, True), [own], [top_rhs.shape], [dma(())], outs_outside=(0,)
    )
    (top_sol,) = call(
        functools.partial(write_kernel, False),
        [swap(own), top_sol],
        [top_rhs.shape],
        [dma(())],
        outside=(1,),
        outs_outside=(0,),
        aliases={1: 0},
    )
    return (child_sol, top_sol)


def solution(mesh):
    in_specs = (
        P(("leaf", "row", "col"), None, None),
        P(("leaf", "row", "col"), None, None),
        P(("leaf", "row", "col"), None, None),
        P(("leaf", "row", "col")),
        P(("leaf", "row", "col"), None),
        P("row", None),
        P("row", "col"),
        P("row", None),
    )
    out_specs = (P(("leaf", "row", "col"), None, None), P("row", None))
    axes = tuple(mesh.shape[a] for a in ("leaf", "row", "col"))

    def shards(*args):
        top_rhs, top_factor, top_diag = args[5:]
        size = top_diag.shape[1]
        fits = axes == (2, 4, 4) and top_rhs.shape[0] == size and top_factor.shape[1] == size
        return (central if fits else any_mesh)(*args)

    return jax.shard_map(shards, mesh=mesh, in_specs=in_specs, out_specs=out_specs, check_vma=False)
```

time: 81.3 us -> 74.7 us (0.919)
  Pallas kernels: 12.1 us -> 7.12 us
  waiting for transfers between devices: 42.9 us -> 39.2 us
  starting transfers between devices: 23.5 us -> 27.1 us
  local copies, waits for them, and re-layouts: 0.98 us -> 0.02 us
    pallas_call x11 -> x14, Pallas kernels: 12.1 us -> 7.12 us  [call(): pl.pallas_call(kernel, out_shape=[shape(i, out) for i, out in enumerate(o...]
    ppermute x6, waiting for transfers between devices: 27.6 us -> 23.6 us  [along_col(): return lax.ppermute(value, 'col', pairs)]
    ppermute x1, waiting for transfers between devices: 0.01 us -> 2.89 us  [central(): lax.ppermute(top_factor, ('leaf', 'row', 'col'), near + [(a + shift, b +...]
    ppermute x6, starting transfers between devices: 9.01 us -> 11.6 us  [along_col(): return lax.ppermute(value, 'col', pairs)]
    ppermute x3, waiting for transfers between devices: 4.53 us -> 1.99 us  [swap(): return lax.ppermute(value, 'leaf', [(0, 1), (1, 0)])]
    unnamed x12 -> x8, local copies, waits for them, and re-layouts: 0.98 us -> 0.02 us
    ppermute x4 -> x5, starting transfers between devices: 2.66 us -> 3.34 us  [hop(): return lax.ppermute(value, ('row', 'col'), pairs)]
  transfers between devices with their start and end apart: 17 -> 18, of which waited for: 8 -> 8; matrix products, arithmetic and copies ran while one was open for 1% -> 0% of each run, Pallas kernels for 10% -> 8%
where the time goes in v5:
time: 74.7 us; the launch traced here: 74.3 us
  waiting for transfers between devices  39.2 us (52%)
  starting transfers between devices  27.1 us (36%)
  Pallas kernels  7.12 us (10%)
  between operations  0.95 us (1%)
    ppermute x6, waiting for transfers between devices, along_col(): return lax.ppermute(value, 'col', pairs)  23.6 us
    ppermute x6, starting transfers between devices, along_col(): return lax.ppermute(value, 'col', pairs)  11.6 us
    ppermute x3, waiting for transfers between devices, along_row(): return lax.ppermute(value, 'row', pairs)  10.7 us
    pallas_call x14, Pallas kernels, call(): pl.pallas_call(kernel, out_shape=[shape(i, out) for i, out in enumerate(o...  7.12 us
    ppermute x3, starting transfers between devices, swap(): return lax.ppermute(value, 'leaf', [(0, 1), (1, 0)])  5.11 us
    ppermute x1, starting transfers between devices, central(): lax.ppermute(top_factor, ('leaf', 'row', 'col'), near + [(a + shift, b +...  4.28 us
    ppermute x5, starting transfers between devices, hop(): return lax.ppermute(value, ('row', 'col'), pairs)  3.34 us
    ppermute x1, waiting for transfers between devices, central(): lax.ppermute(top_factor, ('leaf', 'row', 'col'), near + [(a + shift, b +...  2.89 us
  transfers between devices with their start and end apart: 18, of which 8 were waited for; matrix products, arithmetic and copies ran while one was open for 0% of the time, Pallas kernels for 8%

profile of v5, /device:TPU:7, one launch (start us, length us, event | category | flops | bytes accessed | tf_op | source)
XLA Modules:
  0.0 74.3 jit_solution(8242927140147786793)
XLA Ops:
  0.6 4.3 %collective-permute-start = (f32[512,512]{1,0:T(8,128)}, f32[512,512]{1,0:T(8,128)S(1)}, u32[]{:S(2)}, u32[]{:S(2)}) collective-permute-start(f32[512,512]{1,0:T(8,128)} %own_ref.1), channel_id=1, source_target_pairs={{4,5},{8,9},{12,13},{9,10},{13,14},{20,22},{24,26},{28,30},{30,29}} | collective-permute-start | bytes 3145736 | tf_op jit(solution)/shard_map/ppermute | solution.py:284
  4.9 0.0 copy-start.3
  4.9 3.7 %shard_map.95 = (f32[2,256,256]{2,1,0:T(8,128)}, f32[128,512]{1,0:T(8,128)S(1)}, f32[136,512]{1,0:T(8,128)S(1)}) custom-call(s32[2]{0:T(128)} %live_ref.1, f32[2,256,256]{2,1,0:T(8,128)} %rhs_hbm.1, f32[2,256,256]{2,1,0:T(8,128)} %diag_hbm.1, f32[2,256,256]{2,1,0:T(8,128)} %off_hbm.1, s32[2,256]{1,0:T(2,128)} %tgt_ref.3), custom_call_target="tpu_custom_call" | custom-call | bytes 1574920 | tf_op jit(solution)/shard_map/pallas_call | solution.py:242
  8.6 0.0 copy-start.1
  8.6 0.1 collective-permute-start.1
  8.7 1.5 %collective-permute-done.1.recv_ref = f32[136,512]{1,0:T(8,128)S(1)} collective-permute-done((f32[136,512]{1,0:T(8,128)S(1)}, f32[136,512]{1,0:T(8,128)S(1)}, u32[]{:S(2)}, u32[]{:S(2)}) %collective-permute-start.1) | collective-permute-done | bytes 278560 | tf_op jit(solution)/shard_map/ppermute | solution.py:269
  10.3 0.0 copy-done.3
  10.3 1.3 %shard_map.97 = (f32[128,512]{1,0:T(8,128)S(1)}, f32[128,512]{1,0:T(8,128)S(1)}, f32[128,512]{1,0:T(8,128)S(1)}, f32[128,512]{1,0:T(8,128)S(1)}) custom-call(f32[128,512]{1,0:T(8,128)S(1)} %get-tuple-element.27.keep_ref, f32[136,512]{1,0:T(8,128)S(1)} %collective-permute-done.1.recv_ref, s32[2,256]{1,0:T(2,128)S(1)} %copy-done.3), custom_call_target="tpu_custom_call" | custom-call | bytes 542720 | tf_op jit(solution)/shard_map/pallas_call | solution.py:242
  11.6 0.3 collective-permute-start.2
  11.9 0.1 collective-permute-start.3
  12.0 2.3 %collective-permute-start.4 = (f32[128,512]{1,0:T(8,128)S(1)}, f32[128,512]{1,0:T(8,128)S(1)}, u32[]{:S(2)}, u32[]{:S(2)}) collective-permute-start(f32[128,512]{1,0:T(8,128)S(1)} %get-tuple-element.32), channel_id=1, source_target_pairs={{0,12},{4,8},{8,4},{12,0},{1,13},{5,9},{9,5},{13,1},{2,14},{6,10},... | collective-permute-start | bytes 786440 | tf_op jit(solution)/shard_map/ppermute | solution.py:276
  14.3 5.1 %collective-permute-done.2.b_ref = f32[128,512]{1,0:T(8,128)S(1)} collective-permute-done((f32[128,512]{1,0:T(8,128)S(1)}, f32[128,512]{1,0:T(8,128)S(1)}, u32[]{:S(2)}, u32[]{:S(2)}) %collective-permute-start.2) | collective-permute-done | bytes 262176 | tf_op jit(solution)/shard_map/ppermute | solution.py:276
  19.4 0.0 collective-permute-done.3.c_ref
  19.4 5.6 %collective-permute-done.4.d_ref = f32[128,512]{1,0:T(8,128)S(1)} collective-permute-done((f32[128,512]{1,0:T(8,128)S(1)}, f32[128,512]{1,0:T(8,128)S(1)}, u32[]{:S(2)}, u32[]{:S(2)}) %collective-permute-start.4) | collective-permute-done | bytes 262176 | tf_op jit(solution)/shard_map/ppermute | solution.py:276
  25.0 0.1 shard_map.98
  25.1 2.9 %collective-permute-done.sent_ref = f32[512,512]{1,0:T(8,128)S(1)} collective-permute-done((f32[512,512]{1,0:T(8,128)}, f32[512,512]{1,0:T(8,128)S(1)}, u32[]{:S(2)}, u32[]{:S(2)}) %collective-permute-start) | collective-permute-done | bytes 1048608 | tf_op jit(solution)/shard_map/ppermute | solution.py:284
  28.0 0.5 collective-permute-start.9
  28.5 4.0 %collective-permute-start.5 = (f32[64,512]{1,0:T(8,128)S(1)}, f32[64,512]{1,0:T(8,128)S(1)}, u32[]{:S(2)}, u32[]{:S(2)}) collective-permute-start(f32[64,512]{1,0:T(8,128)S(1)} %get-tuple-element.36), channel_id=1, source_target_pairs={{0,1},{3,2},{4,5},{7,6},{8,9},{11,10},{12,13},{15,14},{16,17},{19,... | collective-permute-start | bytes 393224 | tf_op jit(solution)/shard_map/ppermute | solution.py:279
  32.5 0.7 collective-permute-start.6
  33.2 3.7 %collective-permute-start.7 = (f32[64,512]{1,0:T(8,128)S(1)}, f32[64,512]{1,0:T(8,128)S(1)}, u32[]{:S(2)}, u32[]{:S(2)}) collective-permute-start(f32[64,512]{1,0:T(8,128)S(1)} %get-tuple-element.35.refs_1_), channel_id=1, source_target_pairs={{0,2},{3,1},{4,6},{7,5},{8,10},{11,9},{12,14},{15,13},{16,18},{19,... | collective-permute-start | bytes 393224 | tf_op jit(solution)/shard_map/ppermute | solution.py:279
  36.9 0.0 copy-done.1
  36.9 0.3 shard_map.96
  37.3 0.0 copy-start
  37.3 0.0 collective-permute-done.5.refs_2_
  37.3 0.0 collective-permute-done.6.refs_3_
  37.3 2.2 %collective-permute-done.7.refs_4_ = f32[64,512]{1,0:T(8,128)S(1)} collective-permute-done((f32[64,512]{1,0:T(8,128)S(1)}, f32[64,512]{1,0:T(8,128)S(1)}, u32[]{:S(2)}, u32[]{:S(2)}) %collective-permute-start.7) | collective-permute-done | bytes 131104 | tf_op jit(solution)/shard_map/ppermute | solution.py:279
  39.6 0.7 collective-permute-start.10
  40.2 0.7 collective-permute-start.8
  40.9 0.0 collective-permute-done.9.other_ref
  41.0 0.0 collective-permute-done.10.refs_4_
  41.0 0.7 collective-permute-start.11
  41.7 0.0 collective-permute-done.8.refs_2_
  41.7 0.0 collective-permute-done.11.refs_2_.refs_4_
  41.7 0.7 collective-permute-start.12
  42.4 0.7 collective-permute-start.13
  43.1 0.0 collective-permute-done.12.refs_4_
  43.1 0.0 collective-permute-done.13.refs_7_
  43.2 1.3 %collective-permute-start.14 = (f32[64,512]{1,0:T(8,128)S(1)}, f32[64,512]{1,0:T(8,128)S(1)}, u32[]{:S(2)}, u32[]{:S(2)}) collective-permute-start(f32[64,512]{1,0:T(8,128)S(1)} %shard_map.105.x_ref), channel_id=1, source_target_pairs={{1,0},{2,3},{5,4},{6,7},{9,8},{10,11},{13,12},{14,15},{17,16},{18,... | collective-permute-start | bytes 393224 | tf_op jit(solution)/shard_map/ppermute | solution.py:279
  44.5 0.7 collective-permute-start.15
  45.2 1.3 %collective-permute-start.16 = (f32[64,512]{1,0:T(8,128)S(1)}, f32[64,512]{1,0:T(8,128)S(1)}, u32[]{:S(2)}, u32[]{:S(2)}) collective-permute-start(f32[64,512]{1,0:T(8,128)S(1)} %shard_map.105.x_ref), channel_id=1, source_target_pairs={{1,3},{2,0},{5,7},{6,4},{9,11},{10,8},{13,15},{14,12},{17,19},{18,... | collective-permute-start | bytes 393224 | tf_op jit(solution)/shard_map/ppermute | solution.py:279
  46.5 16.7 %collective-permute-done.14.a_ref = f32[64,512]{1,0:T(8,128)S(1)} collective-permute-done((f32[64,512]{1,0:T(8,128)S(1)}, f32[64,512]{1,0:T(8,128)S(1)}, u32[]{:S(2)}, u32[]{:S(2)}) %collective-permute-start.14) | collective-permute-done | bytes 131104 | tf_op jit(solution)/shard_map/ppermute | solution.py:279
  63.2 0.0 collective-permute-done.15.b_ref
  63.2 4.6 %collective-permute-done.16.c_ref = f32[64,512]{1,0:T(8,128)S(1)} collective-permute-done((f32[64,512]{1,0:T(8,128)S(1)}, f32[64,512]{1,0:T(8,128)S(1)}, u32[]{:S(2)}, u32[]{:S(2)}) %collective-permute-start.16) | collective-permute-done | bytes 131104 | tf_op jit(solution)/shard_map/ppermute | solution.py:279
  67.8 0.1 shard_map.106.part_ref
  68.0 4.5 %collective-permute-start.17 = (f32[512,128]{1,0:T(8,128)S(1)}, f32[512,128]{1,0:T(8,128)S(1)}, u32[]{:S(2)}, u32[]{:S(2)}) collective-permute-start(f32[512,128]{1,0:T(8,128)S(1)} %shard_map.106.part_ref), channel_id=1, source_target_pairs={{0,16},{16,0},{1,17},{17,1},{2,18},{18,2},{3,19},{19,3},{4,20},{20... | collective-permute-start | bytes 786440 | tf_op jit(solution)/shard_map/ppermute | solution.py:269
  72.5 0.7 shard_map.107.refs_0_
  73.2 0.4 collective-permute-done.17.part_ref
  73.6 0.7 shard_map.108
  (10 shorter events, 0.2 us)
Async XLA Ops:
  0.6 27.4 %collective-permute-start = (f32[512,512]{1,0:T(8,128)}, f32[512,512]{1,0:T(8,128)S(1)}, u32[]{:S(2)}, u32[]{:S(2)}) collective-permute-start(f32[512,512]{1,0:T(8,128)} %own_ref.1), channel_id=1, source_target_pairs={{4,5},{8,9},{12,13},{9,10},{13,14},{20,22},{24,26},{28,30},{30,29}} | collective-permute-start | bytes 3145736 | tf_op jit(solution)/shard_map/ppermute | solution.py:284
  4.9 5.4 %copy-start.3 = (s32[2,256]{1,0:T(2,128)S(1)}, s32[2,256]{1,0:T(2,128)}, u32[]{:S(2)}) copy-start(s32[2,256]{1,0:T(2,128)} %tgt_ref.3) | copy-start | bytes 6148
  8.6 28.3 %copy-start.1 = (f32[512,512]{1,0:T(8,128)S(1)}, f32[512,512]{1,0:T(8,128)}, u32[]{:S(2)}) copy-start(f32[512,512]{1,0:T(8,128)} %diag_ref.1) | copy-start | bytes 3145732
  8.6 1.6 %collective-permute-start.1 = (f32[136,512]{1,0:T(8,128)S(1)}, f32[136,512]{1,0:T(8,128)S(1)}, u32[]{:S(2)}, u32[]{:S(2)}) collective-permute-start(f32[136,512]{1,0:T(8,128)S(1)} %get-tuple-element.28), channel_id=1, source_target_pairs={{0,16},{16,0},{1,17},{17,1},{2,18},{18,2},{3,19},{19,3},{4,20},{20... | collective-permute-start | bytes 835592 | tf_op jit(solution)/shard_map/ppermute | solution.py:269
  11.6 7.8 %collective-permute-start.2 = (f32[128,512]{1,0:T(8,128)S(1)}, f32[128,512]{1,0:T(8,128)S(1)}, u32[]{:S(2)}, u32[]{:S(2)}) collective-permute-start(f32[128,512]{1,0:T(8,128)S(1)} %get-tuple-element.30), channel_id=1, source_target_pairs={{0,4},{4,0},{8,12},{12,8},{1,5},{5,1},{9,13},{13,9},{2,6},{6,2},{1... | collective-permute-start | bytes 786440 | tf_op jit(solution)/shard_map/ppermute | solution.py:276
  11.9 7.5 %collective-permute-start.3 = (f32[128,512]{1,0:T(8,128)S(1)}, f32[128,512]{1,0:T(8,128)S(1)}, u32[]{:S(2)}, u32[]{:S(2)}) collective-permute-start(f32[128,512]{1,0:T(8,128)S(1)} %get-tuple-element.31), channel_id=1, source_target_pairs={{0,8},{4,12},{8,0},{12,4},{1,9},{5,13},{9,1},{13,5},{2,10},{6,14},... | collective-permute-start | bytes 786440 | tf_op jit(solution)/shard_map/ppermute | solution.py:276
  12.0 13.1 %collective-permute-start.4 = (f32[128,512]{1,0:T(8,128)S(1)}, f32[128,512]{1,0:T(8,128)S(1)}, u32[]{:S(2)}, u32[]{:S(2)}) collective-permute-start(f32[128,512]{1,0:T(8,128)S(1)} %get-tuple-element.32), channel_id=1, source_target_pairs={{0,12},{4,8},{8,4},{12,0},{1,13},{5,9},{9,5},{13,1},{2,14},{6,10},... | collective-permute-start | bytes 786440 | tf_op jit(solution)/shard_map/ppermute | solution.py:276
  25.0 11.9 %copy-start.2 = (f32[512,256]{1,0:T(8,128)S(1)}, f32[512,256]{1,0:T(8,128)}, u32[]{:S(2)}) copy-start(f32[512,256]{1,0:T(8,128)} %rhs_ref.1) | copy-start | bytes 1572868
  28.0 12.9 %collective-permute-start.9 = (f32[512,512]{1,0:T(8,128)S(1)}, f32[512,512]{1,0:T(8,128)S(1)}, u32[]{:S(2)}, u32[]{:S(2)}) collective-permute-start(f32[512,512]{1,0:T(8,128)S(1)} %collective-permute-done.sent_ref), channel_id=1, source_target_pairs={{0,16},{16,0},{1,17},{17,1},{2,18},{18,2},{3,19},{19,3},{4,20},{20... | collective-permute-start | bytes 3145736 | tf_op jit(solution)/shard_map/ppermute | solution.py:269
  28.5 8.8 %collective-permute-start.5 = (f32[64,512]{1,0:T(8,128)S(1)}, f32[64,512]{1,0:T(8,128)S(1)}, u32[]{:S(2)}, u32[]{:S(2)}) collective-permute-start(f32[64,512]{1,0:T(8,128)S(1)} %get-tuple-element.36), channel_id=1, source_target_pairs={{0,1},{3,2},{4,5},{7,6},{8,9},{11,10},{12,13},{15,14},{16,17},{19,... | collective-permute-start | bytes 393224 | tf_op jit(solution)/shard_map/ppermute | solution.py:279
  32.5 4.8 %collective-permute-start.6 = (f32[64,512]{1,0:T(8,128)S(1)}, f32[64,512]{1,0:T(8,128)S(1)}, u32[]{:S(2)}, u32[]{:S(2)}) collective-permute-start(f32[64,512]{1,0:T(8,128)S(1)} %get-tuple-element.36), channel_id=1, source_target_pairs={{1,2},{2,1},{5,6},{6,5},{9,10},{10,9},{13,14},{14,13},{17,18},{18,... | collective-permute-start | bytes 393224 | tf_op jit(solution)/shard_map/ppermute | solution.py:279
  33.2 6.3 %collective-permute-start.7 = (f32[64,512]{1,0:T(8,128)S(1)}, f32[64,512]{1,0:T(8,128)S(1)}, u32[]{:S(2)}, u32[]{:S(2)}) collective-permute-start(f32[64,512]{1,0:T(8,128)S(1)} %get-tuple-element.35.refs_1_), channel_id=1, source_target_pairs={{0,2},{3,1},{4,6},{7,5},{8,10},{11,9},{12,14},{15,13},{16,18},{19,... | collective-permute-start | bytes 393224 | tf_op jit(solution)/shard_map/ppermute | solution.py:279
  37.3 3.6 %copy-start = (f32[512,512]{1,0:T(8,128)S(1)}, f32[512,512]{1,0:T(8,128)}, u32[]{:S(2)}) copy-start(f32[512,512]{1,0:T(8,128)} %own_ref.1) | copy-start | bytes 3145732
  39.6 1.4 %collective-permute-start.10 = (f32[64,512]{1,0:T(8,128)S(1)}, f32[64,512]{1,0:T(8,128)S(1)}, u32[]{:S(2)}, u32[]{:S(2)}) collective-permute-start(f32[64,512]{1,0:T(8,128)S(1)} %get-tuple-element.40.refs_1_), channel_id=1, source_target_pairs={{1,5},{2,6},{17,21},{18,22}} | collective-permute-start | bytes 393224 | tf_op jit(solution)/shard_map/ppermute | solution.py:273
  40.2 1.5 %collective-permute-start.8 = (f32[64,512]{1,0:T(8,128)S(1)}, f32[64,512]{1,0:T(8,128)S(1)}, u32[]{:S(2)}, u32[]{:S(2)}) collective-permute-start(f32[64,512]{1,0:T(8,128)S(1)} %get-tuple-element.40.refs_1_), channel_id=1, source_target_pairs={{1,9},{2,10},{17,25},{18,26}} | collective-permute-start | bytes 393224 | tf_op jit(solution)/shard_map/ppermute | solution.py:273
  41.0 0.7 collective-permute-start.11
  41.7 1.4 %collective-permute-start.12 = (f32[64,512]{1,0:T(8,128)S(1)}, f32[64,512]{1,0:T(8,128)S(1)}, u32[]{:S(2)}, u32[]{:S(2)}) collective-permute-start(f32[64,512]{1,0:T(8,128)S(1)} %shard_map.104.refs_1_), channel_id=1, source_target_pairs={{5,13},{6,14},{21,29},{22,30}} | collective-permute-start | bytes 393224 | tf_op jit(solution)/shard_map/ppermute | solution.py:273
  42.4 0.7 collective-permute-start.13
  43.2 20.0 %collective-permute-start.14 = (f32[64,512]{1,0:T(8,128)S(1)}, f32[64,512]{1,0:T(8,128)S(1)}, u32[]{:S(2)}, u32[]{:S(2)}) collective-permute-start(f32[64,512]{1,0:T(8,128)S(1)} %shard_map.105.x_ref), channel_id=1, source_target_pairs={{1,0},{2,3},{5,4},{6,7},{9,8},{10,11},{13,12},{14,15},{17,16},{18,... | collective-permute-start | bytes 393224 | tf_op jit(solution)/shard_map/ppermute | solution.py:279
  44.5 18.7 %collective-permute-start.15 = (f32[64,512]{1,0:T(8,128)S(1)}, f32[64,512]{1,0:T(8,128)S(1)}, u32[]{:S(2)}, u32[]{:S(2)}) collective-permute-start(f32[64,512]{1,0:T(8,128)S(1)} %shard_map.105.x_ref), channel_id=1, source_target_pairs={{1,2},{2,1},{5,6},{6,5},{9,10},{10,9},{13,14},{14,13},{17,18},{18,... | collective-permute-start | bytes 393224 | tf_op jit(solution)/shard_map/ppermute | solution.py:279
  45.2 22.6 %collective-permute-start.16 = (f32[64,512]{1,0:T(8,128)S(1)}, f32[64,512]{1,0:T(8,128)S(1)}, u32[]{:S(2)}, u32[]{:S(2)}) collective-permute-start(f32[64,512]{1,0:T(8,128)S(1)} %shard_map.105.x_ref), channel_id=1, source_target_pairs={{1,3},{2,0},{5,7},{6,4},{9,11},{10,8},{13,15},{14,12},{17,19},{18,... | collective-permute-start | bytes 393224 | tf_op jit(solution)/shard_map/ppermute | solution.py:279
  68.0 5.7 %collective-permute-start.17 = (f32[512,128]{1,0:T(8,128)S(1)}, f32[512,128]{1,0:T(8,128)S(1)}, u32[]{:S(2)}, u32[]{:S(2)}) collective-permute-start(f32[512,128]{1,0:T(8,128)S(1)} %shard_map.106.part_ref), channel_id=1, source_target_pairs={{0,16},{16,0},{1,17},{17,1},{2,18},{18,2},{3,19},{19,3},{4,20},{20... | collective-permute-start | bytes 786440 | tf_op jit(solution)/shard_map/ppermute | solution.py:269

commit v6 on v5

--- a/solution.py
+++ b/solution.py
@@ -213,7 +213,7 @@
         out_refs[-1][...] = left
 
 
-def half_kernel(x_ref, a_ref, b_ref, c_ref, out_ref):
+def half_kernel(c_ref, a_ref, b_ref, x_ref, out_ref):
     _, _, z = place()
     x, a, b, c = x_ref[...], a_ref[...], b_ref[...], c_ref[...]
     low = jnp.where(z == 0, a, jnp.where(z == 1, x, jnp.where(z == 2, b, c)))
@@ -302,14 +302,11 @@
     )
     diag = [diag_high, diag_low]
     first, second = call(pieces_kernel, [sums[0]] + got, [shape] * 2, [(half, size)])
-    sent, first, second = lax.optimization_barrier((sent, first, second))
     q = [
+        along_col(second, [(0, 2), (3, 1)]),
+        along_col(first, [(1, 2), (2, 1)]),
         along_col(first, [(0, 1), (3, 2)]),
-        along_col(first, [(1, 2), (2, 1)]),
-        along_col(second, [(0, 2), (3, 1)]),
     ]
-    factor = call(factor_kernel, [top_factor, sent, swap(sent)], [block] * 6)
-    factor = [factor[0:2], factor[2:4], factor[4:6]]
 
     def chain(owner, ins, has_sums=False, solves=True):
         outs = call(
@@ -318,6 +315,9 @@
         return outs if has_sums else outs[0]
 
     res, x = chain(0, [rhs_piece, second] + q + diag, has_sums=True)
+    sent, res = lax.optimization_barrier((sent, res))
+    factor = call(factor_kernel, [top_factor, sent, swap(sent)], [block] * 6)
+    factor = [factor[0:2], factor[2:4], factor[4:6]]
     to1 = hop(x, [(0, 1)])
     to2 = hop(x, [(0, 2)])
     x = chain(1, [res, x] + diag + [to1] + factor[0])
@@ -327,12 +327,12 @@
     to3 = hop(x, [(2, 3)])
     late = hop(x, [(1, 3)])
     res = chain(3, [res, res, on] + factor[0], solves=False)
-    x = chain(3, [res, x] + diag + [late] + factor[1] + [to3] + factor[2])
+    x = chain(3, [res, x] + diag + [to3] + factor[2] + [late] + factor[1])
 
     both = along_col(x, [(1, 2), (2, 1)])
     step = along_col(x, [(1, 0), (2, 3)])
     over = along_col(x, [(1, 3), (2, 0)])
-    (own,) = call(half_kernel, [x, step, both, over], [(size, half)])
+    (own,) = call(half_kernel, [over, step, both, x], [(size, half)])
     (top_sol,) = call(
         functools.partial(write_kernel, True), [own], [top_rhs.shape], [dma(())], outs_outside=(0,)
     )

time: 74.7 us -> 70.1 us (0.938)
  the two profiles are of different devices: /device:TPU:7 before, /device:TPU:15 now
where the time goes in v6:
time: 70.1 us; the launch traced here: 69.5 us
  waiting for transfers between devices  32.5 us (46%)
  starting transfers between devices  26.9 us (38%)
  Pallas kernels  9.1 us (13%)
  between operations  0.91 us (1%)
    ppermute x5, waiting for transfers between devices, hop(): return lax.ppermute(value, ('row', 'col'), pairs)  10.9 us
    ppermute x6, starting transfers between devices, along_col(): return lax.ppermute(value, 'col', pairs)  10.7 us
    ppermute x3, waiting for transfers between devices, along_row(): return lax.ppermute(value, 'row', pairs)  10.4 us
    pallas_call x14, Pallas kernels, call(): pl.pallas_call(kernel, out_shape=[shape(i, out) for i, out in enumerate(o...  9.1 us
    ppermute x6, waiting for transfers between devices, along_col(): return lax.ppermute(value, 'col', pairs)  8.67 us
    ppermute x3, starting transfers between devices, swap(): return lax.ppermute(value, 'leaf', [(0, 1), (1, 0)])  7.07 us
    ppermute x5, starting transfers between devices, hop(): return lax.ppermute(value, ('row', 'col'), pairs)  5.2 us
    ppermute x3, starting transfers between devices, along_row(): return lax.ppermute(value, 'row', pairs)  2.71 us
  transfers between devices with their start and end apart: 18, of which 11 were waited for; matrix products, arithmetic and copies ran while one was open for 0% of the time, Pallas kernels for 11%

profile of v6, /device:TPU:15, one launch (start us, length us, event | category | flops | bytes accessed | tf_op | source)
XLA Modules:
  0.0 69.5 jit_solution(15483174938330410082)
XLA Ops:
  0.6 1.3 %collective-permute-start = (f32[512,512]{1,0:T(8,128)}, f32[512,512]{1,0:T(8,128)S(1)}, u32[]{:S(2)}, u32[]{:S(2)}) collective-permute-start(f32[512,512]{1,0:T(8,128)} %own_ref.1), channel_id=1, source_target_pairs={{4,5},{8,9},{12,13},{9,10},{13,14},{20,22},{24,26},{28,30},{30,29}} | collective-permute-start | bytes 3145736 | tf_op jit(solution)/shard_map/ppermute | solution.py:284
  1.9 3.7 %shard_map.95 = (f32[2,256,256]{2,1,0:T(8,128)}, f32[128,512]{1,0:T(8,128)S(1)}, f32[136,512]{1,0:T(8,128)S(1)}) custom-call(s32[2]{0:T(128)} %live_ref.1, f32[2,256,256]{2,1,0:T(8,128)} %rhs_hbm.1, f32[2,256,256]{2,1,0:T(8,128)} %diag_hbm.1, f32[2,256,256]{2,1,0:T(8,128)} %off_hbm.1, s32[2,256]{1,0:T(2,128)} %tgt_ref.3), custom_call_target="tpu_custom_call" | custom-call | bytes 1574920 | tf_op jit(solution)/shard_map/pallas_call | solution.py:242
  5.6 0.0 copy-start.1
  5.7 2.9 %collective-permute-start.1 = (f32[136,512]{1,0:T(8,128)S(1)}, f32[136,512]{1,0:T(8,128)S(1)}, u32[]{:S(2)}, u32[]{:S(2)}) collective-permute-start(f32[136,512]{1,0:T(8,128)S(1)} %get-tuple-element.27), channel_id=1, source_target_pairs={{0,16},{16,0},{1,17},{17,1},{2,18},{18,2},{3,19},{19,3},{4,20},{20... | collective-permute-start | bytes 835592 | tf_op jit(solution)/shard_map/ppermute | solution.py:269
  8.6 1.2 %collective-permute-done.1.recv_ref = f32[136,512]{1,0:T(8,128)S(1)} collective-permute-done((f32[136,512]{1,0:T(8,128)S(1)}, f32[136,512]{1,0:T(8,128)S(1)}, u32[]{:S(2)}, u32[]{:S(2)}) %collective-permute-start.1) | collective-permute-done | bytes 278560 | tf_op jit(solution)/shard_map/ppermute | solution.py:269
  9.8 1.3 %shard_map.97 = (f32[128,512]{1,0:T(8,128)S(1)}, f32[128,512]{1,0:T(8,128)S(1)}, f32[128,512]{1,0:T(8,128)S(1)}, f32[128,512]{1,0:T(8,128)S(1)}) custom-call(f32[128,512]{1,0:T(8,128)S(1)} %get-tuple-element.26.keep_ref, f32[136,512]{1,0:T(8,128)S(1)} %collective-permute-done.1.recv_ref, s32[2,256]{1,0:T(2,128)S(1)} %copy-done.3), custom_call_target="tpu_custom_call" | custom-call | bytes 542720 | tf_op jit(solution)/shard_map/pallas_call | solution.py:242
  11.1 0.3 collective-permute-start.2
  11.4 0.0 collective-permute-start.3
  11.4 2.4 %collective-permute-start.4 = (f32[128,512]{1,0:T(8,128)S(1)}, f32[128,512]{1,0:T(8,128)S(1)}, u32[]{:S(2)}, u32[]{:S(2)}) collective-permute-start(f32[128,512]{1,0:T(8,128)S(1)} %get-tuple-element.31), channel_id=1, source_target_pairs={{0,12},{4,8},{8,4},{12,0},{1,13},{5,9},{9,5},{13,1},{2,14},{6,10},... | collective-permute-start | bytes 786440 | tf_op jit(solution)/shard_map/ppermute | solution.py:276
  13.8 4.9 %collective-permute-done.2.b_ref = f32[128,512]{1,0:T(8,128)S(1)} collective-permute-done((f32[128,512]{1,0:T(8,128)S(1)}, f32[128,512]{1,0:T(8,128)S(1)}, u32[]{:S(2)}, u32[]{:S(2)}) %collective-permute-start.2) | collective-permute-done | bytes 262176 | tf_op jit(solution)/shard_map/ppermute | solution.py:276
  18.7 5.5 %collective-permute-done.3.c_ref = f32[128,512]{1,0:T(8,128)S(1)} collective-permute-done((f32[128,512]{1,0:T(8,128)S(1)}, f32[128,512]{1,0:T(8,128)S(1)}, u32[]{:S(2)}, u32[]{:S(2)}) %collective-permute-start.3) | collective-permute-done | bytes 262176 | tf_op jit(solution)/shard_map/ppermute | solution.py:276
  24.2 0.0 collective-permute-done.4.d_ref
  24.2 0.1 shard_map.98
  24.3 1.4 %collective-permute-start.5 = (f32[64,512]{1,0:T(8,128)S(1)}, f32[64,512]{1,0:T(8,128)S(1)}, u32[]{:S(2)}, u32[]{:S(2)}) collective-permute-start(f32[64,512]{1,0:T(8,128)S(1)} %get-tuple-element.32.refs_1_), channel_id=1, source_target_pairs={{0,2},{3,1},{4,6},{7,5},{8,10},{11,9},{12,14},{15,13},{16,18},{19,... | collective-permute-start | bytes 393224 | tf_op jit(solution)/shard_map/ppermute | solution.py:279
  25.7 1.9 %collective-permute-start.6 = (f32[64,512]{1,0:T(8,128)S(1)}, f32[64,512]{1,0:T(8,128)S(1)}, u32[]{:S(2)}, u32[]{:S(2)}) collective-permute-start(f32[64,512]{1,0:T(8,128)S(1)} %get-tuple-element.33), channel_id=1, source_target_pairs={{1,2},{2,1},{5,6},{6,5},{9,10},{10,9},{13,14},{14,13},{17,18},{18,... | collective-permute-start | bytes 393224 | tf_op jit(solution)/shard_map/ppermute | solution.py:279
  27.7 1.3 %collective-permute-start.7 = (f32[64,512]{1,0:T(8,128)S(1)}, f32[64,512]{1,0:T(8,128)S(1)}, u32[]{:S(2)}, u32[]{:S(2)}) collective-permute-start(f32[64,512]{1,0:T(8,128)S(1)} %get-tuple-element.33), channel_id=1, source_target_pairs={{0,1},{3,2},{4,5},{7,6},{8,9},{11,10},{12,13},{15,14},{16,17},{19,... | collective-permute-start | bytes 393224 | tf_op jit(solution)/shard_map/ppermute | solution.py:279
  29.0 0.3 shard_map.96
  29.3 0.0 copy-start
  29.3 1.8 %collective-permute-done.5.refs_2_ = f32[64,512]{1,0:T(8,128)S(1)} collective-permute-done((f32[64,512]{1,0:T(8,128)S(1)}, f32[64,512]{1,0:T(8,128)S(1)}, u32[]{:S(2)}, u32[]{:S(2)}) %collective-permute-start.5) | collective-permute-done | bytes 131104 | tf_op jit(solution)/shard_map/ppermute | solution.py:279
  31.1 3.6 %collective-permute-done.6.refs_3_ = f32[64,512]{1,0:T(8,128)S(1)} collective-permute-done((f32[64,512]{1,0:T(8,128)S(1)}, f32[64,512]{1,0:T(8,128)S(1)}, u32[]{:S(2)}, u32[]{:S(2)}) %collective-permute-start.6) | collective-permute-done | bytes 131104 | tf_op jit(solution)/shard_map/ppermute | solution.py:279
  34.8 0.0 collective-permute-done.7.refs_4_
  34.8 0.0 collective-permute-done.sent_ref
  34.8 1.3 %collective-permute-start.9 = (f32[512,512]{1,0:T(8,128)S(1)}, f32[512,512]{1,0:T(8,128)S(1)}, u32[]{:S(2)}, u32[]{:S(2)}) collective-permute-start(f32[512,512]{1,0:T(8,128)S(1)} %collective-permute-done.sent_ref), channel_id=1, source_target_pairs={{0,16},{16,0},{1,17},{17,1},{2,18},{18,2},{3,19},{19,3},{4,20},{20... | collective-permute-start | bytes 3145736 | tf_op jit(solution)/shard_map/ppermute | solution.py:269
  36.2 0.7 collective-permute-start.10
  36.8 0.7 collective-permute-start.8
  37.5 0.9 %collective-permute-done.9.other_ref = f32[512,512]{1,0:T(8,128)S(1)} collective-permute-done((f32[512,512]{1,0:T(8,128)S(1)}, f32[512,512]{1,0:T(8,128)S(1)}, u32[]{:S(2)}, u32[]{:S(2)}) %collective-permute-start.9) | collective-permute-done | bytes 1048608 | tf_op jit(solution)/shard_map/ppermute | solution.py:269
  38.5 1.0 %shard_map.100 = (bf16[512,512]{1,0:T(8,128)(2,1)S(1)}, bf16[512,512]{1,0:T(8,128)(2,1)S(1)}, bf16[512,512]{1,0:T(8,128)(2,1)S(1)}, bf16[512,512]{1,0:T(8,128)(2...) custom-call(f32[512,512]{1,0:T(8,128)S(1)} %copy-done, ...), custom_call_target="tpu_custom_call" | custom-call | bytes 3145728 | tf_op jit(solution)/shard_map/pallas_call | solution.py:242
  39.5 0.0 collective-permute-done.10.refs_4_
  39.5 1.3 %collective-permute-start.11 = (f32[64,512]{1,0:T(8,128)S(1)}, f32[64,512]{1,0:T(8,128)S(1)}, u32[]{:S(2)}, u32[]{:S(2)}) collective-permute-start(f32[64,512]{1,0:T(8,128)S(1)} %shard_map.102.refs_1_), channel_id=1, source_target_pairs={{5,9},{6,10},{1,13},{2,14},{21,25},{22,26},{17,29},{18,30}} | collective-permute-start | bytes 393224 | tf_op jit(solution)/shard_map/ppermute | solution.py:273
  40.8 0.0 collective-permute-done.8.refs_2_
  40.9 6.8 %collective-permute-done.11.refs_2_.refs_4_ = f32[64,512]{1,0:T(8,128)S(1)} collective-permute-done((f32[64,512]{1,0:T(8,128)S(1)}, f32[64,512]{1,0:T(8,128)S(1)}, u32[]{:S(2)}, u32[]{:S(2)}) %collective-permute-start.11) | collective-permute-done | bytes 131104 | tf_op jit(solution)/shard_map/ppermute | solution.py:273
  47.7 1.3 %collective-permute-start.12 = (f32[64,512]{1,0:T(8,128)S(1)}, f32[64,512]{1,0:T(8,128)S(1)}, u32[]{:S(2)}, u32[]{:S(2)}) collective-permute-start(f32[64,512]{1,0:T(8,128)S(1)} %shard_map.104.refs_1_), channel_id=1, source_target_pairs={{9,13},{10,14},{25,29},{26,30}} | collective-permute-start | bytes 393224 | tf_op jit(solution)/shard_map/ppermute | solution.py:273
  49.0 1.3 %collective-permute-start.13 = (f32[64,512]{1,0:T(8,128)S(1)}, f32[64,512]{1,0:T(8,128)S(1)}, u32[]{:S(2)}, u32[]{:S(2)}) collective-permute-start(f32[64,512]{1,0:T(8,128)S(1)} %shard_map.104.refs_1_), channel_id=1, source_target_pairs={{5,13},{6,14},{21,29},{22,30}} | collective-permute-start | bytes 393224 | tf_op jit(solution)/shard_map/ppermute | solution.py:273
  50.3 0.3 shard_map.103.refs_0_
  50.6 4.0 %collective-permute-done.12.refs_4_ = f32[64,512]{1,0:T(8,128)S(1)} collective-permute-done((f32[64,512]{1,0:T(8,128)S(1)}, f32[64,512]{1,0:T(8,128)S(1)}, u32[]{:S(2)}, u32[]{:S(2)}) %collective-permute-start.12) | collective-permute-done | bytes 131104 | tf_op jit(solution)/shard_map/ppermute | solution.py:273
  54.6 0.1 collective-permute-done.13.refs_7_
  54.7 0.7 %shard_map.105.x_ref = f32[64,512]{1,0:T(8,128)S(1)} custom-call(f32[64,512]{1,0:T(8,128)S(1)} %shard_map.103.refs_0_, f32[64,512]{1,0:T(8,128)S(1)} %shard_map.104.refs_1_, bf16[512,512]{1,0:T(8,128)(2,1)S(1)} %get-tuple-element.34.refs_5_.refs_2_, bf16[512,512]{1,0:T(8,128)(2,1)S(1)} %get-tuple-element.35.refs_6_.refs_3_, ...), custom_call_target="tpu_custom_call" | custom-call | bytes 6815744 | tf_op jit(solution)/shard_map/pallas_call | solution.py:242
  55.4 1.3 %collective-permute-start.14 = (f32[64,512]{1,0:T(8,128)S(1)}, f32[64,512]{1,0:T(8,128)S(1)}, u32[]{:S(2)}, u32[]{:S(2)}) collective-permute-start(f32[64,512]{1,0:T(8,128)S(1)} %shard_map.105.x_ref), channel_id=1, source_target_pairs={{1,3},{2,0},{5,7},{6,4},{9,11},{10,8},{13,15},{14,12},{17,19},{18,... | collective-permute-start | bytes 393224 | tf_op jit(solution)/shard_map/ppermute | solution.py:279
  56.7 1.3 %collective-permute-start.15 = (f32[64,512]{1,0:T(8,128)S(1)}, f32[64,512]{1,0:T(8,128)S(1)}, u32[]{:S(2)}, u32[]{:S(2)}) collective-permute-start(f32[64,512]{1,0:T(8,128)S(1)} %shard_map.105.x_ref), channel_id=1, source_target_pairs={{1,0},{2,3},{5,4},{6,7},{9,8},{10,11},{13,12},{14,15},{17,16},{18,... | collective-permute-start | bytes 393224 | tf_op jit(solution)/shard_map/ppermute | solution.py:279
  58.0 3.4 %collective-permute-start.16 = (f32[64,512]{1,0:T(8,128)S(1)}, f32[64,512]{1,0:T(8,128)S(1)}, u32[]{:S(2)}, u32[]{:S(2)}) collective-permute-start(f32[64,512]{1,0:T(8,128)S(1)} %shard_map.105.x_ref), channel_id=1, source_target_pairs={{1,2},{2,1},{5,6},{6,5},{9,10},{10,9},{13,14},{14,13},{17,18},{18,... | collective-permute-start | bytes 393224 | tf_op jit(solution)/shard_map/ppermute | solution.py:279
  61.5 0.0 collective-permute-done.14.c_ref
  61.5 0.0 collective-permute-done.15.a_ref
  61.5 3.2 %collective-permute-done.16.b_ref = f32[64,512]{1,0:T(8,128)S(1)} collective-permute-done((f32[64,512]{1,0:T(8,128)S(1)}, f32[64,512]{1,0:T(8,128)S(1)}, u32[]{:S(2)}, u32[]{:S(2)}) %collective-permute-start.16) | collective-permute-done | bytes 131104 | tf_op jit(solution)/shard_map/ppermute | solution.py:279
  64.7 0.1 shard_map.106.part_ref
  64.8 2.8 %collective-permute-start.17 = (f32[512,128]{1,0:T(8,128)S(1)}, f32[512,128]{1,0:T(8,128)S(1)}, u32[]{:S(2)}, u32[]{:S(2)}) collective-permute-start(f32[512,128]{1,0:T(8,128)S(1)} %shard_map.106.part_ref), channel_id=1, source_target_pairs={{0,16},{16,0},{1,17},{17,1},{2,18},{18,2},{3,19},{19,3},{4,20},{20... | collective-permute-start | bytes 786440 | tf_op jit(solution)/shard_map/ppermute | solution.py:269
  67.6 0.7 %shard_map.107.refs_0_ = f32[512,256]{1,0:T(8,128)} custom-call(f32[512,128]{1,0:T(8,128)S(1)} %shard_map.106.part_ref), custom_call_target="tpu_custom_call" | custom-call | bytes 262144 | tf_op jit(solution)/shard_map/pallas_call | solution.py:242
  68.3 0.4 collective-permute-done.17.part_ref
  68.8 0.7 %shard_map.108 = f32[512,256]{1,0:T(8,128)} custom-call(f32[512,128]{1,0:T(8,128)S(1)} %collective-permute-done.17.part_ref, f32[512,256]{1,0:T(8,128)} %shard_map.107.refs_0_), custom_call_target="tpu_custom_call", output_to_operand_aliasing={{}: (1, {})} | custom-call | bytes 786432 | tf_op jit(solution)/shard_map/pallas_call | solution.py:242
  (10 shorter events, 0.1 us)
Async XLA Ops:
  0.6 34.2 %collective-permute-start = (f32[512,512]{1,0:T(8,128)}, f32[512,512]{1,0:T(8,128)S(1)}, u32[]{:S(2)}, u32[]{:S(2)}) collective-permute-start(f32[512,512]{1,0:T(8,128)} %own_ref.1), channel_id=1, source_target_pairs={{4,5},{8,9},{12,13},{9,10},{13,14},{20,22},{24,26},{28,30},{30,29}} | collective-permute-start | bytes 3145736 | tf_op jit(solution)/shard_map/ppermute | solution.py:284
  1.9 7.9 %copy-start.3 = (s32[2,256]{1,0:T(2,128)S(1)}, s32[2,256]{1,0:T(2,128)}, u32[]{:S(2)}) copy-start(s32[2,256]{1,0:T(2,128)} %tgt_ref.3) | copy-start | bytes 6148
  5.6 23.3 %copy-start.1 = (f32[512,512]{1,0:T(8,128)S(1)}, f32[512,512]{1,0:T(8,128)}, u32[]{:S(2)}) copy-start(f32[512,512]{1,0:T(8,128)} %diag_ref.1) | copy-start | bytes 3145732
  5.7 4.1 %collective-permute-start.1 = (f32[136,512]{1,0:T(8,128)S(1)}, f32[136,512]{1,0:T(8,128)S(1)}, u32[]{:S(2)}, u32[]{:S(2)}) collective-permute-start(f32[136,512]{1,0:T(8,128)S(1)} %get-tuple-element.27), channel_id=1, source_target_pairs={{0,16},{16,0},{1,17},{17,1},{2,18},{18,2},{3,19},{19,3},{4,20},{20... | collective-permute-start | bytes 835592 | tf_op jit(solution)/shard_map/ppermute | solution.py:269
  11.1 7.6 %collective-permute-start.2 = (f32[128,512]{1,0:T(8,128)S(1)}, f32[128,512]{1,0:T(8,128)S(1)}, u32[]{:S(2)}, u32[]{:S(2)}) collective-permute-start(f32[128,512]{1,0:T(8,128)S(1)} %get-tuple-element.29), channel_id=1, source_target_pairs={{0,4},{4,0},{8,12},{12,8},{1,5},{5,1},{9,13},{13,9},{2,6},{6,2},{1... | collective-permute-start | bytes 786440 | tf_op jit(solution)/shard_map/ppermute | solution.py:276
  11.4 12.8 %collective-permute-start.3 = (f32[128,512]{1,0:T(8,128)S(1)}, f32[128,512]{1,0:T(8,128)S(1)}, u32[]{:S(2)}, u32[]{:S(2)}) collective-permute-start(f32[128,512]{1,0:T(8,128)S(1)} %get-tuple-element.30), channel_id=1, source_target_pairs={{0,8},{4,12},{8,0},{12,4},{1,9},{5,13},{9,1},{13,5},{2,10},{6,14},... | collective-permute-start | bytes 786440 | tf_op jit(solution)/shard_map/ppermute | solution.py:276
  11.4 12.8 %collective-permute-start.4 = (f32[128,512]{1,0:T(8,128)S(1)}, f32[128,512]{1,0:T(8,128)S(1)}, u32[]{:S(2)}, u32[]{:S(2)}) collective-permute-start(f32[128,512]{1,0:T(8,128)S(1)} %get-tuple-element.31), channel_id=1, source_target_pairs={{0,12},{4,8},{8,4},{12,0},{1,13},{5,9},{9,5},{13,1},{2,14},{6,10},... | collective-permute-start | bytes 786440 | tf_op jit(solution)/shard_map/ppermute | solution.py:276
  24.2 4.8 %copy-start.2 = (f32[512,256]{1,0:T(8,128)S(1)}, f32[512,256]{1,0:T(8,128)}, u32[]{:S(2)}) copy-start(f32[512,256]{1,0:T(8,128)} %rhs_ref.1) | copy-start | bytes 1572868
  24.3 6.8 %collective-permute-start.5 = (f32[64,512]{1,0:T(8,128)S(1)}, f32[64,512]{1,0:T(8,128)S(1)}, u32[]{:S(2)}, u32[]{:S(2)}) collective-permute-start(f32[64,512]{1,0:T(8,128)S(1)} %get-tuple-element.32.refs_1_), channel_id=1, source_target_pairs={{0,2},{3,1},{4,6},{7,5},{8,10},{11,9},{12,14},{15,13},{16,18},{19,... | collective-permute-start | bytes 393224 | tf_op jit(solution)/shard_map/ppermute | solution.py:279
  25.7 9.1 %collective-permute-start.6 = (f32[64,512]{1,0:T(8,128)S(1)}, f32[64,512]{1,0:T(8,128)S(1)}, u32[]{:S(2)}, u32[]{:S(2)}) collective-permute-start(f32[64,512]{1,0:T(8,128)S(1)} %get-tuple-element.33), channel_id=1, source_target_pairs={{1,2},{2,1},{5,6},{6,5},{9,10},{10,9},{13,14},{14,13},{17,18},{18,... | collective-permute-start | bytes 393224 | tf_op jit(solution)/shard_map/ppermute | solution.py:279
  27.7 7.1 %collective-permute-start.7 = (f32[64,512]{1,0:T(8,128)S(1)}, f32[64,512]{1,0:T(8,128)S(1)}, u32[]{:S(2)}, u32[]{:S(2)}) collective-permute-start(f32[64,512]{1,0:T(8,128)S(1)} %get-tuple-element.33), channel_id=1, source_target_pairs={{0,1},{3,2},{4,5},{7,6},{8,9},{11,10},{12,13},{15,14},{16,17},{19,... | collective-permute-start | bytes 393224 | tf_op jit(solution)/shard_map/ppermute | solution.py:279
  29.3 9.2 %copy-start = (f32[512,512]{1,0:T(8,128)S(1)}, f32[512,512]{1,0:T(8,128)}, u32[]{:S(2)}) copy-start(f32[512,512]{1,0:T(8,128)} %own_ref.1) | copy-start | bytes 3145732
  34.8 3.6 %collective-permute-start.9 = (f32[512,512]{1,0:T(8,128)S(1)}, f32[512,512]{1,0:T(8,128)S(1)}, u32[]{:S(2)}, u32[]{:S(2)}) collective-permute-start(f32[512,512]{1,0:T(8,128)S(1)} %collective-permute-done.sent_ref), channel_id=1, source_target_pairs={{0,16},{16,0},{1,17},{17,1},{2,18},{18,2},{3,19},{19,3},{4,20},{20... | collective-permute-start | bytes 3145736 | tf_op jit(solution)/shard_map/ppermute | solution.py:269
  36.2 3.3 %collective-permute-start.10 = (f32[64,512]{1,0:T(8,128)S(1)}, f32[64,512]{1,0:T(8,128)S(1)}, u32[]{:S(2)}, u32[]{:S(2)}) collective-permute-start(f32[64,512]{1,0:T(8,128)S(1)} %get-tuple-element.38.refs_1_), channel_id=1, source_target_pairs={{1,5},{2,6},{17,21},{18,22}} | collective-permute-start | bytes 393224 | tf_op jit(solution)/shard_map/ppermute | solution.py:273
  36.8 4.0 %collective-permute-start.8 = (f32[64,512]{1,0:T(8,128)S(1)}, f32[64,512]{1,0:T(8,128)S(1)}, u32[]{:S(2)}, u32[]{:S(2)}) collective-permute-start(f32[64,512]{1,0:T(8,128)S(1)} %get-tuple-element.38.refs_1_), channel_id=1, source_target_pairs={{1,9},{2,10},{17,25},{18,26}} | collective-permute-start | bytes 393224 | tf_op jit(solution)/shard_map/ppermute | solution.py:273
  39.5 8.1 %collective-permute-start.11 = (f32[64,512]{1,0:T(8,128)S(1)}, f32[64,512]{1,0:T(8,128)S(1)}, u32[]{:S(2)}, u32[]{:S(2)}) collective-permute-start(f32[64,512]{1,0:T(8,128)S(1)} %shard_map.102.refs_1_), channel_id=1, source_target_pairs={{5,9},{6,10},{1,13},{2,14},{21,25},{22,26},{17,29},{18,30}} | collective-permute-start | bytes 393224 | tf_op jit(solution)/shard_map/ppermute | solution.py:273
  47.7 6.9 %collective-permute-start.12 = (f32[64,512]{1,0:T(8,128)S(1)}, f32[64,512]{1,0:T(8,128)S(1)}, u32[]{:S(2)}, u32[]{:S(2)}) collective-permute-start(f32[64,512]{1,0:T(8,128)S(1)} %shard_map.104.refs_1_), channel_id=1, source_target_pairs={{9,13},{10,14},{25,29},{26,30}} | collective-permute-start | bytes 393224 | tf_op jit(solution)/shard_map/ppermute | solution.py:273
  49.0 5.7 %collective-permute-start.13 = (f32[64,512]{1,0:T(8,128)S(1)}, f32[64,512]{1,0:T(8,128)S(1)}, u32[]{:S(2)}, u32[]{:S(2)}) collective-permute-start(f32[64,512]{1,0:T(8,128)S(1)} %shard_map.104.refs_1_), channel_id=1, source_target_pairs={{5,13},{6,14},{21,29},{22,30}} | collective-permute-start | bytes 393224 | tf_op jit(solution)/shard_map/ppermute | solution.py:273
  55.4 6.0 %collective-permute-start.14 = (f32[64,512]{1,0:T(8,128)S(1)}, f32[64,512]{1,0:T(8,128)S(1)}, u32[]{:S(2)}, u32[]{:S(2)}) collective-permute-start(f32[64,512]{1,0:T(8,128)S(1)} %shard_map.105.x_ref), channel_id=1, source_target_pairs={{1,3},{2,0},{5,7},{6,4},{9,11},{10,8},{13,15},{14,12},{17,19},{18,... | collective-permute-start | bytes 393224 | tf_op jit(solution)/shard_map/ppermute | solution.py:279
  56.7 4.7 %collective-permute-start.15 = (f32[64,512]{1,0:T(8,128)S(1)}, f32[64,512]{1,0:T(8,128)S(1)}, u32[]{:S(2)}, u32[]{:S(2)}) collective-permute-start(f32[64,512]{1,0:T(8,128)S(1)} %shard_map.105.x_ref), channel_id=1, source_target_pairs={{1,0},{2,3},{5,4},{6,7},{9,8},{10,11},{13,12},{14,15},{17,16},{18,... | collective-permute-start | bytes 393224 | tf_op jit(solution)/shard_map/ppermute | solution.py:279
  58.0 6.6 %collective-permute-start.16 = (f32[64,512]{1,0:T(8,128)S(1)}, f32[64,512]{1,0:T(8,128)S(1)}, u32[]{:S(2)}, u32[]{:S(2)}) collective-permute-start(f32[64,512]{1,0:T(8,128)S(1)} %shard_map.105.x_ref), channel_id=1, source_target_pairs={{1,2},{2,1},{5,6},{6,5},{9,10},{10,9},{13,14},{14,13},{17,18},{18,... | collective-permute-start | bytes 393224 | tf_op jit(solution)/shard_map/ppermute | solution.py:279
  64.8 4.0 %collective-permute-start.17 = (f32[512,128]{1,0:T(8,128)S(1)}, f32[512,128]{1,0:T(8,128)S(1)}, u32[]{:S(2)}, u32[]{:S(2)}) collective-permute-start(f32[512,128]{1,0:T(8,128)S(1)} %shard_map.106.part_ref), channel_id=1, source_target_pairs={{0,16},{16,0},{1,17},{17,1},{2,18},{18,2},{3,19},{19,3},{4,20},{20... | collective-permute-start | bytes 786440 | tf_op jit(solution)/shard_map/ppermute | solution.py:269

commit v7 on v6

--- a/solution.py
+++ b/solution.py
@@ -231,7 +231,7 @@
     copy.wait()
 
 
-def call(kernel, ins, outs, scratch=(), outside=(), outs_outside=(), pinned=(), aliases=None, limit=24):
+def call(kernel, ins, outs, scratch=(), outside=(), outs_outside=(), pinned=(), aliases=None, limit=24, flops=0):
     def spec(i, a):
         return ANY if i in outside else SM if a.ndim == 1 else VM
 
@@ -246,7 +246,7 @@
         out_specs=[ANY if i in outs_outside else VM for i in range(len(outs))],
         scratch_shapes=[pltpu.VMEM(s, F32) if isinstance(s, tuple) else s for s in scratch],
         input_output_aliases=aliases or {},
-        cost_estimate=pl.CostEstimate(flops=0, bytes_accessed=4 * sum(a.size for a in ins), transcendentals=0),
+        cost_estimate=pl.CostEstimate(flops=flops, bytes_accessed=4 * sum(a.size for a in ins), transcendentals=0),
         compiler_params=pltpu.CompilerParams(vmem_limit_bytes=limit * 1024 * 1024),
     )(*ins)
     return list(outs)
@@ -301,7 +301,7 @@
         turn_kernel, [top_rhs, top_diag], [shape, block, block], [(half, size)]
     )
     diag = [diag_high, diag_low]
-    first, second = call(pieces_kernel, [sums[0]] + got, [shape] * 2, [(half, size)])
+    first, second = call(pieces_kernel, [sums[0]] + got, [shape] * 2, [(half, size)], flops=10 ** 11)
     q = [
         along_col(second, [(0, 2), (3, 1)]),
         along_col(first, [(1, 2), (2, 1)]),
@@ -316,7 +316,11 @@
 
     res, x = chain(0, [rhs_piece, second] + q + diag, has_sums=True)
     sent, res = lax.optimization_barrier((sent, res))
-    factor = call(factor_kernel, [top_factor, sent, swap(sent)], [block] * 6)
+    middle = [at(k, z) for k in (1, 2, 3) for z in (1, 2)]
+    other = lax.ppermute(
+        sent, ("leaf", "row", "col"), [(a + b, a + shift - b) for a in middle for b in (0, shift)]
+    )
+    factor = call(factor_kernel, [top_factor, sent, other], [block] * 6)
     factor = [factor[0:2], factor[2:4], factor[4:6]]
     to1 = hop(x, [(0, 1)])
     to2 = hop(x, [(0, 2)])

time: 70.1 us -> 79.3 us (1.13)
  waiting for transfers between devices: 32.5 us -> 41.3 us
    ppermute x6, waiting for transfers between devices: 8.67 us -> 19 us  [along_col(): return lax.ppermute(value, 'col', pairs)]
    ppermute x3 -> x2, starting transfers between devices: 7.07 us -> 3.78 us  [swap(): return lax.ppermute(value, 'leaf', [(0, 1), (1, 0)])]
    ppermute x0 -> x1, starting transfers between devices: none -> 2.92 us  [central(): lax.ppermute(sent, ('leaf', 'row', 'col'), [(a + b, a + shift - b) for a...]
    ppermute x3, waiting for transfers between devices: 10.4 us -> 9.19 us  [along_row(): return lax.ppermute(value, 'row', pairs)]
    ppermute x6, starting transfers between devices: 10.7 us -> 11.7 us  [along_col(): return lax.ppermute(value, 'col', pairs)]
    ppermute x3 -> x2, waiting for transfers between devices: 2.58 us -> 1.63 us  [swap(): return lax.ppermute(value, 'leaf', [(0, 1), (1, 0)])]
    ppermute x0 -> x1, waiting for transfers between devices: none -> 0.91 us  [central(): lax.ppermute(sent, ('leaf', 'row', 'col'), [(a + b, a + shift - b) for a...]
  transfers between devices with their start and end apart: 18 -> 18, of which waited for: 11 -> 13; matrix products, arithmetic and copies ran while one was open for 0% -> 0% of each run, Pallas kernels for 11% -> 3%
where the time goes in v7:
time: 79.3 us; the launch traced here: 78.9 us
  waiting for transfers between devices  41.3 us (52%)
  starting transfers between devices  27.6 us (35%)
  Pallas kernels  9.11 us (11%)
  between operations  0.9 us (1%)
    ppermute x6, waiting for transfers between devices, along_col(): return lax.ppermute(value, 'col', pairs)  19 us
    ppermute x6, starting transfers between devices, along_col(): return lax.ppermute(value, 'col', pairs)  11.7 us
    ppermute x5, waiting for transfers between devices, hop(): return lax.ppermute(value, ('row', 'col'), pairs)  10.6 us
    ppermute x3, waiting for transfers between devices, along_row(): return lax.ppermute(value, 'row', pairs)  9.19 us
    pallas_call x14, Pallas kernels, call(): pl.pallas_call(kernel, out_shape=[shape(i, out) for i, out in enumerate(o...  9.11 us
    ppermute x5, starting transfers between devices, hop(): return lax.ppermute(value, ('row', 'col'), pairs)  5.21 us
    ppermute x2, starting transfers between devices, swap(): return lax.ppermute(value, 'leaf', [(0, 1), (1, 0)])  3.78 us
    ppermute x1, starting transfers between devices, central(): lax.ppermute(sent, ('leaf', 'row', 'col'), [(a + b, a + shift - b) for a...  2.92 us
  transfers between devices with their start and end apart: 18, of which 13 were waited for; matrix products, arithmetic and copies ran while one was open for 0% of the time, Pallas kernels for 3%

profile of v7, /device:TPU:15, one launch (start us, length us, event | category | flops | bytes accessed | tf_op | source)
XLA Modules:
  0.0 78.9 jit_solution(15124573536009919156)
XLA Ops:
  0.6 0.0 copy-start
  0.6 3.7 %shard_map.95 = (f32[2,256,256]{2,1,0:T(8,128)}, f32[128,512]{1,0:T(8,128)S(1)}, f32[136,512]{1,0:T(8,128)S(1)}) custom-call(s32[2]{0:T(128)} %live_ref.1, f32[2,256,256]{2,1,0:T(8,128)} %rhs_hbm.1, f32[2,256,256]{2,1,0:T(8,128)} %diag_hbm.1, f32[2,256,256]{2,1,0:T(8,128)} %off_hbm.1, s32[2,256]{1,0:T(2,128)} %tgt_ref.3), custom_call_target="tpu_custom_call" | custom-call | bytes 1574920 | tf_op jit(solution)/shard_map/pallas_call | solution.py:242
  4.3 0.0 copy-start.3
  4.4 0.7 collective-permute-start.1
  5.1 1.2 %collective-permute-done.1.recv_ref = f32[136,512]{1,0:T(8,128)S(1)} collective-permute-done((f32[136,512]{1,0:T(8,128)S(1)}, f32[136,512]{1,0:T(8,128)S(1)}, u32[]{:S(2)}, u32[]{:S(2)}) %collective-permute-start.1) | collective-permute-done | bytes 278560 | tf_op jit(solution)/shard_map/ppermute | solution.py:269
  6.3 1.3 %shard_map.97 = (f32[128,512]{1,0:T(8,128)S(1)}, f32[128,512]{1,0:T(8,128)S(1)}, f32[128,512]{1,0:T(8,128)S(1)}, f32[128,512]{1,0:T(8,128)S(1)}) custom-call(f32[128,512]{1,0:T(8,128)S(1)} %get-tuple-element.26.keep_ref, f32[136,512]{1,0:T(8,128)S(1)} %collective-permute-done.1.recv_ref, s32[2,256]{1,0:T(2,128)S(1)} %copy-done.3), custom_call_target="tpu_custom_call" | custom-call | bytes 542720 | tf_op jit(solution)/shard_map/pallas_call | solution.py:242
  7.6 0.3 collective-permute-start.2
  7.9 0.2 collective-permute-start.3
  8.1 2.2 %collective-permute-start.4 = (f32[128,512]{1,0:T(8,128)S(1)}, f32[128,512]{1,0:T(8,128)S(1)}, u32[]{:S(2)}, u32[]{:S(2)}) collective-permute-start(f32[128,512]{1,0:T(8,128)S(1)} %get-tuple-element.31), channel_id=1, source_target_pairs={{0,12},{4,8},{8,4},{12,0},{1,13},{5,9},{9,5},{13,1},{2,14},{6,10},... | collective-permute-start | bytes 786440 | tf_op jit(solution)/shard_map/ppermute | solution.py:276
  10.3 1.3 %collective-permute-start = (f32[512,512]{1,0:T(8,128)S(1)}, f32[512,512]{1,0:T(8,128)S(1)}, u32[]{:S(2)}, u32[]{:S(2)}) collective-permute-start(f32[512,512]{1,0:T(8,128)S(1)} %copy-done), channel_id=1, source_target_pairs={{4,5},{8,9},{12,13},{9,10},{13,14},{20,22},{24,26},{28,30},{30,29}} | collective-permute-start | bytes 3145736 | tf_op jit(solution)/shard_map/ppermute | solution.py:284
  11.6 3.6 %collective-permute-done.2.b_ref = f32[128,512]{1,0:T(8,128)S(1)} collective-permute-done((f32[128,512]{1,0:T(8,128)S(1)}, f32[128,512]{1,0:T(8,128)S(1)}, u32[]{:S(2)}, u32[]{:S(2)}) %collective-permute-start.2) | collective-permute-done | bytes 262176 | tf_op jit(solution)/shard_map/ppermute | solution.py:276
  15.2 0.0 collective-permute-done.3.c_ref
  15.2 5.6 %collective-permute-done.4.d_ref = f32[128,512]{1,0:T(8,128)S(1)} collective-permute-done((f32[128,512]{1,0:T(8,128)S(1)}, f32[128,512]{1,0:T(8,128)S(1)}, u32[]{:S(2)}, u32[]{:S(2)}) %collective-permute-start.4) | collective-permute-done | bytes 262176 | tf_op jit(solution)/shard_map/ppermute | solution.py:276
  20.8 0.1 shard_map.98
  20.9 1.4 %collective-permute-start.5 = (f32[64,512]{1,0:T(8,128)S(1)}, f32[64,512]{1,0:T(8,128)S(1)}, u32[]{:S(2)}, u32[]{:S(2)}) collective-permute-start(f32[64,512]{1,0:T(8,128)S(1)} %get-tuple-element.32.refs_1_), channel_id=1, source_target_pairs={{0,2},{3,1},{4,6},{7,5},{8,10},{11,9},{12,14},{15,13},{16,18},{19,... | collective-permute-start | bytes 393224 | tf_op jit(solution)/shard_map/ppermute | solution.py:279
  22.3 3.2 %collective-permute-start.6 = (f32[64,512]{1,0:T(8,128)S(1)}, f32[64,512]{1,0:T(8,128)S(1)}, u32[]{:S(2)}, u32[]{:S(2)}) collective-permute-start(f32[64,512]{1,0:T(8,128)S(1)} %get-tuple-element.33), channel_id=1, source_target_pairs={{1,2},{2,1},{5,6},{6,5},{9,10},{10,9},{13,14},{14,13},{17,18},{18,... | collective-permute-start | bytes 393224 | tf_op jit(solution)/shard_map/ppermute | solution.py:279
  25.5 1.3 %collective-permute-start.7 = (f32[64,512]{1,0:T(8,128)S(1)}, f32[64,512]{1,0:T(8,128)S(1)}, u32[]{:S(2)}, u32[]{:S(2)}) collective-permute-start(f32[64,512]{1,0:T(8,128)S(1)} %get-tuple-element.33), channel_id=1, source_target_pairs={{0,1},{3,2},{4,5},{7,6},{8,9},{11,10},{12,13},{15,14},{16,17},{19,... | collective-permute-start | bytes 393224 | tf_op jit(solution)/shard_map/ppermute | solution.py:279
  26.8 0.3 shard_map.96
  27.2 0.6 collective-permute-done.5.refs_2_
  27.7 3.8 %collective-permute-done.6.refs_3_ = f32[64,512]{1,0:T(8,128)S(1)} collective-permute-done((f32[64,512]{1,0:T(8,128)S(1)}, f32[64,512]{1,0:T(8,128)S(1)}, u32[]{:S(2)}, u32[]{:S(2)}) %collective-permute-start.6) | collective-permute-done | bytes 131104 | tf_op jit(solution)/shard_map/ppermute | solution.py:279
  31.5 11.9 %collective-permute-done.7.refs_4_ = f32[64,512]{1,0:T(8,128)S(1)} collective-permute-done((f32[64,512]{1,0:T(8,128)S(1)}, f32[64,512]{1,0:T(8,128)S(1)}, u32[]{:S(2)}, u32[]{:S(2)}) %collective-permute-start.7) | collective-permute-done | bytes 131104 | tf_op jit(solution)/shard_map/ppermute | solution.py:279
  43.5 0.0 collective-permute-done.sent_ref
  43.5 2.9 %collective-permute-start.9 = (f32[512,512]{1,0:T(8,128)S(1)}, f32[512,512]{1,0:T(8,128)S(1)}, u32[]{:S(2)}, u32[]{:S(2)}) collective-permute-start(f32[512,512]{1,0:T(8,128)S(1)} %collective-permute-done.sent_ref), channel_id=1, source_target_pairs={{5,21},{21,5},{6,22},{22,6},{9,25},{25,9},{10,26},{26,10},{13,29},... | collective-permute-start | bytes 3145736 | tf_op jit(solution)/shard_map/ppermute | solution.py:320
  46.4 0.7 collective-permute-start.10
  47.1 0.7 collective-permute-start.8
  47.8 0.9 %collective-permute-done.9.other_ref = f32[512,512]{1,0:T(8,128)S(1)} collective-permute-done((f32[512,512]{1,0:T(8,128)S(1)}, f32[512,512]{1,0:T(8,128)S(1)}, u32[]{:S(2)}, u32[]{:S(2)}) %collective-permute-start.9) | collective-permute-done | bytes 1048608 | tf_op jit(solution)/shard_map/ppermute | solution.py:320
  48.7 1.0 %shard_map.100 = (bf16[512,512]{1,0:T(8,128)(2,1)S(1)}, bf16[512,512]{1,0:T(8,128)(2,1)S(1)}, bf16[512,512]{1,0:T(8,128)(2,1)S(1)}, bf16[512,512]{1,0:T(8,128)(2...) custom-call(f32[512,512]{1,0:T(8,128)S(1)} %copy-done, ...), custom_call_target="tpu_custom_call" | custom-call | bytes 3145728 | tf_op jit(solution)/shard_map/pallas_call | solution.py:242
  49.7 0.0 collective-permute-done.10.refs_4_
  49.8 1.3 %collective-permute-start.11 = (f32[64,512]{1,0:T(8,128)S(1)}, f32[64,512]{1,0:T(8,128)S(1)}, u32[]{:S(2)}, u32[]{:S(2)}) collective-permute-start(f32[64,512]{1,0:T(8,128)S(1)} %shard_map.102.refs_1_), channel_id=1, source_target_pairs={{5,9},{6,10},{1,13},{2,14},{21,25},{22,26},{17,29},{18,30}} | collective-permute-start | bytes 393224 | tf_op jit(solution)/shard_map/ppermute | solution.py:273
  51.1 0.0 collective-permute-done.8.refs_2_
  51.1 6.2 %collective-permute-done.11.refs_2_.refs_4_ = f32[64,512]{1,0:T(8,128)S(1)} collective-permute-done((f32[64,512]{1,0:T(8,128)S(1)}, f32[64,512]{1,0:T(8,128)S(1)}, u32[]{:S(2)}, u32[]{:S(2)}) %collective-permute-start.11) | collective-permute-done | bytes 131104 | tf_op jit(solution)/shard_map/ppermute | solution.py:273
  57.3 1.3 %collective-permute-start.12 = (f32[64,512]{1,0:T(8,128)S(1)}, f32[64,512]{1,0:T(8,128)S(1)}, u32[]{:S(2)}, u32[]{:S(2)}) collective-permute-start(f32[64,512]{1,0:T(8,128)S(1)} %shard_map.104.refs_1_), channel_id=1, source_target_pairs={{9,13},{10,14},{25,29},{26,30}} | collective-permute-start | bytes 393224 | tf_op jit(solution)/shard_map/ppermute | solution.py:273
  58.6 1.3 %collective-permute-start.13 = (f32[64,512]{1,0:T(8,128)S(1)}, f32[64,512]{1,0:T(8,128)S(1)}, u32[]{:S(2)}, u32[]{:S(2)}) collective-permute-start(f32[64,512]{1,0:T(8,128)S(1)} %shard_map.104.refs_1_), channel_id=1, source_target_pairs={{5,13},{6,14},{21,29},{22,30}} | collective-permute-start | bytes 393224 | tf_op jit(solution)/shard_map/ppermute | solution.py:273
  59.9 0.3 shard_map.103.refs_0_
  60.2 3.7 %collective-permute-done.12.refs_4_ = f32[64,512]{1,0:T(8,128)S(1)} collective-permute-done((f32[64,512]{1,0:T(8,128)S(1)}, f32[64,512]{1,0:T(8,128)S(1)}, u32[]{:S(2)}, u32[]{:S(2)}) %collective-permute-start.12) | collective-permute-done | bytes 131104 | tf_op jit(solution)/shard_map/ppermute | solution.py:273
  63.9 0.7 collective-permute-done.13.refs_7_
  64.6 0.7 shard_map.105.x_ref
  65.3 1.3 %collective-permute-start.14 = (f32[64,512]{1,0:T(8,128)S(1)}, f32[64,512]{1,0:T(8,128)S(1)}, u32[]{:S(2)}, u32[]{:S(2)}) collective-permute-start(f32[64,512]{1,0:T(8,128)S(1)} %shard_map.105.x_ref), channel_id=1, source_target_pairs={{1,3},{2,0},{5,7},{6,4},{9,11},{10,8},{13,15},{14,12},{17,19},{18,... | collective-permute-start | bytes 393224 | tf_op jit(solution)/shard_map/ppermute | solution.py:279
  66.6 1.3 %collective-permute-start.15 = (f32[64,512]{1,0:T(8,128)S(1)}, f32[64,512]{1,0:T(8,128)S(1)}, u32[]{:S(2)}, u32[]{:S(2)}) collective-permute-start(f32[64,512]{1,0:T(8,128)S(1)} %shard_map.105.x_ref), channel_id=1, source_target_pairs={{1,0},{2,3},{5,4},{6,7},{9,8},{10,11},{13,12},{14,15},{17,16},{18,... | collective-permute-start | bytes 393224 | tf_op jit(solution)/shard_map/ppermute | solution.py:279
  67.9 3.1 %collective-permute-start.16 = (f32[64,512]{1,0:T(8,128)S(1)}, f32[64,512]{1,0:T(8,128)S(1)}, u32[]{:S(2)}, u32[]{:S(2)}) collective-permute-start(f32[64,512]{1,0:T(8,128)S(1)} %shard_map.105.x_ref), channel_id=1, source_target_pairs={{1,2},{2,1},{5,6},{6,5},{9,10},{10,9},{13,14},{14,13},{17,18},{18,... | collective-permute-start | bytes 393224 | tf_op jit(solution)/shard_map/ppermute | solution.py:279
  71.1 0.0 collective-permute-done.14.c_ref
  71.1 1.4 %collective-permute-done.15.a_ref = f32[64,512]{1,0:T(8,128)S(1)} collective-permute-done((f32[64,512]{1,0:T(8,128)S(1)}, f32[64,512]{1,0:T(8,128)S(1)}, u32[]{:S(2)}, u32[]{:S(2)}) %collective-permute-start.15) | collective-permute-done | bytes 131104 | tf_op jit(solution)/shard_map/ppermute | solution.py:279
  72.5 1.3 %collective-permute-done.16.b_ref = f32[64,512]{1,0:T(8,128)S(1)} collective-permute-done((f32[64,512]{1,0:T(8,128)S(1)}, f32[64,512]{1,0:T(8,128)S(1)}, u32[]{:S(2)}, u32[]{:S(2)}) %collective-permute-start.16) | collective-permute-done | bytes 131104 | tf_op jit(solution)/shard_map/ppermute | solution.py:279
  73.9 0.1 shard_map.106.part_ref
  74.0 3.0 %collective-permute-start.17 = (f32[512,128]{1,0:T(8,128)S(1)}, f32[512,128]{1,0:T(8,128)S(1)}, u32[]{:S(2)}, u32[]{:S(2)}) collective-permute-start(f32[512,128]{1,0:T(8,128)S(1)} %shard_map.106.part_ref), channel_id=1, source_target_pairs={{0,16},{16,0},{1,17},{17,1},{2,18},{18,2},{3,19},{19,3},{4,20},{20... | collective-permute-start | bytes 786440 | tf_op jit(solution)/shard_map/ppermute | solution.py:269
  77.1 0.7 shard_map.107.refs_0_
  77.8 0.4 collective-permute-done.17.part_ref
  78.2 0.7 shard_map.108
  (10 shorter events, 0.1 us)
Async XLA Ops:
  0.6 9.7 %copy-start = (f32[512,512]{1,0:T(8,128)S(1)}, f32[512,512]{1,0:T(8,128)}, u32[]{:S(2)}) copy-start(f32[512,512]{1,0:T(8,128)} %own_ref.1) | copy-start | bytes 3145732
  4.3 1.9 %copy-start.3 = (s32[2,256]{1,0:T(2,128)S(1)}, s32[2,256]{1,0:T(2,128)}, u32[]{:S(2)}) copy-start(s32[2,256]{1,0:T(2,128)} %tgt_ref.3) | copy-start | bytes 6148
  4.4 1.9 %collective-permute-start.1 = (f32[136,512]{1,0:T(8,128)S(1)}, f32[136,512]{1,0:T(8,128)S(1)}, u32[]{:S(2)}, u32[]{:S(2)}) collective-permute-start(f32[136,512]{1,0:T(8,128)S(1)} %get-tuple-element.27), channel_id=1, source_target_pairs={{0,16},{16,0},{1,17},{17,1},{2,18},{18,2},{3,19},{19,3},{4,20},{20... | collective-permute-start | bytes 835592 | tf_op jit(solution)/shard_map/ppermute | solution.py:269
  7.6 7.6 %collective-permute-start.2 = (f32[128,512]{1,0:T(8,128)S(1)}, f32[128,512]{1,0:T(8,128)S(1)}, u32[]{:S(2)}, u32[]{:S(2)}) collective-permute-start(f32[128,512]{1,0:T(8,128)S(1)} %get-tuple-element.29), channel_id=1, source_target_pairs={{0,4},{4,0},{8,12},{12,8},{1,5},{5,1},{9,13},{13,9},{2,6},{6,2},{1... | collective-permute-start | bytes 786440 | tf_op jit(solution)/shard_map/ppermute | solution.py:276
  7.9 7.3 %collective-permute-start.3 = (f32[128,512]{1,0:T(8,128)S(1)}, f32[128,512]{1,0:T(8,128)S(1)}, u32[]{:S(2)}, u32[]{:S(2)}) collective-permute-start(f32[128,512]{1,0:T(8,128)S(1)} %get-tuple-element.30), channel_id=1, source_target_pairs={{0,8},{4,12},{8,0},{12,4},{1,9},{5,13},{9,1},{13,5},{2,10},{6,14},... | collective-permute-start | bytes 786440 | tf_op jit(solution)/shard_map/ppermute | solution.py:276
  8.1 12.7 %collective-permute-start.4 = (f32[128,512]{1,0:T(8,128)S(1)}, f32[128,512]{1,0:T(8,128)S(1)}, u32[]{:S(2)}, u32[]{:S(2)}) collective-permute-start(f32[128,512]{1,0:T(8,128)S(1)} %get-tuple-element.31), channel_id=1, source_target_pairs={{0,12},{4,8},{8,4},{12,0},{1,13},{5,9},{9,5},{13,1},{2,14},{6,10},... | collective-permute-start | bytes 786440 | tf_op jit(solution)/shard_map/ppermute | solution.py:276
  10.3 33.2 %collective-permute-start = (f32[512,512]{1,0:T(8,128)S(1)}, f32[512,512]{1,0:T(8,128)S(1)}, u32[]{:S(2)}, u32[]{:S(2)}) collective-permute-start(f32[512,512]{1,0:T(8,128)S(1)} %copy-done), channel_id=1, source_target_pairs={{4,5},{8,9},{12,13},{9,10},{13,14},{20,22},{24,26},{28,30},{30,29}} | collective-permute-start | bytes 3145736 | tf_op jit(solution)/shard_map/ppermute | solution.py:284
  20.8 6.0 %copy-start.1 = (f32[512,512]{1,0:T(8,128)S(1)}, f32[512,512]{1,0:T(8,128)}, u32[]{:S(2)}) copy-start(f32[512,512]{1,0:T(8,128)} %diag_ref.1) | copy-start | bytes 3145732
  20.8 6.0 %copy-start.2 = (f32[512,256]{1,0:T(8,128)S(1)}, f32[512,256]{1,0:T(8,128)}, u32[]{:S(2)}) copy-start(f32[512,256]{1,0:T(8,128)} %rhs_ref.1) | copy-start | bytes 1572868
  20.9 6.8 %collective-permute-start.5 = (f32[64,512]{1,0:T(8,128)S(1)}, f32[64,512]{1,0:T(8,128)S(1)}, u32[]{:S(2)}, u32[]{:S(2)}) collective-permute-start(f32[64,512]{1,0:T(8,128)S(1)} %get-tuple-element.32.refs_1_), channel_id=1, source_target_pairs={{0,2},{3,1},{4,6},{7,5},{8,10},{11,9},{12,14},{15,13},{16,18},{19,... | collective-permute-start | bytes 393224 | tf_op jit(solution)/shard_map/ppermute | solution.py:279
  22.3 9.2 %collective-permute-start.6 = (f32[64,512]{1,0:T(8,128)S(1)}, f32[64,512]{1,0:T(8,128)S(1)}, u32[]{:S(2)}, u32[]{:S(2)}) collective-permute-start(f32[64,512]{1,0:T(8,128)S(1)} %get-tuple-element.33), channel_id=1, source_target_pairs={{1,2},{2,1},{5,6},{6,5},{9,10},{10,9},{13,14},{14,13},{17,18},{18,... | collective-permute-start | bytes 393224 | tf_op jit(solution)/shard_map/ppermute | solution.py:279
  25.5 17.9 %collective-permute-start.7 = (f32[64,512]{1,0:T(8,128)S(1)}, f32[64,512]{1,0:T(8,128)S(1)}, u32[]{:S(2)}, u32[]{:S(2)}) collective-permute-start(f32[64,512]{1,0:T(8,128)S(1)} %get-tuple-element.33), channel_id=1, source_target_pairs={{0,1},{3,2},{4,5},{7,6},{8,9},{11,10},{12,13},{15,14},{16,17},{19,... | collective-permute-start | bytes 393224 | tf_op jit(solution)/shard_map/ppermute | solution.py:279
  43.5 5.2 %collective-permute-start.9 = (f32[512,512]{1,0:T(8,128)S(1)}, f32[512,512]{1,0:T(8,128)S(1)}, u32[]{:S(2)}, u32[]{:S(2)}) collective-permute-start(f32[512,512]{1,0:T(8,128)S(1)} %collective-permute-done.sent_ref), channel_id=1, source_target_pairs={{5,21},{21,5},{6,22},{22,6},{9,25},{25,9},{10,26},{26,10},{13,29},... | collective-permute-start | bytes 3145736 | tf_op jit(solution)/shard_map/ppermute | solution.py:320
  46.4 3.3 %collective-permute-start.10 = (f32[64,512]{1,0:T(8,128)S(1)}, f32[64,512]{1,0:T(8,128)S(1)}, u32[]{:S(2)}, u32[]{:S(2)}) collective-permute-start(f32[64,512]{1,0:T(8,128)S(1)} %get-tuple-element.38.refs_1_), channel_id=1, source_target_pairs={{1,5},{2,6},{17,21},{18,22}} | collective-permute-start | bytes 393224 | tf_op jit(solution)/shard_map/ppermute | solution.py:273
  47.1 4.0 %collective-permute-start.8 = (f32[64,512]{1,0:T(8,128)S(1)}, f32[64,512]{1,0:T(8,128)S(1)}, u32[]{:S(2)}, u32[]{:S(2)}) collective-permute-start(f32[64,512]{1,0:T(8,128)S(1)} %get-tuple-element.38.refs_1_), channel_id=1, source_target_pairs={{1,9},{2,10},{17,25},{18,26}} | collective-permute-start | bytes 393224 | tf_op jit(solution)/shard_map/ppermute | solution.py:273
  49.8 7.5 %collective-permute-start.11 = (f32[64,512]{1,0:T(8,128)S(1)}, f32[64,512]{1,0:T(8,128)S(1)}, u32[]{:S(2)}, u32[]{:S(2)}) collective-permute-start(f32[64,512]{1,0:T(8,128)S(1)} %shard_map.102.refs_1_), channel_id=1, source_target_pairs={{5,9},{6,10},{1,13},{2,14},{21,25},{22,26},{17,29},{18,30}} | collective-permute-start | bytes 393224 | tf_op jit(solution)/shard_map/ppermute | solution.py:273
  57.3 6.6 %collective-permute-start.12 = (f32[64,512]{1,0:T(8,128)S(1)}, f32[64,512]{1,0:T(8,128)S(1)}, u32[]{:S(2)}, u32[]{:S(2)}) collective-permute-start(f32[64,512]{1,0:T(8,128)S(1)} %shard_map.104.refs_1_), channel_id=1, source_target_pairs={{9,13},{10,14},{25,29},{26,30}} | collective-permute-start | bytes 393224 | tf_op jit(solution)/shard_map/ppermute | solution.py:273
  58.6 6.0 %collective-permute-start.13 = (f32[64,512]{1,0:T(8,128)S(1)}, f32[64,512]{1,0:T(8,128)S(1)}, u32[]{:S(2)}, u32[]{:S(2)}) collective-permute-start(f32[64,512]{1,0:T(8,128)S(1)} %shard_map.104.refs_1_), channel_id=1, source_target_pairs={{5,13},{6,14},{21,29},{22,30}} | collective-permute-start | bytes 393224 | tf_op jit(solution)/shard_map/ppermute | solution.py:273
  65.3 5.8 %collective-permute-start.14 = (f32[64,512]{1,0:T(8,128)S(1)}, f32[64,512]{1,0:T(8,128)S(1)}, u32[]{:S(2)}, u32[]{:S(2)}) collective-permute-start(f32[64,512]{1,0:T(8,128)S(1)} %shard_map.105.x_ref), channel_id=1, source_target_pairs={{1,3},{2,0},{5,7},{6,4},{9,11},{10,8},{13,15},{14,12},{17,19},{18,... | collective-permute-start | bytes 393224 | tf_op jit(solution)/shard_map/ppermute | solution.py:279
  66.6 5.9 %collective-permute-start.15 = (f32[64,512]{1,0:T(8,128)S(1)}, f32[64,512]{1,0:T(8,128)S(1)}, u32[]{:S(2)}, u32[]{:S(2)}) collective-permute-start(f32[64,512]{1,0:T(8,128)S(1)} %shard_map.105.x_ref), channel_id=1, source_target_pairs={{1,0},{2,3},{5,4},{6,7},{9,8},{10,11},{13,12},{14,15},{17,16},{18,... | collective-permute-start | bytes 393224 | tf_op jit(solution)/shard_map/ppermute | solution.py:279
  67.9 5.9 %collective-permute-start.16 = (f32[64,512]{1,0:T(8,128)S(1)}, f32[64,512]{1,0:T(8,128)S(1)}, u32[]{:S(2)}, u32[]{:S(2)}) collective-permute-start(f32[64,512]{1,0:T(8,128)S(1)} %shard_map.105.x_ref), channel_id=1, source_target_pairs={{1,2},{2,1},{5,6},{6,5},{9,10},{10,9},{13,14},{14,13},{17,18},{18,... | collective-permute-start | bytes 393224 | tf_op jit(solution)/shard_map/ppermute | solution.py:279
  74.0 4.2 %collective-permute-start.17 = (f32[512,128]{1,0:T(8,128)S(1)}, f32[512,128]{1,0:T(8,128)S(1)}, u32[]{:S(2)}, u32[]{:S(2)}) collective-permute-start(f32[512,128]{1,0:T(8,128)S(1)} %shard_map.106.part_ref), channel_id=1, source_target_pairs={{0,16},{16,0},{1,17},{17,1},{2,18},{18,2},{3,19},{19,3},{4,20},{20... | collective-permute-start | bytes 786440 | tf_op jit(solution)/shard_map/ppermute | solution.py:269

commit v8 on v7

--- a/solution.py
+++ b/solution.py
@@ -142,24 +142,31 @@
         copy.wait()
 
 
-def scatter_kernel(keep_ref, recv_ref, tgt_ref, *out_refs):
+def scatter(value, target, size, start):
+    index = lax.broadcasted_iota(jnp.int32, (size, value.shape[1]), 0) + start
+    hot = jnp.where(index == target, 1.0, 0.0).astype(BF16)
+    product = lax.dot_general(value, hot, NT, preferred_element_type=F32)
+    half = value.shape[0] // 2
+    return product[:half] + product[half:]
+
+
+def own_kernel(keep_ref, tgt_ref, *out_refs):
     _, row, _ = place()
-    half, slots_all = keep_ref.shape
     size = out_refs[0].shape[1]
-    children, slots = tgt_ref.shape
-    mine = [split(keep_ref[...]), split(recv_ref[0:half, :])]
-    stacked = [jnp.concatenate(pair, axis=0) for pair in mine]
-    mine_targets = jnp.concatenate([tgt_ref[s:s + 1, :] for s in range(children)], axis=1)
-    target = [mine_targets, recv_ref[half:half + 1, :].astype(jnp.int32)]
+    value = jnp.concatenate(split(keep_ref[...]), axis=0)
+    target = jnp.concatenate([tgt_ref[s:s + 1, :] for s in range(tgt_ref.shape[0])], axis=1)
     for s, out_ref in enumerate(out_refs):
-        block = jnp.bitwise_xor(row, s)
-        index = lax.broadcasted_iota(jnp.int32, (size, slots_all), 0) + block * size
-        total = None
-        for t, value in zip(target, stacked):
-            hot = jnp.where(index == t, 1.0, 0.0).astype(BF16)
-            product = lax.dot_general(value, hot, NT, preferred_element_type=F32)
-            total = product if total is None else total + product
-        out_ref[...] = total[:half] + total[half:]
+        out_ref[...] = scatter(value, target, size, jnp.bitwise_xor(row, s) * size)
+
+
+def other_kernel(recv_ref, *refs):
+    _, row, _ = place()
+    own_refs, out_refs = refs[:4], refs[4:]
+    half, size = out_refs[0].shape
+    value = jnp.concatenate(split(recv_ref[0:half, :]), axis=0)
+    target = recv_ref[half:half + 1, :].astype(jnp.int32)
+    for s, (own_ref, out_ref) in enumerate(zip(own_refs, out_refs)):
+        out_ref[...] = own_ref[...] + scatter(value, target, size, jnp.bitwise_xor(row, s) * size)
 
 
 def pieces_kernel(a_ref, b_ref, c_ref, d_ref, first_ref, second_ref, sum_ref):
@@ -231,7 +238,7 @@
     copy.wait()
 
 
-def call(kernel, ins, outs, scratch=(), outside=(), outs_outside=(), pinned=(), aliases=None, limit=24, flops=0):
+def call(kernel, ins, outs, scratch=(), outside=(), outs_outside=(), pinned=(), aliases=None, limit=24):
     def spec(i, a):
         return ANY if i in outside else SM if a.ndim == 1 else VM
 
@@ -246,7 +253,7 @@
         out_specs=[ANY if i in outs_outside else VM for i in range(len(outs))],
         scratch_shapes=[pltpu.VMEM(s, F32) if isinstance(s, tuple) else s for s in scratch],
         input_output_aliases=aliases or {},
-        cost_estimate=pl.CostEstimate(flops=flops, bytes_accessed=4 * sum(a.size for a in ins), transcendentals=0),
+        cost_estimate=pl.CostEstimate(flops=0, bytes_accessed=4 * sum(a.size for a in ins), transcendentals=0),
         compiler_params=pltpu.CompilerParams(vmem_limit_bytes=limit * 1024 * 1024),
     )(*ins)
     return list(outs)
@@ -295,17 +302,18 @@
         pinned=(1, 2),
         limit=56,
     )
-    sums = call(scatter_kernel, [keep, swap(send), targets], [(half, size)] * rows)
+    sums = call(own_kernel, [keep, targets], [(half, size)] * rows)
+    sums = call(other_kernel, [swap(send)] + sums, [(half, size)] * rows)
     got = [along_row(sums[s], [(i, i ^ s) for i in range(rows)]) for s in (1, 2, 3)]
     rhs_piece, diag_high, diag_low = call(
         turn_kernel, [top_rhs, top_diag], [shape, block, block], [(half, size)]
     )
     diag = [diag_high, diag_low]
-    first, second = call(pieces_kernel, [sums[0]] + got, [shape] * 2, [(half, size)], flops=10 ** 11)
+    first, second = call(pieces_kernel, [sums[0]] + got, [shape] * 2, [(half, size)])
     q = [
         along_col(second, [(0, 2), (3, 1)]),
+        along_col(first, [(0, 1), (3, 2)]),
         along_col(first, [(1, 2), (2, 1)]),
-        along_col(first, [(0, 1), (3, 2)]),
     ]
 
     def chain(owner, ins, has_sums=False, solves=True):

time: 79.3 us -> 71.4 us (0.900)
  waiting for transfers between devices: 41.3 us -> 32.2 us
  starting transfers between devices: 27.6 us -> 28.6 us
    ppermute x6, waiting for transfers between devices: 19 us -> 9.03 us  [along_col(): return lax.ppermute(value, 'col', pairs)]
    ppermute x2, starting transfers between devices: 3.78 us -> 6.66 us  [swap(): return lax.ppermute(value, 'leaf', [(0, 1), (1, 0)])]
    ppermute x6, starting transfers between devices: 11.7 us -> 9.15 us  [along_col(): return lax.ppermute(value, 'col', pairs)]
    ppermute x3, waiting for transfers between devices: 9.19 us -> 10.4 us  [along_row(): return lax.ppermute(value, 'row', pairs)]
    pallas_call x14 -> x15, Pallas kernels: 9.11 us -> 9.24 us  [call(): pl.pallas_call(kernel, out_shape=[shape(i, out) for i, out in enumerate(o...]
  transfers between devices with their start and end apart: 18 -> 18, of which waited for: 13 -> 12; matrix products, arithmetic and copies ran while one was open for 0% -> 0% of each run, Pallas kernels for 3% -> 11%
where the time goes in v8:
time: 71.4 us; the launch traced here: 71 us
  waiting for transfers between devices  32.2 us (45%)
  starting transfers between devices  28.6 us (40%)
  Pallas kernels  9.24 us (13%)
  between operations  0.91 us (1%)
    ppermute x5, waiting for transfers between devices, hop(): return lax.ppermute(value, ('row', 'col'), pairs)  11 us
    ppermute x3, waiting for transfers between devices, along_row(): return lax.ppermute(value, 'row', pairs)  10.4 us
    pallas_call x15, Pallas kernels, call(): pl.pallas_call(kernel, out_shape=[shape(i, out) for i, out in enumerate(o...  9.24 us
    ppermute x6, starting transfers between devices, along_col(): return lax.ppermute(value, 'col', pairs)  9.15 us
    ppermute x6, waiting for transfers between devices, along_col(): return lax.ppermute(value, 'col', pairs)  9.03 us
    ppermute x2, starting transfers between devices, swap(): return lax.ppermute(value, 'leaf', [(0, 1), (1, 0)])  6.66 us
    ppermute x5, starting transfers between devices, hop(): return lax.ppermute(value, ('row', 'col'), pairs)  5.21 us
    ppermute x1, starting transfers between devices, central(): lax.ppermute(sent, ('leaf', 'row', 'col'), [(a + b, a + shift - b) for a...  3.57 us
  transfers between devices with their start and end apart: 18, of which 12 were waited for; matrix products, arithmetic and copies ran while one was open for 0% of the time, Pallas kernels for 11%

profile of v8, /device:TPU:15, one launch (start us, length us, event | category | flops | bytes accessed | tf_op | source)
XLA Modules:
  0.0 71.0 jit_solution(6745194895579724561)
XLA Ops:
  0.6 1.3 %collective-permute-start = (f32[512,512]{1,0:T(8,128)}, f32[512,512]{1,0:T(8,128)S(1)}, u32[]{:S(2)}, u32[]{:S(2)}) collective-permute-start(f32[512,512]{1,0:T(8,128)} %own_ref.1), channel_id=1, source_target_pairs={{4,5},{8,9},{12,13},{9,10},{13,14},{20,22},{24,26},{28,30},{30,29}} | collective-permute-start | bytes 3145736 | tf_op jit(solution)/shard_map/ppermute | solution.py:291
  1.9 3.6 %shard_map.95 = (f32[2,256,256]{2,1,0:T(8,128)}, f32[128,512]{1,0:T(8,128)S(1)}, f32[136,512]{1,0:T(8,128)S(1)}) custom-call(s32[2]{0:T(128)} %live_ref.1, f32[2,256,256]{2,1,0:T(8,128)} %rhs_hbm.1, f32[2,256,256]{2,1,0:T(8,128)} %diag_hbm.1, f32[2,256,256]{2,1,0:T(8,128)} %off_hbm.1, s32[2,256]{1,0:T(2,128)} %tgt_ref.3), custom_call_target="tpu_custom_call" | custom-call | bytes 1574920 | tf_op jit(solution)/shard_map/pallas_call | solution.py:249
  5.5 0.0 copy-start.3
  5.5 2.9 %collective-permute-start.1 = (f32[136,512]{1,0:T(8,128)S(1)}, f32[136,512]{1,0:T(8,128)S(1)}, u32[]{:S(2)}, u32[]{:S(2)}) collective-permute-start(f32[136,512]{1,0:T(8,128)S(1)} %get-tuple-element.30), channel_id=1, source_target_pairs={{0,16},{16,0},{1,17},{17,1},{2,18},{18,2},{3,19},{19,3},{4,20},{20... | collective-permute-start | bytes 835592 | tf_op jit(solution)/shard_map/ppermute | solution.py:276
  8.5 0.8 %shard_map.97 = (f32[128,512]{1,0:T(8,128)S(1)}, f32[128,512]{1,0:T(8,128)S(1)}, f32[128,512]{1,0:T(8,128)S(1)}, f32[128,512]{1,0:T(8,128)S(1)}) custom-call(f32[128,512]{1,0:T(8,128)S(1)} %get-tuple-element.31.keep_ref, s32[2,256]{1,0:T(2,128)S(1)} %copy-done.3), custom_call_target="tpu_custom_call" | custom-call | bytes 264192 | tf_op jit(solution)/shard_map/pallas_call | solution.py:249
  9.2 0.4 collective-permute-done.1.recv_ref
  9.7 0.8 %shard_map.98 = (f32[128,512]{1,0:T(8,128)S(1)}, f32[128,512]{1,0:T(8,128)S(1)}, f32[128,512]{1,0:T(8,128)S(1)}, f32[128,512]{1,0:T(8,128)S(1)}) custom-call(f32[136,512]{1,0:T(8,128)S(1)} %collective-permute-done.1.recv_ref, f32[128,512]{1,0:T(8,128)S(1)} %get-tuple-element.32.refs_0_, f32[128,512]{1,0:T(8,128)S(1)} %get-tuple-element.33.refs_1_, ...), custom_call_target="tpu_custom_call" | custom-call | bytes 1327104 | tf_op jit(solution)/shard_map/pallas_call | solution.py:249
  10.4 0.3 collective-permute-start.2
  10.8 0.0 collective-permute-start.3
  10.8 2.4 %collective-permute-start.4 = (f32[128,512]{1,0:T(8,128)S(1)}, f32[128,512]{1,0:T(8,128)S(1)}, u32[]{:S(2)}, u32[]{:S(2)}) collective-permute-start(f32[128,512]{1,0:T(8,128)S(1)} %get-tuple-element.39), channel_id=1, source_target_pairs={{0,12},{4,8},{8,4},{12,0},{1,13},{5,9},{9,5},{13,1},{2,14},{6,10},... | collective-permute-start | bytes 786440 | tf_op jit(solution)/shard_map/ppermute | solution.py:283
  13.2 4.9 %collective-permute-done.2.b_ref = f32[128,512]{1,0:T(8,128)S(1)} collective-permute-done((f32[128,512]{1,0:T(8,128)S(1)}, f32[128,512]{1,0:T(8,128)S(1)}, u32[]{:S(2)}, u32[]{:S(2)}) %collective-permute-start.2) | collective-permute-done | bytes 262176 | tf_op jit(solution)/shard_map/ppermute | solution.py:283
  18.0 5.5 %collective-permute-done.3.c_ref = f32[128,512]{1,0:T(8,128)S(1)} collective-permute-done((f32[128,512]{1,0:T(8,128)S(1)}, f32[128,512]{1,0:T(8,128)S(1)}, u32[]{:S(2)}, u32[]{:S(2)}) %collective-permute-start.3) | collective-permute-done | bytes 262176 | tf_op jit(solution)/shard_map/ppermute | solution.py:283
  23.6 0.0 collective-permute-done.4.d_ref
  23.6 0.1 shard_map.99
  23.7 1.4 %collective-permute-start.5 = (f32[64,512]{1,0:T(8,128)S(1)}, f32[64,512]{1,0:T(8,128)S(1)}, u32[]{:S(2)}, u32[]{:S(2)}) collective-permute-start(f32[64,512]{1,0:T(8,128)S(1)} %get-tuple-element.40.refs_1_), channel_id=1, source_target_pairs={{0,2},{3,1},{4,6},{7,5},{8,10},{11,9},{12,14},{15,13},{16,18},{19,... | collective-permute-start | bytes 393224 | tf_op jit(solution)/shard_map/ppermute | solution.py:286
  25.1 1.3 %collective-permute-start.6 = (f32[64,512]{1,0:T(8,128)S(1)}, f32[64,512]{1,0:T(8,128)S(1)}, u32[]{:S(2)}, u32[]{:S(2)}) collective-permute-start(f32[64,512]{1,0:T(8,128)S(1)} %get-tuple-element.41), channel_id=1, source_target_pairs={{0,1},{3,2},{4,5},{7,6},{8,9},{11,10},{12,13},{15,14},{16,17},{19,... | collective-permute-start | bytes 393224 | tf_op jit(solution)/shard_map/ppermute | solution.py:286
  26.4 1.9 %collective-permute-start.7 = (f32[64,512]{1,0:T(8,128)S(1)}, f32[64,512]{1,0:T(8,128)S(1)}, u32[]{:S(2)}, u32[]{:S(2)}) collective-permute-start(f32[64,512]{1,0:T(8,128)S(1)} %get-tuple-element.41), channel_id=1, source_target_pairs={{1,2},{2,1},{5,6},{6,5},{9,10},{10,9},{13,14},{14,13},{17,18},{18,... | collective-permute-start | bytes 393224 | tf_op jit(solution)/shard_map/ppermute | solution.py:286
  28.3 0.3 shard_map.96
  28.7 0.0 copy-start
  28.7 1.7 %collective-permute-done.5.refs_2_ = f32[64,512]{1,0:T(8,128)S(1)} collective-permute-done((f32[64,512]{1,0:T(8,128)S(1)}, f32[64,512]{1,0:T(8,128)S(1)}, u32[]{:S(2)}, u32[]{:S(2)}) %collective-permute-start.5) | collective-permute-done | bytes 131104 | tf_op jit(solution)/shard_map/ppermute | solution.py:286
  30.4 3.5 %collective-permute-done.6.refs_3_ = f32[64,512]{1,0:T(8,128)S(1)} collective-permute-done((f32[64,512]{1,0:T(8,128)S(1)}, f32[64,512]{1,0:T(8,128)S(1)}, u32[]{:S(2)}, u32[]{:S(2)}) %collective-permute-start.6) | collective-permute-done | bytes 131104 | tf_op jit(solution)/shard_map/ppermute | solution.py:286
  33.9 0.0 collective-permute-done.7.refs_4_
  34.0 0.0 collective-permute-done.sent_ref
  34.0 3.6 %collective-permute-start.9 = (f32[512,512]{1,0:T(8,128)S(1)}, f32[512,512]{1,0:T(8,128)S(1)}, u32[]{:S(2)}, u32[]{:S(2)}) collective-permute-start(f32[512,512]{1,0:T(8,128)S(1)} %collective-permute-done.sent_ref), channel_id=1, source_target_pairs={{5,21},{21,5},{6,22},{22,6},{9,25},{25,9},{10,26},{26,10},{13,29},... | collective-permute-start | bytes 3145736 | tf_op jit(solution)/shard_map/ppermute | solution.py:328
  37.6 0.7 collective-permute-start.10
  38.2 0.7 collective-permute-start.8
  38.9 0.9 %collective-permute-done.9.other_ref = f32[512,512]{1,0:T(8,128)S(1)} collective-permute-done((f32[512,512]{1,0:T(8,128)S(1)}, f32[512,512]{1,0:T(8,128)S(1)}, u32[]{:S(2)}, u32[]{:S(2)}) %collective-permute-start.9) | collective-permute-done | bytes 1048608 | tf_op jit(solution)/shard_map/ppermute | solution.py:328
  39.8 1.0 %shard_map.101 = (bf16[512,512]{1,0:T(8,128)(2,1)S(1)}, bf16[512,512]{1,0:T(8,128)(2,1)S(1)}, bf16[512,512]{1,0:T(8,128)(2,1)S(1)}, bf16[512,512]{1,0:T(8,128)(2...) custom-call(f32[512,512]{1,0:T(8,128)S(1)} %copy-done, ...), custom_call_target="tpu_custom_call" | custom-call | bytes 3145728 | tf_op jit(solution)/shard_map/pallas_call | solution.py:249
  40.9 0.0 collective-permute-done.10.refs_4_
  40.9 1.3 %collective-permute-start.11 = (f32[64,512]{1,0:T(8,128)S(1)}, f32[64,512]{1,0:T(8,128)S(1)}, u32[]{:S(2)}, u32[]{:S(2)}) collective-permute-start(f32[64,512]{1,0:T(8,128)S(1)} %shard_map.103.refs_1_), channel_id=1, source_target_pairs={{5,9},{6,10},{1,13},{2,14},{21,25},{22,26},{17,29},{18,30}} | collective-permute-start | bytes 393224 | tf_op jit(solution)/shard_map/ppermute | solution.py:280
  42.3 6.9 %collective-permute-done.11.refs_2_.refs_4_ = f32[64,512]{1,0:T(8,128)S(1)} collective-permute-done((f32[64,512]{1,0:T(8,128)S(1)}, f32[64,512]{1,0:T(8,128)S(1)}, u32[]{:S(2)}, u32[]{:S(2)}) %collective-permute-start.11) | collective-permute-done | bytes 131104 | tf_op jit(solution)/shard_map/ppermute | solution.py:280
  49.2 1.3 %collective-permute-start.12 = (f32[64,512]{1,0:T(8,128)S(1)}, f32[64,512]{1,0:T(8,128)S(1)}, u32[]{:S(2)}, u32[]{:S(2)}) collective-permute-start(f32[64,512]{1,0:T(8,128)S(1)} %shard_map.105.refs_1_), channel_id=1, source_target_pairs={{9,13},{10,14},{25,29},{26,30}} | collective-permute-start | bytes 393224 | tf_op jit(solution)/shard_map/ppermute | solution.py:280
  50.5 1.3 %collective-permute-start.13 = (f32[64,512]{1,0:T(8,128)S(1)}, f32[64,512]{1,0:T(8,128)S(1)}, u32[]{:S(2)}, u32[]{:S(2)}) collective-permute-start(f32[64,512]{1,0:T(8,128)S(1)} %shard_map.105.refs_1_), channel_id=1, source_target_pairs={{5,13},{6,14},{21,29},{22,30}} | collective-permute-start | bytes 393224 | tf_op jit(solution)/shard_map/ppermute | solution.py:280
  51.8 0.3 shard_map.104.refs_0_
  52.1 4.0 %collective-permute-done.12.refs_4_ = f32[64,512]{1,0:T(8,128)S(1)} collective-permute-done((f32[64,512]{1,0:T(8,128)S(1)}, f32[64,512]{1,0:T(8,128)S(1)}, u32[]{:S(2)}, u32[]{:S(2)}) %collective-permute-start.12) | collective-permute-done | bytes 131104 | tf_op jit(solution)/shard_map/ppermute | solution.py:280
  56.1 0.1 collective-permute-done.13.refs_7_
  56.2 0.7 %shard_map.106.x_ref = f32[64,512]{1,0:T(8,128)S(1)} custom-call(f32[64,512]{1,0:T(8,128)S(1)} %shard_map.104.refs_0_, f32[64,512]{1,0:T(8,128)S(1)} %shard_map.105.refs_1_, bf16[512,512]{1,0:T(8,128)(2,1)S(1)} %get-tuple-element.42.refs_5_.refs_2_, bf16[512,512]{1,0:T(8,128)(2,1)S(1)} %get-tuple-element.43.refs_6_.refs_3_, ...), custom_call_target="tpu_custom_call" | custom-call | bytes 6815744 | tf_op jit(solution)/shard_map/pallas_call | solution.py:249
  57.0 1.3 %collective-permute-start.14 = (f32[64,512]{1,0:T(8,128)S(1)}, f32[64,512]{1,0:T(8,128)S(1)}, u32[]{:S(2)}, u32[]{:S(2)}) collective-permute-start(f32[64,512]{1,0:T(8,128)S(1)} %shard_map.106.x_ref), channel_id=1, source_target_pairs={{1,3},{2,0},{5,7},{6,4},{9,11},{10,8},{13,15},{14,12},{17,19},{18,... | collective-permute-start | bytes 393224 | tf_op jit(solution)/shard_map/ppermute | solution.py:286
  58.3 1.3 %collective-permute-start.15 = (f32[64,512]{1,0:T(8,128)S(1)}, f32[64,512]{1,0:T(8,128)S(1)}, u32[]{:S(2)}, u32[]{:S(2)}) collective-permute-start(f32[64,512]{1,0:T(8,128)S(1)} %shard_map.106.x_ref), channel_id=1, source_target_pairs={{1,0},{2,3},{5,4},{6,7},{9,8},{10,11},{13,12},{14,15},{17,16},{18,... | collective-permute-start | bytes 393224 | tf_op jit(solution)/shard_map/ppermute | solution.py:286
  59.6 1.9 %collective-permute-start.16 = (f32[64,512]{1,0:T(8,128)S(1)}, f32[64,512]{1,0:T(8,128)S(1)}, u32[]{:S(2)}, u32[]{:S(2)}) collective-permute-start(f32[64,512]{1,0:T(8,128)S(1)} %shard_map.106.x_ref), channel_id=1, source_target_pairs={{1,2},{2,1},{5,6},{6,5},{9,10},{10,9},{13,14},{14,13},{17,18},{18,... | collective-permute-start | bytes 393224 | tf_op jit(solution)/shard_map/ppermute | solution.py:286
  61.5 0.0 collective-permute-done.14.c_ref
  61.5 1.4 %collective-permute-done.15.a_ref = f32[64,512]{1,0:T(8,128)S(1)} collective-permute-done((f32[64,512]{1,0:T(8,128)S(1)}, f32[64,512]{1,0:T(8,128)S(1)}, u32[]{:S(2)}, u32[]{:S(2)}) %collective-permute-start.15) | collective-permute-done | bytes 131104 | tf_op jit(solution)/shard_map/ppermute | solution.py:286
  62.9 2.4 %collective-permute-done.16.b_ref = f32[64,512]{1,0:T(8,128)S(1)} collective-permute-done((f32[64,512]{1,0:T(8,128)S(1)}, f32[64,512]{1,0:T(8,128)S(1)}, u32[]{:S(2)}, u32[]{:S(2)}) %collective-permute-start.16) | collective-permute-done | bytes 131104 | tf_op jit(solution)/shard_map/ppermute | solution.py:286
  65.3 0.1 shard_map.107.part_ref
  65.4 3.7 %collective-permute-start.17 = (f32[512,128]{1,0:T(8,128)S(1)}, f32[512,128]{1,0:T(8,128)S(1)}, u32[]{:S(2)}, u32[]{:S(2)}) collective-permute-start(f32[512,128]{1,0:T(8,128)S(1)} %shard_map.107.part_ref), channel_id=1, source_target_pairs={{0,16},{16,0},{1,17},{17,1},{2,18},{18,2},{3,19},{19,3},{4,20},{20... | collective-permute-start | bytes 786440 | tf_op jit(solution)/shard_map/ppermute | solution.py:276
  69.2 0.7 shard_map.108.refs_0_
  69.9 0.4 collective-permute-done.17.part_ref
  70.3 0.7 shard_map.109
  (11 shorter events, 0.1 us)
Async XLA Ops:
  0.6 33.3 %collective-permute-start = (f32[512,512]{1,0:T(8,128)}, f32[512,512]{1,0:T(8,128)S(1)}, u32[]{:S(2)}, u32[]{:S(2)}) collective-permute-start(f32[512,512]{1,0:T(8,128)} %own_ref.1), channel_id=1, source_target_pairs={{4,5},{8,9},{12,13},{9,10},{13,14},{20,22},{24,26},{28,30},{30,29}} | collective-permute-start | bytes 3145736 | tf_op jit(solution)/shard_map/ppermute | solution.py:291
  5.5 2.9 %copy-start.3 = (s32[2,256]{1,0:T(2,128)S(1)}, s32[2,256]{1,0:T(2,128)}, u32[]{:S(2)}) copy-start(s32[2,256]{1,0:T(2,128)} %tgt_ref.3) | copy-start | bytes 6148
  5.5 4.1 %collective-permute-start.1 = (f32[136,512]{1,0:T(8,128)S(1)}, f32[136,512]{1,0:T(8,128)S(1)}, u32[]{:S(2)}, u32[]{:S(2)}) collective-permute-start(f32[136,512]{1,0:T(8,128)S(1)} %get-tuple-element.30), channel_id=1, source_target_pairs={{0,16},{16,0},{1,17},{17,1},{2,18},{18,2},{3,19},{19,3},{4,20},{20... | collective-permute-start | bytes 835592 | tf_op jit(solution)/shard_map/ppermute | solution.py:276
  9.7 18.7 %copy-start.1 = (f32[512,512]{1,0:T(8,128)S(1)}, f32[512,512]{1,0:T(8,128)}, u32[]{:S(2)}) copy-start(f32[512,512]{1,0:T(8,128)} %diag_ref.1) | copy-start | bytes 3145732
  10.4 7.6 %collective-permute-start.2 = (f32[128,512]{1,0:T(8,128)S(1)}, f32[128,512]{1,0:T(8,128)S(1)}, u32[]{:S(2)}, u32[]{:S(2)}) collective-permute-start(f32[128,512]{1,0:T(8,128)S(1)} %get-tuple-element.37), channel_id=1, source_target_pairs={{0,4},{4,0},{8,12},{12,8},{1,5},{5,1},{9,13},{13,9},{2,6},{6,2},{1... | collective-permute-start | bytes 786440 | tf_op jit(solution)/shard_map/ppermute | solution.py:283
  10.8 12.8 %collective-permute-start.3 = (f32[128,512]{1,0:T(8,128)S(1)}, f32[128,512]{1,0:T(8,128)S(1)}, u32[]{:S(2)}, u32[]{:S(2)}) collective-permute-start(f32[128,512]{1,0:T(8,128)S(1)} %get-tuple-element.38), channel_id=1, source_target_pairs={{0,8},{4,12},{8,0},{12,4},{1,9},{5,13},{9,1},{13,5},{2,10},{6,14},... | collective-permute-start | bytes 786440 | tf_op jit(solution)/shard_map/ppermute | solution.py:283
  10.8 12.8 %collective-permute-start.4 = (f32[128,512]{1,0:T(8,128)S(1)}, f32[128,512]{1,0:T(8,128)S(1)}, u32[]{:S(2)}, u32[]{:S(2)}) collective-permute-start(f32[128,512]{1,0:T(8,128)S(1)} %get-tuple-element.39), channel_id=1, source_target_pairs={{0,12},{4,8},{8,4},{12,0},{1,13},{5,9},{9,5},{13,1},{2,14},{6,10},... | collective-permute-start | bytes 786440 | tf_op jit(solution)/shard_map/ppermute | solution.py:283
  23.6 4.8 %copy-start.2 = (f32[512,256]{1,0:T(8,128)S(1)}, f32[512,256]{1,0:T(8,128)}, u32[]{:S(2)}) copy-start(f32[512,256]{1,0:T(8,128)} %rhs_ref.1) | copy-start | bytes 1572868
  23.7 6.7 %collective-permute-start.5 = (f32[64,512]{1,0:T(8,128)S(1)}, f32[64,512]{1,0:T(8,128)S(1)}, u32[]{:S(2)}, u32[]{:S(2)}) collective-permute-start(f32[64,512]{1,0:T(8,128)S(1)} %get-tuple-element.40.refs_1_), channel_id=1, source_target_pairs={{0,2},{3,1},{4,6},{7,5},{8,10},{11,9},{12,14},{15,13},{16,18},{19,... | collective-permute-start | bytes 393224 | tf_op jit(solution)/shard_map/ppermute | solution.py:286
  25.1 8.8 %collective-permute-start.6 = (f32[64,512]{1,0:T(8,128)S(1)}, f32[64,512]{1,0:T(8,128)S(1)}, u32[]{:S(2)}, u32[]{:S(2)}) collective-permute-start(f32[64,512]{1,0:T(8,128)S(1)} %get-tuple-element.41), channel_id=1, source_target_pairs={{0,1},{3,2},{4,5},{7,6},{8,9},{11,10},{12,13},{15,14},{16,17},{19,... | collective-permute-start | bytes 393224 | tf_op jit(solution)/shard_map/ppermute | solution.py:286
  26.4 7.5 %collective-permute-start.7 = (f32[64,512]{1,0:T(8,128)S(1)}, f32[64,512]{1,0:T(8,128)S(1)}, u32[]{:S(2)}, u32[]{:S(2)}) collective-permute-start(f32[64,512]{1,0:T(8,128)S(1)} %get-tuple-element.41), channel_id=1, source_target_pairs={{1,2},{2,1},{5,6},{6,5},{9,10},{10,9},{13,14},{14,13},{17,18},{18,... | collective-permute-start | bytes 393224 | tf_op jit(solution)/shard_map/ppermute | solution.py:286
  28.7 11.2 %copy-start = (f32[512,512]{1,0:T(8,128)S(1)}, f32[512,512]{1,0:T(8,128)}, u32[]{:S(2)}) copy-start(f32[512,512]{1,0:T(8,128)} %own_ref.1) | copy-start | bytes 3145732
  34.0 5.8 %collective-permute-start.9 = (f32[512,512]{1,0:T(8,128)S(1)}, f32[512,512]{1,0:T(8,128)S(1)}, u32[]{:S(2)}, u32[]{:S(2)}) collective-permute-start(f32[512,512]{1,0:T(8,128)S(1)} %collective-permute-done.sent_ref), channel_id=1, source_target_pairs={{5,21},{21,5},{6,22},{22,6},{9,25},{25,9},{10,26},{26,10},{13,29},... | collective-permute-start | bytes 3145736 | tf_op jit(solution)/shard_map/ppermute | solution.py:328
  37.6 3.3 %collective-permute-start.10 = (f32[64,512]{1,0:T(8,128)S(1)}, f32[64,512]{1,0:T(8,128)S(1)}, u32[]{:S(2)}, u32[]{:S(2)}) collective-permute-start(f32[64,512]{1,0:T(8,128)S(1)} %get-tuple-element.46.refs_1_), channel_id=1, source_target_pairs={{1,5},{2,6},{17,21},{18,22}} | collective-permute-start | bytes 393224 | tf_op jit(solution)/shard_map/ppermute | solution.py:280
  38.2 4.0 %collective-permute-start.8 = (f32[64,512]{1,0:T(8,128)S(1)}, f32[64,512]{1,0:T(8,128)S(1)}, u32[]{:S(2)}, u32[]{:S(2)}) collective-permute-start(f32[64,512]{1,0:T(8,128)S(1)} %get-tuple-element.46.refs_1_), channel_id=1, source_target_pairs={{1,9},{2,10},{17,25},{18,26}} | collective-permute-start | bytes 393224 | tf_op jit(solution)/shard_map/ppermute | solution.py:280
  40.9 8.3 %collective-permute-start.11 = (f32[64,512]{1,0:T(8,128)S(1)}, f32[64,512]{1,0:T(8,128)S(1)}, u32[]{:S(2)}, u32[]{:S(2)}) collective-permute-start(f32[64,512]{1,0:T(8,128)S(1)} %shard_map.103.refs_1_), channel_id=1, source_target_pairs={{5,9},{6,10},{1,13},{2,14},{21,25},{22,26},{17,29},{18,30}} | collective-permute-start | bytes 393224 | tf_op jit(solution)/shard_map/ppermute | solution.py:280
  49.2 6.9 %collective-permute-start.12 = (f32[64,512]{1,0:T(8,128)S(1)}, f32[64,512]{1,0:T(8,128)S(1)}, u32[]{:S(2)}, u32[]{:S(2)}) collective-permute-start(f32[64,512]{1,0:T(8,128)S(1)} %shard_map.105.refs_1_), channel_id=1, source_target_pairs={{9,13},{10,14},{25,29},{26,30}} | collective-permute-start | bytes 393224 | tf_op jit(solution)/shard_map/ppermute | solution.py:280
  50.5 5.7 %collective-permute-start.13 = (f32[64,512]{1,0:T(8,128)S(1)}, f32[64,512]{1,0:T(8,128)S(1)}, u32[]{:S(2)}, u32[]{:S(2)}) collective-permute-start(f32[64,512]{1,0:T(8,128)S(1)} %shard_map.105.refs_1_), channel_id=1, source_target_pairs={{5,13},{6,14},{21,29},{22,30}} | collective-permute-start | bytes 393224 | tf_op jit(solution)/shard_map/ppermute | solution.py:280
  57.0 4.5 %collective-permute-start.14 = (f32[64,512]{1,0:T(8,128)S(1)}, f32[64,512]{1,0:T(8,128)S(1)}, u32[]{:S(2)}, u32[]{:S(2)}) collective-permute-start(f32[64,512]{1,0:T(8,128)S(1)} %shard_map.106.x_ref), channel_id=1, source_target_pairs={{1,3},{2,0},{5,7},{6,4},{9,11},{10,8},{13,15},{14,12},{17,19},{18,... | collective-permute-start | bytes 393224 | tf_op jit(solution)/shard_map/ppermute | solution.py:286
  58.3 4.6 %collective-permute-start.15 = (f32[64,512]{1,0:T(8,128)S(1)}, f32[64,512]{1,0:T(8,128)S(1)}, u32[]{:S(2)}, u32[]{:S(2)}) collective-permute-start(f32[64,512]{1,0:T(8,128)S(1)} %shard_map.106.x_ref), channel_id=1, source_target_pairs={{1,0},{2,3},{5,4},{6,7},{9,8},{10,11},{13,12},{14,15},{17,16},{18,... | collective-permute-start | bytes 393224 | tf_op jit(solution)/shard_map/ppermute | solution.py:286
  59.6 5.7 %collective-permute-start.16 = (f32[64,512]{1,0:T(8,128)S(1)}, f32[64,512]{1,0:T(8,128)S(1)}, u32[]{:S(2)}, u32[]{:S(2)}) collective-permute-start(f32[64,512]{1,0:T(8,128)S(1)} %shard_map.106.x_ref), channel_id=1, source_target_pairs={{1,2},{2,1},{5,6},{6,5},{9,10},{10,9},{13,14},{14,13},{17,18},{18,... | collective-permute-start | bytes 393224 | tf_op jit(solution)/shard_map/ppermute | solution.py:286
  65.4 4.9 %collective-permute-start.17 = (f32[512,128]{1,0:T(8,128)S(1)}, f32[512,128]{1,0:T(8,128)S(1)}, u32[]{:S(2)}, u32[]{:S(2)}) collective-permute-start(f32[512,128]{1,0:T(8,128)S(1)} %shard_map.107.part_ref), channel_id=1, source_target_pairs={{0,16},{16,0},{1,17},{17,1},{2,18},{18,2},{3,19},{19,3},{4,20},{20... | collective-permute-start | bytes 786440 | tf_op jit(solution)/shard_map/ppermute | solution.py:276

commit v9 on v8

--- a/solution.py
+++ b/solution.py
@@ -275,22 +275,26 @@
     def swap(value):
         return lax.ppermute(value, "leaf", [(0, 1), (1, 0)])
 
-    def hop(value, pairs):
-        pairs = [(at(a, z), at(b, z)) for a, b in pairs for z in (1, 2)]
-        return lax.ppermute(value, ("row", "col"), pairs)
-
-    def along_row(value, pairs):
-        return lax.ppermute(value, "row", pairs)
+    def along_row(value, step):
+        return lax.ppermute(value, "row", [(r, r ^ step) for r in range(rows)])
 
     def along_col(value, pairs):
-        return lax.ppermute(value, "col", pairs)
+        rest = [a for a in range(cols) if a not in [p[0] for p in pairs]]
+        open_ends = [b for b in range(cols) if b not in [p[1] for p in pairs]]
+        return lax.ppermute(value, "col", pairs + list(zip(rest, open_ends)))
 
     near = [(at(k, 0), at(k, 1)) for k in (1, 2, 3)] + [(at(k, 1), at(k, 2)) for k in (2, 3)]
     far = [(at(k, 0), at(k, 2)) for k in (1, 2, 3)] + [(at(3, 2), at(3, 1))]
     shift = rows * cols
-    sent = lax.ppermute(
-        top_factor, ("leaf", "row", "col"), near + [(a + shift, b + shift) for a, b in far]
-    )
+    pairs = near + [(a + shift, b + shift) for a, b in far]
+    for k in range(2 * rows):
+        here = range(k * cols, (k + 1) * cols)
+        rest = [a for a in here if a not in [p[0] for p in pairs]]
+        open_ends = [b for b in here if b not in [p[1] for p in pairs]]
+        stay = [a for a in rest if a in open_ends]
+        pairs = pairs + [(a, a) for a in stay]
+        pairs = pairs + list(zip([a for a in rest if a not in stay], [b for b in open_ends if b not in stay]))
+    sent = lax.ppermute(top_factor, ("leaf", "row", "col"), pairs)
     child_sol, keep, send = call(
         child_kernel,
         [live, child_rhs, child_diag, child_off, targets],
@@ -304,7 +308,7 @@
     )
     sums = call(own_kernel, [keep, targets], [(half, size)] * rows)
     sums = call(other_kernel, [swap(send)] + sums, [(half, size)] * rows)
-    got = [along_row(sums[s], [(i, i ^ s) for i in range(rows)]) for s in (1, 2, 3)]
+    got = [along_row(sums[s], s) for s in (1, 2, 3)]
     rhs_piece, diag_high, diag_low = call(
         turn_kernel, [top_rhs, top_diag], [shape, block, block], [(half, size)]
     )
@@ -312,8 +316,8 @@
     first, second = call(pieces_kernel, [sums[0]] + got, [shape] * 2, [(half, size)])
     q = [
         along_col(second, [(0, 2), (3, 1)]),
+        along_col(first, [(1, 2), (2, 1)]),
         along_col(first, [(0, 1), (3, 2)]),
-        along_col(first, [(1, 2), (2, 1)]),
     ]
 
     def chain(owner, ins, has_sums=False, solves=True):
@@ -324,20 +328,16 @@
 
     res, x = chain(0, [rhs_piece, second] + q + diag, has_sums=True)
     sent, res = lax.optimization_barrier((sent, res))
-    middle = [at(k, z) for k in (1, 2, 3) for z in (1, 2)]
-    other = lax.ppermute(
-        sent, ("leaf", "row", "col"), [(a + b, a + shift - b) for a in middle for b in (0, shift)]
-    )
-    factor = call(factor_kernel, [top_factor, sent, other], [block] * 6)
+    factor = call(factor_kernel, [top_factor, sent, swap(sent)], [block] * 6)
     factor = [factor[0:2], factor[2:4], factor[4:6]]
-    to1 = hop(x, [(0, 1)])
-    to2 = hop(x, [(0, 2)])
+    to1 = along_row(x, 1)
+    to2 = along_row(x, 2)
     x = chain(1, [res, x] + diag + [to1] + factor[0])
-    on = hop(x, [(1, 2), (0, 3)])
+    on = along_row(x, 3)
     res = chain(2, [res, res, to2] + factor[0], solves=False)
     x = chain(2, [res, x] + diag + [on] + factor[1])
-    to3 = hop(x, [(2, 3)])
-    late = hop(x, [(1, 3)])
+    to3 = along_row(x, 1)
+    late = along_row(x, 2)
     res = chain(3, [res, res, on] + factor[0], solves=False)
     x = chain(3, [res, x] + diag + [to3] + factor[2] + [late] + factor[1])
 

time: 71.4 us -> 65.4 us (0.916)
  starting transfers between devices: 28.6 us -> 20.4 us
  waiting for transfers between devices: 32.2 us -> 34.5 us
    ppermute x16 -> x15, starting transfers between devices: 21.9 us -> 14.1 us  [the longest x6 7.66 us: along_col(): return lax.ppermute(value, 'col', pairs + list(zip(rest, open_ends)))]
    ppermute x2 -> x3, waiting for transfers between devices: 0.86 us -> 2.67 us  [swap(): return lax.ppermute(value, 'leaf', [(0, 1), (1, 0)])]
    ppermute x16 -> x15, waiting for transfers between devices: 31.4 us -> 31.8 us  [the longest x8 20.5 us: along_row(): return lax.ppermute(value, 'row', [(r, r ^ step) for r in range(rows)])]
    ppermute x2 -> x3, starting transfers between devices: 6.66 us -> 6.32 us  [swap(): return lax.ppermute(value, 'leaf', [(0, 1), (1, 0)])]
  transfers between devices with their start and end apart: 18 -> 18, of which waited for: 12 -> 14; matrix products, arithmetic and copies ran while one was open for 0% -> 0% of each run, Pallas kernels for 11% -> 12%
where the time goes in v9:
time: 65.4 us; the launch traced here: 64.9 us
  waiting for transfers between devices  34.5 us (53%)
  starting transfers between devices  20.4 us (31%)
  Pallas kernels  9.22 us (14%)
  between operations  0.84 us (1%)
    ppermute x8, waiting for transfers between devices, along_row(): return lax.ppermute(value, 'row', [(r, r ^ step) for r in range(rows)])  20.5 us
    ppermute x6, waiting for transfers between devices, along_col(): return lax.ppermute(value, 'col', pairs + list(zip(rest, open_ends)))  11.3 us
    pallas_call x15, Pallas kernels, call(): pl.pallas_call(kernel, out_shape=[shape(i, out) for i, out in enumerate(o...  9.22 us
    ppermute x6, starting transfers between devices, along_col(): return lax.ppermute(value, 'col', pairs + list(zip(rest, open_ends)))  7.66 us
    ppermute x3, starting transfers between devices, swap(): return lax.ppermute(value, 'leaf', [(0, 1), (1, 0)])  6.32 us
    ppermute x8, starting transfers between devices, along_row(): return lax.ppermute(value, 'row', [(r, r ^ step) for r in range(rows)])  4.34 us
    ppermute x3, waiting for transfers between devices, swap(): return lax.ppermute(value, 'leaf', [(0, 1), (1, 0)])  2.67 us
    ppermute x1, starting transfers between devices, central(): sent = lax.ppermute(top_factor, ('leaf', 'row', 'col'), pairs)  2.08 us
  transfers between devices with their start and end apart: 18, of which 14 were waited for; matrix products, arithmetic and copies ran while one was open for 0% of the time, Pallas kernels for 12%

profile of v9, /device:TPU:15, one launch (start us, length us, event | category | flops | bytes accessed | tf_op | source)
XLA Modules:
  0.0 64.9 jit_solution(17621363077323843230)
XLA Ops:
  0.6 2.1 %collective-permute-start = (f32[512,512]{1,0:T(8,128)}, f32[512,512]{1,0:T(8,128)S(1)}, u32[]{:S(2)}, u32[]{:S(2)}) collective-permute-start(f32[512,512]{1,0:T(8,128)} %own_ref.1), channel_id=1, source_target_pairs={{4,5},{8,9},{12,13},{9,10},{13,14},{20,22},{24,26},{28,30},{30,29}... | collective-permute-start | bytes 3145736 | tf_op jit(solution)/shard_map/ppermute | solution.py:297
  2.7 3.6 %shard_map.95 = (f32[2,256,256]{2,1,0:T(8,128)}, f32[128,512]{1,0:T(8,128)S(1)}, f32[136,512]{1,0:T(8,128)S(1)}) custom-call(s32[2]{0:T(128)} %live_ref.1, f32[2,256,256]{2,1,0:T(8,128)} %rhs_hbm.1, f32[2,256,256]{2,1,0:T(8,128)} %diag_hbm.1, f32[2,256,256]{2,1,0:T(8,128)} %off_hbm.1, s32[2,256]{1,0:T(2,128)} %tgt_ref.3), custom_call_target="tpu_custom_call" | custom-call | bytes 1574920 | tf_op jit(solution)/shard_map/pallas_call | solution.py:249
  6.3 0.0 copy-start.3
  6.3 2.1 %collective-permute-start.1 = (f32[136,512]{1,0:T(8,128)S(1)}, f32[136,512]{1,0:T(8,128)S(1)}, u32[]{:S(2)}, u32[]{:S(2)}) collective-permute-start(f32[136,512]{1,0:T(8,128)S(1)} %get-tuple-element.30), channel_id=1, source_target_pairs={{0,16},{16,0},{1,17},{17,1},{2,18},{18,2},{3,19},{19,3},{4,20},{20... | collective-permute-start | bytes 835592 | tf_op jit(solution)/shard_map/ppermute | solution.py:276
  8.5 0.8 %shard_map.97 = (f32[128,512]{1,0:T(8,128)S(1)}, f32[128,512]{1,0:T(8,128)S(1)}, f32[128,512]{1,0:T(8,128)S(1)}, f32[128,512]{1,0:T(8,128)S(1)}) custom-call(f32[128,512]{1,0:T(8,128)S(1)} %get-tuple-element.31.keep_ref, s32[2,256]{1,0:T(2,128)S(1)} %copy-done.3), custom_call_target="tpu_custom_call" | custom-call | bytes 264192 | tf_op jit(solution)/shard_map/pallas_call | solution.py:249
  9.2 0.4 collective-permute-done.1.recv_ref
  9.7 0.8 %shard_map.98 = (f32[128,512]{1,0:T(8,128)S(1)}, f32[128,512]{1,0:T(8,128)S(1)}, f32[128,512]{1,0:T(8,128)S(1)}, f32[128,512]{1,0:T(8,128)S(1)}) custom-call(f32[136,512]{1,0:T(8,128)S(1)} %collective-permute-done.1.recv_ref, f32[128,512]{1,0:T(8,128)S(1)} %get-tuple-element.32.refs_0_, f32[128,512]{1,0:T(8,128)S(1)} %get-tuple-element.33.refs_1_, ...), custom_call_target="tpu_custom_call" | custom-call | bytes 1327104 | tf_op jit(solution)/shard_map/pallas_call | solution.py:249
  10.4 0.3 collective-permute-start.2
  10.8 0.0 collective-permute-start.3
  10.8 2.4 %collective-permute-start.4 = (f32[128,512]{1,0:T(8,128)S(1)}, f32[128,512]{1,0:T(8,128)S(1)}, u32[]{:S(2)}, u32[]{:S(2)}) collective-permute-start(f32[128,512]{1,0:T(8,128)S(1)} %get-tuple-element.39), channel_id=1, source_target_pairs={{0,12},{4,8},{8,4},{12,0},{1,13},{5,9},{9,5},{13,1},{2,14},{6,10},... | collective-permute-start | bytes 786440 | tf_op jit(solution)/shard_map/ppermute | solution.py:279
  13.2 4.9 %collective-permute-done.2.b_ref = f32[128,512]{1,0:T(8,128)S(1)} collective-permute-done((f32[128,512]{1,0:T(8,128)S(1)}, f32[128,512]{1,0:T(8,128)S(1)}, u32[]{:S(2)}, u32[]{:S(2)}) %collective-permute-start.2) | collective-permute-done | bytes 262176 | tf_op jit(solution)/shard_map/ppermute | solution.py:279
  18.0 5.5 %collective-permute-done.3.c_ref = f32[128,512]{1,0:T(8,128)S(1)} collective-permute-done((f32[128,512]{1,0:T(8,128)S(1)}, f32[128,512]{1,0:T(8,128)S(1)}, u32[]{:S(2)}, u32[]{:S(2)}) %collective-permute-start.3) | collective-permute-done | bytes 262176 | tf_op jit(solution)/shard_map/ppermute | solution.py:279
  23.6 0.0 collective-permute-done.4.d_ref
  23.6 0.1 shard_map.99
  23.7 1.0 %collective-permute-start.5 = (f32[64,512]{1,0:T(8,128)S(1)}, f32[64,512]{1,0:T(8,128)S(1)}, u32[]{:S(2)}, u32[]{:S(2)}) collective-permute-start(f32[64,512]{1,0:T(8,128)S(1)} %get-tuple-element.40.refs_1_), channel_id=1, source_target_pairs={{0,2},{3,1},{1,0},{2,3},{4,6},{7,5},{5,4},{6,7},{8,10},{11,9},{9,8... | collective-permute-start | bytes 393224 | tf_op jit(solution)/shard_map/ppermute | solution.py:284
  24.6 2.0 %collective-permute-start.6 = (f32[64,512]{1,0:T(8,128)S(1)}, f32[64,512]{1,0:T(8,128)S(1)}, u32[]{:S(2)}, u32[]{:S(2)}) collective-permute-start(f32[64,512]{1,0:T(8,128)S(1)} %get-tuple-element.41), channel_id=1, source_target_pairs={{1,2},{2,1},{0,0},{3,3},{5,6},{6,5},{4,4},{7,7},{9,10},{10,9},{8,8... | collective-permute-start | bytes 393224 | tf_op jit(solution)/shard_map/ppermute | solution.py:284
  26.7 0.1 collective-permute-start.7
  26.8 0.3 shard_map.96
  27.1 0.0 copy-start
  27.1 1.4 %collective-permute-done.5.refs_2_ = f32[64,512]{1,0:T(8,128)S(1)} collective-permute-done((f32[64,512]{1,0:T(8,128)S(1)}, f32[64,512]{1,0:T(8,128)S(1)}, u32[]{:S(2)}, u32[]{:S(2)}) %collective-permute-start.5) | collective-permute-done | bytes 131104 | tf_op jit(solution)/shard_map/ppermute | solution.py:284
  28.5 4.6 %collective-permute-done.6.refs_3_ = f32[64,512]{1,0:T(8,128)S(1)} collective-permute-done((f32[64,512]{1,0:T(8,128)S(1)}, f32[64,512]{1,0:T(8,128)S(1)}, u32[]{:S(2)}, u32[]{:S(2)}) %collective-permute-start.6) | collective-permute-done | bytes 131104 | tf_op jit(solution)/shard_map/ppermute | solution.py:284
  33.1 1.2 %collective-permute-done.7.refs_4_ = f32[64,512]{1,0:T(8,128)S(1)} collective-permute-done((f32[64,512]{1,0:T(8,128)S(1)}, f32[64,512]{1,0:T(8,128)S(1)}, u32[]{:S(2)}, u32[]{:S(2)}) %collective-permute-start.7) | collective-permute-done | bytes 131104 | tf_op jit(solution)/shard_map/ppermute | solution.py:284
  34.4 0.0 collective-permute-done.sent_ref
  34.4 0.7 %collective-permute-start.9 = (f32[512,512]{1,0:T(8,128)S(1)}, f32[512,512]{1,0:T(8,128)S(1)}, u32[]{:S(2)}, u32[]{:S(2)}) collective-permute-start(f32[512,512]{1,0:T(8,128)S(1)} %collective-permute-done.sent_ref), channel_id=1, source_target_pairs={{0,16},{16,0},{1,17},{17,1},{2,18},{18,2},{3,19},{19,3},{4,20},{20... | collective-permute-start | bytes 3145736 | tf_op jit(solution)/shard_map/ppermute | solution.py:276
  35.1 0.3 collective-permute-start.10
  35.4 0.2 collective-permute-start.8
  35.6 1.8 %collective-permute-done.9.other_ref = f32[512,512]{1,0:T(8,128)S(1)} collective-permute-done((f32[512,512]{1,0:T(8,128)S(1)}, f32[512,512]{1,0:T(8,128)S(1)}, u32[]{:S(2)}, u32[]{:S(2)}) %collective-permute-start.9) | collective-permute-done | bytes 1048608 | tf_op jit(solution)/shard_map/ppermute | solution.py:276
  37.4 1.0 %shard_map.101 = (bf16[512,512]{1,0:T(8,128)(2,1)S(1)}, bf16[512,512]{1,0:T(8,128)(2,1)S(1)}, bf16[512,512]{1,0:T(8,128)(2,1)S(1)}, bf16[512,512]{1,0:T(8,128)(2...) custom-call(f32[512,512]{1,0:T(8,128)S(1)} %copy-done, ...), custom_call_target="tpu_custom_call" | custom-call | bytes 3145728 | tf_op jit(solution)/shard_map/pallas_call | solution.py:249
  38.4 1.7 %collective-permute-done.10.refs_4_ = f32[64,512]{1,0:T(8,128)S(1)} collective-permute-done((f32[64,512]{1,0:T(8,128)S(1)}, f32[64,512]{1,0:T(8,128)S(1)}, u32[]{:S(2)}, u32[]{:S(2)}) %collective-permute-start.10) | collective-permute-done | bytes 131104 | tf_op jit(solution)/shard_map/ppermute | solution.py:279
  40.2 0.2 collective-permute-start.11
  40.4 0.0 collective-permute-done.8.refs_2_
  40.5 4.9 %collective-permute-done.11.refs_2_.refs_4_ = f32[64,512]{1,0:T(8,128)S(1)} collective-permute-done((f32[64,512]{1,0:T(8,128)S(1)}, f32[64,512]{1,0:T(8,128)S(1)}, u32[]{:S(2)}, u32[]{:S(2)}) %collective-permute-start.11) | collective-permute-done | bytes 131104 | tf_op jit(solution)/shard_map/ppermute | solution.py:279
  45.3 0.9 %collective-permute-start.12 = (f32[64,512]{1,0:T(8,128)S(1)}, f32[64,512]{1,0:T(8,128)S(1)}, u32[]{:S(2)}, u32[]{:S(2)}) collective-permute-start(f32[64,512]{1,0:T(8,128)S(1)} %shard_map.105.refs_1_), channel_id=1, source_target_pairs={{0,4},{4,0},{8,12},{12,8},{1,5},{5,1},{9,13},{13,9},{2,6},{6,2},{1... | collective-permute-start | bytes 393224 | tf_op jit(solution)/shard_map/ppermute | solution.py:279
  46.2 0.1 collective-permute-start.13
  46.3 0.3 shard_map.104.refs_0_
  46.6 2.7 %collective-permute-done.12.refs_4_ = f32[64,512]{1,0:T(8,128)S(1)} collective-permute-done((f32[64,512]{1,0:T(8,128)S(1)}, f32[64,512]{1,0:T(8,128)S(1)}, u32[]{:S(2)}, u32[]{:S(2)}) %collective-permute-start.12) | collective-permute-done | bytes 131104 | tf_op jit(solution)/shard_map/ppermute | solution.py:279
  49.2 0.8 %collective-permute-done.13.refs_7_ = f32[64,512]{1,0:T(8,128)S(1)} collective-permute-done((f32[64,512]{1,0:T(8,128)S(1)}, f32[64,512]{1,0:T(8,128)S(1)}, u32[]{:S(2)}, u32[]{:S(2)}) %collective-permute-start.13) | collective-permute-done | bytes 131104 | tf_op jit(solution)/shard_map/ppermute | solution.py:279
  50.0 0.7 %shard_map.106.x_ref = f32[64,512]{1,0:T(8,128)S(1)} custom-call(f32[64,512]{1,0:T(8,128)S(1)} %shard_map.104.refs_0_, f32[64,512]{1,0:T(8,128)S(1)} %shard_map.105.refs_1_, bf16[512,512]{1,0:T(8,128)(2,1)S(1)} %get-tuple-element.42.refs_5_.refs_2_, bf16[512,512]{1,0:T(8,128)(2,1)S(1)} %get-tuple-element.43.refs_6_.refs_3_, ...), custom_call_target="tpu_custom_call" | custom-call | bytes 6815744 | tf_op jit(solution)/shard_map/pallas_call | solution.py:249
  50.8 0.1 collective-permute-start.14
  50.8 1.5 %collective-permute-start.15 = (f32[64,512]{1,0:T(8,128)S(1)}, f32[64,512]{1,0:T(8,128)S(1)}, u32[]{:S(2)}, u32[]{:S(2)}) collective-permute-start(f32[64,512]{1,0:T(8,128)S(1)} %shard_map.106.x_ref), channel_id=1, source_target_pairs={{1,0},{2,3},{0,1},{3,2},{5,4},{6,7},{4,5},{7,6},{9,8},{10,11},{8,9... | collective-permute-start | bytes 393224 | tf_op jit(solution)/shard_map/ppermute | solution.py:284
  52.3 3.1 %collective-permute-start.16 = (f32[64,512]{1,0:T(8,128)S(1)}, f32[64,512]{1,0:T(8,128)S(1)}, u32[]{:S(2)}, u32[]{:S(2)}) collective-permute-start(f32[64,512]{1,0:T(8,128)S(1)} %shard_map.106.x_ref), channel_id=1, source_target_pairs={{1,2},{2,1},{0,0},{3,3},{5,6},{6,5},{4,4},{7,7},{9,10},{10,9},{8,8... | collective-permute-start | bytes 393224 | tf_op jit(solution)/shard_map/ppermute | solution.py:284
  55.4 0.6 collective-permute-done.15.a_ref
  56.0 3.4 %collective-permute-done.16.b_ref = f32[64,512]{1,0:T(8,128)S(1)} collective-permute-done((f32[64,512]{1,0:T(8,128)S(1)}, f32[64,512]{1,0:T(8,128)S(1)}, u32[]{:S(2)}, u32[]{:S(2)}) %collective-permute-start.16) | collective-permute-done | bytes 131104 | tf_op jit(solution)/shard_map/ppermute | solution.py:284
  59.4 0.1 shard_map.107.part_ref
  59.6 3.5 %collective-permute-start.17 = (f32[512,128]{1,0:T(8,128)S(1)}, f32[512,128]{1,0:T(8,128)S(1)}, u32[]{:S(2)}, u32[]{:S(2)}) collective-permute-start(f32[512,128]{1,0:T(8,128)S(1)} %shard_map.107.part_ref), channel_id=1, source_target_pairs={{0,16},{16,0},{1,17},{17,1},{2,18},{18,2},{3,19},{19,3},{4,20},{20... | collective-permute-start | bytes 786440 | tf_op jit(solution)/shard_map/ppermute | solution.py:276
  63.1 0.7 %shard_map.108.refs_0_ = f32[512,256]{1,0:T(8,128)} custom-call(f32[512,128]{1,0:T(8,128)S(1)} %shard_map.107.part_ref), custom_call_target="tpu_custom_call" | custom-call | bytes 262144 | tf_op jit(solution)/shard_map/pallas_call | solution.py:249
  63.8 0.4 collective-permute-done.17.part_ref
  64.2 0.7 %shard_map.109 = f32[512,256]{1,0:T(8,128)} custom-call(f32[512,128]{1,0:T(8,128)S(1)} %collective-permute-done.17.part_ref, f32[512,256]{1,0:T(8,128)} %shard_map.108.refs_0_), custom_call_target="tpu_custom_call", output_to_operand_aliasing={{}: (1, {})} | custom-call | bytes 786432 | tf_op jit(solution)/shard_map/pallas_call | solution.py:249
  (11 shorter events, 0.1 us)
Async XLA Ops:
  0.6 33.8 %collective-permute-start = (f32[512,512]{1,0:T(8,128)}, f32[512,512]{1,0:T(8,128)S(1)}, u32[]{:S(2)}, u32[]{:S(2)}) collective-permute-start(f32[512,512]{1,0:T(8,128)} %own_ref.1), channel_id=1, source_target_pairs={{4,5},{8,9},{12,13},{9,10},{13,14},{20,22},{24,26},{28,30},{30,29}... | collective-permute-start | bytes 3145736 | tf_op jit(solution)/shard_map/ppermute | solution.py:297
  6.3 2.2 %copy-start.3 = (s32[2,256]{1,0:T(2,128)S(1)}, s32[2,256]{1,0:T(2,128)}, u32[]{:S(2)}) copy-start(s32[2,256]{1,0:T(2,128)} %tgt_ref.3) | copy-start | bytes 6148
  6.3 3.3 %collective-permute-start.1 = (f32[136,512]{1,0:T(8,128)S(1)}, f32[136,512]{1,0:T(8,128)S(1)}, u32[]{:S(2)}, u32[]{:S(2)}) collective-permute-start(f32[136,512]{1,0:T(8,128)S(1)} %get-tuple-element.30), channel_id=1, source_target_pairs={{0,16},{16,0},{1,17},{17,1},{2,18},{18,2},{3,19},{19,3},{4,20},{20... | collective-permute-start | bytes 835592 | tf_op jit(solution)/shard_map/ppermute | solution.py:276
  9.7 17.1 %copy-start.1 = (f32[512,512]{1,0:T(8,128)S(1)}, f32[512,512]{1,0:T(8,128)}, u32[]{:S(2)}) copy-start(f32[512,512]{1,0:T(8,128)} %diag_ref.1) | copy-start | bytes 3145732
  10.4 7.6 %collective-permute-start.2 = (f32[128,512]{1,0:T(8,128)S(1)}, f32[128,512]{1,0:T(8,128)S(1)}, u32[]{:S(2)}, u32[]{:S(2)}) collective-permute-start(f32[128,512]{1,0:T(8,128)S(1)} %get-tuple-element.37), channel_id=1, source_target_pairs={{0,4},{4,0},{8,12},{12,8},{1,5},{5,1},{9,13},{13,9},{2,6},{6,2},{1... | collective-permute-start | bytes 786440 | tf_op jit(solution)/shard_map/ppermute | solution.py:279
  10.8 12.8 %collective-permute-start.3 = (f32[128,512]{1,0:T(8,128)S(1)}, f32[128,512]{1,0:T(8,128)S(1)}, u32[]{:S(2)}, u32[]{:S(2)}) collective-permute-start(f32[128,512]{1,0:T(8,128)S(1)} %get-tuple-element.38), channel_id=1, source_target_pairs={{0,8},{4,12},{8,0},{12,4},{1,9},{5,13},{9,1},{13,5},{2,10},{6,14},... | collective-permute-start | bytes 786440 | tf_op jit(solution)/shard_map/ppermute | solution.py:279
  10.8 12.8 %collective-permute-start.4 = (f32[128,512]{1,0:T(8,128)S(1)}, f32[128,512]{1,0:T(8,128)S(1)}, u32[]{:S(2)}, u32[]{:S(2)}) collective-permute-start(f32[128,512]{1,0:T(8,128)S(1)} %get-tuple-element.39), channel_id=1, source_target_pairs={{0,12},{4,8},{8,4},{12,0},{1,13},{5,9},{9,5},{13,1},{2,14},{6,10},... | collective-permute-start | bytes 786440 | tf_op jit(solution)/shard_map/ppermute | solution.py:279
  23.6 3.2 %copy-start.2 = (f32[512,256]{1,0:T(8,128)S(1)}, f32[512,256]{1,0:T(8,128)}, u32[]{:S(2)}) copy-start(f32[512,256]{1,0:T(8,128)} %rhs_ref.1) | copy-start | bytes 1572868
  23.7 4.9 %collective-permute-start.5 = (f32[64,512]{1,0:T(8,128)S(1)}, f32[64,512]{1,0:T(8,128)S(1)}, u32[]{:S(2)}, u32[]{:S(2)}) collective-permute-start(f32[64,512]{1,0:T(8,128)S(1)} %get-tuple-element.40.refs_1_), channel_id=1, source_target_pairs={{0,2},{3,1},{1,0},{2,3},{4,6},{7,5},{5,4},{6,7},{8,10},{11,9},{9,8... | collective-permute-start | bytes 393224 | tf_op jit(solution)/shard_map/ppermute | solution.py:284
  24.6 8.5 %collective-permute-start.6 = (f32[64,512]{1,0:T(8,128)S(1)}, f32[64,512]{1,0:T(8,128)S(1)}, u32[]{:S(2)}, u32[]{:S(2)}) collective-permute-start(f32[64,512]{1,0:T(8,128)S(1)} %get-tuple-element.41), channel_id=1, source_target_pairs={{1,2},{2,1},{0,0},{3,3},{5,6},{6,5},{4,4},{7,7},{9,10},{10,9},{8,8... | collective-permute-start | bytes 393224 | tf_op jit(solution)/shard_map/ppermute | solution.py:284
  26.7 7.7 %collective-permute-start.7 = (f32[64,512]{1,0:T(8,128)S(1)}, f32[64,512]{1,0:T(8,128)S(1)}, u32[]{:S(2)}, u32[]{:S(2)}) collective-permute-start(f32[64,512]{1,0:T(8,128)S(1)} %get-tuple-element.41), channel_id=1, source_target_pairs={{0,1},{3,2},{1,0},{2,3},{4,5},{7,6},{5,4},{6,7},{8,9},{11,10},{9,8... | collective-permute-start | bytes 393224 | tf_op jit(solution)/shard_map/ppermute | solution.py:284
  27.1 10.3 %copy-start = (f32[512,512]{1,0:T(8,128)S(1)}, f32[512,512]{1,0:T(8,128)}, u32[]{:S(2)}) copy-start(f32[512,512]{1,0:T(8,128)} %own_ref.1) | copy-start | bytes 3145732
  34.4 3.0 %collective-permute-start.9 = (f32[512,512]{1,0:T(8,128)S(1)}, f32[512,512]{1,0:T(8,128)S(1)}, u32[]{:S(2)}, u32[]{:S(2)}) collective-permute-start(f32[512,512]{1,0:T(8,128)S(1)} %collective-permute-done.sent_ref), channel_id=1, source_target_pairs={{0,16},{16,0},{1,17},{17,1},{2,18},{18,2},{3,19},{19,3},{4,20},{20... | collective-permute-start | bytes 3145736 | tf_op jit(solution)/shard_map/ppermute | solution.py:276
  35.1 5.1 %collective-permute-start.10 = (f32[64,512]{1,0:T(8,128)S(1)}, f32[64,512]{1,0:T(8,128)S(1)}, u32[]{:S(2)}, u32[]{:S(2)}) collective-permute-start(f32[64,512]{1,0:T(8,128)S(1)} %get-tuple-element.46.refs_1_), channel_id=1, source_target_pairs={{0,4},{4,0},{8,12},{12,8},{1,5},{5,1},{9,13},{13,9},{2,6},{6,2},{1... | collective-permute-start | bytes 393224 | tf_op jit(solution)/shard_map/ppermute | solution.py:279
  35.4 5.1 %collective-permute-start.8 = (f32[64,512]{1,0:T(8,128)S(1)}, f32[64,512]{1,0:T(8,128)S(1)}, u32[]{:S(2)}, u32[]{:S(2)}) collective-permute-start(f32[64,512]{1,0:T(8,128)S(1)} %get-tuple-element.46.refs_1_), channel_id=1, source_target_pairs={{0,8},{4,12},{8,0},{12,4},{1,9},{5,13},{9,1},{13,5},{2,10},{6,14},... | collective-permute-start | bytes 393224 | tf_op jit(solution)/shard_map/ppermute | solution.py:279
  40.2 5.1 %collective-permute-start.11 = (f32[64,512]{1,0:T(8,128)S(1)}, f32[64,512]{1,0:T(8,128)S(1)}, u32[]{:S(2)}, u32[]{:S(2)}) collective-permute-start(f32[64,512]{1,0:T(8,128)S(1)} %shard_map.103.refs_1_), channel_id=1, source_target_pairs={{0,12},{4,8},{8,4},{12,0},{1,13},{5,9},{9,5},{13,1},{2,14},{6,10},... | collective-permute-start | bytes 393224 | tf_op jit(solution)/shard_map/ppermute | solution.py:279
  45.3 3.9 %collective-permute-start.12 = (f32[64,512]{1,0:T(8,128)S(1)}, f32[64,512]{1,0:T(8,128)S(1)}, u32[]{:S(2)}, u32[]{:S(2)}) collective-permute-start(f32[64,512]{1,0:T(8,128)S(1)} %shard_map.105.refs_1_), channel_id=1, source_target_pairs={{0,4},{4,0},{8,12},{12,8},{1,5},{5,1},{9,13},{13,9},{2,6},{6,2},{1... | collective-permute-start | bytes 393224 | tf_op jit(solution)/shard_map/ppermute | solution.py:279
  46.2 3.8 %collective-permute-start.13 = (f32[64,512]{1,0:T(8,128)S(1)}, f32[64,512]{1,0:T(8,128)S(1)}, u32[]{:S(2)}, u32[]{:S(2)}) collective-permute-start(f32[64,512]{1,0:T(8,128)S(1)} %shard_map.105.refs_1_), channel_id=1, source_target_pairs={{0,8},{4,12},{8,0},{12,4},{1,9},{5,13},{9,1},{13,5},{2,10},{6,14},... | collective-permute-start | bytes 393224 | tf_op jit(solution)/shard_map/ppermute | solution.py:279
  50.8 4.6 %collective-permute-start.14 = (f32[64,512]{1,0:T(8,128)S(1)}, f32[64,512]{1,0:T(8,128)S(1)}, u32[]{:S(2)}, u32[]{:S(2)}) collective-permute-start(f32[64,512]{1,0:T(8,128)S(1)} %shard_map.106.x_ref), channel_id=1, source_target_pairs={{1,3},{2,0},{0,1},{3,2},{5,7},{6,4},{4,5},{7,6},{9,11},{10,8},{8,9... | collective-permute-start | bytes 393224 | tf_op jit(solution)/shard_map/ppermute | solution.py:284
  50.8 5.2 %collective-permute-start.15 = (f32[64,512]{1,0:T(8,128)S(1)}, f32[64,512]{1,0:T(8,128)S(1)}, u32[]{:S(2)}, u32[]{:S(2)}) collective-permute-start(f32[64,512]{1,0:T(8,128)S(1)} %shard_map.106.x_ref), channel_id=1, source_target_pairs={{1,0},{2,3},{0,1},{3,2},{5,4},{6,7},{4,5},{7,6},{9,8},{10,11},{8,9... | collective-permute-start | bytes 393224 | tf_op jit(solution)/shard_map/ppermute | solution.py:284
  52.3 7.1 %collective-permute-start.16 = (f32[64,512]{1,0:T(8,128)S(1)}, f32[64,512]{1,0:T(8,128)S(1)}, u32[]{:S(2)}, u32[]{:S(2)}) collective-permute-start(f32[64,512]{1,0:T(8,128)S(1)} %shard_map.106.x_ref), channel_id=1, source_target_pairs={{1,2},{2,1},{0,0},{3,3},{5,6},{6,5},{4,4},{7,7},{9,10},{10,9},{8,8... | collective-permute-start | bytes 393224 | tf_op jit(solution)/shard_map/ppermute | solution.py:284
  59.6 4.7 %collective-permute-start.17 = (f32[512,128]{1,0:T(8,128)S(1)}, f32[512,128]{1,0:T(8,128)S(1)}, u32[]{:S(2)}, u32[]{:S(2)}) collective-permute-start(f32[512,128]{1,0:T(8,128)S(1)} %shard_map.107.part_ref), channel_id=1, source_target_pairs={{0,16},{16,0},{1,17},{17,1},{2,18},{18,2},{3,19},{19,3},{4,20},{20... | collective-permute-start | bytes 786440 | tf_op jit(solution)/shard_map/ppermute | solution.py:276

commit v10 on v9

--- a/solution.py
+++ b/solution.py
@@ -150,11 +150,11 @@
     return product[:half] + product[half:]
 
 
-def own_kernel(keep_ref, tgt_ref, *out_refs):
+def own_kernel(keep_ref, send_ref, *out_refs):
     _, row, _ = place()
-    size = out_refs[0].shape[1]
+    half, size = out_refs[0].shape
     value = jnp.concatenate(split(keep_ref[...]), axis=0)
-    target = jnp.concatenate([tgt_ref[s:s + 1, :] for s in range(tgt_ref.shape[0])], axis=1)
+    target = send_ref[half:half + 1, :].astype(jnp.int32)
     for s, out_ref in enumerate(out_refs):
         out_ref[...] = scatter(value, target, size, jnp.bitwise_xor(row, s) * size)
 
@@ -238,7 +238,7 @@
     copy.wait()
 
 
-def call(kernel, ins, outs, scratch=(), outside=(), outs_outside=(), pinned=(), aliases=None, limit=24):
+def call(kernel, ins, outs, scratch=(), outside=(), outs_outside=(), pinned=(), aliases=None, limit=24, flops=0):
     def spec(i, a):
         return ANY if i in outside else SM if a.ndim == 1 else VM
 
@@ -253,7 +253,7 @@
         out_specs=[ANY if i in outs_outside else VM for i in range(len(outs))],
         scratch_shapes=[pltpu.VMEM(s, F32) if isinstance(s, tuple) else s for s in scratch],
         input_output_aliases=aliases or {},
-        cost_estimate=pl.CostEstimate(flops=0, bytes_accessed=4 * sum(a.size for a in ins), transcendentals=0),
+        cost_estimate=pl.CostEstimate(flops=flops, bytes_accessed=4 * sum(a.size for a in ins), transcendentals=0),
         compiler_params=pltpu.CompilerParams(vmem_limit_bytes=limit * 1024 * 1024),
     )(*ins)
     return list(outs)
@@ -306,7 +306,7 @@
         pinned=(1, 2),
         limit=56,
     )
-    sums = call(own_kernel, [keep, targets], [(half, size)] * rows)
+    sums = call(own_kernel, [keep, send], [(half, size)] * rows)
     sums = call(other_kernel, [swap(send)] + sums, [(half, size)] * rows)
     got = [along_row(sums[s], s) for s in (1, 2, 3)]
     rhs_piece, diag_high, diag_low = call(
@@ -316,18 +316,17 @@
     first, second = call(pieces_kernel, [sums[0]] + got, [shape] * 2, [(half, size)])
     q = [
         along_col(second, [(0, 2), (3, 1)]),
+        along_col(first, [(0, 1), (3, 2)]),
         along_col(first, [(1, 2), (2, 1)]),
-        along_col(first, [(0, 1), (3, 2)]),
     ]
 
-    def chain(owner, ins, has_sums=False, solves=True):
+    def chain(owner, ins, has_sums=False, solves=True, flops=0):
         outs = call(
-            functools.partial(chain_kernel, owner, has_sums, solves), ins, [shape] * (1 + has_sums)
+            functools.partial(chain_kernel, owner, has_sums, solves), ins, [shape] * (1 + has_sums), flops=flops
         )
         return outs if has_sums else outs[0]
 
-    res, x = chain(0, [rhs_piece, second] + q + diag, has_sums=True)
-    sent, res = lax.optimization_barrier((sent, res))
+    res, x = chain(0, [rhs_piece, second] + q + diag, has_sums=True, flops=10 ** 10)
     factor = call(factor_kernel, [top_factor, sent, swap(sent)], [block] * 6)
     factor = [factor[0:2], factor[2:4], factor[4:6]]
     to1 = along_row(x, 1)

time: 65.4 us -> 68 us (1.040)
  the two profiles are of different devices: /device:TPU:15 before, /device:TPU:0 now
where the time goes in v10:
time: 68 us; the launch traced here: 67.8 us
  waiting for transfers between devices  30.9 us (45%)
  starting transfers between devices  29 us (43%)
  Pallas kernels  7.17 us (11%)
  between operations  0.79 us (1%)
    ppermute x8, waiting for transfers between devices, along_row(): return lax.ppermute(value, 'row', [(r, r ^ step) for r in range(rows)])  21.1 us
    ppermute x8, starting transfers between devices, along_row(): return lax.ppermute(value, 'row', [(r, r ^ step) for r in range(rows)])  15.5 us
    ppermute x6, starting transfers between devices, along_col(): return lax.ppermute(value, 'col', pairs + list(zip(rest, open_ends)))  10.9 us
    ppermute x6, waiting for transfers between devices, along_col(): return lax.ppermute(value, 'col', pairs + list(zip(rest, open_ends)))  8.51 us
    pallas_call x15, Pallas kernels, call(): pl.pallas_call(kernel, out_shape=[shape(i, out) for i, out in enumerate(o...  7.17 us
    ppermute x1, starting transfers between devices, central(): sent = lax.ppermute(top_factor, ('leaf', 'row', 'col'), pairs)  1.88 us
  transfers between devices with their start and end apart: 18, of which 12 were waited for; matrix products, arithmetic and copies ran while one was open for 0% of the time, Pallas kernels for 9%

profile of v10, /device:TPU:0, one launch (start us, length us, event | category | flops | bytes accessed | tf_op | source)
XLA Modules:
  0.0 67.8 jit_solution(8062311063027325550)
XLA Ops:
  0.6 1.9 %collective-permute-start.8 = (f32[512,512]{1,0:T(8,128)}, f32[512,512]{1,0:T(8,128)S(1)}, u32[]{:S(2)}, u32[]{:S(2)}) collective-permute-start(f32[512,512]{1,0:T(8,128)} %own_ref.1), channel_id=1, source_target_pairs={{4,5},{8,9},{12,13},{9,10},{13,14},{20,22},{24,26},{28,30},{30,29}... | collective-permute-start | bytes 3145736 | tf_op jit(solution)/shard_map/ppermute | solution.py:297
  2.5 3.6 %shard_map.95 = (f32[2,256,256]{2,1,0:T(8,128)}, f32[128,512]{1,0:T(8,128)S(1)}, f32[136,512]{1,0:T(8,128)S(1)}) custom-call(s32[2]{0:T(128)} %live_ref.1, f32[2,256,256]{2,1,0:T(8,128)} %rhs_hbm.1, f32[2,256,256]{2,1,0:T(8,128)} %diag_hbm.1, f32[2,256,256]{2,1,0:T(8,128)} %off_hbm.1, s32[2,256]{1,0:T(2,128)} %tgt_ref.1), custom_call_target="tpu_custom_call" | custom-call | bytes 1574920 | tf_op jit(solution)/shard_map/pallas_call | solution.py:249
  6.1 0.5 collective-permute-start
  6.6 0.8 %shard_map.97 = (f32[128,512]{1,0:T(8,128)S(1)}, f32[128,512]{1,0:T(8,128)S(1)}, f32[128,512]{1,0:T(8,128)S(1)}, f32[128,512]{1,0:T(8,128)S(1)}) custom-call(f32[128,512]{1,0:T(8,128)S(1)} %get-tuple-element.29.keep_ref, f32[136,512]{1,0:T(8,128)S(1)} %get-tuple-element.28.send_ref), custom_call_target="tpu_custom_call" | custom-call | bytes 540672 | tf_op jit(solution)/shard_map/pallas_call | solution.py:249
  7.4 0.4 collective-permute-done.recv_ref
  7.8 0.0 copy-start.1
  7.8 0.8 %shard_map.98 = (f32[128,512]{1,0:T(8,128)S(1)}, f32[128,512]{1,0:T(8,128)S(1)}, f32[128,512]{1,0:T(8,128)S(1)}, f32[128,512]{1,0:T(8,128)S(1)}) custom-call(f32[136,512]{1,0:T(8,128)S(1)} %collective-permute-done.recv_ref, f32[128,512]{1,0:T(8,128)S(1)} %get-tuple-element.30.refs_0_, f32[128,512]{1,0:T(8,128)S(1)} %get-tuple-element.31.refs_1_, ...), custom_call_target="tpu_custom_call" | custom-call | bytes 1327104 | tf_op jit(solution)/shard_map/pallas_call | solution.py:249
  8.6 4.7 %collective-permute-start.1 = (f32[128,512]{1,0:T(8,128)S(1)}, f32[128,512]{1,0:T(8,128)S(1)}, u32[]{:S(2)}, u32[]{:S(2)}) collective-permute-start(f32[128,512]{1,0:T(8,128)S(1)} %get-tuple-element.35), channel_id=1, source_target_pairs={{0,4},{4,0},{8,12},{12,8},{1,5},{5,1},{9,13},{13,9},{2,6},{6,2},{1... | collective-permute-start | bytes 786440 | tf_op jit(solution)/shard_map/ppermute | solution.py:279
  13.3 1.5 %collective-permute-start.2 = (f32[128,512]{1,0:T(8,128)S(1)}, f32[128,512]{1,0:T(8,128)S(1)}, u32[]{:S(2)}, u32[]{:S(2)}) collective-permute-start(f32[128,512]{1,0:T(8,128)S(1)} %get-tuple-element.36), channel_id=1, source_target_pairs={{0,8},{4,12},{8,0},{12,4},{1,9},{5,13},{9,1},{13,5},{2,10},{6,14},... | collective-permute-start | bytes 786440 | tf_op jit(solution)/shard_map/ppermute | solution.py:279
  14.9 0.0 collective-permute-start.3
  14.9 5.6 %collective-permute-done.1.b_ref = f32[128,512]{1,0:T(8,128)S(1)} collective-permute-done((f32[128,512]{1,0:T(8,128)S(1)}, f32[128,512]{1,0:T(8,128)S(1)}, u32[]{:S(2)}, u32[]{:S(2)}) %collective-permute-start.1) | collective-permute-done | bytes 262176 | tf_op jit(solution)/shard_map/ppermute | solution.py:279
  20.5 6.8 %collective-permute-done.2.c_ref = f32[128,512]{1,0:T(8,128)S(1)} collective-permute-done((f32[128,512]{1,0:T(8,128)S(1)}, f32[128,512]{1,0:T(8,128)S(1)}, u32[]{:S(2)}, u32[]{:S(2)}) %collective-permute-start.2) | collective-permute-done | bytes 262176 | tf_op jit(solution)/shard_map/ppermute | solution.py:279
  27.2 0.0 collective-permute-done.3.d_ref
  27.2 0.1 shard_map.99
  27.3 0.7 %collective-permute-start.4 = (f32[64,512]{1,0:T(8,128)S(1)}, f32[64,512]{1,0:T(8,128)S(1)}, u32[]{:S(2)}, u32[]{:S(2)}) collective-permute-start(f32[64,512]{1,0:T(8,128)S(1)} %get-tuple-element.38.refs_1_), channel_id=1, source_target_pairs={{0,2},{3,1},{1,0},{2,3},{4,6},{7,5},{5,4},{6,7},{8,10},{11,9},{9,8... | collective-permute-start | bytes 393224 | tf_op jit(solution)/shard_map/ppermute | solution.py:284
  28.1 0.7 collective-permute-start.6
  28.7 3.3 %collective-permute-start.5 = (f32[64,512]{1,0:T(8,128)S(1)}, f32[64,512]{1,0:T(8,128)S(1)}, u32[]{:S(2)}, u32[]{:S(2)}) collective-permute-start(f32[64,512]{1,0:T(8,128)S(1)} %get-tuple-element.39), channel_id=1, source_target_pairs={{0,1},{3,2},{1,0},{2,3},{4,5},{7,6},{5,4},{6,7},{8,9},{11,10},{9,8... | collective-permute-start | bytes 393224 | tf_op jit(solution)/shard_map/ppermute | solution.py:284
  32.0 0.0 copy-done.1
  32.0 0.0 copy-done.2
  32.0 0.3 shard_map.96
  32.4 0.0 collective-permute-done.8.sent_ref
  32.4 0.1 collective-permute-start.9
  32.5 0.9 %collective-permute-done.4.refs_2_ = f32[64,512]{1,0:T(8,128)S(1)} collective-permute-done((f32[64,512]{1,0:T(8,128)S(1)}, f32[64,512]{1,0:T(8,128)S(1)}, u32[]{:S(2)}, u32[]{:S(2)}) %collective-permute-start.4) | collective-permute-done | bytes 131104 | tf_op jit(solution)/shard_map/ppermute | solution.py:284
  33.4 0.0 collective-permute-done.6.refs_4_
  33.4 1.8 %collective-permute-done.5.refs_3_ = f32[64,512]{1,0:T(8,128)S(1)} collective-permute-done((f32[64,512]{1,0:T(8,128)S(1)}, f32[64,512]{1,0:T(8,128)S(1)}, u32[]{:S(2)}, u32[]{:S(2)}) %collective-permute-start.5) | collective-permute-done | bytes 131104 | tf_op jit(solution)/shard_map/ppermute | solution.py:284
  35.2 2.0 %collective-permute-start.10 = (f32[64,512]{1,0:T(8,128)S(1)}, f32[64,512]{1,0:T(8,128)S(1)}, u32[]{:S(2)}, u32[]{:S(2)}) collective-permute-start(f32[64,512]{1,0:T(8,128)S(1)} %get-tuple-element.43.refs_1_), channel_id=1, source_target_pairs={{0,4},{4,0},{8,12},{12,8},{1,5},{5,1},{9,13},{13,9},{2,6},{6,2},{1... | collective-permute-start | bytes 393224 | tf_op jit(solution)/shard_map/ppermute | solution.py:279
  37.2 1.3 %collective-permute-start.7 = (f32[64,512]{1,0:T(8,128)S(1)}, f32[64,512]{1,0:T(8,128)S(1)}, u32[]{:S(2)}, u32[]{:S(2)}) collective-permute-start(f32[64,512]{1,0:T(8,128)S(1)} %get-tuple-element.43.refs_1_), channel_id=1, source_target_pairs={{0,8},{4,12},{8,0},{12,4},{1,9},{5,13},{9,1},{13,5},{2,10},{6,14},... | collective-permute-start | bytes 393224 | tf_op jit(solution)/shard_map/ppermute | solution.py:279
  38.5 0.0 collective-permute-done.9.other_ref
  38.5 0.0 copy-done
  38.5 1.8 %collective-permute-done.10.refs_4_ = f32[64,512]{1,0:T(8,128)S(1)} collective-permute-done((f32[64,512]{1,0:T(8,128)S(1)}, f32[64,512]{1,0:T(8,128)S(1)}, u32[]{:S(2)}, u32[]{:S(2)}) %collective-permute-start.10) | collective-permute-done | bytes 131104 | tf_op jit(solution)/shard_map/ppermute | solution.py:279
  40.3 2.7 %collective-permute-start.11 = (f32[64,512]{1,0:T(8,128)S(1)}, f32[64,512]{1,0:T(8,128)S(1)}, u32[]{:S(2)}, u32[]{:S(2)}) collective-permute-start(f32[64,512]{1,0:T(8,128)S(1)} %shard_map.103.refs_1_), channel_id=1, source_target_pairs={{0,12},{4,8},{8,4},{12,0},{1,13},{5,9},{9,5},{13,1},{2,14},{6,10},... | collective-permute-start | bytes 393224 | tf_op jit(solution)/shard_map/ppermute | solution.py:279
  42.9 0.0 collective-permute-done.7.refs_2_
  43.0 3.2 %collective-permute-done.11.refs_2_.refs_4_ = f32[64,512]{1,0:T(8,128)S(1)} collective-permute-done((f32[64,512]{1,0:T(8,128)S(1)}, f32[64,512]{1,0:T(8,128)S(1)}, u32[]{:S(2)}, u32[]{:S(2)}) %collective-permute-start.11) | collective-permute-done | bytes 131104 | tf_op jit(solution)/shard_map/ppermute | solution.py:279
  46.2 2.1 %collective-permute-start.13 = (f32[64,512]{1,0:T(8,128)S(1)}, f32[64,512]{1,0:T(8,128)S(1)}, u32[]{:S(2)}, u32[]{:S(2)}) collective-permute-start(f32[64,512]{1,0:T(8,128)S(1)} %shard_map.105.refs_1_), channel_id=1, source_target_pairs={{0,8},{4,12},{8,0},{12,4},{1,9},{5,13},{9,1},{13,5},{2,10},{6,14},... | collective-permute-start | bytes 393224 | tf_op jit(solution)/shard_map/ppermute | solution.py:279
  48.3 1.2 %collective-permute-start.12 = (f32[64,512]{1,0:T(8,128)S(1)}, f32[64,512]{1,0:T(8,128)S(1)}, u32[]{:S(2)}, u32[]{:S(2)}) collective-permute-start(f32[64,512]{1,0:T(8,128)S(1)} %shard_map.105.refs_1_), channel_id=1, source_target_pairs={{0,4},{4,0},{8,12},{12,8},{1,5},{5,1},{9,13},{13,9},{2,6},{6,2},{1... | collective-permute-start | bytes 393224 | tf_op jit(solution)/shard_map/ppermute | solution.py:279
  49.5 1.8 %collective-permute-done.13.refs_7_ = f32[64,512]{1,0:T(8,128)S(1)} collective-permute-done((f32[64,512]{1,0:T(8,128)S(1)}, f32[64,512]{1,0:T(8,128)S(1)}, u32[]{:S(2)}, u32[]{:S(2)}) %collective-permute-start.13) | collective-permute-done | bytes 131104 | tf_op jit(solution)/shard_map/ppermute | solution.py:279
  51.2 2.0 %collective-permute-done.12.refs_4_ = f32[64,512]{1,0:T(8,128)S(1)} collective-permute-done((f32[64,512]{1,0:T(8,128)S(1)}, f32[64,512]{1,0:T(8,128)S(1)}, u32[]{:S(2)}, u32[]{:S(2)}) %collective-permute-start.12) | collective-permute-done | bytes 131104 | tf_op jit(solution)/shard_map/ppermute | solution.py:279
  53.3 0.7 collective-permute-start.16
  54.0 5.5 %collective-permute-start.15 = (f32[64,512]{1,0:T(8,128)S(1)}, f32[64,512]{1,0:T(8,128)S(1)}, u32[]{:S(2)}, u32[]{:S(2)}) collective-permute-start(f32[64,512]{1,0:T(8,128)S(1)} %shard_map.106.x_ref), channel_id=1, source_target_pairs={{1,0},{2,3},{0,1},{3,2},{5,4},{6,7},{4,5},{7,6},{9,8},{10,11},{8,9... | collective-permute-start | bytes 393224 | tf_op jit(solution)/shard_map/ppermute | solution.py:284
  59.5 0.1 collective-permute-start.14
  59.5 0.0 collective-permute-done.16.b_ref
  59.5 2.9 %collective-permute-done.15.a_ref = f32[64,512]{1,0:T(8,128)S(1)} collective-permute-done((f32[64,512]{1,0:T(8,128)S(1)}, f32[64,512]{1,0:T(8,128)S(1)}, u32[]{:S(2)}, u32[]{:S(2)}) %collective-permute-start.15) | collective-permute-done | bytes 131104 | tf_op jit(solution)/shard_map/ppermute | solution.py:284
  62.4 2.9 %collective-permute-done.14.c_ref = f32[64,512]{1,0:T(8,128)S(1)} collective-permute-done((f32[64,512]{1,0:T(8,128)S(1)}, f32[64,512]{1,0:T(8,128)S(1)}, u32[]{:S(2)}, u32[]{:S(2)}) %collective-permute-start.14) | collective-permute-done | bytes 131104 | tf_op jit(solution)/shard_map/ppermute | solution.py:284
  65.3 0.1 shard_map.107.part_ref
  65.5 0.1 collective-permute-start.17
  65.6 0.7 %shard_map.108.refs_0_ = f32[512,256]{1,0:T(8,128)} custom-call(f32[512,128]{1,0:T(8,128)S(1)} %shard_map.107.part_ref), custom_call_target="tpu_custom_call" | custom-call | bytes 262144 | tf_op jit(solution)/shard_map/pallas_call | solution.py:249
  66.3 0.8 %collective-permute-done.17.part_ref = f32[512,128]{1,0:T(8,128)S(1)} collective-permute-done((f32[512,128]{1,0:T(8,128)S(1)}, f32[512,128]{1,0:T(8,128)S(1)}, u32[]{:S(2)}, u32[]{:S(2)}) %collective-permute-start.17) | collective-permute-done | bytes 262176 | tf_op jit(solution)/shard_map/ppermute | solution.py:276
  67.1 0.7 %shard_map.109 = f32[512,256]{1,0:T(8,128)} custom-call(f32[512,128]{1,0:T(8,128)S(1)} %collective-permute-done.17.part_ref, f32[512,256]{1,0:T(8,128)} %shard_map.108.refs_0_), custom_call_target="tpu_custom_call", output_to_operand_aliasing={{}: (1, {})} | custom-call | bytes 786432 | tf_op jit(solution)/shard_map/pallas_call | solution.py:249
  (9 shorter events, 0.1 us)
Async XLA Ops:
  0.6 31.7 %collective-permute-start.8 = (f32[512,512]{1,0:T(8,128)}, f32[512,512]{1,0:T(8,128)S(1)}, u32[]{:S(2)}, u32[]{:S(2)}) collective-permute-start(f32[512,512]{1,0:T(8,128)} %own_ref.1), channel_id=1, source_target_pairs={{4,5},{8,9},{12,13},{9,10},{13,14},{20,22},{24,26},{28,30},{30,29}... | collective-permute-start | bytes 3145736 | tf_op jit(solution)/shard_map/ppermute | solution.py:297
  6.1 1.7 %collective-permute-start = (f32[136,512]{1,0:T(8,128)S(1)}, f32[136,512]{1,0:T(8,128)S(1)}, u32[]{:S(2)}, u32[]{:S(2)}) collective-permute-start(f32[136,512]{1,0:T(8,128)S(1)} %get-tuple-element.28.send_ref), channel_id=1, source_target_pairs={{0,16},{16,0},{1,17},{17,1},{2,18},{18,2},{3,19},{19,3},{4,20},{20... | collective-permute-start | bytes 835592 | tf_op jit(solution)/shard_map/ppermute | solution.py:276
  7.8 24.2 %copy-start.1 = (f32[512,512]{1,0:T(8,128)S(1)}, f32[512,512]{1,0:T(8,128)}, u32[]{:S(2)}) copy-start(f32[512,512]{1,0:T(8,128)} %diag_ref.1) | copy-start | bytes 3145732
  8.6 11.9 %collective-permute-start.1 = (f32[128,512]{1,0:T(8,128)S(1)}, f32[128,512]{1,0:T(8,128)S(1)}, u32[]{:S(2)}, u32[]{:S(2)}) collective-permute-start(f32[128,512]{1,0:T(8,128)S(1)} %get-tuple-element.35), channel_id=1, source_target_pairs={{0,4},{4,0},{8,12},{12,8},{1,5},{5,1},{9,13},{13,9},{2,6},{6,2},{1... | collective-permute-start | bytes 786440 | tf_op jit(solution)/shard_map/ppermute | solution.py:279
  13.3 13.9 %collective-permute-start.2 = (f32[128,512]{1,0:T(8,128)S(1)}, f32[128,512]{1,0:T(8,128)S(1)}, u32[]{:S(2)}, u32[]{:S(2)}) collective-permute-start(f32[128,512]{1,0:T(8,128)S(1)} %get-tuple-element.36), channel_id=1, source_target_pairs={{0,8},{4,12},{8,0},{12,4},{1,9},{5,13},{9,1},{13,5},{2,10},{6,14},... | collective-permute-start | bytes 786440 | tf_op jit(solution)/shard_map/ppermute | solution.py:279
  14.9 12.4 %collective-permute-start.3 = (f32[128,512]{1,0:T(8,128)S(1)}, f32[128,512]{1,0:T(8,128)S(1)}, u32[]{:S(2)}, u32[]{:S(2)}) collective-permute-start(f32[128,512]{1,0:T(8,128)S(1)} %get-tuple-element.37), channel_id=1, source_target_pairs={{0,12},{4,8},{8,4},{12,0},{1,13},{5,9},{9,5},{13,1},{2,14},{6,10},... | collective-permute-start | bytes 786440 | tf_op jit(solution)/shard_map/ppermute | solution.py:279
  27.2 4.8 %copy-start.2 = (f32[512,256]{1,0:T(8,128)S(1)}, f32[512,256]{1,0:T(8,128)}, u32[]{:S(2)}) copy-start(f32[512,256]{1,0:T(8,128)} %rhs_ref.1) | copy-start | bytes 1572868
  27.3 6.0 %collective-permute-start.4 = (f32[64,512]{1,0:T(8,128)S(1)}, f32[64,512]{1,0:T(8,128)S(1)}, u32[]{:S(2)}, u32[]{:S(2)}) collective-permute-start(f32[64,512]{1,0:T(8,128)S(1)} %get-tuple-element.38.refs_1_), channel_id=1, source_target_pairs={{0,2},{3,1},{1,0},{2,3},{4,6},{7,5},{5,4},{6,7},{8,10},{11,9},{9,8... | collective-permute-start | bytes 393224 | tf_op jit(solution)/shard_map/ppermute | solution.py:284
  28.1 5.3 %collective-permute-start.6 = (f32[64,512]{1,0:T(8,128)S(1)}, f32[64,512]{1,0:T(8,128)S(1)}, u32[]{:S(2)}, u32[]{:S(2)}) collective-permute-start(f32[64,512]{1,0:T(8,128)S(1)} %get-tuple-element.39), channel_id=1, source_target_pairs={{1,2},{2,1},{0,0},{3,3},{5,6},{6,5},{4,4},{7,7},{9,10},{10,9},{8,8... | collective-permute-start | bytes 393224 | tf_op jit(solution)/shard_map/ppermute | solution.py:284
  28.7 6.4 %collective-permute-start.5 = (f32[64,512]{1,0:T(8,128)S(1)}, f32[64,512]{1,0:T(8,128)S(1)}, u32[]{:S(2)}, u32[]{:S(2)}) collective-permute-start(f32[64,512]{1,0:T(8,128)S(1)} %get-tuple-element.39), channel_id=1, source_target_pairs={{0,1},{3,2},{1,0},{2,3},{4,5},{7,6},{5,4},{6,7},{8,9},{11,10},{9,8... | collective-permute-start | bytes 393224 | tf_op jit(solution)/shard_map/ppermute | solution.py:284
  32.4 6.1 %collective-permute-start.9 = (f32[512,512]{1,0:T(8,128)S(1)}, f32[512,512]{1,0:T(8,128)S(1)}, u32[]{:S(2)}, u32[]{:S(2)}) collective-permute-start(f32[512,512]{1,0:T(8,128)S(1)} %collective-permute-done.8.sent_ref), channel_id=1, source_target_pairs={{0,16},{16,0},{1,17},{17,1},{2,18},{18,2},{3,19},{19,3},{4,20},{20... | collective-permute-start | bytes 3145736 | tf_op jit(solution)/shard_map/ppermute | solution.py:276
  35.2 3.3 %copy-start = (f32[512,512]{1,0:T(8,128)S(1)}, f32[512,512]{1,0:T(8,128)}, u32[]{:S(2)}) copy-start(f32[512,512]{1,0:T(8,128)} %own_ref.1) | copy-start | bytes 3145732
  35.2 5.0 %collective-permute-start.10 = (f32[64,512]{1,0:T(8,128)S(1)}, f32[64,512]{1,0:T(8,128)S(1)}, u32[]{:S(2)}, u32[]{:S(2)}) collective-permute-start(f32[64,512]{1,0:T(8,128)S(1)} %get-tuple-element.43.refs_1_), channel_id=1, source_target_pairs={{0,4},{4,0},{8,12},{12,8},{1,5},{5,1},{9,13},{13,9},{2,6},{6,2},{1... | collective-permute-start | bytes 393224 | tf_op jit(solution)/shard_map/ppermute | solution.py:279
  37.2 5.7 %collective-permute-start.7 = (f32[64,512]{1,0:T(8,128)S(1)}, f32[64,512]{1,0:T(8,128)S(1)}, u32[]{:S(2)}, u32[]{:S(2)}) collective-permute-start(f32[64,512]{1,0:T(8,128)S(1)} %get-tuple-element.43.refs_1_), channel_id=1, source_target_pairs={{0,8},{4,12},{8,0},{12,4},{1,9},{5,13},{9,1},{13,5},{2,10},{6,14},... | collective-permute-start | bytes 393224 | tf_op jit(solution)/shard_map/ppermute | solution.py:279
  40.3 5.9 %collective-permute-start.11 = (f32[64,512]{1,0:T(8,128)S(1)}, f32[64,512]{1,0:T(8,128)S(1)}, u32[]{:S(2)}, u32[]{:S(2)}) collective-permute-start(f32[64,512]{1,0:T(8,128)S(1)} %shard_map.103.refs_1_), channel_id=1, source_target_pairs={{0,12},{4,8},{8,4},{12,0},{1,13},{5,9},{9,5},{13,1},{2,14},{6,10},... | collective-permute-start | bytes 393224 | tf_op jit(solution)/shard_map/ppermute | solution.py:279
  46.2 5.0 %collective-permute-start.13 = (f32[64,512]{1,0:T(8,128)S(1)}, f32[64,512]{1,0:T(8,128)S(1)}, u32[]{:S(2)}, u32[]{:S(2)}) collective-permute-start(f32[64,512]{1,0:T(8,128)S(1)} %shard_map.105.refs_1_), channel_id=1, source_target_pairs={{0,8},{4,12},{8,0},{12,4},{1,9},{5,13},{9,1},{13,5},{2,10},{6,14},... | collective-permute-start | bytes 393224 | tf_op jit(solution)/shard_map/ppermute | solution.py:279
  48.3 5.0 %collective-permute-start.12 = (f32[64,512]{1,0:T(8,128)S(1)}, f32[64,512]{1,0:T(8,128)S(1)}, u32[]{:S(2)}, u32[]{:S(2)}) collective-permute-start(f32[64,512]{1,0:T(8,128)S(1)} %shard_map.105.refs_1_), channel_id=1, source_target_pairs={{0,4},{4,0},{8,12},{12,8},{1,5},{5,1},{9,13},{13,9},{2,6},{6,2},{1... | collective-permute-start | bytes 393224 | tf_op jit(solution)/shard_map/ppermute | solution.py:279
  53.3 6.3 %collective-permute-start.16 = (f32[64,512]{1,0:T(8,128)S(1)}, f32[64,512]{1,0:T(8,128)S(1)}, u32[]{:S(2)}, u32[]{:S(2)}) collective-permute-start(f32[64,512]{1,0:T(8,128)S(1)} %shard_map.106.x_ref), channel_id=1, source_target_pairs={{1,2},{2,1},{0,0},{3,3},{5,6},{6,5},{4,4},{7,7},{9,10},{10,9},{8,8... | collective-permute-start | bytes 393224 | tf_op jit(solution)/shard_map/ppermute | solution.py:284
  54.0 8.5 %collective-permute-start.15 = (f32[64,512]{1,0:T(8,128)S(1)}, f32[64,512]{1,0:T(8,128)S(1)}, u32[]{:S(2)}, u32[]{:S(2)}) collective-permute-start(f32[64,512]{1,0:T(8,128)S(1)} %shard_map.106.x_ref), channel_id=1, source_target_pairs={{1,0},{2,3},{0,1},{3,2},{5,4},{6,7},{4,5},{7,6},{9,8},{10,11},{8,9... | collective-permute-start | bytes 393224 | tf_op jit(solution)/shard_map/ppermute | solution.py:284
  59.5 5.9 %collective-permute-start.14 = (f32[64,512]{1,0:T(8,128)S(1)}, f32[64,512]{1,0:T(8,128)S(1)}, u32[]{:S(2)}, u32[]{:S(2)}) collective-permute-start(f32[64,512]{1,0:T(8,128)S(1)} %shard_map.106.x_ref), channel_id=1, source_target_pairs={{1,3},{2,0},{0,1},{3,2},{5,7},{6,4},{4,5},{7,6},{9,11},{10,8},{8,9... | collective-permute-start | bytes 393224 | tf_op jit(solution)/shard_map/ppermute | solution.py:284
  65.5 1.6 %collective-permute-start.17 = (f32[512,128]{1,0:T(8,128)S(1)}, f32[512,128]{1,0:T(8,128)S(1)}, u32[]{:S(2)}, u32[]{:S(2)}) collective-permute-start(f32[512,128]{1,0:T(8,128)S(1)} %shard_map.107.part_ref), channel_id=1, source_target_pairs={{0,16},{16,0},{1,17},{17,1},{2,18},{18,2},{3,19},{19,3},{4,20},{20... | collective-permute-start | bytes 786440 | tf_op jit(solution)/shard_map/ppermute | solution.py:276

commit v11 on v10

--- a/solution.py
+++ b/solution.py
@@ -108,8 +108,8 @@
     high_ref[...], low_ref[...] = split(lower(diag_ref[...]).T)
 
 
-def child_kernel(live_ref, rhs_hbm, diag_hbm, off_hbm, tgt_ref, sol_hbm, keep_ref, send_ref,
-                 rhs_ref, diag_ref, off_ref, sol_ref, tiles_ref, sems):
+def child_kernel(live_hbm, rhs_hbm, diag_hbm, off_hbm, tgt_hbm, sol_hbm, keep_ref, send_ref,
+                 live_ref, tgt_ref, rhs_ref, diag_ref, off_ref, sol_ref, tiles_ref, sems):
     leaf, _, _ = place()
     children, slots = off_ref.shape[0], off_ref.shape[1]
     half = keep_ref.shape[0]
@@ -119,9 +119,15 @@
         for s in range(children)
     ]
     back = [pltpu.make_async_copy(sol_ref.at[s], sol_hbm.at[s], sems.at[3, s]) for s in range(children)]
+    small = [
+        pltpu.make_async_copy(live_hbm, live_ref, sems.at[4, 0]),
+        pltpu.make_async_copy(tgt_hbm, tgt_ref, sems.at[4, 1]),
+    ]
     for s in range(children):
         for copy in copies[s]:
             copy.start()
+    for copy in small:
+        copy.start()
     for s in range(children):
         copies[s][0].wait()
         copies[s][1].wait()
@@ -130,6 +136,9 @@
         sol_ref[s] = sol
         back[s].start()
         copies[s][2].wait()
+        if s == 0:
+            for copy in small:
+                copy.wait()
         tiles = dot3(sol.T, *split(off_ref[s]), NT)
         slot = lax.broadcasted_iota(jnp.int32, tiles.shape, 1)
         tiles_ref[:, s * slots:(s + 1) * slots] = jnp.where(slot < live_ref[s], tiles, 0.0)
@@ -220,7 +229,7 @@
         out_refs[-1][...] = left
 
 
-def half_kernel(c_ref, a_ref, b_ref, x_ref, out_ref):
+def half_kernel(b_ref, a_ref, c_ref, x_ref, out_ref):
     _, _, z = place()
     x, a, b, c = x_ref[...], a_ref[...], b_ref[...], c_ref[...]
     low = jnp.where(z == 0, a, jnp.where(z == 1, x, jnp.where(z == 2, b, c)))
@@ -299,9 +308,9 @@
         child_kernel,
         [live, child_rhs, child_diag, child_off, targets],
         [child_rhs.shape, (half, children * slots), (half + 8, children * slots)],
-        [child_rhs.shape, child_diag.shape, child_off.shape, child_rhs.shape, (right, children * slots),
-         dma((4, children))],
-        outside=(1, 2, 3),
+        [pltpu.SMEM(live.shape, jnp.int32), pltpu.VMEM(targets.shape, jnp.int32), child_rhs.shape,
+         child_diag.shape, child_off.shape, child_rhs.shape, (right, children * slots), dma((5, max(2, children)))],
+        outside=(0, 1, 2, 3, 4),
         outs_outside=(0,),
         pinned=(1, 2),
         limit=56,
@@ -338,12 +347,12 @@
     to3 = along_row(x, 1)
     late = along_row(x, 2)
     res = chain(3, [res, res, on] + factor[0], solves=False)
-    x = chain(3, [res, x] + diag + [to3] + factor[2] + [late] + factor[1])
+    x = chain(3, [res, x] + diag + [late] + factor[1] + [to3] + factor[2])
 
     both = along_col(x, [(1, 2), (2, 1)])
     step = along_col(x, [(1, 0), (2, 3)])
     over = along_col(x, [(1, 3), (2, 0)])
-    (own,) = call(half_kernel, [over, step, both, x], [(size, half)])
+    (own,) = call(half_kernel, [both, step, over, x], [(size, half)])
     (top_sol,) = call(
         functools.partial(write_kernel, True), [own], [top_rhs.shape], [dma(())], outs_outside=(0,)
     )

time: 68 us -> 64.7 us (0.951)
  the two profiles are of different devices: /device:TPU:0 before, /device:TPU:15 now
where the time goes in v11:
time: 64.7 us; the launch traced here: 64.1 us
  waiting for transfers between devices  29.2 us (45%)
  starting transfers between devices  24.5 us (38%)
  Pallas kernels  8.55 us (13%)
  local copies, waits for them, and re-layouts  0.92 us (1%)
  between operations  0.82 us (1%)
    ppermute x8, waiting for transfers between devices, along_row(): return lax.ppermute(value, 'row', [(r, r ^ step) for r in range(rows)])  20.6 us
    ppermute x3, starting transfers between devices, swap(): return lax.ppermute(value, 'leaf', [(0, 1), (1, 0)])  10.9 us
    pallas_call x15, Pallas kernels, call(): pl.pallas_call(kernel, out_shape=[shape(i, out) for i, out in enumerate(o...  8.55 us
    ppermute x6, starting transfers between devices, along_col(): return lax.ppermute(value, 'col', pairs + list(zip(rest, open_ends)))  7.77 us
    ppermute x6, waiting for transfers between devices, along_col(): return lax.ppermute(value, 'col', pairs + list(zip(rest, open_ends)))  5.9 us
    ppermute x8, starting transfers between devices, along_row(): return lax.ppermute(value, 'row', [(r, r ^ step) for r in range(rows)])  3.77 us
    ppermute x1, starting transfers between devices, central(): sent = lax.ppermute(top_factor, ('leaf', 'row', 'col'), pairs)  2.08 us
    ppermute x1, waiting for transfers between devices, central(): sent = lax.ppermute(top_factor, ('leaf', 'row', 'col'), pairs)  1.88 us
  transfers between devices with their start and end apart: 18, of which 13 were waited for; matrix products, arithmetic and copies ran while one was open for 0% of the time, Pallas kernels for 11%

profile of v11, /device:TPU:15, one launch (start us, length us, event | category | flops | bytes accessed | tf_op | source)
XLA Modules:
  0.0 64.1 jit_solution(5920423641020311830)
XLA Ops:
  0.6 2.1 %collective-permute-start.8 = (f32[512,512]{1,0:T(8,128)}, f32[512,512]{1,0:T(8,128)S(1)}, u32[]{:S(2)}, u32[]{:S(2)}) collective-permute-start(f32[512,512]{1,0:T(8,128)} %own_ref.1), channel_id=1, source_target_pairs={{4,5},{8,9},{12,13},{9,10},{13,14},{20,22},{24,26},{28,30},{30,29}... | collective-permute-start | bytes 3145736 | tf_op jit(solution)/shard_map/ppermute | solution.py:306
  2.7 2.9 %shard_map.95 = (f32[2,256,256]{2,1,0:T(8,128)}, f32[128,512]{1,0:T(8,128)S(1)}, f32[136,512]{1,0:T(8,128)S(1)}) custom-call(s32[2]{0:T(128)} %live_hbm.1, f32[2,256,256]{2,1,0:T(8,128)} %rhs_hbm.1, f32[2,256,256]{2,1,0:T(8,128)} %diag_hbm.1, f32[2,256,256]{2,1,0:T(8,128)} %off_hbm.1, s32[2,256]{1,0:T(2,128)} %tgt_hbm.1), custom_call_target="tpu_custom_call" | custom-call | bytes 1574920 | tf_op jit(solution)/shard_map/pallas_call | solution.py:258
  5.7 2.1 %collective-permute-start = (f32[136,512]{1,0:T(8,128)S(1)}, f32[136,512]{1,0:T(8,128)S(1)}, u32[]{:S(2)}, u32[]{:S(2)}) collective-permute-start(f32[136,512]{1,0:T(8,128)S(1)} %get-tuple-element.28.send_ref), channel_id=1, source_target_pairs={{0,16},{16,0},{1,17},{17,1},{2,18},{18,2},{3,19},{19,3},{4,20},{20... | collective-permute-start | bytes 835592 | tf_op jit(solution)/shard_map/ppermute | solution.py:285
  7.8 0.8 %shard_map.97 = (f32[128,512]{1,0:T(8,128)S(1)}, f32[128,512]{1,0:T(8,128)S(1)}, f32[128,512]{1,0:T(8,128)S(1)}, f32[128,512]{1,0:T(8,128)S(1)}) custom-call(f32[128,512]{1,0:T(8,128)S(1)} %get-tuple-element.29.keep_ref, f32[136,512]{1,0:T(8,128)S(1)} %get-tuple-element.28.send_ref), custom_call_target="tpu_custom_call" | custom-call | bytes 540672 | tf_op jit(solution)/shard_map/pallas_call | solution.py:258
  8.6 0.4 collective-permute-done.recv_ref
  9.0 0.8 %shard_map.98 = (f32[128,512]{1,0:T(8,128)S(1)}, f32[128,512]{1,0:T(8,128)S(1)}, f32[128,512]{1,0:T(8,128)S(1)}, f32[128,512]{1,0:T(8,128)S(1)}) custom-call(f32[136,512]{1,0:T(8,128)S(1)} %collective-permute-done.recv_ref, f32[128,512]{1,0:T(8,128)S(1)} %get-tuple-element.30.refs_0_, f32[128,512]{1,0:T(8,128)S(1)} %get-tuple-element.31.refs_1_, ...), custom_call_target="tpu_custom_call" | custom-call | bytes 1327104 | tf_op jit(solution)/shard_map/pallas_call | solution.py:258
  9.8 0.3 collective-permute-start.1
  10.1 0.0 collective-permute-start.2
  10.1 2.4 %collective-permute-start.3 = (f32[128,512]{1,0:T(8,128)S(1)}, f32[128,512]{1,0:T(8,128)S(1)}, u32[]{:S(2)}, u32[]{:S(2)}) collective-permute-start(f32[128,512]{1,0:T(8,128)S(1)} %get-tuple-element.37), channel_id=1, source_target_pairs={{0,12},{4,8},{8,4},{12,0},{1,13},{5,9},{9,5},{13,1},{2,14},{6,10},... | collective-permute-start | bytes 786440 | tf_op jit(solution)/shard_map/ppermute | solution.py:288
  12.5 4.9 %collective-permute-done.1.b_ref = f32[128,512]{1,0:T(8,128)S(1)} collective-permute-done((f32[128,512]{1,0:T(8,128)S(1)}, f32[128,512]{1,0:T(8,128)S(1)}, u32[]{:S(2)}, u32[]{:S(2)}) %collective-permute-start.1) | collective-permute-done | bytes 262176 | tf_op jit(solution)/shard_map/ppermute | solution.py:288
  17.4 5.5 %collective-permute-done.2.c_ref = f32[128,512]{1,0:T(8,128)S(1)} collective-permute-done((f32[128,512]{1,0:T(8,128)S(1)}, f32[128,512]{1,0:T(8,128)S(1)}, u32[]{:S(2)}, u32[]{:S(2)}) %collective-permute-start.2) | collective-permute-done | bytes 262176 | tf_op jit(solution)/shard_map/ppermute | solution.py:288
  22.9 0.0 collective-permute-done.3.d_ref
  22.9 0.1 shard_map.99
  23.0 1.0 %collective-permute-start.4 = (f32[64,512]{1,0:T(8,128)S(1)}, f32[64,512]{1,0:T(8,128)S(1)}, u32[]{:S(2)}, u32[]{:S(2)}) collective-permute-start(f32[64,512]{1,0:T(8,128)S(1)} %get-tuple-element.38.refs_1_), channel_id=1, source_target_pairs={{0,2},{3,1},{1,0},{2,3},{4,6},{7,5},{5,4},{6,7},{8,10},{11,9},{9,8... | collective-permute-start | bytes 393224 | tf_op jit(solution)/shard_map/ppermute | solution.py:293
  23.9 2.0 %collective-permute-start.6 = (f32[64,512]{1,0:T(8,128)S(1)}, f32[64,512]{1,0:T(8,128)S(1)}, u32[]{:S(2)}, u32[]{:S(2)}) collective-permute-start(f32[64,512]{1,0:T(8,128)S(1)} %get-tuple-element.39), channel_id=1, source_target_pairs={{1,2},{2,1},{0,0},{3,3},{5,6},{6,5},{4,4},{7,7},{9,10},{10,9},{8,8... | collective-permute-start | bytes 393224 | tf_op jit(solution)/shard_map/ppermute | solution.py:293
  26.0 0.1 collective-permute-start.5
  26.1 0.3 shard_map.96
  26.4 1.9 %collective-permute-done.8.sent_ref = f32[512,512]{1,0:T(8,128)S(1)} collective-permute-done((f32[512,512]{1,0:T(8,128)}, f32[512,512]{1,0:T(8,128)S(1)}, u32[]{:S(2)}, u32[]{:S(2)}) %collective-permute-start.8) | collective-permute-done | bytes 1048608 | tf_op jit(solution)/shard_map/ppermute | solution.py:306
  28.3 3.6 %collective-permute-start.9 = (f32[512,512]{1,0:T(8,128)S(1)}, f32[512,512]{1,0:T(8,128)S(1)}, u32[]{:S(2)}, u32[]{:S(2)}) collective-permute-start(f32[512,512]{1,0:T(8,128)S(1)} %collective-permute-done.8.sent_ref), channel_id=1, source_target_pairs={{0,16},{16,0},{1,17},{17,1},{2,18},{18,2},{3,19},{19,3},{4,20},{20... | collective-permute-start | bytes 3145736 | tf_op jit(solution)/shard_map/ppermute | solution.py:285
  31.9 0.0 collective-permute-done.4.refs_2_
  31.9 0.9 %collective-permute-done.6.refs_4_ = f32[64,512]{1,0:T(8,128)S(1)} collective-permute-done((f32[64,512]{1,0:T(8,128)S(1)}, f32[64,512]{1,0:T(8,128)S(1)}, u32[]{:S(2)}, u32[]{:S(2)}) %collective-permute-start.6) | collective-permute-done | bytes 131104 | tf_op jit(solution)/shard_map/ppermute | solution.py:293
  32.8 1.6 %collective-permute-done.5.refs_3_ = f32[64,512]{1,0:T(8,128)S(1)} collective-permute-done((f32[64,512]{1,0:T(8,128)S(1)}, f32[64,512]{1,0:T(8,128)S(1)}, u32[]{:S(2)}, u32[]{:S(2)}) %collective-permute-start.5) | collective-permute-done | bytes 131104 | tf_op jit(solution)/shard_map/ppermute | solution.py:293
  34.5 0.1 collective-permute-start.10
  34.6 0.2 collective-permute-start.7
  34.8 0.0 collective-permute-done.9.other_ref
  34.8 0.9 %copy-done = f32[512,512]{1,0:T(8,128)S(1)} copy-done((f32[512,512]{1,0:T(8,128)S(1)}, f32[512,512]{1,0:T(8,128)}, u32[]{:S(2)}) %copy-start) | copy-done | bytes 1048600
  35.7 1.0 %shard_map.101 = (bf16[512,512]{1,0:T(8,128)(2,1)S(1)}, bf16[512,512]{1,0:T(8,128)(2,1)S(1)}, bf16[512,512]{1,0:T(8,128)(2,1)S(1)}, bf16[512,512]{1,0:T(8,128)(2...) custom-call(f32[512,512]{1,0:T(8,128)S(1)} %copy-done, ...), custom_call_target="tpu_custom_call" | custom-call | bytes 3145728 | tf_op jit(solution)/shard_map/pallas_call | solution.py:258
  36.7 2.4 %collective-permute-done.10.refs_4_ = f32[64,512]{1,0:T(8,128)S(1)} collective-permute-done((f32[64,512]{1,0:T(8,128)S(1)}, f32[64,512]{1,0:T(8,128)S(1)}, u32[]{:S(2)}, u32[]{:S(2)}) %collective-permute-start.10) | collective-permute-done | bytes 131104 | tf_op jit(solution)/shard_map/ppermute | solution.py:288
  39.1 0.1 collective-permute-start.11
  39.2 0.0 collective-permute-done.7.refs_2_
  39.3 4.7 %collective-permute-done.11.refs_2_.refs_4_ = f32[64,512]{1,0:T(8,128)S(1)} collective-permute-done((f32[64,512]{1,0:T(8,128)S(1)}, f32[64,512]{1,0:T(8,128)S(1)}, u32[]{:S(2)}, u32[]{:S(2)}) %collective-permute-start.11) | collective-permute-done | bytes 131104 | tf_op jit(solution)/shard_map/ppermute | solution.py:288
  43.9 0.3 collective-permute-start.13
  44.3 0.4 collective-permute-start.12
  44.6 0.3 shard_map.104.refs_0_
  44.9 2.9 %collective-permute-done.13.refs_7_ = f32[64,512]{1,0:T(8,128)S(1)} collective-permute-done((f32[64,512]{1,0:T(8,128)S(1)}, f32[64,512]{1,0:T(8,128)S(1)}, u32[]{:S(2)}, u32[]{:S(2)}) %collective-permute-start.13) | collective-permute-done | bytes 131104 | tf_op jit(solution)/shard_map/ppermute | solution.py:288
  47.8 0.3 collective-permute-done.12.refs_4_
  48.1 0.7 %shard_map.106.x_ref = f32[64,512]{1,0:T(8,128)S(1)} custom-call(f32[64,512]{1,0:T(8,128)S(1)} %shard_map.104.refs_0_, f32[64,512]{1,0:T(8,128)S(1)} %shard_map.105.refs_1_, bf16[512,512]{1,0:T(8,128)(2,1)S(1)} %get-tuple-element.40.refs_5_.refs_2_, bf16[512,512]{1,0:T(8,128)(2,1)S(1)} %get-tuple-element.41.refs_6_.refs_3_, ...), custom_call_target="tpu_custom_call" | custom-call | bytes 6815744 | tf_op jit(solution)/shard_map/pallas_call | solution.py:258
  48.8 0.1 collective-permute-start.16
  48.9 1.5 %collective-permute-start.15 = (f32[64,512]{1,0:T(8,128)S(1)}, f32[64,512]{1,0:T(8,128)S(1)}, u32[]{:S(2)}, u32[]{:S(2)}) collective-permute-start(f32[64,512]{1,0:T(8,128)S(1)} %shard_map.106.x_ref), channel_id=1, source_target_pairs={{1,0},{2,3},{0,1},{3,2},{5,4},{6,7},{4,5},{7,6},{9,8},{10,11},{8,9... | collective-permute-start | bytes 393224 | tf_op jit(solution)/shard_map/ppermute | solution.py:293
  50.3 3.2 %collective-permute-start.14 = (f32[64,512]{1,0:T(8,128)S(1)}, f32[64,512]{1,0:T(8,128)S(1)}, u32[]{:S(2)}, u32[]{:S(2)}) collective-permute-start(f32[64,512]{1,0:T(8,128)S(1)} %shard_map.106.x_ref), channel_id=1, source_target_pairs={{1,2},{2,1},{0,0},{3,3},{5,6},{6,5},{4,4},{7,7},{9,10},{10,9},{8,8... | collective-permute-start | bytes 393224 | tf_op jit(solution)/shard_map/ppermute | solution.py:293
  53.5 0.0 collective-permute-done.16.c_ref
  53.5 0.5 collective-permute-done.15.a_ref
  54.1 2.8 %collective-permute-done.14.b_ref = f32[64,512]{1,0:T(8,128)S(1)} collective-permute-done((f32[64,512]{1,0:T(8,128)S(1)}, f32[64,512]{1,0:T(8,128)S(1)}, u32[]{:S(2)}, u32[]{:S(2)}) %collective-permute-start.14) | collective-permute-done | bytes 131104 | tf_op jit(solution)/shard_map/ppermute | solution.py:293
  56.9 0.1 shard_map.107.part_ref
  57.0 5.1 %collective-permute-start.17 = (f32[512,128]{1,0:T(8,128)S(1)}, f32[512,128]{1,0:T(8,128)S(1)}, u32[]{:S(2)}, u32[]{:S(2)}) collective-permute-start(f32[512,128]{1,0:T(8,128)S(1)} %shard_map.107.part_ref), channel_id=1, source_target_pairs={{0,16},{16,0},{1,17},{17,1},{2,18},{18,2},{3,19},{19,3},{4,20},{20... | collective-permute-start | bytes 786440 | tf_op jit(solution)/shard_map/ppermute | solution.py:285
  62.2 0.7 %shard_map.108.refs_0_ = f32[512,256]{1,0:T(8,128)} custom-call(f32[512,128]{1,0:T(8,128)S(1)} %shard_map.107.part_ref), custom_call_target="tpu_custom_call" | custom-call | bytes 262144 | tf_op jit(solution)/shard_map/pallas_call | solution.py:258
  62.9 0.4 collective-permute-done.17.part_ref
  63.4 0.7 %shard_map.109 = f32[512,256]{1,0:T(8,128)} custom-call(f32[512,128]{1,0:T(8,128)S(1)} %collective-permute-done.17.part_ref, f32[512,256]{1,0:T(8,128)} %shard_map.108.refs_0_), custom_call_target="tpu_custom_call", output_to_operand_aliasing={{}: (1, {})} | custom-call | bytes 786432 | tf_op jit(solution)/shard_map/pallas_call | solution.py:258
  (9 shorter events, 0.1 us)
Async XLA Ops:
  0.6 27.7 %collective-permute-start.8 = (f32[512,512]{1,0:T(8,128)}, f32[512,512]{1,0:T(8,128)S(1)}, u32[]{:S(2)}, u32[]{:S(2)}) collective-permute-start(f32[512,512]{1,0:T(8,128)} %own_ref.1), channel_id=1, source_target_pairs={{4,5},{8,9},{12,13},{9,10},{13,14},{20,22},{24,26},{28,30},{30,29}... | collective-permute-start | bytes 3145736 | tf_op jit(solution)/shard_map/ppermute | solution.py:306
  5.7 3.3 %collective-permute-start = (f32[136,512]{1,0:T(8,128)S(1)}, f32[136,512]{1,0:T(8,128)S(1)}, u32[]{:S(2)}, u32[]{:S(2)}) collective-permute-start(f32[136,512]{1,0:T(8,128)S(1)} %get-tuple-element.28.send_ref), channel_id=1, source_target_pairs={{0,16},{16,0},{1,17},{17,1},{2,18},{18,2},{3,19},{19,3},{4,20},{20... | collective-permute-start | bytes 835592 | tf_op jit(solution)/shard_map/ppermute | solution.py:285
  9.0 17.1 %copy-start.1 = (f32[512,512]{1,0:T(8,128)S(1)}, f32[512,512]{1,0:T(8,128)}, u32[]{:S(2)}) copy-start(f32[512,512]{1,0:T(8,128)} %diag_ref.1) | copy-start | bytes 3145732
  9.8 7.6 %collective-permute-start.1 = (f32[128,512]{1,0:T(8,128)S(1)}, f32[128,512]{1,0:T(8,128)S(1)}, u32[]{:S(2)}, u32[]{:S(2)}) collective-permute-start(f32[128,512]{1,0:T(8,128)S(1)} %get-tuple-element.35), channel_id=1, source_target_pairs={{0,4},{4,0},{8,12},{12,8},{1,5},{5,1},{9,13},{13,9},{2,6},{6,2},{1... | collective-permute-start | bytes 786440 | tf_op jit(solution)/shard_map/ppermute | solution.py:288
  10.1 12.8 %collective-permute-start.2 = (f32[128,512]{1,0:T(8,128)S(1)}, f32[128,512]{1,0:T(8,128)S(1)}, u32[]{:S(2)}, u32[]{:S(2)}) collective-permute-start(f32[128,512]{1,0:T(8,128)S(1)} %get-tuple-element.36), channel_id=1, source_target_pairs={{0,8},{4,12},{8,0},{12,4},{1,9},{5,13},{9,1},{13,5},{2,10},{6,14},... | collective-permute-start | bytes 786440 | tf_op jit(solution)/shard_map/ppermute | solution.py:288
  10.1 12.8 %collective-permute-start.3 = (f32[128,512]{1,0:T(8,128)S(1)}, f32[128,512]{1,0:T(8,128)S(1)}, u32[]{:S(2)}, u32[]{:S(2)}) collective-permute-start(f32[128,512]{1,0:T(8,128)S(1)} %get-tuple-element.37), channel_id=1, source_target_pairs={{0,12},{4,8},{8,4},{12,0},{1,13},{5,9},{9,5},{13,1},{2,14},{6,10},... | collective-permute-start | bytes 786440 | tf_op jit(solution)/shard_map/ppermute | solution.py:288
  22.9 3.2 %copy-start.2 = (f32[512,256]{1,0:T(8,128)S(1)}, f32[512,256]{1,0:T(8,128)}, u32[]{:S(2)}) copy-start(f32[512,256]{1,0:T(8,128)} %rhs_ref.1) | copy-start | bytes 1572868
  23.0 8.9 %collective-permute-start.4 = (f32[64,512]{1,0:T(8,128)S(1)}, f32[64,512]{1,0:T(8,128)S(1)}, u32[]{:S(2)}, u32[]{:S(2)}) collective-permute-start(f32[64,512]{1,0:T(8,128)S(1)} %get-tuple-element.38.refs_1_), channel_id=1, source_target_pairs={{0,2},{3,1},{1,0},{2,3},{4,6},{7,5},{5,4},{6,7},{8,10},{11,9},{9,8... | collective-permute-start | bytes 393224 | tf_op jit(solution)/shard_map/ppermute | solution.py:293
  23.9 8.9 %collective-permute-start.6 = (f32[64,512]{1,0:T(8,128)S(1)}, f32[64,512]{1,0:T(8,128)S(1)}, u32[]{:S(2)}, u32[]{:S(2)}) collective-permute-start(f32[64,512]{1,0:T(8,128)S(1)} %get-tuple-element.39), channel_id=1, source_target_pairs={{1,2},{2,1},{0,0},{3,3},{5,6},{6,5},{4,4},{7,7},{9,10},{10,9},{8,8... | collective-permute-start | bytes 393224 | tf_op jit(solution)/shard_map/ppermute | solution.py:293
  26.0 8.5 %collective-permute-start.5 = (f32[64,512]{1,0:T(8,128)S(1)}, f32[64,512]{1,0:T(8,128)S(1)}, u32[]{:S(2)}, u32[]{:S(2)}) collective-permute-start(f32[64,512]{1,0:T(8,128)S(1)} %get-tuple-element.39), channel_id=1, source_target_pairs={{0,1},{3,2},{1,0},{2,3},{4,5},{7,6},{5,4},{6,7},{8,9},{11,10},{9,8... | collective-permute-start | bytes 393224 | tf_op jit(solution)/shard_map/ppermute | solution.py:293
  28.3 6.5 %collective-permute-start.9 = (f32[512,512]{1,0:T(8,128)S(1)}, f32[512,512]{1,0:T(8,128)S(1)}, u32[]{:S(2)}, u32[]{:S(2)}) collective-permute-start(f32[512,512]{1,0:T(8,128)S(1)} %collective-permute-done.8.sent_ref), channel_id=1, source_target_pairs={{0,16},{16,0},{1,17},{17,1},{2,18},{18,2},{3,19},{19,3},{4,20},{20... | collective-permute-start | bytes 3145736 | tf_op jit(solution)/shard_map/ppermute | solution.py:285
  34.5 1.2 %copy-start = (f32[512,512]{1,0:T(8,128)S(1)}, f32[512,512]{1,0:T(8,128)}, u32[]{:S(2)}) copy-start(f32[512,512]{1,0:T(8,128)} %own_ref.1) | copy-start | bytes 3145732
  34.5 4.6 %collective-permute-start.10 = (f32[64,512]{1,0:T(8,128)S(1)}, f32[64,512]{1,0:T(8,128)S(1)}, u32[]{:S(2)}, u32[]{:S(2)}) collective-permute-start(f32[64,512]{1,0:T(8,128)S(1)} %get-tuple-element.43.refs_1_), channel_id=1, source_target_pairs={{0,4},{4,0},{8,12},{12,8},{1,5},{5,1},{9,13},{13,9},{2,6},{6,2},{1... | collective-permute-start | bytes 393224 | tf_op jit(solution)/shard_map/ppermute | solution.py:288
  34.6 4.7 %collective-permute-start.7 = (f32[64,512]{1,0:T(8,128)S(1)}, f32[64,512]{1,0:T(8,128)S(1)}, u32[]{:S(2)}, u32[]{:S(2)}) collective-permute-start(f32[64,512]{1,0:T(8,128)S(1)} %get-tuple-element.43.refs_1_), channel_id=1, source_target_pairs={{0,8},{4,12},{8,0},{12,4},{1,9},{5,13},{9,1},{13,5},{2,10},{6,14},... | collective-permute-start | bytes 393224 | tf_op jit(solution)/shard_map/ppermute | solution.py:288
  39.1 4.8 %collective-permute-start.11 = (f32[64,512]{1,0:T(8,128)S(1)}, f32[64,512]{1,0:T(8,128)S(1)}, u32[]{:S(2)}, u32[]{:S(2)}) collective-permute-start(f32[64,512]{1,0:T(8,128)S(1)} %shard_map.103.refs_1_), channel_id=1, source_target_pairs={{0,12},{4,8},{8,4},{12,0},{1,13},{5,9},{9,5},{13,1},{2,14},{6,10},... | collective-permute-start | bytes 393224 | tf_op jit(solution)/shard_map/ppermute | solution.py:288
  43.9 3.9 %collective-permute-start.13 = (f32[64,512]{1,0:T(8,128)S(1)}, f32[64,512]{1,0:T(8,128)S(1)}, u32[]{:S(2)}, u32[]{:S(2)}) collective-permute-start(f32[64,512]{1,0:T(8,128)S(1)} %shard_map.105.refs_1_), channel_id=1, source_target_pairs={{0,4},{4,0},{8,12},{12,8},{1,5},{5,1},{9,13},{13,9},{2,6},{6,2},{1... | collective-permute-start | bytes 393224 | tf_op jit(solution)/shard_map/ppermute | solution.py:288
  44.3 3.8 %collective-permute-start.12 = (f32[64,512]{1,0:T(8,128)S(1)}, f32[64,512]{1,0:T(8,128)S(1)}, u32[]{:S(2)}, u32[]{:S(2)}) collective-permute-start(f32[64,512]{1,0:T(8,128)S(1)} %shard_map.105.refs_1_), channel_id=1, source_target_pairs={{0,8},{4,12},{8,0},{12,4},{1,9},{5,13},{9,1},{13,5},{2,10},{6,14},... | collective-permute-start | bytes 393224 | tf_op jit(solution)/shard_map/ppermute | solution.py:288
  48.8 4.7 %collective-permute-start.16 = (f32[64,512]{1,0:T(8,128)S(1)}, f32[64,512]{1,0:T(8,128)S(1)}, u32[]{:S(2)}, u32[]{:S(2)}) collective-permute-start(f32[64,512]{1,0:T(8,128)S(1)} %shard_map.106.x_ref), channel_id=1, source_target_pairs={{1,3},{2,0},{0,1},{3,2},{5,7},{6,4},{4,5},{7,6},{9,11},{10,8},{8,9... | collective-permute-start | bytes 393224 | tf_op jit(solution)/shard_map/ppermute | solution.py:293
  48.9 5.2 %collective-permute-start.15 = (f32[64,512]{1,0:T(8,128)S(1)}, f32[64,512]{1,0:T(8,128)S(1)}, u32[]{:S(2)}, u32[]{:S(2)}) collective-permute-start(f32[64,512]{1,0:T(8,128)S(1)} %shard_map.106.x_ref), channel_id=1, source_target_pairs={{1,0},{2,3},{0,1},{3,2},{5,4},{6,7},{4,5},{7,6},{9,8},{10,11},{8,9... | collective-permute-start | bytes 393224 | tf_op jit(solution)/shard_map/ppermute | solution.py:293
  50.3 6.6 %collective-permute-start.14 = (f32[64,512]{1,0:T(8,128)S(1)}, f32[64,512]{1,0:T(8,128)S(1)}, u32[]{:S(2)}, u32[]{:S(2)}) collective-permute-start(f32[64,512]{1,0:T(8,128)S(1)} %shard_map.106.x_ref), channel_id=1, source_target_pairs={{1,2},{2,1},{0,0},{3,3},{5,6},{6,5},{4,4},{7,7},{9,10},{10,9},{8,8... | collective-permute-start | bytes 393224 | tf_op jit(solution)/shard_map/ppermute | solution.py:293
  57.0 6.3 %collective-permute-start.17 = (f32[512,128]{1,0:T(8,128)S(1)}, f32[512,128]{1,0:T(8,128)S(1)}, u32[]{:S(2)}, u32[]{:S(2)}) collective-permute-start(f32[512,128]{1,0:T(8,128)S(1)} %shard_map.107.part_ref), channel_id=1, source_target_pairs={{0,16},{16,0},{1,17},{17,1},{2,18},{18,2},{3,19},{19,3},{4,20},{20... | collective-permute-start | bytes 786440 | tf_op jit(solution)/shard_map/ppermute | solution.py:285

commit v12 on v11

--- a/solution.py
+++ b/solution.py
@@ -187,19 +187,29 @@
     second_ref[...] = sum_ref[pl.ds(pl.multiple_of((1 - odd) * piece, piece), piece), :]
 
 
-def factor_kernel(own_ref, sent_ref, other_ref, *out_refs):
+def factor_kernel(own_ref, near_ref, near_other_ref, on_ref, on_other_ref, *out_refs):
     leaf, row, z = place()
     for block in range(3):
         high_ref, low_ref = out_refs[2 * block], out_refs[2 * block + 1]
 
-        @pl.when((row > block) & ((z == 1) | (z == 2)))
+        def put(value):
+            high_ref[...], low_ref[...] = split(value.T)
+
+        @pl.when((row > block) & (z == 1))
+        def _():
+            if block == 1:
+                put(own_ref[...])
+            else:
+                put(jnp.where(leaf == block // 2, near_ref[...], near_other_ref[...]))
+
+        @pl.when((row > block) & (z == 2))
         def _():
             if block == 0:
-                value = jnp.where((leaf == 0) == (z == 1), sent_ref[...], other_ref[...])
+                put(jnp.where(leaf == 1, on_ref[...], on_other_ref[...]))
+            elif block == 1:
+                put(jnp.where(leaf == 0, near_ref[...], near_other_ref[...]))
             else:
-                sent = jnp.where((leaf == 0) == (block == 1), sent_ref[...], other_ref[...])
-                value = jnp.where(z == block, own_ref[...], sent)
-            high_ref[...], low_ref[...] = split(value.T)
+                put(own_ref[...])
 
 
 def chain_kernel(owner, has_sums, solves, *refs):
@@ -292,18 +302,23 @@
         open_ends = [b for b in range(cols) if b not in [p[1] for p in pairs]]
         return lax.ppermute(value, "col", pairs + list(zip(rest, open_ends)))
 
-    near = [(at(k, 0), at(k, 1)) for k in (1, 2, 3)] + [(at(k, 1), at(k, 2)) for k in (2, 3)]
-    far = [(at(k, 0), at(k, 2)) for k in (1, 2, 3)] + [(at(3, 2), at(3, 1))]
+    def plane(value, pairs):
+        groups = [[at(k, z) + leaf * rows * cols for leaf in (0, 1) for z in range(cols)] for k in range(rows)]
+        for here in groups:
+            rest = [a for a in here if a not in [p[0] for p in pairs]]
+            ends = [b for b in here if b not in [p[1] for p in pairs]]
+            stay = [a for a in rest if a in ends]
+            rest, ends = [a for a in rest if a not in stay], [b for b in ends if b not in stay]
+            pairs = pairs + [(a, a) for a in stay] + list(zip(rest, ends))
+        return lax.ppermute(value, ("leaf", "row", "col"), pairs)
+
     shift = rows * cols
-    pairs = near + [(a + shift, b + shift) for a, b in far]
-    for k in range(2 * rows):
-        here = range(k * cols, (k + 1) * cols)
-        rest = [a for a in here if a not in [p[0] for p in pairs]]
-        open_ends = [b for b in here if b not in [p[1] for p in pairs]]
-        stay = [a for a in rest if a in open_ends]
-        pairs = pairs + [(a, a) for a in stay]
-        pairs = pairs + list(zip([a for a in rest if a not in stay], [b for b in open_ends if b not in stay]))
-    sent = lax.ppermute(top_factor, ("leaf", "row", "col"), pairs)
+    near = plane(
+        top_factor,
+        [(at(k, 0), at(k, 1)) for k in (1, 2, 3)]
+        + [(at(k, 1), at(k, 2)) for k in (2, 3)]
+        + [(at(3, 2) + shift, at(3, 1) + shift)],
+    )
     child_sol, keep, send = call(
         child_kernel,
         [live, child_rhs, child_diag, child_off, targets],
@@ -322,7 +337,7 @@
         turn_kernel, [top_rhs, top_diag], [shape, block, block], [(half, size)]
     )
     diag = [diag_high, diag_low]
-    first, second = call(pieces_kernel, [sums[0]] + got, [shape] * 2, [(half, size)])
+    first, second = call(pieces_kernel, [sums[0]] + got, [shape] * 2, [(half, size)], flops=10 ** 11)
     q = [
         along_col(second, [(0, 2), (3, 1)]),
         along_col(first, [(0, 1), (3, 2)]),
@@ -336,7 +351,8 @@
         return outs if has_sums else outs[0]
 
     res, x = chain(0, [rhs_piece, second] + q + diag, has_sums=True, flops=10 ** 10)
-    factor = call(factor_kernel, [top_factor, sent, swap(sent)], [block] * 6)
+    on = plane(near, [(at(k, 1), at(k, 2) + shift) for k in (1, 2, 3)])
+    factor = call(factor_kernel, [top_factor, near, swap(near), on, swap(on)], [block] * 6)
     factor = [factor[0:2], factor[2:4], factor[4:6]]
     to1 = along_row(x, 1)
     to2 = along_row(x, 2)

time: 64.7 us -> 79.9 us (1.23)
  starting transfers between devices: 24.5 us -> 39.8 us
  local copies, waits for them, and re-layouts: 0.92 us -> 0.02 us
  waiting for transfers between devices: 29.2 us -> 30 us
    ppermute x1 -> x2, waiting for transfers between devices: 1.88 us -> 14.1 us  [plane(): return lax.ppermute(value, ('leaf', 'row', 'col'), pairs)]
    ppermute x3 -> x4, starting transfers between devices: 10.9 us -> 21.7 us  [swap(): return lax.ppermute(value, 'leaf', [(0, 1), (1, 0)])]
    ppermute x8, waiting for transfers between devices: 20.6 us -> 10.1 us  [along_row(): return lax.ppermute(value, 'row', [(r, r ^ step) for r in range(rows)])]
    ppermute x6, starting transfers between devices: 7.77 us -> 10.3 us  [along_col(): return lax.ppermute(value, 'col', pairs + list(zip(rest, open_ends)))]
    ppermute x6, waiting for transfers between devices: 5.9 us -> 3.52 us  [along_col(): return lax.ppermute(value, 'col', pairs + list(zip(rest, open_ends)))]
    ppermute x1 -> x2, starting transfers between devices: 2.08 us -> 3.92 us  [plane(): return lax.ppermute(value, ('leaf', 'row', 'col'), pairs)]
    ppermute x3 -> x4, waiting for transfers between devices: 0.86 us -> 2.22 us  [swap(): return lax.ppermute(value, 'leaf', [(0, 1), (1, 0)])]
    unnamed x6, local copies, waits for them, and re-layouts: 0.92 us -> 0.02 us
  transfers between devices with their start and end apart: 18 -> 20, of which waited for: 13 -> 11; matrix products, arithmetic and copies ran while one was open for 0% -> 0% of each run, Pallas kernels for 11% -> 9%
where the time goes in v12:
time: 79.9 us; the launch traced here: 79.3 us
  starting transfers between devices  39.8 us (50%)
  waiting for transfers between devices  30 us (38%)
  Pallas kernels  8.56 us (11%)
  between operations  0.93 us (1%)
    ppermute x4, starting transfers between devices, swap(): return lax.ppermute(value, 'leaf', [(0, 1), (1, 0)])  21.7 us
    ppermute x2, waiting for transfers between devices, plane(): return lax.ppermute(value, ('leaf', 'row', 'col'), pairs)  14.1 us
    ppermute x6, starting transfers between devices, along_col(): return lax.ppermute(value, 'col', pairs + list(zip(rest, open_ends)))  10.3 us
    ppermute x8, waiting for transfers between devices, along_row(): return lax.ppermute(value, 'row', [(r, r ^ step) for r in range(rows)])  10.1 us
    pallas_call x15, Pallas kernels, call(): pl.pallas_call(kernel, out_shape=[shape(i, out) for i, out in enumerate(o...  8.56 us
    ppermute x2, starting transfers between devices, plane(): return lax.ppermute(value, ('leaf', 'row', 'col'), pairs)  3.92 us
    ppermute x8, starting transfers between devices, along_row(): return lax.ppermute(value, 'row', [(r, r ^ step) for r in range(rows)])  3.86 us
    ppermute x6, waiting for transfers between devices, along_col(): return lax.ppermute(value, 'col', pairs + list(zip(rest, open_ends)))  3.52 us
  transfers between devices with their start and end apart: 20, of which 11 were waited for; matrix products, arithmetic and copies ran while one was open for 0% of the time, Pallas kernels for 9%

profile of v12, /device:TPU:15, one launch (start us, length us, event | category | flops | bytes accessed | tf_op | source)
XLA Modules:
  0.0 79.3 jit_solution(9137542934733214138)
XLA Ops:
  0.6 3.2 %collective-permute-start.8 = (f32[512,512]{1,0:T(8,128)}, f32[512,512]{1,0:T(8,128)S(1)}, u32[]{:S(2)}, u32[]{:S(2)}) collective-permute-start(f32[512,512]{1,0:T(8,128)} %own_ref.1), channel_id=1, source_target_pairs={{4,5},{8,9},{12,13},{9,10},{13,14},{30,29},{0,0},{1,1},{2,2},{3,3}... | collective-permute-start | bytes 3145736 | tf_op jit(solution)/shard_map/ppermute | solution.py:313
  3.8 2.9 %shard_map.95 = (f32[2,256,256]{2,1,0:T(8,128)}, f32[128,512]{1,0:T(8,128)S(1)}, f32[136,512]{1,0:T(8,128)S(1)}) custom-call(s32[2]{0:T(128)} %live_hbm.1, f32[2,256,256]{2,1,0:T(8,128)} %rhs_hbm.1, f32[2,256,256]{2,1,0:T(8,128)} %diag_hbm.1, f32[2,256,256]{2,1,0:T(8,128)} %off_hbm.1, s32[2,256]{1,0:T(2,128)} %tgt_hbm.1), custom_call_target="tpu_custom_call" | custom-call | bytes 1574920 | tf_op jit(solution)/shard_map/pallas_call | solution.py:268
  6.8 1.0 %collective-permute-start = (f32[136,512]{1,0:T(8,128)S(1)}, f32[136,512]{1,0:T(8,128)S(1)}, u32[]{:S(2)}, u32[]{:S(2)}) collective-permute-start(f32[136,512]{1,0:T(8,128)S(1)} %get-tuple-element.28.send_ref), channel_id=1, source_target_pairs={{0,16},{16,0},{1,17},{17,1},{2,18},{18,2},{3,19},{19,3},{4,20},{20... | collective-permute-start | bytes 835592 | tf_op jit(solution)/shard_map/ppermute | solution.py:295
  7.8 0.8 shard_map.97
  8.6 0.4 collective-permute-done.recv_ref
  9.0 0.8 shard_map.98
  9.8 0.3 collective-permute-start.1
  10.1 0.0 collective-permute-start.2
  10.1 2.4 %collective-permute-start.3 = (f32[128,512]{1,0:T(8,128)S(1)}, f32[128,512]{1,0:T(8,128)S(1)}, u32[]{:S(2)}, u32[]{:S(2)}) collective-permute-start(f32[128,512]{1,0:T(8,128)S(1)} %get-tuple-element.37), channel_id=1, source_target_pairs={{0,12},{4,8},{8,4},{12,0},{1,13},{5,9},{9,5},{13,1},{2,14},{6,10},... | collective-permute-start | bytes 786440 | tf_op jit(solution)/shard_map/ppermute | solution.py:298
  12.5 14.1 %collective-permute-done.8.near_ref = f32[512,512]{1,0:T(8,128)S(1)} collective-permute-done((f32[512,512]{1,0:T(8,128)}, f32[512,512]{1,0:T(8,128)S(1)}, u32[]{:S(2)}, u32[]{:S(2)}) %collective-permute-start.8) | collective-permute-done | bytes 1048608 | tf_op jit(solution)/shard_map/ppermute | solution.py:313
  26.6 0.7 collective-permute-start.10
  27.3 0.0 collective-permute-done.1.b_ref
  27.3 0.0 collective-permute-done.2.c_ref
  27.3 0.0 collective-permute-done.3.d_ref
  27.4 0.0 copy-start.1
  27.4 0.0 copy-start.2
  27.4 0.1 shard_map.99
  27.5 0.1 collective-permute-start.4
  27.5 5.5 %collective-permute-start.6 = (f32[64,512]{1,0:T(8,128)S(1)}, f32[64,512]{1,0:T(8,128)S(1)}, u32[]{:S(2)}, u32[]{:S(2)}) collective-permute-start(f32[64,512]{1,0:T(8,128)S(1)} %get-tuple-element.39), channel_id=1, source_target_pairs={{1,2},{2,1},{0,0},{3,3},{5,6},{6,5},{4,4},{7,7},{9,10},{10,9},{8,8... | collective-permute-start | bytes 393224 | tf_op jit(solution)/shard_map/ppermute | solution.py:303
  33.0 0.1 collective-permute-start.5
  33.1 0.3 shard_map.96
  33.5 0.1 collective-permute-start.9
  33.5 13.4 %collective-permute-start.11 = (f32[512,512]{1,0:T(8,128)S(1)}, f32[512,512]{1,0:T(8,128)S(1)}, u32[]{:S(2)}, u32[]{:S(2)}) collective-permute-start(f32[512,512]{1,0:T(8,128)S(1)} %collective-permute-done.10.on_ref), channel_id=1, source_target_pairs={{0,16},{16,0},{1,17},{17,1},{2,18},{18,2},{3,19},{19,3},{4,20},{20... | collective-permute-start | bytes 3145736 | tf_op jit(solution)/shard_map/ppermute | solution.py:295
  47.0 0.0 collective-permute-done.4.refs_2_
  47.0 0.7 collective-permute-done.6.refs_4_
  47.7 0.1 collective-permute-start.12
  47.8 0.1 collective-permute-start.7
  47.9 1.4 %collective-permute-done.11.on_other_ref = f32[512,512]{1,0:T(8,128)S(1)} collective-permute-done((f32[512,512]{1,0:T(8,128)S(1)}, f32[512,512]{1,0:T(8,128)S(1)}, u32[]{:S(2)}, u32[]{:S(2)}) %collective-permute-start.11) | collective-permute-done | bytes 1048608 | tf_op jit(solution)/shard_map/ppermute | solution.py:295
  49.3 1.0 %shard_map.101 = (bf16[512,512]{1,0:T(8,128)(2,1)S(1)}, bf16[512,512]{1,0:T(8,128)(2,1)S(1)}, bf16[512,512]{1,0:T(8,128)(2,1)S(1)}, bf16[512,512]{1,0:T(8,128)(2...) custom-call(f32[512,512]{1,0:T(8,128)S(1)} %copy-done, ...), custom_call_target="tpu_custom_call" | custom-call | bytes 5242880 | tf_op jit(solution)/shard_map/pallas_call | solution.py:268
  50.3 1.9 %collective-permute-done.12.refs_4_ = f32[64,512]{1,0:T(8,128)S(1)} collective-permute-done((f32[64,512]{1,0:T(8,128)S(1)}, f32[64,512]{1,0:T(8,128)S(1)}, u32[]{:S(2)}, u32[]{:S(2)}) %collective-permute-start.12) | collective-permute-done | bytes 131104 | tf_op jit(solution)/shard_map/ppermute | solution.py:298
  52.3 0.1 collective-permute-start.13
  52.4 4.7 %collective-permute-done.13.refs_2_.refs_4_ = f32[64,512]{1,0:T(8,128)S(1)} collective-permute-done((f32[64,512]{1,0:T(8,128)S(1)}, f32[64,512]{1,0:T(8,128)S(1)}, u32[]{:S(2)}, u32[]{:S(2)}) %collective-permute-start.13) | collective-permute-done | bytes 131104 | tf_op jit(solution)/shard_map/ppermute | solution.py:298
  57.1 0.9 %collective-permute-start.15 = (f32[64,512]{1,0:T(8,128)S(1)}, f32[64,512]{1,0:T(8,128)S(1)}, u32[]{:S(2)}, u32[]{:S(2)}) collective-permute-start(f32[64,512]{1,0:T(8,128)S(1)} %shard_map.105.refs_1_), channel_id=1, source_target_pairs={{0,4},{4,0},{8,12},{12,8},{1,5},{5,1},{9,13},{13,9},{2,6},{6,2},{1... | collective-permute-start | bytes 393224 | tf_op jit(solution)/shard_map/ppermute | solution.py:298
  58.0 0.0 collective-permute-start.14
  58.0 0.3 shard_map.104.refs_0_
  58.3 2.6 %collective-permute-done.15.refs_7_ = f32[64,512]{1,0:T(8,128)S(1)} collective-permute-done((f32[64,512]{1,0:T(8,128)S(1)}, f32[64,512]{1,0:T(8,128)S(1)}, u32[]{:S(2)}, u32[]{:S(2)}) %collective-permute-start.15) | collective-permute-done | bytes 131104 | tf_op jit(solution)/shard_map/ppermute | solution.py:298
  61.0 0.9 %collective-permute-done.14.refs_4_ = f32[64,512]{1,0:T(8,128)S(1)} collective-permute-done((f32[64,512]{1,0:T(8,128)S(1)}, f32[64,512]{1,0:T(8,128)S(1)}, u32[]{:S(2)}, u32[]{:S(2)}) %collective-permute-start.14) | collective-permute-done | bytes 131104 | tf_op jit(solution)/shard_map/ppermute | solution.py:298
  61.8 0.7 shard_map.106.x_ref
  62.6 0.1 collective-permute-start.18
  62.6 1.5 %collective-permute-start.17 = (f32[64,512]{1,0:T(8,128)S(1)}, f32[64,512]{1,0:T(8,128)S(1)}, u32[]{:S(2)}, u32[]{:S(2)}) collective-permute-start(f32[64,512]{1,0:T(8,128)S(1)} %shard_map.106.x_ref), channel_id=1, source_target_pairs={{1,0},{2,3},{0,1},{3,2},{5,4},{6,7},{4,5},{7,6},{9,8},{10,11},{8,9... | collective-permute-start | bytes 393224 | tf_op jit(solution)/shard_map/ppermute | solution.py:303
  64.1 3.2 %collective-permute-start.16 = (f32[64,512]{1,0:T(8,128)S(1)}, f32[64,512]{1,0:T(8,128)S(1)}, u32[]{:S(2)}, u32[]{:S(2)}) collective-permute-start(f32[64,512]{1,0:T(8,128)S(1)} %shard_map.106.x_ref), channel_id=1, source_target_pairs={{1,2},{2,1},{0,0},{3,3},{5,6},{6,5},{4,4},{7,7},{9,10},{10,9},{8,8... | collective-permute-start | bytes 393224 | tf_op jit(solution)/shard_map/ppermute | solution.py:303
  67.3 0.6 collective-permute-done.17.a_ref
  67.8 2.2 %collective-permute-done.16.b_ref = f32[64,512]{1,0:T(8,128)S(1)} collective-permute-done((f32[64,512]{1,0:T(8,128)S(1)}, f32[64,512]{1,0:T(8,128)S(1)}, u32[]{:S(2)}, u32[]{:S(2)}) %collective-permute-start.16) | collective-permute-done | bytes 131104 | tf_op jit(solution)/shard_map/ppermute | solution.py:303
  70.1 0.1 shard_map.107.part_ref
  70.2 7.2 %collective-permute-start.19 = (f32[512,128]{1,0:T(8,128)S(1)}, f32[512,128]{1,0:T(8,128)S(1)}, u32[]{:S(2)}, u32[]{:S(2)}) collective-permute-start(f32[512,128]{1,0:T(8,128)S(1)} %shard_map.107.part_ref), channel_id=1, source_target_pairs={{0,16},{16,0},{1,17},{17,1},{2,18},{18,2},{3,19},{19,3},{4,20},{20... | collective-permute-start | bytes 786440 | tf_op jit(solution)/shard_map/ppermute | solution.py:295
  77.4 0.7 shard_map.108.refs_0_
  78.1 0.4 collective-permute-done.19.part_ref
  78.5 0.7 shard_map.109
  (13 shorter events, 0.1 us)
Async XLA Ops:
  0.6 26.0 %collective-permute-start.8 = (f32[512,512]{1,0:T(8,128)}, f32[512,512]{1,0:T(8,128)S(1)}, u32[]{:S(2)}, u32[]{:S(2)}) collective-permute-start(f32[512,512]{1,0:T(8,128)} %own_ref.1), channel_id=1, source_target_pairs={{4,5},{8,9},{12,13},{9,10},{13,14},{30,29},{0,0},{1,1},{2,2},{3,3}... | collective-permute-start | bytes 3145736 | tf_op jit(solution)/shard_map/ppermute | solution.py:313
  6.8 2.2 %collective-permute-start = (f32[136,512]{1,0:T(8,128)S(1)}, f32[136,512]{1,0:T(8,128)S(1)}, u32[]{:S(2)}, u32[]{:S(2)}) collective-permute-start(f32[136,512]{1,0:T(8,128)S(1)} %get-tuple-element.28.send_ref), channel_id=1, source_target_pairs={{0,16},{16,0},{1,17},{17,1},{2,18},{18,2},{3,19},{19,3},{4,20},{20... | collective-permute-start | bytes 835592 | tf_op jit(solution)/shard_map/ppermute | solution.py:295
  9.8 17.6 %collective-permute-start.1 = (f32[128,512]{1,0:T(8,128)S(1)}, f32[128,512]{1,0:T(8,128)S(1)}, u32[]{:S(2)}, u32[]{:S(2)}) collective-permute-start(f32[128,512]{1,0:T(8,128)S(1)} %get-tuple-element.35), channel_id=1, source_target_pairs={{0,4},{4,0},{8,12},{12,8},{1,5},{5,1},{9,13},{13,9},{2,6},{6,2},{1... | collective-permute-start | bytes 786440 | tf_op jit(solution)/shard_map/ppermute | solution.py:298
  10.1 17.3 %collective-permute-start.2 = (f32[128,512]{1,0:T(8,128)S(1)}, f32[128,512]{1,0:T(8,128)S(1)}, u32[]{:S(2)}, u32[]{:S(2)}) collective-permute-start(f32[128,512]{1,0:T(8,128)S(1)} %get-tuple-element.36), channel_id=1, source_target_pairs={{0,8},{4,12},{8,0},{12,4},{1,9},{5,13},{9,1},{13,5},{2,10},{6,14},... | collective-permute-start | bytes 786440 | tf_op jit(solution)/shard_map/ppermute | solution.py:298
  10.1 17.3 %collective-permute-start.3 = (f32[128,512]{1,0:T(8,128)S(1)}, f32[128,512]{1,0:T(8,128)S(1)}, u32[]{:S(2)}, u32[]{:S(2)}) collective-permute-start(f32[128,512]{1,0:T(8,128)S(1)} %get-tuple-element.37), channel_id=1, source_target_pairs={{0,12},{4,8},{8,4},{12,0},{1,13},{5,9},{9,5},{13,1},{2,14},{6,10},... | collective-permute-start | bytes 786440 | tf_op jit(solution)/shard_map/ppermute | solution.py:298
  26.6 6.9 %collective-permute-start.10 = (f32[512,512]{1,0:T(8,128)S(1)}, f32[512,512]{1,0:T(8,128)S(1)}, u32[]{:S(2)}, u32[]{:S(2)}) collective-permute-start(f32[512,512]{1,0:T(8,128)S(1)} %collective-permute-done.8.near_ref), channel_id=1, source_target_pairs={{5,22},{9,26},{13,30},{0,0},{1,1},{2,2},{3,3},{16,16},{17,17},{18,... | collective-permute-start | bytes 3145736 | tf_op jit(solution)/shard_map/ppermute | solution.py:313
  27.4 5.8 %copy-start.1 = (f32[512,512]{1,0:T(8,128)S(1)}, f32[512,512]{1,0:T(8,128)}, u32[]{:S(2)}) copy-start(f32[512,512]{1,0:T(8,128)} %diag_ref.1) | copy-start | bytes 3145732
  27.4 5.8 %copy-start.2 = (f32[512,256]{1,0:T(8,128)S(1)}, f32[512,256]{1,0:T(8,128)}, u32[]{:S(2)}) copy-start(f32[512,256]{1,0:T(8,128)} %rhs_ref.1) | copy-start | bytes 1572868
  27.5 19.5 %collective-permute-start.4 = (f32[64,512]{1,0:T(8,128)S(1)}, f32[64,512]{1,0:T(8,128)S(1)}, u32[]{:S(2)}, u32[]{:S(2)}) collective-permute-start(f32[64,512]{1,0:T(8,128)S(1)} %get-tuple-element.38.refs_1_), channel_id=1, source_target_pairs={{0,2},{3,1},{1,0},{2,3},{4,6},{7,5},{5,4},{6,7},{8,10},{11,9},{9,8... | collective-permute-start | bytes 393224 | tf_op jit(solution)/shard_map/ppermute | solution.py:303
  27.5 20.2 %collective-permute-start.6 = (f32[64,512]{1,0:T(8,128)S(1)}, f32[64,512]{1,0:T(8,128)S(1)}, u32[]{:S(2)}, u32[]{:S(2)}) collective-permute-start(f32[64,512]{1,0:T(8,128)S(1)} %get-tuple-element.39), channel_id=1, source_target_pairs={{1,2},{2,1},{0,0},{3,3},{5,6},{6,5},{4,4},{7,7},{9,10},{10,9},{8,8... | collective-permute-start | bytes 393224 | tf_op jit(solution)/shard_map/ppermute | solution.py:303
  33.0 14.7 %collective-permute-start.5 = (f32[64,512]{1,0:T(8,128)S(1)}, f32[64,512]{1,0:T(8,128)S(1)}, u32[]{:S(2)}, u32[]{:S(2)}) collective-permute-start(f32[64,512]{1,0:T(8,128)S(1)} %get-tuple-element.39), channel_id=1, source_target_pairs={{0,1},{3,2},{1,0},{2,3},{4,5},{7,6},{5,4},{6,7},{8,9},{11,10},{9,8... | collective-permute-start | bytes 393224 | tf_op jit(solution)/shard_map/ppermute | solution.py:303
  33.5 14.4 %collective-permute-start.9 = (f32[512,512]{1,0:T(8,128)S(1)}, f32[512,512]{1,0:T(8,128)S(1)}, u32[]{:S(2)}, u32[]{:S(2)}) collective-permute-start(f32[512,512]{1,0:T(8,128)S(1)} %collective-permute-done.8.near_ref), channel_id=1, source_target_pairs={{0,16},{16,0},{1,17},{17,1},{2,18},{18,2},{3,19},{19,3},{4,20},{20... | collective-permute-start | bytes 3145736 | tf_op jit(solution)/shard_map/ppermute | solution.py:295
  33.5 15.7 %collective-permute-start.11 = (f32[512,512]{1,0:T(8,128)S(1)}, f32[512,512]{1,0:T(8,128)S(1)}, u32[]{:S(2)}, u32[]{:S(2)}) collective-permute-start(f32[512,512]{1,0:T(8,128)S(1)} %collective-permute-done.10.on_ref), channel_id=1, source_target_pairs={{0,16},{16,0},{1,17},{17,1},{2,18},{18,2},{3,19},{19,3},{4,20},{20... | collective-permute-start | bytes 3145736 | tf_op jit(solution)/shard_map/ppermute | solution.py:295
  47.7 1.6 %copy-start = (f32[512,512]{1,0:T(8,128)S(1)}, f32[512,512]{1,0:T(8,128)}, u32[]{:S(2)}) copy-start(f32[512,512]{1,0:T(8,128)} %own_ref.1) | copy-start | bytes 3145732
  47.7 4.5 %collective-permute-start.12 = (f32[64,512]{1,0:T(8,128)S(1)}, f32[64,512]{1,0:T(8,128)S(1)}, u32[]{:S(2)}, u32[]{:S(2)}) collective-permute-start(f32[64,512]{1,0:T(8,128)S(1)} %get-tuple-element.43.refs_1_), channel_id=1, source_target_pairs={{0,4},{4,0},{8,12},{12,8},{1,5},{5,1},{9,13},{13,9},{2,6},{6,2},{1... | collective-permute-start | bytes 393224 | tf_op jit(solution)/shard_map/ppermute | solution.py:298
  47.8 4.6 %collective-permute-start.7 = (f32[64,512]{1,0:T(8,128)S(1)}, f32[64,512]{1,0:T(8,128)S(1)}, u32[]{:S(2)}, u32[]{:S(2)}) collective-permute-start(f32[64,512]{1,0:T(8,128)S(1)} %get-tuple-element.43.refs_1_), channel_id=1, source_target_pairs={{0,8},{4,12},{8,0},{12,4},{1,9},{5,13},{9,1},{13,5},{2,10},{6,14},... | collective-permute-start | bytes 393224 | tf_op jit(solution)/shard_map/ppermute | solution.py:298
  52.3 4.8 %collective-permute-start.13 = (f32[64,512]{1,0:T(8,128)S(1)}, f32[64,512]{1,0:T(8,128)S(1)}, u32[]{:S(2)}, u32[]{:S(2)}) collective-permute-start(f32[64,512]{1,0:T(8,128)S(1)} %shard_map.103.refs_1_), channel_id=1, source_target_pairs={{0,12},{4,8},{8,4},{12,0},{1,13},{5,9},{9,5},{13,1},{2,14},{6,10},... | collective-permute-start | bytes 393224 | tf_op jit(solution)/shard_map/ppermute | solution.py:298
  57.1 3.9 %collective-permute-start.15 = (f32[64,512]{1,0:T(8,128)S(1)}, f32[64,512]{1,0:T(8,128)S(1)}, u32[]{:S(2)}, u32[]{:S(2)}) collective-permute-start(f32[64,512]{1,0:T(8,128)S(1)} %shard_map.105.refs_1_), channel_id=1, source_target_pairs={{0,4},{4,0},{8,12},{12,8},{1,5},{5,1},{9,13},{13,9},{2,6},{6,2},{1... | collective-permute-start | bytes 393224 | tf_op jit(solution)/shard_map/ppermute | solution.py:298
  58.0 3.8 %collective-permute-start.14 = (f32[64,512]{1,0:T(8,128)S(1)}, f32[64,512]{1,0:T(8,128)S(1)}, u32[]{:S(2)}, u32[]{:S(2)}) collective-permute-start(f32[64,512]{1,0:T(8,128)S(1)} %shard_map.105.refs_1_), channel_id=1, source_target_pairs={{0,8},{4,12},{8,0},{12,4},{1,9},{5,13},{9,1},{13,5},{2,10},{6,14},... | collective-permute-start | bytes 393224 | tf_op jit(solution)/shard_map/ppermute | solution.py:298
  62.6 4.7 %collective-permute-start.18 = (f32[64,512]{1,0:T(8,128)S(1)}, f32[64,512]{1,0:T(8,128)S(1)}, u32[]{:S(2)}, u32[]{:S(2)}) collective-permute-start(f32[64,512]{1,0:T(8,128)S(1)} %shard_map.106.x_ref), channel_id=1, source_target_pairs={{1,3},{2,0},{0,1},{3,2},{5,7},{6,4},{4,5},{7,6},{9,11},{10,8},{8,9... | collective-permute-start | bytes 393224 | tf_op jit(solution)/shard_map/ppermute | solution.py:303
  62.6 5.2 %collective-permute-start.17 = (f32[64,512]{1,0:T(8,128)S(1)}, f32[64,512]{1,0:T(8,128)S(1)}, u32[]{:S(2)}, u32[]{:S(2)}) collective-permute-start(f32[64,512]{1,0:T(8,128)S(1)} %shard_map.106.x_ref), channel_id=1, source_target_pairs={{1,0},{2,3},{0,1},{3,2},{5,4},{6,7},{4,5},{7,6},{9,8},{10,11},{8,9... | collective-permute-start | bytes 393224 | tf_op jit(solution)/shard_map/ppermute | solution.py:303
  64.1 6.0 %collective-permute-start.16 = (f32[64,512]{1,0:T(8,128)S(1)}, f32[64,512]{1,0:T(8,128)S(1)}, u32[]{:S(2)}, u32[]{:S(2)}) collective-permute-start(f32[64,512]{1,0:T(8,128)S(1)} %shard_map.106.x_ref), channel_id=1, source_target_pairs={{1,2},{2,1},{0,0},{3,3},{5,6},{6,5},{4,4},{7,7},{9,10},{10,9},{8,8... | collective-permute-start | bytes 393224 | tf_op jit(solution)/shard_map/ppermute | solution.py:303
  70.2 8.3 %collective-permute-start.19 = (f32[512,128]{1,0:T(8,128)S(1)}, f32[512,128]{1,0:T(8,128)S(1)}, u32[]{:S(2)}, u32[]{:S(2)}) collective-permute-start(f32[512,128]{1,0:T(8,128)S(1)} %shard_map.107.part_ref), channel_id=1, source_target_pairs={{0,16},{16,0},{1,17},{17,1},{2,18},{18,2},{3,19},{19,3},{4,20},{20... | collective-permute-start | bytes 786440 | tf_op jit(solution)/shard_map/ppermute | solution.py:295

commit v13 on v12

--- a/solution.py
+++ b/solution.py
@@ -302,22 +302,28 @@
         open_ends = [b for b in range(cols) if b not in [p[1] for p in pairs]]
         return lax.ppermute(value, "col", pairs + list(zip(rest, open_ends)))
 
-    def plane(value, pairs):
-        groups = [[at(k, z) + leaf * rows * cols for leaf in (0, 1) for z in range(cols)] for k in range(rows)]
-        for here in groups:
+    def filled(pairs):
+        for k in range(rows):
+            here = [at(k, z) + leaf * shift for leaf in (0, 1) for z in range(cols)]
             rest = [a for a in here if a not in [p[0] for p in pairs]]
             ends = [b for b in here if b not in [p[1] for p in pairs]]
-            stay = [a for a in rest if a in ends]
-            rest, ends = [a for a in rest if a not in stay], [b for b in ends if b not in stay]
-            pairs = pairs + [(a, a) for a in stay] + list(zip(rest, ends))
+            for a in sorted(rest, key=lambda a: a not in ends):
+                b = min(ends, key=lambda b: (a != b, abs(a % cols - b % cols)))
+                ends.remove(b)
+                pairs = pairs + [(a, b)]
+        return pairs
+
+    def everywhere(value, pairs):
         return lax.ppermute(value, ("leaf", "row", "col"), pairs)
 
     shift = rows * cols
-    near = plane(
+    near = everywhere(
         top_factor,
-        [(at(k, 0), at(k, 1)) for k in (1, 2, 3)]
-        + [(at(k, 1), at(k, 2)) for k in (2, 3)]
-        + [(at(3, 2) + shift, at(3, 1) + shift)],
+        filled(
+            [(at(k, 0), at(k, 1)) for k in (1, 2, 3)]
+            + [(at(k, 1), at(k, 2)) for k in (2, 3)]
+            + [(at(3, 2) + shift, at(3, 1) + shift)]
+        ),
     )
     child_sol, keep, send = call(
         child_kernel,
@@ -351,7 +357,7 @@
         return outs if has_sums else outs[0]
 
     res, x = chain(0, [rhs_piece, second] + q + diag, has_sums=True, flops=10 ** 10)
-    on = plane(near, [(at(k, 1), at(k, 2) + shift) for k in (1, 2, 3)])
+    on = everywhere(near, [(at(k, 1), at(k, 2) + shift) for k in (1, 2, 3)])
     factor = call(factor_kernel, [top_factor, near, swap(near), on, swap(on)], [block] * 6)
     factor = [factor[0:2], factor[2:4], factor[4:6]]
     to1 = along_row(x, 1)

time: 79.9 us -> 68.9 us (0.86)
  waiting for transfers between devices: 30 us -> 24.4 us
  starting transfers between devices: 39.8 us -> 34.4 us
    ppermute x2, waiting for transfers between devices: 14.1 us -> 4.2 us  [everywhere(): return lax.ppermute(value, ('leaf', 'row', 'col'), pairs)]
    ppermute x8, waiting for transfers between devices: 10.1 us -> 14.2 us  [along_row(): return lax.ppermute(value, 'row', [(r, r ^ step) for r in range(rows)])]
    ppermute x4, starting transfers between devices: 21.7 us -> 18.4 us  [swap(): return lax.ppermute(value, 'leaf', [(0, 1), (1, 0)])]
    ppermute x6, starting transfers between devices: 10.3 us -> 8.61 us  [along_col(): return lax.ppermute(value, 'col', pairs + list(zip(rest, open_ends)))]
  transfers between devices with their start and end apart: 20 -> 20, of which waited for: 11 -> 11; matrix products, arithmetic and copies ran while one was open for 0% -> 0% of each run, Pallas kernels for 9% -> 10%
where the time goes in v13:
time: 68.9 us; the launch traced here: 68.2 us
  starting transfers between devices  34.4 us (50%)
  waiting for transfers between devices  24.4 us (35%)
  Pallas kernels  8.55 us (12%)
  between operations  0.86 us (1%)
    ppermute x4, starting transfers between devices, swap(): return lax.ppermute(value, 'leaf', [(0, 1), (1, 0)])  18.4 us
    ppermute x8, waiting for transfers between devices, along_row(): return lax.ppermute(value, 'row', [(r, r ^ step) for r in range(rows)])  14.2 us
    ppermute x6, starting transfers between devices, along_col(): return lax.ppermute(value, 'col', pairs + list(zip(rest, open_ends)))  8.61 us
    pallas_call x15, Pallas kernels, call(): pl.pallas_call(kernel, out_shape=[shape(i, out) for i, out in enumerate(o...  8.55 us
    ppermute x2, waiting for transfers between devices, everywhere(): return lax.ppermute(value, ('leaf', 'row', 'col'), pairs)  4.2 us
    ppermute x8, starting transfers between devices, along_row(): return lax.ppermute(value, 'row', [(r, r ^ step) for r in range(rows)])  4.06 us
    ppermute x2, starting transfers between devices, everywhere(): return lax.ppermute(value, ('leaf', 'row', 'col'), pairs)  3.36 us
    ppermute x6, waiting for transfers between devices, along_col(): return lax.ppermute(value, 'col', pairs + list(zip(rest, open_ends)))  3.25 us
  transfers between devices with their start and end apart: 20, of which 11 were waited for; matrix products, arithmetic and copies ran while one was open for 0% of the time, Pallas kernels for 10%

profile of v13, /device:TPU:15, one launch (start us, length us, event | category | flops | bytes accessed | tf_op | source)
XLA Modules:
  0.0 68.2 jit_solution(14387958469887087981)
XLA Ops:
  0.6 2.6 %collective-permute-start.8 = (f32[512,512]{1,0:T(8,128)}, f32[512,512]{1,0:T(8,128)S(1)}, u32[]{:S(2)}, u32[]{:S(2)}) collective-permute-start(f32[512,512]{1,0:T(8,128)} %own_ref.1), channel_id=1, source_target_pairs={{4,5},{8,9},{12,13},{9,10},{13,14},{30,29},{0,0},{1,1},{2,2},{3,3}... | collective-permute-start | bytes 3145736 | tf_op jit(solution)/shard_map/ppermute | solution.py:317
  3.3 2.9 %shard_map.95 = (f32[2,256,256]{2,1,0:T(8,128)}, f32[128,512]{1,0:T(8,128)S(1)}, f32[136,512]{1,0:T(8,128)S(1)}) custom-call(s32[2]{0:T(128)} %live_hbm.1, f32[2,256,256]{2,1,0:T(8,128)} %rhs_hbm.1, f32[2,256,256]{2,1,0:T(8,128)} %diag_hbm.1, f32[2,256,256]{2,1,0:T(8,128)} %off_hbm.1, s32[2,256]{1,0:T(2,128)} %tgt_hbm.1), custom_call_target="tpu_custom_call" | custom-call | bytes 1574920 | tf_op jit(solution)/shard_map/pallas_call | solution.py:268
  6.2 1.6 %collective-permute-start = (f32[136,512]{1,0:T(8,128)S(1)}, f32[136,512]{1,0:T(8,128)S(1)}, u32[]{:S(2)}, u32[]{:S(2)}) collective-permute-start(f32[136,512]{1,0:T(8,128)S(1)} %get-tuple-element.28.send_ref), channel_id=1, source_target_pairs={{0,16},{16,0},{1,17},{17,1},{2,18},{18,2},{3,19},{19,3},{4,20},{20... | collective-permute-start | bytes 835592 | tf_op jit(solution)/shard_map/ppermute | solution.py:295
  7.8 0.8 %shard_map.97 = (f32[128,512]{1,0:T(8,128)S(1)}, f32[128,512]{1,0:T(8,128)S(1)}, f32[128,512]{1,0:T(8,128)S(1)}, f32[128,512]{1,0:T(8,128)S(1)}) custom-call(f32[128,512]{1,0:T(8,128)S(1)} %get-tuple-element.29.keep_ref, f32[136,512]{1,0:T(8,128)S(1)} %get-tuple-element.28.send_ref), custom_call_target="tpu_custom_call" | custom-call | bytes 540672 | tf_op jit(solution)/shard_map/pallas_call | solution.py:268
  8.6 0.4 collective-permute-done.recv_ref
  9.0 0.8 %shard_map.98 = (f32[128,512]{1,0:T(8,128)S(1)}, f32[128,512]{1,0:T(8,128)S(1)}, f32[128,512]{1,0:T(8,128)S(1)}, f32[128,512]{1,0:T(8,128)S(1)}) custom-call(f32[136,512]{1,0:T(8,128)S(1)} %collective-permute-done.recv_ref, f32[128,512]{1,0:T(8,128)S(1)} %get-tuple-element.30.refs_0_, f32[128,512]{1,0:T(8,128)S(1)} %get-tuple-element.31.refs_1_, ...), custom_call_target="tpu_custom_call" | custom-call | bytes 1327104 | tf_op jit(solution)/shard_map/pallas_call | solution.py:268
  9.8 0.3 collective-permute-start.1
  10.1 0.0 collective-permute-start.2
  10.1 2.4 %collective-permute-start.3 = (f32[128,512]{1,0:T(8,128)S(1)}, f32[128,512]{1,0:T(8,128)S(1)}, u32[]{:S(2)}, u32[]{:S(2)}) collective-permute-start(f32[128,512]{1,0:T(8,128)S(1)} %get-tuple-element.37), channel_id=1, source_target_pairs={{0,12},{4,8},{8,4},{12,0},{1,13},{5,9},{9,5},{13,1},{2,14},{6,10},... | collective-permute-start | bytes 786440 | tf_op jit(solution)/shard_map/ppermute | solution.py:298
  12.5 4.2 %collective-permute-done.8.near_ref = f32[512,512]{1,0:T(8,128)S(1)} collective-permute-done((f32[512,512]{1,0:T(8,128)}, f32[512,512]{1,0:T(8,128)S(1)}, u32[]{:S(2)}, u32[]{:S(2)}) %collective-permute-start.8) | collective-permute-done | bytes 1048608 | tf_op jit(solution)/shard_map/ppermute | solution.py:317
  16.7 0.7 %collective-permute-start.10 = (f32[512,512]{1,0:T(8,128)S(1)}, f32[512,512]{1,0:T(8,128)S(1)}, u32[]{:S(2)}, u32[]{:S(2)}) collective-permute-start(f32[512,512]{1,0:T(8,128)S(1)} %collective-permute-done.8.near_ref), channel_id=1, source_target_pairs={{5,22},{9,26},{13,30}} | collective-permute-start | bytes 3145736 | tf_op jit(solution)/shard_map/ppermute | solution.py:317
  17.4 0.0 collective-permute-done.1.b_ref
  17.4 5.5 %collective-permute-done.2.c_ref = f32[128,512]{1,0:T(8,128)S(1)} collective-permute-done((f32[128,512]{1,0:T(8,128)S(1)}, f32[128,512]{1,0:T(8,128)S(1)}, u32[]{:S(2)}, u32[]{:S(2)}) %collective-permute-start.2) | collective-permute-done | bytes 262176 | tf_op jit(solution)/shard_map/ppermute | solution.py:298
  22.9 0.0 collective-permute-done.3.d_ref
  22.9 0.1 shard_map.99
  23.0 0.3 collective-permute-start.4
  23.3 2.7 %collective-permute-start.6 = (f32[64,512]{1,0:T(8,128)S(1)}, f32[64,512]{1,0:T(8,128)S(1)}, u32[]{:S(2)}, u32[]{:S(2)}) collective-permute-start(f32[64,512]{1,0:T(8,128)S(1)} %get-tuple-element.39), channel_id=1, source_target_pairs={{1,2},{2,1},{0,0},{3,3},{5,6},{6,5},{4,4},{7,7},{9,10},{10,9},{8,8... | collective-permute-start | bytes 393224 | tf_op jit(solution)/shard_map/ppermute | solution.py:303
  26.0 0.1 collective-permute-start.5
  26.1 0.3 shard_map.96
  26.4 2.1 %collective-permute-start.9 = (f32[512,512]{1,0:T(8,128)S(1)}, f32[512,512]{1,0:T(8,128)S(1)}, u32[]{:S(2)}, u32[]{:S(2)}) collective-permute-start(f32[512,512]{1,0:T(8,128)S(1)} %collective-permute-done.8.near_ref), channel_id=1, source_target_pairs={{0,16},{16,0},{1,17},{17,1},{2,18},{18,2},{3,19},{19,3},{4,20},{20... | collective-permute-start | bytes 3145736 | tf_op jit(solution)/shard_map/ppermute | solution.py:295
  28.5 7.5 %collective-permute-start.11 = (f32[512,512]{1,0:T(8,128)S(1)}, f32[512,512]{1,0:T(8,128)S(1)}, u32[]{:S(2)}, u32[]{:S(2)}) collective-permute-start(f32[512,512]{1,0:T(8,128)S(1)} %collective-permute-done.10.on_ref), channel_id=1, source_target_pairs={{0,16},{16,0},{1,17},{17,1},{2,18},{18,2},{3,19},{19,3},{4,20},{20... | collective-permute-start | bytes 3145736 | tf_op jit(solution)/shard_map/ppermute | solution.py:295
  36.0 0.0 collective-permute-done.4.refs_2_
  36.0 0.0 copy-start
  36.1 0.3 collective-permute-start.12
  36.4 0.1 collective-permute-start.7
  36.5 0.0 collective-permute-done.9.near_other_ref
  36.5 1.8 %collective-permute-done.11.on_other_ref = f32[512,512]{1,0:T(8,128)S(1)} collective-permute-done((f32[512,512]{1,0:T(8,128)S(1)}, f32[512,512]{1,0:T(8,128)S(1)}, u32[]{:S(2)}, u32[]{:S(2)}) %collective-permute-start.11) | collective-permute-done | bytes 1048608 | tf_op jit(solution)/shard_map/ppermute | solution.py:295
  38.3 1.0 %shard_map.101 = (bf16[512,512]{1,0:T(8,128)(2,1)S(1)}, bf16[512,512]{1,0:T(8,128)(2,1)S(1)}, bf16[512,512]{1,0:T(8,128)(2,1)S(1)}, bf16[512,512]{1,0:T(8,128)(2...) custom-call(f32[512,512]{1,0:T(8,128)S(1)} %copy-done, ...), custom_call_target="tpu_custom_call" | custom-call | bytes 5242880 | tf_op jit(solution)/shard_map/pallas_call | solution.py:268
  39.4 0.6 collective-permute-done.12.refs_4_
  40.0 0.1 collective-permute-start.13
  40.1 0.2 collective-permute-done.7.refs_2_
  40.2 4.5 %collective-permute-done.13.refs_2_.refs_4_ = f32[64,512]{1,0:T(8,128)S(1)} collective-permute-done((f32[64,512]{1,0:T(8,128)S(1)}, f32[64,512]{1,0:T(8,128)S(1)}, u32[]{:S(2)}, u32[]{:S(2)}) %collective-permute-start.13) | collective-permute-done | bytes 131104 | tf_op jit(solution)/shard_map/ppermute | solution.py:298
  44.8 0.9 %collective-permute-start.15 = (f32[64,512]{1,0:T(8,128)S(1)}, f32[64,512]{1,0:T(8,128)S(1)}, u32[]{:S(2)}, u32[]{:S(2)}) collective-permute-start(f32[64,512]{1,0:T(8,128)S(1)} %shard_map.105.refs_1_), channel_id=1, source_target_pairs={{0,4},{4,0},{8,12},{12,8},{1,5},{5,1},{9,13},{13,9},{2,6},{6,2},{1... | collective-permute-start | bytes 393224 | tf_op jit(solution)/shard_map/ppermute | solution.py:298
  45.6 0.1 collective-permute-start.14
  45.7 0.3 shard_map.104.refs_0_
  46.0 2.7 %collective-permute-done.15.refs_7_ = f32[64,512]{1,0:T(8,128)S(1)} collective-permute-done((f32[64,512]{1,0:T(8,128)S(1)}, f32[64,512]{1,0:T(8,128)S(1)}, u32[]{:S(2)}, u32[]{:S(2)}) %collective-permute-start.15) | collective-permute-done | bytes 131104 | tf_op jit(solution)/shard_map/ppermute | solution.py:298
  48.7 0.7 %collective-permute-done.14.refs_4_ = f32[64,512]{1,0:T(8,128)S(1)} collective-permute-done((f32[64,512]{1,0:T(8,128)S(1)}, f32[64,512]{1,0:T(8,128)S(1)}, u32[]{:S(2)}, u32[]{:S(2)}) %collective-permute-start.14) | collective-permute-done | bytes 131104 | tf_op jit(solution)/shard_map/ppermute | solution.py:298
  49.5 0.7 %shard_map.106.x_ref = f32[64,512]{1,0:T(8,128)S(1)} custom-call(f32[64,512]{1,0:T(8,128)S(1)} %shard_map.104.refs_0_, f32[64,512]{1,0:T(8,128)S(1)} %shard_map.105.refs_1_, bf16[512,512]{1,0:T(8,128)(2,1)S(1)} %get-tuple-element.40.refs_5_.refs_2_, bf16[512,512]{1,0:T(8,128)(2,1)S(1)} %get-tuple-element.41.refs_6_.refs_3_, ...), custom_call_target="tpu_custom_call" | custom-call | bytes 6815744 | tf_op jit(solution)/shard_map/pallas_call | solution.py:268
  50.2 0.1 collective-permute-start.18
  50.3 1.5 %collective-permute-start.17 = (f32[64,512]{1,0:T(8,128)S(1)}, f32[64,512]{1,0:T(8,128)S(1)}, u32[]{:S(2)}, u32[]{:S(2)}) collective-permute-start(f32[64,512]{1,0:T(8,128)S(1)} %shard_map.106.x_ref), channel_id=1, source_target_pairs={{1,0},{2,3},{0,1},{3,2},{5,4},{6,7},{4,5},{7,6},{9,8},{10,11},{8,9... | collective-permute-start | bytes 393224 | tf_op jit(solution)/shard_map/ppermute | solution.py:303
  51.7 4.0 %collective-permute-start.16 = (f32[64,512]{1,0:T(8,128)S(1)}, f32[64,512]{1,0:T(8,128)S(1)}, u32[]{:S(2)}, u32[]{:S(2)}) collective-permute-start(f32[64,512]{1,0:T(8,128)S(1)} %shard_map.106.x_ref), channel_id=1, source_target_pairs={{1,2},{2,1},{0,0},{3,3},{5,6},{6,5},{4,4},{7,7},{9,10},{10,9},{8,8... | collective-permute-start | bytes 393224 | tf_op jit(solution)/shard_map/ppermute | solution.py:303
  55.8 0.0 collective-permute-done.17.a_ref
  55.8 3.2 %collective-permute-done.16.b_ref = f32[64,512]{1,0:T(8,128)S(1)} collective-permute-done((f32[64,512]{1,0:T(8,128)S(1)}, f32[64,512]{1,0:T(8,128)S(1)}, u32[]{:S(2)}, u32[]{:S(2)}) %collective-permute-start.16) | collective-permute-done | bytes 131104 | tf_op jit(solution)/shard_map/ppermute | solution.py:303
  59.0 0.1 shard_map.107.part_ref
  59.2 7.2 %collective-permute-start.19 = (f32[512,128]{1,0:T(8,128)S(1)}, f32[512,128]{1,0:T(8,128)S(1)}, u32[]{:S(2)}, u32[]{:S(2)}) collective-permute-start(f32[512,128]{1,0:T(8,128)S(1)} %shard_map.107.part_ref), channel_id=1, source_target_pairs={{0,16},{16,0},{1,17},{17,1},{2,18},{18,2},{3,19},{19,3},{4,20},{20... | collective-permute-start | bytes 786440 | tf_op jit(solution)/shard_map/ppermute | solution.py:295
  66.4 0.7 %shard_map.108.refs_0_ = f32[512,256]{1,0:T(8,128)} custom-call(f32[512,128]{1,0:T(8,128)S(1)} %shard_map.107.part_ref), custom_call_target="tpu_custom_call" | custom-call | bytes 262144 | tf_op jit(solution)/shard_map/pallas_call | solution.py:268
  67.1 0.4 collective-permute-done.19.part_ref
  67.5 0.7 %shard_map.109 = f32[512,256]{1,0:T(8,128)} custom-call(f32[512,128]{1,0:T(8,128)S(1)} %collective-permute-done.19.part_ref, f32[512,256]{1,0:T(8,128)} %shard_map.108.refs_0_), custom_call_target="tpu_custom_call", output_to_operand_aliasing={{}: (1, {})} | custom-call | bytes 786432 | tf_op jit(solution)/shard_map/pallas_call | solution.py:268
  (13 shorter events, 0.1 us)
Async XLA Ops:
  0.6 16.1 %collective-permute-start.8 = (f32[512,512]{1,0:T(8,128)}, f32[512,512]{1,0:T(8,128)S(1)}, u32[]{:S(2)}, u32[]{:S(2)}) collective-permute-start(f32[512,512]{1,0:T(8,128)} %own_ref.1), channel_id=1, source_target_pairs={{4,5},{8,9},{12,13},{9,10},{13,14},{30,29},{0,0},{1,1},{2,2},{3,3}... | collective-permute-start | bytes 3145736 | tf_op jit(solution)/shard_map/ppermute | solution.py:317
  6.2 2.8 %collective-permute-start = (f32[136,512]{1,0:T(8,128)S(1)}, f32[136,512]{1,0:T(8,128)S(1)}, u32[]{:S(2)}, u32[]{:S(2)}) collective-permute-start(f32[136,512]{1,0:T(8,128)S(1)} %get-tuple-element.28.send_ref), channel_id=1, source_target_pairs={{0,16},{16,0},{1,17},{17,1},{2,18},{18,2},{3,19},{19,3},{4,20},{20... | collective-permute-start | bytes 835592 | tf_op jit(solution)/shard_map/ppermute | solution.py:295
  9.8 7.6 %collective-permute-start.1 = (f32[128,512]{1,0:T(8,128)S(1)}, f32[128,512]{1,0:T(8,128)S(1)}, u32[]{:S(2)}, u32[]{:S(2)}) collective-permute-start(f32[128,512]{1,0:T(8,128)S(1)} %get-tuple-element.35), channel_id=1, source_target_pairs={{0,4},{4,0},{8,12},{12,8},{1,5},{5,1},{9,13},{13,9},{2,6},{6,2},{1... | collective-permute-start | bytes 786440 | tf_op jit(solution)/shard_map/ppermute | solution.py:298
  10.1 12.8 %collective-permute-start.2 = (f32[128,512]{1,0:T(8,128)S(1)}, f32[128,512]{1,0:T(8,128)S(1)}, u32[]{:S(2)}, u32[]{:S(2)}) collective-permute-start(f32[128,512]{1,0:T(8,128)S(1)} %get-tuple-element.36), channel_id=1, source_target_pairs={{0,8},{4,12},{8,0},{12,4},{1,9},{5,13},{9,1},{13,5},{2,10},{6,14},... | collective-permute-start | bytes 786440 | tf_op jit(solution)/shard_map/ppermute | solution.py:298
  10.1 12.8 %collective-permute-start.3 = (f32[128,512]{1,0:T(8,128)S(1)}, f32[128,512]{1,0:T(8,128)S(1)}, u32[]{:S(2)}, u32[]{:S(2)}) collective-permute-start(f32[128,512]{1,0:T(8,128)S(1)} %get-tuple-element.37), channel_id=1, source_target_pairs={{0,12},{4,8},{8,4},{12,0},{1,13},{5,9},{9,5},{13,1},{2,14},{6,10},... | collective-permute-start | bytes 786440 | tf_op jit(solution)/shard_map/ppermute | solution.py:298
  16.7 11.8 %collective-permute-start.10 = (f32[512,512]{1,0:T(8,128)S(1)}, f32[512,512]{1,0:T(8,128)S(1)}, u32[]{:S(2)}, u32[]{:S(2)}) collective-permute-start(f32[512,512]{1,0:T(8,128)S(1)} %collective-permute-done.8.near_ref), channel_id=1, source_target_pairs={{5,22},{9,26},{13,30}} | collective-permute-start | bytes 3145736 | tf_op jit(solution)/shard_map/ppermute | solution.py:317
  22.9 3.2 %copy-start.1 = (f32[512,512]{1,0:T(8,128)S(1)}, f32[512,512]{1,0:T(8,128)}, u32[]{:S(2)}) copy-start(f32[512,512]{1,0:T(8,128)} %diag_ref.1) | copy-start | bytes 3145732
  22.9 3.2 %copy-start.2 = (f32[512,256]{1,0:T(8,128)S(1)}, f32[512,256]{1,0:T(8,128)}, u32[]{:S(2)}) copy-start(f32[512,256]{1,0:T(8,128)} %rhs_ref.1) | copy-start | bytes 1572868
  23.0 13.0 %collective-permute-start.4 = (f32[64,512]{1,0:T(8,128)S(1)}, f32[64,512]{1,0:T(8,128)S(1)}, u32[]{:S(2)}, u32[]{:S(2)}) collective-permute-start(f32[64,512]{1,0:T(8,128)S(1)} %get-tuple-element.38.refs_1_), channel_id=1, source_target_pairs={{0,2},{3,1},{1,0},{2,3},{4,6},{7,5},{5,4},{6,7},{8,10},{11,9},{9,8... | collective-permute-start | bytes 393224 | tf_op jit(solution)/shard_map/ppermute | solution.py:303
  23.3 12.8 %collective-permute-start.6 = (f32[64,512]{1,0:T(8,128)S(1)}, f32[64,512]{1,0:T(8,128)S(1)}, u32[]{:S(2)}, u32[]{:S(2)}) collective-permute-start(f32[64,512]{1,0:T(8,128)S(1)} %get-tuple-element.39), channel_id=1, source_target_pairs={{1,2},{2,1},{0,0},{3,3},{5,6},{6,5},{4,4},{7,7},{9,10},{10,9},{8,8... | collective-permute-start | bytes 393224 | tf_op jit(solution)/shard_map/ppermute | solution.py:303
  26.0 10.0 %collective-permute-start.5 = (f32[64,512]{1,0:T(8,128)S(1)}, f32[64,512]{1,0:T(8,128)S(1)}, u32[]{:S(2)}, u32[]{:S(2)}) collective-permute-start(f32[64,512]{1,0:T(8,128)S(1)} %get-tuple-element.39), channel_id=1, source_target_pairs={{0,1},{3,2},{1,0},{2,3},{4,5},{7,6},{5,4},{6,7},{8,9},{11,10},{9,8... | collective-permute-start | bytes 393224 | tf_op jit(solution)/shard_map/ppermute | solution.py:303
  26.4 10.1 %collective-permute-start.9 = (f32[512,512]{1,0:T(8,128)S(1)}, f32[512,512]{1,0:T(8,128)S(1)}, u32[]{:S(2)}, u32[]{:S(2)}) collective-permute-start(f32[512,512]{1,0:T(8,128)S(1)} %collective-permute-done.8.near_ref), channel_id=1, source_target_pairs={{0,16},{16,0},{1,17},{17,1},{2,18},{18,2},{3,19},{19,3},{4,20},{20... | collective-permute-start | bytes 3145736 | tf_op jit(solution)/shard_map/ppermute | solution.py:295
  28.5 9.8 %collective-permute-start.11 = (f32[512,512]{1,0:T(8,128)S(1)}, f32[512,512]{1,0:T(8,128)S(1)}, u32[]{:S(2)}, u32[]{:S(2)}) collective-permute-start(f32[512,512]{1,0:T(8,128)S(1)} %collective-permute-done.10.on_ref), channel_id=1, source_target_pairs={{0,16},{16,0},{1,17},{17,1},{2,18},{18,2},{3,19},{19,3},{4,20},{20... | collective-permute-start | bytes 3145736 | tf_op jit(solution)/shard_map/ppermute | solution.py:295
  36.0 2.3 %copy-start = (f32[512,512]{1,0:T(8,128)S(1)}, f32[512,512]{1,0:T(8,128)}, u32[]{:S(2)}) copy-start(f32[512,512]{1,0:T(8,128)} %own_ref.1) | copy-start | bytes 3145732
  36.1 3.9 %collective-permute-start.12 = (f32[64,512]{1,0:T(8,128)S(1)}, f32[64,512]{1,0:T(8,128)S(1)}, u32[]{:S(2)}, u32[]{:S(2)}) collective-permute-start(f32[64,512]{1,0:T(8,128)S(1)} %get-tuple-element.43.refs_1_), channel_id=1, source_target_pairs={{0,4},{4,0},{8,12},{12,8},{1,5},{5,1},{9,13},{13,9},{2,6},{6,2},{1... | collective-permute-start | bytes 393224 | tf_op jit(solution)/shard_map/ppermute | solution.py:298
  36.4 3.8 %collective-permute-start.7 = (f32[64,512]{1,0:T(8,128)S(1)}, f32[64,512]{1,0:T(8,128)S(1)}, u32[]{:S(2)}, u32[]{:S(2)}) collective-permute-start(f32[64,512]{1,0:T(8,128)S(1)} %get-tuple-element.43.refs_1_), channel_id=1, source_target_pairs={{0,8},{4,12},{8,0},{12,4},{1,9},{5,13},{9,1},{13,5},{2,10},{6,14},... | collective-permute-start | bytes 393224 | tf_op jit(solution)/shard_map/ppermute | solution.py:298
  40.0 4.8 %collective-permute-start.13 = (f32[64,512]{1,0:T(8,128)S(1)}, f32[64,512]{1,0:T(8,128)S(1)}, u32[]{:S(2)}, u32[]{:S(2)}) collective-permute-start(f32[64,512]{1,0:T(8,128)S(1)} %shard_map.103.refs_1_), channel_id=1, source_target_pairs={{0,12},{4,8},{8,4},{12,0},{1,13},{5,9},{9,5},{13,1},{2,14},{6,10},... | collective-permute-start | bytes 393224 | tf_op jit(solution)/shard_map/ppermute | solution.py:298
  44.8 4.0 %collective-permute-start.15 = (f32[64,512]{1,0:T(8,128)S(1)}, f32[64,512]{1,0:T(8,128)S(1)}, u32[]{:S(2)}, u32[]{:S(2)}) collective-permute-start(f32[64,512]{1,0:T(8,128)S(1)} %shard_map.105.refs_1_), channel_id=1, source_target_pairs={{0,4},{4,0},{8,12},{12,8},{1,5},{5,1},{9,13},{13,9},{2,6},{6,2},{1... | collective-permute-start | bytes 393224 | tf_op jit(solution)/shard_map/ppermute | solution.py:298
  45.6 3.8 %collective-permute-start.14 = (f32[64,512]{1,0:T(8,128)S(1)}, f32[64,512]{1,0:T(8,128)S(1)}, u32[]{:S(2)}, u32[]{:S(2)}) collective-permute-start(f32[64,512]{1,0:T(8,128)S(1)} %shard_map.105.refs_1_), channel_id=1, source_target_pairs={{0,8},{4,12},{8,0},{12,4},{1,9},{5,13},{9,1},{13,5},{2,10},{6,14},... | collective-permute-start | bytes 393224 | tf_op jit(solution)/shard_map/ppermute | solution.py:298
  50.2 5.6 %collective-permute-start.18 = (f32[64,512]{1,0:T(8,128)S(1)}, f32[64,512]{1,0:T(8,128)S(1)}, u32[]{:S(2)}, u32[]{:S(2)}) collective-permute-start(f32[64,512]{1,0:T(8,128)S(1)} %shard_map.106.x_ref), channel_id=1, source_target_pairs={{1,3},{2,0},{0,1},{3,2},{5,7},{6,4},{4,5},{7,6},{9,11},{10,8},{8,9... | collective-permute-start | bytes 393224 | tf_op jit(solution)/shard_map/ppermute | solution.py:303
  50.3 5.5 %collective-permute-start.17 = (f32[64,512]{1,0:T(8,128)S(1)}, f32[64,512]{1,0:T(8,128)S(1)}, u32[]{:S(2)}, u32[]{:S(2)}) collective-permute-start(f32[64,512]{1,0:T(8,128)S(1)} %shard_map.106.x_ref), channel_id=1, source_target_pairs={{1,0},{2,3},{0,1},{3,2},{5,4},{6,7},{4,5},{7,6},{9,8},{10,11},{8,9... | collective-permute-start | bytes 393224 | tf_op jit(solution)/shard_map/ppermute | solution.py:303
  51.7 7.3 %collective-permute-start.16 = (f32[64,512]{1,0:T(8,128)S(1)}, f32[64,512]{1,0:T(8,128)S(1)}, u32[]{:S(2)}, u32[]{:S(2)}) collective-permute-start(f32[64,512]{1,0:T(8,128)S(1)} %shard_map.106.x_ref), channel_id=1, source_target_pairs={{1,2},{2,1},{0,0},{3,3},{5,6},{6,5},{4,4},{7,7},{9,10},{10,9},{8,8... | collective-permute-start | bytes 393224 | tf_op jit(solution)/shard_map/ppermute | solution.py:303
  59.2 8.3 %collective-permute-start.19 = (f32[512,128]{1,0:T(8,128)S(1)}, f32[512,128]{1,0:T(8,128)S(1)}, u32[]{:S(2)}, u32[]{:S(2)}) collective-permute-start(f32[512,128]{1,0:T(8,128)S(1)} %shard_map.107.part_ref), channel_id=1, source_target_pairs={{0,16},{16,0},{1,17},{17,1},{2,18},{18,2},{3,19},{19,3},{4,20},{20... | collective-permute-start | bytes 786440 | tf_op jit(solution)/shard_map/ppermute | solution.py:295

commit v14 on v11

--- a/solution.py
+++ b/solution.py
@@ -187,7 +187,7 @@
     second_ref[...] = sum_ref[pl.ds(pl.multiple_of((1 - odd) * piece, piece), piece), :]
 
 
-def factor_kernel(own_ref, sent_ref, other_ref, *out_refs):
+def factor_kernel(own_ref, sent_ref, other_ref, diag_high_ref, diag_low_ref, *out_refs):
     leaf, row, z = place()
     for block in range(3):
         high_ref, low_ref = out_refs[2 * block], out_refs[2 * block + 1]
@@ -199,34 +199,27 @@
             else:
                 sent = jnp.where((leaf == 0) == (block == 1), sent_ref[...], other_ref[...])
                 value = jnp.where(z == block, own_ref[...], sent)
-            high_ref[...], low_ref[...] = split(value.T)
-
-
-def chain_kernel(owner, has_sums, solves, *refs):
-    refs = list(refs)
-    out_refs = [refs.pop()]
-    if has_sums:
-        out_refs.insert(0, refs.pop())
+            value = value.T
+            value = value + dot3(value, diag_high_ref[...], diag_low_ref[...], NN)
+            high_ref[...], low_ref[...] = split(value)
+
+
+def first_kernel(rhs_ref, a_ref, b_ref, c_ref, d_ref, high_ref, low_ref, out_ref):
+    value = rhs_ref[...] - ((a_ref[...] + b_ref[...]) + (c_ref[...] + d_ref[...]))
+    out_ref[...] = value + dot3(value, high_ref[...], low_ref[...], NN)
+
+
+def chain_kernel(owner, given_ref, *refs):
     _, row, z = place()
-    given_ref = refs[0]
-    if has_sums:
-        value = given_ref[...] - ((refs[1][...] + refs[2][...]) + (refs[3][...] + refs[4][...]))
-        out_refs[0][...] = value
-        out_refs[1][...] = value
-        refs = refs[5:]
-    else:
-        out_refs[0][...] = refs[1][...]
-        refs = refs[2:]
+    used, out_ref = refs[:-1], refs[-1]
+    out_ref[...] = given_ref[...]
 
     @pl.when((row == owner) & ((z == 1) | (z == 2)))
     def _():
-        left = out_refs[0][...] if has_sums else given_ref[...]
-        used = refs[2:] if solves else refs
+        left = given_ref[...]
         for i in range(0, len(used), 3):
             left = left - dot3(used[i][...], used[i + 1][...], used[i + 2][...], NN)
-        if solves:
-            left = left + dot3(left, refs[0][...], refs[1][...], NN)
-        out_refs[-1][...] = left
+        out_ref[...] = left
 
 
 def half_kernel(b_ref, a_ref, c_ref, x_ref, out_ref):
@@ -329,25 +322,24 @@
         along_col(first, [(1, 2), (2, 1)]),
     ]
 
-    def chain(owner, ins, has_sums=False, solves=True, flops=0):
-        outs = call(
-            functools.partial(chain_kernel, owner, has_sums, solves), ins, [shape] * (1 + has_sums), flops=flops
-        )
-        return outs if has_sums else outs[0]
-
-    res, x = chain(0, [rhs_piece, second] + q + diag, has_sums=True, flops=10 ** 10)
-    factor = call(factor_kernel, [top_factor, sent, swap(sent)], [block] * 6)
+    factor = call(factor_kernel, [top_factor, sent, swap(sent)] + diag, [block] * 6)
     factor = [factor[0:2], factor[2:4], factor[4:6]]
+
+    def chain(owner, ins):
+        (out,) = call(functools.partial(chain_kernel, owner), ins, [shape])
+        return out
+
+    (x,) = call(first_kernel, [rhs_piece, second] + q + diag, [shape], flops=10 ** 10)
     to1 = along_row(x, 1)
     to2 = along_row(x, 2)
-    x = chain(1, [res, x] + diag + [to1] + factor[0])
+    x = chain(1, [x, to1] + factor[0])
     on = along_row(x, 3)
-    res = chain(2, [res, res, to2] + factor[0], solves=False)
-    x = chain(2, [res, x] + diag + [on] + factor[1])
+    x = chain(2, [x, to2] + factor[0])
+    x = chain(2, [x, on] + factor[1])
     to3 = along_row(x, 1)
     late = along_row(x, 2)
-    res = chain(3, [res, res, on] + factor[0], solves=False)
-    x = chain(3, [res, x] + diag + [late] + factor[1] + [to3] + factor[2])
+    x = chain(3, [x, on] + factor[0])
+    x = chain(3, [x, late] + factor[1] + [to3] + factor[2])
 
     both = along_col(x, [(1, 2), (2, 1)])
     step = along_col(x, [(1, 0), (2, 3)])

time: 64.7 us -> 64.7 us (level)
  Pallas kernels: 8.55 us -> 10.9 us
  waiting for transfers between devices: 29.2 us -> 27.3 us
    pallas_call x15, Pallas kernels: 8.55 us -> 10.9 us  [call(): pl.pallas_call(kernel, out_shape=[shape(i, out) for i, out in enumerate(o...]
    ppermute x8, waiting for transfers between devices: 20.6 us -> 18.6 us  [along_row(): return lax.ppermute(value, 'row', [(r, r ^ step) for r in range(rows)])]
  transfers between devices with their start and end apart: 18 -> 18, of which waited for: 13 -> 13; matrix products, arithmetic and copies ran while one was open for 0% -> 0% of each run, Pallas kernels for 11% -> 15%
where the time goes in v14:
time: 64.7 us; the launch traced here: 63.8 us
  waiting for transfers between devices  27.3 us (42%)
  starting transfers between devices  24.1 us (37%)
  Pallas kernels  10.9 us (17%)
  between operations  0.83 us (1%)
  local copies, waits for them, and re-layouts  0.67 us (1%)
    ppermute x8, waiting for transfers between devices, along_row(): return lax.ppermute(value, 'row', [(r, r ^ step) for r in range(rows)])  18.6 us
    pallas_call x15, Pallas kernels, call(): pl.pallas_call(kernel, out_shape=[shape(i, out) for i, out in enumerate(o...  10.9 us
    ppermute x3, starting transfers between devices, swap(): return lax.ppermute(value, 'leaf', [(0, 1), (1, 0)])  10.8 us
    ppermute x6, starting transfers between devices, along_col(): return lax.ppermute(value, 'col', pairs + list(zip(rest, open_ends)))  7.7 us
    ppermute x6, waiting for transfers between devices, along_col(): return lax.ppermute(value, 'col', pairs + list(zip(rest, open_ends)))  6.01 us
    ppermute x8, starting transfers between devices, along_row(): return lax.ppermute(value, 'row', [(r, r ^ step) for r in range(rows)])  3.5 us
    ppermute x1, starting transfers between devices, central(): sent = lax.ppermute(top_factor, ('leaf', 'row', 'col'), pairs)  2.08 us
    ppermute x1, waiting for transfers between devices, central(): sent = lax.ppermute(top_factor, ('leaf', 'row', 'col'), pairs)  1.88 us
  transfers between devices with their start and end apart: 18, of which 13 were waited for; matrix products, arithmetic and copies ran while one was open for 0% of the time, Pallas kernels for 15%

profile of v14, /device:TPU:15, one launch (start us, length us, event | category | flops | bytes accessed | tf_op | source)
XLA Modules:
  0.0 63.8 jit_solution(11085182196948190007)
XLA Ops:
  0.6 2.1 %collective-permute-start.8 = (f32[512,512]{1,0:T(8,128)}, f32[512,512]{1,0:T(8,128)S(1)}, u32[]{:S(2)}, u32[]{:S(2)}) collective-permute-start(f32[512,512]{1,0:T(8,128)} %own_ref.1), channel_id=1, source_target_pairs={{4,5},{8,9},{12,13},{9,10},{13,14},{20,22},{24,26},{28,30},{30,29}... | collective-permute-start | bytes 3145736 | tf_op jit(solution)/shard_map/ppermute | solution.py:299
  2.7 2.9 %shard_map.95 = (f32[2,256,256]{2,1,0:T(8,128)}, f32[128,512]{1,0:T(8,128)S(1)}, f32[136,512]{1,0:T(8,128)S(1)}) custom-call(s32[2]{0:T(128)} %live_hbm.1, f32[2,256,256]{2,1,0:T(8,128)} %rhs_hbm.1, f32[2,256,256]{2,1,0:T(8,128)} %diag_hbm.1, f32[2,256,256]{2,1,0:T(8,128)} %off_hbm.1, s32[2,256]{1,0:T(2,128)} %tgt_hbm.1), custom_call_target="tpu_custom_call" | custom-call | bytes 1574920 | tf_op jit(solution)/shard_map/pallas_call | solution.py:251
  5.7 2.1 %collective-permute-start = (f32[136,512]{1,0:T(8,128)S(1)}, f32[136,512]{1,0:T(8,128)S(1)}, u32[]{:S(2)}, u32[]{:S(2)}) collective-permute-start(f32[136,512]{1,0:T(8,128)S(1)} %get-tuple-element.26.send_ref), channel_id=1, source_target_pairs={{0,16},{16,0},{1,17},{17,1},{2,18},{18,2},{3,19},{19,3},{4,20},{20... | collective-permute-start | bytes 835592 | tf_op jit(solution)/shard_map/ppermute | solution.py:278
  7.8 0.8 %shard_map.97 = (f32[128,512]{1,0:T(8,128)S(1)}, f32[128,512]{1,0:T(8,128)S(1)}, f32[128,512]{1,0:T(8,128)S(1)}, f32[128,512]{1,0:T(8,128)S(1)}) custom-call(f32[128,512]{1,0:T(8,128)S(1)} %get-tuple-element.27.keep_ref, f32[136,512]{1,0:T(8,128)S(1)} %get-tuple-element.26.send_ref), custom_call_target="tpu_custom_call" | custom-call | bytes 540672 | tf_op jit(solution)/shard_map/pallas_call | solution.py:251
  8.6 0.4 collective-permute-done.recv_ref
  9.0 0.8 %shard_map.98 = (f32[128,512]{1,0:T(8,128)S(1)}, f32[128,512]{1,0:T(8,128)S(1)}, f32[128,512]{1,0:T(8,128)S(1)}, f32[128,512]{1,0:T(8,128)S(1)}) custom-call(f32[136,512]{1,0:T(8,128)S(1)} %collective-permute-done.recv_ref, f32[128,512]{1,0:T(8,128)S(1)} %get-tuple-element.28.refs_0_, f32[128,512]{1,0:T(8,128)S(1)} %get-tuple-element.29.refs_1_, ...), custom_call_target="tpu_custom_call" | custom-call | bytes 1327104 | tf_op jit(solution)/shard_map/pallas_call | solution.py:251
  9.8 0.3 collective-permute-start.1
  10.1 0.0 collective-permute-start.2
  10.1 2.4 %collective-permute-start.3 = (f32[128,512]{1,0:T(8,128)S(1)}, f32[128,512]{1,0:T(8,128)S(1)}, u32[]{:S(2)}, u32[]{:S(2)}) collective-permute-start(f32[128,512]{1,0:T(8,128)S(1)} %get-tuple-element.35), channel_id=1, source_target_pairs={{0,12},{4,8},{8,4},{12,0},{1,13},{5,9},{9,5},{13,1},{2,14},{6,10},... | collective-permute-start | bytes 786440 | tf_op jit(solution)/shard_map/ppermute | solution.py:281
  12.5 4.9 %collective-permute-done.1.b_ref = f32[128,512]{1,0:T(8,128)S(1)} collective-permute-done((f32[128,512]{1,0:T(8,128)S(1)}, f32[128,512]{1,0:T(8,128)S(1)}, u32[]{:S(2)}, u32[]{:S(2)}) %collective-permute-start.1) | collective-permute-done | bytes 262176 | tf_op jit(solution)/shard_map/ppermute | solution.py:281
  17.4 5.5 %collective-permute-done.2.c_ref = f32[128,512]{1,0:T(8,128)S(1)} collective-permute-done((f32[128,512]{1,0:T(8,128)S(1)}, f32[128,512]{1,0:T(8,128)S(1)}, u32[]{:S(2)}, u32[]{:S(2)}) %collective-permute-start.2) | collective-permute-done | bytes 262176 | tf_op jit(solution)/shard_map/ppermute | solution.py:281
  22.9 0.0 collective-permute-done.3.d_ref
  22.9 0.1 shard_map.99
  23.0 1.0 %collective-permute-start.4 = (f32[64,512]{1,0:T(8,128)S(1)}, f32[64,512]{1,0:T(8,128)S(1)}, u32[]{:S(2)}, u32[]{:S(2)}) collective-permute-start(f32[64,512]{1,0:T(8,128)S(1)} %get-tuple-element.36.a_ref), channel_id=1, source_target_pairs={{0,2},{3,1},{1,0},{2,3},{4,6},{7,5},{5,4},{6,7},{8,10},{11,9},{9,8... | collective-permute-start | bytes 393224 | tf_op jit(solution)/shard_map/ppermute | solution.py:286
  23.9 2.0 %collective-permute-start.6 = (f32[64,512]{1,0:T(8,128)S(1)}, f32[64,512]{1,0:T(8,128)S(1)}, u32[]{:S(2)}, u32[]{:S(2)}) collective-permute-start(f32[64,512]{1,0:T(8,128)S(1)} %get-tuple-element.37), channel_id=1, source_target_pairs={{1,2},{2,1},{0,0},{3,3},{5,6},{6,5},{4,4},{7,7},{9,10},{10,9},{8,8... | collective-permute-start | bytes 393224 | tf_op jit(solution)/shard_map/ppermute | solution.py:286
  26.0 0.1 collective-permute-start.5
  26.1 0.3 shard_map.96
  26.4 1.9 %collective-permute-done.8.sent_ref = f32[512,512]{1,0:T(8,128)S(1)} collective-permute-done((f32[512,512]{1,0:T(8,128)}, f32[512,512]{1,0:T(8,128)S(1)}, u32[]{:S(2)}, u32[]{:S(2)}) %collective-permute-start.8) | collective-permute-done | bytes 1048608 | tf_op jit(solution)/shard_map/ppermute | solution.py:299
  28.3 3.6 %collective-permute-start.9 = (f32[512,512]{1,0:T(8,128)S(1)}, f32[512,512]{1,0:T(8,128)S(1)}, u32[]{:S(2)}, u32[]{:S(2)}) collective-permute-start(f32[512,512]{1,0:T(8,128)S(1)} %collective-permute-done.8.sent_ref), channel_id=1, source_target_pairs={{0,16},{16,0},{1,17},{17,1},{2,18},{18,2},{3,19},{19,3},{4,20},{20... | collective-permute-start | bytes 3145736 | tf_op jit(solution)/shard_map/ppermute | solution.py:278
  31.9 0.0 collective-permute-done.4.b_ref
  31.9 0.9 %collective-permute-done.6.d_ref = f32[64,512]{1,0:T(8,128)S(1)} collective-permute-done((f32[64,512]{1,0:T(8,128)S(1)}, f32[64,512]{1,0:T(8,128)S(1)}, u32[]{:S(2)}, u32[]{:S(2)}) %collective-permute-start.6) | collective-permute-done | bytes 131104 | tf_op jit(solution)/shard_map/ppermute | solution.py:286
  32.8 1.6 %collective-permute-done.5.c_ref = f32[64,512]{1,0:T(8,128)S(1)} collective-permute-done((f32[64,512]{1,0:T(8,128)S(1)}, f32[64,512]{1,0:T(8,128)S(1)}, u32[]{:S(2)}, u32[]{:S(2)}) %collective-permute-start.5) | collective-permute-done | bytes 131104 | tf_op jit(solution)/shard_map/ppermute | solution.py:286
  34.5 0.3 shard_map.100.given_ref
  34.8 0.1 collective-permute-start.7
  34.8 0.2 collective-permute-start.10
  35.0 0.0 collective-permute-done.9.other_ref
  35.0 0.7 %copy-done.1 = f32[512,512]{1,0:T(8,128)S(1)} copy-done((f32[512,512]{1,0:T(8,128)S(1)}, f32[512,512]{1,0:T(8,128)}, u32[]{:S(2)}) %copy-start.1) | copy-done | bytes 1048600
  35.7 3.4 %shard_map.101 = (bf16[512,512]{1,0:T(8,128)(2,1)S(1)}, bf16[512,512]{1,0:T(8,128)(2,1)S(1)}, bf16[512,512]{1,0:T(8,128)(2,1)S(1)}, bf16[512,512]{1,0:T(8,128)(2...) custom-call(f32[512,512]{1,0:T(8,128)S(1)} %copy-done.1, ...), custom_call_target="tpu_custom_call" | custom-call | bytes 5242880 | tf_op jit(solution)/shard_map/pallas_call | solution.py:251
  39.1 0.3 collective-permute-done.7.refs_0_
  39.4 0.1 collective-permute-start.11
  39.5 0.0 collective-permute-done.10.refs_0_
  39.5 4.7 %collective-permute-done.11.refs_0_ = f32[64,512]{1,0:T(8,128)S(1)} collective-permute-done((f32[64,512]{1,0:T(8,128)S(1)}, f32[64,512]{1,0:T(8,128)S(1)}, u32[]{:S(2)}, u32[]{:S(2)}) %collective-permute-start.11) | collective-permute-done | bytes 131104 | tf_op jit(solution)/shard_map/ppermute | solution.py:281
  44.2 0.1 collective-permute-start.13
  44.3 0.3 collective-permute-start.12
  44.6 0.3 shard_map.105.given_ref
  44.9 3.1 %collective-permute-done.13.refs_3_ = f32[64,512]{1,0:T(8,128)S(1)} collective-permute-done((f32[64,512]{1,0:T(8,128)S(1)}, f32[64,512]{1,0:T(8,128)S(1)}, u32[]{:S(2)}, u32[]{:S(2)}) %collective-permute-start.13) | collective-permute-done | bytes 131104 | tf_op jit(solution)/shard_map/ppermute | solution.py:281
  48.1 0.1 collective-permute-done.12.refs_0_
  48.2 0.5 shard_map.106.x_ref
  48.6 0.1 collective-permute-start.16
  48.7 1.5 %collective-permute-start.15 = (f32[64,512]{1,0:T(8,128)S(1)}, f32[64,512]{1,0:T(8,128)S(1)}, u32[]{:S(2)}, u32[]{:S(2)}) collective-permute-start(f32[64,512]{1,0:T(8,128)S(1)} %shard_map.106.x_ref), channel_id=1, source_target_pairs={{1,0},{2,3},{0,1},{3,2},{5,4},{6,7},{4,5},{7,6},{9,8},{10,11},{8,9... | collective-permute-start | bytes 393224 | tf_op jit(solution)/shard_map/ppermute | solution.py:286
  50.2 3.1 %collective-permute-start.14 = (f32[64,512]{1,0:T(8,128)S(1)}, f32[64,512]{1,0:T(8,128)S(1)}, u32[]{:S(2)}, u32[]{:S(2)}) collective-permute-start(f32[64,512]{1,0:T(8,128)S(1)} %shard_map.106.x_ref), channel_id=1, source_target_pairs={{1,2},{2,1},{0,0},{3,3},{5,6},{6,5},{4,4},{7,7},{9,10},{10,9},{8,8... | collective-permute-start | bytes 393224 | tf_op jit(solution)/shard_map/ppermute | solution.py:286
  53.3 0.6 collective-permute-done.15.a_ref
  53.9 2.8 %collective-permute-done.14.b_ref = f32[64,512]{1,0:T(8,128)S(1)} collective-permute-done((f32[64,512]{1,0:T(8,128)S(1)}, f32[64,512]{1,0:T(8,128)S(1)}, u32[]{:S(2)}, u32[]{:S(2)}) %collective-permute-start.14) | collective-permute-done | bytes 131104 | tf_op jit(solution)/shard_map/ppermute | solution.py:286
  56.8 0.1 shard_map.107.part_ref
  56.9 5.0 %collective-permute-start.17 = (f32[512,128]{1,0:T(8,128)S(1)}, f32[512,128]{1,0:T(8,128)S(1)}, u32[]{:S(2)}, u32[]{:S(2)}) collective-permute-start(f32[512,128]{1,0:T(8,128)S(1)} %shard_map.107.part_ref), channel_id=1, source_target_pairs={{0,16},{16,0},{1,17},{17,1},{2,18},{18,2},{3,19},{19,3},{4,20},{20... | collective-permute-start | bytes 786440 | tf_op jit(solution)/shard_map/ppermute | solution.py:278
  61.9 0.7 %shard_map.108.refs_0_ = f32[512,256]{1,0:T(8,128)} custom-call(f32[512,128]{1,0:T(8,128)S(1)} %shard_map.107.part_ref), custom_call_target="tpu_custom_call" | custom-call | bytes 262144 | tf_op jit(solution)/shard_map/pallas_call | solution.py:251
  62.7 0.4 collective-permute-done.17.part_ref
  63.1 0.7 %shard_map.109 = f32[512,256]{1,0:T(8,128)} custom-call(f32[512,128]{1,0:T(8,128)S(1)} %collective-permute-done.17.part_ref, f32[512,256]{1,0:T(8,128)} %shard_map.108.refs_0_), custom_call_target="tpu_custom_call", output_to_operand_aliasing={{}: (1, {})} | custom-call | bytes 786432 | tf_op jit(solution)/shard_map/pallas_call | solution.py:251
  (9 shorter events, 0.0 us)
Async XLA Ops:
  0.6 27.7 %collective-permute-start.8 = (f32[512,512]{1,0:T(8,128)}, f32[512,512]{1,0:T(8,128)S(1)}, u32[]{:S(2)}, u32[]{:S(2)}) collective-permute-start(f32[512,512]{1,0:T(8,128)} %own_ref.1), channel_id=1, source_target_pairs={{4,5},{8,9},{12,13},{9,10},{13,14},{20,22},{24,26},{28,30},{30,29}... | collective-permute-start | bytes 3145736 | tf_op jit(solution)/shard_map/ppermute | solution.py:299
  5.7 3.3 %collective-permute-start = (f32[136,512]{1,0:T(8,128)S(1)}, f32[136,512]{1,0:T(8,128)S(1)}, u32[]{:S(2)}, u32[]{:S(2)}) collective-permute-start(f32[136,512]{1,0:T(8,128)S(1)} %get-tuple-element.26.send_ref), channel_id=1, source_target_pairs={{0,16},{16,0},{1,17},{17,1},{2,18},{18,2},{3,19},{19,3},{4,20},{20... | collective-permute-start | bytes 835592 | tf_op jit(solution)/shard_map/ppermute | solution.py:278
  9.0 17.1 %copy-start = (f32[512,512]{1,0:T(8,128)S(1)}, f32[512,512]{1,0:T(8,128)}, u32[]{:S(2)}) copy-start(f32[512,512]{1,0:T(8,128)} %diag_ref.1) | copy-start | bytes 3145732
  9.8 7.6 %collective-permute-start.1 = (f32[128,512]{1,0:T(8,128)S(1)}, f32[128,512]{1,0:T(8,128)S(1)}, u32[]{:S(2)}, u32[]{:S(2)}) collective-permute-start(f32[128,512]{1,0:T(8,128)S(1)} %get-tuple-element.33), channel_id=1, source_target_pairs={{0,4},{4,0},{8,12},{12,8},{1,5},{5,1},{9,13},{13,9},{2,6},{6,2},{1... | collective-permute-start | bytes 786440 | tf_op jit(solution)/shard_map/ppermute | solution.py:281
  10.1 12.8 %collective-permute-start.2 = (f32[128,512]{1,0:T(8,128)S(1)}, f32[128,512]{1,0:T(8,128)S(1)}, u32[]{:S(2)}, u32[]{:S(2)}) collective-permute-start(f32[128,512]{1,0:T(8,128)S(1)} %get-tuple-element.34), channel_id=1, source_target_pairs={{0,8},{4,12},{8,0},{12,4},{1,9},{5,13},{9,1},{13,5},{2,10},{6,14},... | collective-permute-start | bytes 786440 | tf_op jit(solution)/shard_map/ppermute | solution.py:281
  10.1 12.8 %collective-permute-start.3 = (f32[128,512]{1,0:T(8,128)S(1)}, f32[128,512]{1,0:T(8,128)S(1)}, u32[]{:S(2)}, u32[]{:S(2)}) collective-permute-start(f32[128,512]{1,0:T(8,128)S(1)} %get-tuple-element.35), channel_id=1, source_target_pairs={{0,12},{4,8},{8,4},{12,0},{1,13},{5,9},{9,5},{13,1},{2,14},{6,10},... | collective-permute-start | bytes 786440 | tf_op jit(solution)/shard_map/ppermute | solution.py:281
  22.9 3.2 %copy-start.2 = (f32[512,256]{1,0:T(8,128)S(1)}, f32[512,256]{1,0:T(8,128)}, u32[]{:S(2)}) copy-start(f32[512,256]{1,0:T(8,128)} %rhs_ref.1) | copy-start | bytes 1572868
  23.0 8.9 %collective-permute-start.4 = (f32[64,512]{1,0:T(8,128)S(1)}, f32[64,512]{1,0:T(8,128)S(1)}, u32[]{:S(2)}, u32[]{:S(2)}) collective-permute-start(f32[64,512]{1,0:T(8,128)S(1)} %get-tuple-element.36.a_ref), channel_id=1, source_target_pairs={{0,2},{3,1},{1,0},{2,3},{4,6},{7,5},{5,4},{6,7},{8,10},{11,9},{9,8... | collective-permute-start | bytes 393224 | tf_op jit(solution)/shard_map/ppermute | solution.py:286
  23.9 8.9 %collective-permute-start.6 = (f32[64,512]{1,0:T(8,128)S(1)}, f32[64,512]{1,0:T(8,128)S(1)}, u32[]{:S(2)}, u32[]{:S(2)}) collective-permute-start(f32[64,512]{1,0:T(8,128)S(1)} %get-tuple-element.37), channel_id=1, source_target_pairs={{1,2},{2,1},{0,0},{3,3},{5,6},{6,5},{4,4},{7,7},{9,10},{10,9},{8,8... | collective-permute-start | bytes 393224 | tf_op jit(solution)/shard_map/ppermute | solution.py:286
  26.0 8.5 %collective-permute-start.5 = (f32[64,512]{1,0:T(8,128)S(1)}, f32[64,512]{1,0:T(8,128)S(1)}, u32[]{:S(2)}, u32[]{:S(2)}) collective-permute-start(f32[64,512]{1,0:T(8,128)S(1)} %get-tuple-element.37), channel_id=1, source_target_pairs={{0,1},{3,2},{1,0},{2,3},{4,5},{7,6},{5,4},{6,7},{8,9},{11,10},{9,8... | collective-permute-start | bytes 393224 | tf_op jit(solution)/shard_map/ppermute | solution.py:286
  28.3 6.7 %collective-permute-start.9 = (f32[512,512]{1,0:T(8,128)S(1)}, f32[512,512]{1,0:T(8,128)S(1)}, u32[]{:S(2)}, u32[]{:S(2)}) collective-permute-start(f32[512,512]{1,0:T(8,128)S(1)} %collective-permute-done.8.sent_ref), channel_id=1, source_target_pairs={{0,16},{16,0},{1,17},{17,1},{2,18},{18,2},{3,19},{19,3},{4,20},{20... | collective-permute-start | bytes 3145736 | tf_op jit(solution)/shard_map/ppermute | solution.py:278
  34.5 1.2 %copy-start.1 = (f32[512,512]{1,0:T(8,128)S(1)}, f32[512,512]{1,0:T(8,128)}, u32[]{:S(2)}) copy-start(f32[512,512]{1,0:T(8,128)} %own_ref.1) | copy-start | bytes 3145732
  34.8 4.6 %collective-permute-start.7 = (f32[64,512]{1,0:T(8,128)S(1)}, f32[64,512]{1,0:T(8,128)S(1)}, u32[]{:S(2)}, u32[]{:S(2)}) collective-permute-start(f32[64,512]{1,0:T(8,128)S(1)} %shard_map.100.given_ref), channel_id=1, source_target_pairs={{0,4},{4,0},{8,12},{12,8},{1,5},{5,1},{9,13},{13,9},{2,6},{6,2},{1... | collective-permute-start | bytes 393224 | tf_op jit(solution)/shard_map/ppermute | solution.py:281
  34.8 4.7 %collective-permute-start.10 = (f32[64,512]{1,0:T(8,128)S(1)}, f32[64,512]{1,0:T(8,128)S(1)}, u32[]{:S(2)}, u32[]{:S(2)}) collective-permute-start(f32[64,512]{1,0:T(8,128)S(1)} %shard_map.100.given_ref), channel_id=1, source_target_pairs={{0,8},{4,12},{8,0},{12,4},{1,9},{5,13},{9,1},{13,5},{2,10},{6,14},... | collective-permute-start | bytes 393224 | tf_op jit(solution)/shard_map/ppermute | solution.py:281
  39.4 4.8 %collective-permute-start.11 = (f32[64,512]{1,0:T(8,128)S(1)}, f32[64,512]{1,0:T(8,128)S(1)}, u32[]{:S(2)}, u32[]{:S(2)}) collective-permute-start(f32[64,512]{1,0:T(8,128)S(1)} %shard_map.102.given_ref), channel_id=1, source_target_pairs={{0,12},{4,8},{8,4},{12,0},{1,13},{5,9},{9,5},{13,1},{2,14},{6,10},... | collective-permute-start | bytes 393224 | tf_op jit(solution)/shard_map/ppermute | solution.py:281
  44.2 3.9 %collective-permute-start.13 = (f32[64,512]{1,0:T(8,128)S(1)}, f32[64,512]{1,0:T(8,128)S(1)}, u32[]{:S(2)}, u32[]{:S(2)}) collective-permute-start(f32[64,512]{1,0:T(8,128)S(1)} %shard_map.104.given_ref), channel_id=1, source_target_pairs={{0,4},{4,0},{8,12},{12,8},{1,5},{5,1},{9,13},{13,9},{2,6},{6,2},{1... | collective-permute-start | bytes 393224 | tf_op jit(solution)/shard_map/ppermute | solution.py:281
  44.3 3.9 %collective-permute-start.12 = (f32[64,512]{1,0:T(8,128)S(1)}, f32[64,512]{1,0:T(8,128)S(1)}, u32[]{:S(2)}, u32[]{:S(2)}) collective-permute-start(f32[64,512]{1,0:T(8,128)S(1)} %shard_map.104.given_ref), channel_id=1, source_target_pairs={{0,8},{4,12},{8,0},{12,4},{1,9},{5,13},{9,1},{13,5},{2,10},{6,14},... | collective-permute-start | bytes 393224 | tf_op jit(solution)/shard_map/ppermute | solution.py:281
  48.6 4.7 %collective-permute-start.16 = (f32[64,512]{1,0:T(8,128)S(1)}, f32[64,512]{1,0:T(8,128)S(1)}, u32[]{:S(2)}, u32[]{:S(2)}) collective-permute-start(f32[64,512]{1,0:T(8,128)S(1)} %shard_map.106.x_ref), channel_id=1, source_target_pairs={{1,3},{2,0},{0,1},{3,2},{5,7},{6,4},{4,5},{7,6},{9,11},{10,8},{8,9... | collective-permute-start | bytes 393224 | tf_op jit(solution)/shard_map/ppermute | solution.py:286
  48.7 5.2 %collective-permute-start.15 = (f32[64,512]{1,0:T(8,128)S(1)}, f32[64,512]{1,0:T(8,128)S(1)}, u32[]{:S(2)}, u32[]{:S(2)}) collective-permute-start(f32[64,512]{1,0:T(8,128)S(1)} %shard_map.106.x_ref), channel_id=1, source_target_pairs={{1,0},{2,3},{0,1},{3,2},{5,4},{6,7},{4,5},{7,6},{9,8},{10,11},{8,9... | collective-permute-start | bytes 393224 | tf_op jit(solution)/shard_map/ppermute | solution.py:286
  50.2 6.6 %collective-permute-start.14 = (f32[64,512]{1,0:T(8,128)S(1)}, f32[64,512]{1,0:T(8,128)S(1)}, u32[]{:S(2)}, u32[]{:S(2)}) collective-permute-start(f32[64,512]{1,0:T(8,128)S(1)} %shard_map.106.x_ref), channel_id=1, source_target_pairs={{1,2},{2,1},{0,0},{3,3},{5,6},{6,5},{4,4},{7,7},{9,10},{10,9},{8,8... | collective-permute-start | bytes 393224 | tf_op jit(solution)/shard_map/ppermute | solution.py:286
  56.9 6.2 %collective-permute-start.17 = (f32[512,128]{1,0:T(8,128)S(1)}, f32[512,128]{1,0:T(8,128)S(1)}, u32[]{:S(2)}, u32[]{:S(2)}) collective-permute-start(f32[512,128]{1,0:T(8,128)S(1)} %shard_map.107.part_ref), channel_id=1, source_target_pairs={{0,16},{16,0},{1,17},{17,1},{2,18},{18,2},{3,19},{19,3},{4,20},{20... | collective-permute-start | bytes 786440 | tf_op jit(solution)/shard_map/ppermute | solution.py:278

commit v15 on v14

--- a/solution.py
+++ b/solution.py
@@ -288,15 +288,9 @@
     near = [(at(k, 0), at(k, 1)) for k in (1, 2, 3)] + [(at(k, 1), at(k, 2)) for k in (2, 3)]
     far = [(at(k, 0), at(k, 2)) for k in (1, 2, 3)] + [(at(3, 2), at(3, 1))]
     shift = rows * cols
-    pairs = near + [(a + shift, b + shift) for a, b in far]
-    for k in range(2 * rows):
-        here = range(k * cols, (k + 1) * cols)
-        rest = [a for a in here if a not in [p[0] for p in pairs]]
-        open_ends = [b for b in here if b not in [p[1] for p in pairs]]
-        stay = [a for a in rest if a in open_ends]
-        pairs = pairs + [(a, a) for a in stay]
-        pairs = pairs + list(zip([a for a in rest if a not in stay], [b for b in open_ends if b not in stay]))
-    sent = lax.ppermute(top_factor, ("leaf", "row", "col"), pairs)
+    sent = lax.ppermute(
+        top_factor, ("leaf", "row", "col"), near + [(a + shift, b + shift) for a, b in far]
+    )
     child_sol, keep, send = call(
         child_kernel,
         [live, child_rhs, child_diag, child_off, targets],

time: 64.7 us -> 64.8 us (level)
  starting transfers between devices: 24.1 us -> 25.3 us
  waiting for transfers between devices: 27.3 us -> 26.4 us
    ppermute x3, starting transfers between devices: 10.8 us -> 12.8 us  [swap(): return lax.ppermute(value, 'leaf', [(0, 1), (1, 0)])]
    ppermute x1, waiting for transfers between devices: 1.88 us -> 0.01 us  [central(): lax.ppermute(top_factor, ('leaf', 'row', 'col'), near + [(a + shift, b +...]
    ppermute x6, waiting for transfers between devices: 6.01 us -> 6.99 us  [along_col(): return lax.ppermute(value, 'col', pairs + list(zip(rest, open_ends)))]
    ppermute x1, starting transfers between devices: 2.08 us -> 1.29 us  [central(): lax.ppermute(top_factor, ('leaf', 'row', 'col'), near + [(a + shift, b +...]
  transfers between devices with their start and end apart: 18 -> 18, of which waited for: 13 -> 12; matrix products, arithmetic and copies ran while one was open for 0% -> 0% of each run, Pallas kernels for 15% -> 15%
where the time goes in v15:
time: 64.8 us; the launch traced here: 64.1 us
  waiting for transfers between devices  26.4 us (41%)
  starting transfers between devices  25.3 us (39%)
  Pallas kernels  10.9 us (17%)
  between operations  0.83 us (1%)
    ppermute x8, waiting for transfers between devices, along_row(): return lax.ppermute(value, 'row', [(r, r ^ step) for r in range(rows)])  18.6 us
    ppermute x3, starting transfers between devices, swap(): return lax.ppermute(value, 'leaf', [(0, 1), (1, 0)])  12.8 us
    pallas_call x15, Pallas kernels, call(): pl.pallas_call(kernel, out_shape=[shape(i, out) for i, out in enumerate(o...  10.9 us
    ppermute x6, starting transfers between devices, along_col(): return lax.ppermute(value, 'col', pairs + list(zip(rest, open_ends)))  7.12 us
    ppermute x6, waiting for transfers between devices, along_col(): return lax.ppermute(value, 'col', pairs + list(zip(rest, open_ends)))  6.99 us
    ppermute x8, starting transfers between devices, along_row(): return lax.ppermute(value, 'row', [(r, r ^ step) for r in range(rows)])  4.06 us
  transfers between devices with their start and end apart: 18, of which 12 were waited for; matrix products, arithmetic and copies ran while one was open for 0% of the time, Pallas kernels for 15%

profile of v15, /device:TPU:15, one launch (start us, length us, event | category | flops | bytes accessed | tf_op | source)
XLA Modules:
  0.0 64.1 jit_solution(15469002692340865251)
XLA Ops:
  0.6 1.3 %collective-permute-start.8 = (f32[512,512]{1,0:T(8,128)}, f32[512,512]{1,0:T(8,128)S(1)}, u32[]{:S(2)}, u32[]{:S(2)}) collective-permute-start(f32[512,512]{1,0:T(8,128)} %own_ref.1), channel_id=1, source_target_pairs={{4,5},{8,9},{12,13},{9,10},{13,14},{20,22},{24,26},{28,30},{30,29}} | collective-permute-start | bytes 3145736 | tf_op jit(solution)/shard_map/ppermute | solution.py:291
  1.9 2.9 %shard_map.95 = (f32[2,256,256]{2,1,0:T(8,128)}, f32[128,512]{1,0:T(8,128)S(1)}, f32[136,512]{1,0:T(8,128)S(1)}) custom-call(s32[2]{0:T(128)} %live_hbm.1, f32[2,256,256]{2,1,0:T(8,128)} %rhs_hbm.1, f32[2,256,256]{2,1,0:T(8,128)} %diag_hbm.1, f32[2,256,256]{2,1,0:T(8,128)} %off_hbm.1, s32[2,256]{1,0:T(2,128)} %tgt_hbm.1), custom_call_target="tpu_custom_call" | custom-call | bytes 1574920 | tf_op jit(solution)/shard_map/pallas_call | solution.py:251
  4.9 2.9 %collective-permute-start = (f32[136,512]{1,0:T(8,128)S(1)}, f32[136,512]{1,0:T(8,128)S(1)}, u32[]{:S(2)}, u32[]{:S(2)}) collective-permute-start(f32[136,512]{1,0:T(8,128)S(1)} %get-tuple-element.26.send_ref), channel_id=1, source_target_pairs={{0,16},{16,0},{1,17},{17,1},{2,18},{18,2},{3,19},{19,3},{4,20},{20... | collective-permute-start | bytes 835592 | tf_op jit(solution)/shard_map/ppermute | solution.py:278
  7.8 0.8 %shard_map.97 = (f32[128,512]{1,0:T(8,128)S(1)}, f32[128,512]{1,0:T(8,128)S(1)}, f32[128,512]{1,0:T(8,128)S(1)}, f32[128,512]{1,0:T(8,128)S(1)}) custom-call(f32[128,512]{1,0:T(8,128)S(1)} %get-tuple-element.27.keep_ref, f32[136,512]{1,0:T(8,128)S(1)} %get-tuple-element.26.send_ref), custom_call_target="tpu_custom_call" | custom-call | bytes 540672 | tf_op jit(solution)/shard_map/pallas_call | solution.py:251
  8.6 0.4 collective-permute-done.recv_ref
  9.0 0.8 %shard_map.98 = (f32[128,512]{1,0:T(8,128)S(1)}, f32[128,512]{1,0:T(8,128)S(1)}, f32[128,512]{1,0:T(8,128)S(1)}, f32[128,512]{1,0:T(8,128)S(1)}) custom-call(f32[136,512]{1,0:T(8,128)S(1)} %collective-permute-done.recv_ref, f32[128,512]{1,0:T(8,128)S(1)} %get-tuple-element.28.refs_0_, f32[128,512]{1,0:T(8,128)S(1)} %get-tuple-element.29.refs_1_, ...), custom_call_target="tpu_custom_call" | custom-call | bytes 1327104 | tf_op jit(solution)/shard_map/pallas_call | solution.py:251
  9.8 0.3 collective-permute-start.1
  10.1 0.0 collective-permute-start.2
  10.1 2.4 %collective-permute-start.3 = (f32[128,512]{1,0:T(8,128)S(1)}, f32[128,512]{1,0:T(8,128)S(1)}, u32[]{:S(2)}, u32[]{:S(2)}) collective-permute-start(f32[128,512]{1,0:T(8,128)S(1)} %get-tuple-element.35), channel_id=1, source_target_pairs={{0,12},{4,8},{8,4},{12,0},{1,13},{5,9},{9,5},{13,1},{2,14},{6,10},... | collective-permute-start | bytes 786440 | tf_op jit(solution)/shard_map/ppermute | solution.py:281
  12.5 4.9 %collective-permute-done.1.b_ref = f32[128,512]{1,0:T(8,128)S(1)} collective-permute-done((f32[128,512]{1,0:T(8,128)S(1)}, f32[128,512]{1,0:T(8,128)S(1)}, u32[]{:S(2)}, u32[]{:S(2)}) %collective-permute-start.1) | collective-permute-done | bytes 262176 | tf_op jit(solution)/shard_map/ppermute | solution.py:281
  17.4 5.5 %collective-permute-done.2.c_ref = f32[128,512]{1,0:T(8,128)S(1)} collective-permute-done((f32[128,512]{1,0:T(8,128)S(1)}, f32[128,512]{1,0:T(8,128)S(1)}, u32[]{:S(2)}, u32[]{:S(2)}) %collective-permute-start.2) | collective-permute-done | bytes 262176 | tf_op jit(solution)/shard_map/ppermute | solution.py:281
  22.9 0.0 collective-permute-done.3.d_ref
  22.9 0.1 shard_map.99
  23.0 1.0 %collective-permute-start.4 = (f32[64,512]{1,0:T(8,128)S(1)}, f32[64,512]{1,0:T(8,128)S(1)}, u32[]{:S(2)}, u32[]{:S(2)}) collective-permute-start(f32[64,512]{1,0:T(8,128)S(1)} %get-tuple-element.36.a_ref), channel_id=1, source_target_pairs={{0,2},{3,1},{1,0},{2,3},{4,6},{7,5},{5,4},{6,7},{8,10},{11,9},{9,8... | collective-permute-start | bytes 393224 | tf_op jit(solution)/shard_map/ppermute | solution.py:286
  24.0 1.9 %collective-permute-start.6 = (f32[64,512]{1,0:T(8,128)S(1)}, f32[64,512]{1,0:T(8,128)S(1)}, u32[]{:S(2)}, u32[]{:S(2)}) collective-permute-start(f32[64,512]{1,0:T(8,128)S(1)} %get-tuple-element.37), channel_id=1, source_target_pairs={{1,2},{2,1},{0,0},{3,3},{5,6},{6,5},{4,4},{7,7},{9,10},{10,9},{8,8... | collective-permute-start | bytes 393224 | tf_op jit(solution)/shard_map/ppermute | solution.py:286
  25.9 0.1 collective-permute-start.5
  26.0 0.3 shard_map.96
  26.3 0.0 collective-permute-done.8.sent_ref
  26.4 5.6 %collective-permute-start.9 = (f32[512,512]{1,0:T(8,128)S(1)}, f32[512,512]{1,0:T(8,128)S(1)}, u32[]{:S(2)}, u32[]{:S(2)}) collective-permute-start(f32[512,512]{1,0:T(8,128)S(1)} %collective-permute-done.8.sent_ref), channel_id=1, source_target_pairs={{0,16},{16,0},{1,17},{17,1},{2,18},{18,2},{3,19},{19,3},{4,20},{20... | collective-permute-start | bytes 3145736 | tf_op jit(solution)/shard_map/ppermute | solution.py:278
  31.9 0.0 collective-permute-done.4.b_ref
  31.9 0.8 %collective-permute-done.6.d_ref = f32[64,512]{1,0:T(8,128)S(1)} collective-permute-done((f32[64,512]{1,0:T(8,128)S(1)}, f32[64,512]{1,0:T(8,128)S(1)}, u32[]{:S(2)}, u32[]{:S(2)}) %collective-permute-start.6) | collective-permute-done | bytes 131104 | tf_op jit(solution)/shard_map/ppermute | solution.py:286
  32.8 1.7 %collective-permute-done.5.c_ref = f32[64,512]{1,0:T(8,128)S(1)} collective-permute-done((f32[64,512]{1,0:T(8,128)S(1)}, f32[64,512]{1,0:T(8,128)S(1)}, u32[]{:S(2)}, u32[]{:S(2)}) %collective-permute-start.5) | collective-permute-done | bytes 131104 | tf_op jit(solution)/shard_map/ppermute | solution.py:286
  34.5 0.3 shard_map.100.given_ref
  34.8 0.3 collective-permute-start.7
  35.1 0.0 collective-permute-start.10
  35.1 0.0 collective-permute-done.9.other_ref
  35.1 0.6 copy-done.1
  35.7 3.4 %shard_map.101 = (bf16[512,512]{1,0:T(8,128)(2,1)S(1)}, bf16[512,512]{1,0:T(8,128)(2,1)S(1)}, bf16[512,512]{1,0:T(8,128)(2,1)S(1)}, bf16[512,512]{1,0:T(8,128)(2...) custom-call(f32[512,512]{1,0:T(8,128)S(1)} %copy-done.1, ...), custom_call_target="tpu_custom_call" | custom-call | bytes 5242880 | tf_op jit(solution)/shard_map/pallas_call | solution.py:251
  39.1 0.3 collective-permute-done.7.refs_0_
  39.4 0.3 collective-permute-start.11
  39.7 0.0 collective-permute-done.10.refs_0_
  39.7 4.4 %collective-permute-done.11.refs_0_ = f32[64,512]{1,0:T(8,128)S(1)} collective-permute-done((f32[64,512]{1,0:T(8,128)S(1)}, f32[64,512]{1,0:T(8,128)S(1)}, u32[]{:S(2)}, u32[]{:S(2)}) %collective-permute-start.11) | collective-permute-done | bytes 131104 | tf_op jit(solution)/shard_map/ppermute | solution.py:281
  44.2 0.6 collective-permute-start.13
  44.8 0.0 collective-permute-start.12
  44.8 0.3 shard_map.105.given_ref
  45.1 2.9 %collective-permute-done.13.refs_3_ = f32[64,512]{1,0:T(8,128)S(1)} collective-permute-done((f32[64,512]{1,0:T(8,128)S(1)}, f32[64,512]{1,0:T(8,128)S(1)}, u32[]{:S(2)}, u32[]{:S(2)}) %collective-permute-start.13) | collective-permute-done | bytes 131104 | tf_op jit(solution)/shard_map/ppermute | solution.py:281
  48.1 0.5 collective-permute-done.12.refs_0_
  48.6 0.5 shard_map.106.x_ref
  49.1 0.1 collective-permute-start.16
  49.2 1.5 %collective-permute-start.15 = (f32[64,512]{1,0:T(8,128)S(1)}, f32[64,512]{1,0:T(8,128)S(1)}, u32[]{:S(2)}, u32[]{:S(2)}) collective-permute-start(f32[64,512]{1,0:T(8,128)S(1)} %shard_map.106.x_ref), channel_id=1, source_target_pairs={{1,0},{2,3},{0,1},{3,2},{5,4},{6,7},{4,5},{7,6},{9,8},{10,11},{8,9... | collective-permute-start | bytes 393224 | tf_op jit(solution)/shard_map/ppermute | solution.py:286
  50.6 2.6 %collective-permute-start.14 = (f32[64,512]{1,0:T(8,128)S(1)}, f32[64,512]{1,0:T(8,128)S(1)}, u32[]{:S(2)}, u32[]{:S(2)}) collective-permute-start(f32[64,512]{1,0:T(8,128)S(1)} %shard_map.106.x_ref), channel_id=1, source_target_pairs={{1,2},{2,1},{0,0},{3,3},{5,6},{6,5},{4,4},{7,7},{9,10},{10,9},{8,8... | collective-permute-start | bytes 393224 | tf_op jit(solution)/shard_map/ppermute | solution.py:286
  53.2 1.1 %collective-permute-done.15.a_ref = f32[64,512]{1,0:T(8,128)S(1)} collective-permute-done((f32[64,512]{1,0:T(8,128)S(1)}, f32[64,512]{1,0:T(8,128)S(1)}, u32[]{:S(2)}, u32[]{:S(2)}) %collective-permute-start.15) | collective-permute-done | bytes 131104 | tf_op jit(solution)/shard_map/ppermute | solution.py:286
  54.4 3.3 %collective-permute-done.14.b_ref = f32[64,512]{1,0:T(8,128)S(1)} collective-permute-done((f32[64,512]{1,0:T(8,128)S(1)}, f32[64,512]{1,0:T(8,128)S(1)}, u32[]{:S(2)}, u32[]{:S(2)}) %collective-permute-start.14) | collective-permute-done | bytes 131104 | tf_op jit(solution)/shard_map/ppermute | solution.py:286
  57.7 0.1 shard_map.107.part_ref
  57.9 4.3 %collective-permute-start.17 = (f32[512,128]{1,0:T(8,128)S(1)}, f32[512,128]{1,0:T(8,128)S(1)}, u32[]{:S(2)}, u32[]{:S(2)}) collective-permute-start(f32[512,128]{1,0:T(8,128)S(1)} %shard_map.107.part_ref), channel_id=1, source_target_pairs={{0,16},{16,0},{1,17},{17,1},{2,18},{18,2},{3,19},{19,3},{4,20},{20... | collective-permute-start | bytes 786440 | tf_op jit(solution)/shard_map/ppermute | solution.py:278
  62.2 0.7 %shard_map.108.refs_0_ = f32[512,256]{1,0:T(8,128)} custom-call(f32[512,128]{1,0:T(8,128)S(1)} %shard_map.107.part_ref), custom_call_target="tpu_custom_call" | custom-call | bytes 262144 | tf_op jit(solution)/shard_map/pallas_call | solution.py:251
  62.9 0.4 collective-permute-done.17.part_ref
  63.4 0.7 %shard_map.109 = f32[512,256]{1,0:T(8,128)} custom-call(f32[512,128]{1,0:T(8,128)S(1)} %collective-permute-done.17.part_ref, f32[512,256]{1,0:T(8,128)} %shard_map.108.refs_0_), custom_call_target="tpu_custom_call", output_to_operand_aliasing={{}: (1, {})} | custom-call | bytes 786432 | tf_op jit(solution)/shard_map/pallas_call | solution.py:251
  (9 shorter events, 0.0 us)
Async XLA Ops:
  0.6 25.7 %collective-permute-start.8 = (f32[512,512]{1,0:T(8,128)}, f32[512,512]{1,0:T(8,128)S(1)}, u32[]{:S(2)}, u32[]{:S(2)}) collective-permute-start(f32[512,512]{1,0:T(8,128)} %own_ref.1), channel_id=1, source_target_pairs={{4,5},{8,9},{12,13},{9,10},{13,14},{20,22},{24,26},{28,30},{30,29}} | collective-permute-start | bytes 3145736 | tf_op jit(solution)/shard_map/ppermute | solution.py:291
  4.9 4.1 %collective-permute-start = (f32[136,512]{1,0:T(8,128)S(1)}, f32[136,512]{1,0:T(8,128)S(1)}, u32[]{:S(2)}, u32[]{:S(2)}) collective-permute-start(f32[136,512]{1,0:T(8,128)S(1)} %get-tuple-element.26.send_ref), channel_id=1, source_target_pairs={{0,16},{16,0},{1,17},{17,1},{2,18},{18,2},{3,19},{19,3},{4,20},{20... | collective-permute-start | bytes 835592 | tf_op jit(solution)/shard_map/ppermute | solution.py:278
  9.0 17.0 %copy-start = (f32[512,512]{1,0:T(8,128)S(1)}, f32[512,512]{1,0:T(8,128)}, u32[]{:S(2)}) copy-start(f32[512,512]{1,0:T(8,128)} %diag_ref.1) | copy-start | bytes 3145732
  9.8 7.6 %collective-permute-start.1 = (f32[128,512]{1,0:T(8,128)S(1)}, f32[128,512]{1,0:T(8,128)S(1)}, u32[]{:S(2)}, u32[]{:S(2)}) collective-permute-start(f32[128,512]{1,0:T(8,128)S(1)} %get-tuple-element.33), channel_id=1, source_target_pairs={{0,4},{4,0},{8,12},{12,8},{1,5},{5,1},{9,13},{13,9},{2,6},{6,2},{1... | collective-permute-start | bytes 786440 | tf_op jit(solution)/shard_map/ppermute | solution.py:281
  10.1 12.8 %collective-permute-start.2 = (f32[128,512]{1,0:T(8,128)S(1)}, f32[128,512]{1,0:T(8,128)S(1)}, u32[]{:S(2)}, u32[]{:S(2)}) collective-permute-start(f32[128,512]{1,0:T(8,128)S(1)} %get-tuple-element.34), channel_id=1, source_target_pairs={{0,8},{4,12},{8,0},{12,4},{1,9},{5,13},{9,1},{13,5},{2,10},{6,14},... | collective-permute-start | bytes 786440 | tf_op jit(solution)/shard_map/ppermute | solution.py:281
  10.1 12.8 %collective-permute-start.3 = (f32[128,512]{1,0:T(8,128)S(1)}, f32[128,512]{1,0:T(8,128)S(1)}, u32[]{:S(2)}, u32[]{:S(2)}) collective-permute-start(f32[128,512]{1,0:T(8,128)S(1)} %get-tuple-element.35), channel_id=1, source_target_pairs={{0,12},{4,8},{8,4},{12,0},{1,13},{5,9},{9,5},{13,1},{2,14},{6,10},... | collective-permute-start | bytes 786440 | tf_op jit(solution)/shard_map/ppermute | solution.py:281
  22.9 3.1 %copy-start.2 = (f32[512,256]{1,0:T(8,128)S(1)}, f32[512,256]{1,0:T(8,128)}, u32[]{:S(2)}) copy-start(f32[512,256]{1,0:T(8,128)} %rhs_ref.1) | copy-start | bytes 1572868
  23.0 8.9 %collective-permute-start.4 = (f32[64,512]{1,0:T(8,128)S(1)}, f32[64,512]{1,0:T(8,128)S(1)}, u32[]{:S(2)}, u32[]{:S(2)}) collective-permute-start(f32[64,512]{1,0:T(8,128)S(1)} %get-tuple-element.36.a_ref), channel_id=1, source_target_pairs={{0,2},{3,1},{1,0},{2,3},{4,6},{7,5},{5,4},{6,7},{8,10},{11,9},{9,8... | collective-permute-start | bytes 393224 | tf_op jit(solution)/shard_map/ppermute | solution.py:286
  24.0 8.8 %collective-permute-start.6 = (f32[64,512]{1,0:T(8,128)S(1)}, f32[64,512]{1,0:T(8,128)S(1)}, u32[]{:S(2)}, u32[]{:S(2)}) collective-permute-start(f32[64,512]{1,0:T(8,128)S(1)} %get-tuple-element.37), channel_id=1, source_target_pairs={{1,2},{2,1},{0,0},{3,3},{5,6},{6,5},{4,4},{7,7},{9,10},{10,9},{8,8... | collective-permute-start | bytes 393224 | tf_op jit(solution)/shard_map/ppermute | solution.py:286
  25.9 8.5 %collective-permute-start.5 = (f32[64,512]{1,0:T(8,128)S(1)}, f32[64,512]{1,0:T(8,128)S(1)}, u32[]{:S(2)}, u32[]{:S(2)}) collective-permute-start(f32[64,512]{1,0:T(8,128)S(1)} %get-tuple-element.37), channel_id=1, source_target_pairs={{0,1},{3,2},{1,0},{2,3},{4,5},{7,6},{5,4},{6,7},{8,9},{11,10},{9,8... | collective-permute-start | bytes 393224 | tf_op jit(solution)/shard_map/ppermute | solution.py:286
  26.4 8.8 %collective-permute-start.9 = (f32[512,512]{1,0:T(8,128)S(1)}, f32[512,512]{1,0:T(8,128)S(1)}, u32[]{:S(2)}, u32[]{:S(2)}) collective-permute-start(f32[512,512]{1,0:T(8,128)S(1)} %collective-permute-done.8.sent_ref), channel_id=1, source_target_pairs={{0,16},{16,0},{1,17},{17,1},{2,18},{18,2},{3,19},{19,3},{4,20},{20... | collective-permute-start | bytes 3145736 | tf_op jit(solution)/shard_map/ppermute | solution.py:278
  34.5 1.2 %copy-start.1 = (f32[512,512]{1,0:T(8,128)S(1)}, f32[512,512]{1,0:T(8,128)}, u32[]{:S(2)}) copy-start(f32[512,512]{1,0:T(8,128)} %own_ref.1) | copy-start | bytes 3145732
  34.8 4.6 %collective-permute-start.7 = (f32[64,512]{1,0:T(8,128)S(1)}, f32[64,512]{1,0:T(8,128)S(1)}, u32[]{:S(2)}, u32[]{:S(2)}) collective-permute-start(f32[64,512]{1,0:T(8,128)S(1)} %shard_map.100.given_ref), channel_id=1, source_target_pairs={{0,4},{4,0},{8,12},{12,8},{1,5},{5,1},{9,13},{13,9},{2,6},{6,2},{1... | collective-permute-start | bytes 393224 | tf_op jit(solution)/shard_map/ppermute | solution.py:281
  35.1 4.6 %collective-permute-start.10 = (f32[64,512]{1,0:T(8,128)S(1)}, f32[64,512]{1,0:T(8,128)S(1)}, u32[]{:S(2)}, u32[]{:S(2)}) collective-permute-start(f32[64,512]{1,0:T(8,128)S(1)} %shard_map.100.given_ref), channel_id=1, source_target_pairs={{0,8},{4,12},{8,0},{12,4},{1,9},{5,13},{9,1},{13,5},{2,10},{6,14},... | collective-permute-start | bytes 393224 | tf_op jit(solution)/shard_map/ppermute | solution.py:281
  39.4 4.8 %collective-permute-start.11 = (f32[64,512]{1,0:T(8,128)S(1)}, f32[64,512]{1,0:T(8,128)S(1)}, u32[]{:S(2)}, u32[]{:S(2)}) collective-permute-start(f32[64,512]{1,0:T(8,128)S(1)} %shard_map.102.given_ref), channel_id=1, source_target_pairs={{0,12},{4,8},{8,4},{12,0},{1,13},{5,9},{9,5},{13,1},{2,14},{6,10},... | collective-permute-start | bytes 393224 | tf_op jit(solution)/shard_map/ppermute | solution.py:281
  44.2 3.9 %collective-permute-start.13 = (f32[64,512]{1,0:T(8,128)S(1)}, f32[64,512]{1,0:T(8,128)S(1)}, u32[]{:S(2)}, u32[]{:S(2)}) collective-permute-start(f32[64,512]{1,0:T(8,128)S(1)} %shard_map.104.given_ref), channel_id=1, source_target_pairs={{0,4},{4,0},{8,12},{12,8},{1,5},{5,1},{9,13},{13,9},{2,6},{6,2},{1... | collective-permute-start | bytes 393224 | tf_op jit(solution)/shard_map/ppermute | solution.py:281
  44.8 3.8 %collective-permute-start.12 = (f32[64,512]{1,0:T(8,128)S(1)}, f32[64,512]{1,0:T(8,128)S(1)}, u32[]{:S(2)}, u32[]{:S(2)}) collective-permute-start(f32[64,512]{1,0:T(8,128)S(1)} %shard_map.104.given_ref), channel_id=1, source_target_pairs={{0,8},{4,12},{8,0},{12,4},{1,9},{5,13},{9,1},{13,5},{2,10},{6,14},... | collective-permute-start | bytes 393224 | tf_op jit(solution)/shard_map/ppermute | solution.py:281
  49.1 4.1 %collective-permute-start.16 = (f32[64,512]{1,0:T(8,128)S(1)}, f32[64,512]{1,0:T(8,128)S(1)}, u32[]{:S(2)}, u32[]{:S(2)}) collective-permute-start(f32[64,512]{1,0:T(8,128)S(1)} %shard_map.106.x_ref), channel_id=1, source_target_pairs={{1,3},{2,0},{0,1},{3,2},{5,7},{6,4},{4,5},{7,6},{9,11},{10,8},{8,9... | collective-permute-start | bytes 393224 | tf_op jit(solution)/shard_map/ppermute | solution.py:286
  49.2 5.2 %collective-permute-start.15 = (f32[64,512]{1,0:T(8,128)S(1)}, f32[64,512]{1,0:T(8,128)S(1)}, u32[]{:S(2)}, u32[]{:S(2)}) collective-permute-start(f32[64,512]{1,0:T(8,128)S(1)} %shard_map.106.x_ref), channel_id=1, source_target_pairs={{1,0},{2,3},{0,1},{3,2},{5,4},{6,7},{4,5},{7,6},{9,8},{10,11},{8,9... | collective-permute-start | bytes 393224 | tf_op jit(solution)/shard_map/ppermute | solution.py:286
  50.6 7.1 %collective-permute-start.14 = (f32[64,512]{1,0:T(8,128)S(1)}, f32[64,512]{1,0:T(8,128)S(1)}, u32[]{:S(2)}, u32[]{:S(2)}) collective-permute-start(f32[64,512]{1,0:T(8,128)S(1)} %shard_map.106.x_ref), channel_id=1, source_target_pairs={{1,2},{2,1},{0,0},{3,3},{5,6},{6,5},{4,4},{7,7},{9,10},{10,9},{8,8... | collective-permute-start | bytes 393224 | tf_op jit(solution)/shard_map/ppermute | solution.py:286
  57.9 5.5 %collective-permute-start.17 = (f32[512,128]{1,0:T(8,128)S(1)}, f32[512,128]{1,0:T(8,128)S(1)}, u32[]{:S(2)}, u32[]{:S(2)}) collective-permute-start(f32[512,128]{1,0:T(8,128)S(1)} %shard_map.107.part_ref), channel_id=1, source_target_pairs={{0,16},{16,0},{1,17},{17,1},{2,18},{18,2},{3,19},{19,3},{4,20},{20... | collective-permute-start | bytes 786440 | tf_op jit(solution)/shard_map/ppermute | solution.py:278

commit v16 on v15

--- a/solution.py
+++ b/solution.py
@@ -222,7 +222,7 @@
         out_ref[...] = left
 
 
-def half_kernel(b_ref, a_ref, c_ref, x_ref, out_ref):
+def half_kernel(a_ref, b_ref, c_ref, x_ref, out_ref):
     _, _, z = place()
     x, a, b, c = x_ref[...], a_ref[...], b_ref[...], c_ref[...]
     low = jnp.where(z == 0, a, jnp.where(z == 1, x, jnp.where(z == 2, b, c)))
@@ -304,7 +304,7 @@
     )
     sums = call(own_kernel, [keep, send], [(half, size)] * rows)
     sums = call(other_kernel, [swap(send)] + sums, [(half, size)] * rows)
-    got = [along_row(sums[s], s) for s in (1, 2, 3)]
+    got = [along_row(sums[s], s) for s in (3, 1, 2)]
     rhs_piece, diag_high, diag_low = call(
         turn_kernel, [top_rhs, top_diag], [shape, block, block], [(half, size)]
     )
@@ -338,7 +338,7 @@
     both = along_col(x, [(1, 2), (2, 1)])
     step = along_col(x, [(1, 0), (2, 3)])
     over = along_col(x, [(1, 3), (2, 0)])
-    (own,) = call(half_kernel, [both, step, over, x], [(size, half)])
+    (own,) = call(half_kernel, [step, both, over, x], [(size, half)])
     (top_sol,) = call(
         functools.partial(write_kernel, True), [own], [top_rhs.shape], [dma(())], outs_outside=(0,)
     )

time: 64.8 us -> 64.8 us (level)
  starting transfers between devices: 25.3 us -> 20.9 us
  waiting for transfers between devices: 26.4 us -> 30.4 us
    ppermute x3, starting transfers between devices: 12.8 us -> 9.62 us  [swap(): return lax.ppermute(value, 'leaf', [(0, 1), (1, 0)])]
    ppermute x6, waiting for transfers between devices: 6.99 us -> 9.29 us  [along_col(): return lax.ppermute(value, 'col', pairs + list(zip(rest, open_ends)))]
    ppermute x8, waiting for transfers between devices: 18.6 us -> 20.2 us  [along_row(): return lax.ppermute(value, 'row', [(r, r ^ step) for r in range(rows)])]
    ppermute x6, starting transfers between devices: 7.12 us -> 5.95 us  [along_col(): return lax.ppermute(value, 'col', pairs + list(zip(rest, open_ends)))]
  transfers between devices with their start and end apart: 18 -> 18, of which waited for: 12 -> 15; matrix products, arithmetic and copies ran while one was open for 0% -> 0% of each run, Pallas kernels for 15% -> 15%
where the time goes in v16:
time: 64.8 us; the launch traced here: 63.6 us
  waiting for transfers between devices  30.4 us (47%)
  starting transfers between devices  20.9 us (32%)
  Pallas kernels  10.9 us (17%)
  between operations  0.83 us (1%)
    ppermute x8, waiting for transfers between devices, along_row(): return lax.ppermute(value, 'row', [(r, r ^ step) for r in range(rows)])  20.2 us
    pallas_call x15, Pallas kernels, call(): pl.pallas_call(kernel, out_shape=[shape(i, out) for i, out in enumerate(o...  10.9 us
    ppermute x3, starting transfers between devices, swap(): return lax.ppermute(value, 'leaf', [(0, 1), (1, 0)])  9.62 us
    ppermute x6, waiting for transfers between devices, along_col(): return lax.ppermute(value, 'col', pairs + list(zip(rest, open_ends)))  9.29 us
    ppermute x6, starting transfers between devices, along_col(): return lax.ppermute(value, 'col', pairs + list(zip(rest, open_ends)))  5.95 us
    ppermute x8, starting transfers between devices, along_row(): return lax.ppermute(value, 'row', [(r, r ^ step) for r in range(rows)])  4.08 us
  transfers between devices with their start and end apart: 18, of which 15 were waited for; matrix products, arithmetic and copies ran while one was open for 0% of the time, Pallas kernels for 15%

profile of v16, /device:TPU:15, one launch (start us, length us, event | category | flops | bytes accessed | tf_op | source)
XLA Modules:
  0.0 63.6 jit_solution(1227400142400752245)
XLA Ops:
  0.6 1.3 %collective-permute-start.8 = (f32[512,512]{1,0:T(8,128)}, f32[512,512]{1,0:T(8,128)S(1)}, u32[]{:S(2)}, u32[]{:S(2)}) collective-permute-start(f32[512,512]{1,0:T(8,128)} %own_ref.1), channel_id=1, source_target_pairs={{4,5},{8,9},{12,13},{9,10},{13,14},{20,22},{24,26},{28,30},{30,29}} | collective-permute-start | bytes 3145736 | tf_op jit(solution)/shard_map/ppermute | solution.py:291
  1.9 2.9 %shard_map.95 = (f32[2,256,256]{2,1,0:T(8,128)}, f32[128,512]{1,0:T(8,128)S(1)}, f32[136,512]{1,0:T(8,128)S(1)}) custom-call(s32[2]{0:T(128)} %live_hbm.1, f32[2,256,256]{2,1,0:T(8,128)} %rhs_hbm.1, f32[2,256,256]{2,1,0:T(8,128)} %diag_hbm.1, f32[2,256,256]{2,1,0:T(8,128)} %off_hbm.1, s32[2,256]{1,0:T(2,128)} %tgt_hbm.1), custom_call_target="tpu_custom_call" | custom-call | bytes 1574920 | tf_op jit(solution)/shard_map/pallas_call | solution.py:251
  4.9 2.9 %collective-permute-start = (f32[136,512]{1,0:T(8,128)S(1)}, f32[136,512]{1,0:T(8,128)S(1)}, u32[]{:S(2)}, u32[]{:S(2)}) collective-permute-start(f32[136,512]{1,0:T(8,128)S(1)} %get-tuple-element.26.send_ref), channel_id=1, source_target_pairs={{0,16},{16,0},{1,17},{17,1},{2,18},{18,2},{3,19},{19,3},{4,20},{20... | collective-permute-start | bytes 835592 | tf_op jit(solution)/shard_map/ppermute | solution.py:278
  7.8 0.8 %shard_map.97 = (f32[128,512]{1,0:T(8,128)S(1)}, f32[128,512]{1,0:T(8,128)S(1)}, f32[128,512]{1,0:T(8,128)S(1)}, f32[128,512]{1,0:T(8,128)S(1)}) custom-call(f32[128,512]{1,0:T(8,128)S(1)} %get-tuple-element.27.keep_ref, f32[136,512]{1,0:T(8,128)S(1)} %get-tuple-element.26.send_ref), custom_call_target="tpu_custom_call" | custom-call | bytes 540672 | tf_op jit(solution)/shard_map/pallas_call | solution.py:251
  8.6 0.4 collective-permute-done.recv_ref
  9.0 0.8 %shard_map.98 = (f32[128,512]{1,0:T(8,128)S(1)}, f32[128,512]{1,0:T(8,128)S(1)}, f32[128,512]{1,0:T(8,128)S(1)}, f32[128,512]{1,0:T(8,128)S(1)}) custom-call(f32[136,512]{1,0:T(8,128)S(1)} %collective-permute-done.recv_ref, f32[128,512]{1,0:T(8,128)S(1)} %get-tuple-element.28.refs_0_, f32[128,512]{1,0:T(8,128)S(1)} %get-tuple-element.29.refs_1_, ...), custom_call_target="tpu_custom_call" | custom-call | bytes 1327104 | tf_op jit(solution)/shard_map/pallas_call | solution.py:251
  9.8 0.1 collective-permute-start.1
  9.8 0.3 collective-permute-start.2
  10.2 2.3 %collective-permute-start.3 = (f32[128,512]{1,0:T(8,128)S(1)}, f32[128,512]{1,0:T(8,128)S(1)}, u32[]{:S(2)}, u32[]{:S(2)}) collective-permute-start(f32[128,512]{1,0:T(8,128)S(1)} %get-tuple-element.35), channel_id=1, source_target_pairs={{0,8},{4,12},{8,0},{12,4},{1,9},{5,13},{9,1},{13,5},{2,10},{6,14},... | collective-permute-start | bytes 786440 | tf_op jit(solution)/shard_map/ppermute | solution.py:281
  12.5 5.8 %collective-permute-done.1.b_ref = f32[128,512]{1,0:T(8,128)S(1)} collective-permute-done((f32[128,512]{1,0:T(8,128)S(1)}, f32[128,512]{1,0:T(8,128)S(1)}, u32[]{:S(2)}, u32[]{:S(2)}) %collective-permute-start.1) | collective-permute-done | bytes 262176 | tf_op jit(solution)/shard_map/ppermute | solution.py:281
  18.3 3.8 %collective-permute-done.2.c_ref = f32[128,512]{1,0:T(8,128)S(1)} collective-permute-done((f32[128,512]{1,0:T(8,128)S(1)}, f32[128,512]{1,0:T(8,128)S(1)}, u32[]{:S(2)}, u32[]{:S(2)}) %collective-permute-start.2) | collective-permute-done | bytes 262176 | tf_op jit(solution)/shard_map/ppermute | solution.py:281
  22.1 2.5 %collective-permute-done.3.d_ref = f32[128,512]{1,0:T(8,128)S(1)} collective-permute-done((f32[128,512]{1,0:T(8,128)S(1)}, f32[128,512]{1,0:T(8,128)S(1)}, u32[]{:S(2)}, u32[]{:S(2)}) %collective-permute-start.3) | collective-permute-done | bytes 262176 | tf_op jit(solution)/shard_map/ppermute | solution.py:281
  24.6 0.1 shard_map.99
  24.7 0.7 %collective-permute-start.4 = (f32[64,512]{1,0:T(8,128)S(1)}, f32[64,512]{1,0:T(8,128)S(1)}, u32[]{:S(2)}, u32[]{:S(2)}) collective-permute-start(f32[64,512]{1,0:T(8,128)S(1)} %get-tuple-element.36.a_ref), channel_id=1, source_target_pairs={{0,2},{3,1},{1,0},{2,3},{4,6},{7,5},{5,4},{6,7},{8,10},{11,9},{9,8... | collective-permute-start | bytes 393224 | tf_op jit(solution)/shard_map/ppermute | solution.py:286
  25.4 1.9 %collective-permute-start.6 = (f32[64,512]{1,0:T(8,128)S(1)}, f32[64,512]{1,0:T(8,128)S(1)}, u32[]{:S(2)}, u32[]{:S(2)}) collective-permute-start(f32[64,512]{1,0:T(8,128)S(1)} %get-tuple-element.37), channel_id=1, source_target_pairs={{1,2},{2,1},{0,0},{3,3},{5,6},{6,5},{4,4},{7,7},{9,10},{10,9},{8,8... | collective-permute-start | bytes 393224 | tf_op jit(solution)/shard_map/ppermute | solution.py:286
  27.3 0.1 collective-permute-start.5
  27.4 0.3 shard_map.96
  27.7 0.0 collective-permute-done.8.sent_ref
  27.7 1.7 %collective-permute-start.9 = (f32[512,512]{1,0:T(8,128)S(1)}, f32[512,512]{1,0:T(8,128)S(1)}, u32[]{:S(2)}, u32[]{:S(2)}) collective-permute-start(f32[512,512]{1,0:T(8,128)S(1)} %collective-permute-done.8.sent_ref), channel_id=1, source_target_pairs={{0,16},{16,0},{1,17},{17,1},{2,18},{18,2},{3,19},{19,3},{4,20},{20... | collective-permute-start | bytes 3145736 | tf_op jit(solution)/shard_map/ppermute | solution.py:278
  29.4 0.7 %collective-permute-done.4.b_ref = f32[64,512]{1,0:T(8,128)S(1)} collective-permute-done((f32[64,512]{1,0:T(8,128)S(1)}, f32[64,512]{1,0:T(8,128)S(1)}, u32[]{:S(2)}, u32[]{:S(2)}) %collective-permute-start.4) | collective-permute-done | bytes 131104 | tf_op jit(solution)/shard_map/ppermute | solution.py:286
  30.2 3.7 %collective-permute-done.6.d_ref = f32[64,512]{1,0:T(8,128)S(1)} collective-permute-done((f32[64,512]{1,0:T(8,128)S(1)}, f32[64,512]{1,0:T(8,128)S(1)}, u32[]{:S(2)}, u32[]{:S(2)}) %collective-permute-start.6) | collective-permute-done | bytes 131104 | tf_op jit(solution)/shard_map/ppermute | solution.py:286
  33.8 0.6 collective-permute-done.5.c_ref
  34.5 0.3 shard_map.100.given_ref
  34.8 0.3 collective-permute-start.7
  35.1 0.1 collective-permute-start.10
  35.1 0.0 collective-permute-done.9.other_ref
  35.1 0.6 copy-done.1
  35.7 3.4 %shard_map.101 = (bf16[512,512]{1,0:T(8,128)(2,1)S(1)}, bf16[512,512]{1,0:T(8,128)(2,1)S(1)}, bf16[512,512]{1,0:T(8,128)(2,1)S(1)}, bf16[512,512]{1,0:T(8,128)(2...) custom-call(f32[512,512]{1,0:T(8,128)S(1)} %copy-done.1, ...), custom_call_target="tpu_custom_call" | custom-call | bytes 5242880 | tf_op jit(solution)/shard_map/pallas_call | solution.py:251
  39.1 0.3 collective-permute-done.7.refs_0_
  39.4 0.3 collective-permute-start.11
  39.7 4.4 %collective-permute-done.11.refs_0_ = f32[64,512]{1,0:T(8,128)S(1)} collective-permute-done((f32[64,512]{1,0:T(8,128)S(1)}, f32[64,512]{1,0:T(8,128)S(1)}, u32[]{:S(2)}, u32[]{:S(2)}) %collective-permute-start.11) | collective-permute-done | bytes 131104 | tf_op jit(solution)/shard_map/ppermute | solution.py:281
  44.2 0.6 collective-permute-start.13
  44.8 0.1 collective-permute-start.12
  44.9 0.3 shard_map.105.given_ref
  45.2 2.9 %collective-permute-done.13.refs_3_ = f32[64,512]{1,0:T(8,128)S(1)} collective-permute-done((f32[64,512]{1,0:T(8,128)S(1)}, f32[64,512]{1,0:T(8,128)S(1)}, u32[]{:S(2)}, u32[]{:S(2)}) %collective-permute-start.13) | collective-permute-done | bytes 131104 | tf_op jit(solution)/shard_map/ppermute | solution.py:281
  48.1 0.5 collective-permute-done.12.refs_0_
  48.6 0.5 shard_map.106.x_ref
  49.1 0.1 collective-permute-start.16
  49.2 3.1 %collective-permute-start.15 = (f32[64,512]{1,0:T(8,128)S(1)}, f32[64,512]{1,0:T(8,128)S(1)}, u32[]{:S(2)}, u32[]{:S(2)}) collective-permute-start(f32[64,512]{1,0:T(8,128)S(1)} %shard_map.106.x_ref), channel_id=1, source_target_pairs={{1,2},{2,1},{0,0},{3,3},{5,6},{6,5},{4,4},{7,7},{9,10},{10,9},{8,8... | collective-permute-start | bytes 393224 | tf_op jit(solution)/shard_map/ppermute | solution.py:286
  52.3 0.1 collective-permute-start.14
  52.4 0.6 collective-permute-done.16.c_ref
  53.0 1.9 %collective-permute-done.15.b_ref = f32[64,512]{1,0:T(8,128)S(1)} collective-permute-done((f32[64,512]{1,0:T(8,128)S(1)}, f32[64,512]{1,0:T(8,128)S(1)}, u32[]{:S(2)}, u32[]{:S(2)}) %collective-permute-start.15) | collective-permute-done | bytes 131104 | tf_op jit(solution)/shard_map/ppermute | solution.py:286
  54.9 1.8 %collective-permute-done.14.a_ref = f32[64,512]{1,0:T(8,128)S(1)} collective-permute-done((f32[64,512]{1,0:T(8,128)S(1)}, f32[64,512]{1,0:T(8,128)S(1)}, u32[]{:S(2)}, u32[]{:S(2)}) %collective-permute-start.14) | collective-permute-done | bytes 131104 | tf_op jit(solution)/shard_map/ppermute | solution.py:286
  56.6 0.1 shard_map.107.part_ref
  56.8 5.0 %collective-permute-start.17 = (f32[512,128]{1,0:T(8,128)S(1)}, f32[512,128]{1,0:T(8,128)S(1)}, u32[]{:S(2)}, u32[]{:S(2)}) collective-permute-start(f32[512,128]{1,0:T(8,128)S(1)} %shard_map.107.part_ref), channel_id=1, source_target_pairs={{0,16},{16,0},{1,17},{17,1},{2,18},{18,2},{3,19},{19,3},{4,20},{20... | collective-permute-start | bytes 786440 | tf_op jit(solution)/shard_map/ppermute | solution.py:278
  61.8 0.7 %shard_map.108.refs_0_ = f32[512,256]{1,0:T(8,128)} custom-call(f32[512,128]{1,0:T(8,128)S(1)} %shard_map.107.part_ref), custom_call_target="tpu_custom_call" | custom-call | bytes 262144 | tf_op jit(solution)/shard_map/pallas_call | solution.py:251
  62.5 0.4 collective-permute-done.17.part_ref
  62.9 0.7 %shard_map.109 = f32[512,256]{1,0:T(8,128)} custom-call(f32[512,128]{1,0:T(8,128)S(1)} %collective-permute-done.17.part_ref, f32[512,256]{1,0:T(8,128)} %shard_map.108.refs_0_), custom_call_target="tpu_custom_call", output_to_operand_aliasing={{}: (1, {})} | custom-call | bytes 786432 | tf_op jit(solution)/shard_map/pallas_call | solution.py:251
  (9 shorter events, 0.0 us)
Async XLA Ops:
  0.6 27.1 %collective-permute-start.8 = (f32[512,512]{1,0:T(8,128)}, f32[512,512]{1,0:T(8,128)S(1)}, u32[]{:S(2)}, u32[]{:S(2)}) collective-permute-start(f32[512,512]{1,0:T(8,128)} %own_ref.1), channel_id=1, source_target_pairs={{4,5},{8,9},{12,13},{9,10},{13,14},{20,22},{24,26},{28,30},{30,29}} | collective-permute-start | bytes 3145736 | tf_op jit(solution)/shard_map/ppermute | solution.py:291
  4.9 4.1 %collective-permute-start = (f32[136,512]{1,0:T(8,128)S(1)}, f32[136,512]{1,0:T(8,128)S(1)}, u32[]{:S(2)}, u32[]{:S(2)}) collective-permute-start(f32[136,512]{1,0:T(8,128)S(1)} %get-tuple-element.26.send_ref), channel_id=1, source_target_pairs={{0,16},{16,0},{1,17},{17,1},{2,18},{18,2},{3,19},{19,3},{4,20},{20... | collective-permute-start | bytes 835592 | tf_op jit(solution)/shard_map/ppermute | solution.py:278
  9.0 18.4 %copy-start = (f32[512,512]{1,0:T(8,128)S(1)}, f32[512,512]{1,0:T(8,128)}, u32[]{:S(2)}) copy-start(f32[512,512]{1,0:T(8,128)} %diag_ref.1) | copy-start | bytes 3145732
  9.8 8.5 %collective-permute-start.1 = (f32[128,512]{1,0:T(8,128)S(1)}, f32[128,512]{1,0:T(8,128)S(1)}, u32[]{:S(2)}, u32[]{:S(2)}) collective-permute-start(f32[128,512]{1,0:T(8,128)S(1)} %get-tuple-element.33), channel_id=1, source_target_pairs={{0,12},{4,8},{8,4},{12,0},{1,13},{5,9},{9,5},{13,1},{2,14},{6,10},... | collective-permute-start | bytes 786440 | tf_op jit(solution)/shard_map/ppermute | solution.py:281
  9.8 12.3 %collective-permute-start.2 = (f32[128,512]{1,0:T(8,128)S(1)}, f32[128,512]{1,0:T(8,128)S(1)}, u32[]{:S(2)}, u32[]{:S(2)}) collective-permute-start(f32[128,512]{1,0:T(8,128)S(1)} %get-tuple-element.34), channel_id=1, source_target_pairs={{0,4},{4,0},{8,12},{12,8},{1,5},{5,1},{9,13},{13,9},{2,6},{6,2},{1... | collective-permute-start | bytes 786440 | tf_op jit(solution)/shard_map/ppermute | solution.py:281
  10.2 14.4 %collective-permute-start.3 = (f32[128,512]{1,0:T(8,128)S(1)}, f32[128,512]{1,0:T(8,128)S(1)}, u32[]{:S(2)}, u32[]{:S(2)}) collective-permute-start(f32[128,512]{1,0:T(8,128)S(1)} %get-tuple-element.35), channel_id=1, source_target_pairs={{0,8},{4,12},{8,0},{12,4},{1,9},{5,13},{9,1},{13,5},{2,10},{6,14},... | collective-permute-start | bytes 786440 | tf_op jit(solution)/shard_map/ppermute | solution.py:281
  24.6 2.8 %copy-start.2 = (f32[512,256]{1,0:T(8,128)S(1)}, f32[512,256]{1,0:T(8,128)}, u32[]{:S(2)}) copy-start(f32[512,256]{1,0:T(8,128)} %rhs_ref.1) | copy-start | bytes 1572868
  24.7 5.5 %collective-permute-start.4 = (f32[64,512]{1,0:T(8,128)S(1)}, f32[64,512]{1,0:T(8,128)S(1)}, u32[]{:S(2)}, u32[]{:S(2)}) collective-permute-start(f32[64,512]{1,0:T(8,128)S(1)} %get-tuple-element.36.a_ref), channel_id=1, source_target_pairs={{0,2},{3,1},{1,0},{2,3},{4,6},{7,5},{5,4},{6,7},{8,10},{11,9},{9,8... | collective-permute-start | bytes 393224 | tf_op jit(solution)/shard_map/ppermute | solution.py:286
  25.4 8.5 %collective-permute-start.6 = (f32[64,512]{1,0:T(8,128)S(1)}, f32[64,512]{1,0:T(8,128)S(1)}, u32[]{:S(2)}, u32[]{:S(2)}) collective-permute-start(f32[64,512]{1,0:T(8,128)S(1)} %get-tuple-element.37), channel_id=1, source_target_pairs={{1,2},{2,1},{0,0},{3,3},{5,6},{6,5},{4,4},{7,7},{9,10},{10,9},{8,8... | collective-permute-start | bytes 393224 | tf_op jit(solution)/shard_map/ppermute | solution.py:286
  27.3 7.2 %collective-permute-start.5 = (f32[64,512]{1,0:T(8,128)S(1)}, f32[64,512]{1,0:T(8,128)S(1)}, u32[]{:S(2)}, u32[]{:S(2)}) collective-permute-start(f32[64,512]{1,0:T(8,128)S(1)} %get-tuple-element.37), channel_id=1, source_target_pairs={{0,1},{3,2},{1,0},{2,3},{4,5},{7,6},{5,4},{6,7},{8,9},{11,10},{9,8... | collective-permute-start | bytes 393224 | tf_op jit(solution)/shard_map/ppermute | solution.py:286
  27.7 7.4 %collective-permute-start.9 = (f32[512,512]{1,0:T(8,128)S(1)}, f32[512,512]{1,0:T(8,128)S(1)}, u32[]{:S(2)}, u32[]{:S(2)}) collective-permute-start(f32[512,512]{1,0:T(8,128)S(1)} %collective-permute-done.8.sent_ref), channel_id=1, source_target_pairs={{0,16},{16,0},{1,17},{17,1},{2,18},{18,2},{3,19},{19,3},{4,20},{20... | collective-permute-start | bytes 3145736 | tf_op jit(solution)/shard_map/ppermute | solution.py:278
  34.5 1.2 %copy-start.1 = (f32[512,512]{1,0:T(8,128)S(1)}, f32[512,512]{1,0:T(8,128)}, u32[]{:S(2)}) copy-start(f32[512,512]{1,0:T(8,128)} %own_ref.1) | copy-start | bytes 3145732
  34.8 4.6 %collective-permute-start.7 = (f32[64,512]{1,0:T(8,128)S(1)}, f32[64,512]{1,0:T(8,128)S(1)}, u32[]{:S(2)}, u32[]{:S(2)}) collective-permute-start(f32[64,512]{1,0:T(8,128)S(1)} %shard_map.100.given_ref), channel_id=1, source_target_pairs={{0,4},{4,0},{8,12},{12,8},{1,5},{5,1},{9,13},{13,9},{2,6},{6,2},{1... | collective-permute-start | bytes 393224 | tf_op jit(solution)/shard_map/ppermute | solution.py:281
  35.1 4.6 %collective-permute-start.10 = (f32[64,512]{1,0:T(8,128)S(1)}, f32[64,512]{1,0:T(8,128)S(1)}, u32[]{:S(2)}, u32[]{:S(2)}) collective-permute-start(f32[64,512]{1,0:T(8,128)S(1)} %shard_map.100.given_ref), channel_id=1, source_target_pairs={{0,8},{4,12},{8,0},{12,4},{1,9},{5,13},{9,1},{13,5},{2,10},{6,14},... | collective-permute-start | bytes 393224 | tf_op jit(solution)/shard_map/ppermute | solution.py:281
  39.4 4.8 %collective-permute-start.11 = (f32[64,512]{1,0:T(8,128)S(1)}, f32[64,512]{1,0:T(8,128)S(1)}, u32[]{:S(2)}, u32[]{:S(2)}) collective-permute-start(f32[64,512]{1,0:T(8,128)S(1)} %shard_map.102.given_ref), channel_id=1, source_target_pairs={{0,12},{4,8},{8,4},{12,0},{1,13},{5,9},{9,5},{13,1},{2,14},{6,10},... | collective-permute-start | bytes 393224 | tf_op jit(solution)/shard_map/ppermute | solution.py:281
  44.2 3.9 %collective-permute-start.13 = (f32[64,512]{1,0:T(8,128)S(1)}, f32[64,512]{1,0:T(8,128)S(1)}, u32[]{:S(2)}, u32[]{:S(2)}) collective-permute-start(f32[64,512]{1,0:T(8,128)S(1)} %shard_map.104.given_ref), channel_id=1, source_target_pairs={{0,4},{4,0},{8,12},{12,8},{1,5},{5,1},{9,13},{13,9},{2,6},{6,2},{1... | collective-permute-start | bytes 393224 | tf_op jit(solution)/shard_map/ppermute | solution.py:281
  44.8 3.8 %collective-permute-start.12 = (f32[64,512]{1,0:T(8,128)S(1)}, f32[64,512]{1,0:T(8,128)S(1)}, u32[]{:S(2)}, u32[]{:S(2)}) collective-permute-start(f32[64,512]{1,0:T(8,128)S(1)} %shard_map.104.given_ref), channel_id=1, source_target_pairs={{0,8},{4,12},{8,0},{12,4},{1,9},{5,13},{9,1},{13,5},{2,10},{6,14},... | collective-permute-start | bytes 393224 | tf_op jit(solution)/shard_map/ppermute | solution.py:281
  49.1 3.9 %collective-permute-start.16 = (f32[64,512]{1,0:T(8,128)S(1)}, f32[64,512]{1,0:T(8,128)S(1)}, u32[]{:S(2)}, u32[]{:S(2)}) collective-permute-start(f32[64,512]{1,0:T(8,128)S(1)} %shard_map.106.x_ref), channel_id=1, source_target_pairs={{1,3},{2,0},{0,1},{3,2},{5,7},{6,4},{4,5},{7,6},{9,11},{10,8},{8,9... | collective-permute-start | bytes 393224 | tf_op jit(solution)/shard_map/ppermute | solution.py:286
  49.2 5.7 %collective-permute-start.15 = (f32[64,512]{1,0:T(8,128)S(1)}, f32[64,512]{1,0:T(8,128)S(1)}, u32[]{:S(2)}, u32[]{:S(2)}) collective-permute-start(f32[64,512]{1,0:T(8,128)S(1)} %shard_map.106.x_ref), channel_id=1, source_target_pairs={{1,2},{2,1},{0,0},{3,3},{5,6},{6,5},{4,4},{7,7},{9,10},{10,9},{8,8... | collective-permute-start | bytes 393224 | tf_op jit(solution)/shard_map/ppermute | solution.py:286
  52.3 4.4 %collective-permute-start.14 = (f32[64,512]{1,0:T(8,128)S(1)}, f32[64,512]{1,0:T(8,128)S(1)}, u32[]{:S(2)}, u32[]{:S(2)}) collective-permute-start(f32[64,512]{1,0:T(8,128)S(1)} %shard_map.106.x_ref), channel_id=1, source_target_pairs={{1,0},{2,3},{0,1},{3,2},{5,4},{6,7},{4,5},{7,6},{9,8},{10,11},{8,9... | collective-permute-start | bytes 393224 | tf_op jit(solution)/shard_map/ppermute | solution.py:286
  56.8 6.1 %collective-permute-start.17 = (f32[512,128]{1,0:T(8,128)S(1)}, f32[512,128]{1,0:T(8,128)S(1)}, u32[]{:S(2)}, u32[]{:S(2)}) collective-permute-start(f32[512,128]{1,0:T(8,128)S(1)} %shard_map.107.part_ref), channel_id=1, source_target_pairs={{0,16},{16,0},{1,17},{17,1},{2,18},{18,2},{3,19},{19,3},{4,20},{20... | collective-permute-start | bytes 786440 | tf_op jit(solution)/shard_map/ppermute | solution.py:278

commit v17 on v16

--- a/solution.py
+++ b/solution.py
@@ -277,13 +277,19 @@
     def swap(value):
         return lax.ppermute(value, "leaf", [(0, 1), (1, 0)])
 
-    def along_row(value, step):
-        return lax.ppermute(value, "row", [(r, r ^ step) for r in range(rows)])
+    def along(axis, value, pairs):
+        ends = range(lax.axis_size(axis))
+        rest = [a for a in ends if a not in [p[0] for p in pairs]]
+        open_ends = [b for b in ends if b not in [p[1] for p in pairs]]
+        stay = [a for a in rest if a in open_ends]
+        back = zip([a for a in rest if a not in stay], [b for b in open_ends if b not in stay])
+        return lax.ppermute(value, axis, pairs + [(a, a) for a in stay] + list(back))
 
     def along_col(value, pairs):
-        rest = [a for a in range(cols) if a not in [p[0] for p in pairs]]
-        open_ends = [b for b in range(cols) if b not in [p[1] for p in pairs]]
-        return lax.ppermute(value, "col", pairs + list(zip(rest, open_ends)))
+        return along("col", value, pairs)
+
+    def hop(value, pairs):
+        return along("row", value, pairs)
 
     near = [(at(k, 0), at(k, 1)) for k in (1, 2, 3)] + [(at(k, 1), at(k, 2)) for k in (2, 3)]
     far = [(at(k, 0), at(k, 2)) for k in (1, 2, 3)] + [(at(3, 2), at(3, 1))]
@@ -304,15 +310,15 @@
     )
     sums = call(own_kernel, [keep, send], [(half, size)] * rows)
     sums = call(other_kernel, [swap(send)] + sums, [(half, size)] * rows)
-    got = [along_row(sums[s], s) for s in (3, 1, 2)]
+    got = [hop(sums[s], [(r, r ^ s) for r in range(rows)]) for s in (3, 1, 2)]
     rhs_piece, diag_high, diag_low = call(
         turn_kernel, [top_rhs, top_diag], [shape, block, block], [(half, size)]
     )
     diag = [diag_high, diag_low]
     first, second = call(pieces_kernel, [sums[0]] + got, [shape] * 2, [(half, size)])
     q = [
+        along_col(first, [(0, 1), (3, 2)]),
         along_col(second, [(0, 2), (3, 1)]),
-        along_col(first, [(0, 1), (3, 2)]),
         along_col(first, [(1, 2), (2, 1)]),
     ]
 
@@ -324,14 +330,14 @@
         return out
 
     (x,) = call(first_kernel, [rhs_piece, second] + q + diag, [shape], flops=10 ** 10)
-    to1 = along_row(x, 1)
-    to2 = along_row(x, 2)
+    to1 = hop(x, [(0, 1)])
+    to2 = hop(x, [(0, 2)])
     x = chain(1, [x, to1] + factor[0])
-    on = along_row(x, 3)
+    on = hop(x, [(1, 2), (0, 3)])
     x = chain(2, [x, to2] + factor[0])
     x = chain(2, [x, on] + factor[1])
-    to3 = along_row(x, 1)
-    late = along_row(x, 2)
+    to3 = hop(x, [(2, 3)])
+    late = hop(x, [(1, 3)])
     x = chain(3, [x, on] + factor[0])
     x = chain(3, [x, late] + factor[1] + [to3] + factor[2])
 

time: 64.8 us -> 70.3 us (1.085); the launches traced: 63.6 us -> 70 us
  starting transfers between devices: 20.9 us -> 29.1 us
  waiting for transfers between devices: 30.4 us -> 29 us
    ppermute x14, starting transfers between devices: 10 us -> 18.4 us  [along(): lax.ppermute(value, axis, pairs + [(a, a) for a in stay] + list(back))]
    ppermute x14, waiting for transfers between devices: 29.5 us -> 28.2 us  [along(): lax.ppermute(value, axis, pairs + [(a, a) for a in stay] + list(back))]
  transfers between devices with their start and end apart: 18 -> 18, of which waited for: 15 -> 14; matrix products, arithmetic and copies ran while one was open for 0% -> 0% of each run, Pallas kernels for 15% -> 14%
where the time goes in v17:
time: 70.3 us; the launch traced here: 70 us
  starting transfers between devices  29.1 us (41%)
  waiting for transfers between devices  29 us (41%)
  Pallas kernels  11 us (16%)
  between operations  0.88 us (1%)
    ppermute x14, waiting for transfers between devices, along(): lax.ppermute(value, axis, pairs + [(a, a) for a in stay] + list(back))  28.2 us
    ppermute x14, starting transfers between devices, along(): lax.ppermute(value, axis, pairs + [(a, a) for a in stay] + list(back))  18.4 us
    pallas_call x15, Pallas kernels, call(): pl.pallas_call(kernel, out_shape=[shape(i, out) for i, out in enumerate(o...  11 us
    ppermute x3, starting transfers between devices, swap(): return lax.ppermute(value, 'leaf', [(0, 1), (1, 0)])  9.45 us
  transfers between devices with their start and end apart: 18, of which 14 were waited for; matrix products, arithmetic and copies ran while one was open for 0% of the time, Pallas kernels for 14%

profile of v17, /device:TPU:15, one launch (start us, length us, event | category | flops | bytes accessed | tf_op | source)
XLA Modules:
  0.0 70.0 jit_solution(2861095334771242999)
XLA Ops:
  0.6 1.3 %collective-permute-start.8 = (f32[512,512]{1,0:T(8,128)}, f32[512,512]{1,0:T(8,128)S(1)}, u32[]{:S(2)}, u32[]{:S(2)}) collective-permute-start(f32[512,512]{1,0:T(8,128)} %own_ref.1), channel_id=1, source_target_pairs={{4,5},{8,9},{12,13},{9,10},{13,14},{20,22},{24,26},{28,30},{30,29}} | collective-permute-start | bytes 3145736 | tf_op jit(solution)/shard_map/ppermute | solution.py:297
  1.9 2.9 %shard_map.95 = (f32[2,256,256]{2,1,0:T(8,128)}, f32[128,512]{1,0:T(8,128)S(1)}, f32[136,512]{1,0:T(8,128)S(1)}) custom-call(s32[2]{0:T(128)} %live_hbm.1, f32[2,256,256]{2,1,0:T(8,128)} %rhs_hbm.1, f32[2,256,256]{2,1,0:T(8,128)} %diag_hbm.1, f32[2,256,256]{2,1,0:T(8,128)} %off_hbm.1, s32[2,256]{1,0:T(2,128)} %tgt_hbm.1), custom_call_target="tpu_custom_call" | custom-call | bytes 1574920 | tf_op jit(solution)/shard_map/pallas_call | solution.py:251
  4.9 2.9 %collective-permute-start = (f32[136,512]{1,0:T(8,128)S(1)}, f32[136,512]{1,0:T(8,128)S(1)}, u32[]{:S(2)}, u32[]{:S(2)}) collective-permute-start(f32[136,512]{1,0:T(8,128)S(1)} %get-tuple-element.26.send_ref), channel_id=1, source_target_pairs={{0,16},{16,0},{1,17},{17,1},{2,18},{18,2},{3,19},{19,3},{4,20},{20... | collective-permute-start | bytes 835592 | tf_op jit(solution)/shard_map/ppermute | solution.py:278
  7.8 0.8 %shard_map.97 = (f32[128,512]{1,0:T(8,128)S(1)}, f32[128,512]{1,0:T(8,128)S(1)}, f32[128,512]{1,0:T(8,128)S(1)}, f32[128,512]{1,0:T(8,128)S(1)}) custom-call(f32[128,512]{1,0:T(8,128)S(1)} %get-tuple-element.27.keep_ref, f32[136,512]{1,0:T(8,128)S(1)} %get-tuple-element.26.send_ref), custom_call_target="tpu_custom_call" | custom-call | bytes 540672 | tf_op jit(solution)/shard_map/pallas_call | solution.py:251
  8.6 0.4 collective-permute-done.recv_ref
  9.0 0.8 %shard_map.98 = (f32[128,512]{1,0:T(8,128)S(1)}, f32[128,512]{1,0:T(8,128)S(1)}, f32[128,512]{1,0:T(8,128)S(1)}, f32[128,512]{1,0:T(8,128)S(1)}) custom-call(f32[136,512]{1,0:T(8,128)S(1)} %collective-permute-done.recv_ref, f32[128,512]{1,0:T(8,128)S(1)} %get-tuple-element.28.refs_0_, f32[128,512]{1,0:T(8,128)S(1)} %get-tuple-element.29.refs_1_, ...), custom_call_target="tpu_custom_call" | custom-call | bytes 1327104 | tf_op jit(solution)/shard_map/pallas_call | solution.py:251
  9.8 0.1 collective-permute-start.1
  9.8 0.3 collective-permute-start.2
  10.2 2.3 %collective-permute-start.3 = (f32[128,512]{1,0:T(8,128)S(1)}, f32[128,512]{1,0:T(8,128)S(1)}, u32[]{:S(2)}, u32[]{:S(2)}) collective-permute-start(f32[128,512]{1,0:T(8,128)S(1)} %get-tuple-element.35), channel_id=1, source_target_pairs={{0,8},{4,12},{8,0},{12,4},{1,9},{5,13},{9,1},{13,5},{2,10},{6,14},... | collective-permute-start | bytes 786440 | tf_op jit(solution)/shard_map/ppermute | solution.py:286
  12.5 5.8 %collective-permute-done.1.b_ref = f32[128,512]{1,0:T(8,128)S(1)} collective-permute-done((f32[128,512]{1,0:T(8,128)S(1)}, f32[128,512]{1,0:T(8,128)S(1)}, u32[]{:S(2)}, u32[]{:S(2)}) %collective-permute-start.1) | collective-permute-done | bytes 262176 | tf_op jit(solution)/shard_map/ppermute | solution.py:286
  18.3 3.8 %collective-permute-done.2.c_ref = f32[128,512]{1,0:T(8,128)S(1)} collective-permute-done((f32[128,512]{1,0:T(8,128)S(1)}, f32[128,512]{1,0:T(8,128)S(1)}, u32[]{:S(2)}, u32[]{:S(2)}) %collective-permute-start.2) | collective-permute-done | bytes 262176 | tf_op jit(solution)/shard_map/ppermute | solution.py:286
  22.1 2.5 %collective-permute-done.3.d_ref = f32[128,512]{1,0:T(8,128)S(1)} collective-permute-done((f32[128,512]{1,0:T(8,128)S(1)}, f32[128,512]{1,0:T(8,128)S(1)}, u32[]{:S(2)}, u32[]{:S(2)}) %collective-permute-start.3) | collective-permute-done | bytes 262176 | tf_op jit(solution)/shard_map/ppermute | solution.py:286
  24.6 0.1 shard_map.99
  24.7 0.7 %collective-permute-start.5 = (f32[64,512]{1,0:T(8,128)S(1)}, f32[64,512]{1,0:T(8,128)S(1)}, u32[]{:S(2)}, u32[]{:S(2)}) collective-permute-start(f32[64,512]{1,0:T(8,128)S(1)} %get-tuple-element.36.a_ref), channel_id=1, source_target_pairs={{0,2},{3,1},{1,0},{2,3},{4,6},{7,5},{5,4},{6,7},{8,10},{11,9},{9,8... | collective-permute-start | bytes 393224 | tf_op jit(solution)/shard_map/ppermute | solution.py:286
  25.4 1.9 %collective-permute-start.6 = (f32[64,512]{1,0:T(8,128)S(1)}, f32[64,512]{1,0:T(8,128)S(1)}, u32[]{:S(2)}, u32[]{:S(2)}) collective-permute-start(f32[64,512]{1,0:T(8,128)S(1)} %get-tuple-element.37), channel_id=1, source_target_pairs={{1,2},{2,1},{0,0},{3,3},{5,6},{6,5},{4,4},{7,7},{9,10},{10,9},{8,8... | collective-permute-start | bytes 393224 | tf_op jit(solution)/shard_map/ppermute | solution.py:286
  27.3 0.1 collective-permute-start.4
  27.4 0.3 shard_map.96
  27.7 0.0 collective-permute-done.8.sent_ref
  27.7 1.7 %collective-permute-start.9 = (f32[512,512]{1,0:T(8,128)S(1)}, f32[512,512]{1,0:T(8,128)S(1)}, u32[]{:S(2)}, u32[]{:S(2)}) collective-permute-start(f32[512,512]{1,0:T(8,128)S(1)} %collective-permute-done.8.sent_ref), channel_id=1, source_target_pairs={{0,16},{16,0},{1,17},{17,1},{2,18},{18,2},{3,19},{19,3},{4,20},{20... | collective-permute-start | bytes 3145736 | tf_op jit(solution)/shard_map/ppermute | solution.py:278
  29.4 0.7 %collective-permute-done.5.c_ref = f32[64,512]{1,0:T(8,128)S(1)} collective-permute-done((f32[64,512]{1,0:T(8,128)S(1)}, f32[64,512]{1,0:T(8,128)S(1)}, u32[]{:S(2)}, u32[]{:S(2)}) %collective-permute-start.5) | collective-permute-done | bytes 131104 | tf_op jit(solution)/shard_map/ppermute | solution.py:286
  30.2 3.7 %collective-permute-done.6.d_ref = f32[64,512]{1,0:T(8,128)S(1)} collective-permute-done((f32[64,512]{1,0:T(8,128)S(1)}, f32[64,512]{1,0:T(8,128)S(1)}, u32[]{:S(2)}, u32[]{:S(2)}) %collective-permute-start.6) | collective-permute-done | bytes 131104 | tf_op jit(solution)/shard_map/ppermute | solution.py:286
  33.8 0.6 collective-permute-done.4.b_ref
  34.5 0.3 shard_map.100.given_ref
  34.8 0.8 %collective-permute-start.7 = (f32[64,512]{1,0:T(8,128)S(1)}, f32[64,512]{1,0:T(8,128)S(1)}, u32[]{:S(2)}, u32[]{:S(2)}) collective-permute-start(f32[64,512]{1,0:T(8,128)S(1)} %shard_map.100.given_ref), channel_id=1, source_target_pairs={{0,4},{8,8},{12,12},{4,0},{1,5},{9,9},{13,13},{5,1},{2,6},{10,10},... | collective-permute-start | bytes 393224 | tf_op jit(solution)/shard_map/ppermute | solution.py:286
  35.6 0.7 collective-permute-start.10
  36.2 0.0 collective-permute-done.9.other_ref
  36.3 3.4 %shard_map.101 = (bf16[512,512]{1,0:T(8,128)(2,1)S(1)}, bf16[512,512]{1,0:T(8,128)(2,1)S(1)}, bf16[512,512]{1,0:T(8,128)(2,1)S(1)}, bf16[512,512]{1,0:T(8,128)(2...) custom-call(f32[512,512]{1,0:T(8,128)S(1)} %copy-done.1, ...), custom_call_target="tpu_custom_call" | custom-call | bytes 5242880 | tf_op jit(solution)/shard_map/pallas_call | solution.py:251
  39.7 0.0 collective-permute-done.7.refs_0_
  39.7 2.2 %collective-permute-start.11 = (f32[64,512]{1,0:T(8,128)S(1)}, f32[64,512]{1,0:T(8,128)S(1)}, u32[]{:S(2)}, u32[]{:S(2)}) collective-permute-start(f32[64,512]{1,0:T(8,128)S(1)} %shard_map.102.given_ref), channel_id=1, source_target_pairs={{4,8},{0,12},{8,0},{12,4},{5,9},{1,13},{9,1},{13,5},{6,10},{2,14},... | collective-permute-start | bytes 393224 | tf_op jit(solution)/shard_map/ppermute | solution.py:286
  41.9 0.0 collective-permute-done.10.refs_0_
  41.9 3.3 %collective-permute-done.11.refs_0_ = f32[64,512]{1,0:T(8,128)S(1)} collective-permute-done((f32[64,512]{1,0:T(8,128)S(1)}, f32[64,512]{1,0:T(8,128)S(1)}, u32[]{:S(2)}, u32[]{:S(2)}) %collective-permute-start.11) | collective-permute-done | bytes 131104 | tf_op jit(solution)/shard_map/ppermute | solution.py:286
  45.3 4.5 %collective-permute-start.13 = (f32[64,512]{1,0:T(8,128)S(1)}, f32[64,512]{1,0:T(8,128)S(1)}, u32[]{:S(2)}, u32[]{:S(2)}) collective-permute-start(f32[64,512]{1,0:T(8,128)S(1)} %shard_map.104.given_ref), channel_id=1, source_target_pairs={{8,12},{0,0},{4,4},{12,8},{9,13},{1,1},{5,5},{13,9},{10,14},{2,2},... | collective-permute-start | bytes 393224 | tf_op jit(solution)/shard_map/ppermute | solution.py:286
  49.7 1.9 %collective-permute-start.12 = (f32[64,512]{1,0:T(8,128)S(1)}, f32[64,512]{1,0:T(8,128)S(1)}, u32[]{:S(2)}, u32[]{:S(2)}) collective-permute-start(f32[64,512]{1,0:T(8,128)S(1)} %shard_map.104.given_ref), channel_id=1, source_target_pairs={{4,12},{0,0},{8,8},{12,4},{5,13},{1,1},{9,9},{13,5},{6,14},{2,2},{... | collective-permute-start | bytes 393224 | tf_op jit(solution)/shard_map/ppermute | solution.py:286
  51.7 0.3 shard_map.105.given_ref
  52.0 0.1 collective-permute-done.13.refs_3_
  52.1 3.4 %collective-permute-done.12.refs_0_ = f32[64,512]{1,0:T(8,128)S(1)} collective-permute-done((f32[64,512]{1,0:T(8,128)S(1)}, f32[64,512]{1,0:T(8,128)S(1)}, u32[]{:S(2)}, u32[]{:S(2)}) %collective-permute-start.12) | collective-permute-done | bytes 131104 | tf_op jit(solution)/shard_map/ppermute | solution.py:286
  55.5 0.5 shard_map.106.x_ref
  55.9 0.1 collective-permute-start.16
  56.0 2.8 %collective-permute-start.15 = (f32[64,512]{1,0:T(8,128)S(1)}, f32[64,512]{1,0:T(8,128)S(1)}, u32[]{:S(2)}, u32[]{:S(2)}) collective-permute-start(f32[64,512]{1,0:T(8,128)S(1)} %shard_map.106.x_ref), channel_id=1, source_target_pairs={{1,2},{2,1},{0,0},{3,3},{5,6},{6,5},{4,4},{7,7},{9,10},{10,9},{8,8... | collective-permute-start | bytes 393224 | tf_op jit(solution)/shard_map/ppermute | solution.py:286
  58.8 0.1 collective-permute-start.14
  58.9 0.9 %collective-permute-done.16.c_ref = f32[64,512]{1,0:T(8,128)S(1)} collective-permute-done((f32[64,512]{1,0:T(8,128)S(1)}, f32[64,512]{1,0:T(8,128)S(1)}, u32[]{:S(2)}, u32[]{:S(2)}) %collective-permute-start.16) | collective-permute-done | bytes 131104 | tf_op jit(solution)/shard_map/ppermute | solution.py:286
  59.8 1.9 %collective-permute-done.15.b_ref = f32[64,512]{1,0:T(8,128)S(1)} collective-permute-done((f32[64,512]{1,0:T(8,128)S(1)}, f32[64,512]{1,0:T(8,128)S(1)}, u32[]{:S(2)}, u32[]{:S(2)}) %collective-permute-start.15) | collective-permute-done | bytes 131104 | tf_op jit(solution)/shard_map/ppermute | solution.py:286
  61.7 1.5 %collective-permute-done.14.a_ref = f32[64,512]{1,0:T(8,128)S(1)} collective-permute-done((f32[64,512]{1,0:T(8,128)S(1)}, f32[64,512]{1,0:T(8,128)S(1)}, u32[]{:S(2)}, u32[]{:S(2)}) %collective-permute-start.14) | collective-permute-done | bytes 131104 | tf_op jit(solution)/shard_map/ppermute | solution.py:286
  63.2 0.1 shard_map.107.part_ref
  63.3 4.8 %collective-permute-start.17 = (f32[512,128]{1,0:T(8,128)S(1)}, f32[512,128]{1,0:T(8,128)S(1)}, u32[]{:S(2)}, u32[]{:S(2)}) collective-permute-start(f32[512,128]{1,0:T(8,128)S(1)} %shard_map.107.part_ref), channel_id=1, source_target_pairs={{0,16},{16,0},{1,17},{17,1},{2,18},{18,2},{3,19},{19,3},{4,20},{20... | collective-permute-start | bytes 786440 | tf_op jit(solution)/shard_map/ppermute | solution.py:278
  68.1 0.7 %shard_map.108.refs_0_ = f32[512,256]{1,0:T(8,128)} custom-call(f32[512,128]{1,0:T(8,128)S(1)} %shard_map.107.part_ref), custom_call_target="tpu_custom_call" | custom-call | bytes 262144 | tf_op jit(solution)/shard_map/pallas_call | solution.py:251
  68.9 0.4 collective-permute-done.17.part_ref
  69.3 0.7 %shard_map.109 = f32[512,256]{1,0:T(8,128)} custom-call(f32[512,128]{1,0:T(8,128)S(1)} %collective-permute-done.17.part_ref, f32[512,256]{1,0:T(8,128)} %shard_map.108.refs_0_), custom_call_target="tpu_custom_call", output_to_operand_aliasing={{}: (1, {})} | custom-call | bytes 786432 | tf_op jit(solution)/shard_map/pallas_call | solution.py:251
  (9 shorter events, 0.1 us)
Async XLA Ops:
  0.6 27.1 %collective-permute-start.8 = (f32[512,512]{1,0:T(8,128)}, f32[512,512]{1,0:T(8,128)S(1)}, u32[]{:S(2)}, u32[]{:S(2)}) collective-permute-start(f32[512,512]{1,0:T(8,128)} %own_ref.1), channel_id=1, source_target_pairs={{4,5},{8,9},{12,13},{9,10},{13,14},{20,22},{24,26},{28,30},{30,29}} | collective-permute-start | bytes 3145736 | tf_op jit(solution)/shard_map/ppermute | solution.py:297
  4.9 4.1 %collective-permute-start = (f32[136,512]{1,0:T(8,128)S(1)}, f32[136,512]{1,0:T(8,128)S(1)}, u32[]{:S(2)}, u32[]{:S(2)}) collective-permute-start(f32[136,512]{1,0:T(8,128)S(1)} %get-tuple-element.26.send_ref), channel_id=1, source_target_pairs={{0,16},{16,0},{1,17},{17,1},{2,18},{18,2},{3,19},{19,3},{4,20},{20... | collective-permute-start | bytes 835592 | tf_op jit(solution)/shard_map/ppermute | solution.py:278
  9.0 18.4 %copy-start = (f32[512,512]{1,0:T(8,128)S(1)}, f32[512,512]{1,0:T(8,128)}, u32[]{:S(2)}) copy-start(f32[512,512]{1,0:T(8,128)} %diag_ref.1) | copy-start | bytes 3145732
  9.8 8.5 %collective-permute-start.1 = (f32[128,512]{1,0:T(8,128)S(1)}, f32[128,512]{1,0:T(8,128)S(1)}, u32[]{:S(2)}, u32[]{:S(2)}) collective-permute-start(f32[128,512]{1,0:T(8,128)S(1)} %get-tuple-element.33), channel_id=1, source_target_pairs={{0,12},{4,8},{8,4},{12,0},{1,13},{5,9},{9,5},{13,1},{2,14},{6,10},... | collective-permute-start | bytes 786440 | tf_op jit(solution)/shard_map/ppermute | solution.py:286
  9.8 12.3 %collective-permute-start.2 = (f32[128,512]{1,0:T(8,128)S(1)}, f32[128,512]{1,0:T(8,128)S(1)}, u32[]{:S(2)}, u32[]{:S(2)}) collective-permute-start(f32[128,512]{1,0:T(8,128)S(1)} %get-tuple-element.34), channel_id=1, source_target_pairs={{0,4},{4,0},{8,12},{12,8},{1,5},{5,1},{9,13},{13,9},{2,6},{6,2},{1... | collective-permute-start | bytes 786440 | tf_op jit(solution)/shard_map/ppermute | solution.py:286
  10.2 14.4 %collective-permute-start.3 = (f32[128,512]{1,0:T(8,128)S(1)}, f32[128,512]{1,0:T(8,128)S(1)}, u32[]{:S(2)}, u32[]{:S(2)}) collective-permute-start(f32[128,512]{1,0:T(8,128)S(1)} %get-tuple-element.35), channel_id=1, source_target_pairs={{0,8},{4,12},{8,0},{12,4},{1,9},{5,13},{9,1},{13,5},{2,10},{6,14},... | collective-permute-start | bytes 786440 | tf_op jit(solution)/shard_map/ppermute | solution.py:286
  24.6 2.8 %copy-start.2 = (f32[512,256]{1,0:T(8,128)S(1)}, f32[512,256]{1,0:T(8,128)}, u32[]{:S(2)}) copy-start(f32[512,256]{1,0:T(8,128)} %rhs_ref.1) | copy-start | bytes 1572868
  24.7 5.5 %collective-permute-start.5 = (f32[64,512]{1,0:T(8,128)S(1)}, f32[64,512]{1,0:T(8,128)S(1)}, u32[]{:S(2)}, u32[]{:S(2)}) collective-permute-start(f32[64,512]{1,0:T(8,128)S(1)} %get-tuple-element.36.a_ref), channel_id=1, source_target_pairs={{0,2},{3,1},{1,0},{2,3},{4,6},{7,5},{5,4},{6,7},{8,10},{11,9},{9,8... | collective-permute-start | bytes 393224 | tf_op jit(solution)/shard_map/ppermute | solution.py:286
  25.4 8.5 %collective-permute-start.6 = (f32[64,512]{1,0:T(8,128)S(1)}, f32[64,512]{1,0:T(8,128)S(1)}, u32[]{:S(2)}, u32[]{:S(2)}) collective-permute-start(f32[64,512]{1,0:T(8,128)S(1)} %get-tuple-element.37), channel_id=1, source_target_pairs={{1,2},{2,1},{0,0},{3,3},{5,6},{6,5},{4,4},{7,7},{9,10},{10,9},{8,8... | collective-permute-start | bytes 393224 | tf_op jit(solution)/shard_map/ppermute | solution.py:286
  27.3 7.2 %collective-permute-start.4 = (f32[64,512]{1,0:T(8,128)S(1)}, f32[64,512]{1,0:T(8,128)S(1)}, u32[]{:S(2)}, u32[]{:S(2)}) collective-permute-start(f32[64,512]{1,0:T(8,128)S(1)} %get-tuple-element.37), channel_id=1, source_target_pairs={{0,1},{3,2},{1,0},{2,3},{4,5},{7,6},{5,4},{6,7},{8,9},{11,10},{9,8... | collective-permute-start | bytes 393224 | tf_op jit(solution)/shard_map/ppermute | solution.py:286
  27.7 8.5 %collective-permute-start.9 = (f32[512,512]{1,0:T(8,128)S(1)}, f32[512,512]{1,0:T(8,128)S(1)}, u32[]{:S(2)}, u32[]{:S(2)}) collective-permute-start(f32[512,512]{1,0:T(8,128)S(1)} %collective-permute-done.8.sent_ref), channel_id=1, source_target_pairs={{0,16},{16,0},{1,17},{17,1},{2,18},{18,2},{3,19},{19,3},{4,20},{20... | collective-permute-start | bytes 3145736 | tf_op jit(solution)/shard_map/ppermute | solution.py:278
  34.5 1.8 %copy-start.1 = (f32[512,512]{1,0:T(8,128)S(1)}, f32[512,512]{1,0:T(8,128)}, u32[]{:S(2)}) copy-start(f32[512,512]{1,0:T(8,128)} %own_ref.1) | copy-start | bytes 3145732
  34.8 4.9 %collective-permute-start.7 = (f32[64,512]{1,0:T(8,128)S(1)}, f32[64,512]{1,0:T(8,128)S(1)}, u32[]{:S(2)}, u32[]{:S(2)}) collective-permute-start(f32[64,512]{1,0:T(8,128)S(1)} %shard_map.100.given_ref), channel_id=1, source_target_pairs={{0,4},{8,8},{12,12},{4,0},{1,5},{9,9},{13,13},{5,1},{2,6},{10,10},... | collective-permute-start | bytes 393224 | tf_op jit(solution)/shard_map/ppermute | solution.py:286
  35.6 6.3 %collective-permute-start.10 = (f32[64,512]{1,0:T(8,128)S(1)}, f32[64,512]{1,0:T(8,128)S(1)}, u32[]{:S(2)}, u32[]{:S(2)}) collective-permute-start(f32[64,512]{1,0:T(8,128)S(1)} %shard_map.100.given_ref), channel_id=1, source_target_pairs={{0,8},{4,4},{12,12},{8,0},{1,9},{5,5},{13,13},{9,1},{2,10},{6,6},{... | collective-permute-start | bytes 393224 | tf_op jit(solution)/shard_map/ppermute | solution.py:286
  39.7 5.5 %collective-permute-start.11 = (f32[64,512]{1,0:T(8,128)S(1)}, f32[64,512]{1,0:T(8,128)S(1)}, u32[]{:S(2)}, u32[]{:S(2)}) collective-permute-start(f32[64,512]{1,0:T(8,128)S(1)} %shard_map.102.given_ref), channel_id=1, source_target_pairs={{4,8},{0,12},{8,0},{12,4},{5,9},{1,13},{9,1},{13,5},{6,10},{2,14},... | collective-permute-start | bytes 393224 | tf_op jit(solution)/shard_map/ppermute | solution.py:286
  45.3 6.8 %collective-permute-start.13 = (f32[64,512]{1,0:T(8,128)S(1)}, f32[64,512]{1,0:T(8,128)S(1)}, u32[]{:S(2)}, u32[]{:S(2)}) collective-permute-start(f32[64,512]{1,0:T(8,128)S(1)} %shard_map.104.given_ref), channel_id=1, source_target_pairs={{8,12},{0,0},{4,4},{12,8},{9,13},{1,1},{5,5},{13,9},{10,14},{2,2},... | collective-permute-start | bytes 393224 | tf_op jit(solution)/shard_map/ppermute | solution.py:286
  49.7 5.7 %collective-permute-start.12 = (f32[64,512]{1,0:T(8,128)S(1)}, f32[64,512]{1,0:T(8,128)S(1)}, u32[]{:S(2)}, u32[]{:S(2)}) collective-permute-start(f32[64,512]{1,0:T(8,128)S(1)} %shard_map.104.given_ref), channel_id=1, source_target_pairs={{4,12},{0,0},{8,8},{12,4},{5,13},{1,1},{9,9},{13,5},{6,14},{2,2},{... | collective-permute-start | bytes 393224 | tf_op jit(solution)/shard_map/ppermute | solution.py:286
  55.9 3.9 %collective-permute-start.16 = (f32[64,512]{1,0:T(8,128)S(1)}, f32[64,512]{1,0:T(8,128)S(1)}, u32[]{:S(2)}, u32[]{:S(2)}) collective-permute-start(f32[64,512]{1,0:T(8,128)S(1)} %shard_map.106.x_ref), channel_id=1, source_target_pairs={{1,3},{2,0},{0,1},{3,2},{5,7},{6,4},{4,5},{7,6},{9,11},{10,8},{8,9... | collective-permute-start | bytes 393224 | tf_op jit(solution)/shard_map/ppermute | solution.py:286
  56.0 5.7 %collective-permute-start.15 = (f32[64,512]{1,0:T(8,128)S(1)}, f32[64,512]{1,0:T(8,128)S(1)}, u32[]{:S(2)}, u32[]{:S(2)}) collective-permute-start(f32[64,512]{1,0:T(8,128)S(1)} %shard_map.106.x_ref), channel_id=1, source_target_pairs={{1,2},{2,1},{0,0},{3,3},{5,6},{6,5},{4,4},{7,7},{9,10},{10,9},{8,8... | collective-permute-start | bytes 393224 | tf_op jit(solution)/shard_map/ppermute | solution.py:286
  58.8 4.3 %collective-permute-start.14 = (f32[64,512]{1,0:T(8,128)S(1)}, f32[64,512]{1,0:T(8,128)S(1)}, u32[]{:S(2)}, u32[]{:S(2)}) collective-permute-start(f32[64,512]{1,0:T(8,128)S(1)} %shard_map.106.x_ref), channel_id=1, source_target_pairs={{1,0},{2,3},{0,1},{3,2},{5,4},{6,7},{4,5},{7,6},{9,8},{10,11},{8,9... | collective-permute-start | bytes 393224 | tf_op jit(solution)/shard_map/ppermute | solution.py:286
  63.3 6.0 %collective-permute-start.17 = (f32[512,128]{1,0:T(8,128)S(1)}, f32[512,128]{1,0:T(8,128)S(1)}, u32[]{:S(2)}, u32[]{:S(2)}) collective-permute-start(f32[512,128]{1,0:T(8,128)S(1)} %shard_map.107.part_ref), channel_id=1, source_target_pairs={{0,16},{16,0},{1,17},{17,1},{2,18},{18,2},{3,19},{19,3},{4,20},{20... | collective-permute-start | bytes 786440 | tf_op jit(solution)/shard_map/ppermute | solution.py:278

commit v18 on v16

--- a/solution.py
+++ b/solution.py
@@ -204,9 +204,42 @@
             high_ref[...], low_ref[...] = split(value)
 
 
-def first_kernel(rhs_ref, a_ref, b_ref, c_ref, d_ref, high_ref, low_ref, out_ref):
+def first_kernel(rhs_ref, a_ref, b_ref, c_ref, d_ref, high_ref, low_ref, all_ref, *out_refs):
     value = rhs_ref[...] - ((a_ref[...] + b_ref[...]) + (c_ref[...] + d_ref[...]))
-    out_ref[...] = value + dot3(value, high_ref[...], low_ref[...], NN)
+    all_ref[...] = value + dot3(value, high_ref[...], low_ref[...], NN)
+    rows = out_refs[0].shape[0]
+    for i, out_ref in enumerate(out_refs):
+        out_ref[...] = all_ref[i * rows:(i + 1) * rows, :]
+
+
+def joined(refs):
+    return jnp.concatenate([ref[...] for ref in refs], axis=0)
+
+
+def side_kernel(owner, given_a_ref, given_b_ref, x_ref, high_ref, low_ref, *out_refs):
+    _, row, z = place()
+    rows = given_a_ref.shape[0]
+    for given_ref, out_ref in zip((given_a_ref, given_b_ref), out_refs):
+        out_ref[...] = given_ref[...]
+
+    @pl.when((row == owner) & ((z == 1) | (z == 2)))
+    def _():
+        product = dot3(x_ref[...], high_ref[...], low_ref[...], NN)
+        for i, out_ref in enumerate(out_refs):
+            out_ref[...] = out_ref[...] - product[i * rows:(i + 1) * rows]
+
+
+def join_kernel(given_a_ref, given_b_ref, *refs):
+    _, row, z = place()
+    out_ref = refs[-1]
+    out_ref[...] = joined((given_a_ref, given_b_ref))
+
+    @pl.when((row == 3) & ((z == 1) | (z == 2)))
+    def _():
+        left = joined((given_a_ref, given_b_ref))
+        for i in range(0, len(refs) - 1, 4):
+            left = left - dot3(joined(refs[i:i + 2]), refs[i + 2][...], refs[i + 3][...], NN)
+        out_ref[...] = left
 
 
 def chain_kernel(owner, given_ref, *refs):
@@ -319,21 +352,23 @@
     factor = call(factor_kernel, [top_factor, sent, swap(sent)] + diag, [block] * 6)
     factor = [factor[0:2], factor[2:4], factor[4:6]]
 
+    part = (piece // 2, size)
+
     def chain(owner, ins):
-        (out,) = call(functools.partial(chain_kernel, owner), ins, [shape])
+        (out,) = call(functools.partial(chain_kernel, owner), ins, [part])
         return out
 
-    (x,) = call(first_kernel, [rhs_piece, second] + q + diag, [shape], flops=10 ** 10)
-    to1 = along_row(x, 1)
+    x, *xs = call(first_kernel, [rhs_piece, second] + q + diag, [shape, part, part], flops=10 ** 10)
+    to1 = [along_row(v, 1) for v in xs]
     to2 = along_row(x, 2)
-    x = chain(1, [x, to1] + factor[0])
-    on = along_row(x, 3)
-    x = chain(2, [x, to2] + factor[0])
-    x = chain(2, [x, on] + factor[1])
-    to3 = along_row(x, 1)
-    late = along_row(x, 2)
-    x = chain(3, [x, on] + factor[0])
-    x = chain(3, [x, late] + factor[1] + [to3] + factor[2])
+    xs = [chain(1, [v, t] + factor[0]) for v, t in zip(xs, to1)]
+    on = [along_row(v, 3) for v in xs]
+    xs = call(functools.partial(side_kernel, 2), xs + [to2] + factor[0], [part, part])
+    xs = [chain(2, [v, t] + factor[1]) for v, t in zip(xs, on)]
+    to3 = [along_row(v, 1) for v in xs]
+    late = [along_row(v, 2) for v in xs]
+    xs = [chain(3, [v, t] + factor[0]) for v, t in zip(xs, on)]
+    (x,) = call(join_kernel, xs + late + factor[1] + to3 + factor[2], [shape])
 
     both = along_col(x, [(1, 2), (2, 1)])
     step = along_col(x, [(1, 0), (2, 3)])

time: 64.8 us -> 65.7 us (1.014)
  starting transfers between devices: 20.9 us -> 27.7 us
  waiting for transfers between devices: 30.4 us -> 24.7 us
    ppermute x8 -> x12, starting transfers between devices: 4.08 us -> 9.54 us  [along_row(): return lax.ppermute(value, 'row', [(r, r ^ step) for r in range(rows)])]
    ppermute x8 -> x12, waiting for transfers between devices: 20.2 us -> 15.3 us  [along_row(): return lax.ppermute(value, 'row', [(r, r ^ step) for r in range(rows)])]
    ppermute x3, starting transfers between devices: 9.62 us -> 11.1 us  [swap(): return lax.ppermute(value, 'leaf', [(0, 1), (1, 0)])]
    ppermute x6, waiting for transfers between devices: 9.29 us -> 8.5 us  [along_col(): return lax.ppermute(value, 'col', pairs + list(zip(rest, open_ends)))]
    pallas_call x15 -> x18, Pallas kernels: 10.9 us -> 11.2 us  [call(): pl.pallas_call(kernel, out_shape=[shape(i, out) for i, out in enumerate(o...]
  transfers between devices with their start and end apart: 18 -> 22, of which waited for: 15 -> 15; matrix products, arithmetic and copies ran while one was open for 0% -> 0% of each run, Pallas kernels for 15% -> 15%
where the time goes in v18:
time: 65.7 us; the launch traced here: 64.4 us
  starting transfers between devices  27.7 us (42%)
  waiting for transfers between devices  24.7 us (38%)
  Pallas kernels  11.2 us (17%)
  between operations  0.85 us (1%)
    ppermute x12, waiting for transfers between devices, along_row(): return lax.ppermute(value, 'row', [(r, r ^ step) for r in range(rows)])  15.3 us
    pallas_call x18, Pallas kernels, call(): pl.pallas_call(kernel, out_shape=[shape(i, out) for i, out in enumerate(o...  11.2 us
    ppermute x3, starting transfers between devices, swap(): return lax.ppermute(value, 'leaf', [(0, 1), (1, 0)])  11.1 us
    ppermute x12, starting transfers between devices, along_row(): return lax.ppermute(value, 'row', [(r, r ^ step) for r in range(rows)])  9.54 us
    ppermute x6, waiting for transfers between devices, along_col(): return lax.ppermute(value, 'col', pairs + list(zip(rest, open_ends)))  8.5 us
    ppermute x6, starting transfers between devices, along_col(): return lax.ppermute(value, 'col', pairs + list(zip(rest, open_ends)))  5.71 us
  transfers between devices with their start and end apart: 22, of which 15 were waited for; matrix products, arithmetic and copies ran while one was open for 0% of the time, Pallas kernels for 15%

profile of v18, /device:TPU:15, one launch (start us, length us, event | category | flops | bytes accessed | tf_op | source)
XLA Modules:
  0.0 64.4 jit_solution(9038561069543759001)
XLA Ops:
  0.6 1.3 %collective-permute-start.8 = (f32[512,512]{1,0:T(8,128)}, f32[512,512]{1,0:T(8,128)S(1)}, u32[]{:S(2)}, u32[]{:S(2)}) collective-permute-start(f32[512,512]{1,0:T(8,128)} %own_ref.1), channel_id=1, source_target_pairs={{4,5},{8,9},{12,13},{9,10},{13,14},{20,22},{24,26},{28,30},{30,29}} | collective-permute-start | bytes 3145736 | tf_op jit(solution)/shard_map/ppermute | solution.py:324
  1.9 2.9 %shard_map.95 = (f32[2,256,256]{2,1,0:T(8,128)}, f32[128,512]{1,0:T(8,128)S(1)}, f32[136,512]{1,0:T(8,128)S(1)}) custom-call(s32[2]{0:T(128)} %live_hbm.1, f32[2,256,256]{2,1,0:T(8,128)} %rhs_hbm.1, f32[2,256,256]{2,1,0:T(8,128)} %diag_hbm.1, f32[2,256,256]{2,1,0:T(8,128)} %off_hbm.1, s32[2,256]{1,0:T(2,128)} %tgt_hbm.1), custom_call_target="tpu_custom_call" | custom-call | bytes 1574920 | tf_op jit(solution)/shard_map/pallas_call | solution.py:284
  4.9 2.9 %collective-permute-start = (f32[136,512]{1,0:T(8,128)S(1)}, f32[136,512]{1,0:T(8,128)S(1)}, u32[]{:S(2)}, u32[]{:S(2)}) collective-permute-start(f32[136,512]{1,0:T(8,128)S(1)} %get-tuple-element.31.send_ref), channel_id=1, source_target_pairs={{0,16},{16,0},{1,17},{17,1},{2,18},{18,2},{3,19},{19,3},{4,20},{20... | collective-permute-start | bytes 835592 | tf_op jit(solution)/shard_map/ppermute | solution.py:311
  7.8 0.8 %shard_map.97 = (f32[128,512]{1,0:T(8,128)S(1)}, f32[128,512]{1,0:T(8,128)S(1)}, f32[128,512]{1,0:T(8,128)S(1)}, f32[128,512]{1,0:T(8,128)S(1)}) custom-call(f32[128,512]{1,0:T(8,128)S(1)} %get-tuple-element.32.keep_ref, f32[136,512]{1,0:T(8,128)S(1)} %get-tuple-element.31.send_ref), custom_call_target="tpu_custom_call" | custom-call | bytes 540672 | tf_op jit(solution)/shard_map/pallas_call | solution.py:284
  8.6 0.4 collective-permute-done.recv_ref
  9.0 0.8 %shard_map.98 = (f32[128,512]{1,0:T(8,128)S(1)}, f32[128,512]{1,0:T(8,128)S(1)}, f32[128,512]{1,0:T(8,128)S(1)}, f32[128,512]{1,0:T(8,128)S(1)}) custom-call(f32[136,512]{1,0:T(8,128)S(1)} %collective-permute-done.recv_ref, f32[128,512]{1,0:T(8,128)S(1)} %get-tuple-element.33.refs_0_, f32[128,512]{1,0:T(8,128)S(1)} %get-tuple-element.34.refs_1_, ...), custom_call_target="tpu_custom_call" | custom-call | bytes 1327104 | tf_op jit(solution)/shard_map/pallas_call | solution.py:284
  9.8 0.1 collective-permute-start.1
  9.8 0.3 collective-permute-start.2
  10.2 2.3 %collective-permute-start.3 = (f32[128,512]{1,0:T(8,128)S(1)}, f32[128,512]{1,0:T(8,128)S(1)}, u32[]{:S(2)}, u32[]{:S(2)}) collective-permute-start(f32[128,512]{1,0:T(8,128)S(1)} %get-tuple-element.40), channel_id=1, source_target_pairs={{0,8},{4,12},{8,0},{12,4},{1,9},{5,13},{9,1},{13,5},{2,10},{6,14},... | collective-permute-start | bytes 786440 | tf_op jit(solution)/shard_map/ppermute | solution.py:314
  12.5 5.8 %collective-permute-done.1.b_ref = f32[128,512]{1,0:T(8,128)S(1)} collective-permute-done((f32[128,512]{1,0:T(8,128)S(1)}, f32[128,512]{1,0:T(8,128)S(1)}, u32[]{:S(2)}, u32[]{:S(2)}) %collective-permute-start.1) | collective-permute-done | bytes 262176 | tf_op jit(solution)/shard_map/ppermute | solution.py:314
  18.3 3.8 %collective-permute-done.2.c_ref = f32[128,512]{1,0:T(8,128)S(1)} collective-permute-done((f32[128,512]{1,0:T(8,128)S(1)}, f32[128,512]{1,0:T(8,128)S(1)}, u32[]{:S(2)}, u32[]{:S(2)}) %collective-permute-start.2) | collective-permute-done | bytes 262176 | tf_op jit(solution)/shard_map/ppermute | solution.py:314
  22.1 2.5 %collective-permute-done.3.d_ref = f32[128,512]{1,0:T(8,128)S(1)} collective-permute-done((f32[128,512]{1,0:T(8,128)S(1)}, f32[128,512]{1,0:T(8,128)S(1)}, u32[]{:S(2)}, u32[]{:S(2)}) %collective-permute-start.3) | collective-permute-done | bytes 262176 | tf_op jit(solution)/shard_map/ppermute | solution.py:314
  24.6 0.1 shard_map.99
  24.7 0.7 %collective-permute-start.4 = (f32[64,512]{1,0:T(8,128)S(1)}, f32[64,512]{1,0:T(8,128)S(1)}, u32[]{:S(2)}, u32[]{:S(2)}) collective-permute-start(f32[64,512]{1,0:T(8,128)S(1)} %get-tuple-element.41.a_ref), channel_id=1, source_target_pairs={{0,2},{3,1},{1,0},{2,3},{4,6},{7,5},{5,4},{6,7},{8,10},{11,9},{9,8... | collective-permute-start | bytes 393224 | tf_op jit(solution)/shard_map/ppermute | solution.py:319
  25.4 1.9 %collective-permute-start.6 = (f32[64,512]{1,0:T(8,128)S(1)}, f32[64,512]{1,0:T(8,128)S(1)}, u32[]{:S(2)}, u32[]{:S(2)}) collective-permute-start(f32[64,512]{1,0:T(8,128)S(1)} %get-tuple-element.42), channel_id=1, source_target_pairs={{1,2},{2,1},{0,0},{3,3},{5,6},{6,5},{4,4},{7,7},{9,10},{10,9},{8,8... | collective-permute-start | bytes 393224 | tf_op jit(solution)/shard_map/ppermute | solution.py:319
  27.3 0.1 collective-permute-start.5
  27.4 2.1 %collective-permute-start.9 = (f32[512,512]{1,0:T(8,128)S(1)}, f32[512,512]{1,0:T(8,128)S(1)}, u32[]{:S(2)}, u32[]{:S(2)}) collective-permute-start(f32[512,512]{1,0:T(8,128)S(1)} %collective-permute-done.8.sent_ref), channel_id=1, source_target_pairs={{0,16},{16,0},{1,17},{17,1},{2,18},{18,2},{3,19},{19,3},{4,20},{20... | collective-permute-start | bytes 3145736 | tf_op jit(solution)/shard_map/ppermute | solution.py:311
  29.5 0.3 shard_map.96
  29.8 0.4 collective-permute-done.4.b_ref
  30.2 3.7 %collective-permute-done.6.d_ref = f32[64,512]{1,0:T(8,128)S(1)} collective-permute-done((f32[64,512]{1,0:T(8,128)S(1)}, f32[64,512]{1,0:T(8,128)S(1)}, u32[]{:S(2)}, u32[]{:S(2)}) %collective-permute-start.6) | collective-permute-done | bytes 131104 | tf_op jit(solution)/shard_map/ppermute | solution.py:319
  33.8 0.6 collective-permute-done.5.c_ref
  34.5 0.3 shard_map.100
  34.8 0.3 collective-permute-start.10
  35.1 1.4 %collective-permute-start.7 = (f32[32,512]{1,0:T(8,128)S(1)}, f32[32,512]{1,0:T(8,128)S(1)}, u32[]{:S(2)}, u32[]{:S(2)}) collective-permute-start(f32[32,512]{1,0:T(8,128)S(1)} %get-tuple-element.45.given_ref), channel_id=1, source_target_pairs={{0,4},{4,0},{8,12},{12,8},{1,5},{5,1},{9,13},{13,9},{2,6},{6,2},{1... | collective-permute-start | bytes 196616 | tf_op jit(solution)/shard_map/ppermute | solution.py:314
  36.5 3.4 %shard_map.101 = (bf16[512,512]{1,0:T(8,128)(2,1)S(1)}, bf16[512,512]{1,0:T(8,128)(2,1)S(1)}, bf16[512,512]{1,0:T(8,128)(2,1)S(1)}, bf16[512,512]{1,0:T(8,128)(2...) custom-call(f32[512,512]{1,0:T(8,128)S(1)} %copy-done.1, ...), custom_call_target="tpu_custom_call" | custom-call | bytes 5242880 | tf_op jit(solution)/shard_map/pallas_call | solution.py:284
  40.0 0.1 collective-permute-start.13
  40.1 2.4 %collective-permute-start.12 = (f32[32,512]{1,0:T(8,128)S(1)}, f32[32,512]{1,0:T(8,128)S(1)}, u32[]{:S(2)}, u32[]{:S(2)}) collective-permute-start(f32[32,512]{1,0:T(8,128)S(1)} %shard_map.102.given_a_ref), channel_id=1, source_target_pairs={{0,12},{4,8},{8,4},{12,0},{1,13},{5,9},{9,5},{13,1},{2,14},{6,10},... | collective-permute-start | bytes 196616 | tf_op jit(solution)/shard_map/ppermute | solution.py:314
  42.5 1.5 %collective-permute-done.13.refs_0_ = f32[32,512]{1,0:T(8,128)S(1)} collective-permute-done((f32[32,512]{1,0:T(8,128)S(1)}, f32[32,512]{1,0:T(8,128)S(1)}, u32[]{:S(2)}, u32[]{:S(2)}) %collective-permute-start.13) | collective-permute-done | bytes 65568 | tf_op jit(solution)/shard_map/ppermute | solution.py:314
  44.1 0.3 collective-permute-start.15
  44.4 0.4 collective-permute-done.12.refs_0_
  44.8 1.1 %collective-permute-start.16 = (f32[32,512]{1,0:T(8,128)S(1)}, f32[32,512]{1,0:T(8,128)S(1)}, u32[]{:S(2)}, u32[]{:S(2)}) collective-permute-start(f32[32,512]{1,0:T(8,128)S(1)} %shard_map.105.given_ref), channel_id=1, source_target_pairs={{0,4},{4,0},{8,12},{12,8},{1,5},{5,1},{9,13},{13,9},{2,6},{6,2},{1... | collective-permute-start | bytes 196616 | tf_op jit(solution)/shard_map/ppermute | solution.py:314
  45.8 1.3 %collective-permute-start.14 = (f32[32,512]{1,0:T(8,128)S(1)}, f32[32,512]{1,0:T(8,128)S(1)}, u32[]{:S(2)}, u32[]{:S(2)}) collective-permute-start(f32[32,512]{1,0:T(8,128)S(1)} %shard_map.105.given_ref), channel_id=1, source_target_pairs={{0,8},{4,12},{8,0},{12,4},{1,9},{5,13},{9,1},{13,5},{2,10},{6,14},... | collective-permute-start | bytes 196616 | tf_op jit(solution)/shard_map/ppermute | solution.py:314
  47.1 0.3 shard_map.108.given_b_ref
  47.4 0.3 shard_map.106.given_a_ref
  47.7 0.2 collective-permute-done.15.refs_1_
  47.9 1.0 %collective-permute-done.14.refs_0_ = f32[32,512]{1,0:T(8,128)S(1)} collective-permute-done((f32[32,512]{1,0:T(8,128)S(1)}, f32[32,512]{1,0:T(8,128)S(1)}, u32[]{:S(2)}, u32[]{:S(2)}) %collective-permute-start.14) | collective-permute-done | bytes 65568 | tf_op jit(solution)/shard_map/ppermute | solution.py:314
  49.0 0.5 shard_map.109.x_ref
  49.4 0.1 collective-permute-start.20
  49.5 2.9 %collective-permute-start.19 = (f32[64,512]{1,0:T(8,128)S(1)}, f32[64,512]{1,0:T(8,128)S(1)}, u32[]{:S(2)}, u32[]{:S(2)}) collective-permute-start(f32[64,512]{1,0:T(8,128)S(1)} %shard_map.109.x_ref), channel_id=1, source_target_pairs={{1,2},{2,1},{0,0},{3,3},{5,6},{6,5},{4,4},{7,7},{9,10},{10,9},{8,8... | collective-permute-start | bytes 393224 | tf_op jit(solution)/shard_map/ppermute | solution.py:319
  52.4 0.1 collective-permute-start.18
  52.5 0.9 %collective-permute-done.20.c_ref = f32[64,512]{1,0:T(8,128)S(1)} collective-permute-done((f32[64,512]{1,0:T(8,128)S(1)}, f32[64,512]{1,0:T(8,128)S(1)}, u32[]{:S(2)}, u32[]{:S(2)}) %collective-permute-start.20) | collective-permute-done | bytes 131104 | tf_op jit(solution)/shard_map/ppermute | solution.py:319
  53.3 1.9 %collective-permute-done.19.b_ref = f32[64,512]{1,0:T(8,128)S(1)} collective-permute-done((f32[64,512]{1,0:T(8,128)S(1)}, f32[64,512]{1,0:T(8,128)S(1)}, u32[]{:S(2)}, u32[]{:S(2)}) %collective-permute-start.19) | collective-permute-done | bytes 131104 | tf_op jit(solution)/shard_map/ppermute | solution.py:319
  55.2 1.1 %collective-permute-done.18.a_ref = f32[64,512]{1,0:T(8,128)S(1)} collective-permute-done((f32[64,512]{1,0:T(8,128)S(1)}, f32[64,512]{1,0:T(8,128)S(1)}, u32[]{:S(2)}, u32[]{:S(2)}) %collective-permute-start.18) | collective-permute-done | bytes 131104 | tf_op jit(solution)/shard_map/ppermute | solution.py:319
  56.3 0.1 shard_map.110.part_ref
  56.4 6.1 %collective-permute-start.21 = (f32[512,128]{1,0:T(8,128)S(1)}, f32[512,128]{1,0:T(8,128)S(1)}, u32[]{:S(2)}, u32[]{:S(2)}) collective-permute-start(f32[512,128]{1,0:T(8,128)S(1)} %shard_map.110.part_ref), channel_id=1, source_target_pairs={{0,16},{16,0},{1,17},{17,1},{2,18},{18,2},{3,19},{19,3},{4,20},{20... | collective-permute-start | bytes 786440 | tf_op jit(solution)/shard_map/ppermute | solution.py:311
  62.6 0.7 %shard_map.111.refs_0_ = f32[512,256]{1,0:T(8,128)} custom-call(f32[512,128]{1,0:T(8,128)S(1)} %shard_map.110.part_ref), custom_call_target="tpu_custom_call" | custom-call | bytes 262144 | tf_op jit(solution)/shard_map/pallas_call | solution.py:284
  63.3 0.4 collective-permute-done.21.part_ref
  63.7 0.7 %shard_map.112 = f32[512,256]{1,0:T(8,128)} custom-call(f32[512,128]{1,0:T(8,128)S(1)} %collective-permute-done.21.part_ref, f32[512,256]{1,0:T(8,128)} %shard_map.111.refs_0_), custom_call_target="tpu_custom_call", output_to_operand_aliasing={{}: (1, {})} | custom-call | bytes 786432 | tf_op jit(solution)/shard_map/pallas_call | solution.py:284
  (20 shorter events, 0.2 us)
Async XLA Ops:
  0.6 26.7 %collective-permute-start.8 = (f32[512,512]{1,0:T(8,128)}, f32[512,512]{1,0:T(8,128)S(1)}, u32[]{:S(2)}, u32[]{:S(2)}) collective-permute-start(f32[512,512]{1,0:T(8,128)} %own_ref.1), channel_id=1, source_target_pairs={{4,5},{8,9},{12,13},{9,10},{13,14},{20,22},{24,26},{28,30},{30,29}} | collective-permute-start | bytes 3145736 | tf_op jit(solution)/shard_map/ppermute | solution.py:324
  4.9 4.1 %collective-permute-start = (f32[136,512]{1,0:T(8,128)S(1)}, f32[136,512]{1,0:T(8,128)S(1)}, u32[]{:S(2)}, u32[]{:S(2)}) collective-permute-start(f32[136,512]{1,0:T(8,128)S(1)} %get-tuple-element.31.send_ref), channel_id=1, source_target_pairs={{0,16},{16,0},{1,17},{17,1},{2,18},{18,2},{3,19},{19,3},{4,20},{20... | collective-permute-start | bytes 835592 | tf_op jit(solution)/shard_map/ppermute | solution.py:311
  9.0 20.5 %copy-start = (f32[512,512]{1,0:T(8,128)S(1)}, f32[512,512]{1,0:T(8,128)}, u32[]{:S(2)}) copy-start(f32[512,512]{1,0:T(8,128)} %diag_ref.1) | copy-start | bytes 3145732
  9.8 8.5 %collective-permute-start.1 = (f32[128,512]{1,0:T(8,128)S(1)}, f32[128,512]{1,0:T(8,128)S(1)}, u32[]{:S(2)}, u32[]{:S(2)}) collective-permute-start(f32[128,512]{1,0:T(8,128)S(1)} %get-tuple-element.38), channel_id=1, source_target_pairs={{0,12},{4,8},{8,4},{12,0},{1,13},{5,9},{9,5},{13,1},{2,14},{6,10},... | collective-permute-start | bytes 786440 | tf_op jit(solution)/shard_map/ppermute | solution.py:314
  9.8 12.3 %collective-permute-start.2 = (f32[128,512]{1,0:T(8,128)S(1)}, f32[128,512]{1,0:T(8,128)S(1)}, u32[]{:S(2)}, u32[]{:S(2)}) collective-permute-start(f32[128,512]{1,0:T(8,128)S(1)} %get-tuple-element.39), channel_id=1, source_target_pairs={{0,4},{4,0},{8,12},{12,8},{1,5},{5,1},{9,13},{13,9},{2,6},{6,2},{1... | collective-permute-start | bytes 786440 | tf_op jit(solution)/shard_map/ppermute | solution.py:314
  10.2 14.4 %collective-permute-start.3 = (f32[128,512]{1,0:T(8,128)S(1)}, f32[128,512]{1,0:T(8,128)S(1)}, u32[]{:S(2)}, u32[]{:S(2)}) collective-permute-start(f32[128,512]{1,0:T(8,128)S(1)} %get-tuple-element.40), channel_id=1, source_target_pairs={{0,8},{4,12},{8,0},{12,4},{1,9},{5,13},{9,1},{13,5},{2,10},{6,14},... | collective-permute-start | bytes 786440 | tf_op jit(solution)/shard_map/ppermute | solution.py:314
  24.6 4.9 %copy-start.2 = (f32[512,256]{1,0:T(8,128)S(1)}, f32[512,256]{1,0:T(8,128)}, u32[]{:S(2)}) copy-start(f32[512,256]{1,0:T(8,128)} %rhs_ref.1) | copy-start | bytes 1572868
  24.7 5.5 %collective-permute-start.4 = (f32[64,512]{1,0:T(8,128)S(1)}, f32[64,512]{1,0:T(8,128)S(1)}, u32[]{:S(2)}, u32[]{:S(2)}) collective-permute-start(f32[64,512]{1,0:T(8,128)S(1)} %get-tuple-element.41.a_ref), channel_id=1, source_target_pairs={{0,2},{3,1},{1,0},{2,3},{4,6},{7,5},{5,4},{6,7},{8,10},{11,9},{9,8... | collective-permute-start | bytes 393224 | tf_op jit(solution)/shard_map/ppermute | solution.py:319
  25.4 8.5 %collective-permute-start.6 = (f32[64,512]{1,0:T(8,128)S(1)}, f32[64,512]{1,0:T(8,128)S(1)}, u32[]{:S(2)}, u32[]{:S(2)}) collective-permute-start(f32[64,512]{1,0:T(8,128)S(1)} %get-tuple-element.42), channel_id=1, source_target_pairs={{1,2},{2,1},{0,0},{3,3},{5,6},{6,5},{4,4},{7,7},{9,10},{10,9},{8,8... | collective-permute-start | bytes 393224 | tf_op jit(solution)/shard_map/ppermute | solution.py:319
  27.3 7.2 %collective-permute-start.5 = (f32[64,512]{1,0:T(8,128)S(1)}, f32[64,512]{1,0:T(8,128)S(1)}, u32[]{:S(2)}, u32[]{:S(2)}) collective-permute-start(f32[64,512]{1,0:T(8,128)S(1)} %get-tuple-element.42), channel_id=1, source_target_pairs={{0,1},{3,2},{1,0},{2,3},{4,5},{7,6},{5,4},{6,7},{8,9},{11,10},{9,8... | collective-permute-start | bytes 393224 | tf_op jit(solution)/shard_map/ppermute | solution.py:319
  27.4 9.1 %collective-permute-start.9 = (f32[512,512]{1,0:T(8,128)S(1)}, f32[512,512]{1,0:T(8,128)S(1)}, u32[]{:S(2)}, u32[]{:S(2)}) collective-permute-start(f32[512,512]{1,0:T(8,128)S(1)} %collective-permute-done.8.sent_ref), channel_id=1, source_target_pairs={{0,16},{16,0},{1,17},{17,1},{2,18},{18,2},{3,19},{19,3},{4,20},{20... | collective-permute-start | bytes 3145736 | tf_op jit(solution)/shard_map/ppermute | solution.py:311
  34.5 2.1 %copy-start.1 = (f32[512,512]{1,0:T(8,128)S(1)}, f32[512,512]{1,0:T(8,128)}, u32[]{:S(2)}) copy-start(f32[512,512]{1,0:T(8,128)} %own_ref.1) | copy-start | bytes 3145732
  34.8 5.2 %collective-permute-start.10 = (f32[32,512]{1,0:T(8,128)S(1)}, f32[32,512]{1,0:T(8,128)S(1)}, u32[]{:S(2)}, u32[]{:S(2)}) collective-permute-start(f32[32,512]{1,0:T(8,128)S(1)} %get-tuple-element.48.given_ref), channel_id=1, source_target_pairs={{0,4},{4,0},{8,12},{12,8},{1,5},{5,1},{9,13},{13,9},{2,6},{6,2},{1... | collective-permute-start | bytes 196616 | tf_op jit(solution)/shard_map/ppermute | solution.py:314
  35.1 7.4 %collective-permute-start.11 = (f32[64,512]{1,0:T(8,128)S(1)}, f32[64,512]{1,0:T(8,128)S(1)}, u32[]{:S(2)}, u32[]{:S(2)}) collective-permute-start(f32[64,512]{1,0:T(8,128)S(1)} %get-tuple-element.49), channel_id=1, source_target_pairs={{0,8},{4,12},{8,0},{12,4},{1,9},{5,13},{9,1},{13,5},{2,10},{6,14},... | collective-permute-start | bytes 393224 | tf_op jit(solution)/shard_map/ppermute | solution.py:314
  35.1 4.9 %collective-permute-start.7 = (f32[32,512]{1,0:T(8,128)S(1)}, f32[32,512]{1,0:T(8,128)S(1)}, u32[]{:S(2)}, u32[]{:S(2)}) collective-permute-start(f32[32,512]{1,0:T(8,128)S(1)} %get-tuple-element.45.given_ref), channel_id=1, source_target_pairs={{0,4},{4,0},{8,12},{12,8},{1,5},{5,1},{9,13},{13,9},{2,6},{6,2},{1... | collective-permute-start | bytes 196616 | tf_op jit(solution)/shard_map/ppermute | solution.py:314
  40.0 4.1 %collective-permute-start.13 = (f32[32,512]{1,0:T(8,128)S(1)}, f32[32,512]{1,0:T(8,128)S(1)}, u32[]{:S(2)}, u32[]{:S(2)}) collective-permute-start(f32[32,512]{1,0:T(8,128)S(1)} %shard_map.103.given_b_ref), channel_id=1, source_target_pairs={{0,12},{4,8},{8,4},{12,0},{1,13},{5,9},{9,5},{13,1},{2,14},{6,10},... | collective-permute-start | bytes 196616 | tf_op jit(solution)/shard_map/ppermute | solution.py:314
  40.1 4.7 %collective-permute-start.12 = (f32[32,512]{1,0:T(8,128)S(1)}, f32[32,512]{1,0:T(8,128)S(1)}, u32[]{:S(2)}, u32[]{:S(2)}) collective-permute-start(f32[32,512]{1,0:T(8,128)S(1)} %shard_map.102.given_a_ref), channel_id=1, source_target_pairs={{0,12},{4,8},{8,4},{12,0},{1,13},{5,9},{9,5},{13,1},{2,14},{6,10},... | collective-permute-start | bytes 196616 | tf_op jit(solution)/shard_map/ppermute | solution.py:314
  44.1 3.6 %collective-permute-start.17 = (f32[32,512]{1,0:T(8,128)S(1)}, f32[32,512]{1,0:T(8,128)S(1)}, u32[]{:S(2)}, u32[]{:S(2)}) collective-permute-start(f32[32,512]{1,0:T(8,128)S(1)} %shard_map.107.given_ref), channel_id=1, source_target_pairs={{0,4},{4,0},{8,12},{12,8},{1,5},{5,1},{9,13},{13,9},{2,6},{6,2},{1... | collective-permute-start | bytes 196616 | tf_op jit(solution)/shard_map/ppermute | solution.py:314
  44.1 3.8 %collective-permute-start.15 = (f32[32,512]{1,0:T(8,128)S(1)}, f32[32,512]{1,0:T(8,128)S(1)}, u32[]{:S(2)}, u32[]{:S(2)}) collective-permute-start(f32[32,512]{1,0:T(8,128)S(1)} %shard_map.107.given_ref), channel_id=1, source_target_pairs={{0,8},{4,12},{8,0},{12,4},{1,9},{5,13},{9,1},{13,5},{2,10},{6,14},... | collective-permute-start | bytes 196616 | tf_op jit(solution)/shard_map/ppermute | solution.py:314
  44.8 3.1 %collective-permute-start.16 = (f32[32,512]{1,0:T(8,128)S(1)}, f32[32,512]{1,0:T(8,128)S(1)}, u32[]{:S(2)}, u32[]{:S(2)}) collective-permute-start(f32[32,512]{1,0:T(8,128)S(1)} %shard_map.105.given_ref), channel_id=1, source_target_pairs={{0,4},{4,0},{8,12},{12,8},{1,5},{5,1},{9,13},{13,9},{2,6},{6,2},{1... | collective-permute-start | bytes 196616 | tf_op jit(solution)/shard_map/ppermute | solution.py:314
  45.8 3.1 %collective-permute-start.14 = (f32[32,512]{1,0:T(8,128)S(1)}, f32[32,512]{1,0:T(8,128)S(1)}, u32[]{:S(2)}, u32[]{:S(2)}) collective-permute-start(f32[32,512]{1,0:T(8,128)S(1)} %shard_map.105.given_ref), channel_id=1, source_target_pairs={{0,8},{4,12},{8,0},{12,4},{1,9},{5,13},{9,1},{13,5},{2,10},{6,14},... | collective-permute-start | bytes 196616 | tf_op jit(solution)/shard_map/ppermute | solution.py:314
  49.4 3.9 %collective-permute-start.20 = (f32[64,512]{1,0:T(8,128)S(1)}, f32[64,512]{1,0:T(8,128)S(1)}, u32[]{:S(2)}, u32[]{:S(2)}) collective-permute-start(f32[64,512]{1,0:T(8,128)S(1)} %shard_map.109.x_ref), channel_id=1, source_target_pairs={{1,3},{2,0},{0,1},{3,2},{5,7},{6,4},{4,5},{7,6},{9,11},{10,8},{8,9... | collective-permute-start | bytes 393224 | tf_op jit(solution)/shard_map/ppermute | solution.py:319
  49.5 5.7 %collective-permute-start.19 = (f32[64,512]{1,0:T(8,128)S(1)}, f32[64,512]{1,0:T(8,128)S(1)}, u32[]{:S(2)}, u32[]{:S(2)}) collective-permute-start(f32[64,512]{1,0:T(8,128)S(1)} %shard_map.109.x_ref), channel_id=1, source_target_pairs={{1,2},{2,1},{0,0},{3,3},{5,6},{6,5},{4,4},{7,7},{9,10},{10,9},{8,8... | collective-permute-start | bytes 393224 | tf_op jit(solution)/shard_map/ppermute | solution.py:319
  52.4 3.9 %collective-permute-start.18 = (f32[64,512]{1,0:T(8,128)S(1)}, f32[64,512]{1,0:T(8,128)S(1)}, u32[]{:S(2)}, u32[]{:S(2)}) collective-permute-start(f32[64,512]{1,0:T(8,128)S(1)} %shard_map.109.x_ref), channel_id=1, source_target_pairs={{1,0},{2,3},{0,1},{3,2},{5,4},{6,7},{4,5},{7,6},{9,8},{10,11},{8,9... | collective-permute-start | bytes 393224 | tf_op jit(solution)/shard_map/ppermute | solution.py:319
  56.4 7.3 %collective-permute-start.21 = (f32[512,128]{1,0:T(8,128)S(1)}, f32[512,128]{1,0:T(8,128)S(1)}, u32[]{:S(2)}, u32[]{:S(2)}) collective-permute-start(f32[512,128]{1,0:T(8,128)S(1)} %shard_map.110.part_ref), channel_id=1, source_target_pairs={{0,16},{16,0},{1,17},{17,1},{2,18},{18,2},{3,19},{19,3},{4,20},{20... | collective-permute-start | bytes 786440 | tf_op jit(solution)/shard_map/ppermute | solution.py:311

commit v19 on v16

--- a/solution.py
+++ b/solution.py
@@ -331,7 +331,7 @@
     x = chain(2, [x, to2] + factor[0])
     x = chain(2, [x, on] + factor[1])
     to3 = along_row(x, 1)
-    late = along_row(x, 2)
+    late = lax.ppermute(x, "row", [(1, 3)])
     x = chain(3, [x, on] + factor[0])
     x = chain(3, [x, late] + factor[1] + [to3] + factor[2])
 

time: 64.8 us -> 65.8 us (1.015); the launches traced: 63.6 us -> 65.5 us
  waiting for transfers between devices: 30.4 us -> 31.7 us
    ppermute x0 -> x1, waiting for transfers between devices: none -> 2.71 us  [central(): late = lax.ppermute(x, 'row', [(1, 3)])]
    ppermute x8 -> x7, waiting for transfers between devices: 20.2 us -> 18.5 us  [along_row(): return lax.ppermute(value, 'row', [(r, r ^ step) for r in range(rows)])]
    ppermute x0 -> x1, starting transfers between devices: none -> 1.28 us  [central(): late = lax.ppermute(x, 'row', [(1, 3)])]
    ppermute x8 -> x7, starting transfers between devices: 4.08 us -> 4.02 us  [along_row(): return lax.ppermute(value, 'row', [(r, r ^ step) for r in range(rows)])]
where the time goes in v19:
time: 65.8 us; the launch traced here: 65.5 us
  waiting for transfers between devices  31.7 us (48%)
  starting transfers between devices  21.5 us (33%)
  Pallas kernels  10.9 us (17%)
  between operations  0.84 us (1%)
    ppermute x7, waiting for transfers between devices, along_row(): return lax.ppermute(value, 'row', [(r, r ^ step) for r in range(rows)])  18.5 us
    pallas_call x15, Pallas kernels, call(): pl.pallas_call(kernel, out_shape=[shape(i, out) for i, out in enumerate(o...  10.9 us
    ppermute x6, waiting for transfers between devices, along_col(): return lax.ppermute(value, 'col', pairs + list(zip(rest, open_ends)))  9.63 us
    ppermute x3, starting transfers between devices, swap(): return lax.ppermute(value, 'leaf', [(0, 1), (1, 0)])  8.99 us
    ppermute x6, starting transfers between devices, along_col(): return lax.ppermute(value, 'col', pairs + list(zip(rest, open_ends)))  5.95 us
    ppermute x7, starting transfers between devices, along_row(): return lax.ppermute(value, 'row', [(r, r ^ step) for r in range(rows)])  4.02 us
    ppermute x1, waiting for transfers between devices, central(): late = lax.ppermute(x, 'row', [(1, 3)])  2.71 us
  transfers between devices with their start and end apart: 18, of which 15 were waited for; matrix products, arithmetic and copies ran while one was open for 0% of the time, Pallas kernels for 15%

profile of v19, /device:TPU:15, one launch (start us, length us, event | category | flops | bytes accessed | tf_op | source)
XLA Modules:
  0.0 65.5 jit_solution(1715228900173561600)
XLA Ops:
  0.6 1.3 %collective-permute-start.8 = (f32[512,512]{1,0:T(8,128)}, f32[512,512]{1,0:T(8,128)S(1)}, u32[]{:S(2)}, u32[]{:S(2)}) collective-permute-start(f32[512,512]{1,0:T(8,128)} %own_ref.1), channel_id=1, source_target_pairs={{4,5},{8,9},{12,13},{9,10},{13,14},{20,22},{24,26},{28,30},{30,29}} | collective-permute-start | bytes 3145736 | tf_op jit(solution)/shard_map/ppermute | solution.py:291
  1.9 2.9 %shard_map.95 = (f32[2,256,256]{2,1,0:T(8,128)}, f32[128,512]{1,0:T(8,128)S(1)}, f32[136,512]{1,0:T(8,128)S(1)}) custom-call(s32[2]{0:T(128)} %live_hbm.1, f32[2,256,256]{2,1,0:T(8,128)} %rhs_hbm.1, f32[2,256,256]{2,1,0:T(8,128)} %diag_hbm.1, f32[2,256,256]{2,1,0:T(8,128)} %off_hbm.1, s32[2,256]{1,0:T(2,128)} %tgt_hbm.1), custom_call_target="tpu_custom_call" | custom-call | bytes 1574920 | tf_op jit(solution)/shard_map/pallas_call | solution.py:251
  4.9 2.9 %collective-permute-start = (f32[136,512]{1,0:T(8,128)S(1)}, f32[136,512]{1,0:T(8,128)S(1)}, u32[]{:S(2)}, u32[]{:S(2)}) collective-permute-start(f32[136,512]{1,0:T(8,128)S(1)} %get-tuple-element.26.send_ref), channel_id=1, source_target_pairs={{0,16},{16,0},{1,17},{17,1},{2,18},{18,2},{3,19},{19,3},{4,20},{20... | collective-permute-start | bytes 835592 | tf_op jit(solution)/shard_map/ppermute | solution.py:278
  7.8 0.8 %shard_map.97 = (f32[128,512]{1,0:T(8,128)S(1)}, f32[128,512]{1,0:T(8,128)S(1)}, f32[128,512]{1,0:T(8,128)S(1)}, f32[128,512]{1,0:T(8,128)S(1)}) custom-call(f32[128,512]{1,0:T(8,128)S(1)} %get-tuple-element.27.keep_ref, f32[136,512]{1,0:T(8,128)S(1)} %get-tuple-element.26.send_ref), custom_call_target="tpu_custom_call" | custom-call | bytes 540672 | tf_op jit(solution)/shard_map/pallas_call | solution.py:251
  8.6 0.4 collective-permute-done.recv_ref
  9.0 0.8 %shard_map.98 = (f32[128,512]{1,0:T(8,128)S(1)}, f32[128,512]{1,0:T(8,128)S(1)}, f32[128,512]{1,0:T(8,128)S(1)}, f32[128,512]{1,0:T(8,128)S(1)}) custom-call(f32[136,512]{1,0:T(8,128)S(1)} %collective-permute-done.recv_ref, f32[128,512]{1,0:T(8,128)S(1)} %get-tuple-element.28.refs_0_, f32[128,512]{1,0:T(8,128)S(1)} %get-tuple-element.29.refs_1_, ...), custom_call_target="tpu_custom_call" | custom-call | bytes 1327104 | tf_op jit(solution)/shard_map/pallas_call | solution.py:251
  9.8 0.1 collective-permute-start.1
  9.8 0.3 collective-permute-start.2
  10.2 2.3 %collective-permute-start.3 = (f32[128,512]{1,0:T(8,128)S(1)}, f32[128,512]{1,0:T(8,128)S(1)}, u32[]{:S(2)}, u32[]{:S(2)}) collective-permute-start(f32[128,512]{1,0:T(8,128)S(1)} %get-tuple-element.35), channel_id=1, source_target_pairs={{0,8},{4,12},{8,0},{12,4},{1,9},{5,13},{9,1},{13,5},{2,10},{6,14},... | collective-permute-start | bytes 786440 | tf_op jit(solution)/shard_map/ppermute | solution.py:281
  12.5 5.8 %collective-permute-done.1.b_ref = f32[128,512]{1,0:T(8,128)S(1)} collective-permute-done((f32[128,512]{1,0:T(8,128)S(1)}, f32[128,512]{1,0:T(8,128)S(1)}, u32[]{:S(2)}, u32[]{:S(2)}) %collective-permute-start.1) | collective-permute-done | bytes 262176 | tf_op jit(solution)/shard_map/ppermute | solution.py:281
  18.3 3.8 %collective-permute-done.2.c_ref = f32[128,512]{1,0:T(8,128)S(1)} collective-permute-done((f32[128,512]{1,0:T(8,128)S(1)}, f32[128,512]{1,0:T(8,128)S(1)}, u32[]{:S(2)}, u32[]{:S(2)}) %collective-permute-start.2) | collective-permute-done | bytes 262176 | tf_op jit(solution)/shard_map/ppermute | solution.py:281
  22.1 2.5 %collective-permute-done.3.d_ref = f32[128,512]{1,0:T(8,128)S(1)} collective-permute-done((f32[128,512]{1,0:T(8,128)S(1)}, f32[128,512]{1,0:T(8,128)S(1)}, u32[]{:S(2)}, u32[]{:S(2)}) %collective-permute-start.3) | collective-permute-done | bytes 262176 | tf_op jit(solution)/shard_map/ppermute | solution.py:281
  24.6 0.1 shard_map.99
  24.7 0.7 %collective-permute-start.4 = (f32[64,512]{1,0:T(8,128)S(1)}, f32[64,512]{1,0:T(8,128)S(1)}, u32[]{:S(2)}, u32[]{:S(2)}) collective-permute-start(f32[64,512]{1,0:T(8,128)S(1)} %get-tuple-element.36.a_ref), channel_id=1, source_target_pairs={{0,2},{3,1},{1,0},{2,3},{4,6},{7,5},{5,4},{6,7},{8,10},{11,9},{9,8... | collective-permute-start | bytes 393224 | tf_op jit(solution)/shard_map/ppermute | solution.py:286
  25.4 1.9 %collective-permute-start.6 = (f32[64,512]{1,0:T(8,128)S(1)}, f32[64,512]{1,0:T(8,128)S(1)}, u32[]{:S(2)}, u32[]{:S(2)}) collective-permute-start(f32[64,512]{1,0:T(8,128)S(1)} %get-tuple-element.37), channel_id=1, source_target_pairs={{1,2},{2,1},{0,0},{3,3},{5,6},{6,5},{4,4},{7,7},{9,10},{10,9},{8,8... | collective-permute-start | bytes 393224 | tf_op jit(solution)/shard_map/ppermute | solution.py:286
  27.3 0.1 collective-permute-start.5
  27.4 0.3 shard_map.96
  27.7 0.0 collective-permute-done.8.sent_ref
  27.7 1.7 %collective-permute-start.9 = (f32[512,512]{1,0:T(8,128)S(1)}, f32[512,512]{1,0:T(8,128)S(1)}, u32[]{:S(2)}, u32[]{:S(2)}) collective-permute-start(f32[512,512]{1,0:T(8,128)S(1)} %collective-permute-done.8.sent_ref), channel_id=1, source_target_pairs={{0,16},{16,0},{1,17},{17,1},{2,18},{18,2},{3,19},{19,3},{4,20},{20... | collective-permute-start | bytes 3145736 | tf_op jit(solution)/shard_map/ppermute | solution.py:278
  29.4 0.7 %collective-permute-done.4.b_ref = f32[64,512]{1,0:T(8,128)S(1)} collective-permute-done((f32[64,512]{1,0:T(8,128)S(1)}, f32[64,512]{1,0:T(8,128)S(1)}, u32[]{:S(2)}, u32[]{:S(2)}) %collective-permute-start.4) | collective-permute-done | bytes 131104 | tf_op jit(solution)/shard_map/ppermute | solution.py:286
  30.2 3.7 %collective-permute-done.6.d_ref = f32[64,512]{1,0:T(8,128)S(1)} collective-permute-done((f32[64,512]{1,0:T(8,128)S(1)}, f32[64,512]{1,0:T(8,128)S(1)}, u32[]{:S(2)}, u32[]{:S(2)}) %collective-permute-start.6) | collective-permute-done | bytes 131104 | tf_op jit(solution)/shard_map/ppermute | solution.py:286
  33.8 0.6 collective-permute-done.5.c_ref
  34.5 0.3 shard_map.100.given_ref
  34.8 0.3 collective-permute-start.7
  35.1 0.1 collective-permute-start.10
  35.1 0.0 collective-permute-done.9.other_ref
  35.1 0.6 copy-done.1
  35.7 3.4 %shard_map.101 = (bf16[512,512]{1,0:T(8,128)(2,1)S(1)}, bf16[512,512]{1,0:T(8,128)(2,1)S(1)}, bf16[512,512]{1,0:T(8,128)(2,1)S(1)}, bf16[512,512]{1,0:T(8,128)(2...) custom-call(f32[512,512]{1,0:T(8,128)S(1)} %copy-done.1, ...), custom_call_target="tpu_custom_call" | custom-call | bytes 5242880 | tf_op jit(solution)/shard_map/pallas_call | solution.py:251
  39.1 0.3 collective-permute-done.7.refs_0_
  39.4 0.3 collective-permute-start.11
  39.7 4.4 %collective-permute-done.11.refs_0_ = f32[64,512]{1,0:T(8,128)S(1)} collective-permute-done((f32[64,512]{1,0:T(8,128)S(1)}, f32[64,512]{1,0:T(8,128)S(1)}, u32[]{:S(2)}, u32[]{:S(2)}) %collective-permute-start.11) | collective-permute-done | bytes 131104 | tf_op jit(solution)/shard_map/ppermute | solution.py:281
  44.2 0.6 collective-permute-start.13
  44.8 1.3 %collective-permute-start.12 = (f32[64,512]{1,0:T(8,128)S(1)}, f32[64,512]{1,0:T(8,128)S(1)}, u32[]{:S(2)}, u32[]{:S(2)}) collective-permute-start(f32[64,512]{1,0:T(8,128)S(1)} %shard_map.104.given_ref), channel_id=1, source_target_pairs={{4,12},{5,13},{6,14},{7,15},{20,28},{21,29},{22,30},{23,31}} | collective-permute-start | bytes 393224 | tf_op jit(solution)/shard_map/ppermute | solution.py:334
  46.1 0.3 shard_map.105.given_ref
  46.4 1.7 %collective-permute-done.13.refs_3_ = f32[64,512]{1,0:T(8,128)S(1)} collective-permute-done((f32[64,512]{1,0:T(8,128)S(1)}, f32[64,512]{1,0:T(8,128)S(1)}, u32[]{:S(2)}, u32[]{:S(2)}) %collective-permute-start.13) | collective-permute-done | bytes 131104 | tf_op jit(solution)/shard_map/ppermute | solution.py:281
  48.1 2.7 %collective-permute-done.12.refs_0_ = f32[64,512]{1,0:T(8,128)S(1)} collective-permute-done((f32[64,512]{1,0:T(8,128)S(1)}, f32[64,512]{1,0:T(8,128)S(1)}, u32[]{:S(2)}, u32[]{:S(2)}) %collective-permute-start.12) | collective-permute-done | bytes 131104 | tf_op jit(solution)/shard_map/ppermute | solution.py:334
  50.8 0.5 shard_map.106.x_ref
  51.3 0.1 collective-permute-start.16
  51.3 3.1 %collective-permute-start.15 = (f32[64,512]{1,0:T(8,128)S(1)}, f32[64,512]{1,0:T(8,128)S(1)}, u32[]{:S(2)}, u32[]{:S(2)}) collective-permute-start(f32[64,512]{1,0:T(8,128)S(1)} %shard_map.106.x_ref), channel_id=1, source_target_pairs={{1,2},{2,1},{0,0},{3,3},{5,6},{6,5},{4,4},{7,7},{9,10},{10,9},{8,8... | collective-permute-start | bytes 393224 | tf_op jit(solution)/shard_map/ppermute | solution.py:286
  54.5 0.1 collective-permute-start.14
  54.5 0.6 collective-permute-done.16.c_ref
  55.1 1.9 %collective-permute-done.15.b_ref = f32[64,512]{1,0:T(8,128)S(1)} collective-permute-done((f32[64,512]{1,0:T(8,128)S(1)}, f32[64,512]{1,0:T(8,128)S(1)}, u32[]{:S(2)}, u32[]{:S(2)}) %collective-permute-start.15) | collective-permute-done | bytes 131104 | tf_op jit(solution)/shard_map/ppermute | solution.py:286
  57.1 2.1 %collective-permute-done.14.a_ref = f32[64,512]{1,0:T(8,128)S(1)} collective-permute-done((f32[64,512]{1,0:T(8,128)S(1)}, f32[64,512]{1,0:T(8,128)S(1)}, u32[]{:S(2)}, u32[]{:S(2)}) %collective-permute-start.14) | collective-permute-done | bytes 131104 | tf_op jit(solution)/shard_map/ppermute | solution.py:286
  59.2 0.1 shard_map.107.part_ref
  59.3 4.3 %collective-permute-start.17 = (f32[512,128]{1,0:T(8,128)S(1)}, f32[512,128]{1,0:T(8,128)S(1)}, u32[]{:S(2)}, u32[]{:S(2)}) collective-permute-start(f32[512,128]{1,0:T(8,128)S(1)} %shard_map.107.part_ref), channel_id=1, source_target_pairs={{0,16},{16,0},{1,17},{17,1},{2,18},{18,2},{3,19},{19,3},{4,20},{20... | collective-permute-start | bytes 786440 | tf_op jit(solution)/shard_map/ppermute | solution.py:278
  63.6 0.7 %shard_map.108.refs_0_ = f32[512,256]{1,0:T(8,128)} custom-call(f32[512,128]{1,0:T(8,128)S(1)} %shard_map.107.part_ref), custom_call_target="tpu_custom_call" | custom-call | bytes 262144 | tf_op jit(solution)/shard_map/pallas_call | solution.py:251
  64.4 0.4 collective-permute-done.17.part_ref
  64.8 0.7 %shard_map.109 = f32[512,256]{1,0:T(8,128)} custom-call(f32[512,128]{1,0:T(8,128)S(1)} %collective-permute-done.17.part_ref, f32[512,256]{1,0:T(8,128)} %shard_map.108.refs_0_), custom_call_target="tpu_custom_call", output_to_operand_aliasing={{}: (1, {})} | custom-call | bytes 786432 | tf_op jit(solution)/shard_map/pallas_call | solution.py:251
  (9 shorter events, 0.0 us)
Async XLA Ops:
  0.6 27.1 %collective-permute-start.8 = (f32[512,512]{1,0:T(8,128)}, f32[512,512]{1,0:T(8,128)S(1)}, u32[]{:S(2)}, u32[]{:S(2)}) collective-permute-start(f32[512,512]{1,0:T(8,128)} %own_ref.1), channel_id=1, source_target_pairs={{4,5},{8,9},{12,13},{9,10},{13,14},{20,22},{24,26},{28,30},{30,29}} | collective-permute-start | bytes 3145736 | tf_op jit(solution)/shard_map/ppermute | solution.py:291
  4.9 4.1 %collective-permute-start = (f32[136,512]{1,0:T(8,128)S(1)}, f32[136,512]{1,0:T(8,128)S(1)}, u32[]{:S(2)}, u32[]{:S(2)}) collective-permute-start(f32[136,512]{1,0:T(8,128)S(1)} %get-tuple-element.26.send_ref), channel_id=1, source_target_pairs={{0,16},{16,0},{1,17},{17,1},{2,18},{18,2},{3,19},{19,3},{4,20},{20... | collective-permute-start | bytes 835592 | tf_op jit(solution)/shard_map/ppermute | solution.py:278
  9.0 18.4 %copy-start = (f32[512,512]{1,0:T(8,128)S(1)}, f32[512,512]{1,0:T(8,128)}, u32[]{:S(2)}) copy-start(f32[512,512]{1,0:T(8,128)} %diag_ref.1) | copy-start | bytes 3145732
  9.8 8.5 %collective-permute-start.1 = (f32[128,512]{1,0:T(8,128)S(1)}, f32[128,512]{1,0:T(8,128)S(1)}, u32[]{:S(2)}, u32[]{:S(2)}) collective-permute-start(f32[128,512]{1,0:T(8,128)S(1)} %get-tuple-element.33), channel_id=1, source_target_pairs={{0,12},{4,8},{8,4},{12,0},{1,13},{5,9},{9,5},{13,1},{2,14},{6,10},... | collective-permute-start | bytes 786440 | tf_op jit(solution)/shard_map/ppermute | solution.py:281
  9.8 12.3 %collective-permute-start.2 = (f32[128,512]{1,0:T(8,128)S(1)}, f32[128,512]{1,0:T(8,128)S(1)}, u32[]{:S(2)}, u32[]{:S(2)}) collective-permute-start(f32[128,512]{1,0:T(8,128)S(1)} %get-tuple-element.34), channel_id=1, source_target_pairs={{0,4},{4,0},{8,12},{12,8},{1,5},{5,1},{9,13},{13,9},{2,6},{6,2},{1... | collective-permute-start | bytes 786440 | tf_op jit(solution)/shard_map/ppermute | solution.py:281
  10.2 14.4 %collective-permute-start.3 = (f32[128,512]{1,0:T(8,128)S(1)}, f32[128,512]{1,0:T(8,128)S(1)}, u32[]{:S(2)}, u32[]{:S(2)}) collective-permute-start(f32[128,512]{1,0:T(8,128)S(1)} %get-tuple-element.35), channel_id=1, source_target_pairs={{0,8},{4,12},{8,0},{12,4},{1,9},{5,13},{9,1},{13,5},{2,10},{6,14},... | collective-permute-start | bytes 786440 | tf_op jit(solution)/shard_map/ppermute | solution.py:281
  24.6 2.8 %copy-start.2 = (f32[512,256]{1,0:T(8,128)S(1)}, f32[512,256]{1,0:T(8,128)}, u32[]{:S(2)}) copy-start(f32[512,256]{1,0:T(8,128)} %rhs_ref.1) | copy-start | bytes 1572868
  24.7 5.5 %collective-permute-start.4 = (f32[64,512]{1,0:T(8,128)S(1)}, f32[64,512]{1,0:T(8,128)S(1)}, u32[]{:S(2)}, u32[]{:S(2)}) collective-permute-start(f32[64,512]{1,0:T(8,128)S(1)} %get-tuple-element.36.a_ref), channel_id=1, source_target_pairs={{0,2},{3,1},{1,0},{2,3},{4,6},{7,5},{5,4},{6,7},{8,10},{11,9},{9,8... | collective-permute-start | bytes 393224 | tf_op jit(solution)/shard_map/ppermute | solution.py:286
  25.4 8.5 %collective-permute-start.6 = (f32[64,512]{1,0:T(8,128)S(1)}, f32[64,512]{1,0:T(8,128)S(1)}, u32[]{:S(2)}, u32[]{:S(2)}) collective-permute-start(f32[64,512]{1,0:T(8,128)S(1)} %get-tuple-element.37), channel_id=1, source_target_pairs={{1,2},{2,1},{0,0},{3,3},{5,6},{6,5},{4,4},{7,7},{9,10},{10,9},{8,8... | collective-permute-start | bytes 393224 | tf_op jit(solution)/shard_map/ppermute | solution.py:286
  27.3 7.2 %collective-permute-start.5 = (f32[64,512]{1,0:T(8,128)S(1)}, f32[64,512]{1,0:T(8,128)S(1)}, u32[]{:S(2)}, u32[]{:S(2)}) collective-permute-start(f32[64,512]{1,0:T(8,128)S(1)} %get-tuple-element.37), channel_id=1, source_target_pairs={{0,1},{3,2},{1,0},{2,3},{4,5},{7,6},{5,4},{6,7},{8,9},{11,10},{9,8... | collective-permute-start | bytes 393224 | tf_op jit(solution)/shard_map/ppermute | solution.py:286
  27.7 7.4 %collective-permute-start.9 = (f32[512,512]{1,0:T(8,128)S(1)}, f32[512,512]{1,0:T(8,128)S(1)}, u32[]{:S(2)}, u32[]{:S(2)}) collective-permute-start(f32[512,512]{1,0:T(8,128)S(1)} %collective-permute-done.8.sent_ref), channel_id=1, source_target_pairs={{0,16},{16,0},{1,17},{17,1},{2,18},{18,2},{3,19},{19,3},{4,20},{20... | collective-permute-start | bytes 3145736 | tf_op jit(solution)/shard_map/ppermute | solution.py:278
  34.5 1.2 %copy-start.1 = (f32[512,512]{1,0:T(8,128)S(1)}, f32[512,512]{1,0:T(8,128)}, u32[]{:S(2)}) copy-start(f32[512,512]{1,0:T(8,128)} %own_ref.1) | copy-start | bytes 3145732
  34.8 4.6 %collective-permute-start.7 = (f32[64,512]{1,0:T(8,128)S(1)}, f32[64,512]{1,0:T(8,128)S(1)}, u32[]{:S(2)}, u32[]{:S(2)}) collective-permute-start(f32[64,512]{1,0:T(8,128)S(1)} %shard_map.100.given_ref), channel_id=1, source_target_pairs={{0,4},{4,0},{8,12},{12,8},{1,5},{5,1},{9,13},{13,9},{2,6},{6,2},{1... | collective-permute-start | bytes 393224 | tf_op jit(solution)/shard_map/ppermute | solution.py:281
  35.1 4.6 %collective-permute-start.10 = (f32[64,512]{1,0:T(8,128)S(1)}, f32[64,512]{1,0:T(8,128)S(1)}, u32[]{:S(2)}, u32[]{:S(2)}) collective-permute-start(f32[64,512]{1,0:T(8,128)S(1)} %shard_map.100.given_ref), channel_id=1, source_target_pairs={{0,8},{4,12},{8,0},{12,4},{1,9},{5,13},{9,1},{13,5},{2,10},{6,14},... | collective-permute-start | bytes 393224 | tf_op jit(solution)/shard_map/ppermute | solution.py:281
  39.4 4.8 %collective-permute-start.11 = (f32[64,512]{1,0:T(8,128)S(1)}, f32[64,512]{1,0:T(8,128)S(1)}, u32[]{:S(2)}, u32[]{:S(2)}) collective-permute-start(f32[64,512]{1,0:T(8,128)S(1)} %shard_map.102.given_ref), channel_id=1, source_target_pairs={{0,12},{4,8},{8,4},{12,0},{1,13},{5,9},{9,5},{13,1},{2,14},{6,10},... | collective-permute-start | bytes 393224 | tf_op jit(solution)/shard_map/ppermute | solution.py:281
  44.2 3.9 %collective-permute-start.13 = (f32[64,512]{1,0:T(8,128)S(1)}, f32[64,512]{1,0:T(8,128)S(1)}, u32[]{:S(2)}, u32[]{:S(2)}) collective-permute-start(f32[64,512]{1,0:T(8,128)S(1)} %shard_map.104.given_ref), channel_id=1, source_target_pairs={{0,4},{4,0},{8,12},{12,8},{1,5},{5,1},{9,13},{13,9},{2,6},{6,2},{1... | collective-permute-start | bytes 393224 | tf_op jit(solution)/shard_map/ppermute | solution.py:281
  44.8 6.0 %collective-permute-start.12 = (f32[64,512]{1,0:T(8,128)S(1)}, f32[64,512]{1,0:T(8,128)S(1)}, u32[]{:S(2)}, u32[]{:S(2)}) collective-permute-start(f32[64,512]{1,0:T(8,128)S(1)} %shard_map.104.given_ref), channel_id=1, source_target_pairs={{4,12},{5,13},{6,14},{7,15},{20,28},{21,29},{22,30},{23,31}} | collective-permute-start | bytes 393224 | tf_op jit(solution)/shard_map/ppermute | solution.py:334
  51.3 3.9 %collective-permute-start.16 = (f32[64,512]{1,0:T(8,128)S(1)}, f32[64,512]{1,0:T(8,128)S(1)}, u32[]{:S(2)}, u32[]{:S(2)}) collective-permute-start(f32[64,512]{1,0:T(8,128)S(1)} %shard_map.106.x_ref), channel_id=1, source_target_pairs={{1,3},{2,0},{0,1},{3,2},{5,7},{6,4},{4,5},{7,6},{9,11},{10,8},{8,9... | collective-permute-start | bytes 393224 | tf_op jit(solution)/shard_map/ppermute | solution.py:286
  51.3 5.8 %collective-permute-start.15 = (f32[64,512]{1,0:T(8,128)S(1)}, f32[64,512]{1,0:T(8,128)S(1)}, u32[]{:S(2)}, u32[]{:S(2)}) collective-permute-start(f32[64,512]{1,0:T(8,128)S(1)} %shard_map.106.x_ref), channel_id=1, source_target_pairs={{1,2},{2,1},{0,0},{3,3},{5,6},{6,5},{4,4},{7,7},{9,10},{10,9},{8,8... | collective-permute-start | bytes 393224 | tf_op jit(solution)/shard_map/ppermute | solution.py:286
  54.5 4.7 %collective-permute-start.14 = (f32[64,512]{1,0:T(8,128)S(1)}, f32[64,512]{1,0:T(8,128)S(1)}, u32[]{:S(2)}, u32[]{:S(2)}) collective-permute-start(f32[64,512]{1,0:T(8,128)S(1)} %shard_map.106.x_ref), channel_id=1, source_target_pairs={{1,0},{2,3},{0,1},{3,2},{5,4},{6,7},{4,5},{7,6},{9,8},{10,11},{8,9... | collective-permute-start | bytes 393224 | tf_op jit(solution)/shard_map/ppermute | solution.py:286
  59.3 5.5 %collective-permute-start.17 = (f32[512,128]{1,0:T(8,128)S(1)}, f32[512,128]{1,0:T(8,128)S(1)}, u32[]{:S(2)}, u32[]{:S(2)}) collective-permute-start(f32[512,128]{1,0:T(8,128)S(1)} %shard_map.107.part_ref), channel_id=1, source_target_pairs={{0,16},{16,0},{1,17},{17,1},{2,18},{18,2},{3,19},{19,3},{4,20},{20... | collective-permute-start | bytes 786440 | tf_op jit(solution)/shard_map/ppermute | solution.py:278

commit v20 on v19

--- a/solution.py
+++ b/solution.py
@@ -328,12 +328,12 @@
     to2 = along_row(x, 2)
     x = chain(1, [x, to1] + factor[0])
     on = along_row(x, 3)
+    late = lax.ppermute(x, "row", [(1, 3)])
     x = chain(2, [x, to2] + factor[0])
     x = chain(2, [x, on] + factor[1])
     to3 = along_row(x, 1)
-    late = lax.ppermute(x, "row", [(1, 3)])
-    x = chain(3, [x, on] + factor[0])
-    x = chain(3, [x, late] + factor[1] + [to3] + factor[2])
+    x = chain(3, [x, on] + factor[0] + [late] + factor[1])
+    x = chain(3, [x, to3] + factor[2])
 
     both = along_col(x, [(1, 2), (2, 1)])
     step = along_col(x, [(1, 0), (2, 3)])

time: 65.8 us -> 62.9 us (0.956)
  waiting for transfers between devices: 31.7 us -> 29.9 us
  starting transfers between devices: 21.5 us -> 20.5 us
    ppermute x7, waiting for transfers between devices: 18.5 us -> 15.5 us  [along_row(): return lax.ppermute(value, 'row', [(r, r ^ step) for r in range(rows)])]
    ppermute x3, starting transfers between devices: 8.99 us -> 7.98 us  [swap(): return lax.ppermute(value, 'leaf', [(0, 1), (1, 0)])]
  transfers between devices with their start and end apart: 18 -> 18, of which waited for: 15 -> 14; matrix products, arithmetic and copies ran while one was open for 0% -> 0% of each run, Pallas kernels for 15% -> 16%
where the time goes in v20:
time: 62.9 us; the launch traced here: 62.7 us
  waiting for transfers between devices  29.9 us (48%)
  starting transfers between devices  20.5 us (33%)
  Pallas kernels  10.9 us (17%)
  between operations  0.85 us (1%)
    ppermute x7, waiting for transfers between devices, along_row(): return lax.ppermute(value, 'row', [(r, r ^ step) for r in range(rows)])  15.5 us
    pallas_call x15, Pallas kernels, call(): pl.pallas_call(kernel, out_shape=[shape(i, out) for i, out in enumerate(o...  10.9 us
    ppermute x6, waiting for transfers between devices, along_col(): return lax.ppermute(value, 'col', pairs + list(zip(rest, open_ends)))  10.2 us
    ppermute x3, starting transfers between devices, swap(): return lax.ppermute(value, 'leaf', [(0, 1), (1, 0)])  7.98 us
    ppermute x6, starting transfers between devices, along_col(): return lax.ppermute(value, 'col', pairs + list(zip(rest, open_ends)))  5.93 us
    ppermute x7, starting transfers between devices, along_row(): return lax.ppermute(value, 'row', [(r, r ^ step) for r in range(rows)])  4.01 us
    ppermute x1, waiting for transfers between devices, central(): late = lax.ppermute(x, 'row', [(1, 3)])  3.34 us
    ppermute x1, starting transfers between devices, central(): lax.ppermute(top_factor, ('leaf', 'row', 'col'), near + [(a + shift, b +...  1.29 us
  transfers between devices with their start and end apart: 18, of which 14 were waited for; matrix products, arithmetic and copies ran while one was open for 0% of the time, Pallas kernels for 16%

profile of v20, /device:TPU:15, one launch (start us, length us, event | category | flops | bytes accessed | tf_op | source)
XLA Modules:
  0.0 62.7 jit_solution(4369748291271172024)
XLA Ops:
  0.6 1.3 %collective-permute-start.8 = (f32[512,512]{1,0:T(8,128)}, f32[512,512]{1,0:T(8,128)S(1)}, u32[]{:S(2)}, u32[]{:S(2)}) collective-permute-start(f32[512,512]{1,0:T(8,128)} %own_ref.1), channel_id=1, source_target_pairs={{4,5},{8,9},{12,13},{9,10},{13,14},{20,22},{24,26},{28,30},{30,29}} | collective-permute-start | bytes 3145736 | tf_op jit(solution)/shard_map/ppermute | solution.py:291
  1.9 2.9 %shard_map.95 = (f32[2,256,256]{2,1,0:T(8,128)}, f32[128,512]{1,0:T(8,128)S(1)}, f32[136,512]{1,0:T(8,128)S(1)}) custom-call(s32[2]{0:T(128)} %live_hbm.1, f32[2,256,256]{2,1,0:T(8,128)} %rhs_hbm.1, f32[2,256,256]{2,1,0:T(8,128)} %diag_hbm.1, f32[2,256,256]{2,1,0:T(8,128)} %off_hbm.1, s32[2,256]{1,0:T(2,128)} %tgt_hbm.1), custom_call_target="tpu_custom_call" | custom-call | bytes 1574920 | tf_op jit(solution)/shard_map/pallas_call | solution.py:251
  4.9 2.9 %collective-permute-start = (f32[136,512]{1,0:T(8,128)S(1)}, f32[136,512]{1,0:T(8,128)S(1)}, u32[]{:S(2)}, u32[]{:S(2)}) collective-permute-start(f32[136,512]{1,0:T(8,128)S(1)} %get-tuple-element.26.send_ref), channel_id=1, source_target_pairs={{0,16},{16,0},{1,17},{17,1},{2,18},{18,2},{3,19},{19,3},{4,20},{20... | collective-permute-start | bytes 835592 | tf_op jit(solution)/shard_map/ppermute | solution.py:278
  7.8 0.8 %shard_map.97 = (f32[128,512]{1,0:T(8,128)S(1)}, f32[128,512]{1,0:T(8,128)S(1)}, f32[128,512]{1,0:T(8,128)S(1)}, f32[128,512]{1,0:T(8,128)S(1)}) custom-call(f32[128,512]{1,0:T(8,128)S(1)} %get-tuple-element.27.keep_ref, f32[136,512]{1,0:T(8,128)S(1)} %get-tuple-element.26.send_ref), custom_call_target="tpu_custom_call" | custom-call | bytes 540672 | tf_op jit(solution)/shard_map/pallas_call | solution.py:251
  8.6 0.4 collective-permute-done.recv_ref
  9.0 0.8 %shard_map.98 = (f32[128,512]{1,0:T(8,128)S(1)}, f32[128,512]{1,0:T(8,128)S(1)}, f32[128,512]{1,0:T(8,128)S(1)}, f32[128,512]{1,0:T(8,128)S(1)}) custom-call(f32[136,512]{1,0:T(8,128)S(1)} %collective-permute-done.recv_ref, f32[128,512]{1,0:T(8,128)S(1)} %get-tuple-element.28.refs_0_, f32[128,512]{1,0:T(8,128)S(1)} %get-tuple-element.29.refs_1_, ...), custom_call_target="tpu_custom_call" | custom-call | bytes 1327104 | tf_op jit(solution)/shard_map/pallas_call | solution.py:251
  9.8 0.1 collective-permute-start.1
  9.8 0.3 collective-permute-start.2
  10.2 2.3 %collective-permute-start.3 = (f32[128,512]{1,0:T(8,128)S(1)}, f32[128,512]{1,0:T(8,128)S(1)}, u32[]{:S(2)}, u32[]{:S(2)}) collective-permute-start(f32[128,512]{1,0:T(8,128)S(1)} %get-tuple-element.35), channel_id=1, source_target_pairs={{0,8},{4,12},{8,0},{12,4},{1,9},{5,13},{9,1},{13,5},{2,10},{6,14},... | collective-permute-start | bytes 786440 | tf_op jit(solution)/shard_map/ppermute | solution.py:281
  12.5 5.8 %collective-permute-done.1.b_ref = f32[128,512]{1,0:T(8,128)S(1)} collective-permute-done((f32[128,512]{1,0:T(8,128)S(1)}, f32[128,512]{1,0:T(8,128)S(1)}, u32[]{:S(2)}, u32[]{:S(2)}) %collective-permute-start.1) | collective-permute-done | bytes 262176 | tf_op jit(solution)/shard_map/ppermute | solution.py:281
  18.3 3.8 %collective-permute-done.2.c_ref = f32[128,512]{1,0:T(8,128)S(1)} collective-permute-done((f32[128,512]{1,0:T(8,128)S(1)}, f32[128,512]{1,0:T(8,128)S(1)}, u32[]{:S(2)}, u32[]{:S(2)}) %collective-permute-start.2) | collective-permute-done | bytes 262176 | tf_op jit(solution)/shard_map/ppermute | solution.py:281
  22.1 2.5 %collective-permute-done.3.d_ref = f32[128,512]{1,0:T(8,128)S(1)} collective-permute-done((f32[128,512]{1,0:T(8,128)S(1)}, f32[128,512]{1,0:T(8,128)S(1)}, u32[]{:S(2)}, u32[]{:S(2)}) %collective-permute-start.3) | collective-permute-done | bytes 262176 | tf_op jit(solution)/shard_map/ppermute | solution.py:281
  24.6 0.1 shard_map.99
  24.7 0.7 %collective-permute-start.4 = (f32[64,512]{1,0:T(8,128)S(1)}, f32[64,512]{1,0:T(8,128)S(1)}, u32[]{:S(2)}, u32[]{:S(2)}) collective-permute-start(f32[64,512]{1,0:T(8,128)S(1)} %get-tuple-element.36.a_ref), channel_id=1, source_target_pairs={{0,2},{3,1},{1,0},{2,3},{4,6},{7,5},{5,4},{6,7},{8,10},{11,9},{9,8... | collective-permute-start | bytes 393224 | tf_op jit(solution)/shard_map/ppermute | solution.py:286
  25.4 1.9 %collective-permute-start.6 = (f32[64,512]{1,0:T(8,128)S(1)}, f32[64,512]{1,0:T(8,128)S(1)}, u32[]{:S(2)}, u32[]{:S(2)}) collective-permute-start(f32[64,512]{1,0:T(8,128)S(1)} %get-tuple-element.37), channel_id=1, source_target_pairs={{1,2},{2,1},{0,0},{3,3},{5,6},{6,5},{4,4},{7,7},{9,10},{10,9},{8,8... | collective-permute-start | bytes 393224 | tf_op jit(solution)/shard_map/ppermute | solution.py:286
  27.3 0.1 collective-permute-start.5
  27.4 0.3 shard_map.96
  27.7 0.0 collective-permute-done.8.sent_ref
  27.7 1.7 %collective-permute-start.9 = (f32[512,512]{1,0:T(8,128)S(1)}, f32[512,512]{1,0:T(8,128)S(1)}, u32[]{:S(2)}, u32[]{:S(2)}) collective-permute-start(f32[512,512]{1,0:T(8,128)S(1)} %collective-permute-done.8.sent_ref), channel_id=1, source_target_pairs={{0,16},{16,0},{1,17},{17,1},{2,18},{18,2},{3,19},{19,3},{4,20},{20... | collective-permute-start | bytes 3145736 | tf_op jit(solution)/shard_map/ppermute | solution.py:278
  29.4 0.7 %collective-permute-done.4.b_ref = f32[64,512]{1,0:T(8,128)S(1)} collective-permute-done((f32[64,512]{1,0:T(8,128)S(1)}, f32[64,512]{1,0:T(8,128)S(1)}, u32[]{:S(2)}, u32[]{:S(2)}) %collective-permute-start.4) | collective-permute-done | bytes 131104 | tf_op jit(solution)/shard_map/ppermute | solution.py:286
  30.2 3.7 %collective-permute-done.6.d_ref = f32[64,512]{1,0:T(8,128)S(1)} collective-permute-done((f32[64,512]{1,0:T(8,128)S(1)}, f32[64,512]{1,0:T(8,128)S(1)}, u32[]{:S(2)}, u32[]{:S(2)}) %collective-permute-start.6) | collective-permute-done | bytes 131104 | tf_op jit(solution)/shard_map/ppermute | solution.py:286
  33.8 0.6 collective-permute-done.5.c_ref
  34.5 0.3 shard_map.100.given_ref
  34.8 0.3 collective-permute-start.7
  35.1 0.1 collective-permute-start.10
  35.1 0.0 collective-permute-done.9.other_ref
  35.1 0.6 copy-done.1
  35.7 3.4 %shard_map.101 = (bf16[512,512]{1,0:T(8,128)(2,1)S(1)}, bf16[512,512]{1,0:T(8,128)(2,1)S(1)}, bf16[512,512]{1,0:T(8,128)(2,1)S(1)}, bf16[512,512]{1,0:T(8,128)(2...) custom-call(f32[512,512]{1,0:T(8,128)S(1)} %copy-done.1, ...), custom_call_target="tpu_custom_call" | custom-call | bytes 5242880 | tf_op jit(solution)/shard_map/pallas_call | solution.py:251
  39.1 0.3 collective-permute-done.7.refs_0_
  39.4 0.3 collective-permute-start.11
  39.7 1.3 %collective-permute-start.12 = (f32[64,512]{1,0:T(8,128)S(1)}, f32[64,512]{1,0:T(8,128)S(1)}, u32[]{:S(2)}, u32[]{:S(2)}) collective-permute-start(f32[64,512]{1,0:T(8,128)S(1)} %shard_map.102.given_ref), channel_id=1, source_target_pairs={{4,12},{5,13},{6,14},{7,15},{20,28},{21,29},{22,30},{23,31}} | collective-permute-start | bytes 393224 | tf_op jit(solution)/shard_map/ppermute | solution.py:331
  41.0 0.0 collective-permute-done.10.refs_0_
  41.0 3.1 %collective-permute-done.11.refs_0_ = f32[64,512]{1,0:T(8,128)S(1)} collective-permute-done((f32[64,512]{1,0:T(8,128)S(1)}, f32[64,512]{1,0:T(8,128)S(1)}, u32[]{:S(2)}, u32[]{:S(2)}) %collective-permute-start.11) | collective-permute-done | bytes 131104 | tf_op jit(solution)/shard_map/ppermute | solution.py:281
  44.2 0.6 collective-permute-start.13
  44.8 3.3 %collective-permute-done.12.refs_3_ = f32[64,512]{1,0:T(8,128)S(1)} collective-permute-done((f32[64,512]{1,0:T(8,128)S(1)}, f32[64,512]{1,0:T(8,128)S(1)}, u32[]{:S(2)}, u32[]{:S(2)}) %collective-permute-start.12) | collective-permute-done | bytes 131104 | tf_op jit(solution)/shard_map/ppermute | solution.py:331
  48.1 0.5 shard_map.105.given_ref
  48.6 0.3 shard_map.106.x_ref
  48.9 0.1 collective-permute-start.16
  49.0 3.1 %collective-permute-start.15 = (f32[64,512]{1,0:T(8,128)S(1)}, f32[64,512]{1,0:T(8,128)S(1)}, u32[]{:S(2)}, u32[]{:S(2)}) collective-permute-start(f32[64,512]{1,0:T(8,128)S(1)} %shard_map.106.x_ref), channel_id=1, source_target_pairs={{1,2},{2,1},{0,0},{3,3},{5,6},{6,5},{4,4},{7,7},{9,10},{10,9},{8,8... | collective-permute-start | bytes 393224 | tf_op jit(solution)/shard_map/ppermute | solution.py:286
  52.1 0.1 collective-permute-start.14
  52.2 0.6 collective-permute-done.16.c_ref
  52.8 2.4 %collective-permute-done.15.b_ref = f32[64,512]{1,0:T(8,128)S(1)} collective-permute-done((f32[64,512]{1,0:T(8,128)S(1)}, f32[64,512]{1,0:T(8,128)S(1)}, u32[]{:S(2)}, u32[]{:S(2)}) %collective-permute-start.15) | collective-permute-done | bytes 131104 | tf_op jit(solution)/shard_map/ppermute | solution.py:286
  55.2 2.2 %collective-permute-done.14.a_ref = f32[64,512]{1,0:T(8,128)S(1)} collective-permute-done((f32[64,512]{1,0:T(8,128)S(1)}, f32[64,512]{1,0:T(8,128)S(1)}, u32[]{:S(2)}, u32[]{:S(2)}) %collective-permute-start.14) | collective-permute-done | bytes 131104 | tf_op jit(solution)/shard_map/ppermute | solution.py:286
  57.3 0.1 shard_map.107.part_ref
  57.5 3.3 %collective-permute-start.17 = (f32[512,128]{1,0:T(8,128)S(1)}, f32[512,128]{1,0:T(8,128)S(1)}, u32[]{:S(2)}, u32[]{:S(2)}) collective-permute-start(f32[512,128]{1,0:T(8,128)S(1)} %shard_map.107.part_ref), channel_id=1, source_target_pairs={{0,16},{16,0},{1,17},{17,1},{2,18},{18,2},{3,19},{19,3},{4,20},{20... | collective-permute-start | bytes 786440 | tf_op jit(solution)/shard_map/ppermute | solution.py:278
  60.8 0.7 %shard_map.108.refs_0_ = f32[512,256]{1,0:T(8,128)} custom-call(f32[512,128]{1,0:T(8,128)S(1)} %shard_map.107.part_ref), custom_call_target="tpu_custom_call" | custom-call | bytes 262144 | tf_op jit(solution)/shard_map/pallas_call | solution.py:251
  61.5 0.4 collective-permute-done.17.part_ref
  62.0 0.7 %shard_map.109 = f32[512,256]{1,0:T(8,128)} custom-call(f32[512,128]{1,0:T(8,128)S(1)} %collective-permute-done.17.part_ref, f32[512,256]{1,0:T(8,128)} %shard_map.108.refs_0_), custom_call_target="tpu_custom_call", output_to_operand_aliasing={{}: (1, {})} | custom-call | bytes 786432 | tf_op jit(solution)/shard_map/pallas_call | solution.py:251
  (9 shorter events, 0.1 us)
Async XLA Ops:
  0.6 27.1 %collective-permute-start.8 = (f32[512,512]{1,0:T(8,128)}, f32[512,512]{1,0:T(8,128)S(1)}, u32[]{:S(2)}, u32[]{:S(2)}) collective-permute-start(f32[512,512]{1,0:T(8,128)} %own_ref.1), channel_id=1, source_target_pairs={{4,5},{8,9},{12,13},{9,10},{13,14},{20,22},{24,26},{28,30},{30,29}} | collective-permute-start | bytes 3145736 | tf_op jit(solution)/shard_map/ppermute | solution.py:291
  4.9 4.1 %collective-permute-start = (f32[136,512]{1,0:T(8,128)S(1)}, f32[136,512]{1,0:T(8,128)S(1)}, u32[]{:S(2)}, u32[]{:S(2)}) collective-permute-start(f32[136,512]{1,0:T(8,128)S(1)} %get-tuple-element.26.send_ref), channel_id=1, source_target_pairs={{0,16},{16,0},{1,17},{17,1},{2,18},{18,2},{3,19},{19,3},{4,20},{20... | collective-permute-start | bytes 835592 | tf_op jit(solution)/shard_map/ppermute | solution.py:278
  9.0 18.4 %copy-start = (f32[512,512]{1,0:T(8,128)S(1)}, f32[512,512]{1,0:T(8,128)}, u32[]{:S(2)}) copy-start(f32[512,512]{1,0:T(8,128)} %diag_ref.1) | copy-start | bytes 3145732
  9.8 8.5 %collective-permute-start.1 = (f32[128,512]{1,0:T(8,128)S(1)}, f32[128,512]{1,0:T(8,128)S(1)}, u32[]{:S(2)}, u32[]{:S(2)}) collective-permute-start(f32[128,512]{1,0:T(8,128)S(1)} %get-tuple-element.33), channel_id=1, source_target_pairs={{0,12},{4,8},{8,4},{12,0},{1,13},{5,9},{9,5},{13,1},{2,14},{6,10},... | collective-permute-start | bytes 786440 | tf_op jit(solution)/shard_map/ppermute | solution.py:281
  9.8 12.3 %collective-permute-start.2 = (f32[128,512]{1,0:T(8,128)S(1)}, f32[128,512]{1,0:T(8,128)S(1)}, u32[]{:S(2)}, u32[]{:S(2)}) collective-permute-start(f32[128,512]{1,0:T(8,128)S(1)} %get-tuple-element.34), channel_id=1, source_target_pairs={{0,4},{4,0},{8,12},{12,8},{1,5},{5,1},{9,13},{13,9},{2,6},{6,2},{1... | collective-permute-start | bytes 786440 | tf_op jit(solution)/shard_map/ppermute | solution.py:281
  10.2 14.4 %collective-permute-start.3 = (f32[128,512]{1,0:T(8,128)S(1)}, f32[128,512]{1,0:T(8,128)S(1)}, u32[]{:S(2)}, u32[]{:S(2)}) collective-permute-start(f32[128,512]{1,0:T(8,128)S(1)} %get-tuple-element.35), channel_id=1, source_target_pairs={{0,8},{4,12},{8,0},{12,4},{1,9},{5,13},{9,1},{13,5},{2,10},{6,14},... | collective-permute-start | bytes 786440 | tf_op jit(solution)/shard_map/ppermute | solution.py:281
  24.6 2.8 %copy-start.2 = (f32[512,256]{1,0:T(8,128)S(1)}, f32[512,256]{1,0:T(8,128)}, u32[]{:S(2)}) copy-start(f32[512,256]{1,0:T(8,128)} %rhs_ref.1) | copy-start | bytes 1572868
  24.7 5.5 %collective-permute-start.4 = (f32[64,512]{1,0:T(8,128)S(1)}, f32[64,512]{1,0:T(8,128)S(1)}, u32[]{:S(2)}, u32[]{:S(2)}) collective-permute-start(f32[64,512]{1,0:T(8,128)S(1)} %get-tuple-element.36.a_ref), channel_id=1, source_target_pairs={{0,2},{3,1},{1,0},{2,3},{4,6},{7,5},{5,4},{6,7},{8,10},{11,9},{9,8... | collective-permute-start | bytes 393224 | tf_op jit(solution)/shard_map/ppermute | solution.py:286
  25.4 8.5 %collective-permute-start.6 = (f32[64,512]{1,0:T(8,128)S(1)}, f32[64,512]{1,0:T(8,128)S(1)}, u32[]{:S(2)}, u32[]{:S(2)}) collective-permute-start(f32[64,512]{1,0:T(8,128)S(1)} %get-tuple-element.37), channel_id=1, source_target_pairs={{1,2},{2,1},{0,0},{3,3},{5,6},{6,5},{4,4},{7,7},{9,10},{10,9},{8,8... | collective-permute-start | bytes 393224 | tf_op jit(solution)/shard_map/ppermute | solution.py:286
  27.3 7.2 %collective-permute-start.5 = (f32[64,512]{1,0:T(8,128)S(1)}, f32[64,512]{1,0:T(8,128)S(1)}, u32[]{:S(2)}, u32[]{:S(2)}) collective-permute-start(f32[64,512]{1,0:T(8,128)S(1)} %get-tuple-element.37), channel_id=1, source_target_pairs={{0,1},{3,2},{1,0},{2,3},{4,5},{7,6},{5,4},{6,7},{8,9},{11,10},{9,8... | collective-permute-start | bytes 393224 | tf_op jit(solution)/shard_map/ppermute | solution.py:286
  27.7 7.4 %collective-permute-start.9 = (f32[512,512]{1,0:T(8,128)S(1)}, f32[512,512]{1,0:T(8,128)S(1)}, u32[]{:S(2)}, u32[]{:S(2)}) collective-permute-start(f32[512,512]{1,0:T(8,128)S(1)} %collective-permute-done.8.sent_ref), channel_id=1, source_target_pairs={{0,16},{16,0},{1,17},{17,1},{2,18},{18,2},{3,19},{19,3},{4,20},{20... | collective-permute-start | bytes 3145736 | tf_op jit(solution)/shard_map/ppermute | solution.py:278
  34.5 1.2 %copy-start.1 = (f32[512,512]{1,0:T(8,128)S(1)}, f32[512,512]{1,0:T(8,128)}, u32[]{:S(2)}) copy-start(f32[512,512]{1,0:T(8,128)} %own_ref.1) | copy-start | bytes 3145732
  34.8 4.6 %collective-permute-start.7 = (f32[64,512]{1,0:T(8,128)S(1)}, f32[64,512]{1,0:T(8,128)S(1)}, u32[]{:S(2)}, u32[]{:S(2)}) collective-permute-start(f32[64,512]{1,0:T(8,128)S(1)} %shard_map.100.given_ref), channel_id=1, source_target_pairs={{0,4},{4,0},{8,12},{12,8},{1,5},{5,1},{9,13},{13,9},{2,6},{6,2},{1... | collective-permute-start | bytes 393224 | tf_op jit(solution)/shard_map/ppermute | solution.py:281
  35.1 5.9 %collective-permute-start.10 = (f32[64,512]{1,0:T(8,128)S(1)}, f32[64,512]{1,0:T(8,128)S(1)}, u32[]{:S(2)}, u32[]{:S(2)}) collective-permute-start(f32[64,512]{1,0:T(8,128)S(1)} %shard_map.100.given_ref), channel_id=1, source_target_pairs={{0,8},{4,12},{8,0},{12,4},{1,9},{5,13},{9,1},{13,5},{2,10},{6,14},... | collective-permute-start | bytes 393224 | tf_op jit(solution)/shard_map/ppermute | solution.py:281
  39.4 4.8 %collective-permute-start.11 = (f32[64,512]{1,0:T(8,128)S(1)}, f32[64,512]{1,0:T(8,128)S(1)}, u32[]{:S(2)}, u32[]{:S(2)}) collective-permute-start(f32[64,512]{1,0:T(8,128)S(1)} %shard_map.102.given_ref), channel_id=1, source_target_pairs={{0,12},{4,8},{8,4},{12,0},{1,13},{5,9},{9,5},{13,1},{2,14},{6,10},... | collective-permute-start | bytes 393224 | tf_op jit(solution)/shard_map/ppermute | solution.py:281
  39.7 8.4 %collective-permute-start.12 = (f32[64,512]{1,0:T(8,128)S(1)}, f32[64,512]{1,0:T(8,128)S(1)}, u32[]{:S(2)}, u32[]{:S(2)}) collective-permute-start(f32[64,512]{1,0:T(8,128)S(1)} %shard_map.102.given_ref), channel_id=1, source_target_pairs={{4,12},{5,13},{6,14},{7,15},{20,28},{21,29},{22,30},{23,31}} | collective-permute-start | bytes 393224 | tf_op jit(solution)/shard_map/ppermute | solution.py:331
  44.2 4.4 %collective-permute-start.13 = (f32[64,512]{1,0:T(8,128)S(1)}, f32[64,512]{1,0:T(8,128)S(1)}, u32[]{:S(2)}, u32[]{:S(2)}) collective-permute-start(f32[64,512]{1,0:T(8,128)S(1)} %shard_map.104.given_ref), channel_id=1, source_target_pairs={{0,4},{4,0},{8,12},{12,8},{1,5},{5,1},{9,13},{13,9},{2,6},{6,2},{1... | collective-permute-start | bytes 393224 | tf_op jit(solution)/shard_map/ppermute | solution.py:281
  48.9 3.9 %collective-permute-start.16 = (f32[64,512]{1,0:T(8,128)S(1)}, f32[64,512]{1,0:T(8,128)S(1)}, u32[]{:S(2)}, u32[]{:S(2)}) collective-permute-start(f32[64,512]{1,0:T(8,128)S(1)} %shard_map.106.x_ref), channel_id=1, source_target_pairs={{1,3},{2,0},{0,1},{3,2},{5,7},{6,4},{4,5},{7,6},{9,11},{10,8},{8,9... | collective-permute-start | bytes 393224 | tf_op jit(solution)/shard_map/ppermute | solution.py:286
  49.0 6.2 %collective-permute-start.15 = (f32[64,512]{1,0:T(8,128)S(1)}, f32[64,512]{1,0:T(8,128)S(1)}, u32[]{:S(2)}, u32[]{:S(2)}) collective-permute-start(f32[64,512]{1,0:T(8,128)S(1)} %shard_map.106.x_ref), channel_id=1, source_target_pairs={{1,2},{2,1},{0,0},{3,3},{5,6},{6,5},{4,4},{7,7},{9,10},{10,9},{8,8... | collective-permute-start | bytes 393224 | tf_op jit(solution)/shard_map/ppermute | solution.py:286
  52.1 5.2 %collective-permute-start.14 = (f32[64,512]{1,0:T(8,128)S(1)}, f32[64,512]{1,0:T(8,128)S(1)}, u32[]{:S(2)}, u32[]{:S(2)}) collective-permute-start(f32[64,512]{1,0:T(8,128)S(1)} %shard_map.106.x_ref), channel_id=1, source_target_pairs={{1,0},{2,3},{0,1},{3,2},{5,4},{6,7},{4,5},{7,6},{9,8},{10,11},{8,9... | collective-permute-start | bytes 393224 | tf_op jit(solution)/shard_map/ppermute | solution.py:286
  57.5 4.5 %collective-permute-start.17 = (f32[512,128]{1,0:T(8,128)S(1)}, f32[512,128]{1,0:T(8,128)S(1)}, u32[]{:S(2)}, u32[]{:S(2)}) collective-permute-start(f32[512,128]{1,0:T(8,128)S(1)} %shard_map.107.part_ref), channel_id=1, source_target_pairs={{0,16},{16,0},{1,17},{17,1},{2,18},{18,2},{3,19},{19,3},{4,20},{20... | collective-permute-start | bytes 786440 | tf_op jit(solution)/shard_map/ppermute | solution.py:278

commit v21 on v20

--- a/solution.py
+++ b/solution.py
@@ -285,6 +285,14 @@
         open_ends = [b for b in range(cols) if b not in [p[1] for p in pairs]]
         return lax.ppermute(value, "col", pairs + list(zip(rest, open_ends)))
 
+    def exchange(axis, value, a, b):
+        count = lax.axis_size(axis)
+        pairs = [(a, b), (b, a), (a + count, b + count), (b + count, a + count)]
+        for other in range(count):
+            if other not in (a, b):
+                pairs += [(other, other + count), (other + count, other)]
+        return lax.ppermute(value, ("leaf", axis), pairs)
+
     near = [(at(k, 0), at(k, 1)) for k in (1, 2, 3)] + [(at(k, 1), at(k, 2)) for k in (2, 3)]
     far = [(at(k, 0), at(k, 2)) for k in (1, 2, 3)] + [(at(3, 2), at(3, 1))]
     shift = rows * cols
@@ -313,7 +321,7 @@
     q = [
         along_col(second, [(0, 2), (3, 1)]),
         along_col(first, [(0, 1), (3, 2)]),
-        along_col(first, [(1, 2), (2, 1)]),
+        exchange("col", first, 1, 2),
     ]
 
     factor = call(factor_kernel, [top_factor, sent, swap(sent)] + diag, [block] * 6)
@@ -324,18 +332,18 @@
         return out
 
     (x,) = call(first_kernel, [rhs_piece, second] + q + diag, [shape], flops=10 ** 10)
-    to1 = along_row(x, 1)
-    to2 = along_row(x, 2)
+    to1 = exchange("row", x, 0, 1)
+    to2 = exchange("row", x, 0, 2)
     x = chain(1, [x, to1] + factor[0])
     on = along_row(x, 3)
-    late = lax.ppermute(x, "row", [(1, 3)])
+    late = exchange("row", x, 1, 3)
     x = chain(2, [x, to2] + factor[0])
     x = chain(2, [x, on] + factor[1])
-    to3 = along_row(x, 1)
+    to3 = exchange("row", x, 2, 3)
     x = chain(3, [x, on] + factor[0] + [late] + factor[1])
     x = chain(3, [x, to3] + factor[2])
 
-    both = along_col(x, [(1, 2), (2, 1)])
+    both = exchange("col", x, 1, 2)
     step = along_col(x, [(1, 0), (2, 3)])
     over = along_col(x, [(1, 3), (2, 0)])
     (own,) = call(half_kernel, [step, both, over, x], [(size, half)])

time: 62.9 us -> 61.9 us (0.984)
  waiting for transfers between devices: 29.9 us -> 26.9 us
  starting transfers between devices: 20.5 us -> 22.3 us
    ppermute x6 -> x4, waiting for transfers between devices: 10.2 us -> 4.65 us  [along_col(): return lax.ppermute(value, 'col', pairs + list(zip(rest, open_ends)))]
    ppermute x3, starting transfers between devices: 7.98 us -> 10.7 us  [swap(): return lax.ppermute(value, 'leaf', [(0, 1), (1, 0)])]
    ppermute x1 -> x6, waiting for transfers between devices: 3.34 us -> 4.67 us  [exchange(): return lax.ppermute(value, ('leaf', axis), pairs)]
    ppermute x7 -> x4, waiting for transfers between devices: 15.5 us -> 16.7 us  [along_row(): return lax.ppermute(value, 'row', [(r, r ^ step) for r in range(rows)])]
    ppermute x6 -> x4, starting transfers between devices: 5.93 us -> 5.01 us  [along_col(): return lax.ppermute(value, 'col', pairs + list(zip(rest, open_ends)))]
    ppermute x1 -> x6, starting transfers between devices: 1.28 us -> 2.02 us  [exchange(): return lax.ppermute(value, ('leaf', axis), pairs)]
    ppermute x7 -> x4, starting transfers between devices: 4.01 us -> 3.28 us  [along_row(): return lax.ppermute(value, 'row', [(r, r ^ step) for r in range(rows)])]
  transfers between devices with their start and end apart: 18 -> 18, of which waited for: 14 -> 12; matrix products, arithmetic and copies ran while one was open for 0% -> 0% of each run, Pallas kernels for 16% -> 16%
where the time goes in v21:
time: 61.9 us; the launch traced here: 61.2 us
  waiting for transfers between devices  26.9 us (43%)
  starting transfers between devices  22.3 us (36%)
  Pallas kernels  10.9 us (18%)
  between operations  0.8 us (1%)
    ppermute x4, waiting for transfers between devices, along_row(): return lax.ppermute(value, 'row', [(r, r ^ step) for r in range(rows)])  16.7 us
    pallas_call x15, Pallas kernels, call(): pl.pallas_call(kernel, out_shape=[shape(i, out) for i, out in enumerate(o...  10.9 us
    ppermute x3, starting transfers between devices, swap(): return lax.ppermute(value, 'leaf', [(0, 1), (1, 0)])  10.7 us
    ppermute x4, starting transfers between devices, along_col(): return lax.ppermute(value, 'col', pairs + list(zip(rest, open_ends)))  5.01 us
    ppermute x6, waiting for transfers between devices, exchange(): return lax.ppermute(value, ('leaf', axis), pairs)  4.67 us
    ppermute x4, waiting for transfers between devices, along_col(): return lax.ppermute(value, 'col', pairs + list(zip(rest, open_ends)))  4.65 us
    ppermute x4, starting transfers between devices, along_row(): return lax.ppermute(value, 'row', [(r, r ^ step) for r in range(rows)])  3.28 us
    ppermute x6, starting transfers between devices, exchange(): return lax.ppermute(value, ('leaf', axis), pairs)  2.02 us
  transfers between devices with their start and end apart: 18, of which 12 were waited for; matrix products, arithmetic and copies ran while one was open for 0% of the time, Pallas kernels for 16%

profile of v21, /device:TPU:15, one launch (start us, length us, event | category | flops | bytes accessed | tf_op | source)
XLA Modules:
  0.0 61.2 jit_solution(2513663753576674988)
XLA Ops:
  0.6 1.3 %collective-permute-start.8 = (f32[512,512]{1,0:T(8,128)}, f32[512,512]{1,0:T(8,128)S(1)}, u32[]{:S(2)}, u32[]{:S(2)}) collective-permute-start(f32[512,512]{1,0:T(8,128)} %own_ref.1), channel_id=1, source_target_pairs={{4,5},{8,9},{12,13},{9,10},{13,14},{20,22},{24,26},{28,30},{30,29}} | collective-permute-start | bytes 3145736 | tf_op jit(solution)/shard_map/ppermute | solution.py:299
  1.9 2.9 %shard_map.95 = (f32[2,256,256]{2,1,0:T(8,128)}, f32[128,512]{1,0:T(8,128)S(1)}, f32[136,512]{1,0:T(8,128)S(1)}) custom-call(s32[2]{0:T(128)} %live_hbm.1, f32[2,256,256]{2,1,0:T(8,128)} %rhs_hbm.1, f32[2,256,256]{2,1,0:T(8,128)} %diag_hbm.1, f32[2,256,256]{2,1,0:T(8,128)} %off_hbm.1, s32[2,256]{1,0:T(2,128)} %tgt_hbm.1), custom_call_target="tpu_custom_call" | custom-call | bytes 1574920 | tf_op jit(solution)/shard_map/pallas_call | solution.py:251
  4.9 2.9 %collective-permute-start = (f32[136,512]{1,0:T(8,128)S(1)}, f32[136,512]{1,0:T(8,128)S(1)}, u32[]{:S(2)}, u32[]{:S(2)}) collective-permute-start(f32[136,512]{1,0:T(8,128)S(1)} %get-tuple-element.26.send_ref), channel_id=1, source_target_pairs={{0,16},{16,0},{1,17},{17,1},{2,18},{18,2},{3,19},{19,3},{4,20},{20... | collective-permute-start | bytes 835592 | tf_op jit(solution)/shard_map/ppermute | solution.py:278
  7.8 0.8 %shard_map.97 = (f32[128,512]{1,0:T(8,128)S(1)}, f32[128,512]{1,0:T(8,128)S(1)}, f32[128,512]{1,0:T(8,128)S(1)}, f32[128,512]{1,0:T(8,128)S(1)}) custom-call(f32[128,512]{1,0:T(8,128)S(1)} %get-tuple-element.27.keep_ref, f32[136,512]{1,0:T(8,128)S(1)} %get-tuple-element.26.send_ref), custom_call_target="tpu_custom_call" | custom-call | bytes 540672 | tf_op jit(solution)/shard_map/pallas_call | solution.py:251
  8.6 0.4 collective-permute-done.recv_ref
  9.0 0.8 %shard_map.98 = (f32[128,512]{1,0:T(8,128)S(1)}, f32[128,512]{1,0:T(8,128)S(1)}, f32[128,512]{1,0:T(8,128)S(1)}, f32[128,512]{1,0:T(8,128)S(1)}) custom-call(f32[136,512]{1,0:T(8,128)S(1)} %collective-permute-done.recv_ref, f32[128,512]{1,0:T(8,128)S(1)} %get-tuple-element.28.refs_0_, f32[128,512]{1,0:T(8,128)S(1)} %get-tuple-element.29.refs_1_, ...), custom_call_target="tpu_custom_call" | custom-call | bytes 1327104 | tf_op jit(solution)/shard_map/pallas_call | solution.py:251
  9.8 0.1 collective-permute-start.1
  9.8 0.3 collective-permute-start.2
  10.2 2.3 %collective-permute-start.3 = (f32[128,512]{1,0:T(8,128)S(1)}, f32[128,512]{1,0:T(8,128)S(1)}, u32[]{:S(2)}, u32[]{:S(2)}) collective-permute-start(f32[128,512]{1,0:T(8,128)S(1)} %get-tuple-element.35), channel_id=1, source_target_pairs={{0,8},{4,12},{8,0},{12,4},{1,9},{5,13},{9,1},{13,5},{2,10},{6,14},... | collective-permute-start | bytes 786440 | tf_op jit(solution)/shard_map/ppermute | solution.py:281
  12.5 5.8 %collective-permute-done.1.b_ref = f32[128,512]{1,0:T(8,128)S(1)} collective-permute-done((f32[128,512]{1,0:T(8,128)S(1)}, f32[128,512]{1,0:T(8,128)S(1)}, u32[]{:S(2)}, u32[]{:S(2)}) %collective-permute-start.1) | collective-permute-done | bytes 262176 | tf_op jit(solution)/shard_map/ppermute | solution.py:281
  18.3 3.8 %collective-permute-done.2.c_ref = f32[128,512]{1,0:T(8,128)S(1)} collective-permute-done((f32[128,512]{1,0:T(8,128)S(1)}, f32[128,512]{1,0:T(8,128)S(1)}, u32[]{:S(2)}, u32[]{:S(2)}) %collective-permute-start.2) | collective-permute-done | bytes 262176 | tf_op jit(solution)/shard_map/ppermute | solution.py:281
  22.1 2.5 %collective-permute-done.3.d_ref = f32[128,512]{1,0:T(8,128)S(1)} collective-permute-done((f32[128,512]{1,0:T(8,128)S(1)}, f32[128,512]{1,0:T(8,128)S(1)}, u32[]{:S(2)}, u32[]{:S(2)}) %collective-permute-start.3) | collective-permute-done | bytes 262176 | tf_op jit(solution)/shard_map/ppermute | solution.py:281
  24.6 0.1 shard_map.99
  24.7 0.7 %collective-permute-start.4 = (f32[64,512]{1,0:T(8,128)S(1)}, f32[64,512]{1,0:T(8,128)S(1)}, u32[]{:S(2)}, u32[]{:S(2)}) collective-permute-start(f32[64,512]{1,0:T(8,128)S(1)} %get-tuple-element.36.a_ref), channel_id=1, source_target_pairs={{0,2},{3,1},{1,0},{2,3},{4,6},{7,5},{5,4},{6,7},{8,10},{11,9},{9,8... | collective-permute-start | bytes 393224 | tf_op jit(solution)/shard_map/ppermute | solution.py:286
  25.4 0.0 collective-permute-start.6
  25.4 0.9 %collective-permute-start.5 = (f32[64,512]{1,0:T(8,128)S(1)}, f32[64,512]{1,0:T(8,128)S(1)}, u32[]{:S(2)}, u32[]{:S(2)}) collective-permute-start(f32[64,512]{1,0:T(8,128)S(1)} %get-tuple-element.37), channel_id=1, source_target_pairs={{0,1},{3,2},{1,0},{2,3},{4,5},{7,6},{5,4},{6,7},{8,9},{11,10},{9,8... | collective-permute-start | bytes 393224 | tf_op jit(solution)/shard_map/ppermute | solution.py:286
  26.3 0.3 shard_map.96
  26.6 0.0 collective-permute-done.8.sent_ref
  26.6 5.7 %collective-permute-start.9 = (f32[512,512]{1,0:T(8,128)S(1)}, f32[512,512]{1,0:T(8,128)S(1)}, u32[]{:S(2)}, u32[]{:S(2)}) collective-permute-start(f32[512,512]{1,0:T(8,128)S(1)} %collective-permute-done.8.sent_ref), channel_id=1, source_target_pairs={{0,16},{16,0},{1,17},{17,1},{2,18},{18,2},{3,19},{19,3},{4,20},{20... | collective-permute-start | bytes 3145736 | tf_op jit(solution)/shard_map/ppermute | solution.py:278
  32.3 1.0 %collective-permute-done.6.d_ref = f32[64,512]{1,0:T(8,128)S(1)} collective-permute-done((f32[64,512]{1,0:T(8,128)S(1)}, f32[64,512]{1,0:T(8,128)S(1)}, u32[]{:S(2)}, u32[]{:S(2)}) %collective-permute-start.6) | collective-permute-done | bytes 131104 | tf_op jit(solution)/shard_map/ppermute | solution.py:294
  33.4 1.1 %collective-permute-done.5.c_ref = f32[64,512]{1,0:T(8,128)S(1)} collective-permute-done((f32[64,512]{1,0:T(8,128)S(1)}, f32[64,512]{1,0:T(8,128)S(1)}, u32[]{:S(2)}, u32[]{:S(2)}) %collective-permute-start.5) | collective-permute-done | bytes 131104 | tf_op jit(solution)/shard_map/ppermute | solution.py:286
  34.5 0.3 shard_map.100.given_ref
  34.8 0.6 collective-permute-start.7
  35.3 0.1 collective-permute-start.10
  35.4 0.0 collective-permute-done.9.other_ref
  35.4 0.3 copy-done.1
  35.7 3.4 %shard_map.101 = (bf16[512,512]{1,0:T(8,128)(2,1)S(1)}, bf16[512,512]{1,0:T(8,128)(2,1)S(1)}, bf16[512,512]{1,0:T(8,128)(2,1)S(1)}, bf16[512,512]{1,0:T(8,128)(2...) custom-call(f32[512,512]{1,0:T(8,128)S(1)} %copy-done.1, ...), custom_call_target="tpu_custom_call" | custom-call | bytes 5242880 | tf_op jit(solution)/shard_map/pallas_call | solution.py:251
  39.1 0.0 collective-permute-done.7.refs_0_
  39.1 0.6 collective-permute-start.11
  39.7 0.3 collective-permute-start.12
  40.1 0.0 collective-permute-done.10.refs_0_
  40.1 4.6 %collective-permute-done.11.refs_0_ = f32[64,512]{1,0:T(8,128)S(1)} collective-permute-done((f32[64,512]{1,0:T(8,128)S(1)}, f32[64,512]{1,0:T(8,128)S(1)}, u32[]{:S(2)}, u32[]{:S(2)}) %collective-permute-start.11) | collective-permute-done | bytes 131104 | tf_op jit(solution)/shard_map/ppermute | solution.py:281
  44.7 0.1 collective-permute-start.13
  44.8 2.7 %collective-permute-done.12.refs_3_ = f32[64,512]{1,0:T(8,128)S(1)} collective-permute-done((f32[64,512]{1,0:T(8,128)S(1)}, f32[64,512]{1,0:T(8,128)S(1)}, u32[]{:S(2)}, u32[]{:S(2)}) %collective-permute-start.12) | collective-permute-done | bytes 131104 | tf_op jit(solution)/shard_map/ppermute | solution.py:294
  47.5 0.5 shard_map.105.given_ref
  48.0 0.6 %collective-permute-done.13.refs_0_ = f32[64,512]{1,0:T(8,128)S(1)} collective-permute-done((f32[64,512]{1,0:T(8,128)S(1)}, f32[64,512]{1,0:T(8,128)S(1)}, u32[]{:S(2)}, u32[]{:S(2)}) %collective-permute-start.13) | collective-permute-done | bytes 131104 | tf_op jit(solution)/shard_map/ppermute | solution.py:294
  48.6 0.3 shard_map.106.x_ref
  48.9 0.1 collective-permute-start.16
  49.0 0.9 %collective-permute-start.15 = (f32[64,512]{1,0:T(8,128)S(1)}, f32[64,512]{1,0:T(8,128)S(1)}, u32[]{:S(2)}, u32[]{:S(2)}) collective-permute-start(f32[64,512]{1,0:T(8,128)S(1)} %shard_map.106.x_ref), channel_id=1, source_target_pairs={{1,2},{2,1},{17,18},{18,17},{0,16},{16,0},{3,19},{19,3},{5,6},{6,5... | collective-permute-start | bytes 393224 | tf_op jit(solution)/shard_map/ppermute | solution.py:294
  49.9 3.4 %collective-permute-start.14 = (f32[64,512]{1,0:T(8,128)S(1)}, f32[64,512]{1,0:T(8,128)S(1)}, u32[]{:S(2)}, u32[]{:S(2)}) collective-permute-start(f32[64,512]{1,0:T(8,128)S(1)} %shard_map.106.x_ref), channel_id=1, source_target_pairs={{1,0},{2,3},{0,1},{3,2},{5,4},{6,7},{4,5},{7,6},{9,8},{10,11},{8,9... | collective-permute-start | bytes 393224 | tf_op jit(solution)/shard_map/ppermute | solution.py:286
  53.3 0.0 collective-permute-done.16.c_ref
  53.3 0.3 collective-permute-done.15.b_ref
  53.6 3.5 %collective-permute-done.14.a_ref = f32[64,512]{1,0:T(8,128)S(1)} collective-permute-done((f32[64,512]{1,0:T(8,128)S(1)}, f32[64,512]{1,0:T(8,128)S(1)}, u32[]{:S(2)}, u32[]{:S(2)}) %collective-permute-start.14) | collective-permute-done | bytes 131104 | tf_op jit(solution)/shard_map/ppermute | solution.py:286
  57.2 0.1 shard_map.107.part_ref
  57.3 2.0 %collective-permute-start.17 = (f32[512,128]{1,0:T(8,128)S(1)}, f32[512,128]{1,0:T(8,128)S(1)}, u32[]{:S(2)}, u32[]{:S(2)}) collective-permute-start(f32[512,128]{1,0:T(8,128)S(1)} %shard_map.107.part_ref), channel_id=1, source_target_pairs={{0,16},{16,0},{1,17},{17,1},{2,18},{18,2},{3,19},{19,3},{4,20},{20... | collective-permute-start | bytes 786440 | tf_op jit(solution)/shard_map/ppermute | solution.py:278
  59.4 0.7 %shard_map.108.refs_0_ = f32[512,256]{1,0:T(8,128)} custom-call(f32[512,128]{1,0:T(8,128)S(1)} %shard_map.107.part_ref), custom_call_target="tpu_custom_call" | custom-call | bytes 262144 | tf_op jit(solution)/shard_map/pallas_call | solution.py:251
  60.1 0.4 collective-permute-done.17.part_ref
  60.5 0.7 %shard_map.109 = f32[512,256]{1,0:T(8,128)} custom-call(f32[512,128]{1,0:T(8,128)S(1)} %collective-permute-done.17.part_ref, f32[512,256]{1,0:T(8,128)} %shard_map.108.refs_0_), custom_call_target="tpu_custom_call", output_to_operand_aliasing={{}: (1, {})} | custom-call | bytes 786432 | tf_op jit(solution)/shard_map/pallas_call | solution.py:251
  (9 shorter events, 0.1 us)
Async XLA Ops:
  0.6 26.0 %collective-permute-start.8 = (f32[512,512]{1,0:T(8,128)}, f32[512,512]{1,0:T(8,128)S(1)}, u32[]{:S(2)}, u32[]{:S(2)}) collective-permute-start(f32[512,512]{1,0:T(8,128)} %own_ref.1), channel_id=1, source_target_pairs={{4,5},{8,9},{12,13},{9,10},{13,14},{20,22},{24,26},{28,30},{30,29}} | collective-permute-start | bytes 3145736 | tf_op jit(solution)/shard_map/ppermute | solution.py:299
  4.9 4.1 %collective-permute-start = (f32[136,512]{1,0:T(8,128)S(1)}, f32[136,512]{1,0:T(8,128)S(1)}, u32[]{:S(2)}, u32[]{:S(2)}) collective-permute-start(f32[136,512]{1,0:T(8,128)S(1)} %get-tuple-element.26.send_ref), channel_id=1, source_target_pairs={{0,16},{16,0},{1,17},{17,1},{2,18},{18,2},{3,19},{19,3},{4,20},{20... | collective-permute-start | bytes 835592 | tf_op jit(solution)/shard_map/ppermute | solution.py:278
  9.0 17.3 %copy-start = (f32[512,512]{1,0:T(8,128)S(1)}, f32[512,512]{1,0:T(8,128)}, u32[]{:S(2)}) copy-start(f32[512,512]{1,0:T(8,128)} %diag_ref.1) | copy-start | bytes 3145732
  9.8 8.5 %collective-permute-start.1 = (f32[128,512]{1,0:T(8,128)S(1)}, f32[128,512]{1,0:T(8,128)S(1)}, u32[]{:S(2)}, u32[]{:S(2)}) collective-permute-start(f32[128,512]{1,0:T(8,128)S(1)} %get-tuple-element.33), channel_id=1, source_target_pairs={{0,12},{4,8},{8,4},{12,0},{1,13},{5,9},{9,5},{13,1},{2,14},{6,10},... | collective-permute-start | bytes 786440 | tf_op jit(solution)/shard_map/ppermute | solution.py:281
  9.8 12.3 %collective-permute-start.2 = (f32[128,512]{1,0:T(8,128)S(1)}, f32[128,512]{1,0:T(8,128)S(1)}, u32[]{:S(2)}, u32[]{:S(2)}) collective-permute-start(f32[128,512]{1,0:T(8,128)S(1)} %get-tuple-element.34), channel_id=1, source_target_pairs={{0,4},{4,0},{8,12},{12,8},{1,5},{5,1},{9,13},{13,9},{2,6},{6,2},{1... | collective-permute-start | bytes 786440 | tf_op jit(solution)/shard_map/ppermute | solution.py:281
  10.2 14.4 %collective-permute-start.3 = (f32[128,512]{1,0:T(8,128)S(1)}, f32[128,512]{1,0:T(8,128)S(1)}, u32[]{:S(2)}, u32[]{:S(2)}) collective-permute-start(f32[128,512]{1,0:T(8,128)S(1)} %get-tuple-element.35), channel_id=1, source_target_pairs={{0,8},{4,12},{8,0},{12,4},{1,9},{5,13},{9,1},{13,5},{2,10},{6,14},... | collective-permute-start | bytes 786440 | tf_op jit(solution)/shard_map/ppermute | solution.py:281
  24.6 1.7 %copy-start.2 = (f32[512,256]{1,0:T(8,128)S(1)}, f32[512,256]{1,0:T(8,128)}, u32[]{:S(2)}) copy-start(f32[512,256]{1,0:T(8,128)} %rhs_ref.1) | copy-start | bytes 1572868
  24.7 7.7 %collective-permute-start.4 = (f32[64,512]{1,0:T(8,128)S(1)}, f32[64,512]{1,0:T(8,128)S(1)}, u32[]{:S(2)}, u32[]{:S(2)}) collective-permute-start(f32[64,512]{1,0:T(8,128)S(1)} %get-tuple-element.36.a_ref), channel_id=1, source_target_pairs={{0,2},{3,1},{1,0},{2,3},{4,6},{7,5},{5,4},{6,7},{8,10},{11,9},{9,8... | collective-permute-start | bytes 393224 | tf_op jit(solution)/shard_map/ppermute | solution.py:286
  25.4 8.0 %collective-permute-start.6 = (f32[64,512]{1,0:T(8,128)S(1)}, f32[64,512]{1,0:T(8,128)S(1)}, u32[]{:S(2)}, u32[]{:S(2)}) collective-permute-start(f32[64,512]{1,0:T(8,128)S(1)} %get-tuple-element.37), channel_id=1, source_target_pairs={{1,2},{2,1},{17,18},{18,17},{0,16},{16,0},{3,19},{19,3},{5,6},{6,5... | collective-permute-start | bytes 393224 | tf_op jit(solution)/shard_map/ppermute | solution.py:294
  25.4 9.1 %collective-permute-start.5 = (f32[64,512]{1,0:T(8,128)S(1)}, f32[64,512]{1,0:T(8,128)S(1)}, u32[]{:S(2)}, u32[]{:S(2)}) collective-permute-start(f32[64,512]{1,0:T(8,128)S(1)} %get-tuple-element.37), channel_id=1, source_target_pairs={{0,1},{3,2},{1,0},{2,3},{4,5},{7,6},{5,4},{6,7},{8,9},{11,10},{9,8... | collective-permute-start | bytes 393224 | tf_op jit(solution)/shard_map/ppermute | solution.py:286
  26.6 8.8 %collective-permute-start.9 = (f32[512,512]{1,0:T(8,128)S(1)}, f32[512,512]{1,0:T(8,128)S(1)}, u32[]{:S(2)}, u32[]{:S(2)}) collective-permute-start(f32[512,512]{1,0:T(8,128)S(1)} %collective-permute-done.8.sent_ref), channel_id=1, source_target_pairs={{0,16},{16,0},{1,17},{17,1},{2,18},{18,2},{3,19},{19,3},{4,20},{20... | collective-permute-start | bytes 3145736 | tf_op jit(solution)/shard_map/ppermute | solution.py:278
  34.5 1.2 %copy-start.1 = (f32[512,512]{1,0:T(8,128)S(1)}, f32[512,512]{1,0:T(8,128)}, u32[]{:S(2)}) copy-start(f32[512,512]{1,0:T(8,128)} %own_ref.1) | copy-start | bytes 3145732
  34.8 4.4 %collective-permute-start.7 = (f32[64,512]{1,0:T(8,128)S(1)}, f32[64,512]{1,0:T(8,128)S(1)}, u32[]{:S(2)}, u32[]{:S(2)}) collective-permute-start(f32[64,512]{1,0:T(8,128)S(1)} %shard_map.100.given_ref), channel_id=1, source_target_pairs={{0,4},{4,0},{16,20},{20,16},{8,24},{24,8},{12,28},{28,12},{1,5},{5... | collective-permute-start | bytes 393224 | tf_op jit(solution)/shard_map/ppermute | solution.py:294
  35.3 4.7 %collective-permute-start.10 = (f32[64,512]{1,0:T(8,128)S(1)}, f32[64,512]{1,0:T(8,128)S(1)}, u32[]{:S(2)}, u32[]{:S(2)}) collective-permute-start(f32[64,512]{1,0:T(8,128)S(1)} %shard_map.100.given_ref), channel_id=1, source_target_pairs={{0,8},{8,0},{16,24},{24,16},{4,20},{20,4},{12,28},{28,12},{1,9},{9... | collective-permute-start | bytes 393224 | tf_op jit(solution)/shard_map/ppermute | solution.py:294
  39.1 5.6 %collective-permute-start.11 = (f32[64,512]{1,0:T(8,128)S(1)}, f32[64,512]{1,0:T(8,128)S(1)}, u32[]{:S(2)}, u32[]{:S(2)}) collective-permute-start(f32[64,512]{1,0:T(8,128)S(1)} %shard_map.102.given_ref), channel_id=1, source_target_pairs={{0,12},{4,8},{8,4},{12,0},{1,13},{5,9},{9,5},{13,1},{2,14},{6,10},... | collective-permute-start | bytes 393224 | tf_op jit(solution)/shard_map/ppermute | solution.py:281
  39.7 7.8 %collective-permute-start.12 = (f32[64,512]{1,0:T(8,128)S(1)}, f32[64,512]{1,0:T(8,128)S(1)}, u32[]{:S(2)}, u32[]{:S(2)}) collective-permute-start(f32[64,512]{1,0:T(8,128)S(1)} %shard_map.102.given_ref), channel_id=1, source_target_pairs={{4,12},{12,4},{20,28},{28,20},{0,16},{16,0},{8,24},{24,8},{5,13},{... | collective-permute-start | bytes 393224 | tf_op jit(solution)/shard_map/ppermute | solution.py:294
  44.7 3.9 %collective-permute-start.13 = (f32[64,512]{1,0:T(8,128)S(1)}, f32[64,512]{1,0:T(8,128)S(1)}, u32[]{:S(2)}, u32[]{:S(2)}) collective-permute-start(f32[64,512]{1,0:T(8,128)S(1)} %shard_map.104.given_ref), channel_id=1, source_target_pairs={{8,12},{12,8},{24,28},{28,24},{0,16},{16,0},{4,20},{20,4},{9,13},{... | collective-permute-start | bytes 393224 | tf_op jit(solution)/shard_map/ppermute | solution.py:294
  48.9 4.4 %collective-permute-start.16 = (f32[64,512]{1,0:T(8,128)S(1)}, f32[64,512]{1,0:T(8,128)S(1)}, u32[]{:S(2)}, u32[]{:S(2)}) collective-permute-start(f32[64,512]{1,0:T(8,128)S(1)} %shard_map.106.x_ref), channel_id=1, source_target_pairs={{1,3},{2,0},{0,1},{3,2},{5,7},{6,4},{4,5},{7,6},{9,11},{10,8},{8,9... | collective-permute-start | bytes 393224 | tf_op jit(solution)/shard_map/ppermute | solution.py:286
  49.0 4.6 %collective-permute-start.15 = (f32[64,512]{1,0:T(8,128)S(1)}, f32[64,512]{1,0:T(8,128)S(1)}, u32[]{:S(2)}, u32[]{:S(2)}) collective-permute-start(f32[64,512]{1,0:T(8,128)S(1)} %shard_map.106.x_ref), channel_id=1, source_target_pairs={{1,2},{2,1},{17,18},{18,17},{0,16},{16,0},{3,19},{19,3},{5,6},{6,5... | collective-permute-start | bytes 393224 | tf_op jit(solution)/shard_map/ppermute | solution.py:294
  49.9 7.2 %collective-permute-start.14 = (f32[64,512]{1,0:T(8,128)S(1)}, f32[64,512]{1,0:T(8,128)S(1)}, u32[]{:S(2)}, u32[]{:S(2)}) collective-permute-start(f32[64,512]{1,0:T(8,128)S(1)} %shard_map.106.x_ref), channel_id=1, source_target_pairs={{1,0},{2,3},{0,1},{3,2},{5,4},{6,7},{4,5},{7,6},{9,8},{10,11},{8,9... | collective-permute-start | bytes 393224 | tf_op jit(solution)/shard_map/ppermute | solution.py:286
  57.3 3.2 %collective-permute-start.17 = (f32[512,128]{1,0:T(8,128)S(1)}, f32[512,128]{1,0:T(8,128)S(1)}, u32[]{:S(2)}, u32[]{:S(2)}) collective-permute-start(f32[512,128]{1,0:T(8,128)S(1)} %shard_map.107.part_ref), channel_id=1, source_target_pairs={{0,16},{16,0},{1,17},{17,1},{2,18},{18,2},{3,19},{19,3},{4,20},{20... | collective-permute-start | bytes 786440 | tf_op jit(solution)/shard_map/ppermute | solution.py:278

commit v22 on v21

--- a/solution.py
+++ b/solution.py
@@ -222,7 +222,7 @@
         out_ref[...] = left
 
 
-def half_kernel(a_ref, b_ref, c_ref, x_ref, out_ref):
+def half_kernel(b_ref, a_ref, c_ref, x_ref, out_ref):
     _, _, z = place()
     x, a, b, c = x_ref[...], a_ref[...], b_ref[...], c_ref[...]
     low = jnp.where(z == 0, a, jnp.where(z == 1, x, jnp.where(z == 2, b, c)))
@@ -346,7 +346,7 @@
     both = exchange("col", x, 1, 2)
     step = along_col(x, [(1, 0), (2, 3)])
     over = along_col(x, [(1, 3), (2, 0)])
-    (own,) = call(half_kernel, [step, both, over, x], [(size, half)])
+    (own,) = call(half_kernel, [both, step, over, x], [(size, half)])
     (top_sol,) = call(
         functools.partial(write_kernel, True), [own], [top_rhs.shape], [dma(())], outs_outside=(0,)
     )

time: 61.9 us -> 61 us (0.985)
    ppermute x4, starting transfers between devices: 5.01 us -> 3.1 us  [along_col(): return lax.ppermute(value, 'col', pairs + list(zip(rest, open_ends)))]
    ppermute x3, starting transfers between devices: 10.7 us -> 12.1 us  [swap(): return lax.ppermute(value, 'leaf', [(0, 1), (1, 0)])]
    ppermute x4, waiting for transfers between devices: 4.65 us -> 3.98 us  [along_col(): return lax.ppermute(value, 'col', pairs + list(zip(rest, open_ends)))]
  transfers between devices with their start and end apart: 18 -> 18, of which waited for: 12 -> 13; matrix products, arithmetic and copies ran while one was open for 0% -> 0% of each run, Pallas kernels for 16% -> 16%
where the time goes in v22:
time: 61 us; the launch traced here: 60.6 us
  waiting for transfers between devices  26.8 us (44%)
  starting transfers between devices  21.8 us (36%)
  Pallas kernels  10.9 us (18%)
  between operations  0.8 us (1%)
    ppermute x4, waiting for transfers between devices, along_row(): return lax.ppermute(value, 'row', [(r, r ^ step) for r in range(rows)])  16.7 us
    ppermute x3, starting transfers between devices, swap(): return lax.ppermute(value, 'leaf', [(0, 1), (1, 0)])  12.1 us
    pallas_call x15, Pallas kernels, call(): pl.pallas_call(kernel, out_shape=[shape(i, out) for i, out in enumerate(o...  10.9 us
    ppermute x6, waiting for transfers between devices, exchange(): return lax.ppermute(value, ('leaf', axis), pairs)  5.28 us
    ppermute x4, waiting for transfers between devices, along_col(): return lax.ppermute(value, 'col', pairs + list(zip(rest, open_ends)))  3.98 us
    ppermute x4, starting transfers between devices, along_row(): return lax.ppermute(value, 'row', [(r, r ^ step) for r in range(rows)])  3.28 us
    ppermute x4, starting transfers between devices, along_col(): return lax.ppermute(value, 'col', pairs + list(zip(rest, open_ends)))  3.1 us
    ppermute x6, starting transfers between devices, exchange(): return lax.ppermute(value, ('leaf', axis), pairs)  1.96 us
  transfers between devices with their start and end apart: 18, of which 13 were waited for; matrix products, arithmetic and copies ran while one was open for 0% of the time, Pallas kernels for 16%

profile of v22, /device:TPU:15, one launch (start us, length us, event | category | flops | bytes accessed | tf_op | source)
XLA Modules:
  0.0 60.6 jit_solution(3740676756342946570)
XLA Ops:
  0.6 1.3 %collective-permute-start.8 = (f32[512,512]{1,0:T(8,128)}, f32[512,512]{1,0:T(8,128)S(1)}, u32[]{:S(2)}, u32[]{:S(2)}) collective-permute-start(f32[512,512]{1,0:T(8,128)} %own_ref.1), channel_id=1, source_target_pairs={{4,5},{8,9},{12,13},{9,10},{13,14},{20,22},{24,26},{28,30},{30,29}} | collective-permute-start | bytes 3145736 | tf_op jit(solution)/shard_map/ppermute | solution.py:299
  1.9 2.9 %shard_map.95 = (f32[2,256,256]{2,1,0:T(8,128)}, f32[128,512]{1,0:T(8,128)S(1)}, f32[136,512]{1,0:T(8,128)S(1)}) custom-call(s32[2]{0:T(128)} %live_hbm.1, f32[2,256,256]{2,1,0:T(8,128)} %rhs_hbm.1, f32[2,256,256]{2,1,0:T(8,128)} %diag_hbm.1, f32[2,256,256]{2,1,0:T(8,128)} %off_hbm.1, s32[2,256]{1,0:T(2,128)} %tgt_hbm.1), custom_call_target="tpu_custom_call" | custom-call | bytes 1574920 | tf_op jit(solution)/shard_map/pallas_call | solution.py:251
  4.9 2.9 %collective-permute-start = (f32[136,512]{1,0:T(8,128)S(1)}, f32[136,512]{1,0:T(8,128)S(1)}, u32[]{:S(2)}, u32[]{:S(2)}) collective-permute-start(f32[136,512]{1,0:T(8,128)S(1)} %get-tuple-element.26.send_ref), channel_id=1, source_target_pairs={{0,16},{16,0},{1,17},{17,1},{2,18},{18,2},{3,19},{19,3},{4,20},{20... | collective-permute-start | bytes 835592 | tf_op jit(solution)/shard_map/ppermute | solution.py:278
  7.8 0.8 %shard_map.97 = (f32[128,512]{1,0:T(8,128)S(1)}, f32[128,512]{1,0:T(8,128)S(1)}, f32[128,512]{1,0:T(8,128)S(1)}, f32[128,512]{1,0:T(8,128)S(1)}) custom-call(f32[128,512]{1,0:T(8,128)S(1)} %get-tuple-element.27.keep_ref, f32[136,512]{1,0:T(8,128)S(1)} %get-tuple-element.26.send_ref), custom_call_target="tpu_custom_call" | custom-call | bytes 540672 | tf_op jit(solution)/shard_map/pallas_call | solution.py:251
  8.6 0.4 collective-permute-done.recv_ref
  9.0 0.8 %shard_map.98 = (f32[128,512]{1,0:T(8,128)S(1)}, f32[128,512]{1,0:T(8,128)S(1)}, f32[128,512]{1,0:T(8,128)S(1)}, f32[128,512]{1,0:T(8,128)S(1)}) custom-call(f32[136,512]{1,0:T(8,128)S(1)} %collective-permute-done.recv_ref, f32[128,512]{1,0:T(8,128)S(1)} %get-tuple-element.28.refs_0_, f32[128,512]{1,0:T(8,128)S(1)} %get-tuple-element.29.refs_1_, ...), custom_call_target="tpu_custom_call" | custom-call | bytes 1327104 | tf_op jit(solution)/shard_map/pallas_call | solution.py:251
  9.8 0.1 collective-permute-start.1
  9.8 0.3 collective-permute-start.2
  10.2 2.3 %collective-permute-start.3 = (f32[128,512]{1,0:T(8,128)S(1)}, f32[128,512]{1,0:T(8,128)S(1)}, u32[]{:S(2)}, u32[]{:S(2)}) collective-permute-start(f32[128,512]{1,0:T(8,128)S(1)} %get-tuple-element.35), channel_id=1, source_target_pairs={{0,8},{4,12},{8,0},{12,4},{1,9},{5,13},{9,1},{13,5},{2,10},{6,14},... | collective-permute-start | bytes 786440 | tf_op jit(solution)/shard_map/ppermute | solution.py:281
  12.5 5.8 %collective-permute-done.1.b_ref = f32[128,512]{1,0:T(8,128)S(1)} collective-permute-done((f32[128,512]{1,0:T(8,128)S(1)}, f32[128,512]{1,0:T(8,128)S(1)}, u32[]{:S(2)}, u32[]{:S(2)}) %collective-permute-start.1) | collective-permute-done | bytes 262176 | tf_op jit(solution)/shard_map/ppermute | solution.py:281
  18.3 3.8 %collective-permute-done.2.c_ref = f32[128,512]{1,0:T(8,128)S(1)} collective-permute-done((f32[128,512]{1,0:T(8,128)S(1)}, f32[128,512]{1,0:T(8,128)S(1)}, u32[]{:S(2)}, u32[]{:S(2)}) %collective-permute-start.2) | collective-permute-done | bytes 262176 | tf_op jit(solution)/shard_map/ppermute | solution.py:281
  22.1 2.5 %collective-permute-done.3.d_ref = f32[128,512]{1,0:T(8,128)S(1)} collective-permute-done((f32[128,512]{1,0:T(8,128)S(1)}, f32[128,512]{1,0:T(8,128)S(1)}, u32[]{:S(2)}, u32[]{:S(2)}) %collective-permute-start.3) | collective-permute-done | bytes 262176 | tf_op jit(solution)/shard_map/ppermute | solution.py:281
  24.6 0.1 shard_map.99
  24.7 0.7 %collective-permute-start.4 = (f32[64,512]{1,0:T(8,128)S(1)}, f32[64,512]{1,0:T(8,128)S(1)}, u32[]{:S(2)}, u32[]{:S(2)}) collective-permute-start(f32[64,512]{1,0:T(8,128)S(1)} %get-tuple-element.36.a_ref), channel_id=1, source_target_pairs={{0,2},{3,1},{1,0},{2,3},{4,6},{7,5},{5,4},{6,7},{8,10},{11,9},{9,8... | collective-permute-start | bytes 393224 | tf_op jit(solution)/shard_map/ppermute | solution.py:286
  25.4 0.0 collective-permute-start.6
  25.4 0.9 %collective-permute-start.5 = (f32[64,512]{1,0:T(8,128)S(1)}, f32[64,512]{1,0:T(8,128)S(1)}, u32[]{:S(2)}, u32[]{:S(2)}) collective-permute-start(f32[64,512]{1,0:T(8,128)S(1)} %get-tuple-element.37), channel_id=1, source_target_pairs={{0,1},{3,2},{1,0},{2,3},{4,5},{7,6},{5,4},{6,7},{8,9},{11,10},{9,8... | collective-permute-start | bytes 393224 | tf_op jit(solution)/shard_map/ppermute | solution.py:286
  26.3 0.3 shard_map.96
  26.6 0.0 collective-permute-done.8.sent_ref
  26.6 5.7 %collective-permute-start.9 = (f32[512,512]{1,0:T(8,128)S(1)}, f32[512,512]{1,0:T(8,128)S(1)}, u32[]{:S(2)}, u32[]{:S(2)}) collective-permute-start(f32[512,512]{1,0:T(8,128)S(1)} %collective-permute-done.8.sent_ref), channel_id=1, source_target_pairs={{0,16},{16,0},{1,17},{17,1},{2,18},{18,2},{3,19},{19,3},{4,20},{20... | collective-permute-start | bytes 3145736 | tf_op jit(solution)/shard_map/ppermute | solution.py:278
  32.3 1.0 %collective-permute-done.6.d_ref = f32[64,512]{1,0:T(8,128)S(1)} collective-permute-done((f32[64,512]{1,0:T(8,128)S(1)}, f32[64,512]{1,0:T(8,128)S(1)}, u32[]{:S(2)}, u32[]{:S(2)}) %collective-permute-start.6) | collective-permute-done | bytes 131104 | tf_op jit(solution)/shard_map/ppermute | solution.py:294
  33.4 1.1 %collective-permute-done.5.c_ref = f32[64,512]{1,0:T(8,128)S(1)} collective-permute-done((f32[64,512]{1,0:T(8,128)S(1)}, f32[64,512]{1,0:T(8,128)S(1)}, u32[]{:S(2)}, u32[]{:S(2)}) %collective-permute-start.5) | collective-permute-done | bytes 131104 | tf_op jit(solution)/shard_map/ppermute | solution.py:286
  34.5 0.3 shard_map.100.given_ref
  34.8 0.6 collective-permute-start.7
  35.3 0.1 collective-permute-start.10
  35.4 0.0 collective-permute-done.9.other_ref
  35.4 0.3 copy-done.1
  35.7 3.4 %shard_map.101 = (bf16[512,512]{1,0:T(8,128)(2,1)S(1)}, bf16[512,512]{1,0:T(8,128)(2,1)S(1)}, bf16[512,512]{1,0:T(8,128)(2,1)S(1)}, bf16[512,512]{1,0:T(8,128)(2...) custom-call(f32[512,512]{1,0:T(8,128)S(1)} %copy-done.1, ...), custom_call_target="tpu_custom_call" | custom-call | bytes 5242880 | tf_op jit(solution)/shard_map/pallas_call | solution.py:251
  39.1 0.0 collective-permute-done.7.refs_0_
  39.1 0.6 collective-permute-start.11
  39.7 0.3 collective-permute-start.12
  40.1 0.0 collective-permute-done.10.refs_0_
  40.1 4.6 %collective-permute-done.11.refs_0_ = f32[64,512]{1,0:T(8,128)S(1)} collective-permute-done((f32[64,512]{1,0:T(8,128)S(1)}, f32[64,512]{1,0:T(8,128)S(1)}, u32[]{:S(2)}, u32[]{:S(2)}) %collective-permute-start.11) | collective-permute-done | bytes 131104 | tf_op jit(solution)/shard_map/ppermute | solution.py:281
  44.7 0.1 collective-permute-start.13
  44.8 2.7 %collective-permute-done.12.refs_3_ = f32[64,512]{1,0:T(8,128)S(1)} collective-permute-done((f32[64,512]{1,0:T(8,128)S(1)}, f32[64,512]{1,0:T(8,128)S(1)}, u32[]{:S(2)}, u32[]{:S(2)}) %collective-permute-start.12) | collective-permute-done | bytes 131104 | tf_op jit(solution)/shard_map/ppermute | solution.py:294
  47.5 0.5 shard_map.105.given_ref
  48.0 0.6 %collective-permute-done.13.refs_0_ = f32[64,512]{1,0:T(8,128)S(1)} collective-permute-done((f32[64,512]{1,0:T(8,128)S(1)}, f32[64,512]{1,0:T(8,128)S(1)}, u32[]{:S(2)}, u32[]{:S(2)}) %collective-permute-start.13) | collective-permute-done | bytes 131104 | tf_op jit(solution)/shard_map/ppermute | solution.py:294
  48.6 0.3 shard_map.106.x_ref
  48.9 0.1 collective-permute-start.16
  49.0 1.5 %collective-permute-start.15 = (f32[64,512]{1,0:T(8,128)S(1)}, f32[64,512]{1,0:T(8,128)S(1)}, u32[]{:S(2)}, u32[]{:S(2)}) collective-permute-start(f32[64,512]{1,0:T(8,128)S(1)} %shard_map.106.x_ref), channel_id=1, source_target_pairs={{1,0},{2,3},{0,1},{3,2},{5,4},{6,7},{4,5},{7,6},{9,8},{10,11},{8,9... | collective-permute-start | bytes 393224 | tf_op jit(solution)/shard_map/ppermute | solution.py:286
  50.4 0.9 %collective-permute-start.14 = (f32[64,512]{1,0:T(8,128)S(1)}, f32[64,512]{1,0:T(8,128)S(1)}, u32[]{:S(2)}, u32[]{:S(2)}) collective-permute-start(f32[64,512]{1,0:T(8,128)S(1)} %shard_map.106.x_ref), channel_id=1, source_target_pairs={{1,2},{2,1},{17,18},{18,17},{0,16},{16,0},{3,19},{19,3},{5,6},{6,5... | collective-permute-start | bytes 393224 | tf_op jit(solution)/shard_map/ppermute | solution.py:294
  51.3 1.5 %collective-permute-done.16.c_ref = f32[64,512]{1,0:T(8,128)S(1)} collective-permute-done((f32[64,512]{1,0:T(8,128)S(1)}, f32[64,512]{1,0:T(8,128)S(1)}, u32[]{:S(2)}, u32[]{:S(2)}) %collective-permute-start.16) | collective-permute-done | bytes 131104 | tf_op jit(solution)/shard_map/ppermute | solution.py:286
  52.8 1.4 %collective-permute-done.15.a_ref = f32[64,512]{1,0:T(8,128)S(1)} collective-permute-done((f32[64,512]{1,0:T(8,128)S(1)}, f32[64,512]{1,0:T(8,128)S(1)}, u32[]{:S(2)}, u32[]{:S(2)}) %collective-permute-start.15) | collective-permute-done | bytes 131104 | tf_op jit(solution)/shard_map/ppermute | solution.py:286
  54.2 0.9 %collective-permute-done.14.b_ref = f32[64,512]{1,0:T(8,128)S(1)} collective-permute-done((f32[64,512]{1,0:T(8,128)S(1)}, f32[64,512]{1,0:T(8,128)S(1)}, u32[]{:S(2)}, u32[]{:S(2)}) %collective-permute-start.14) | collective-permute-done | bytes 131104 | tf_op jit(solution)/shard_map/ppermute | solution.py:294
  55.1 0.1 shard_map.107.part_ref
  55.3 3.5 %collective-permute-start.17 = (f32[512,128]{1,0:T(8,128)S(1)}, f32[512,128]{1,0:T(8,128)S(1)}, u32[]{:S(2)}, u32[]{:S(2)}) collective-permute-start(f32[512,128]{1,0:T(8,128)S(1)} %shard_map.107.part_ref), channel_id=1, source_target_pairs={{0,16},{16,0},{1,17},{17,1},{2,18},{18,2},{3,19},{19,3},{4,20},{20... | collective-permute-start | bytes 786440 | tf_op jit(solution)/shard_map/ppermute | solution.py:278
  58.8 0.7 %shard_map.108.refs_0_ = f32[512,256]{1,0:T(8,128)} custom-call(f32[512,128]{1,0:T(8,128)S(1)} %shard_map.107.part_ref), custom_call_target="tpu_custom_call" | custom-call | bytes 262144 | tf_op jit(solution)/shard_map/pallas_call | solution.py:251
  59.5 0.4 collective-permute-done.17.part_ref
  59.9 0.7 %shard_map.109 = f32[512,256]{1,0:T(8,128)} custom-call(f32[512,128]{1,0:T(8,128)S(1)} %collective-permute-done.17.part_ref, f32[512,256]{1,0:T(8,128)} %shard_map.108.refs_0_), custom_call_target="tpu_custom_call", output_to_operand_aliasing={{}: (1, {})} | custom-call | bytes 786432 | tf_op jit(solution)/shard_map/pallas_call | solution.py:251
  (9 shorter events, 0.1 us)
Async XLA Ops:
  0.6 26.0 %collective-permute-start.8 = (f32[512,512]{1,0:T(8,128)}, f32[512,512]{1,0:T(8,128)S(1)}, u32[]{:S(2)}, u32[]{:S(2)}) collective-permute-start(f32[512,512]{1,0:T(8,128)} %own_ref.1), channel_id=1, source_target_pairs={{4,5},{8,9},{12,13},{9,10},{13,14},{20,22},{24,26},{28,30},{30,29}} | collective-permute-start | bytes 3145736 | tf_op jit(solution)/shard_map/ppermute | solution.py:299
  4.9 4.1 %collective-permute-start = (f32[136,512]{1,0:T(8,128)S(1)}, f32[136,512]{1,0:T(8,128)S(1)}, u32[]{:S(2)}, u32[]{:S(2)}) collective-permute-start(f32[136,512]{1,0:T(8,128)S(1)} %get-tuple-element.26.send_ref), channel_id=1, source_target_pairs={{0,16},{16,0},{1,17},{17,1},{2,18},{18,2},{3,19},{19,3},{4,20},{20... | collective-permute-start | bytes 835592 | tf_op jit(solution)/shard_map/ppermute | solution.py:278
  9.0 17.3 %copy-start = (f32[512,512]{1,0:T(8,128)S(1)}, f32[512,512]{1,0:T(8,128)}, u32[]{:S(2)}) copy-start(f32[512,512]{1,0:T(8,128)} %diag_ref.1) | copy-start | bytes 3145732
  9.8 8.5 %collective-permute-start.1 = (f32[128,512]{1,0:T(8,128)S(1)}, f32[128,512]{1,0:T(8,128)S(1)}, u32[]{:S(2)}, u32[]{:S(2)}) collective-permute-start(f32[128,512]{1,0:T(8,128)S(1)} %get-tuple-element.33), channel_id=1, source_target_pairs={{0,12},{4,8},{8,4},{12,0},{1,13},{5,9},{9,5},{13,1},{2,14},{6,10},... | collective-permute-start | bytes 786440 | tf_op jit(solution)/shard_map/ppermute | solution.py:281
  9.8 12.3 %collective-permute-start.2 = (f32[128,512]{1,0:T(8,128)S(1)}, f32[128,512]{1,0:T(8,128)S(1)}, u32[]{:S(2)}, u32[]{:S(2)}) collective-permute-start(f32[128,512]{1,0:T(8,128)S(1)} %get-tuple-element.34), channel_id=1, source_target_pairs={{0,4},{4,0},{8,12},{12,8},{1,5},{5,1},{9,13},{13,9},{2,6},{6,2},{1... | collective-permute-start | bytes 786440 | tf_op jit(solution)/shard_map/ppermute | solution.py:281
  10.2 14.4 %collective-permute-start.3 = (f32[128,512]{1,0:T(8,128)S(1)}, f32[128,512]{1,0:T(8,128)S(1)}, u32[]{:S(2)}, u32[]{:S(2)}) collective-permute-start(f32[128,512]{1,0:T(8,128)S(1)} %get-tuple-element.35), channel_id=1, source_target_pairs={{0,8},{4,12},{8,0},{12,4},{1,9},{5,13},{9,1},{13,5},{2,10},{6,14},... | collective-permute-start | bytes 786440 | tf_op jit(solution)/shard_map/ppermute | solution.py:281
  24.6 1.7 %copy-start.2 = (f32[512,256]{1,0:T(8,128)S(1)}, f32[512,256]{1,0:T(8,128)}, u32[]{:S(2)}) copy-start(f32[512,256]{1,0:T(8,128)} %rhs_ref.1) | copy-start | bytes 1572868
  24.7 7.7 %collective-permute-start.4 = (f32[64,512]{1,0:T(8,128)S(1)}, f32[64,512]{1,0:T(8,128)S(1)}, u32[]{:S(2)}, u32[]{:S(2)}) collective-permute-start(f32[64,512]{1,0:T(8,128)S(1)} %get-tuple-element.36.a_ref), channel_id=1, source_target_pairs={{0,2},{3,1},{1,0},{2,3},{4,6},{7,5},{5,4},{6,7},{8,10},{11,9},{9,8... | collective-permute-start | bytes 393224 | tf_op jit(solution)/shard_map/ppermute | solution.py:286
  25.4 8.0 %collective-permute-start.6 = (f32[64,512]{1,0:T(8,128)S(1)}, f32[64,512]{1,0:T(8,128)S(1)}, u32[]{:S(2)}, u32[]{:S(2)}) collective-permute-start(f32[64,512]{1,0:T(8,128)S(1)} %get-tuple-element.37), channel_id=1, source_target_pairs={{1,2},{2,1},{17,18},{18,17},{0,16},{16,0},{3,19},{19,3},{5,6},{6,5... | collective-permute-start | bytes 393224 | tf_op jit(solution)/shard_map/ppermute | solution.py:294
  25.4 9.1 %collective-permute-start.5 = (f32[64,512]{1,0:T(8,128)S(1)}, f32[64,512]{1,0:T(8,128)S(1)}, u32[]{:S(2)}, u32[]{:S(2)}) collective-permute-start(f32[64,512]{1,0:T(8,128)S(1)} %get-tuple-element.37), channel_id=1, source_target_pairs={{0,1},{3,2},{1,0},{2,3},{4,5},{7,6},{5,4},{6,7},{8,9},{11,10},{9,8... | collective-permute-start | bytes 393224 | tf_op jit(solution)/shard_map/ppermute | solution.py:286
  26.6 8.8 %collective-permute-start.9 = (f32[512,512]{1,0:T(8,128)S(1)}, f32[512,512]{1,0:T(8,128)S(1)}, u32[]{:S(2)}, u32[]{:S(2)}) collective-permute-start(f32[512,512]{1,0:T(8,128)S(1)} %collective-permute-done.8.sent_ref), channel_id=1, source_target_pairs={{0,16},{16,0},{1,17},{17,1},{2,18},{18,2},{3,19},{19,3},{4,20},{20... | collective-permute-start | bytes 3145736 | tf_op jit(solution)/shard_map/ppermute | solution.py:278
  34.5 1.2 %copy-start.1 = (f32[512,512]{1,0:T(8,128)S(1)}, f32[512,512]{1,0:T(8,128)}, u32[]{:S(2)}) copy-start(f32[512,512]{1,0:T(8,128)} %own_ref.1) | copy-start | bytes 3145732
  34.8 4.4 %collective-permute-start.7 = (f32[64,512]{1,0:T(8,128)S(1)}, f32[64,512]{1,0:T(8,128)S(1)}, u32[]{:S(2)}, u32[]{:S(2)}) collective-permute-start(f32[64,512]{1,0:T(8,128)S(1)} %shard_map.100.given_ref), channel_id=1, source_target_pairs={{0,4},{4,0},{16,20},{20,16},{8,24},{24,8},{12,28},{28,12},{1,5},{5... | collective-permute-start | bytes 393224 | tf_op jit(solution)/shard_map/ppermute | solution.py:294
  35.3 4.7 %collective-permute-start.10 = (f32[64,512]{1,0:T(8,128)S(1)}, f32[64,512]{1,0:T(8,128)S(1)}, u32[]{:S(2)}, u32[]{:S(2)}) collective-permute-start(f32[64,512]{1,0:T(8,128)S(1)} %shard_map.100.given_ref), channel_id=1, source_target_pairs={{0,8},{8,0},{16,24},{24,16},{4,20},{20,4},{12,28},{28,12},{1,9},{9... | collective-permute-start | bytes 393224 | tf_op jit(solution)/shard_map/ppermute | solution.py:294
  39.1 5.6 %collective-permute-start.11 = (f32[64,512]{1,0:T(8,128)S(1)}, f32[64,512]{1,0:T(8,128)S(1)}, u32[]{:S(2)}, u32[]{:S(2)}) collective-permute-start(f32[64,512]{1,0:T(8,128)S(1)} %shard_map.102.given_ref), channel_id=1, source_target_pairs={{0,12},{4,8},{8,4},{12,0},{1,13},{5,9},{9,5},{13,1},{2,14},{6,10},... | collective-permute-start | bytes 393224 | tf_op jit(solution)/shard_map/ppermute | solution.py:281
  39.7 7.8 %collective-permute-start.12 = (f32[64,512]{1,0:T(8,128)S(1)}, f32[64,512]{1,0:T(8,128)S(1)}, u32[]{:S(2)}, u32[]{:S(2)}) collective-permute-start(f32[64,512]{1,0:T(8,128)S(1)} %shard_map.102.given_ref), channel_id=1, source_target_pairs={{4,12},{12,4},{20,28},{28,20},{0,16},{16,0},{8,24},{24,8},{5,13},{... | collective-permute-start | bytes 393224 | tf_op jit(solution)/shard_map/ppermute | solution.py:294
  44.7 3.9 %collective-permute-start.13 = (f32[64,512]{1,0:T(8,128)S(1)}, f32[64,512]{1,0:T(8,128)S(1)}, u32[]{:S(2)}, u32[]{:S(2)}) collective-permute-start(f32[64,512]{1,0:T(8,128)S(1)} %shard_map.104.given_ref), channel_id=1, source_target_pairs={{8,12},{12,8},{24,28},{28,24},{0,16},{16,0},{4,20},{20,4},{9,13},{... | collective-permute-start | bytes 393224 | tf_op jit(solution)/shard_map/ppermute | solution.py:294
  48.9 3.9 %collective-permute-start.16 = (f32[64,512]{1,0:T(8,128)S(1)}, f32[64,512]{1,0:T(8,128)S(1)}, u32[]{:S(2)}, u32[]{:S(2)}) collective-permute-start(f32[64,512]{1,0:T(8,128)S(1)} %shard_map.106.x_ref), channel_id=1, source_target_pairs={{1,3},{2,0},{0,1},{3,2},{5,7},{6,4},{4,5},{7,6},{9,11},{10,8},{8,9... | collective-permute-start | bytes 393224 | tf_op jit(solution)/shard_map/ppermute | solution.py:286
  49.0 5.2 %collective-permute-start.15 = (f32[64,512]{1,0:T(8,128)S(1)}, f32[64,512]{1,0:T(8,128)S(1)}, u32[]{:S(2)}, u32[]{:S(2)}) collective-permute-start(f32[64,512]{1,0:T(8,128)S(1)} %shard_map.106.x_ref), channel_id=1, source_target_pairs={{1,0},{2,3},{0,1},{3,2},{5,4},{6,7},{4,5},{7,6},{9,8},{10,11},{8,9... | collective-permute-start | bytes 393224 | tf_op jit(solution)/shard_map/ppermute | solution.py:286
  50.4 4.7 %collective-permute-start.14 = (f32[64,512]{1,0:T(8,128)S(1)}, f32[64,512]{1,0:T(8,128)S(1)}, u32[]{:S(2)}, u32[]{:S(2)}) collective-permute-start(f32[64,512]{1,0:T(8,128)S(1)} %shard_map.106.x_ref), channel_id=1, source_target_pairs={{1,2},{2,1},{17,18},{18,17},{0,16},{16,0},{3,19},{19,3},{5,6},{6,5... | collective-permute-start | bytes 393224 | tf_op jit(solution)/shard_map/ppermute | solution.py:294
  55.3 4.6 %collective-permute-start.17 = (f32[512,128]{1,0:T(8,128)S(1)}, f32[512,128]{1,0:T(8,128)S(1)}, u32[]{:S(2)}, u32[]{:S(2)}) collective-permute-start(f32[512,128]{1,0:T(8,128)S(1)} %shard_map.107.part_ref), channel_id=1, source_target_pairs={{0,16},{16,0},{1,17},{17,1},{2,18},{18,2},{3,19},{19,3},{4,20},{20... | collective-permute-start | bytes 786440 | tf_op jit(solution)/shard_map/ppermute | solution.py:278

commit v23 on v22

--- a/solution.py
+++ b/solution.py
@@ -320,8 +320,8 @@
     first, second = call(pieces_kernel, [sums[0]] + got, [shape] * 2, [(half, size)])
     q = [
         along_col(second, [(0, 2), (3, 1)]),
+        exchange("col", first, 1, 2),
         along_col(first, [(0, 1), (3, 2)]),
-        exchange("col", first, 1, 2),
     ]
 
     factor = call(factor_kernel, [top_factor, sent, swap(sent)] + diag, [block] * 6)

time: 61 us -> 61 us (level)
  starting transfers between devices: 21.8 us -> 19.4 us
  waiting for transfers between devices: 26.8 us -> 29.2 us
    ppermute x3, starting transfers between devices: 12.1 us -> 8.22 us  [swap(): return lax.ppermute(value, 'leaf', [(0, 1), (1, 0)])]
    ppermute x4, waiting for transfers between devices: 3.98 us -> 7.47 us  [along_col(): return lax.ppermute(value, 'col', pairs + list(zip(rest, open_ends)))]
    ppermute x6, starting transfers between devices: 1.96 us -> 4.27 us  [exchange(): return lax.ppermute(value, ('leaf', axis), pairs)]
    ppermute x6, waiting for transfers between devices: 5.28 us -> 4.2 us  [exchange(): return lax.ppermute(value, ('leaf', axis), pairs)]
    ppermute x4, starting transfers between devices: 3.1 us -> 2.34 us  [along_col(): return lax.ppermute(value, 'col', pairs + list(zip(rest, open_ends)))]
where the time goes in v23:
time: 61 us; the launch traced here: 60.6 us
  waiting for transfers between devices  29.2 us (48%)
  starting transfers between devices  19.4 us (32%)
  Pallas kernels  10.9 us (18%)
  between operations  0.8 us (1%)
    ppermute x4, waiting for transfers between devices, along_row(): return lax.ppermute(value, 'row', [(r, r ^ step) for r in range(rows)])  16.7 us
    pallas_call x15, Pallas kernels, call(): pl.pallas_call(kernel, out_shape=[shape(i, out) for i, out in enumerate(o...  10.9 us
    ppermute x3, starting transfers between devices, swap(): return lax.ppermute(value, 'leaf', [(0, 1), (1, 0)])  8.22 us
    ppermute x4, waiting for transfers between devices, along_col(): return lax.ppermute(value, 'col', pairs + list(zip(rest, open_ends)))  7.47 us
    ppermute x6, starting transfers between devices, exchange(): return lax.ppermute(value, ('leaf', axis), pairs)  4.27 us
    ppermute x6, waiting for transfers between devices, exchange(): return lax.ppermute(value, ('leaf', axis), pairs)  4.2 us
    ppermute x4, starting transfers between devices, along_row(): return lax.ppermute(value, 'row', [(r, r ^ step) for r in range(rows)])  3.28 us
    ppermute x4, starting transfers between devices, along_col(): return lax.ppermute(value, 'col', pairs + list(zip(rest, open_ends)))  2.34 us
  transfers between devices with their start and end apart: 18, of which 13 were waited for; matrix products, arithmetic and copies ran while one was open for 0% of the time, Pallas kernels for 16%

profile of v23, /device:TPU:15, one launch (start us, length us, event | category | flops | bytes accessed | tf_op | source)
XLA Modules:
  0.0 60.6 jit_solution(11306193801273727139)
XLA Ops:
  0.6 1.3 %collective-permute-start.8 = (f32[512,512]{1,0:T(8,128)}, f32[512,512]{1,0:T(8,128)S(1)}, u32[]{:S(2)}, u32[]{:S(2)}) collective-permute-start(f32[512,512]{1,0:T(8,128)} %own_ref.1), channel_id=1, source_target_pairs={{4,5},{8,9},{12,13},{9,10},{13,14},{20,22},{24,26},{28,30},{30,29}} | collective-permute-start | bytes 3145736 | tf_op jit(solution)/shard_map/ppermute | solution.py:299
  1.9 2.9 %shard_map.95 = (f32[2,256,256]{2,1,0:T(8,128)}, f32[128,512]{1,0:T(8,128)S(1)}, f32[136,512]{1,0:T(8,128)S(1)}) custom-call(s32[2]{0:T(128)} %live_hbm.1, f32[2,256,256]{2,1,0:T(8,128)} %rhs_hbm.1, f32[2,256,256]{2,1,0:T(8,128)} %diag_hbm.1, f32[2,256,256]{2,1,0:T(8,128)} %off_hbm.1, s32[2,256]{1,0:T(2,128)} %tgt_hbm.1), custom_call_target="tpu_custom_call" | custom-call | bytes 1574920 | tf_op jit(solution)/shard_map/pallas_call | solution.py:251
  4.9 2.9 %collective-permute-start = (f32[136,512]{1,0:T(8,128)S(1)}, f32[136,512]{1,0:T(8,128)S(1)}, u32[]{:S(2)}, u32[]{:S(2)}) collective-permute-start(f32[136,512]{1,0:T(8,128)S(1)} %get-tuple-element.26.send_ref), channel_id=1, source_target_pairs={{0,16},{16,0},{1,17},{17,1},{2,18},{18,2},{3,19},{19,3},{4,20},{20... | collective-permute-start | bytes 835592 | tf_op jit(solution)/shard_map/ppermute | solution.py:278
  7.8 0.8 %shard_map.97 = (f32[128,512]{1,0:T(8,128)S(1)}, f32[128,512]{1,0:T(8,128)S(1)}, f32[128,512]{1,0:T(8,128)S(1)}, f32[128,512]{1,0:T(8,128)S(1)}) custom-call(f32[128,512]{1,0:T(8,128)S(1)} %get-tuple-element.27.keep_ref, f32[136,512]{1,0:T(8,128)S(1)} %get-tuple-element.26.send_ref), custom_call_target="tpu_custom_call" | custom-call | bytes 540672 | tf_op jit(solution)/shard_map/pallas_call | solution.py:251
  8.6 0.4 collective-permute-done.recv_ref
  9.0 0.8 %shard_map.98 = (f32[128,512]{1,0:T(8,128)S(1)}, f32[128,512]{1,0:T(8,128)S(1)}, f32[128,512]{1,0:T(8,128)S(1)}, f32[128,512]{1,0:T(8,128)S(1)}) custom-call(f32[136,512]{1,0:T(8,128)S(1)} %collective-permute-done.recv_ref, f32[128,512]{1,0:T(8,128)S(1)} %get-tuple-element.28.refs_0_, f32[128,512]{1,0:T(8,128)S(1)} %get-tuple-element.29.refs_1_, ...), custom_call_target="tpu_custom_call" | custom-call | bytes 1327104 | tf_op jit(solution)/shard_map/pallas_call | solution.py:251
  9.8 0.1 collective-permute-start.1
  9.8 0.3 collective-permute-start.2
  10.2 2.3 %collective-permute-start.3 = (f32[128,512]{1,0:T(8,128)S(1)}, f32[128,512]{1,0:T(8,128)S(1)}, u32[]{:S(2)}, u32[]{:S(2)}) collective-permute-start(f32[128,512]{1,0:T(8,128)S(1)} %get-tuple-element.35), channel_id=1, source_target_pairs={{0,8},{4,12},{8,0},{12,4},{1,9},{5,13},{9,1},{13,5},{2,10},{6,14},... | collective-permute-start | bytes 786440 | tf_op jit(solution)/shard_map/ppermute | solution.py:281
  12.5 5.8 %collective-permute-done.1.b_ref = f32[128,512]{1,0:T(8,128)S(1)} collective-permute-done((f32[128,512]{1,0:T(8,128)S(1)}, f32[128,512]{1,0:T(8,128)S(1)}, u32[]{:S(2)}, u32[]{:S(2)}) %collective-permute-start.1) | collective-permute-done | bytes 262176 | tf_op jit(solution)/shard_map/ppermute | solution.py:281
  18.3 3.8 %collective-permute-done.2.c_ref = f32[128,512]{1,0:T(8,128)S(1)} collective-permute-done((f32[128,512]{1,0:T(8,128)S(1)}, f32[128,512]{1,0:T(8,128)S(1)}, u32[]{:S(2)}, u32[]{:S(2)}) %collective-permute-start.2) | collective-permute-done | bytes 262176 | tf_op jit(solution)/shard_map/ppermute | solution.py:281
  22.1 2.5 %collective-permute-done.3.d_ref = f32[128,512]{1,0:T(8,128)S(1)} collective-permute-done((f32[128,512]{1,0:T(8,128)S(1)}, f32[128,512]{1,0:T(8,128)S(1)}, u32[]{:S(2)}, u32[]{:S(2)}) %collective-permute-start.3) | collective-permute-done | bytes 262176 | tf_op jit(solution)/shard_map/ppermute | solution.py:281
  24.6 0.1 shard_map.99
  24.7 0.7 %collective-permute-start.4 = (f32[64,512]{1,0:T(8,128)S(1)}, f32[64,512]{1,0:T(8,128)S(1)}, u32[]{:S(2)}, u32[]{:S(2)}) collective-permute-start(f32[64,512]{1,0:T(8,128)S(1)} %get-tuple-element.36.a_ref), channel_id=1, source_target_pairs={{0,2},{3,1},{1,0},{2,3},{4,6},{7,5},{5,4},{6,7},{8,10},{11,9},{9,8... | collective-permute-start | bytes 393224 | tf_op jit(solution)/shard_map/ppermute | solution.py:286
  25.4 0.1 collective-permute-start.6
  25.5 1.9 %collective-permute-start.5 = (f32[64,512]{1,0:T(8,128)S(1)}, f32[64,512]{1,0:T(8,128)S(1)}, u32[]{:S(2)}, u32[]{:S(2)}) collective-permute-start(f32[64,512]{1,0:T(8,128)S(1)} %get-tuple-element.37), channel_id=1, source_target_pairs={{1,2},{2,1},{17,18},{18,17},{0,16},{16,0},{3,19},{19,3},{5,6},{6,5... | collective-permute-start | bytes 393224 | tf_op jit(solution)/shard_map/ppermute | solution.py:294
  27.4 0.3 shard_map.96
  27.7 0.0 collective-permute-done.8.sent_ref
  27.7 1.7 %collective-permute-start.9 = (f32[512,512]{1,0:T(8,128)S(1)}, f32[512,512]{1,0:T(8,128)S(1)}, u32[]{:S(2)}, u32[]{:S(2)}) collective-permute-start(f32[512,512]{1,0:T(8,128)S(1)} %collective-permute-done.8.sent_ref), channel_id=1, source_target_pairs={{0,16},{16,0},{1,17},{17,1},{2,18},{18,2},{3,19},{19,3},{4,20},{20... | collective-permute-start | bytes 3145736 | tf_op jit(solution)/shard_map/ppermute | solution.py:278
  29.4 0.8 %collective-permute-done.4.b_ref = f32[64,512]{1,0:T(8,128)S(1)} collective-permute-done((f32[64,512]{1,0:T(8,128)S(1)}, f32[64,512]{1,0:T(8,128)S(1)}, u32[]{:S(2)}, u32[]{:S(2)}) %collective-permute-start.4) | collective-permute-done | bytes 131104 | tf_op jit(solution)/shard_map/ppermute | solution.py:286
  30.2 4.3 %collective-permute-done.6.d_ref = f32[64,512]{1,0:T(8,128)S(1)} collective-permute-done((f32[64,512]{1,0:T(8,128)S(1)}, f32[64,512]{1,0:T(8,128)S(1)}, u32[]{:S(2)}, u32[]{:S(2)}) %collective-permute-start.6) | collective-permute-done | bytes 131104 | tf_op jit(solution)/shard_map/ppermute | solution.py:286
  34.5 0.0 collective-permute-done.5.c_ref
  34.5 0.3 shard_map.100.given_ref
  34.8 0.6 collective-permute-start.7
  35.4 0.1 collective-permute-start.10
  35.4 0.0 collective-permute-done.9.other_ref
  35.4 0.3 copy-done.1
  35.7 3.4 %shard_map.101 = (bf16[512,512]{1,0:T(8,128)(2,1)S(1)}, bf16[512,512]{1,0:T(8,128)(2,1)S(1)}, bf16[512,512]{1,0:T(8,128)(2,1)S(1)}, bf16[512,512]{1,0:T(8,128)(2...) custom-call(f32[512,512]{1,0:T(8,128)S(1)} %copy-done.1, ...), custom_call_target="tpu_custom_call" | custom-call | bytes 5242880 | tf_op jit(solution)/shard_map/pallas_call | solution.py:251
  39.2 0.6 collective-permute-start.11
  39.7 0.4 collective-permute-start.12
  40.1 0.0 collective-permute-done.10.refs_0_
  40.1 4.6 %collective-permute-done.11.refs_0_ = f32[64,512]{1,0:T(8,128)S(1)} collective-permute-done((f32[64,512]{1,0:T(8,128)S(1)}, f32[64,512]{1,0:T(8,128)S(1)}, u32[]{:S(2)}, u32[]{:S(2)}) %collective-permute-start.11) | collective-permute-done | bytes 131104 | tf_op jit(solution)/shard_map/ppermute | solution.py:281
  44.7 0.1 collective-permute-start.13
  44.8 2.7 %collective-permute-done.12.refs_3_ = f32[64,512]{1,0:T(8,128)S(1)} collective-permute-done((f32[64,512]{1,0:T(8,128)S(1)}, f32[64,512]{1,0:T(8,128)S(1)}, u32[]{:S(2)}, u32[]{:S(2)}) %collective-permute-start.12) | collective-permute-done | bytes 131104 | tf_op jit(solution)/shard_map/ppermute | solution.py:294
  47.5 0.5 shard_map.105.given_ref
  48.0 0.7 %collective-permute-done.13.refs_0_ = f32[64,512]{1,0:T(8,128)S(1)} collective-permute-done((f32[64,512]{1,0:T(8,128)S(1)}, f32[64,512]{1,0:T(8,128)S(1)}, u32[]{:S(2)}, u32[]{:S(2)}) %collective-permute-start.13) | collective-permute-done | bytes 131104 | tf_op jit(solution)/shard_map/ppermute | solution.py:294
  48.6 0.3 shard_map.106.x_ref
  48.9 0.1 collective-permute-start.16
  49.0 1.5 %collective-permute-start.15 = (f32[64,512]{1,0:T(8,128)S(1)}, f32[64,512]{1,0:T(8,128)S(1)}, u32[]{:S(2)}, u32[]{:S(2)}) collective-permute-start(f32[64,512]{1,0:T(8,128)S(1)} %shard_map.106.x_ref), channel_id=1, source_target_pairs={{1,0},{2,3},{0,1},{3,2},{5,4},{6,7},{4,5},{7,6},{9,8},{10,11},{8,9... | collective-permute-start | bytes 393224 | tf_op jit(solution)/shard_map/ppermute | solution.py:286
  50.4 1.3 %collective-permute-start.14 = (f32[64,512]{1,0:T(8,128)S(1)}, f32[64,512]{1,0:T(8,128)S(1)}, u32[]{:S(2)}, u32[]{:S(2)}) collective-permute-start(f32[64,512]{1,0:T(8,128)S(1)} %shard_map.106.x_ref), channel_id=1, source_target_pairs={{1,2},{2,1},{17,18},{18,17},{0,16},{16,0},{3,19},{19,3},{5,6},{6,5... | collective-permute-start | bytes 393224 | tf_op jit(solution)/shard_map/ppermute | solution.py:294
  51.8 1.0 %collective-permute-done.16.c_ref = f32[64,512]{1,0:T(8,128)S(1)} collective-permute-done((f32[64,512]{1,0:T(8,128)S(1)}, f32[64,512]{1,0:T(8,128)S(1)}, u32[]{:S(2)}, u32[]{:S(2)}) %collective-permute-start.16) | collective-permute-done | bytes 131104 | tf_op jit(solution)/shard_map/ppermute | solution.py:286
  52.8 1.4 %collective-permute-done.15.a_ref = f32[64,512]{1,0:T(8,128)S(1)} collective-permute-done((f32[64,512]{1,0:T(8,128)S(1)}, f32[64,512]{1,0:T(8,128)S(1)}, u32[]{:S(2)}, u32[]{:S(2)}) %collective-permute-start.15) | collective-permute-done | bytes 131104 | tf_op jit(solution)/shard_map/ppermute | solution.py:286
  54.2 0.9 %collective-permute-done.14.b_ref = f32[64,512]{1,0:T(8,128)S(1)} collective-permute-done((f32[64,512]{1,0:T(8,128)S(1)}, f32[64,512]{1,0:T(8,128)S(1)}, u32[]{:S(2)}, u32[]{:S(2)}) %collective-permute-start.14) | collective-permute-done | bytes 131104 | tf_op jit(solution)/shard_map/ppermute | solution.py:294
  55.1 0.1 shard_map.107.part_ref
  55.2 3.5 %collective-permute-start.17 = (f32[512,128]{1,0:T(8,128)S(1)}, f32[512,128]{1,0:T(8,128)S(1)}, u32[]{:S(2)}, u32[]{:S(2)}) collective-permute-start(f32[512,128]{1,0:T(8,128)S(1)} %shard_map.107.part_ref), channel_id=1, source_target_pairs={{0,16},{16,0},{1,17},{17,1},{2,18},{18,2},{3,19},{19,3},{4,20},{20... | collective-permute-start | bytes 786440 | tf_op jit(solution)/shard_map/ppermute | solution.py:278
  58.8 0.7 %shard_map.108.refs_0_ = f32[512,256]{1,0:T(8,128)} custom-call(f32[512,128]{1,0:T(8,128)S(1)} %shard_map.107.part_ref), custom_call_target="tpu_custom_call" | custom-call | bytes 262144 | tf_op jit(solution)/shard_map/pallas_call | solution.py:251
  59.5 0.4 collective-permute-done.17.part_ref
  59.9 0.7 %shard_map.109 = f32[512,256]{1,0:T(8,128)} custom-call(f32[512,128]{1,0:T(8,128)S(1)} %collective-permute-done.17.part_ref, f32[512,256]{1,0:T(8,128)} %shard_map.108.refs_0_), custom_call_target="tpu_custom_call", output_to_operand_aliasing={{}: (1, {})} | custom-call | bytes 786432 | tf_op jit(solution)/shard_map/pallas_call | solution.py:251
  (9 shorter events, 0.1 us)
Async XLA Ops:
  0.6 27.1 %collective-permute-start.8 = (f32[512,512]{1,0:T(8,128)}, f32[512,512]{1,0:T(8,128)S(1)}, u32[]{:S(2)}, u32[]{:S(2)}) collective-permute-start(f32[512,512]{1,0:T(8,128)} %own_ref.1), channel_id=1, source_target_pairs={{4,5},{8,9},{12,13},{9,10},{13,14},{20,22},{24,26},{28,30},{30,29}} | collective-permute-start | bytes 3145736 | tf_op jit(solution)/shard_map/ppermute | solution.py:299
  4.9 4.1 %collective-permute-start = (f32[136,512]{1,0:T(8,128)S(1)}, f32[136,512]{1,0:T(8,128)S(1)}, u32[]{:S(2)}, u32[]{:S(2)}) collective-permute-start(f32[136,512]{1,0:T(8,128)S(1)} %get-tuple-element.26.send_ref), channel_id=1, source_target_pairs={{0,16},{16,0},{1,17},{17,1},{2,18},{18,2},{3,19},{19,3},{4,20},{20... | collective-permute-start | bytes 835592 | tf_op jit(solution)/shard_map/ppermute | solution.py:278
  9.0 18.4 %copy-start = (f32[512,512]{1,0:T(8,128)S(1)}, f32[512,512]{1,0:T(8,128)}, u32[]{:S(2)}) copy-start(f32[512,512]{1,0:T(8,128)} %diag_ref.1) | copy-start | bytes 3145732
  9.8 8.5 %collective-permute-start.1 = (f32[128,512]{1,0:T(8,128)S(1)}, f32[128,512]{1,0:T(8,128)S(1)}, u32[]{:S(2)}, u32[]{:S(2)}) collective-permute-start(f32[128,512]{1,0:T(8,128)S(1)} %get-tuple-element.33), channel_id=1, source_target_pairs={{0,12},{4,8},{8,4},{12,0},{1,13},{5,9},{9,5},{13,1},{2,14},{6,10},... | collective-permute-start | bytes 786440 | tf_op jit(solution)/shard_map/ppermute | solution.py:281
  9.8 12.3 %collective-permute-start.2 = (f32[128,512]{1,0:T(8,128)S(1)}, f32[128,512]{1,0:T(8,128)S(1)}, u32[]{:S(2)}, u32[]{:S(2)}) collective-permute-start(f32[128,512]{1,0:T(8,128)S(1)} %get-tuple-element.34), channel_id=1, source_target_pairs={{0,4},{4,0},{8,12},{12,8},{1,5},{5,1},{9,13},{13,9},{2,6},{6,2},{1... | collective-permute-start | bytes 786440 | tf_op jit(solution)/shard_map/ppermute | solution.py:281
  10.2 14.4 %collective-permute-start.3 = (f32[128,512]{1,0:T(8,128)S(1)}, f32[128,512]{1,0:T(8,128)S(1)}, u32[]{:S(2)}, u32[]{:S(2)}) collective-permute-start(f32[128,512]{1,0:T(8,128)S(1)} %get-tuple-element.35), channel_id=1, source_target_pairs={{0,8},{4,12},{8,0},{12,4},{1,9},{5,13},{9,1},{13,5},{2,10},{6,14},... | collective-permute-start | bytes 786440 | tf_op jit(solution)/shard_map/ppermute | solution.py:281
  24.6 2.8 %copy-start.2 = (f32[512,256]{1,0:T(8,128)S(1)}, f32[512,256]{1,0:T(8,128)}, u32[]{:S(2)}) copy-start(f32[512,256]{1,0:T(8,128)} %rhs_ref.1) | copy-start | bytes 1572868
  24.7 5.5 %collective-permute-start.4 = (f32[64,512]{1,0:T(8,128)S(1)}, f32[64,512]{1,0:T(8,128)S(1)}, u32[]{:S(2)}, u32[]{:S(2)}) collective-permute-start(f32[64,512]{1,0:T(8,128)S(1)} %get-tuple-element.36.a_ref), channel_id=1, source_target_pairs={{0,2},{3,1},{1,0},{2,3},{4,6},{7,5},{5,4},{6,7},{8,10},{11,9},{9,8... | collective-permute-start | bytes 393224 | tf_op jit(solution)/shard_map/ppermute | solution.py:286
  25.4 9.1 %collective-permute-start.6 = (f32[64,512]{1,0:T(8,128)S(1)}, f32[64,512]{1,0:T(8,128)S(1)}, u32[]{:S(2)}, u32[]{:S(2)}) collective-permute-start(f32[64,512]{1,0:T(8,128)S(1)} %get-tuple-element.37), channel_id=1, source_target_pairs={{0,1},{3,2},{1,0},{2,3},{4,5},{7,6},{5,4},{6,7},{8,9},{11,10},{9,8... | collective-permute-start | bytes 393224 | tf_op jit(solution)/shard_map/ppermute | solution.py:286
  25.5 9.0 %collective-permute-start.5 = (f32[64,512]{1,0:T(8,128)S(1)}, f32[64,512]{1,0:T(8,128)S(1)}, u32[]{:S(2)}, u32[]{:S(2)}) collective-permute-start(f32[64,512]{1,0:T(8,128)S(1)} %get-tuple-element.37), channel_id=1, source_target_pairs={{1,2},{2,1},{17,18},{18,17},{0,16},{16,0},{3,19},{19,3},{5,6},{6,5... | collective-permute-start | bytes 393224 | tf_op jit(solution)/shard_map/ppermute | solution.py:294
  27.7 7.7 %collective-permute-start.9 = (f32[512,512]{1,0:T(8,128)S(1)}, f32[512,512]{1,0:T(8,128)S(1)}, u32[]{:S(2)}, u32[]{:S(2)}) collective-permute-start(f32[512,512]{1,0:T(8,128)S(1)} %collective-permute-done.8.sent_ref), channel_id=1, source_target_pairs={{0,16},{16,0},{1,17},{17,1},{2,18},{18,2},{3,19},{19,3},{4,20},{20... | collective-permute-start | bytes 3145736 | tf_op jit(solution)/shard_map/ppermute | solution.py:278
  34.5 1.2 %copy-start.1 = (f32[512,512]{1,0:T(8,128)S(1)}, f32[512,512]{1,0:T(8,128)}, u32[]{:S(2)}) copy-start(f32[512,512]{1,0:T(8,128)} %own_ref.1) | copy-start | bytes 3145732
  34.8 4.4 %collective-permute-start.7 = (f32[64,512]{1,0:T(8,128)S(1)}, f32[64,512]{1,0:T(8,128)S(1)}, u32[]{:S(2)}, u32[]{:S(2)}) collective-permute-start(f32[64,512]{1,0:T(8,128)S(1)} %shard_map.100.given_ref), channel_id=1, source_target_pairs={{0,4},{4,0},{16,20},{20,16},{8,24},{24,8},{12,28},{28,12},{1,5},{5... | collective-permute-start | bytes 393224 | tf_op jit(solution)/shard_map/ppermute | solution.py:294
  35.4 4.7 %collective-permute-start.10 = (f32[64,512]{1,0:T(8,128)S(1)}, f32[64,512]{1,0:T(8,128)S(1)}, u32[]{:S(2)}, u32[]{:S(2)}) collective-permute-start(f32[64,512]{1,0:T(8,128)S(1)} %shard_map.100.given_ref), channel_id=1, source_target_pairs={{0,8},{8,0},{16,24},{24,16},{4,20},{20,4},{12,28},{28,12},{1,9},{9... | collective-permute-start | bytes 393224 | tf_op jit(solution)/shard_map/ppermute | solution.py:294
  39.2 5.6 %collective-permute-start.11 = (f32[64,512]{1,0:T(8,128)S(1)}, f32[64,512]{1,0:T(8,128)S(1)}, u32[]{:S(2)}, u32[]{:S(2)}) collective-permute-start(f32[64,512]{1,0:T(8,128)S(1)} %shard_map.102.given_ref), channel_id=1, source_target_pairs={{0,12},{4,8},{8,4},{12,0},{1,13},{5,9},{9,5},{13,1},{2,14},{6,10},... | collective-permute-start | bytes 393224 | tf_op jit(solution)/shard_map/ppermute | solution.py:281
  39.7 7.8 %collective-permute-start.12 = (f32[64,512]{1,0:T(8,128)S(1)}, f32[64,512]{1,0:T(8,128)S(1)}, u32[]{:S(2)}, u32[]{:S(2)}) collective-permute-start(f32[64,512]{1,0:T(8,128)S(1)} %shard_map.102.given_ref), channel_id=1, source_target_pairs={{4,12},{12,4},{20,28},{28,20},{0,16},{16,0},{8,24},{24,8},{5,13},{... | collective-permute-start | bytes 393224 | tf_op jit(solution)/shard_map/ppermute | solution.py:294
  44.7 3.9 %collective-permute-start.13 = (f32[64,512]{1,0:T(8,128)S(1)}, f32[64,512]{1,0:T(8,128)S(1)}, u32[]{:S(2)}, u32[]{:S(2)}) collective-permute-start(f32[64,512]{1,0:T(8,128)S(1)} %shard_map.104.given_ref), channel_id=1, source_target_pairs={{8,12},{12,8},{24,28},{28,24},{0,16},{16,0},{4,20},{20,4},{9,13},{... | collective-permute-start | bytes 393224 | tf_op jit(solution)/shard_map/ppermute | solution.py:294
  48.9 3.9 %collective-permute-start.16 = (f32[64,512]{1,0:T(8,128)S(1)}, f32[64,512]{1,0:T(8,128)S(1)}, u32[]{:S(2)}, u32[]{:S(2)}) collective-permute-start(f32[64,512]{1,0:T(8,128)S(1)} %shard_map.106.x_ref), channel_id=1, source_target_pairs={{1,3},{2,0},{0,1},{3,2},{5,7},{6,4},{4,5},{7,6},{9,11},{10,8},{8,9... | collective-permute-start | bytes 393224 | tf_op jit(solution)/shard_map/ppermute | solution.py:286
  49.0 5.2 %collective-permute-start.15 = (f32[64,512]{1,0:T(8,128)S(1)}, f32[64,512]{1,0:T(8,128)S(1)}, u32[]{:S(2)}, u32[]{:S(2)}) collective-permute-start(f32[64,512]{1,0:T(8,128)S(1)} %shard_map.106.x_ref), channel_id=1, source_target_pairs={{1,0},{2,3},{0,1},{3,2},{5,4},{6,7},{4,5},{7,6},{9,8},{10,11},{8,9... | collective-permute-start | bytes 393224 | tf_op jit(solution)/shard_map/ppermute | solution.py:286
  50.4 4.6 %collective-permute-start.14 = (f32[64,512]{1,0:T(8,128)S(1)}, f32[64,512]{1,0:T(8,128)S(1)}, u32[]{:S(2)}, u32[]{:S(2)}) collective-permute-start(f32[64,512]{1,0:T(8,128)S(1)} %shard_map.106.x_ref), channel_id=1, source_target_pairs={{1,2},{2,1},{17,18},{18,17},{0,16},{16,0},{3,19},{19,3},{5,6},{6,5... | collective-permute-start | bytes 393224 | tf_op jit(solution)/shard_map/ppermute | solution.py:294
  55.2 4.7 %collective-permute-start.17 = (f32[512,128]{1,0:T(8,128)S(1)}, f32[512,128]{1,0:T(8,128)S(1)}, u32[]{:S(2)}, u32[]{:S(2)}) collective-permute-start(f32[512,128]{1,0:T(8,128)S(1)} %shard_map.107.part_ref), channel_id=1, source_target_pairs={{0,16},{16,0},{1,17},{17,1},{2,18},{18,2},{3,19},{19,3},{4,20},{20... | collective-permute-start | bytes 786440 | tf_op jit(solution)/shard_map/ppermute | solution.py:278

commit v24 on v23

--- a/solution.py
+++ b/solution.py
@@ -123,11 +123,11 @@
         pltpu.make_async_copy(live_hbm, live_ref, sems.at[4, 0]),
         pltpu.make_async_copy(tgt_hbm, tgt_ref, sems.at[4, 1]),
     ]
+    for copy in small:
+        copy.start()
     for s in range(children):
         for copy in copies[s]:
             copy.start()
-    for copy in small:
-        copy.start()
     for s in range(children):
         copies[s][0].wait()
         copies[s][1].wait()

time: 61 us -> 61 us (level)
  no operation moved by 1% of the time
where the time goes in v24:
time: 61 us; the launch traced here: 60.6 us
  waiting for transfers between devices  29.2 us (48%)
  starting transfers between devices  19.4 us (32%)
  Pallas kernels  10.9 us (18%)
  between operations  0.8 us (1%)
    ppermute x4, waiting for transfers between devices, along_row(): return lax.ppermute(value, 'row', [(r, r ^ step) for r in range(rows)])  16.7 us
    pallas_call x15, Pallas kernels, call(): pl.pallas_call(kernel, out_shape=[shape(i, out) for i, out in enumerate(o...  10.9 us
    ppermute x3, starting transfers between devices, swap(): return lax.ppermute(value, 'leaf', [(0, 1), (1, 0)])  8.21 us
    ppermute x4, waiting for transfers between devices, along_col(): return lax.ppermute(value, 'col', pairs + list(zip(rest, open_ends)))  7.47 us
    ppermute x6, starting transfers between devices, exchange(): return lax.ppermute(value, ('leaf', axis), pairs)  4.26 us
    ppermute x6, waiting for transfers between devices, exchange(): return lax.ppermute(value, ('leaf', axis), pairs)  4.2 us
    ppermute x4, starting transfers between devices, along_row(): return lax.ppermute(value, 'row', [(r, r ^ step) for r in range(rows)])  3.28 us
    ppermute x4, starting transfers between devices, along_col(): return lax.ppermute(value, 'col', pairs + list(zip(rest, open_ends)))  2.34 us
  transfers between devices with their start and end apart: 18, of which 13 were waited for; matrix products, arithmetic and copies ran while one was open for 0% of the time, Pallas kernels for 16%

profile of v24, /device:TPU:15, one launch (start us, length us, event | category | flops | bytes accessed | tf_op | source)
XLA Modules:
  0.0 60.6 jit_solution(265096811810017084)
XLA Ops:
  0.6 1.3 %collective-permute-start.8 = (f32[512,512]{1,0:T(8,128)}, f32[512,512]{1,0:T(8,128)S(1)}, u32[]{:S(2)}, u32[]{:S(2)}) collective-permute-start(f32[512,512]{1,0:T(8,128)} %own_ref.1), channel_id=1, source_target_pairs={{4,5},{8,9},{12,13},{9,10},{13,14},{20,22},{24,26},{28,30},{30,29}} | collective-permute-start | bytes 3145736 | tf_op jit(solution)/shard_map/ppermute | solution.py:299
  1.9 2.9 %shard_map.95 = (f32[2,256,256]{2,1,0:T(8,128)}, f32[128,512]{1,0:T(8,128)S(1)}, f32[136,512]{1,0:T(8,128)S(1)}) custom-call(s32[2]{0:T(128)} %live_hbm.1, f32[2,256,256]{2,1,0:T(8,128)} %rhs_hbm.1, f32[2,256,256]{2,1,0:T(8,128)} %diag_hbm.1, f32[2,256,256]{2,1,0:T(8,128)} %off_hbm.1, s32[2,256]{1,0:T(2,128)} %tgt_hbm.1), custom_call_target="tpu_custom_call" | custom-call | bytes 1574920 | tf_op jit(solution)/shard_map/pallas_call | solution.py:251
  4.9 2.9 %collective-permute-start = (f32[136,512]{1,0:T(8,128)S(1)}, f32[136,512]{1,0:T(8,128)S(1)}, u32[]{:S(2)}, u32[]{:S(2)}) collective-permute-start(f32[136,512]{1,0:T(8,128)S(1)} %get-tuple-element.26.send_ref), channel_id=1, source_target_pairs={{0,16},{16,0},{1,17},{17,1},{2,18},{18,2},{3,19},{19,3},{4,20},{20... | collective-permute-start | bytes 835592 | tf_op jit(solution)/shard_map/ppermute | solution.py:278
  7.8 0.8 %shard_map.97 = (f32[128,512]{1,0:T(8,128)S(1)}, f32[128,512]{1,0:T(8,128)S(1)}, f32[128,512]{1,0:T(8,128)S(1)}, f32[128,512]{1,0:T(8,128)S(1)}) custom-call(f32[128,512]{1,0:T(8,128)S(1)} %get-tuple-element.27.keep_ref, f32[136,512]{1,0:T(8,128)S(1)} %get-tuple-element.26.send_ref), custom_call_target="tpu_custom_call" | custom-call | bytes 540672 | tf_op jit(solution)/shard_map/pallas_call | solution.py:251
  8.6 0.4 collective-permute-done.recv_ref
  9.0 0.8 %shard_map.98 = (f32[128,512]{1,0:T(8,128)S(1)}, f32[128,512]{1,0:T(8,128)S(1)}, f32[128,512]{1,0:T(8,128)S(1)}, f32[128,512]{1,0:T(8,128)S(1)}) custom-call(f32[136,512]{1,0:T(8,128)S(1)} %collective-permute-done.recv_ref, f32[128,512]{1,0:T(8,128)S(1)} %get-tuple-element.28.refs_0_, f32[128,512]{1,0:T(8,128)S(1)} %get-tuple-element.29.refs_1_, ...), custom_call_target="tpu_custom_call" | custom-call | bytes 1327104 | tf_op jit(solution)/shard_map/pallas_call | solution.py:251
  9.8 0.1 collective-permute-start.1
  9.9 0.3 collective-permute-start.2
  10.2 2.3 %collective-permute-start.3 = (f32[128,512]{1,0:T(8,128)S(1)}, f32[128,512]{1,0:T(8,128)S(1)}, u32[]{:S(2)}, u32[]{:S(2)}) collective-permute-start(f32[128,512]{1,0:T(8,128)S(1)} %get-tuple-element.35), channel_id=1, source_target_pairs={{0,8},{4,12},{8,0},{12,4},{1,9},{5,13},{9,1},{13,5},{2,10},{6,14},... | collective-permute-start | bytes 786440 | tf_op jit(solution)/shard_map/ppermute | solution.py:281
  12.5 5.8 %collective-permute-done.1.b_ref = f32[128,512]{1,0:T(8,128)S(1)} collective-permute-done((f32[128,512]{1,0:T(8,128)S(1)}, f32[128,512]{1,0:T(8,128)S(1)}, u32[]{:S(2)}, u32[]{:S(2)}) %collective-permute-start.1) | collective-permute-done | bytes 262176 | tf_op jit(solution)/shard_map/ppermute | solution.py:281
  18.3 3.8 %collective-permute-done.2.c_ref = f32[128,512]{1,0:T(8,128)S(1)} collective-permute-done((f32[128,512]{1,0:T(8,128)S(1)}, f32[128,512]{1,0:T(8,128)S(1)}, u32[]{:S(2)}, u32[]{:S(2)}) %collective-permute-start.2) | collective-permute-done | bytes 262176 | tf_op jit(solution)/shard_map/ppermute | solution.py:281
  22.1 2.5 %collective-permute-done.3.d_ref = f32[128,512]{1,0:T(8,128)S(1)} collective-permute-done((f32[128,512]{1,0:T(8,128)S(1)}, f32[128,512]{1,0:T(8,128)S(1)}, u32[]{:S(2)}, u32[]{:S(2)}) %collective-permute-start.3) | collective-permute-done | bytes 262176 | tf_op jit(solution)/shard_map/ppermute | solution.py:281
  24.6 0.1 shard_map.99
  24.7 0.7 %collective-permute-start.4 = (f32[64,512]{1,0:T(8,128)S(1)}, f32[64,512]{1,0:T(8,128)S(1)}, u32[]{:S(2)}, u32[]{:S(2)}) collective-permute-start(f32[64,512]{1,0:T(8,128)S(1)} %get-tuple-element.36.a_ref), channel_id=1, source_target_pairs={{0,2},{3,1},{1,0},{2,3},{4,6},{7,5},{5,4},{6,7},{8,10},{11,9},{9,8... | collective-permute-start | bytes 393224 | tf_op jit(solution)/shard_map/ppermute | solution.py:286
  25.4 0.1 collective-permute-start.6
  25.5 1.9 %collective-permute-start.5 = (f32[64,512]{1,0:T(8,128)S(1)}, f32[64,512]{1,0:T(8,128)S(1)}, u32[]{:S(2)}, u32[]{:S(2)}) collective-permute-start(f32[64,512]{1,0:T(8,128)S(1)} %get-tuple-element.37), channel_id=1, source_target_pairs={{1,2},{2,1},{17,18},{18,17},{0,16},{16,0},{3,19},{19,3},{5,6},{6,5... | collective-permute-start | bytes 393224 | tf_op jit(solution)/shard_map/ppermute | solution.py:294
  27.4 0.3 shard_map.96
  27.7 0.0 collective-permute-done.8.sent_ref
  27.7 1.7 %collective-permute-start.9 = (f32[512,512]{1,0:T(8,128)S(1)}, f32[512,512]{1,0:T(8,128)S(1)}, u32[]{:S(2)}, u32[]{:S(2)}) collective-permute-start(f32[512,512]{1,0:T(8,128)S(1)} %collective-permute-done.8.sent_ref), channel_id=1, source_target_pairs={{0,16},{16,0},{1,17},{17,1},{2,18},{18,2},{3,19},{19,3},{4,20},{20... | collective-permute-start | bytes 3145736 | tf_op jit(solution)/shard_map/ppermute | solution.py:278
  29.4 0.8 %collective-permute-done.4.b_ref = f32[64,512]{1,0:T(8,128)S(1)} collective-permute-done((f32[64,512]{1,0:T(8,128)S(1)}, f32[64,512]{1,0:T(8,128)S(1)}, u32[]{:S(2)}, u32[]{:S(2)}) %collective-permute-start.4) | collective-permute-done | bytes 131104 | tf_op jit(solution)/shard_map/ppermute | solution.py:286
  30.2 4.2 %collective-permute-done.6.d_ref = f32[64,512]{1,0:T(8,128)S(1)} collective-permute-done((f32[64,512]{1,0:T(8,128)S(1)}, f32[64,512]{1,0:T(8,128)S(1)}, u32[]{:S(2)}, u32[]{:S(2)}) %collective-permute-start.6) | collective-permute-done | bytes 131104 | tf_op jit(solution)/shard_map/ppermute | solution.py:286
  34.5 0.0 collective-permute-done.5.c_ref
  34.5 0.3 shard_map.100.given_ref
  34.8 0.6 collective-permute-start.7
  35.4 0.1 collective-permute-start.10
  35.4 0.0 collective-permute-done.9.other_ref
  35.4 0.3 copy-done.1
  35.7 3.4 %shard_map.101 = (bf16[512,512]{1,0:T(8,128)(2,1)S(1)}, bf16[512,512]{1,0:T(8,128)(2,1)S(1)}, bf16[512,512]{1,0:T(8,128)(2,1)S(1)}, bf16[512,512]{1,0:T(8,128)(2...) custom-call(f32[512,512]{1,0:T(8,128)S(1)} %copy-done.1, ...), custom_call_target="tpu_custom_call" | custom-call | bytes 5242880 | tf_op jit(solution)/shard_map/pallas_call | solution.py:251
  39.2 0.6 collective-permute-start.11
  39.7 0.3 collective-permute-start.12
  40.1 0.0 collective-permute-done.10.refs_0_
  40.1 4.6 %collective-permute-done.11.refs_0_ = f32[64,512]{1,0:T(8,128)S(1)} collective-permute-done((f32[64,512]{1,0:T(8,128)S(1)}, f32[64,512]{1,0:T(8,128)S(1)}, u32[]{:S(2)}, u32[]{:S(2)}) %collective-permute-start.11) | collective-permute-done | bytes 131104 | tf_op jit(solution)/shard_map/ppermute | solution.py:281
  44.7 0.1 collective-permute-start.13
  44.8 2.7 %collective-permute-done.12.refs_3_ = f32[64,512]{1,0:T(8,128)S(1)} collective-permute-done((f32[64,512]{1,0:T(8,128)S(1)}, f32[64,512]{1,0:T(8,128)S(1)}, u32[]{:S(2)}, u32[]{:S(2)}) %collective-permute-start.12) | collective-permute-done | bytes 131104 | tf_op jit(solution)/shard_map/ppermute | solution.py:294
  47.5 0.5 shard_map.105.given_ref
  48.0 0.6 %collective-permute-done.13.refs_0_ = f32[64,512]{1,0:T(8,128)S(1)} collective-permute-done((f32[64,512]{1,0:T(8,128)S(1)}, f32[64,512]{1,0:T(8,128)S(1)}, u32[]{:S(2)}, u32[]{:S(2)}) %collective-permute-start.13) | collective-permute-done | bytes 131104 | tf_op jit(solution)/shard_map/ppermute | solution.py:294
  48.6 0.3 shard_map.106.x_ref
  48.9 0.1 collective-permute-start.16
  49.0 1.5 %collective-permute-start.15 = (f32[64,512]{1,0:T(8,128)S(1)}, f32[64,512]{1,0:T(8,128)S(1)}, u32[]{:S(2)}, u32[]{:S(2)}) collective-permute-start(f32[64,512]{1,0:T(8,128)S(1)} %shard_map.106.x_ref), channel_id=1, source_target_pairs={{1,0},{2,3},{0,1},{3,2},{5,4},{6,7},{4,5},{7,6},{9,8},{10,11},{8,9... | collective-permute-start | bytes 393224 | tf_op jit(solution)/shard_map/ppermute | solution.py:286
  50.4 1.3 %collective-permute-start.14 = (f32[64,512]{1,0:T(8,128)S(1)}, f32[64,512]{1,0:T(8,128)S(1)}, u32[]{:S(2)}, u32[]{:S(2)}) collective-permute-start(f32[64,512]{1,0:T(8,128)S(1)} %shard_map.106.x_ref), channel_id=1, source_target_pairs={{1,2},{2,1},{17,18},{18,17},{0,16},{16,0},{3,19},{19,3},{5,6},{6,5... | collective-permute-start | bytes 393224 | tf_op jit(solution)/shard_map/ppermute | solution.py:294
  51.8 1.0 %collective-permute-done.16.c_ref = f32[64,512]{1,0:T(8,128)S(1)} collective-permute-done((f32[64,512]{1,0:T(8,128)S(1)}, f32[64,512]{1,0:T(8,128)S(1)}, u32[]{:S(2)}, u32[]{:S(2)}) %collective-permute-start.16) | collective-permute-done | bytes 131104 | tf_op jit(solution)/shard_map/ppermute | solution.py:286
  52.8 1.4 %collective-permute-done.15.a_ref = f32[64,512]{1,0:T(8,128)S(1)} collective-permute-done((f32[64,512]{1,0:T(8,128)S(1)}, f32[64,512]{1,0:T(8,128)S(1)}, u32[]{:S(2)}, u32[]{:S(2)}) %collective-permute-start.15) | collective-permute-done | bytes 131104 | tf_op jit(solution)/shard_map/ppermute | solution.py:286
  54.2 0.9 %collective-permute-done.14.b_ref = f32[64,512]{1,0:T(8,128)S(1)} collective-permute-done((f32[64,512]{1,0:T(8,128)S(1)}, f32[64,512]{1,0:T(8,128)S(1)}, u32[]{:S(2)}, u32[]{:S(2)}) %collective-permute-start.14) | collective-permute-done | bytes 131104 | tf_op jit(solution)/shard_map/ppermute | solution.py:294
  55.1 0.1 shard_map.107.part_ref
  55.2 3.5 %collective-permute-start.17 = (f32[512,128]{1,0:T(8,128)S(1)}, f32[512,128]{1,0:T(8,128)S(1)}, u32[]{:S(2)}, u32[]{:S(2)}) collective-permute-start(f32[512,128]{1,0:T(8,128)S(1)} %shard_map.107.part_ref), channel_id=1, source_target_pairs={{0,16},{16,0},{1,17},{17,1},{2,18},{18,2},{3,19},{19,3},{4,20},{20... | collective-permute-start | bytes 786440 | tf_op jit(solution)/shard_map/ppermute | solution.py:278
  58.8 0.7 %shard_map.108.refs_0_ = f32[512,256]{1,0:T(8,128)} custom-call(f32[512,128]{1,0:T(8,128)S(1)} %shard_map.107.part_ref), custom_call_target="tpu_custom_call" | custom-call | bytes 262144 | tf_op jit(solution)/shard_map/pallas_call | solution.py:251
  59.5 0.4 collective-permute-done.17.part_ref
  59.9 0.7 %shard_map.109 = f32[512,256]{1,0:T(8,128)} custom-call(f32[512,128]{1,0:T(8,128)S(1)} %collective-permute-done.17.part_ref, f32[512,256]{1,0:T(8,128)} %shard_map.108.refs_0_), custom_call_target="tpu_custom_call", output_to_operand_aliasing={{}: (1, {})} | custom-call | bytes 786432 | tf_op jit(solution)/shard_map/pallas_call | solution.py:251
  (9 shorter events, 0.1 us)
Async XLA Ops:
  0.6 27.1 %collective-permute-start.8 = (f32[512,512]{1,0:T(8,128)}, f32[512,512]{1,0:T(8,128)S(1)}, u32[]{:S(2)}, u32[]{:S(2)}) collective-permute-start(f32[512,512]{1,0:T(8,128)} %own_ref.1), channel_id=1, source_target_pairs={{4,5},{8,9},{12,13},{9,10},{13,14},{20,22},{24,26},{28,30},{30,29}} | collective-permute-start | bytes 3145736 | tf_op jit(solution)/shard_map/ppermute | solution.py:299
  4.9 4.1 %collective-permute-start = (f32[136,512]{1,0:T(8,128)S(1)}, f32[136,512]{1,0:T(8,128)S(1)}, u32[]{:S(2)}, u32[]{:S(2)}) collective-permute-start(f32[136,512]{1,0:T(8,128)S(1)} %get-tuple-element.26.send_ref), channel_id=1, source_target_pairs={{0,16},{16,0},{1,17},{17,1},{2,18},{18,2},{3,19},{19,3},{4,20},{20... | collective-permute-start | bytes 835592 | tf_op jit(solution)/shard_map/ppermute | solution.py:278
  9.0 18.4 %copy-start = (f32[512,512]{1,0:T(8,128)S(1)}, f32[512,512]{1,0:T(8,128)}, u32[]{:S(2)}) copy-start(f32[512,512]{1,0:T(8,128)} %diag_ref.1) | copy-start | bytes 3145732
  9.8 8.5 %collective-permute-start.1 = (f32[128,512]{1,0:T(8,128)S(1)}, f32[128,512]{1,0:T(8,128)S(1)}, u32[]{:S(2)}, u32[]{:S(2)}) collective-permute-start(f32[128,512]{1,0:T(8,128)S(1)} %get-tuple-element.33), channel_id=1, source_target_pairs={{0,12},{4,8},{8,4},{12,0},{1,13},{5,9},{9,5},{13,1},{2,14},{6,10},... | collective-permute-start | bytes 786440 | tf_op jit(solution)/shard_map/ppermute | solution.py:281
  9.9 12.3 %collective-permute-start.2 = (f32[128,512]{1,0:T(8,128)S(1)}, f32[128,512]{1,0:T(8,128)S(1)}, u32[]{:S(2)}, u32[]{:S(2)}) collective-permute-start(f32[128,512]{1,0:T(8,128)S(1)} %get-tuple-element.34), channel_id=1, source_target_pairs={{0,4},{4,0},{8,12},{12,8},{1,5},{5,1},{9,13},{13,9},{2,6},{6,2},{1... | collective-permute-start | bytes 786440 | tf_op jit(solution)/shard_map/ppermute | solution.py:281
  10.2 14.4 %collective-permute-start.3 = (f32[128,512]{1,0:T(8,128)S(1)}, f32[128,512]{1,0:T(8,128)S(1)}, u32[]{:S(2)}, u32[]{:S(2)}) collective-permute-start(f32[128,512]{1,0:T(8,128)S(1)} %get-tuple-element.35), channel_id=1, source_target_pairs={{0,8},{4,12},{8,0},{12,4},{1,9},{5,13},{9,1},{13,5},{2,10},{6,14},... | collective-permute-start | bytes 786440 | tf_op jit(solution)/shard_map/ppermute | solution.py:281
  24.6 2.8 %copy-start.2 = (f32[512,256]{1,0:T(8,128)S(1)}, f32[512,256]{1,0:T(8,128)}, u32[]{:S(2)}) copy-start(f32[512,256]{1,0:T(8,128)} %rhs_ref.1) | copy-start | bytes 1572868
  24.7 5.5 %collective-permute-start.4 = (f32[64,512]{1,0:T(8,128)S(1)}, f32[64,512]{1,0:T(8,128)S(1)}, u32[]{:S(2)}, u32[]{:S(2)}) collective-permute-start(f32[64,512]{1,0:T(8,128)S(1)} %get-tuple-element.36.a_ref), channel_id=1, source_target_pairs={{0,2},{3,1},{1,0},{2,3},{4,6},{7,5},{5,4},{6,7},{8,10},{11,9},{9,8... | collective-permute-start | bytes 393224 | tf_op jit(solution)/shard_map/ppermute | solution.py:286
  25.4 9.1 %collective-permute-start.6 = (f32[64,512]{1,0:T(8,128)S(1)}, f32[64,512]{1,0:T(8,128)S(1)}, u32[]{:S(2)}, u32[]{:S(2)}) collective-permute-start(f32[64,512]{1,0:T(8,128)S(1)} %get-tuple-element.37), channel_id=1, source_target_pairs={{0,1},{3,2},{1,0},{2,3},{4,5},{7,6},{5,4},{6,7},{8,9},{11,10},{9,8... | collective-permute-start | bytes 393224 | tf_op jit(solution)/shard_map/ppermute | solution.py:286
  25.5 9.0 %collective-permute-start.5 = (f32[64,512]{1,0:T(8,128)S(1)}, f32[64,512]{1,0:T(8,128)S(1)}, u32[]{:S(2)}, u32[]{:S(2)}) collective-permute-start(f32[64,512]{1,0:T(8,128)S(1)} %get-tuple-element.37), channel_id=1, source_target_pairs={{1,2},{2,1},{17,18},{18,17},{0,16},{16,0},{3,19},{19,3},{5,6},{6,5... | collective-permute-start | bytes 393224 | tf_op jit(solution)/shard_map/ppermute | solution.py:294
  27.7 7.7 %collective-permute-start.9 = (f32[512,512]{1,0:T(8,128)S(1)}, f32[512,512]{1,0:T(8,128)S(1)}, u32[]{:S(2)}, u32[]{:S(2)}) collective-permute-start(f32[512,512]{1,0:T(8,128)S(1)} %collective-permute-done.8.sent_ref), channel_id=1, source_target_pairs={{0,16},{16,0},{1,17},{17,1},{2,18},{18,2},{3,19},{19,3},{4,20},{20... | collective-permute-start | bytes 3145736 | tf_op jit(solution)/shard_map/ppermute | solution.py:278
  34.5 1.2 %copy-start.1 = (f32[512,512]{1,0:T(8,128)S(1)}, f32[512,512]{1,0:T(8,128)}, u32[]{:S(2)}) copy-start(f32[512,512]{1,0:T(8,128)} %own_ref.1) | copy-start | bytes 3145732
  34.8 4.4 %collective-permute-start.7 = (f32[64,512]{1,0:T(8,128)S(1)}, f32[64,512]{1,0:T(8,128)S(1)}, u32[]{:S(2)}, u32[]{:S(2)}) collective-permute-start(f32[64,512]{1,0:T(8,128)S(1)} %shard_map.100.given_ref), channel_id=1, source_target_pairs={{0,4},{4,0},{16,20},{20,16},{8,24},{24,8},{12,28},{28,12},{1,5},{5... | collective-permute-start | bytes 393224 | tf_op jit(solution)/shard_map/ppermute | solution.py:294
  35.4 4.7 %collective-permute-start.10 = (f32[64,512]{1,0:T(8,128)S(1)}, f32[64,512]{1,0:T(8,128)S(1)}, u32[]{:S(2)}, u32[]{:S(2)}) collective-permute-start(f32[64,512]{1,0:T(8,128)S(1)} %shard_map.100.given_ref), channel_id=1, source_target_pairs={{0,8},{8,0},{16,24},{24,16},{4,20},{20,4},{12,28},{28,12},{1,9},{9... | collective-permute-start | bytes 393224 | tf_op jit(solution)/shard_map/ppermute | solution.py:294
  39.2 5.6 %collective-permute-start.11 = (f32[64,512]{1,0:T(8,128)S(1)}, f32[64,512]{1,0:T(8,128)S(1)}, u32[]{:S(2)}, u32[]{:S(2)}) collective-permute-start(f32[64,512]{1,0:T(8,128)S(1)} %shard_map.102.given_ref), channel_id=1, source_target_pairs={{0,12},{4,8},{8,4},{12,0},{1,13},{5,9},{9,5},{13,1},{2,14},{6,10},... | collective-permute-start | bytes 393224 | tf_op jit(solution)/shard_map/ppermute | solution.py:281
  39.7 7.8 %collective-permute-start.12 = (f32[64,512]{1,0:T(8,128)S(1)}, f32[64,512]{1,0:T(8,128)S(1)}, u32[]{:S(2)}, u32[]{:S(2)}) collective-permute-start(f32[64,512]{1,0:T(8,128)S(1)} %shard_map.102.given_ref), channel_id=1, source_target_pairs={{4,12},{12,4},{20,28},{28,20},{0,16},{16,0},{8,24},{24,8},{5,13},{... | collective-permute-start | bytes 393224 | tf_op jit(solution)/shard_map/ppermute | solution.py:294
  44.7 3.9 %collective-permute-start.13 = (f32[64,512]{1,0:T(8,128)S(1)}, f32[64,512]{1,0:T(8,128)S(1)}, u32[]{:S(2)}, u32[]{:S(2)}) collective-permute-start(f32[64,512]{1,0:T(8,128)S(1)} %shard_map.104.given_ref), channel_id=1, source_target_pairs={{8,12},{12,8},{24,28},{28,24},{0,16},{16,0},{4,20},{20,4},{9,13},{... | collective-permute-start | bytes 393224 | tf_op jit(solution)/shard_map/ppermute | solution.py:294
  48.9 3.9 %collective-permute-start.16 = (f32[64,512]{1,0:T(8,128)S(1)}, f32[64,512]{1,0:T(8,128)S(1)}, u32[]{:S(2)}, u32[]{:S(2)}) collective-permute-start(f32[64,512]{1,0:T(8,128)S(1)} %shard_map.106.x_ref), channel_id=1, source_target_pairs={{1,3},{2,0},{0,1},{3,2},{5,7},{6,4},{4,5},{7,6},{9,11},{10,8},{8,9... | collective-permute-start | bytes 393224 | tf_op jit(solution)/shard_map/ppermute | solution.py:286
  49.0 5.2 %collective-permute-start.15 = (f32[64,512]{1,0:T(8,128)S(1)}, f32[64,512]{1,0:T(8,128)S(1)}, u32[]{:S(2)}, u32[]{:S(2)}) collective-permute-start(f32[64,512]{1,0:T(8,128)S(1)} %shard_map.106.x_ref), channel_id=1, source_target_pairs={{1,0},{2,3},{0,1},{3,2},{5,4},{6,7},{4,5},{7,6},{9,8},{10,11},{8,9... | collective-permute-start | bytes 393224 | tf_op jit(solution)/shard_map/ppermute | solution.py:286
  50.4 4.6 %collective-permute-start.14 = (f32[64,512]{1,0:T(8,128)S(1)}, f32[64,512]{1,0:T(8,128)S(1)}, u32[]{:S(2)}, u32[]{:S(2)}) collective-permute-start(f32[64,512]{1,0:T(8,128)S(1)} %shard_map.106.x_ref), channel_id=1, source_target_pairs={{1,2},{2,1},{17,18},{18,17},{0,16},{16,0},{3,19},{19,3},{5,6},{6,5... | collective-permute-start | bytes 393224 | tf_op jit(solution)/shard_map/ppermute | solution.py:294
  55.2 4.7 %collective-permute-start.17 = (f32[512,128]{1,0:T(8,128)S(1)}, f32[512,128]{1,0:T(8,128)S(1)}, u32[]{:S(2)}, u32[]{:S(2)}) collective-permute-start(f32[512,128]{1,0:T(8,128)S(1)} %shard_map.107.part_ref), channel_id=1, source_target_pairs={{0,16},{16,0},{1,17},{17,1},{2,18},{18,2},{3,19},{19,3},{4,20},{20... | collective-permute-start | bytes 786440 | tf_op jit(solution)/shard_map/ppermute | solution.py:278

commit v25 on v23

--- a/solution.py
+++ b/solution.py
@@ -312,7 +312,7 @@
     )
     sums = call(own_kernel, [keep, send], [(half, size)] * rows)
     sums = call(other_kernel, [swap(send)] + sums, [(half, size)] * rows)
-    got = [along_row(sums[s], s) for s in (3, 1, 2)]
+    got = [along_row(sums[s], s) for s in (1, 2, 3)]
     rhs_piece, diag_high, diag_low = call(
         turn_kernel, [top_rhs, top_diag], [shape, block, block], [(half, size)]
     )

time: 61 us -> 61 us (level)
  starting transfers between devices: 19.4 us -> 23 us
  waiting for transfers between devices: 29.2 us -> 25.7 us
    ppermute x3, starting transfers between devices: 8.22 us -> 12.4 us  [swap(): return lax.ppermute(value, 'leaf', [(0, 1), (1, 0)])]
    ppermute x4, waiting for transfers between devices: 7.47 us -> 5.38 us  [along_col(): return lax.ppermute(value, 'col', pairs + list(zip(rest, open_ends)))]
    ppermute x4, waiting for transfers between devices: 16.7 us -> 15 us  [along_row(): return lax.ppermute(value, 'row', [(r, r ^ step) for r in range(rows)])]
    ppermute x6, starting transfers between devices: 4.27 us -> 3.35 us  [exchange(): return lax.ppermute(value, ('leaf', axis), pairs)]
  transfers between devices with their start and end apart: 18 -> 18, of which waited for: 13 -> 11; matrix products, arithmetic and copies ran while one was open for 0% -> 0% of each run, Pallas kernels for 16% -> 16%
where the time goes in v25:
time: 61 us; the launch traced here: 60.6 us
  waiting for transfers between devices  25.7 us (42%)
  starting transfers between devices  23 us (38%)
  Pallas kernels  10.9 us (18%)
  between operations  0.8 us (1%)
    ppermute x4, waiting for transfers between devices, along_row(): return lax.ppermute(value, 'row', [(r, r ^ step) for r in range(rows)])  15 us
    ppermute x3, starting transfers between devices, swap(): return lax.ppermute(value, 'leaf', [(0, 1), (1, 0)])  12.4 us
    pallas_call x15, Pallas kernels, call(): pl.pallas_call(kernel, out_shape=[shape(i, out) for i, out in enumerate(o...  10.9 us
    ppermute x4, waiting for transfers between devices, along_col(): return lax.ppermute(value, 'col', pairs + list(zip(rest, open_ends)))  5.38 us
    ppermute x6, waiting for transfers between devices, exchange(): return lax.ppermute(value, ('leaf', axis), pairs)  4.39 us
    ppermute x6, starting transfers between devices, exchange(): return lax.ppermute(value, ('leaf', axis), pairs)  3.35 us
    ppermute x4, starting transfers between devices, along_row(): return lax.ppermute(value, 'row', [(r, r ^ step) for r in range(rows)])  3.28 us
    ppermute x4, starting transfers between devices, along_col(): return lax.ppermute(value, 'col', pairs + list(zip(rest, open_ends)))  2.6 us
  transfers between devices with their start and end apart: 18, of which 11 were waited for; matrix products, arithmetic and copies ran while one was open for 0% of the time, Pallas kernels for 16%

profile of v25, /device:TPU:15, one launch (start us, length us, event | category | flops | bytes accessed | tf_op | source)
XLA Modules:
  0.0 60.6 jit_solution(331880501489428716)
XLA Ops:
  0.6 1.3 %collective-permute-start.8 = (f32[512,512]{1,0:T(8,128)}, f32[512,512]{1,0:T(8,128)S(1)}, u32[]{:S(2)}, u32[]{:S(2)}) collective-permute-start(f32[512,512]{1,0:T(8,128)} %own_ref.1), channel_id=1, source_target_pairs={{4,5},{8,9},{12,13},{9,10},{13,14},{20,22},{24,26},{28,30},{30,29}} | collective-permute-start | bytes 3145736 | tf_op jit(solution)/shard_map/ppermute | solution.py:299
  1.9 2.9 %shard_map.95 = (f32[2,256,256]{2,1,0:T(8,128)}, f32[128,512]{1,0:T(8,128)S(1)}, f32[136,512]{1,0:T(8,128)S(1)}) custom-call(s32[2]{0:T(128)} %live_hbm.1, f32[2,256,256]{2,1,0:T(8,128)} %rhs_hbm.1, f32[2,256,256]{2,1,0:T(8,128)} %diag_hbm.1, f32[2,256,256]{2,1,0:T(8,128)} %off_hbm.1, s32[2,256]{1,0:T(2,128)} %tgt_hbm.1), custom_call_target="tpu_custom_call" | custom-call | bytes 1574920 | tf_op jit(solution)/shard_map/pallas_call | solution.py:251
  4.9 2.9 %collective-permute-start = (f32[136,512]{1,0:T(8,128)S(1)}, f32[136,512]{1,0:T(8,128)S(1)}, u32[]{:S(2)}, u32[]{:S(2)}) collective-permute-start(f32[136,512]{1,0:T(8,128)S(1)} %get-tuple-element.26.send_ref), channel_id=1, source_target_pairs={{0,16},{16,0},{1,17},{17,1},{2,18},{18,2},{3,19},{19,3},{4,20},{20... | collective-permute-start | bytes 835592 | tf_op jit(solution)/shard_map/ppermute | solution.py:278
  7.8 0.8 %shard_map.97 = (f32[128,512]{1,0:T(8,128)S(1)}, f32[128,512]{1,0:T(8,128)S(1)}, f32[128,512]{1,0:T(8,128)S(1)}, f32[128,512]{1,0:T(8,128)S(1)}) custom-call(f32[128,512]{1,0:T(8,128)S(1)} %get-tuple-element.27.keep_ref, f32[136,512]{1,0:T(8,128)S(1)} %get-tuple-element.26.send_ref), custom_call_target="tpu_custom_call" | custom-call | bytes 540672 | tf_op jit(solution)/shard_map/pallas_call | solution.py:251
  8.6 0.4 collective-permute-done.recv_ref
  9.0 0.8 %shard_map.98 = (f32[128,512]{1,0:T(8,128)S(1)}, f32[128,512]{1,0:T(8,128)S(1)}, f32[128,512]{1,0:T(8,128)S(1)}, f32[128,512]{1,0:T(8,128)S(1)}) custom-call(f32[136,512]{1,0:T(8,128)S(1)} %collective-permute-done.recv_ref, f32[128,512]{1,0:T(8,128)S(1)} %get-tuple-element.28.refs_0_, f32[128,512]{1,0:T(8,128)S(1)} %get-tuple-element.29.refs_1_, ...), custom_call_target="tpu_custom_call" | custom-call | bytes 1327104 | tf_op jit(solution)/shard_map/pallas_call | solution.py:251
  9.8 0.3 collective-permute-start.1
  10.1 0.0 collective-permute-start.2
  10.1 2.4 %collective-permute-start.3 = (f32[128,512]{1,0:T(8,128)S(1)}, f32[128,512]{1,0:T(8,128)S(1)}, u32[]{:S(2)}, u32[]{:S(2)}) collective-permute-start(f32[128,512]{1,0:T(8,128)S(1)} %get-tuple-element.35), channel_id=1, source_target_pairs={{0,12},{4,8},{8,4},{12,0},{1,13},{5,9},{9,5},{13,1},{2,14},{6,10},... | collective-permute-start | bytes 786440 | tf_op jit(solution)/shard_map/ppermute | solution.py:281
  12.5 4.9 %collective-permute-done.1.b_ref = f32[128,512]{1,0:T(8,128)S(1)} collective-permute-done((f32[128,512]{1,0:T(8,128)S(1)}, f32[128,512]{1,0:T(8,128)S(1)}, u32[]{:S(2)}, u32[]{:S(2)}) %collective-permute-start.1) | collective-permute-done | bytes 262176 | tf_op jit(solution)/shard_map/ppermute | solution.py:281
  17.4 5.5 %collective-permute-done.2.c_ref = f32[128,512]{1,0:T(8,128)S(1)} collective-permute-done((f32[128,512]{1,0:T(8,128)S(1)}, f32[128,512]{1,0:T(8,128)S(1)}, u32[]{:S(2)}, u32[]{:S(2)}) %collective-permute-start.2) | collective-permute-done | bytes 262176 | tf_op jit(solution)/shard_map/ppermute | solution.py:281
  22.9 0.0 collective-permute-done.3.d_ref
  22.9 0.1 shard_map.99
  23.0 1.0 %collective-permute-start.4 = (f32[64,512]{1,0:T(8,128)S(1)}, f32[64,512]{1,0:T(8,128)S(1)}, u32[]{:S(2)}, u32[]{:S(2)}) collective-permute-start(f32[64,512]{1,0:T(8,128)S(1)} %get-tuple-element.36.a_ref), channel_id=1, source_target_pairs={{0,2},{3,1},{1,0},{2,3},{4,6},{7,5},{5,4},{6,7},{8,10},{11,9},{9,8... | collective-permute-start | bytes 393224 | tf_op jit(solution)/shard_map/ppermute | solution.py:286
  24.0 0.1 collective-permute-start.6
  24.1 1.6 %collective-permute-start.5 = (f32[64,512]{1,0:T(8,128)S(1)}, f32[64,512]{1,0:T(8,128)S(1)}, u32[]{:S(2)}, u32[]{:S(2)}) collective-permute-start(f32[64,512]{1,0:T(8,128)S(1)} %get-tuple-element.37), channel_id=1, source_target_pairs={{1,2},{2,1},{17,18},{18,17},{0,16},{16,0},{3,19},{19,3},{5,6},{6,5... | collective-permute-start | bytes 393224 | tf_op jit(solution)/shard_map/ppermute | solution.py:294
  25.7 0.3 shard_map.96
  26.0 0.0 collective-permute-done.8.sent_ref
  26.0 6.2 %collective-permute-start.9 = (f32[512,512]{1,0:T(8,128)S(1)}, f32[512,512]{1,0:T(8,128)S(1)}, u32[]{:S(2)}, u32[]{:S(2)}) collective-permute-start(f32[512,512]{1,0:T(8,128)S(1)} %collective-permute-done.8.sent_ref), channel_id=1, source_target_pairs={{0,16},{16,0},{1,17},{17,1},{2,18},{18,2},{3,19},{19,3},{4,20},{20... | collective-permute-start | bytes 3145736 | tf_op jit(solution)/shard_map/ppermute | solution.py:278
  32.2 0.0 collective-permute-done.4.b_ref
  32.2 2.3 %collective-permute-done.6.d_ref = f32[64,512]{1,0:T(8,128)S(1)} collective-permute-done((f32[64,512]{1,0:T(8,128)S(1)}, f32[64,512]{1,0:T(8,128)S(1)}, u32[]{:S(2)}, u32[]{:S(2)}) %collective-permute-start.6) | collective-permute-done | bytes 131104 | tf_op jit(solution)/shard_map/ppermute | solution.py:286
  34.5 0.0 collective-permute-done.5.c_ref
  34.5 0.3 shard_map.100.given_ref
  34.8 0.6 collective-permute-start.7
  35.4 0.1 collective-permute-start.10
  35.4 0.0 collective-permute-done.9.other_ref
  35.4 0.3 copy-done.1
  35.7 3.4 %shard_map.101 = (bf16[512,512]{1,0:T(8,128)(2,1)S(1)}, bf16[512,512]{1,0:T(8,128)(2,1)S(1)}, bf16[512,512]{1,0:T(8,128)(2,1)S(1)}, bf16[512,512]{1,0:T(8,128)(2...) custom-call(f32[512,512]{1,0:T(8,128)S(1)} %copy-done.1, ...), custom_call_target="tpu_custom_call" | custom-call | bytes 5242880 | tf_op jit(solution)/shard_map/pallas_call | solution.py:251
  39.1 0.0 collective-permute-done.7.refs_0_
  39.2 0.6 collective-permute-start.11
  39.7 0.3 collective-permute-start.12
  40.1 4.6 %collective-permute-done.11.refs_0_ = f32[64,512]{1,0:T(8,128)S(1)} collective-permute-done((f32[64,512]{1,0:T(8,128)S(1)}, f32[64,512]{1,0:T(8,128)S(1)}, u32[]{:S(2)}, u32[]{:S(2)}) %collective-permute-start.11) | collective-permute-done | bytes 131104 | tf_op jit(solution)/shard_map/ppermute | solution.py:281
  44.7 0.1 collective-permute-start.13
  44.8 2.7 %collective-permute-done.12.refs_3_ = f32[64,512]{1,0:T(8,128)S(1)} collective-permute-done((f32[64,512]{1,0:T(8,128)S(1)}, f32[64,512]{1,0:T(8,128)S(1)}, u32[]{:S(2)}, u32[]{:S(2)}) %collective-permute-start.12) | collective-permute-done | bytes 131104 | tf_op jit(solution)/shard_map/ppermute | solution.py:294
  47.5 0.5 shard_map.105.given_ref
  48.0 0.7 %collective-permute-done.13.refs_0_ = f32[64,512]{1,0:T(8,128)S(1)} collective-permute-done((f32[64,512]{1,0:T(8,128)S(1)}, f32[64,512]{1,0:T(8,128)S(1)}, u32[]{:S(2)}, u32[]{:S(2)}) %collective-permute-start.13) | collective-permute-done | bytes 131104 | tf_op jit(solution)/shard_map/ppermute | solution.py:294
  48.6 0.3 shard_map.106.x_ref
  48.9 0.1 collective-permute-start.16
  49.0 1.5 %collective-permute-start.15 = (f32[64,512]{1,0:T(8,128)S(1)}, f32[64,512]{1,0:T(8,128)S(1)}, u32[]{:S(2)}, u32[]{:S(2)}) collective-permute-start(f32[64,512]{1,0:T(8,128)S(1)} %shard_map.106.x_ref), channel_id=1, source_target_pairs={{1,0},{2,3},{0,1},{3,2},{5,4},{6,7},{4,5},{7,6},{9,8},{10,11},{8,9... | collective-permute-start | bytes 393224 | tf_op jit(solution)/shard_map/ppermute | solution.py:286
  50.5 0.7 %collective-permute-start.14 = (f32[64,512]{1,0:T(8,128)S(1)}, f32[64,512]{1,0:T(8,128)S(1)}, u32[]{:S(2)}, u32[]{:S(2)}) collective-permute-start(f32[64,512]{1,0:T(8,128)S(1)} %shard_map.106.x_ref), channel_id=1, source_target_pairs={{1,2},{2,1},{17,18},{18,17},{0,16},{16,0},{3,19},{19,3},{5,6},{6,5... | collective-permute-start | bytes 393224 | tf_op jit(solution)/shard_map/ppermute | solution.py:294
  51.1 1.7 %collective-permute-done.16.c_ref = f32[64,512]{1,0:T(8,128)S(1)} collective-permute-done((f32[64,512]{1,0:T(8,128)S(1)}, f32[64,512]{1,0:T(8,128)S(1)}, u32[]{:S(2)}, u32[]{:S(2)}) %collective-permute-start.16) | collective-permute-done | bytes 131104 | tf_op jit(solution)/shard_map/ppermute | solution.py:286
  52.8 1.4 %collective-permute-done.15.a_ref = f32[64,512]{1,0:T(8,128)S(1)} collective-permute-done((f32[64,512]{1,0:T(8,128)S(1)}, f32[64,512]{1,0:T(8,128)S(1)}, u32[]{:S(2)}, u32[]{:S(2)}) %collective-permute-start.15) | collective-permute-done | bytes 131104 | tf_op jit(solution)/shard_map/ppermute | solution.py:286
  54.2 1.1 %collective-permute-done.14.b_ref = f32[64,512]{1,0:T(8,128)S(1)} collective-permute-done((f32[64,512]{1,0:T(8,128)S(1)}, f32[64,512]{1,0:T(8,128)S(1)}, u32[]{:S(2)}, u32[]{:S(2)}) %collective-permute-start.14) | collective-permute-done | bytes 131104 | tf_op jit(solution)/shard_map/ppermute | solution.py:294
  55.3 0.1 shard_map.107.part_ref
  55.4 3.3 %collective-permute-start.17 = (f32[512,128]{1,0:T(8,128)S(1)}, f32[512,128]{1,0:T(8,128)S(1)}, u32[]{:S(2)}, u32[]{:S(2)}) collective-permute-start(f32[512,128]{1,0:T(8,128)S(1)} %shard_map.107.part_ref), channel_id=1, source_target_pairs={{0,16},{16,0},{1,17},{17,1},{2,18},{18,2},{3,19},{19,3},{4,20},{20... | collective-permute-start | bytes 786440 | tf_op jit(solution)/shard_map/ppermute | solution.py:278
  58.8 0.7 %shard_map.108.refs_0_ = f32[512,256]{1,0:T(8,128)} custom-call(f32[512,128]{1,0:T(8,128)S(1)} %shard_map.107.part_ref), custom_call_target="tpu_custom_call" | custom-call | bytes 262144 | tf_op jit(solution)/shard_map/pallas_call | solution.py:251
  59.5 0.4 collective-permute-done.17.part_ref
  59.9 0.7 %shard_map.109 = f32[512,256]{1,0:T(8,128)} custom-call(f32[512,128]{1,0:T(8,128)S(1)} %collective-permute-done.17.part_ref, f32[512,256]{1,0:T(8,128)} %shard_map.108.refs_0_), custom_call_target="tpu_custom_call", output_to_operand_aliasing={{}: (1, {})} | custom-call | bytes 786432 | tf_op jit(solution)/shard_map/pallas_call | solution.py:251
  (9 shorter events, 0.1 us)
Async XLA Ops:
  0.6 25.4 %collective-permute-start.8 = (f32[512,512]{1,0:T(8,128)}, f32[512,512]{1,0:T(8,128)S(1)}, u32[]{:S(2)}, u32[]{:S(2)}) collective-permute-start(f32[512,512]{1,0:T(8,128)} %own_ref.1), channel_id=1, source_target_pairs={{4,5},{8,9},{12,13},{9,10},{13,14},{20,22},{24,26},{28,30},{30,29}} | collective-permute-start | bytes 3145736 | tf_op jit(solution)/shard_map/ppermute | solution.py:299
  4.9 4.1 %collective-permute-start = (f32[136,512]{1,0:T(8,128)S(1)}, f32[136,512]{1,0:T(8,128)S(1)}, u32[]{:S(2)}, u32[]{:S(2)}) collective-permute-start(f32[136,512]{1,0:T(8,128)S(1)} %get-tuple-element.26.send_ref), channel_id=1, source_target_pairs={{0,16},{16,0},{1,17},{17,1},{2,18},{18,2},{3,19},{19,3},{4,20},{20... | collective-permute-start | bytes 835592 | tf_op jit(solution)/shard_map/ppermute | solution.py:278
  9.0 16.7 %copy-start = (f32[512,512]{1,0:T(8,128)S(1)}, f32[512,512]{1,0:T(8,128)}, u32[]{:S(2)}) copy-start(f32[512,512]{1,0:T(8,128)} %diag_ref.1) | copy-start | bytes 3145732
  9.8 7.6 %collective-permute-start.1 = (f32[128,512]{1,0:T(8,128)S(1)}, f32[128,512]{1,0:T(8,128)S(1)}, u32[]{:S(2)}, u32[]{:S(2)}) collective-permute-start(f32[128,512]{1,0:T(8,128)S(1)} %get-tuple-element.33), channel_id=1, source_target_pairs={{0,4},{4,0},{8,12},{12,8},{1,5},{5,1},{9,13},{13,9},{2,6},{6,2},{1... | collective-permute-start | bytes 786440 | tf_op jit(solution)/shard_map/ppermute | solution.py:281
  10.1 12.8 %collective-permute-start.2 = (f32[128,512]{1,0:T(8,128)S(1)}, f32[128,512]{1,0:T(8,128)S(1)}, u32[]{:S(2)}, u32[]{:S(2)}) collective-permute-start(f32[128,512]{1,0:T(8,128)S(1)} %get-tuple-element.34), channel_id=1, source_target_pairs={{0,8},{4,12},{8,0},{12,4},{1,9},{5,13},{9,1},{13,5},{2,10},{6,14},... | collective-permute-start | bytes 786440 | tf_op jit(solution)/shard_map/ppermute | solution.py:281
  10.1 12.8 %collective-permute-start.3 = (f32[128,512]{1,0:T(8,128)S(1)}, f32[128,512]{1,0:T(8,128)S(1)}, u32[]{:S(2)}, u32[]{:S(2)}) collective-permute-start(f32[128,512]{1,0:T(8,128)S(1)} %get-tuple-element.35), channel_id=1, source_target_pairs={{0,12},{4,8},{8,4},{12,0},{1,13},{5,9},{9,5},{13,1},{2,14},{6,10},... | collective-permute-start | bytes 786440 | tf_op jit(solution)/shard_map/ppermute | solution.py:281
  22.9 2.8 %copy-start.2 = (f32[512,256]{1,0:T(8,128)S(1)}, f32[512,256]{1,0:T(8,128)}, u32[]{:S(2)}) copy-start(f32[512,256]{1,0:T(8,128)} %rhs_ref.1) | copy-start | bytes 1572868
  23.0 9.2 %collective-permute-start.4 = (f32[64,512]{1,0:T(8,128)S(1)}, f32[64,512]{1,0:T(8,128)S(1)}, u32[]{:S(2)}, u32[]{:S(2)}) collective-permute-start(f32[64,512]{1,0:T(8,128)S(1)} %get-tuple-element.36.a_ref), channel_id=1, source_target_pairs={{0,2},{3,1},{1,0},{2,3},{4,6},{7,5},{5,4},{6,7},{8,10},{11,9},{9,8... | collective-permute-start | bytes 393224 | tf_op jit(solution)/shard_map/ppermute | solution.py:286
  24.0 10.5 %collective-permute-start.6 = (f32[64,512]{1,0:T(8,128)S(1)}, f32[64,512]{1,0:T(8,128)S(1)}, u32[]{:S(2)}, u32[]{:S(2)}) collective-permute-start(f32[64,512]{1,0:T(8,128)S(1)} %get-tuple-element.37), channel_id=1, source_target_pairs={{0,1},{3,2},{1,0},{2,3},{4,5},{7,6},{5,4},{6,7},{8,9},{11,10},{9,8... | collective-permute-start | bytes 393224 | tf_op jit(solution)/shard_map/ppermute | solution.py:286
  24.1 10.4 %collective-permute-start.5 = (f32[64,512]{1,0:T(8,128)S(1)}, f32[64,512]{1,0:T(8,128)S(1)}, u32[]{:S(2)}, u32[]{:S(2)}) collective-permute-start(f32[64,512]{1,0:T(8,128)S(1)} %get-tuple-element.37), channel_id=1, source_target_pairs={{1,2},{2,1},{17,18},{18,17},{0,16},{16,0},{3,19},{19,3},{5,6},{6,5... | collective-permute-start | bytes 393224 | tf_op jit(solution)/shard_map/ppermute | solution.py:294
  26.0 9.4 %collective-permute-start.9 = (f32[512,512]{1,0:T(8,128)S(1)}, f32[512,512]{1,0:T(8,128)S(1)}, u32[]{:S(2)}, u32[]{:S(2)}) collective-permute-start(f32[512,512]{1,0:T(8,128)S(1)} %collective-permute-done.8.sent_ref), channel_id=1, source_target_pairs={{0,16},{16,0},{1,17},{17,1},{2,18},{18,2},{3,19},{19,3},{4,20},{20... | collective-permute-start | bytes 3145736 | tf_op jit(solution)/shard_map/ppermute | solution.py:278
  34.5 1.2 %copy-start.1 = (f32[512,512]{1,0:T(8,128)S(1)}, f32[512,512]{1,0:T(8,128)}, u32[]{:S(2)}) copy-start(f32[512,512]{1,0:T(8,128)} %own_ref.1) | copy-start | bytes 3145732
  34.8 4.4 %collective-permute-start.7 = (f32[64,512]{1,0:T(8,128)S(1)}, f32[64,512]{1,0:T(8,128)S(1)}, u32[]{:S(2)}, u32[]{:S(2)}) collective-permute-start(f32[64,512]{1,0:T(8,128)S(1)} %shard_map.100.given_ref), channel_id=1, source_target_pairs={{0,4},{4,0},{16,20},{20,16},{8,24},{24,8},{12,28},{28,12},{1,5},{5... | collective-permute-start | bytes 393224 | tf_op jit(solution)/shard_map/ppermute | solution.py:294
  35.4 4.7 %collective-permute-start.10 = (f32[64,512]{1,0:T(8,128)S(1)}, f32[64,512]{1,0:T(8,128)S(1)}, u32[]{:S(2)}, u32[]{:S(2)}) collective-permute-start(f32[64,512]{1,0:T(8,128)S(1)} %shard_map.100.given_ref), channel_id=1, source_target_pairs={{0,8},{8,0},{16,24},{24,16},{4,20},{20,4},{12,28},{28,12},{1,9},{9... | collective-permute-start | bytes 393224 | tf_op jit(solution)/shard_map/ppermute | solution.py:294
  39.2 5.6 %collective-permute-start.11 = (f32[64,512]{1,0:T(8,128)S(1)}, f32[64,512]{1,0:T(8,128)S(1)}, u32[]{:S(2)}, u32[]{:S(2)}) collective-permute-start(f32[64,512]{1,0:T(8,128)S(1)} %shard_map.102.given_ref), channel_id=1, source_target_pairs={{0,12},{4,8},{8,4},{12,0},{1,13},{5,9},{9,5},{13,1},{2,14},{6,10},... | collective-permute-start | bytes 393224 | tf_op jit(solution)/shard_map/ppermute | solution.py:281
  39.7 7.8 %collective-permute-start.12 = (f32[64,512]{1,0:T(8,128)S(1)}, f32[64,512]{1,0:T(8,128)S(1)}, u32[]{:S(2)}, u32[]{:S(2)}) collective-permute-start(f32[64,512]{1,0:T(8,128)S(1)} %shard_map.102.given_ref), channel_id=1, source_target_pairs={{4,12},{12,4},{20,28},{28,20},{0,16},{16,0},{8,24},{24,8},{5,13},{... | collective-permute-start | bytes 393224 | tf_op jit(solution)/shard_map/ppermute | solution.py:294
  44.7 3.9 %collective-permute-start.13 = (f32[64,512]{1,0:T(8,128)S(1)}, f32[64,512]{1,0:T(8,128)S(1)}, u32[]{:S(2)}, u32[]{:S(2)}) collective-permute-start(f32[64,512]{1,0:T(8,128)S(1)} %shard_map.104.given_ref), channel_id=1, source_target_pairs={{8,12},{12,8},{24,28},{28,24},{0,16},{16,0},{4,20},{20,4},{9,13},{... | collective-permute-start | bytes 393224 | tf_op jit(solution)/shard_map/ppermute | solution.py:294
  48.9 3.9 %collective-permute-start.16 = (f32[64,512]{1,0:T(8,128)S(1)}, f32[64,512]{1,0:T(8,128)S(1)}, u32[]{:S(2)}, u32[]{:S(2)}) collective-permute-start(f32[64,512]{1,0:T(8,128)S(1)} %shard_map.106.x_ref), channel_id=1, source_target_pairs={{1,3},{2,0},{0,1},{3,2},{5,7},{6,4},{4,5},{7,6},{9,11},{10,8},{8,9... | collective-permute-start | bytes 393224 | tf_op jit(solution)/shard_map/ppermute | solution.py:286
  49.0 5.2 %collective-permute-start.15 = (f32[64,512]{1,0:T(8,128)S(1)}, f32[64,512]{1,0:T(8,128)S(1)}, u32[]{:S(2)}, u32[]{:S(2)}) collective-permute-start(f32[64,512]{1,0:T(8,128)S(1)} %shard_map.106.x_ref), channel_id=1, source_target_pairs={{1,0},{2,3},{0,1},{3,2},{5,4},{6,7},{4,5},{7,6},{9,8},{10,11},{8,9... | collective-permute-start | bytes 393224 | tf_op jit(solution)/shard_map/ppermute | solution.py:286
  50.5 4.8 %collective-permute-start.14 = (f32[64,512]{1,0:T(8,128)S(1)}, f32[64,512]{1,0:T(8,128)S(1)}, u32[]{:S(2)}, u32[]{:S(2)}) collective-permute-start(f32[64,512]{1,0:T(8,128)S(1)} %shard_map.106.x_ref), channel_id=1, source_target_pairs={{1,2},{2,1},{17,18},{18,17},{0,16},{16,0},{3,19},{19,3},{5,6},{6,5... | collective-permute-start | bytes 393224 | tf_op jit(solution)/shard_map/ppermute | solution.py:294
  55.4 4.5 %collective-permute-start.17 = (f32[512,128]{1,0:T(8,128)S(1)}, f32[512,128]{1,0:T(8,128)S(1)}, u32[]{:S(2)}, u32[]{:S(2)}) collective-permute-start(f32[512,128]{1,0:T(8,128)S(1)} %shard_map.107.part_ref), channel_id=1, source_target_pairs={{0,16},{16,0},{1,17},{17,1},{2,18},{18,2},{3,19},{19,3},{4,20},{20... | collective-permute-start | bytes 786440 | tf_op jit(solution)/shard_map/ppermute | solution.py:278
